TPU v7x, 32 devices: a whole 2x2x4 slice. The times are simulated.
32 devices in a mesh: patch: 4 (over y, x), shot: 8 (over z, core).
Axes of the slice: x: 2, y: 2, z: 4, core: 2. Of those that a mesh axis runs over, the one named last changes fastest.
Arguments:
- estimate: bfloat16 [256, 512, 1024], P('shot', 'patch'), may hold values from -6 to 6
- observed: bfloat16 [256, 512, 1024], P('shot', 'patch'), may hold values from -6 to 6
- random_source_delays: int32 [256], replicated, may hold values from 0 to 255
- thresholds: float32 [512], replicated, may hold values from 0.5 to 3
Outputs:
- updated: float32 [256, 512, 1024], P('shot', 'patch')
- misfit: float32 [256], P('shot')
All inputs are finite; a program needn't handle non-finite values.
Results may differ from a plain program's by a relative error of at most 0.0084.
Values may be sent and summed in bfloat16 or wider, within the bound.
No kernel may reach another device: no remote copies, remote signals or barrier semaphores. Data moves between devices by JAX's collectives and lax.ppermute only.
A program may use at most 256 MiB of HBM per device.

v0:
```python
import jax
import jax.numpy as jnp
from jax import lax
from jax.sharding import PartitionSpec as P

NT = 1024
F = 512
SOURCE_SPACING = 512


correction_step_length = 0.5


def padded_2(shard, sides, width):
    for axis, dim in sides:
        peers, length = (lax.axis_size(axis), shard.shape[dim])
        up = [(i, (i + 1) % peers) for i in range(peers - 1)]
        down = [(j, i) for i, j in up]
        last = lax.slice_in_dim(shard, length - width, length, axis=dim)
        leading = lax.slice_in_dim(shard, 0, width, axis=dim)
        before = lax.ppermute(last, axis, up)
        after = lax.ppermute(leading, axis, down)
        shard = jnp.concatenate([before, shard, after], axis=dim)
    return shard


def delayed(traces, offset):
    length = traces.shape[-1]
    padded = jnp.pad(traces, ((0, 0), (length, length)))
    return lax.dynamic_slice_in_dim(padded, length - offset, length, 1)


def combined_data_panel(
    extended_receiver_signal, source_onset_moments_extended, initial_source_panel
):
    source_ordinal = extended_receiver_signal.shape[0] - 2
    record_window = lax.dynamic_slice_in_dim(
        source_onset_moments_extended, initial_source_panel + 2, source_ordinal + 2
    )
    subsequent_source_panel = record_window[2:] - record_window[1:-1]
    prior_source_panel = record_window[1:-1] - record_window[:-2]
    center = extended_receiver_signal[1:-1]
    later = jax.vmap(delayed)(extended_receiver_signal[2:], subsequent_source_panel)
    earlier = jax.vmap(delayed)(extended_receiver_signal[:-2], -prior_source_panel)
    return center + later + earlier


def time_tables():
    freq = jnp.arange(F, dtype=jnp.int32)
    sample = jnp.arange(NT, dtype=jnp.int32)
    phase = (freq[:, None] * sample[None, :] % NT).astype(jnp.float32)
    angle = 2.0 * jnp.pi * phase / NT
    root = jnp.sqrt(jnp.float32(NT))
    forward = jnp.stack([jnp.cos(angle) / root, -jnp.sin(angle) / root]).astype(jnp.bfloat16)
    weight = jnp.where(freq == 0, 1.0, 2.0).astype(jnp.float32)[:, None] / root
    inverse = jnp.stack([weight * jnp.cos(angle), -weight * jnp.sin(angle)]).astype(jnp.bfloat16)
    return (forward, inverse)


def shot_tables(source_panels):
    index = jnp.arange(source_panels, dtype=jnp.int32)
    phase = (index[:, None] * index[None, :] % source_panels).astype(jnp.float32)
    angle = 2.0 * jnp.pi * phase / source_panels
    root = jnp.sqrt(jnp.float32(source_panels))
    cosine = jnp.cos(angle) / root
    sine = jnp.sin(angle) / root
    across = jnp.stack([jnp.stack([cosine, sine]), jnp.stack([-sine, cosine])]).astype(jnp.bfloat16)
    back = jnp.stack([jnp.stack([cosine, -sine]), jnp.stack([sine, cosine])]).astype(jnp.bfloat16)
    return (across, back)


def shrink(wavenum, level):
    magnitude = jnp.sqrt(wavenum[0] * wavenum[0] + wavenum[1] * wavenum[1])
    factor = jnp.maximum(magnitude - level, 0.0) / jnp.maximum(magnitude, level)
    return (wavenum * factor[None]).astype(jnp.bfloat16)


def local(estimate, observed, random_source_delays, thresholds):
    shots_here = estimate.shape[0]
    total_sources = random_source_delays.shape[0]
    initial_source_panel = lax.axis_index("shot") * shots_here
    source_onset_moments = (
        jnp.arange(total_sources, dtype=jnp.int32) * SOURCE_SPACING + random_source_delays
    )
    source_onset_moments_extended = jnp.pad(source_onset_moments, (3, 3), mode="edge")
    present_gather = estimate.astype(jnp.float32)
    early_source_approximation = padded_2(estimate, (("shot", 0),), 1)
    resid = observed.astype(jnp.float32) - combined_data_panel(
        early_source_approximation.astype(jnp.float32),
        source_onset_moments_extended,
        initial_source_panel,
    )
    misfit_margin_samples = padded_2(resid, (("shot", 0),), 1)
    energy = jnp.sum(resid * resid, axis=(1, 2))
    misfit = lax.psum(energy, "patch") / (resid.shape[1] * lax.axis_size("patch") * NT)
    advanced_estimate = (
        present_gather
        + correction_step_length
        * combined_data_panel(
            misfit_margin_samples, source_onset_moments_extended, initial_source_panel
        )
    ).astype(jnp.bfloat16)
    forward, inverse = time_tables()
    spectra = jnp.einsum(
        "srt,pft->pfsr", advanced_estimate, forward, preferred_element_type=jnp.float32
    ).astype(jnp.bfloat16)
    share = F // lax.axis_size("shot")
    level = lax.dynamic_slice_in_dim(thresholds, lax.axis_index("shot") * share, share)
    across, back = shot_tables(total_sources)
    wavenum = jnp.einsum(
        "pqks,qfsr->pfkr",
        across,
        lax.all_to_all(spectra, "shot", split_axis=1, concat_axis=2, tiled=True),
        preferred_element_type=jnp.float32,
    )
    shrunk = shrink(wavenum, level[:, None, None])
    restored = jnp.einsum(
        "pqks,qfsr->pfkr", back, shrunk, preferred_element_type=jnp.float32
    ).astype(jnp.bfloat16)
    restored_here = lax.all_to_all(restored, "shot", split_axis=2, concat_axis=1, tiled=True)
    updated = jnp.einsum(
        "pft,pfsr->srt", inverse, restored_here, preferred_element_type=jnp.float32
    )
    return (updated, misfit)


def solution(mesh):
    in_specs = (P("shot", "patch", None), P("shot", "patch", None), P(), P())
    out_specs = (P("shot", "patch", None), P("shot"))
    return jax.shard_map(local, mesh=mesh, in_specs=in_specs, out_specs=out_specs, check_vma=False)
```

profile of v0, /device:TPU:0, one launch (start us, length us, event | category | flops | bytes accessed | tf_op | source)
XLA Modules:
  0.0 1215.8 jit_solution(1047258687391414595)
XLA Ops:
  9.7 4.7 maximum_convert_fusion
  14.4 12.4 %fusion.60 = (f32[32,128,1024]{2,1,0:T(8,128)}, f32[32,128,1024]{2,1,0:T(8,128)}) fusion(f32[34,128,1024]{2,1,0:T(8,128)S(1)} %maximum_convert_fusion), kind=kLoop, calls=%fused_computation.106 | loop fusion | bytes 67108864 | tf_op jit(solution)/shard_map/slice | solution.py:43
  26.8 3.7 copy-done
  30.6 23.1 %pad.15 = f32[32,128,3072]{2,1,0:T(8,128)} pad(f32[32,128,1024]{2,1,0:T(8,128)} %get-tuple-element.76, f32[]{:T(128)} %constant.71.clone.1), padding=0_0x0_0x1024_1024 | pad | bytes 67108864 | tf_op jit(solution)/shard_map/vmap(jit(_pad))/pad | solution.py:29
  53.7 8.0 broadcast.387.clone.1
  61.7 126.2 %while.4 = (s32[]{:T(128)}, f32[32,128,3072]{2,1,0:T(8,128)}, s32[32,3]{0,1:T(4,128)S(1)}, f32[32,128,1024]{2,1,0:T(8,128)}, s32[]{:T(128)}) while((s32[]{:T(128)}, f32[32,128,3072]{2,1,0:T(8,128)}, s32[32,3]{0,1:T(4,128)S(1)}, f32[32,128,1024]{2,1,0:T(8,128)}, s32[]{:T(128)}) %tuple.83), condition=%wide.while_cond, body=%wide.while_body.sunk | while | flops 2 | bytes 1050217 | solution.py:30
  113.5 3.4 dynamic-slice_dynamic-update-slice_fusion.8
  117.5 3.4 dynamic-slice_dynamic-update-slice_fusion.8
  145.1 3.4 dynamic-slice_dynamic-update-slice_fusion.8
  149.1 3.4 dynamic-slice_dynamic-update-slice_fusion.8
  188.0 23.1 %pad.16 = f32[32,128,3072]{2,1,0:T(8,128)} pad(f32[32,128,1024]{2,1,0:T(8,128)} %get-tuple-element.77, f32[]{:T(128)} %constant.71.clone.1), padding=0_0x0_0x1024_1024 | pad | bytes 67108864 | tf_op jit(solution)/shard_map/vmap(jit(_pad))/pad | solution.py:29
  211.1 8.3 broadcast.387.clone
  219.4 125.4 %while.5 = (s32[]{:T(128)}, f32[32,128,3072]{2,1,0:T(8,128)}, s32[32,3]{0,1:T(4,128)S(1)}, f32[32,128,1024]{2,1,0:T(8,128)}, s32[]{:T(128)}) while((s32[]{:T(128)}, f32[32,128,3072]{2,1,0:T(8,128)}, s32[32,3]{0,1:T(4,128)S(1)}, f32[32,128,1024]{2,1,0:T(8,128)}, s32[]{:T(128)}) %tuple.80), condition=%wide.while_cond.1, body=%wide.while_body.1.sunk | while | flops 2 | bytes 1050217 | solution.py:30
  344.8 19.8 %multiply_reduce_fusion = (f32[32]{0:T(128)S(1)}, f32[32,128,1024]{2,1,0:T(8,128)S(1)}) fusion(f32[32,128,1024]{2,1,0:T(8,128)} %get-tuple-element.17, f32[32,128,1024]{2,1,0:T(8,128)} %get-tuple-element.9, f32[34,128,1024]{2,1,0:T(8,128)} %copy-done, bf16[32,128,1024]{2,1,0:T(8,128)(2,1)} %param.5), kind=kLoop, calls=%fused_computation.17 | loop fusion | flops 25165792 | bytes 75497600 | tf_op jit(solution)/shard_map/reduce_sum | solution.py:94
  364.7 6.2 copy-done.1
  373.2 7.5 collective-permute-start.3
  380.7 8.6 multiply_convert_fusion.3
  389.3 43.5 %select_maximum_fusion.1 = (f32[32,128,3072]{2,1,0:T(8,128)}, f32[32,128,3072]{2,1,0:T(8,128)}) fusion(f32[1,128,1024]{2,1,0:T(8,128)S(1)} %collective-permute-done.2, f32[32,128,1024]{2,1,0:T(8,128)} %copy-done.1, f32[1,128,1024]{2,1,0:T(8,128)S(1)} %collective-permute-done.3), kind=kLoop, calls=%fused_computation.11 | loop fusion | flops 113246208 | bytes 118489088 | tf_op jit(solution)/shard_map/concatenate | solution.py:23
  432.8 7.9 broadcast.387.clone.3
  440.7 124.7 %while.6 = (s32[]{:T(128)}, f32[32,128,3072]{2,1,0:T(8,128)}, s32[32,3]{0,1:T(4,128)S(1)}, f32[32,128,1024]{2,1,0:T(8,128)}, s32[]{:T(128)}) while((s32[]{:T(128)}, f32[32,128,3072]{2,1,0:T(8,128)}, s32[32,3]{0,1:T(4,128)S(1)}, f32[32,128,1024]{2,1,0:T(8,128)}, s32[]{:T(128)}) %tuple.93), condition=%wide.while_cond.2, body=%wide.while_body.2.sunk | while | flops 2 | bytes 1050217 | solution.py:30
  565.4 7.9 broadcast.387.clone.2
  573.3 129.0 %while.7 = (s32[]{:T(128)}, f32[32,128,3072]{2,1,0:T(8,128)}, s32[32,3]{0,1:T(4,128)S(1)}, f32[32,128,1024]{2,1,0:T(8,128)}, s32[]{:T(128)}) while((s32[]{:T(128)}, f32[32,128,3072]{2,1,0:T(8,128)}, s32[32,3]{0,1:T(4,128)S(1)}, f32[32,128,1024]{2,1,0:T(8,128)}, s32[]{:T(128)}) %tuple.92), condition=%wide.while_cond.3, body=%wide.while_body.3.sunk | while | flops 2 | bytes 1050217 | solution.py:30
  577.9 3.4 dynamic-slice_dynamic-update-slice_fusion.11
  581.9 3.4 dynamic-slice_dynamic-update-slice_fusion.11
  586.0 3.4 dynamic-slice_dynamic-update-slice_fusion.11
  590.0 3.4 dynamic-slice_dynamic-update-slice_fusion.11
  594.0 3.4 dynamic-slice_dynamic-update-slice_fusion.11
  598.1 3.4 dynamic-slice_dynamic-update-slice_fusion.11
  602.1 3.4 dynamic-slice_dynamic-update-slice_fusion.11
  610.2 3.4 dynamic-slice_dynamic-update-slice_fusion.11
  614.2 3.4 dynamic-slice_dynamic-update-slice_fusion.11
  618.2 3.4 dynamic-slice_dynamic-update-slice_fusion.11
  622.3 3.4 dynamic-slice_dynamic-update-slice_fusion.11
  626.3 3.4 dynamic-slice_dynamic-update-slice_fusion.11
  630.3 3.4 dynamic-slice_dynamic-update-slice_fusion.11
  634.4 3.4 dynamic-slice_dynamic-update-slice_fusion.11
  642.4 3.4 dynamic-slice_dynamic-update-slice_fusion.11
  646.4 3.4 dynamic-slice_dynamic-update-slice_fusion.11
  650.5 3.4 dynamic-slice_dynamic-update-slice_fusion.11
  658.5 3.4 dynamic-slice_dynamic-update-slice_fusion.11
  662.6 3.4 dynamic-slice_dynamic-update-slice_fusion.11
  666.6 3.4 dynamic-slice_dynamic-update-slice_fusion.11
  674.6 3.4 dynamic-slice_dynamic-update-slice_fusion.11
  678.7 3.4 dynamic-slice_dynamic-update-slice_fusion.11
  682.7 3.4 dynamic-slice_dynamic-update-slice_fusion.11
  686.7 3.4 dynamic-slice_dynamic-update-slice_fusion.11
  690.8 3.4 dynamic-slice_dynamic-update-slice_fusion.11
  694.8 3.4 dynamic-slice_dynamic-update-slice_fusion.11
  702.2 24.8 %fusion.14 = bf16[2,512,32,128]{3,1,2,0:T(8,128)(2,1)} fusion(f32[32,128,1024]{2,1,0:T(8,128)} %get-tuple-element.33, f32[32,128,1024]{2,1,0:T(8,128)} %copy-done.1, f32[32,128,1024]{2,1,0:T(8,128)} %get-tuple-element.25, bf16[32,128,1024]{2,1,0:T(8,128)(2,1)} %param.4, bf16[1,512,1024]{2,1,0:T(8,128)(2,1)S(1)} %get-tuple-element.96, ...), kind=kOutput, calls=%fused_computation.35 | convolution fusion | flops 8623489024 | bytes 69206016 | tf_op jit(solution)/shard_map/srt,pft->pfsr/dot_general | solution.py:104
  727.0 12.2 %copy.19 = bf16[2,512,32,128]{3,2,0,1:T(8,128)(2,1)} copy(bf16[2,512,32,128]{3,1,2,0:T(8,128)(2,1)} %fusion.14) | data formatting | bytes 16777216 | tf_op jit(solution)/shard_map/convert_element_type | solution.py:106
  739.2 5.6 all-to-all-start
  747.8 181.2 %all-to-all-done = bf16[2,512,32,128]{3,2,0,1:T(8,128)(2,1)} async-done(((bf16[2,512,32,128]{3,2,0,1:T(8,128)(2,1)}), bf16[2,512,32,128]{3,2,0,1:T(8,128)(2,1)}, u32[]{:S(2)}, u32[]{:S(2)}) %all-to-all-start) | async-done | bytes 8388640 | tf_op jit(solution)/shard_map/all_to_all | solution.py:113
  929.0 9.4 copy.21
  938.4 7.0 convolution_bitcast_fusion.1
  945.5 6.9 divide_bitcast_fusion
  954.2 15.0 %fusion.17 = bf16[2,64,256,128]{2,3,0,1:T(8,128)(2,1)} fusion(f32[2,64,256,128]{2,3,0,1:T(8,128)} %copy-done.2, f32[64,256,128]{1,2,0:T(8,128)} %divide_bitcast_fusion, bf16[1,2,256,256]{3,2,1,0:T(8,128)(2,1)S(1)} %get-tuple-element.89, bf16[1,2,256,256]{3,2,1,0:T(8,128)(2,1)S(1)} %get-tuple-element.84), kind=kOutput, calls=%fused_computation.36 | convolution fusion | flops 4308598784 | bytes 34078720 | tf_op jit(solution)/shard_map/pqks,qfsr->pfkr/dot_general | solution.py:117
  969.2 21.1 %copy.23 = bf16[2,64,256,128]{3,0,1,2:T(2,128)(2,1)} copy(bf16[2,64,256,128]{2,3,0,1:T(8,128)(2,1)} %fusion.17) | data formatting | bytes 16777216 | tf_op jit(solution)/shard_map/convert_element_type | solution.py:119
  990.3 5.0 all-to-all-start.1
  995.3 8.7 multiply_convert_fusion.1
  1004.0 10.1 psum.7
  1014.6 164.5 %all-to-all-done.1 = bf16[2,64,256,128]{3,0,1,2:T(2,128)(2,1)} async-done(((bf16[2,64,256,128]{3,0,1,2:T(2,128)(2,1)}), bf16[2,64,256,128]{3,0,1,2:T(2,128)(2,1)}, u32[]{:S(2)}, u32[]{:S(2)}) %all-to-all-start.1) | async-done | bytes 8388640 | tf_op jit(solution)/shard_map/all_to_all | solution.py:120
  1179.1 12.2 %copy.24 = bf16[2,64,256,128]{3,2,1,0:T(8,128)(2,1)} copy(bf16[2,64,256,128]{3,0,1,2:T(2,128)(2,1)} %all-to-all-done.1) | data formatting | bytes 16777216 | tf_op jit(solution)/shard_map/all_to_all | solution.py:120
  1191.3 8.8 copy.25
  1200.1 15.5 %convolution_bitcast_fusion = f32[32,128,1024]{2,1,0:T(8,128)} fusion(bf16[2,512,32,128]{3,2,1,0:T(8,128)(2,1)} %bitcast.92, bf16[1,512,1024]{2,1,0:T(8,128)(2,1)S(1)} %get-tuple-element.100, bf16[1,512,1024]{2,1,0:T(8,128)(2,1)S(1)} %get-tuple-element.101), kind=kOutput, calls=%fused_computation.21 | convolution fusion | flops 8590983168 | bytes 27262976 | tf_op jit(solution)/shard_map/pft,pfsr->srt/dot_general | solution.py:121
  (383 shorter events, 420.3 us)
Async XLA Ops:
  1.7 6.6 collective-permute-start
  4.1 5.6 collective-permute-start.1
  14.4 16.1 %copy-start = (f32[34,128,1024]{2,1,0:T(8,128)}, f32[34,128,1024]{2,1,0:T(8,128)S(1)}, u32[]{:S(2)}) copy-start(f32[34,128,1024]{2,1,0:T(8,128)S(1)} %maximum_convert_fusion) | copy-start | bytes 53477380
  364.6 6.2 copy-start.1
  371.9 17.4 %collective-permute-start.2 = (f32[1,128,1024]{2,1,0:T(8,128)}, f32[1,128,1024]{2,1,0:T(8,128)S(1)}, u32[]{:S(2)}, u32[]{:S(2)}) collective-permute-start(f32[1,128,1024]{2,1,0:T(8,128)} %get-tuple-element.80), channel_id=1, source_target_pairs={{1,0},{2,1},{3,2},{4,3},{5,4},{6,5},{7,6},{9,8},{10,9},{11,10},{12... | collective-permute-start | bytes 1572872 | tf_op jit(solution)/shard_map/ppermute | solution.py:22
  373.2 16.1 %collective-permute-start.3 = (f32[1,128,1024]{2,1,0:T(8,128)}, f32[1,128,1024]{2,1,0:T(8,128)S(1)}, u32[]{:S(2)}, u32[]{:S(2)}) collective-permute-start(f32[1,128,1024]{2,1,0:T(8,128)} %get-tuple-element.81), channel_id=1, source_target_pairs={{0,1},{1,2},{2,3},{3,4},{4,5},{5,6},{6,7},{8,9},{9,10},{10,11},{11... | collective-permute-start | bytes 1572872 | tf_op jit(solution)/shard_map/ppermute | solution.py:21
  739.2 189.8 %all-to-all-start = ((bf16[2,512,32,128]{3,2,0,1:T(8,128)(2,1)}), bf16[2,512,32,128]{3,2,0,1:T(8,128)(2,1)}, u32[]{:S(2)}, u32[]{:S(2)}) async-start(bf16[2,512,32,128]{3,2,0,1:T(8,128)(2,1)} %copy.19), calls=%async_computation | async-start | bytes 16777216 | tf_op jit(solution)/shard_map/all_to_all | solution.py:113
  945.5 8.7 copy-start.2
  990.3 188.9 %all-to-all-start.1 = ((bf16[2,64,256,128]{3,0,1,2:T(2,128)(2,1)}), bf16[2,64,256,128]{3,0,1,2:T(2,128)(2,1)}, u32[]{:S(2)}, u32[]{:S(2)}) async-start(bf16[2,64,256,128]{3,0,1,2:T(2,128)(2,1)} %copy.23), calls=%async_computation.1 | async-start | bytes 16777216 | tf_op jit(solution)/shard_map/all_to_all | solution.py:120
where the time goes:
time: 1230 us; the launch traced here: 1220 us
  local copies, waits for them, and re-layouts  676 us (55%)
  waiting for transfers between devices  347 us (28%)
  other arithmetic  95.7 us (8%)
  matrix products  62.4 us (5%)
  starting transfers between devices  23 us (2%)
    gather x384, local copies, waits for them, and re-layouts  505 us
    all_to_all x1, waiting for transfers between devices, local(): lax.all_to_all(spectra, 'shot', split_axis=1, concat_axis=2, tiled=True)  181 us
    all_to_all x1, waiting for transfers between devices, local(): lax.all_to_all(restored, 'shot', split_axis=2, concat_axis=1, tiled=True)  165 us
    pad x2, local copies, waits for them, and re-layouts, delayed(): padded = jnp.pad(traces, ((0, 0), (length, length)))  46.3 us
    unnamed x11, local copies, waits for them, and re-layouts  43.7 us
    concatenate x1, other arithmetic, padded_2(): shard = jnp.concatenate([before, shard, after], axis=dim)  43.5 us
    dot_general x1, matrix products, local(): jnp.einsum('srt,pft->pfsr', advanced_estimate, forward, preferred_element...  24.8 us
  transfers between devices with their start and end apart: 6, of which 3 were waited for; matrix products, arithmetic and copies ran while one was open for 2% of the time, Pallas kernels for 0%

commit v1 on v0

v1 whole, which is shorter than its diff:
```python
import functools

import jax
import jax.numpy as jnp
import ml_dtypes
import numpy as np
from jax import lax
from jax.experimental import pallas as pl
from jax.experimental.pallas import tpu as pltpu
from jax.sharding import PartitionSpec as P

F = 512
SOURCE_SPACING = 512
JITTER = 256
STEP = 0.5
LANES = 128
NEAR = SOURCE_SPACING - JITTER
FAR = SOURCE_SPACING + JITTER
HALO = 3


def time_tables(samples, blocks):
    freq = np.arange(F, dtype=np.int32)
    sample = np.arange(samples, dtype=np.int32)
    phase = (freq[:, None] * sample[None, :] % samples).astype(np.float32)
    angle = np.float32(2.0 * np.pi) * phase / np.float32(samples)
    root = np.sqrt(np.float32(samples))
    weight = np.where(freq == 0, 1.0, 2.0).astype(np.float32)[:, None] / root
    forward = np.stack([np.cos(angle) / root, -np.sin(angle) / root])
    inverse = np.stack([weight * np.cos(angle), -weight * np.sin(angle)])

    def ordered(table):
        table = table.astype(np.float32).astype(ml_dtypes.bfloat16)
        table = table.reshape(2, blocks, F // blocks, samples).transpose(1, 0, 2, 3)
        return table.reshape(2 * F, samples)

    return np.ascontiguousarray(ordered(forward).T), ordered(inverse)


def shot_table(shots):
    index = np.arange(shots, dtype=np.int32)
    phase = (index[:, None] * index[None, :] % shots).astype(np.float32)
    angle = np.float32(2.0 * np.pi) * phase / np.float32(shots)
    root = np.sqrt(np.float32(shots))
    table = np.concatenate([np.cos(angle) / root, np.sin(angle) / root])
    return table.astype(np.float32).astype(ml_dtypes.bfloat16)


def blend_into(
    first_ref, delay_ref, est_ref, obs_ref, before_ref, after_ref, energy_ref, est32, res32, store
):
    shots, rows, samples = est_ref.shape
    columns = samples // LANES
    margin = (FAR - NEAR) // LANES
    inner = (samples - NEAR) // LANES
    skip = NEAR // LANES
    total = delay_ref.shape[0]
    first = first_ref[0]
    lane = lax.broadcasted_iota(jnp.int32, (1, rows, LANES), 2)

    def ahead(shot):
        shot = jnp.clip(shot, 0, total - 2)
        return jnp.clip(SOURCE_SPACING + delay_ref[shot + 1] - delay_ref[shot], NEAR + 1, FAR - 1)

    def window(field, slot, start):
        column, rest = start // LANES, start % LANES
        wide = field[slot, pl.ds(column, inner + 1)]
        turned = pltpu.roll(
            wide.reshape((inner + 1) * rows, LANES), (LANES - rest) % LANES, 1
        ).reshape(inner + 1, rows, LANES)
        return jnp.where(lane < LANES - rest, turned[:-1], turned[1:])

    def blended(field, slot, shot):
        later = window(field, slot + 1, margin * LANES + NEAR - ahead(shot))
        earlier = window(field, slot - 1, margin * LANES + ahead(shot - 1))
        return later, earlier

    def fill(field, slot, values):
        blank = jnp.zeros((margin, rows, LANES), jnp.float32)
        field[slot, pl.ds(0, margin)] = blank
        field[slot, pl.ds(margin + columns, margin)] = blank
        for column in range(columns):
            field[slot, margin + column] = values(column)

    def cut(ref, shot):
        return lambda column: ref[shot, :, column * LANES : (column + 1) * LANES].astype(jnp.float32)

    for slot in range(2):
        fill(est32, slot, cut(before_ref, slot))
        fill(est32, shots + 2 + slot, cut(after_ref, slot))

    def load(shot, carry):
        fill(est32, shot + 2, cut(est_ref, shot))
        return carry

    lax.fori_loop(0, shots, load, 0)

    def residual(place, values):
        shot = first + place - 1
        inside = jnp.logical_and(shot >= 0, shot < total)
        later, earlier = blended(est32, place + 1, shot)
        power = jnp.zeros((rows, LANES), jnp.float32)
        cells = []
        for column in range(columns):
            cell = est32[place + 1, margin + column]
            if column >= skip:
                cell = cell + later[column - skip]
            if column < inner:
                cell = cell + earlier[column]
            cell = jnp.where(inside, values(column) - cell, 0.0)
            power = power + cell * cell
            cells.append(cell)
        fill(res32, place, lambda column: cells[column])
        return power

    residual(0, cut(before_ref, 2))
    residual(shots + 1, cut(after_ref, 2))

    def middle(shot, carry):
        power = residual(shot + 1, cut(obs_ref, shot))
        energy_ref[pl.ds(shot, 1), :] = jnp.sum(power, axis=0, keepdims=True)
        return carry

    lax.fori_loop(0, shots, middle, 0)

    def step(shot, carry):
        later, earlier = blended(res32, shot + 1, first + shot)
        for column in range(columns):
            cell = res32[shot + 1, margin + column]
            if column >= skip:
                cell = cell + later[column - skip]
            if column < inner:
                cell = cell + earlier[column]
            cell = est32[shot + 2, margin + column] + STEP * cell
            store(shot, column, cell.astype(jnp.bfloat16))
        return carry

    lax.fori_loop(0, shots, step, 0)


def spectra_kernel(
    first_ref, delay_ref, est_ref, obs_ref, before_ref, after_ref, table_ref, out_ref, energy_ref,
    est32, res32, stepped,
):
    shots, rows, samples = est_ref.shape
    blocks, _, _, width = out_ref.shape

    def store(shot, column, values):
        start = pl.multiple_of(shot * rows, rows)
        stepped[pl.ds(start, rows), column * LANES : (column + 1) * LANES] = values

    blend_into(
        first_ref, delay_ref, est_ref, obs_ref, before_ref, after_ref, energy_ref, est32, res32, store
    )
    group = min(shots, max(1, 256 // rows))

    def transform(part, carry):
        start = pl.multiple_of(part * (group * rows), group * rows)
        result = jnp.dot(
            stepped[pl.ds(start, group * rows), :], table_ref[...], preferred_element_type=jnp.float32
        ).astype(jnp.bfloat16)
        for block in range(blocks):
            out_ref[block, pl.ds(part * group, group)] = result[
                :, block * width : (block + 1) * width
            ].reshape(group, rows, width)
        return carry

    lax.fori_loop(0, shots // group, transform, 0)


def step_kernel(
    first_ref, delay_ref, est_ref, obs_ref, before_ref, after_ref, out_ref, energy_ref, est32, res32
):
    def store(shot, column, values):
        out_ref[shot, :, column * LANES : (column + 1) * LANES] = values

    blend_into(
        first_ref, delay_ref, est_ref, obs_ref, before_ref, after_ref, energy_ref, est32, res32, store
    )


def shots_kernel(spectra_ref, table_ref, level_ref, out_ref, wide, back):
    blocks, held, rows, width = spectra_ref.shape
    shots = blocks * held
    half = width // 2
    wide[...] = spectra_ref[...].reshape(shots * rows, width).astype(jnp.float32)
    level = level_ref[...]
    sign = jnp.where(
        lax.broadcasted_iota(jnp.int32, (1, width), 1) < half, jnp.float32(1.0), jnp.float32(-1.0)
    )

    def pair(index, carry):
        picks = [pl.ds(index * 2 + turn, shots, stride=rows) for turn in range(2)]
        block = jnp.concatenate([wide[pick, :] for pick in picks], axis=1).astype(jnp.bfloat16)
        both = jnp.dot(table_ref[...], block, preferred_element_type=jnp.float32)
        kept = []
        for turn in range(2):
            own = both[:, turn * width : (turn + 1) * width]
            wave = own[:shots] + sign * pltpu.roll(own[shots:], half, 1)
            power = wave * wave
            power = power + pltpu.roll(power, half, 1)
            factor = jnp.maximum(1.0 - level * lax.rsqrt(power), 0.0)
            kept.append((wave * factor).astype(jnp.bfloat16))
        both = jnp.dot(table_ref[...], jnp.concatenate(kept, axis=1), preferred_element_type=jnp.float32)
        for turn in range(2):
            own = both[:, turn * width : (turn + 1) * width]
            back[picks[turn], :] = own[:shots] - sign * pltpu.roll(own[shots:], half, 1)
        return carry

    lax.fori_loop(0, rows // 2, pair, 0)
    out_ref[...] = back[...].astype(jnp.bfloat16).reshape(out_ref.shape)


def update_kernel(*refs):
    restored_ref, table_ref, out_ref = refs[0], refs[1], refs[-1]
    blocks, held, rows, width = restored_ref.shape
    block = jnp.concatenate(
        [restored_ref[index].reshape(held * rows, width) for index in range(blocks)], axis=1
    )
    out_ref[...] = jnp.dot(block, table_ref[...], preferred_element_type=jnp.float32).reshape(out_ref.shape)


def whole(shape):
    return pl.BlockSpec(shape, lambda *_: (0,) * len(shape))


def blend_specs(shots, rows, samples, chunk):
    at = lambda *_: (0, chunk, 0)
    return [
        pl.BlockSpec(memory_space=pltpu.SMEM),
        pl.BlockSpec(memory_space=pltpu.SMEM),
        pl.BlockSpec((shots, rows, samples), at),
        pl.BlockSpec((shots, rows, samples), at),
        pl.BlockSpec((HALO, rows, samples), at),
        pl.BlockSpec((HALO, rows, samples), at),
    ]


def blend_scratch(shots, rows, samples):
    columns = (samples + 2 * (FAR - NEAR)) // LANES
    return [
        pltpu.VMEM((shots + 4, columns, rows, LANES), jnp.float32),
        pltpu.VMEM((shots + 2, columns, rows, LANES), jnp.float32),
    ]


PARAMS = pltpu.CompilerParams(vmem_limit_bytes=48 * 1024 * 1024)


def spectra_of(first, delays, fields, table, rows, chunk, blocks):
    shots, _, samples = fields[0].shape
    width = 2 * F // blocks
    return pl.pallas_call(
        spectra_kernel,
        grid=(1,),
        in_specs=blend_specs(shots, rows, samples, chunk) + [whole(table.shape)],
        out_specs=[whole((blocks, shots, rows, width)), whole((shots, LANES))],
        out_shape=[
            jax.ShapeDtypeStruct((blocks, shots, rows, width), jnp.bfloat16),
            jax.ShapeDtypeStruct((shots, LANES), jnp.float32),
        ],
        scratch_shapes=blend_scratch(shots, rows, samples)
        + [pltpu.VMEM((shots * rows, samples), jnp.bfloat16)],
        compiler_params=PARAMS,
        cost_estimate=pl.CostEstimate(
            flops=4 * F * shots * rows * samples,
            bytes_accessed=3 * 2 * shots * rows * samples + table.size * 2,
            transcendentals=0,
        ),
        name="spectra",
    )(first, delays, *fields, table)


def stepped_of(first, delays, fields, rows, chunk):
    shots, _, samples = fields[0].shape
    return pl.pallas_call(
        step_kernel,
        grid=(1,),
        in_specs=blend_specs(shots, rows, samples, chunk),
        out_specs=[whole((shots, rows, samples)), whole((shots, LANES))],
        out_shape=[
            jax.ShapeDtypeStruct((shots, rows, samples), jnp.bfloat16),
            jax.ShapeDtypeStruct((shots, LANES), jnp.float32),
        ],
        scratch_shapes=blend_scratch(shots, rows, samples),
        compiler_params=PARAMS,
        name="stepped",
    )(first, delays, *fields)


def shrunk_of(spectra, table, level):
    blocks, held, rows, width = spectra.shape
    shots = blocks * held
    return pl.pallas_call(
        shots_kernel,
        grid=(1,),
        in_specs=[whole(spectra.shape), whole(table.shape), whole(level.shape)],
        out_specs=whole(spectra.shape),
        out_shape=jax.ShapeDtypeStruct(spectra.shape, jnp.bfloat16),
        scratch_shapes=[pltpu.VMEM((shots * rows, width), jnp.float32)] * 2,
        compiler_params=PARAMS,
        cost_estimate=pl.CostEstimate(
            flops=8 * shots * shots * rows * width,
            bytes_accessed=2 * 2 * spectra.size + table.size * 2,
            transcendentals=spectra.size,
        ),
        name="shrink",
    )(spectra, table, level)


def updated_of(restored, table, chunk, receivers, onto):
    blocks, shots, rows, width = restored.shape
    samples = table.shape[1]
    group = min(shots, max(1, 256 // rows))
    in_specs = [
        pl.BlockSpec((blocks, group, rows, width), lambda step: (0, step, 0, 0)),
        whole(table.shape),
    ]
    operands = [restored, table]
    if onto is not None:
        in_specs.append(pl.BlockSpec(memory_space=pl.ANY))
        operands.append(onto)
    return pl.pallas_call(
        update_kernel,
        grid=(shots // group,),
        in_specs=in_specs,
        out_specs=pl.BlockSpec((group, rows, samples), lambda step: (step, chunk, 0)),
        out_shape=jax.ShapeDtypeStruct((shots, receivers, samples), jnp.float32),
        input_output_aliases={} if onto is None else {2: 0},
        compiler_params=PARAMS,
        cost_estimate=pl.CostEstimate(
            flops=4 * F * shots * rows * samples,
            bytes_accessed=2 * restored.size + 2 * table.size + 4 * shots * rows * samples,
            transcendentals=0,
        ),
        name="update",
    )(*operands)


def swapped(array):
    return lax.all_to_all(array, "shot", split_axis=0, concat_axis=0, tiled=True)


def spectral_by_einsum(stepped, forward, inverse, table, level, peers):
    shots, receivers, samples = stepped.shape
    total = table.shape[1]
    share = F // peers
    spectra = jnp.einsum(
        "srt,tdpf->dpfsr",
        stepped,
        forward.reshape(samples, peers, 2, share),
        preferred_element_type=jnp.float32,
    ).astype(jnp.bfloat16)
    mixed = swapped(spectra).transpose(1, 2, 0, 3, 4).reshape(2, share, total, receivers)
    cosine, sine = table[:total], table[total:]
    across = jnp.stack([jnp.stack([cosine, sine]), jnp.stack([-sine, cosine])])
    wave = jnp.einsum("pqks,qfsr->pfkr", across, mixed, preferred_element_type=jnp.float32)
    magnitude = jnp.sqrt(wave[0] * wave[0] + wave[1] * wave[1])
    bound = level[:, None, None]
    factor = jnp.maximum(magnitude - bound, 0.0) / jnp.maximum(magnitude, bound)
    shrunk = (wave * factor[None]).astype(jnp.bfloat16)
    back = jnp.stack([jnp.stack([cosine, -sine]), jnp.stack([sine, cosine])])
    restored = jnp.einsum(
        "pqks,qfkr->pfsr", back, shrunk, preferred_element_type=jnp.float32
    ).astype(jnp.bfloat16)
    restored = restored.reshape(2, share, peers, shots, receivers).transpose(2, 0, 1, 3, 4)
    return jnp.einsum(
        "dpft,dpfsr->srt",
        inverse.reshape(peers, 2, share, samples),
        swapped(restored),
        preferred_element_type=jnp.float32,
    )


def local(estimate, observed, random_source_delays, thresholds):
    shots, receivers, samples = estimate.shape
    peers = lax.axis_size("shot")
    rank = lax.axis_index("shot")
    total = random_source_delays.shape[0]
    share = F // peers
    rows = min(16, receivers)
    chunks = receivers // rows
    first = jnp.reshape(rank * shots, (1,)).astype(jnp.int32)
    up = [(i, i + 1) for i in range(peers - 1)]
    down = [(j, i) for i, j in up]
    tail = jnp.concatenate([estimate[shots - 2 :], observed[shots - 1 :]])
    head = jnp.concatenate([estimate[:2], observed[:1]])
    before = lax.ppermute(tail, "shot", up)
    after = lax.ppermute(head, "shot", down)
    fields = (estimate, observed, before, after)
    forward, inverse = (jnp.asarray(table) for table in time_tables(samples, peers))
    table = jnp.asarray(shot_table(total))
    level = lax.dynamic_slice_in_dim(thresholds, rank * share, share)
    energy = 0.0
    if (2 * share) % LANES == 0:
        levels = jnp.tile(level, 2)[None, :]
        updated = None
        for chunk in range(chunks):
            spectra, power = spectra_of(
                first, random_source_delays, fields, forward, rows, chunk, peers
            )
            energy = energy + power
            restored = shrunk_of(swapped(spectra), table, levels)
            updated = updated_of(swapped(restored), inverse, chunk, receivers, updated)
    else:
        parts = []
        for chunk in range(chunks):
            part, power = stepped_of(first, random_source_delays, fields, rows, chunk)
            energy = energy + power
            parts.append(part)
        updated = spectral_by_einsum(
            jnp.concatenate(parts, axis=1), forward, inverse, table, level, peers
        )
    misfit = lax.psum(jnp.sum(energy, axis=1), "patch") / (
        receivers * lax.axis_size("patch") * samples
    )
    return updated, misfit


def solution(mesh):
    in_specs = (P("shot", "patch", None), P("shot", "patch", None), P(), P())
    out_specs = (P("shot", "patch", None), P("shot"))
    return jax.shard_map(local, mesh=mesh, in_specs=in_specs, out_specs=out_specs, check_vma=False)
```

time: 1230 us -> 542 us (0.44); the launches traced: 1220 us -> 541 us
  local copies, waits for them, and re-layouts: 676 us -> 23 us
  Pallas kernels: 0 us -> 180 us
  waiting for transfers between devices: 347 us -> 244 us
  other arithmetic: 95.7 us -> 2.57 us
  matrix products: 62.4 us -> 0 us
  starting transfers between devices: 23 us -> 79.3 us
    gather x384 -> x0, local copies, waits for them, and re-layouts: 505 us -> none
    pallas_call x0 -> x24, Pallas kernels: none -> 180 us  [the longest x8 90.9 us: spectra_of(): pl.pallas_call(spectra_kernel, grid=(1,), in_specs=blend_specs(shots, row...]
    all_to_all x2 -> x16, waiting for transfers between devices: 346 us -> 239 us  [swapped(): lax.all_to_all(array, 'shot', split_axis=0, concat_axis=0, tiled=True)]
    all_to_all x2 -> x16, starting transfers between devices: 10.6 us -> 75.6 us  [swapped(): lax.all_to_all(array, 'shot', split_axis=0, concat_axis=0, tiled=True)]
    dot_general x4 -> x0, matrix products: 62.4 us -> none  [the longest x1 24.8 us: local(): jnp.einsum('srt,pft->pfsr', advanced_estimate, forward, preferred_element...]
    pad x2 -> x0, local copies, waits for them, and re-layouts: 46.3 us -> none  [delayed(): padded = jnp.pad(traces, ((0, 0), (length, length)))]
    concatenate x2, other arithmetic: 43.6 us -> 1.94 us  [the longest x1 0.99 us: local(): head = jnp.concatenate([estimate[:2], observed[:1]])]
    convert_element_type x2 -> x0, local copies, waits for them, and re-layouts: 33.2 us -> none  [the longest x1 21.1 us: local(): restored = jnp.einsum('pqks,qfsr->pfkr', back, shrunk, preferred_element_...]
  transfers between devices with their start and end apart: 6 -> 18, of which waited for: 3 -> 16; matrix products, arithmetic and copies ran while one was open for 2% -> 0% of each run, Pallas kernels for 0% -> 31%
where the time goes in v1:
time: 542 us; the launch traced here: 541 us
  waiting for transfers between devices  244 us (45%)
  Pallas kernels  180 us (33%)
  starting transfers between devices  79.3 us (15%)
  local copies, waits for them, and re-layouts  23 us (4%)
  blocking collectives  9.92 us (2%)
    all_to_all x16, waiting for transfers between devices, swapped(): lax.all_to_all(array, 'shot', split_axis=0, concat_axis=0, tiled=True)  239 us
    pallas_call x8, Pallas kernels, spectra_of(): pl.pallas_call(spectra_kernel, grid=(1,), in_specs=blend_specs(shots, row...  90.9 us
    all_to_all x16, starting transfers between devices, swapped(): lax.all_to_all(array, 'shot', split_axis=0, concat_axis=0, tiled=True)  75.6 us
    pallas_call x8, Pallas kernels, shrunk_of(): pl.pallas_call(shots_kernel, grid=(1,), in_specs=[whole(spectra.shape), w...  62.9 us
    pallas_call x8, Pallas kernels, updated_of(): pl.pallas_call(update_kernel, grid=(shots // group,), in_specs=in_specs,...  26.6 us
    unnamed x46, local copies, waits for them, and re-layouts  19.6 us
  transfers between devices with their start and end apart: 18, of which 16 were waited for; matrix products, arithmetic and copies ran while one was open for 0% of the time, Pallas kernels for 31%

profile of v1, /device:TPU:0, one launch (start us, length us, event | category | flops | bytes accessed | tf_op | source)
XLA Modules:
  0.0 540.6 jit_solution(5407724003915297166)
XLA Ops:
  0.6 1.4 fusion
  2.1 1.1 fusion.1
  4.1 2.4 collective-permute-start
  7.5 1.3 collective-permute-start.1
  8.8 5.3 collective-permute-done.1.after_ref
  14.2 1.6 copy-done.1
  16.4 11.4 %spectra.15 = (bf16[8,32,16,128]{3,2,1,0:T(8,128)(2,1)S(1)}, f32[32,128]{1,0:T(8,128)S(1)}) custom-call(s32[1]{0:T(128)} %bitcast.first_ref, s32[256]{0:T(256)S(1)} %copy-done.21, bf16[32,128,1024]{2,1,0:T(8,128)(2,1)} %est_ref.15, bf16[32,128,1024]{2,1,0:T(8,128)(2,1)} %obs_ref.15, bf16[3,128,1024]{2,1,0:T(8,128)(2,1)S(1)} %collective-permute-done.before_ref, ...), custom_call_target="tpu_custom_call" | custom-call | flops 1073741824 | bytes 5242880 | tf_op jit(solution)/shard_map/spectra/pallas_call | solution.py:253
  28.8 13.1 %all-to-all-start.14 = ((bf16[8,32,16,128]{3,2,1,0:T(8,128)(2,1)}), bf16[8,32,16,128]{3,2,1,0:T(8,128)(2,1)}, u32[]{:S(2)}, u32[]{:S(2)}) async-start(bf16[8,32,16,128]{3,2,1,0:T(8,128)(2,1)} %copy-done.20), calls=%async_computation.14 | async-start | bytes 2097152 | tf_op jit(solution)/shard_map/all_to_all | solution.py:341
  41.9 11.4 %spectra.14 = (bf16[8,32,16,128]{3,2,1,0:T(8,128)(2,1)S(1)}, f32[32,128]{1,0:T(8,128)S(1)}) custom-call(s32[1]{0:T(128)} %bitcast.first_ref, s32[256]{0:T(256)S(1)} %copy-done.21, bf16[32,128,1024]{2,1,0:T(8,128)(2,1)} %est_ref.15, bf16[32,128,1024]{2,1,0:T(8,128)(2,1)} %obs_ref.15, bf16[3,128,1024]{2,1,0:T(8,128)(2,1)S(1)} %collective-permute-done.before_ref, ...), custom_call_target="tpu_custom_call" | custom-call | flops 1073741824 | bytes 5242880 | tf_op jit(solution)/shard_map/spectra/pallas_call | solution.py:253
  54.2 14.5 %all-to-all-done.14.spectra_ref = bf16[8,32,16,128]{3,2,1,0:T(8,128)(2,1)} async-done(((bf16[8,32,16,128]{3,2,1,0:T(8,128)(2,1)}), bf16[8,32,16,128]{3,2,1,0:T(8,128)(2,1)}, u32[]{:S(2)}, u32[]{:S(2)}) %all-to-all-start.14) | async-done | bytes 1048608 | tf_op jit(solution)/shard_map/all_to_all | solution.py:341
  68.8 4.2 all-to-all-start.12
  73.0 11.4 %spectra.13 = (bf16[8,32,16,128]{3,2,1,0:T(8,128)(2,1)S(1)}, f32[32,128]{1,0:T(8,128)S(1)}) custom-call(s32[1]{0:T(128)} %bitcast.first_ref, s32[256]{0:T(256)S(1)} %copy-done.21, bf16[32,128,1024]{2,1,0:T(8,128)(2,1)} %est_ref.15, bf16[32,128,1024]{2,1,0:T(8,128)(2,1)} %obs_ref.15, bf16[3,128,1024]{2,1,0:T(8,128)(2,1)S(1)} %collective-permute-done.before_ref, ...), custom_call_target="tpu_custom_call" | custom-call | flops 1073741824 | bytes 5242880 | tf_op jit(solution)/shard_map/spectra/pallas_call | solution.py:253
  85.4 14.2 %all-to-all-done.12.spectra_ref = bf16[8,32,16,128]{3,2,1,0:T(8,128)(2,1)} async-done(((bf16[8,32,16,128]{3,2,1,0:T(8,128)(2,1)}), bf16[8,32,16,128]{3,2,1,0:T(8,128)(2,1)}, u32[]{:S(2)}, u32[]{:S(2)}) %all-to-all-start.12) | async-done | bytes 1048608 | tf_op jit(solution)/shard_map/all_to_all | solution.py:341
  99.6 4.3 all-to-all-start.10
  103.9 11.4 %spectra.12 = (bf16[8,32,16,128]{3,2,1,0:T(8,128)(2,1)S(1)}, f32[32,128]{1,0:T(8,128)S(1)}) custom-call(s32[1]{0:T(128)} %bitcast.first_ref, s32[256]{0:T(256)S(1)} %copy-done.21, bf16[32,128,1024]{2,1,0:T(8,128)(2,1)} %est_ref.15, bf16[32,128,1024]{2,1,0:T(8,128)(2,1)} %obs_ref.15, bf16[3,128,1024]{2,1,0:T(8,128)(2,1)S(1)} %collective-permute-done.before_ref, ...), custom_call_target="tpu_custom_call" | custom-call | flops 1073741824 | bytes 5242880 | tf_op jit(solution)/shard_map/spectra/pallas_call | solution.py:253
  116.2 14.2 %all-to-all-done.10.spectra_ref = bf16[8,32,16,128]{3,2,1,0:T(8,128)(2,1)} async-done(((bf16[8,32,16,128]{3,2,1,0:T(8,128)(2,1)}), bf16[8,32,16,128]{3,2,1,0:T(8,128)(2,1)}, u32[]{:S(2)}, u32[]{:S(2)}) %all-to-all-start.10) | async-done | bytes 1048608 | tf_op jit(solution)/shard_map/all_to_all | solution.py:341
  130.5 4.2 all-to-all-start.8
  134.7 11.4 %spectra.11 = (bf16[8,32,16,128]{3,2,1,0:T(8,128)(2,1)S(1)}, f32[32,128]{1,0:T(8,128)S(1)}) custom-call(s32[1]{0:T(128)} %bitcast.first_ref, s32[256]{0:T(256)S(1)} %copy-done.21, bf16[32,128,1024]{2,1,0:T(8,128)(2,1)} %est_ref.15, bf16[32,128,1024]{2,1,0:T(8,128)(2,1)} %obs_ref.15, bf16[3,128,1024]{2,1,0:T(8,128)(2,1)S(1)} %collective-permute-done.before_ref, ...), custom_call_target="tpu_custom_call" | custom-call | flops 1073741824 | bytes 5242880 | tf_op jit(solution)/shard_map/spectra/pallas_call | solution.py:253
  147.1 14.2 %all-to-all-done.8.spectra_ref = bf16[8,32,16,128]{3,2,1,0:T(8,128)(2,1)} async-done(((bf16[8,32,16,128]{3,2,1,0:T(8,128)(2,1)}), bf16[8,32,16,128]{3,2,1,0:T(8,128)(2,1)}, u32[]{:S(2)}, u32[]{:S(2)}) %all-to-all-start.8) | async-done | bytes 1048608 | tf_op jit(solution)/shard_map/all_to_all | solution.py:341
  161.3 4.2 all-to-all-start.6
  165.6 11.4 %spectra.10 = (bf16[8,32,16,128]{3,2,1,0:T(8,128)(2,1)S(1)}, f32[32,128]{1,0:T(8,128)S(1)}) custom-call(s32[1]{0:T(128)} %bitcast.first_ref, s32[256]{0:T(256)S(1)} %copy-done.21, bf16[32,128,1024]{2,1,0:T(8,128)(2,1)} %est_ref.15, bf16[32,128,1024]{2,1,0:T(8,128)(2,1)} %obs_ref.15, bf16[3,128,1024]{2,1,0:T(8,128)(2,1)S(1)} %collective-permute-done.before_ref, ...), custom_call_target="tpu_custom_call" | custom-call | flops 1073741824 | bytes 5242880 | tf_op jit(solution)/shard_map/spectra/pallas_call | solution.py:253
  177.9 14.2 %all-to-all-done.6.spectra_ref = bf16[8,32,16,128]{3,2,1,0:T(8,128)(2,1)} async-done(((bf16[8,32,16,128]{3,2,1,0:T(8,128)(2,1)}), bf16[8,32,16,128]{3,2,1,0:T(8,128)(2,1)}, u32[]{:S(2)}, u32[]{:S(2)}) %all-to-all-start.6) | async-done | bytes 1048608 | tf_op jit(solution)/shard_map/all_to_all | solution.py:341
  192.2 4.2 all-to-all-start.4
  196.4 11.4 %spectra.9 = (bf16[8,32,16,128]{3,2,1,0:T(8,128)(2,1)S(1)}, f32[32,128]{1,0:T(8,128)S(1)}) custom-call(s32[1]{0:T(128)} %bitcast.first_ref, s32[256]{0:T(256)S(1)} %copy-done.21, bf16[32,128,1024]{2,1,0:T(8,128)(2,1)} %est_ref.15, bf16[32,128,1024]{2,1,0:T(8,128)(2,1)} %obs_ref.15, bf16[3,128,1024]{2,1,0:T(8,128)(2,1)S(1)} %collective-permute-done.before_ref, ...), custom_call_target="tpu_custom_call" | custom-call | flops 1073741824 | bytes 5242880 | tf_op jit(solution)/shard_map/spectra/pallas_call | solution.py:253
  207.8 1.1 copy-done.7
  208.9 14.1 %all-to-all-done.4.spectra_ref = bf16[8,32,16,128]{3,2,1,0:T(8,128)(2,1)} async-done(((bf16[8,32,16,128]{3,2,1,0:T(8,128)(2,1)}), bf16[8,32,16,128]{3,2,1,0:T(8,128)(2,1)}, u32[]{:S(2)}, u32[]{:S(2)}) %all-to-all-start.4) | async-done | bytes 1048608 | tf_op jit(solution)/shard_map/all_to_all | solution.py:341
  223.0 4.2 all-to-all-start.2
  227.3 11.4 %spectra.8 = (bf16[8,32,16,128]{3,2,1,0:T(8,128)(2,1)S(1)}, f32[32,128]{1,0:T(8,128)S(1)}) custom-call(s32[1]{0:T(128)} %bitcast.first_ref, s32[256]{0:T(256)S(1)} %copy-done.21, bf16[32,128,1024]{2,1,0:T(8,128)(2,1)} %est_ref.15, bf16[32,128,1024]{2,1,0:T(8,128)(2,1)} %obs_ref.15, bf16[3,128,1024]{2,1,0:T(8,128)(2,1)S(1)} %collective-permute-done.before_ref, ...), custom_call_target="tpu_custom_call" | custom-call | flops 1073741824 | bytes 5242880 | tf_op jit(solution)/shard_map/spectra/pallas_call | solution.py:253
  239.6 14.2 %all-to-all-done.2.spectra_ref = bf16[8,32,16,128]{3,2,1,0:T(8,128)(2,1)} async-done(((bf16[8,32,16,128]{3,2,1,0:T(8,128)(2,1)}), bf16[8,32,16,128]{3,2,1,0:T(8,128)(2,1)}, u32[]{:S(2)}, u32[]{:S(2)}) %all-to-all-start.2) | async-done | bytes 1048608 | tf_op jit(solution)/shard_map/all_to_all | solution.py:341
  253.9 3.6 all-to-all-start
  258.3 8.0 %shrink.15 = bf16[8,32,16,128]{3,2,1,0:T(8,128)(2,1)S(1)} custom-call(bf16[8,32,16,128]{3,2,1,0:T(8,128)(2,1)} %all-to-all-done.14.spectra_ref, bf16[512,256]{1,0:T(8,128)(2,1)S(1)} %copy-done.22, f32[1,128]{1,0:T(1,128)S(1)} %broadcast_in_dim_tile.3.level_ref), custom_call_target="tpu_custom_call" | custom-call | flops 1073741824 | bytes 2359296 | tf_op jit(solution)/shard_map/shrink/pallas_call | solution.py:294
  267.4 16.6 %all-to-all-done.spectra_ref = bf16[8,32,16,128]{3,2,1,0:T(8,128)(2,1)S(1)} async-done(((bf16[8,32,16,128]{3,2,1,0:T(8,128)(2,1)}), bf16[8,32,16,128]{3,2,1,0:T(8,128)(2,1)S(1)}, u32[]{:S(2)}, u32[]{:S(2)}) %all-to-all-start) | async-done | bytes 1048608 | tf_op jit(solution)/shard_map/all_to_all | solution.py:341
  283.9 3.6 all-to-all-start.15
  287.5 8.0 %shrink.14 = bf16[8,32,16,128]{3,2,1,0:T(8,128)(2,1)S(1)} custom-call(bf16[8,32,16,128]{3,2,1,0:T(8,128)(2,1)} %all-to-all-done.12.spectra_ref, bf16[512,256]{1,0:T(8,128)(2,1)S(1)} %copy-done.22, f32[1,128]{1,0:T(1,128)S(1)} %broadcast_in_dim_tile.3.level_ref), custom_call_target="tpu_custom_call" | custom-call | flops 1073741824 | bytes 2359296 | tf_op jit(solution)/shard_map/shrink/pallas_call | solution.py:294
  296.5 17.5 %all-to-all-done.15.refs_0_ = bf16[8,32,16,128]{3,2,1,0:T(8,128)(2,1)S(1)} async-done(((bf16[8,32,16,128]{3,2,1,0:T(8,128)(2,1)}), bf16[8,32,16,128]{3,2,1,0:T(8,128)(2,1)S(1)}, u32[]{:S(2)}, u32[]{:S(2)}) %all-to-all-start.15) | async-done | bytes 1048608 | tf_op jit(solution)/shard_map/all_to_all | solution.py:341
  314.0 4.2 all-to-all-start.13
  318.3 8.0 %shrink.13 = bf16[8,32,16,128]{3,2,1,0:T(8,128)(2,1)S(1)} custom-call(bf16[8,32,16,128]{3,2,1,0:T(8,128)(2,1)} %all-to-all-done.10.spectra_ref, bf16[512,256]{1,0:T(8,128)(2,1)S(1)} %copy-done.22, f32[1,128]{1,0:T(1,128)S(1)} %broadcast_in_dim_tile.3.level_ref), custom_call_target="tpu_custom_call" | custom-call | flops 1073741824 | bytes 2359296 | tf_op jit(solution)/shard_map/shrink/pallas_call | solution.py:294
  327.4 17.5 %all-to-all-done.13.refs_0_ = bf16[8,32,16,128]{3,2,1,0:T(8,128)(2,1)} async-done(((bf16[8,32,16,128]{3,2,1,0:T(8,128)(2,1)}), bf16[8,32,16,128]{3,2,1,0:T(8,128)(2,1)}, u32[]{:S(2)}, u32[]{:S(2)}) %all-to-all-start.13) | async-done | bytes 1048608 | tf_op jit(solution)/shard_map/all_to_all | solution.py:341
  344.9 4.4 all-to-all-start.11
  349.3 8.0 %shrink.12 = bf16[8,32,16,128]{3,2,1,0:T(8,128)(2,1)S(1)} custom-call(bf16[8,32,16,128]{3,2,1,0:T(8,128)(2,1)} %all-to-all-done.8.spectra_ref, bf16[512,256]{1,0:T(8,128)(2,1)S(1)} %copy-done.22, f32[1,128]{1,0:T(1,128)S(1)} %broadcast_in_dim_tile.3.level_ref), custom_call_target="tpu_custom_call" | custom-call | flops 1073741824 | bytes 2359296 | tf_op jit(solution)/shard_map/shrink/pallas_call | solution.py:294
  358.3 17.4 %all-to-all-done.11.refs_0_ = bf16[8,32,16,128]{3,2,1,0:T(8,128)(2,1)} async-done(((bf16[8,32,16,128]{3,2,1,0:T(8,128)(2,1)}), bf16[8,32,16,128]{3,2,1,0:T(8,128)(2,1)}, u32[]{:S(2)}, u32[]{:S(2)}) %all-to-all-start.11) | async-done | bytes 1048608 | tf_op jit(solution)/shard_map/all_to_all | solution.py:341
  375.7 4.2 all-to-all-start.9
  380.0 8.0 %shrink.11 = bf16[8,32,16,128]{3,2,1,0:T(8,128)(2,1)S(1)} custom-call(bf16[8,32,16,128]{3,2,1,0:T(8,128)(2,1)} %all-to-all-done.6.spectra_ref, bf16[512,256]{1,0:T(8,128)(2,1)S(1)} %copy-done.22, f32[1,128]{1,0:T(1,128)S(1)} %broadcast_in_dim_tile.3.level_ref), custom_call_target="tpu_custom_call" | custom-call | flops 1073741824 | bytes 2359296 | tf_op jit(solution)/shard_map/shrink/pallas_call | solution.py:294
  389.1 17.5 %all-to-all-done.9.refs_0_ = bf16[8,32,16,128]{3,2,1,0:T(8,128)(2,1)} async-done(((bf16[8,32,16,128]{3,2,1,0:T(8,128)(2,1)}), bf16[8,32,16,128]{3,2,1,0:T(8,128)(2,1)}, u32[]{:S(2)}, u32[]{:S(2)}) %all-to-all-start.9) | async-done | bytes 1048608 | tf_op jit(solution)/shard_map/all_to_all | solution.py:341
  406.6 4.2 all-to-all-start.7
  410.8 8.0 %shrink.10 = bf16[8,32,16,128]{3,2,1,0:T(8,128)(2,1)S(1)} custom-call(bf16[8,32,16,128]{3,2,1,0:T(8,128)(2,1)} %all-to-all-done.4.spectra_ref, bf16[512,256]{1,0:T(8,128)(2,1)S(1)} %copy-done.22, f32[1,128]{1,0:T(1,128)S(1)} %broadcast_in_dim_tile.3.level_ref), custom_call_target="tpu_custom_call" | custom-call | flops 1073741824 | bytes 2359296 | tf_op jit(solution)/shard_map/shrink/pallas_call | solution.py:294
  419.8 17.6 %all-to-all-done.7.refs_0_ = bf16[8,32,16,128]{3,2,1,0:T(8,128)(2,1)} async-done(((bf16[8,32,16,128]{3,2,1,0:T(8,128)(2,1)}), bf16[8,32,16,128]{3,2,1,0:T(8,128)(2,1)}, u32[]{:S(2)}, u32[]{:S(2)}) %all-to-all-start.7) | async-done | bytes 1048608 | tf_op jit(solution)/shard_map/all_to_all | solution.py:341
  437.4 4.2 all-to-all-start.5
  441.7 8.0 %shrink.9 = bf16[8,32,16,128]{3,2,1,0:T(8,128)(2,1)S(1)} custom-call(bf16[8,32,16,128]{3,2,1,0:T(8,128)(2,1)} %all-to-all-done.2.spectra_ref, bf16[512,256]{1,0:T(8,128)(2,1)S(1)} %copy-done.22, f32[1,128]{1,0:T(1,128)S(1)} %broadcast_in_dim_tile.3.level_ref), custom_call_target="tpu_custom_call" | custom-call | flops 1073741824 | bytes 2359296 | tf_op jit(solution)/shard_map/shrink/pallas_call | solution.py:294
  450.7 17.5 %all-to-all-done.5.refs_0_ = bf16[8,32,16,128]{3,2,1,0:T(8,128)(2,1)} async-done(((bf16[8,32,16,128]{3,2,1,0:T(8,128)(2,1)}), bf16[8,32,16,128]{3,2,1,0:T(8,128)(2,1)}, u32[]{:S(2)}, u32[]{:S(2)}) %all-to-all-start.5) | async-done | bytes 1048608 | tf_op jit(solution)/shard_map/all_to_all | solution.py:341
  468.2 4.2 all-to-all-start.3
  472.5 1.2 copy-done.4
  473.7 6.8 %shrink.8 = bf16[8,32,16,128]{3,2,1,0:T(8,128)(2,1)S(1)} custom-call(bf16[8,32,16,128]{3,2,1,0:T(8,128)(2,1)S(1)} %copy-done.4, bf16[512,256]{1,0:T(8,128)(2,1)S(1)} %copy-done.22, f32[1,128]{1,0:T(1,128)S(1)} %broadcast_in_dim_tile.3.level_ref), custom_call_target="tpu_custom_call" | custom-call | flops 1073741824 | bytes 2359296 | tf_op jit(solution)/shard_map/shrink/pallas_call | solution.py:294
  481.5 17.6 %all-to-all-done.3.refs_0_ = bf16[8,32,16,128]{3,2,1,0:T(8,128)(2,1)} async-done(((bf16[8,32,16,128]{3,2,1,0:T(8,128)(2,1)}), bf16[8,32,16,128]{3,2,1,0:T(8,128)(2,1)}, u32[]{:S(2)}, u32[]{:S(2)}) %all-to-all-start.3) | async-done | bytes 1048608 | tf_op jit(solution)/shard_map/all_to_all | solution.py:341
  499.1 4.3 all-to-all-start.1
  503.5 9.9 %psum.7 = f32[32]{0:T(128)S(1)} all-reduce(f32[32]{0:T(128)S(1)} %add_reduce_fusion), channel_id=1, replica_groups=mesh['patch'=4,'shot'=8] {'patch'}, use_global_device_ids=true, to_apply=%region_1.0 | all-reduce | flops 32 | bytes 256 | tf_op jit(solution)/shard_map/psum | solution.py:414
  513.9 2.5 update.8.refs_2_
  516.4 3.4 update.9.refs_2_
  519.9 3.4 update.10.refs_2_
  523.3 3.4 update.11.refs_2_
  526.8 3.4 update.12.refs_2_
  530.2 3.4 update.13.refs_2_
  533.7 3.4 update.14.refs_2_
  537.1 3.4 update.15
  (52 shorter events, 19.2 us)
Async XLA Ops:
  0.6 41.3 %copy-start.2 = (bf16[1024,1024]{1,0:T(8,128)(2,1)S(1)}, bf16[1024,1024]{1,0:T(8,128)(2,1)}, u32[]{:S(2)}) copy-start(bf16[1024,1024]{1,0:T(8,128)(2,1)} %constant.23.clone.table_ref) | copy-start | bytes 6291460
  4.1 4.7 collective-permute-start
  7.5 6.7 %collective-permute-start.1 = (bf16[3,128,1024]{2,1,0:T(8,128)(2,1)}, bf16[3,128,1024]{2,1,0:T(8,128)(2,1)}, u32[]{:S(2)}, u32[]{:S(2)}) collective-permute-start(bf16[3,128,1024]{2,1,0:T(8,128)(2,1)} %pad_maximum_fusion.1), channel_id=1, source_target_pairs={{1,0},{2,1},{3,2},{4,3},{5,4},{6,5},{7,6},{9,8},{10,9},{11,10},{12... | collective-permute-start | bytes 2359304 | tf_op jit(solution)/shard_map/ppermute | solution.py:389
  14.2 1.6 copy-start.1
  15.7 0.7 copy-start.21
  27.8 1.0 copy-start.20
  28.8 40.0 %all-to-all-start.14 = ((bf16[8,32,16,128]{3,2,1,0:T(8,128)(2,1)}), bf16[8,32,16,128]{3,2,1,0:T(8,128)(2,1)}, u32[]{:S(2)}, u32[]{:S(2)}) async-start(bf16[8,32,16,128]{3,2,1,0:T(8,128)(2,1)} %copy-done.20), calls=%async_computation.14 | async-start | bytes 2097152 | tf_op jit(solution)/shard_map/all_to_all | solution.py:341
  53.3 1.0 copy-start.8
  68.8 30.8 %all-to-all-start.12 = ((bf16[8,32,16,128]{3,2,1,0:T(8,128)(2,1)}), bf16[8,32,16,128]{3,2,1,0:T(8,128)(2,1)}, u32[]{:S(2)}, u32[]{:S(2)}) async-start(bf16[8,32,16,128]{3,2,1,0:T(8,128)(2,1)} %copy-done.8), calls=%async_computation.12 | async-start | bytes 2097152 | tf_op jit(solution)/shard_map/all_to_all | solution.py:341
  84.4 1.0 copy-start.9
  99.6 30.9 %all-to-all-start.10 = ((bf16[8,32,16,128]{3,2,1,0:T(8,128)(2,1)}), bf16[8,32,16,128]{3,2,1,0:T(8,128)(2,1)}, u32[]{:S(2)}, u32[]{:S(2)}) async-start(bf16[8,32,16,128]{3,2,1,0:T(8,128)(2,1)} %copy-done.9), calls=%async_computation.10 | async-start | bytes 2097152 | tf_op jit(solution)/shard_map/all_to_all | solution.py:341
  115.3 1.0 copy-start.10
  130.5 30.8 %all-to-all-start.8 = ((bf16[8,32,16,128]{3,2,1,0:T(8,128)(2,1)}), bf16[8,32,16,128]{3,2,1,0:T(8,128)(2,1)}, u32[]{:S(2)}, u32[]{:S(2)}) async-start(bf16[8,32,16,128]{3,2,1,0:T(8,128)(2,1)} %copy-done.10), calls=%async_computation.8 | async-start | bytes 2097152 | tf_op jit(solution)/shard_map/all_to_all | solution.py:341
  146.1 1.0 copy-start.11
  161.3 30.8 %all-to-all-start.6 = ((bf16[8,32,16,128]{3,2,1,0:T(8,128)(2,1)}), bf16[8,32,16,128]{3,2,1,0:T(8,128)(2,1)}, u32[]{:S(2)}, u32[]{:S(2)}) async-start(bf16[8,32,16,128]{3,2,1,0:T(8,128)(2,1)} %copy-done.11), calls=%async_computation.6 | async-start | bytes 2097152 | tf_op jit(solution)/shard_map/all_to_all | solution.py:341
  176.9 1.0 copy-start.12
  192.2 30.8 %all-to-all-start.4 = ((bf16[8,32,16,128]{3,2,1,0:T(8,128)(2,1)}), bf16[8,32,16,128]{3,2,1,0:T(8,128)(2,1)}, u32[]{:S(2)}, u32[]{:S(2)}) async-start(bf16[8,32,16,128]{3,2,1,0:T(8,128)(2,1)} %copy-done.12), calls=%async_computation.4 | async-start | bytes 2097152 | tf_op jit(solution)/shard_map/all_to_all | solution.py:341
  207.8 1.1 copy-start.7
  208.9 49.4 %copy-start.22 = (bf16[512,256]{1,0:T(8,128)(2,1)S(1)}, bf16[512,256]{1,0:T(8,128)(2,1)}, u32[]{:S(2)}) copy-start(bf16[512,256]{1,0:T(8,128)(2,1)} %constant.25.clone.table_ref) | copy-start | bytes 786436
  223.0 30.8 %all-to-all-start.2 = ((bf16[8,32,16,128]{3,2,1,0:T(8,128)(2,1)}), bf16[8,32,16,128]{3,2,1,0:T(8,128)(2,1)}, u32[]{:S(2)}, u32[]{:S(2)}) async-start(bf16[8,32,16,128]{3,2,1,0:T(8,128)(2,1)} %copy-done.7), calls=%async_computation.2 | async-start | bytes 2097152 | tf_op jit(solution)/shard_map/all_to_all | solution.py:341
  238.6 1.0 copy-start.6
  253.9 30.1 %all-to-all-start = ((bf16[8,32,16,128]{3,2,1,0:T(8,128)(2,1)}), bf16[8,32,16,128]{3,2,1,0:T(8,128)(2,1)S(1)}, u32[]{:S(2)}, u32[]{:S(2)}) async-start(bf16[8,32,16,128]{3,2,1,0:T(8,128)(2,1)} %copy-done.6), calls=%async_computation | async-start | bytes 2097152 | tf_op jit(solution)/shard_map/all_to_all | solution.py:341
  266.3 1.1 copy-start.14
  283.9 34.3 %copy-start.3 = (bf16[8,32,16,128]{3,2,1,0:T(8,128)(2,1)}, bf16[8,32,16,128]{3,2,1,0:T(8,128)(2,1)S(1)}, u32[]{:S(2)}) copy-start(bf16[8,32,16,128]{3,2,1,0:T(8,128)(2,1)S(1)} %all-to-all-done.spectra_ref) | copy-start | bytes 3145732
  283.9 30.1 %all-to-all-start.15 = ((bf16[8,32,16,128]{3,2,1,0:T(8,128)(2,1)}), bf16[8,32,16,128]{3,2,1,0:T(8,128)(2,1)S(1)}, u32[]{:S(2)}, u32[]{:S(2)}) async-start(bf16[8,32,16,128]{3,2,1,0:T(8,128)(2,1)} %copy-done.14), calls=%async_computation.15 | async-start | bytes 2097152 | tf_op jit(solution)/shard_map/all_to_all | solution.py:341
  295.5 1.0 copy-start.15
  314.0 30.8 %all-to-all-start.13 = ((bf16[8,32,16,128]{3,2,1,0:T(8,128)(2,1)}), bf16[8,32,16,128]{3,2,1,0:T(8,128)(2,1)}, u32[]{:S(2)}, u32[]{:S(2)}) async-start(bf16[8,32,16,128]{3,2,1,0:T(8,128)(2,1)} %copy-done.15), calls=%async_computation.13 | async-start | bytes 2097152 | tf_op jit(solution)/shard_map/all_to_all | solution.py:341
  326.3 1.1 copy-start.16
  327.4 186.6 %copy-start = (bf16[1024,1024]{1,0:T(8,128)(2,1)S(1)}, bf16[1024,1024]{1,0:T(8,128)(2,1)}, u32[]{:S(2)}) copy-start(bf16[1024,1024]{1,0:T(8,128)(2,1)} %constant.24.clone.refs_1_) | copy-start | bytes 6291460
  344.9 30.9 %all-to-all-start.11 = ((bf16[8,32,16,128]{3,2,1,0:T(8,128)(2,1)}), bf16[8,32,16,128]{3,2,1,0:T(8,128)(2,1)}, u32[]{:S(2)}, u32[]{:S(2)}) async-start(bf16[8,32,16,128]{3,2,1,0:T(8,128)(2,1)} %copy-done.16), calls=%async_computation.11 | async-start | bytes 2097152 | tf_op jit(solution)/shard_map/all_to_all | solution.py:341
  357.3 1.0 copy-start.17
  375.7 30.8 %all-to-all-start.9 = ((bf16[8,32,16,128]{3,2,1,0:T(8,128)(2,1)}), bf16[8,32,16,128]{3,2,1,0:T(8,128)(2,1)}, u32[]{:S(2)}, u32[]{:S(2)}) async-start(bf16[8,32,16,128]{3,2,1,0:T(8,128)(2,1)} %copy-done.17), calls=%async_computation.9 | async-start | bytes 2097152 | tf_op jit(solution)/shard_map/all_to_all | solution.py:341
  388.0 1.1 copy-start.18
  406.6 30.8 %all-to-all-start.7 = ((bf16[8,32,16,128]{3,2,1,0:T(8,128)(2,1)}), bf16[8,32,16,128]{3,2,1,0:T(8,128)(2,1)}, u32[]{:S(2)}, u32[]{:S(2)}) async-start(bf16[8,32,16,128]{3,2,1,0:T(8,128)(2,1)} %copy-done.18), calls=%async_computation.7 | async-start | bytes 2097152 | tf_op jit(solution)/shard_map/all_to_all | solution.py:341
  418.8 1.0 copy-start.19
  437.4 30.8 %all-to-all-start.5 = ((bf16[8,32,16,128]{3,2,1,0:T(8,128)(2,1)}), bf16[8,32,16,128]{3,2,1,0:T(8,128)(2,1)}, u32[]{:S(2)}, u32[]{:S(2)}) async-start(bf16[8,32,16,128]{3,2,1,0:T(8,128)(2,1)} %copy-done.19), calls=%async_computation.5 | async-start | bytes 2097152 | tf_op jit(solution)/shard_map/all_to_all | solution.py:341
  449.7 1.1 copy-start.13
  468.2 30.8 %all-to-all-start.3 = ((bf16[8,32,16,128]{3,2,1,0:T(8,128)(2,1)}), bf16[8,32,16,128]{3,2,1,0:T(8,128)(2,1)}, u32[]{:S(2)}, u32[]{:S(2)}) async-start(bf16[8,32,16,128]{3,2,1,0:T(8,128)(2,1)} %copy-done.13), calls=%async_computation.3 | async-start | bytes 2097152 | tf_op jit(solution)/shard_map/all_to_all | solution.py:341
  472.5 1.2 copy-start.4
  480.5 1.0 copy-start.5
  499.1 38.0 %all-to-all-start.1 = ((bf16[8,32,16,128]{3,2,1,0:T(8,128)(2,1)}), bf16[8,32,16,128]{3,2,1,0:T(8,128)(2,1)}, u32[]{:S(2)}, u32[]{:S(2)}) async-start(bf16[8,32,16,128]{3,2,1,0:T(8,128)(2,1)} %copy-done.5), calls=%async_computation.1 | async-start | bytes 2097152 | tf_op jit(solution)/shard_map/all_to_all | solution.py:341

commit v2 on v1

--- a/solution.py
+++ b/solution.py
@@ -139,11 +139,11 @@
 
 
 def spectra_kernel(
-    first_ref, delay_ref, est_ref, obs_ref, before_ref, after_ref, table_ref, out_ref, energy_ref,
-    est32, res32, stepped,
+    first_ref, delay_ref, est_ref, obs_ref, before_ref, after_ref, table_ref, _, *refs
 ):
+    *out_refs, energy_ref, est32, res32, stepped = refs
     shots, rows, samples = est_ref.shape
-    blocks, _, _, width = out_ref.shape
+    width = out_refs[0].shape[2]
 
     def store(shot, column, values):
         start = pl.multiple_of(shot * rows, rows)
@@ -159,9 +159,9 @@
         result = jnp.dot(
             stepped[pl.ds(start, group * rows), :], table_ref[...], preferred_element_type=jnp.float32
         ).astype(jnp.bfloat16)
-        for block in range(blocks):
-            out_ref[block, pl.ds(part * group, group)] = result[
-                :, block * width : (block + 1) * width
+        for slot, out_ref in enumerate(out_refs):
+            out_ref[pl.ds(part * group, group)] = result[
+                :, slot * width : (slot + 1) * width
             ].reshape(group, rows, width)
         return carry
 
@@ -179,11 +179,16 @@
     )
 
 
-def shots_kernel(spectra_ref, table_ref, level_ref, out_ref, wide, back):
-    blocks, held, rows, width = spectra_ref.shape
-    shots = blocks * held
+def shots_kernel(across_ref, back_ref, level_ref, _, *refs):
+    peers = (len(refs) - 2) // 2
+    spectra_refs, out_refs, (wide, back) = refs[:peers], refs[peers : 2 * peers], refs[2 * peers :]
+    held, rows, width = spectra_refs[0].shape
+    shots = peers * held
     half = width // 2
-    wide[...] = spectra_ref[...].reshape(shots * rows, width).astype(jnp.float32)
+    for slot, ref in enumerate(spectra_refs):
+        wide[pl.ds(slot * held * rows, held * rows), :] = (
+            ref[...].reshape(held * rows, width).astype(jnp.float32)
+        )
     level = level_ref[...]
     sign = jnp.where(
         lax.broadcasted_iota(jnp.int32, (1, width), 1) < half, jnp.float32(1.0), jnp.float32(-1.0)
@@ -192,7 +197,7 @@
     def pair(index, carry):
         picks = [pl.ds(index * 2 + turn, shots, stride=rows) for turn in range(2)]
         block = jnp.concatenate([wide[pick, :] for pick in picks], axis=1).astype(jnp.bfloat16)
-        both = jnp.dot(table_ref[...], block, preferred_element_type=jnp.float32)
+        both = jnp.dot(across_ref[...], block, preferred_element_type=jnp.float32)
         kept = []
         for turn in range(2):
             own = both[:, turn * width : (turn + 1) * width]
@@ -201,23 +206,27 @@
             power = power + pltpu.roll(power, half, 1)
             factor = jnp.maximum(1.0 - level * lax.rsqrt(power), 0.0)
             kept.append((wave * factor).astype(jnp.bfloat16))
-        both = jnp.dot(table_ref[...], jnp.concatenate(kept, axis=1), preferred_element_type=jnp.float32)
+        both = jnp.dot(back_ref[...], jnp.concatenate(kept, axis=1), preferred_element_type=jnp.float32)
         for turn in range(2):
             own = both[:, turn * width : (turn + 1) * width]
             back[picks[turn], :] = own[:shots] - sign * pltpu.roll(own[shots:], half, 1)
         return carry
 
     lax.fori_loop(0, rows // 2, pair, 0)
-    out_ref[...] = back[...].astype(jnp.bfloat16).reshape(out_ref.shape)
-
-
-def update_kernel(*refs):
-    restored_ref, table_ref, out_ref = refs[0], refs[1], refs[-1]
-    blocks, held, rows, width = restored_ref.shape
+    for slot, ref in enumerate(out_refs):
+        ref[...] = (
+            back[pl.ds(slot * held * rows, held * rows), :].astype(jnp.bfloat16).reshape(ref.shape)
+        )
+
+
+def update_kernel(peers, table_ref, _, *refs):
+    restored_refs, (out_ref, turn_ref) = refs[:peers], refs[-2:]
+    held, rows, width = restored_refs[0].shape
     block = jnp.concatenate(
-        [restored_ref[index].reshape(held * rows, width) for index in range(blocks)], axis=1
+        [ref[...].reshape(held * rows, width) for ref in restored_refs], axis=1
     )
     out_ref[...] = jnp.dot(block, table_ref[...], preferred_element_type=jnp.float32).reshape(out_ref.shape)
+    turn_ref[...] = jnp.zeros_like(turn_ref)
 
 
 def whole(shape):
@@ -247,18 +256,19 @@
 PARAMS = pltpu.CompilerParams(vmem_limit_bytes=48 * 1024 * 1024)
 
 
-def spectra_of(first, delays, fields, table, rows, chunk, blocks):
+ANYWHERE = pl.BlockSpec(memory_space=pl.ANY)
+
+
+def spectra_of(first, delays, fields, table, rows, chunk, peers, after):
     shots, _, samples = fields[0].shape
-    width = 2 * F // blocks
-    return pl.pallas_call(
+    block = (shots, rows, 2 * F // peers)
+    *spectra, energy = pl.pallas_call(
         spectra_kernel,
         grid=(1,),
-        in_specs=blend_specs(shots, rows, samples, chunk) + [whole(table.shape)],
-        out_specs=[whole((blocks, shots, rows, width)), whole((shots, LANES))],
-        out_shape=[
-            jax.ShapeDtypeStruct((blocks, shots, rows, width), jnp.bfloat16),
-            jax.ShapeDtypeStruct((shots, LANES), jnp.float32),
-        ],
+        in_specs=blend_specs(shots, rows, samples, chunk) + [whole(table.shape), ANYWHERE],
+        out_specs=[whole(block)] * peers + [whole((shots, LANES))],
+        out_shape=[jax.ShapeDtypeStruct(block, jnp.bfloat16)] * peers
+        + [jax.ShapeDtypeStruct((shots, LANES), jnp.float32)],
         scratch_shapes=blend_scratch(shots, rows, samples)
         + [pltpu.VMEM((shots * rows, samples), jnp.bfloat16)],
         compiler_params=PARAMS,
@@ -268,7 +278,8 @@
             transcendentals=0,
         ),
         name="spectra",
-    )(first, delays, *fields, table)
+    )(first, delays, *fields, table, after)
+    return spectra, energy
 
 
 def stepped_of(first, delays, fields, rows, chunk):
@@ -288,53 +299,74 @@
     )(first, delays, *fields)
 
 
-def shrunk_of(spectra, table, level):
-    blocks, held, rows, width = spectra.shape
-    shots = blocks * held
+def shrunk_of(spectra, across, back, level, after):
+    held, rows, width = spectra[0].shape
+    peers = len(spectra)
+    shots = peers * held
+    size = spectra[0].size * peers
     return pl.pallas_call(
         shots_kernel,
         grid=(1,),
-        in_specs=[whole(spectra.shape), whole(table.shape), whole(level.shape)],
-        out_specs=whole(spectra.shape),
-        out_shape=jax.ShapeDtypeStruct(spectra.shape, jnp.bfloat16),
+        in_specs=[whole(across.shape), whole(back.shape), whole(level.shape), ANYWHERE]
+        + [whole(spectra[0].shape)] * peers,
+        out_specs=[whole(spectra[0].shape)] * peers,
+        out_shape=[jax.ShapeDtypeStruct(spectra[0].shape, jnp.bfloat16)] * peers,
         scratch_shapes=[pltpu.VMEM((shots * rows, width), jnp.float32)] * 2,
         compiler_params=PARAMS,
         cost_estimate=pl.CostEstimate(
-            flops=8 * shots * shots * rows * width,
-            bytes_accessed=2 * 2 * spectra.size + table.size * 2,
-            transcendentals=spectra.size,
+            flops=8 * shots * size, bytes_accessed=4 * size + 4 * across.size, transcendentals=size
         ),
         name="shrink",
-    )(spectra, table, level)
-
-
-def updated_of(restored, table, chunk, receivers, onto):
-    blocks, shots, rows, width = restored.shape
+    )(across, back, level, after, *spectra)
+
+
+def updated_of(restored, table, chunk, receivers, onto, after):
+    shots, rows, width = restored[0].shape
+    peers = len(restored)
     samples = table.shape[1]
     group = min(shots, max(1, 256 // rows))
-    in_specs = [
-        pl.BlockSpec((blocks, group, rows, width), lambda step: (0, step, 0, 0)),
-        whole(table.shape),
-    ]
-    operands = [restored, table]
+    in_specs = [whole(table.shape), ANYWHERE]
+    in_specs += [pl.BlockSpec((group, rows, width), lambda step: (step, 0, 0))] * peers
+    operands = [table, after, *restored]
     if onto is not None:
-        in_specs.append(pl.BlockSpec(memory_space=pl.ANY))
+        in_specs.append(ANYWHERE)
         operands.append(onto)
     return pl.pallas_call(
-        update_kernel,
+        functools.partial(update_kernel, peers),
         grid=(shots // group,),
         in_specs=in_specs,
-        out_specs=pl.BlockSpec((group, rows, samples), lambda step: (step, chunk, 0)),
-        out_shape=jax.ShapeDtypeStruct((shots, receivers, samples), jnp.float32),
-        input_output_aliases={} if onto is None else {2: 0},
+        out_specs=[
+            pl.BlockSpec((group, rows, samples), lambda step: (step, chunk, 0)),
+            whole((8, LANES)),
+        ],
+        out_shape=[
+            jax.ShapeDtypeStruct((shots, receivers, samples), jnp.float32),
+            jax.ShapeDtypeStruct((8, LANES), jnp.float32),
+        ],
+        input_output_aliases={} if onto is None else {len(operands) - 1: 0},
         compiler_params=PARAMS,
         cost_estimate=pl.CostEstimate(
             flops=4 * F * shots * rows * samples,
-            bytes_accessed=2 * restored.size + 2 * table.size + 4 * shots * rows * samples,
+            bytes_accessed=2 * restored[0].size * peers + 2 * table.size + 4 * shots * rows * samples,
             transcendentals=0,
         ),
         name="update",
     )(*operands)
+
+
+def exchanged(blocks):
+    peers = len(blocks)
+    return [
+        block if slot == 0 else lax.ppermute(block, "shot", [(i, i ^ slot) for i in range(peers)])
+        for slot, block in enumerate(blocks)
+    ]
+
+
+def chunks_of(receivers):
+    if receivers == 128:
+        return [(16, 0), (16, 1), (32, 1), (32, 2), (16, 6), (16, 7)]
+    rows = min(16, receivers)
+    return [(rows, index) for index in range(receivers // rows)]
 
 
 def swapped(array):
@@ -378,8 +410,6 @@
     rank = lax.axis_index("shot")
     total = random_source_delays.shape[0]
     share = F // peers
-    rows = min(16, receivers)
-    chunks = receivers // rows
     first = jnp.reshape(rank * shots, (1,)).astype(jnp.int32)
     up = [(i, i + 1) for i in range(peers - 1)]
     down = [(j, i) for i, j in up]
@@ -391,21 +421,45 @@
     forward, inverse = (jnp.asarray(table) for table in time_tables(samples, peers))
     table = jnp.asarray(shot_table(total))
     level = lax.dynamic_slice_in_dim(thresholds, rank * share, share)
+    chunks = chunks_of(receivers)
     energy = 0.0
-    if (2 * share) % LANES == 0:
+    if (2 * share) % LANES == 0 and peers & (peers - 1) == 0:
+        order = rank ^ jnp.arange(peers, dtype=jnp.int32)
+        forward = jnp.take(forward.reshape(samples, peers, 2 * share), order, axis=1)
+        forward = forward.reshape(samples, 2 * F)
+        inverse = jnp.take(inverse.reshape(peers, 2 * share, samples), order, axis=0)
+        inverse = inverse.reshape(2 * F, samples)
+        across = jnp.take(table.reshape(2 * total, peers, shots), order, axis=1)
+        across = across.reshape(2 * total, total)
+        back = jnp.take(table.reshape(2, peers, shots, total), order, axis=1)
+        back = back.reshape(2 * total, total)
         levels = jnp.tile(level, 2)[None, :]
-        updated = None
-        for chunk in range(chunks):
-            spectra, power = spectra_of(
-                first, random_source_delays, fields, forward, rows, chunk, peers
-            )
-            energy = energy + power
-            restored = shrunk_of(swapped(spectra), table, levels)
-            updated = updated_of(swapped(restored), inverse, chunk, receivers, updated)
+        updated, last = None, levels
+        lag = 2
+        ahead, behind = {}, {}
+        for turn in range(len(chunks) + 2 * lag):
+            if turn < len(chunks):
+                rows, index = chunks[turn]
+                spectra, power = spectra_of(
+                    first, random_source_delays, fields, forward, rows, index, peers, last
+                )
+                last = power
+                energy = energy + power
+                ahead[turn] = exchanged(spectra)
+            place = turn - lag
+            if place in ahead:
+                shrunk = shrunk_of(ahead.pop(place), across, back, levels, last)
+                last = shrunk[0]
+                behind[place] = exchanged(shrunk)
+            place = turn - 2 * lag
+            if place in behind:
+                updated, last = updated_of(
+                    behind.pop(place), inverse, chunks[place][1], receivers, updated, last
+                )
     else:
         parts = []
-        for chunk in range(chunks):
-            part, power = stepped_of(first, random_source_delays, fields, rows, chunk)
+        for rows, index in chunks:
+            part, power = stepped_of(first, random_source_delays, fields, rows, index)
             energy = energy + power
             parts.append(part)
         updated = spectral_by_einsum(

time: 542 us -> 442 us (0.82)
  waiting for transfers between devices: 244 us -> 93.7 us
  starting transfers between devices: 79.3 us -> 149 us
  Pallas kernels: 180 us -> 159 us
    all_to_all x16 -> x0, waiting for transfers between devices: 239 us -> none  [swapped(): lax.all_to_all(array, 'shot', split_axis=0, concat_axis=0, tiled=True)]
    ppermute x0 -> x84, starting transfers between devices: none -> 145 us  [exchanged(): lax.ppermute(block, 'shot', [(i, i ^ slot) for i in range(peers)])]
    ppermute x0 -> x84, waiting for transfers between devices: none -> 93.7 us  [exchanged(): lax.ppermute(block, 'shot', [(i, i ^ slot) for i in range(peers)])]
    all_to_all x16 -> x0, starting transfers between devices: 75.6 us -> none  [swapped(): lax.all_to_all(array, 'shot', split_axis=0, concat_axis=0, tiled=True)]
    pallas_call x8 -> x6, Pallas kernels: 90.9 us -> 78.3 us  [spectra_of(): pl.pallas_call(spectra_kernel, grid=(1,), in_specs=blend_specs(shots, row...]
    unnamed x46 -> x68, local copies, waits for them, and re-layouts: 19.6 us -> 7.35 us
    pallas_call x16 -> x12, Pallas kernels: 89.5 us -> 80.5 us  [the longest x6 61.1 us: shrunk_of(): pl.pallas_call(shots_kernel, grid=(1,), in_specs=[whole(across.shape), wh...]
    gather x0 -> x6, local copies, waits for them, and re-layouts: none -> 7.84 us  [the longest x1 3.86 us: local(): jnp.take(forward.reshape(samples, peers, 2 * share), order, axis=1)]
  transfers between devices with their start and end apart: 18 -> 86, of which waited for: 16 -> 20; matrix products, arithmetic and copies ran while one was open for 0% -> 3% of each run, Pallas kernels for 31% -> 33%
where the time goes in v2:
time: 442 us; the launch traced here: 437 us
  Pallas kernels  159 us (36%)
  starting transfers between devices  149 us (34%)
  waiting for transfers between devices  93.7 us (21%)
  local copies, waits for them, and re-layouts  18.8 us (4%)
  blocking collectives  9.92 us (2%)
  other arithmetic  5.53 us (1%)
    ppermute x84, starting transfers between devices, exchanged(): lax.ppermute(block, 'shot', [(i, i ^ slot) for i in range(peers)])  145 us
    ppermute x84, waiting for transfers between devices, exchanged(): lax.ppermute(block, 'shot', [(i, i ^ slot) for i in range(peers)])  93.7 us
    pallas_call x6, Pallas kernels, spectra_of(): pl.pallas_call(spectra_kernel, grid=(1,), in_specs=blend_specs(shots, row...  78.3 us
    pallas_call x6, Pallas kernels, shrunk_of(): pl.pallas_call(shots_kernel, grid=(1,), in_specs=[whole(across.shape), wh...  61.1 us
    pallas_call x6, Pallas kernels, updated_of(): pl.pallas_call(functools.partial(update_kernel, peers), grid=(shots // gr...  19.4 us
    psum x1, blocking collectives, local(): lax.psum(jnp.sum(energy, axis=1), 'patch')  9.92 us
  transfers between devices with their start and end apart: 86, of which 20 were waited for; matrix products, arithmetic and copies ran while one was open for 3% of the time, Pallas kernels for 33%

profile of v2, /device:TPU:0, one launch (start us, length us, event | category | flops | bytes accessed | tf_op | source)
XLA Modules:
  0.0 437.0 jit_solution(297417287178387076)
XLA Ops:
  4.0 2.4 collective-permute-start
  11.9 3.9 gather_fusion.3
  15.7 2.0 gather_fusion
  17.8 2.8 bitcast_select_fusion
  20.7 11.6 %spectra.6 = (bf16[32,16,128]{2,1,0:T(8,128)(2,1)S(1)}, bf16[32,16,128]{2,1,0:T(8,128)(2,1)S(1)}, bf16[32,16,128]{2,1,0:T(8,128)(2,1)S(1)}, bf16[32,16,128]{2,1,...) custom-call(s32[1]{0:T(128)} %bitcast.7.first_ref, ...), custom_call_target="tpu_custom_call" | custom-call | flops 1073741824 | bytes 5242880 | tf_op jit(solution)/shard_map/spectra/pallas_call | solution.py:265
  32.3 3.3 collective-permute-start.2
  37.4 2.8 collective-permute-start.5
  40.3 11.6 %spectra.7 = (bf16[32,16,128]{2,1,0:T(8,128)(2,1)S(1)}, bf16[32,16,128]{2,1,0:T(8,128)(2,1)S(1)}, bf16[32,16,128]{2,1,0:T(8,128)(2,1)S(1)}, bf16[32,16,128]{2,1,...) custom-call(s32[1]{0:T(128)} %bitcast.7.first_ref, ...), custom_call_target="tpu_custom_call" | custom-call | flops 1073741824 | bytes 5242880 | tf_op jit(solution)/shard_map/spectra/pallas_call | solution.py:265
  51.9 3.7 collective-permute-start.7
  57.5 15.9 %spectra.8 = (bf16[32,32,128]{2,1,0:T(8,128)(2,1)S(1)}, bf16[32,32,128]{2,1,0:T(8,128)(2,1)S(1)}, bf16[32,32,128]{2,1,0:T(8,128)(2,1)S(1)}, bf16[32,32,128]{2,1,...) custom-call(s32[1]{0:T(128)} %bitcast.7.first_ref, ...), custom_call_target="tpu_custom_call" | custom-call | flops 2147483648 | bytes 8388608 | tf_op jit(solution)/shard_map/spectra/pallas_call | solution.py:265
  73.5 2.6 collective-permute-start.12
  76.3 3.6 collective-permute-start.14
  79.9 6.8 %shrink.6 = (bf16[32,16,128]{2,1,0:T(8,128)(2,1)S(1)}, bf16[32,16,128]{2,1,0:T(8,128)(2,1)S(1)}, bf16[32,16,128]{2,1,0:T(8,128)(2,1)S(1)}, bf16[32,16,128]{2,1,0...) custom-call(bf16[512,256]{1,0:T(8,128)(2,1)S(1)} %get-tuple-element., ...), custom_call_target="tpu_custom_call" | custom-call | flops 1073741824 | bytes 2621440 | tf_op jit(solution)/shard_map/shrink/pallas_call | solution.py:307
  87.1 2.0 collective-permute-done.12.refs_4_
  89.2 2.0 collective-permute-done.13.refs_5_
  91.2 3.2 collective-permute-start.25
  94.4 5.1 %collective-permute-start.26 = (bf16[32,16,128]{2,1,0:T(8,128)(2,1)S(1)}, bf16[32,16,128]{2,1,0:T(8,128)(2,1)S(1)}, u32[]{:S(2)}, u32[]{:S(2)}) collective-permute-start(bf16[32,16,128]{2,1,0:T(8,128)(2,1)S(1)} %get-tuple-element.150), channel_id=1, source_target_pairs={{0,4},{1,5},{2,6},{3,7},{4,0},{5,1},{6,2},{7,3},{8,12},{9,13},{10,... | collective-permute-start | bytes 393224 | tf_op jit(solution)/shard_map/ppermute | solution.py:360
  103.9 2.6 collective-permute-done.26.refs_4_
  106.5 2.0 collective-permute-start.29
  108.5 3.4 collective-permute-done.27.refs_5_
  113.8 2.9 collective-permute-done.28.refs_6_
  117.4 5.2 %collective-permute-start.19 = (bf16[32,32,128]{2,1,0:T(8,128)(2,1)S(1)}, bf16[32,32,128]{2,1,0:T(8,128)(2,1)S(1)}, u32[]{:S(2)}, u32[]{:S(2)}) collective-permute-start(bf16[32,32,128]{2,1,0:T(8,128)(2,1)S(1)} %get-tuple-element.142), channel_id=1, source_target_pairs={{0,4},{1,5},{2,6},{3,7},{4,0},{5,1},{6,2},{7,3},{8,12},{9,13},{10,... | collective-permute-start | bytes 786440 | tf_op jit(solution)/shard_map/ppermute | solution.py:360
  126.2 2.5 collective-permute-start.22
  128.7 15.9 %spectra.9 = (bf16[32,32,128]{2,1,0:T(8,128)(2,1)S(1)}, bf16[32,32,128]{2,1,0:T(8,128)(2,1)S(1)}, bf16[32,32,128]{2,1,0:T(8,128)(2,1)S(1)}, bf16[32,32,128]{2,1,...) custom-call(s32[1]{0:T(128)} %bitcast.7.first_ref, ...), custom_call_target="tpu_custom_call" | custom-call | flops 2147483648 | bytes 8388608 | tf_op jit(solution)/shard_map/spectra/pallas_call | solution.py:265
  144.6 6.8 %shrink.7 = (bf16[32,16,128]{2,1,0:T(8,128)(2,1)S(1)}, bf16[32,16,128]{2,1,0:T(8,128)(2,1)S(1)}, bf16[32,16,128]{2,1,0:T(8,128)(2,1)S(1)}, bf16[32,16,128]{2,1,0...) custom-call(bf16[512,256]{1,0:T(8,128)(2,1)S(1)} %get-tuple-element., ...), custom_call_target="tpu_custom_call" | custom-call | flops 1073741824 | bytes 2621440 | tf_op jit(solution)/shard_map/shrink/pallas_call | solution.py:307
  152.1 4.8 %collective-permute-done.20.refs_5_ = bf16[32,32,128]{2,1,0:T(8,128)(2,1)S(1)} collective-permute-done((bf16[32,32,128]{2,1,0:T(8,128)(2,1)S(1)}, bf16[32,32,128]{2,1,0:T(8,128)(2,1)S(1)}, u32[]{:S(2)}, u32[]{:S(2)}) %collective-permute-start.20) | collective-permute-done | bytes 262176 | tf_op jit(solution)/shard_map/ppermute | solution.py:360
  156.8 11.6 %spectra.10 = (bf16[32,16,128]{2,1,0:T(8,128)(2,1)S(1)}, bf16[32,16,128]{2,1,0:T(8,128)(2,1)S(1)}, bf16[32,16,128]{2,1,0:T(8,128)(2,1)S(1)}, bf16[32,16,128]{2,1...) custom-call(s32[1]{0:T(128)} %bitcast.7.first_ref, ...), custom_call_target="tpu_custom_call" | custom-call | flops 1073741824 | bytes 5242880 | tf_op jit(solution)/shard_map/spectra/pallas_call | solution.py:265
  168.4 2.9 collective-permute-start.40
  175.4 16.5 %shrink.8 = (bf16[32,32,128]{2,1,0:T(8,128)(2,1)S(1)}, bf16[32,32,128]{2,1,0:T(8,128)(2,1)S(1)}, bf16[32,32,128]{2,1,0:T(8,128)(2,1)S(1)}, bf16[32,32,128]{2,1,0...) custom-call(bf16[512,256]{1,0:T(8,128)(2,1)S(1)} %get-tuple-element., ...), custom_call_target="tpu_custom_call" | custom-call | flops 2147483648 | bytes 4718592 | tf_op jit(solution)/shard_map/shrink/pallas_call | solution.py:307
  193.4 2.5 update.6
  200.8 11.7 %spectra.11 = (bf16[32,16,128]{2,1,0:T(8,128)(2,1)S(1)}, bf16[32,16,128]{2,1,0:T(8,128)(2,1)S(1)}, bf16[32,16,128]{2,1,0:T(8,128)(2,1)S(1)}, bf16[32,16,128]{2,1...) custom-call(s32[1]{0:T(128)} %bitcast.7.first_ref, ...), custom_call_target="tpu_custom_call" | custom-call | flops 1073741824 | bytes 5242880 | tf_op jit(solution)/shard_map/spectra/pallas_call | solution.py:265
  216.7 2.1 collective-permute-start.61
  220.4 3.1 collective-permute-start.31
  223.5 2.5 collective-permute-done.59.refs_2_
  226.0 2.3 collective-permute-done.60.refs_3_
  228.4 2.1 collective-permute-start.63
  232.1 2.6 collective-permute-done.62.refs_5_
  234.7 2.8 collective-permute-start.32
  237.5 2.9 collective-permute-done.63.refs_6_
  240.4 4.7 %collective-permute-start.33 = (bf16[32,32,128]{2,1,0:T(8,128)(2,1)S(1)}, bf16[32,32,128]{2,1,0:T(8,128)(2,1)S(1)}, u32[]{:S(2)}, u32[]{:S(2)}) collective-permute-start(bf16[32,32,128]{2,1,0:T(8,128)(2,1)S(1)} %get-tuple-element.160), channel_id=1, source_target_pairs={{0,4},{1,5},{2,6},{3,7},{4,0},{5,1},{6,2},{7,3},{8,12},{9,13},{10,... | collective-permute-start | bytes 786440 | tf_op jit(solution)/shard_map/ppermute | solution.py:360
  245.1 2.5 collective-permute-start.34
  248.1 2.8 collective-permute-start.36
  251.6 23.1 %collective-permute-done.33.refs_4_ = bf16[32,32,128]{2,1,0:T(8,128)(2,1)S(1)} collective-permute-done((bf16[32,32,128]{2,1,0:T(8,128)(2,1)S(1)}, bf16[32,32,128]{2,1,0:T(8,128)(2,1)S(1)}, u32[]{:S(2)}, u32[]{:S(2)}) %collective-permute-start.33) | collective-permute-done | bytes 262176 | tf_op jit(solution)/shard_map/ppermute | solution.py:360
  274.7 4.0 collective-permute-done.34.refs_5_
  279.2 8.1 %collective-permute-start.54 = (bf16[32,32,128]{2,1,0:T(8,128)(2,1)S(1)}, bf16[32,32,128]{2,1,0:T(8,128)(2,1)S(1)}, u32[]{:S(2)}, u32[]{:S(2)}) collective-permute-start(bf16[32,32,128]{2,1,0:T(8,128)(2,1)S(1)} %get-tuple-element.186), channel_id=1, source_target_pairs={{0,4},{1,5},{2,6},{3,7},{4,0},{5,1},{6,2},{7,3},{8,12},{9,13},{10,... | collective-permute-start | bytes 786440 | tf_op jit(solution)/shard_map/ppermute | solution.py:360
  287.3 10.7 %collective-permute-start.55 = (bf16[32,32,128]{2,1,0:T(8,128)(2,1)S(1)}, bf16[32,32,128]{2,1,0:T(8,128)(2,1)S(1)}, u32[]{:S(2)}, u32[]{:S(2)}) collective-permute-start(bf16[32,32,128]{2,1,0:T(8,128)(2,1)S(1)} %get-tuple-element.187), channel_id=1, source_target_pairs={{0,5},{1,4},{2,7},{3,6},{4,1},{5,0},{6,3},{7,2},{8,13},{9,12},{10,... | collective-permute-start | bytes 786440 | tf_op jit(solution)/shard_map/ppermute | solution.py:360
  298.0 17.4 %shrink.9 = (bf16[32,32,128]{2,1,0:T(8,128)(2,1)S(1)}, bf16[32,32,128]{2,1,0:T(8,128)(2,1)S(1)}, bf16[32,32,128]{2,1,0:T(8,128)(2,1)S(1)}, bf16[32,32,128]{2,1,0...) custom-call(bf16[512,256]{1,0:T(8,128)(2,1)S(1)} %get-tuple-element., ...), custom_call_target="tpu_custom_call" | custom-call | flops 2147483648 | bytes 4718592 | tf_op jit(solution)/shard_map/shrink/pallas_call | solution.py:307
  318.9 2.4 update.7
  321.4 6.8 %shrink.10 = (bf16[32,16,128]{2,1,0:T(8,128)(2,1)S(1)}, bf16[32,16,128]{2,1,0:T(8,128)(2,1)S(1)}, bf16[32,16,128]{2,1,0:T(8,128)(2,1)S(1)}, bf16[32,16,128]{2,1,...) custom-call(bf16[512,256]{1,0:T(8,128)(2,1)S(1)} %get-tuple-element., ...), custom_call_target="tpu_custom_call" | custom-call | flops 1073741824 | bytes 2621440 | tf_op jit(solution)/shard_map/shrink/pallas_call | solution.py:307
  330.1 5.9 %collective-permute-start.75 = (bf16[32,16,128]{2,1,0:T(8,128)(2,1)S(1)}, bf16[32,16,128]{2,1,0:T(8,128)(2,1)S(1)}, u32[]{:S(2)}, u32[]{:S(2)}) collective-permute-start(bf16[32,16,128]{2,1,0:T(8,128)(2,1)S(1)} %get-tuple-element.213), channel_id=1, source_target_pairs={{0,4},{1,5},{2,6},{3,7},{4,0},{5,1},{6,2},{7,3},{8,12},{9,13},{10,... | collective-permute-start | bytes 393224 | tf_op jit(solution)/shard_map/ppermute | solution.py:360
  336.0 7.8 %collective-permute-start.76 = (bf16[32,16,128]{2,1,0:T(8,128)(2,1)S(1)}, bf16[32,16,128]{2,1,0:T(8,128)(2,1)S(1)}, u32[]{:S(2)}, u32[]{:S(2)}) collective-permute-start(bf16[32,16,128]{2,1,0:T(8,128)(2,1)S(1)} %get-tuple-element.214), channel_id=1, source_target_pairs={{0,5},{1,4},{2,7},{3,6},{4,1},{5,0},{6,3},{7,2},{8,13},{9,12},{10,... | collective-permute-start | bytes 393224 | tf_op jit(solution)/shard_map/ppermute | solution.py:360
  345.7 4.1 update.8
  349.8 6.8 %shrink.11 = (bf16[32,16,128]{2,1,0:T(8,128)(2,1)S(1)}, bf16[32,16,128]{2,1,0:T(8,128)(2,1)S(1)}, bf16[32,16,128]{2,1,0:T(8,128)(2,1)S(1)}, bf16[32,16,128]{2,1,...) custom-call(bf16[512,256]{1,0:T(8,128)(2,1)S(1)} %get-tuple-element., ...), custom_call_target="tpu_custom_call" | custom-call | flops 1073741824 | bytes 2621440 | tf_op jit(solution)/shard_map/shrink/pallas_call | solution.py:307
  358.0 2.8 collective-permute-start.78
  365.9 3.1 collective-permute-start.67
  372.7 2.8 collective-permute-start.70
  376.8 9.9 %psum.7 = f32[32]{0:T(128)S(1)} all-reduce(f32[32]{0:T(128)S(1)} %add_reduce_fusion), channel_id=1, replica_groups=mesh['patch'=4,'shot'=8] {'patch'}, use_global_device_ids=true, to_apply=%region_1.2 | all-reduce | flops 32 | bytes 256 | tf_op jit(solution)/shard_map/psum | solution.py:468
  387.2 15.5 %collective-permute-done.68.refs_4_ = bf16[32,32,128]{2,1,0:T(8,128)(2,1)} collective-permute-done((bf16[32,32,128]{2,1,0:T(8,128)(2,1)}, bf16[32,32,128]{2,1,0:T(8,128)(2,1)}, u32[]{:S(2)}, u32[]{:S(2)}) %collective-permute-start.68) | collective-permute-done | bytes 262176 | tf_op jit(solution)/shard_map/ppermute | solution.py:360
  402.7 6.6 %collective-permute-done.69.refs_5_ = bf16[32,32,128]{2,1,0:T(8,128)(2,1)} collective-permute-done((bf16[32,32,128]{2,1,0:T(8,128)(2,1)}, bf16[32,32,128]{2,1,0:T(8,128)(2,1)}, u32[]{:S(2)}, u32[]{:S(2)}) %collective-permute-start.69) | collective-permute-done | bytes 262176 | tf_op jit(solution)/shard_map/ppermute | solution.py:360
  409.3 3.3 collective-permute-start.84
  414.1 5.5 %update.9 = (f32[32,128,1024]{2,1,0:T(8,128)}, f32[8,128]{1,0:T(8,128)S(1)}) custom-call(bf16[1024,1024]{1,0:T(8,128)(2,1)S(1)} %get-tuple-element.233.table_ref, bf16[32,16,128]{2,1,0:T(8,128)(2,1)S(1)} %get-tuple-element.200._.refs_0_, bf16[32,32,128]{2,1,0:T(8,128)(2,1)S(1)} %get-tuple-element.164._.refs_0_, ...), custom_call_target="tpu_custom_call", output_to_operand_aliasing={{0}: (10, {})} | custom-call | flops 2147483648 | bytes 8388608 | tf_op jit(solution)/shard_map/update/pallas_call | solution.py:334
  419.6 2.5 update.10
  422.1 11.3 %collective-permute-done.82.refs_4_ = bf16[32,16,128]{2,1,0:T(8,128)(2,1)S(1)} collective-permute-done((bf16[32,16,128]{2,1,0:T(8,128)(2,1)}, bf16[32,16,128]{2,1,0:T(8,128)(2,1)S(1)}, u32[]{:S(2)}, u32[]{:S(2)}) %collective-permute-start.82) | collective-permute-done | bytes 131104 | tf_op jit(solution)/shard_map/ppermute | solution.py:360
  434.5 2.4 update.11
  (220 shorter events, 65.7 us)
Async XLA Ops:
  4.0 16.6 %collective-permute-start = (bf16[3,128,1024]{2,1,0:T(8,128)(2,1)}, bf16[3,128,1024]{2,1,0:T(8,128)(2,1)S(1)}, u32[]{:S(2)}, u32[]{:S(2)}) collective-permute-start(bf16[3,128,1024]{2,1,0:T(8,128)(2,1)} %pad_maximum_fusion), channel_id=1, source_target_pairs={{0,1},{1,2},{2,3},{3,4},{4,5},{5,6},{6,7},{8,9},{9,10},{10,11},{11... | collective-permute-start | bytes 2359304 | tf_op jit(solution)/shard_map/ppermute | solution.py:418
  32.3 19.6 %collective-permute-start.2 = (bf16[32,16,128]{2,1,0:T(8,128)(2,1)S(1)}, bf16[32,16,128]{2,1,0:T(8,128)(2,1)S(1)}, u32[]{:S(2)}, u32[]{:S(2)}) collective-permute-start(bf16[32,16,128]{2,1,0:T(8,128)(2,1)S(1)} %get-tuple-element.119), channel_id=1, source_target_pairs={{0,1},{1,0},{2,3},{3,2},{4,5},{5,4},{6,7},{7,6},{8,9},{9,8},{10,11... | collective-permute-start | bytes 393224 | tf_op jit(solution)/shard_map/ppermute | solution.py:360
  35.6 19.9 %collective-permute-start.3 = (bf16[32,16,128]{2,1,0:T(8,128)(2,1)S(1)}, bf16[32,16,128]{2,1,0:T(8,128)(2,1)S(1)}, u32[]{:S(2)}, u32[]{:S(2)}) collective-permute-start(bf16[32,16,128]{2,1,0:T(8,128)(2,1)S(1)} %get-tuple-element.120), channel_id=1, source_target_pairs={{0,2},{1,3},{2,0},{3,1},{4,6},{5,7},{6,4},{7,5},{8,10},{9,11},{10,... | collective-permute-start | bytes 393224 | tf_op jit(solution)/shard_map/ppermute | solution.py:360
  37.3 18.4 %collective-permute-start.4 = (bf16[32,16,128]{2,1,0:T(8,128)(2,1)S(1)}, bf16[32,16,128]{2,1,0:T(8,128)(2,1)S(1)}, u32[]{:S(2)}, u32[]{:S(2)}) collective-permute-start(bf16[32,16,128]{2,1,0:T(8,128)(2,1)S(1)} %get-tuple-element.121), channel_id=1, source_target_pairs={{0,3},{1,2},{2,1},{3,0},{4,7},{5,6},{6,5},{7,4},{8,11},{9,10},{10,... | collective-permute-start | bytes 393224 | tf_op jit(solution)/shard_map/ppermute | solution.py:360
  37.4 18.5 %collective-permute-start.5 = (bf16[32,16,128]{2,1,0:T(8,128)(2,1)S(1)}, bf16[32,16,128]{2,1,0:T(8,128)(2,1)S(1)}, u32[]{:S(2)}, u32[]{:S(2)}) collective-permute-start(bf16[32,16,128]{2,1,0:T(8,128)(2,1)S(1)} %get-tuple-element.122), channel_id=1, source_target_pairs={{0,4},{1,5},{2,6},{3,7},{4,0},{5,1},{6,2},{7,3},{8,12},{9,13},{10,... | collective-permute-start | bytes 393224 | tf_op jit(solution)/shard_map/ppermute | solution.py:360
  40.1 15.8 %collective-permute-start.6 = (bf16[32,16,128]{2,1,0:T(8,128)(2,1)S(1)}, bf16[32,16,128]{2,1,0:T(8,128)(2,1)S(1)}, u32[]{:S(2)}, u32[]{:S(2)}) collective-permute-start(bf16[32,16,128]{2,1,0:T(8,128)(2,1)S(1)} %get-tuple-element.123), channel_id=1, source_target_pairs={{0,5},{1,4},{2,7},{3,6},{4,1},{5,0},{6,3},{7,2},{8,13},{9,12},{10,... | collective-permute-start | bytes 393224 | tf_op jit(solution)/shard_map/ppermute | solution.py:360
  51.9 21.6 %collective-permute-start.7 = (bf16[32,16,128]{2,1,0:T(8,128)(2,1)S(1)}, bf16[32,16,128]{2,1,0:T(8,128)(2,1)S(1)}, u32[]{:S(2)}, u32[]{:S(2)}) collective-permute-start(bf16[32,16,128]{2,1,0:T(8,128)(2,1)S(1)} %get-tuple-element.124), channel_id=1, source_target_pairs={{0,6},{1,7},{2,4},{3,5},{4,2},{5,3},{6,0},{7,1},{8,14},{9,15},{10,... | collective-permute-start | bytes 393224 | tf_op jit(solution)/shard_map/ppermute | solution.py:360
  55.5 20.5 %collective-permute-start.8 = (bf16[32,16,128]{2,1,0:T(8,128)(2,1)S(1)}, bf16[32,16,128]{2,1,0:T(8,128)(2,1)S(1)}, u32[]{:S(2)}, u32[]{:S(2)}) collective-permute-start(bf16[32,16,128]{2,1,0:T(8,128)(2,1)S(1)} %get-tuple-element.125), channel_id=1, source_target_pairs={{0,7},{1,6},{2,5},{3,4},{4,3},{5,2},{6,1},{7,0},{8,15},{9,14},{10,... | collective-permute-start | bytes 393224 | tf_op jit(solution)/shard_map/ppermute | solution.py:360
  55.7 20.6 %collective-permute-start.9 = (bf16[32,16,128]{2,1,0:T(8,128)(2,1)S(1)}, bf16[32,16,128]{2,1,0:T(8,128)(2,1)S(1)}, u32[]{:S(2)}, u32[]{:S(2)}) collective-permute-start(bf16[32,16,128]{2,1,0:T(8,128)(2,1)S(1)} %get-tuple-element.129), channel_id=1, source_target_pairs={{0,1},{1,0},{2,3},{3,2},{4,5},{5,4},{6,7},{7,6},{8,9},{9,8},{10,11... | collective-permute-start | bytes 393224 | tf_op jit(solution)/shard_map/ppermute | solution.py:360
  55.9 30.8 %collective-permute-start.10 = (bf16[32,16,128]{2,1,0:T(8,128)(2,1)S(1)}, bf16[32,16,128]{2,1,0:T(8,128)(2,1)S(1)}, u32[]{:S(2)}, u32[]{:S(2)}) collective-permute-start(bf16[32,16,128]{2,1,0:T(8,128)(2,1)S(1)} %get-tuple-element.130), channel_id=1, source_target_pairs={{0,2},{1,3},{2,0},{3,1},{4,6},{5,7},{6,4},{7,5},{8,10},{9,11},{10,... | collective-permute-start | bytes 393224 | tf_op jit(solution)/shard_map/ppermute | solution.py:360
  55.9 30.9 %collective-permute-start.11 = (bf16[32,16,128]{2,1,0:T(8,128)(2,1)S(1)}, bf16[32,16,128]{2,1,0:T(8,128)(2,1)S(1)}, u32[]{:S(2)}, u32[]{:S(2)}) collective-permute-start(bf16[32,16,128]{2,1,0:T(8,128)(2,1)S(1)} %get-tuple-element.131), channel_id=1, source_target_pairs={{0,3},{1,2},{2,1},{3,0},{4,7},{5,6},{6,5},{7,4},{8,11},{9,10},{10,... | collective-permute-start | bytes 393224 | tf_op jit(solution)/shard_map/ppermute | solution.py:360
  76.3 18.1 %collective-permute-start.14 = (bf16[32,16,128]{2,1,0:T(8,128)(2,1)S(1)}, bf16[32,16,128]{2,1,0:T(8,128)(2,1)S(1)}, u32[]{:S(2)}, u32[]{:S(2)}) collective-permute-start(bf16[32,16,128]{2,1,0:T(8,128)(2,1)S(1)} %get-tuple-element.134), channel_id=1, source_target_pairs={{0,6},{1,7},{2,4},{3,5},{4,2},{5,3},{6,0},{7,1},{8,14},{9,15},{10,... | collective-permute-start | bytes 393224 | tf_op jit(solution)/shard_map/ppermute | solution.py:360
  99.4 25.6 %collective-permute-start.16 = (bf16[32,32,128]{2,1,0:T(8,128)(2,1)S(1)}, bf16[32,32,128]{2,1,0:T(8,128)(2,1)S(1)}, u32[]{:S(2)}, u32[]{:S(2)}) collective-permute-start(bf16[32,32,128]{2,1,0:T(8,128)(2,1)S(1)} %get-tuple-element.139), channel_id=1, source_target_pairs={{0,1},{1,0},{2,3},{3,2},{4,5},{5,4},{6,7},{7,6},{8,9},{9,8},{10,11... | collective-permute-start | bytes 786440 | tf_op jit(solution)/shard_map/ppermute | solution.py:360
  99.4 26.7 %collective-permute-start.17 = (bf16[32,32,128]{2,1,0:T(8,128)(2,1)S(1)}, bf16[32,32,128]{2,1,0:T(8,128)(2,1)S(1)}, u32[]{:S(2)}, u32[]{:S(2)}) collective-permute-start(bf16[32,32,128]{2,1,0:T(8,128)(2,1)S(1)} %get-tuple-element.140), channel_id=1, source_target_pairs={{0,2},{1,3},{2,0},{3,1},{4,6},{5,7},{6,4},{7,5},{8,10},{9,11},{10,... | collective-permute-start | bytes 786440 | tf_op jit(solution)/shard_map/ppermute | solution.py:360
  106.5 16.1 %collective-permute-start.29 = (bf16[32,16,128]{2,1,0:T(8,128)(2,1)S(1)}, bf16[32,16,128]{2,1,0:T(8,128)(2,1)S(1)}, u32[]{:S(2)}, u32[]{:S(2)}) collective-permute-start(bf16[32,16,128]{2,1,0:T(8,128)(2,1)S(1)} %get-tuple-element.153), channel_id=1, source_target_pairs={{0,7},{1,6},{2,5},{3,4},{4,3},{5,2},{6,1},{7,0},{8,15},{9,14},{10,... | collective-permute-start | bytes 393224 | tf_op jit(solution)/shard_map/ppermute | solution.py:360
  111.8 39.6 %collective-permute-start.18 = (bf16[32,32,128]{2,1,0:T(8,128)(2,1)S(1)}, bf16[32,32,128]{2,1,0:T(8,128)(2,1)S(1)}, u32[]{:S(2)}, u32[]{:S(2)}) collective-permute-start(bf16[32,32,128]{2,1,0:T(8,128)(2,1)S(1)} %get-tuple-element.141), channel_id=1, source_target_pairs={{0,3},{1,2},{2,1},{3,0},{4,7},{5,6},{6,5},{7,4},{8,11},{9,10},{10,... | collective-permute-start | bytes 786440 | tf_op jit(solution)/shard_map/ppermute | solution.py:360
  117.4 34.7 %collective-permute-start.19 = (bf16[32,32,128]{2,1,0:T(8,128)(2,1)S(1)}, bf16[32,32,128]{2,1,0:T(8,128)(2,1)S(1)}, u32[]{:S(2)}, u32[]{:S(2)}) collective-permute-start(bf16[32,32,128]{2,1,0:T(8,128)(2,1)S(1)} %get-tuple-element.142), channel_id=1, source_target_pairs={{0,4},{1,5},{2,6},{3,7},{4,0},{5,1},{6,2},{7,3},{8,12},{9,13},{10,... | collective-permute-start | bytes 786440 | tf_op jit(solution)/shard_map/ppermute | solution.py:360
  123.3 33.6 %collective-permute-start.20 = (bf16[32,32,128]{2,1,0:T(8,128)(2,1)S(1)}, bf16[32,32,128]{2,1,0:T(8,128)(2,1)S(1)}, u32[]{:S(2)}, u32[]{:S(2)}) collective-permute-start(bf16[32,32,128]{2,1,0:T(8,128)(2,1)S(1)} %get-tuple-element.143), channel_id=1, source_target_pairs={{0,5},{1,4},{2,7},{3,6},{4,1},{5,0},{6,3},{7,2},{8,13},{9,12},{10,... | collective-permute-start | bytes 786440 | tf_op jit(solution)/shard_map/ppermute | solution.py:360
  125.1 43.3 %collective-permute-start.21 = (bf16[32,32,128]{2,1,0:T(8,128)(2,1)S(1)}, bf16[32,32,128]{2,1,0:T(8,128)(2,1)S(1)}, u32[]{:S(2)}, u32[]{:S(2)}) collective-permute-start(bf16[32,32,128]{2,1,0:T(8,128)(2,1)S(1)} %get-tuple-element.144), channel_id=1, source_target_pairs={{0,6},{1,7},{2,4},{3,5},{4,2},{5,3},{6,0},{7,1},{8,14},{9,15},{10,... | collective-permute-start | bytes 786440 | tf_op jit(solution)/shard_map/ppermute | solution.py:360
  126.2 45.2 %collective-permute-start.22 = (bf16[32,32,128]{2,1,0:T(8,128)(2,1)S(1)}, bf16[32,32,128]{2,1,0:T(8,128)(2,1)S(1)}, u32[]{:S(2)}, u32[]{:S(2)}) collective-permute-start(bf16[32,32,128]{2,1,0:T(8,128)(2,1)S(1)} %get-tuple-element.145), channel_id=1, source_target_pairs={{0,7},{1,6},{2,5},{3,4},{4,3},{5,2},{6,1},{7,0},{8,15},{9,14},{10,... | collective-permute-start | bytes 786440 | tf_op jit(solution)/shard_map/ppermute | solution.py:360
  151.4 20.1 %collective-permute-start.37 = (bf16[32,16,128]{2,1,0:T(8,128)(2,1)S(1)}, bf16[32,16,128]{2,1,0:T(8,128)(2,1)S(1)}, u32[]{:S(2)}, u32[]{:S(2)}) collective-permute-start(bf16[32,16,128]{2,1,0:T(8,128)(2,1)S(1)} %get-tuple-element.165), channel_id=1, source_target_pairs={{0,1},{1,0},{2,3},{3,2},{4,5},{5,4},{6,7},{7,6},{8,9},{9,8},{10,11... | collective-permute-start | bytes 393224 | tf_op jit(solution)/shard_map/ppermute | solution.py:360
  152.1 21.3 %collective-permute-start.38 = (bf16[32,16,128]{2,1,0:T(8,128)(2,1)S(1)}, bf16[32,16,128]{2,1,0:T(8,128)(2,1)S(1)}, u32[]{:S(2)}, u32[]{:S(2)}) collective-permute-start(bf16[32,16,128]{2,1,0:T(8,128)(2,1)S(1)} %get-tuple-element.166), channel_id=1, source_target_pairs={{0,2},{1,3},{2,0},{3,1},{4,6},{5,7},{6,4},{7,5},{8,10},{9,11},{10,... | collective-permute-start | bytes 393224 | tf_op jit(solution)/shard_map/ppermute | solution.py:360
  156.8 17.9 %collective-permute-start.39 = (bf16[32,16,128]{2,1,0:T(8,128)(2,1)S(1)}, bf16[32,16,128]{2,1,0:T(8,128)(2,1)S(1)}, u32[]{:S(2)}, u32[]{:S(2)}) collective-permute-start(bf16[32,16,128]{2,1,0:T(8,128)(2,1)S(1)} %get-tuple-element.167), channel_id=1, source_target_pairs={{0,3},{1,2},{2,1},{3,0},{4,7},{5,6},{6,5},{7,4},{8,11},{9,10},{10,... | collective-permute-start | bytes 393224 | tf_op jit(solution)/shard_map/ppermute | solution.py:360
  168.4 23.5 %collective-permute-start.40 = (bf16[32,16,128]{2,1,0:T(8,128)(2,1)S(1)}, bf16[32,16,128]{2,1,0:T(8,128)(2,1)S(1)}, u32[]{:S(2)}, u32[]{:S(2)}) collective-permute-start(bf16[32,16,128]{2,1,0:T(8,128)(2,1)S(1)} %get-tuple-element.168), channel_id=1, source_target_pairs={{0,4},{1,5},{2,6},{3,7},{4,0},{5,1},{6,2},{7,3},{8,12},{9,13},{10,... | collective-permute-start | bytes 393224 | tf_op jit(solution)/shard_map/ppermute | solution.py:360
  171.3 20.7 %collective-permute-start.41 = (bf16[32,16,128]{2,1,0:T(8,128)(2,1)S(1)}, bf16[32,16,128]{2,1,0:T(8,128)(2,1)S(1)}, u32[]{:S(2)}, u32[]{:S(2)}) collective-permute-start(bf16[32,16,128]{2,1,0:T(8,128)(2,1)S(1)} %get-tuple-element.169), channel_id=1, source_target_pairs={{0,5},{1,4},{2,7},{3,6},{4,1},{5,0},{6,3},{7,2},{8,13},{9,12},{10,... | collective-permute-start | bytes 393224 | tf_op jit(solution)/shard_map/ppermute | solution.py:360
  171.5 24.4 %collective-permute-start.42 = (bf16[32,16,128]{2,1,0:T(8,128)(2,1)S(1)}, bf16[32,16,128]{2,1,0:T(8,128)(2,1)S(1)}, u32[]{:S(2)}, u32[]{:S(2)}) collective-permute-start(bf16[32,16,128]{2,1,0:T(8,128)(2,1)S(1)} %get-tuple-element.170), channel_id=1, source_target_pairs={{0,6},{1,7},{2,4},{3,5},{4,2},{5,3},{6,0},{7,1},{8,14},{9,15},{10,... | collective-permute-start | bytes 393224 | tf_op jit(solution)/shard_map/ppermute | solution.py:360
  173.4 23.7 %collective-permute-start.43 = (bf16[32,16,128]{2,1,0:T(8,128)(2,1)S(1)}, bf16[32,16,128]{2,1,0:T(8,128)(2,1)S(1)}, u32[]{:S(2)}, u32[]{:S(2)}) collective-permute-start(bf16[32,16,128]{2,1,0:T(8,128)(2,1)S(1)} %get-tuple-element.171), channel_id=1, source_target_pairs={{0,7},{1,6},{2,5},{3,4},{4,3},{5,2},{6,1},{7,0},{8,15},{9,14},{10,... | collective-permute-start | bytes 393224 | tf_op jit(solution)/shard_map/ppermute | solution.py:360
  174.7 24.2 %collective-permute-start.44 = (bf16[32,16,128]{2,1,0:T(8,128)(2,1)S(1)}, bf16[32,16,128]{2,1,0:T(8,128)(2,1)S(1)}, u32[]{:S(2)}, u32[]{:S(2)}) collective-permute-start(bf16[32,16,128]{2,1,0:T(8,128)(2,1)S(1)} %get-tuple-element.175), channel_id=1, source_target_pairs={{0,1},{1,0},{2,3},{3,2},{4,5},{5,4},{6,7},{7,6},{8,9},{9,8},{10,11... | collective-permute-start | bytes 393224 | tf_op jit(solution)/shard_map/ppermute | solution.py:360
  191.9 20.6 %collective-permute-start.45 = (bf16[32,16,128]{2,1,0:T(8,128)(2,1)S(1)}, bf16[32,16,128]{2,1,0:T(8,128)(2,1)S(1)}, u32[]{:S(2)}, u32[]{:S(2)}) collective-permute-start(bf16[32,16,128]{2,1,0:T(8,128)(2,1)S(1)} %get-tuple-element.176), channel_id=1, source_target_pairs={{0,2},{1,3},{2,0},{3,1},{4,6},{5,7},{6,4},{7,5},{8,10},{9,11},{10,... | collective-permute-start | bytes 393224 | tf_op jit(solution)/shard_map/ppermute | solution.py:360
  192.0 21.8 %collective-permute-start.46 = (bf16[32,16,128]{2,1,0:T(8,128)(2,1)S(1)}, bf16[32,16,128]{2,1,0:T(8,128)(2,1)S(1)}, u32[]{:S(2)}, u32[]{:S(2)}) collective-permute-start(bf16[32,16,128]{2,1,0:T(8,128)(2,1)S(1)} %get-tuple-element.177), channel_id=1, source_target_pairs={{0,3},{1,2},{2,1},{3,0},{4,7},{5,6},{6,5},{7,4},{8,11},{9,10},{10,... | collective-permute-start | bytes 393224 | tf_op jit(solution)/shard_map/ppermute | solution.py:360
  195.9 18.8 %collective-permute-start.47 = (bf16[32,16,128]{2,1,0:T(8,128)(2,1)S(1)}, bf16[32,16,128]{2,1,0:T(8,128)(2,1)S(1)}, u32[]{:S(2)}, u32[]{:S(2)}) collective-permute-start(bf16[32,16,128]{2,1,0:T(8,128)(2,1)S(1)} %get-tuple-element.178), channel_id=1, source_target_pairs={{0,4},{1,5},{2,6},{3,7},{4,0},{5,1},{6,2},{7,3},{8,12},{9,13},{10,... | collective-permute-start | bytes 393224 | tf_op jit(solution)/shard_map/ppermute | solution.py:360
  197.1 17.5 %collective-permute-start.48 = (bf16[32,16,128]{2,1,0:T(8,128)(2,1)S(1)}, bf16[32,16,128]{2,1,0:T(8,128)(2,1)S(1)}, u32[]{:S(2)}, u32[]{:S(2)}) collective-permute-start(bf16[32,16,128]{2,1,0:T(8,128)(2,1)S(1)} %get-tuple-element.179), channel_id=1, source_target_pairs={{0,5},{1,4},{2,7},{3,6},{4,1},{5,0},{6,3},{7,2},{8,13},{9,12},{10,... | collective-permute-start | bytes 393224 | tf_op jit(solution)/shard_map/ppermute | solution.py:360
  198.9 17.2 %collective-permute-start.49 = (bf16[32,16,128]{2,1,0:T(8,128)(2,1)S(1)}, bf16[32,16,128]{2,1,0:T(8,128)(2,1)S(1)}, u32[]{:S(2)}, u32[]{:S(2)}) collective-permute-start(bf16[32,16,128]{2,1,0:T(8,128)(2,1)S(1)} %get-tuple-element.180), channel_id=1, source_target_pairs={{0,6},{1,7},{2,4},{3,5},{4,2},{5,3},{6,0},{7,1},{8,14},{9,15},{10,... | collective-permute-start | bytes 393224 | tf_op jit(solution)/shard_map/ppermute | solution.py:360
  220.1 27.5 %collective-permute-start.30 = (bf16[32,32,128]{2,1,0:T(8,128)(2,1)S(1)}, bf16[32,32,128]{2,1,0:T(8,128)(2,1)S(1)}, u32[]{:S(2)}, u32[]{:S(2)}) collective-permute-start(bf16[32,32,128]{2,1,0:T(8,128)(2,1)S(1)} %get-tuple-element.157), channel_id=1, source_target_pairs={{0,1},{1,0},{2,3},{3,2},{4,5},{5,4},{6,7},{7,6},{8,9},{9,8},{10,11... | collective-permute-start | bytes 786440 | tf_op jit(solution)/shard_map/ppermute | solution.py:360
  220.4 27.7 %collective-permute-start.31 = (bf16[32,32,128]{2,1,0:T(8,128)(2,1)S(1)}, bf16[32,32,128]{2,1,0:T(8,128)(2,1)S(1)}, u32[]{:S(2)}, u32[]{:S(2)}) collective-permute-start(bf16[32,32,128]{2,1,0:T(8,128)(2,1)S(1)} %get-tuple-element.158), channel_id=1, source_target_pairs={{0,2},{1,3},{2,0},{3,1},{4,6},{5,7},{6,4},{7,5},{8,10},{9,11},{10,... | collective-permute-start | bytes 786440 | tf_op jit(solution)/shard_map/ppermute | solution.py:360
  234.7 16.5 %collective-permute-start.32 = (bf16[32,32,128]{2,1,0:T(8,128)(2,1)S(1)}, bf16[32,32,128]{2,1,0:T(8,128)(2,1)S(1)}, u32[]{:S(2)}, u32[]{:S(2)}) collective-permute-start(bf16[32,32,128]{2,1,0:T(8,128)(2,1)S(1)} %get-tuple-element.159), channel_id=1, source_target_pairs={{0,3},{1,2},{2,1},{3,0},{4,7},{5,6},{6,5},{7,4},{8,11},{9,10},{10,... | collective-permute-start | bytes 786440 | tf_op jit(solution)/shard_map/ppermute | solution.py:360
  240.4 34.3 %collective-permute-start.33 = (bf16[32,32,128]{2,1,0:T(8,128)(2,1)S(1)}, bf16[32,32,128]{2,1,0:T(8,128)(2,1)S(1)}, u32[]{:S(2)}, u32[]{:S(2)}) collective-permute-start(bf16[32,32,128]{2,1,0:T(8,128)(2,1)S(1)} %get-tuple-element.160), channel_id=1, source_target_pairs={{0,4},{1,5},{2,6},{3,7},{4,0},{5,1},{6,2},{7,3},{8,12},{9,13},{10,... | collective-permute-start | bytes 786440 | tf_op jit(solution)/shard_map/ppermute | solution.py:360
  245.1 33.7 %collective-permute-start.34 = (bf16[32,32,128]{2,1,0:T(8,128)(2,1)S(1)}, bf16[32,32,128]{2,1,0:T(8,128)(2,1)S(1)}, u32[]{:S(2)}, u32[]{:S(2)}) collective-permute-start(bf16[32,32,128]{2,1,0:T(8,128)(2,1)S(1)} %get-tuple-element.161), channel_id=1, source_target_pairs={{0,5},{1,4},{2,7},{3,6},{4,1},{5,0},{6,3},{7,2},{8,13},{9,12},{10,... | collective-permute-start | bytes 786440 | tf_op jit(solution)/shard_map/ppermute | solution.py:360
  247.6 31.6 %collective-permute-start.35 = (bf16[32,32,128]{2,1,0:T(8,128)(2,1)S(1)}, bf16[32,32,128]{2,1,0:T(8,128)(2,1)S(1)}, u32[]{:S(2)}, u32[]{:S(2)}) collective-permute-start(bf16[32,32,128]{2,1,0:T(8,128)(2,1)S(1)} %get-tuple-element.162), channel_id=1, source_target_pairs={{0,6},{1,7},{2,4},{3,5},{4,2},{5,3},{6,0},{7,1},{8,14},{9,15},{10,... | collective-permute-start | bytes 786440 | tf_op jit(solution)/shard_map/ppermute | solution.py:360
  248.1 39.2 %collective-permute-start.36 = (bf16[32,32,128]{2,1,0:T(8,128)(2,1)S(1)}, bf16[32,32,128]{2,1,0:T(8,128)(2,1)S(1)}, u32[]{:S(2)}, u32[]{:S(2)}) collective-permute-start(bf16[32,32,128]{2,1,0:T(8,128)(2,1)S(1)} %get-tuple-element.163), channel_id=1, source_target_pairs={{0,7},{1,6},{2,5},{3,4},{4,3},{5,2},{6,1},{7,0},{8,15},{9,14},{10,... | collective-permute-start | bytes 786440 | tf_op jit(solution)/shard_map/ppermute | solution.py:360
  251.2 64.1 %collective-permute-start.51 = (bf16[32,32,128]{2,1,0:T(8,128)(2,1)S(1)}, bf16[32,32,128]{2,1,0:T(8,128)(2,1)S(1)}, u32[]{:S(2)}, u32[]{:S(2)}) collective-permute-start(bf16[32,32,128]{2,1,0:T(8,128)(2,1)S(1)} %get-tuple-element.183), channel_id=1, source_target_pairs={{0,1},{1,0},{2,3},{3,2},{4,5},{5,4},{6,7},{7,6},{8,9},{9,8},{10,11... | collective-permute-start | bytes 786440 | tf_op jit(solution)/shard_map/ppermute | solution.py:360
  274.7 42.3 %collective-permute-start.52 = (bf16[32,32,128]{2,1,0:T(8,128)(2,1)S(1)}, bf16[32,32,128]{2,1,0:T(8,128)(2,1)S(1)}, u32[]{:S(2)}, u32[]{:S(2)}) collective-permute-start(bf16[32,32,128]{2,1,0:T(8,128)(2,1)S(1)} %get-tuple-element.184), channel_id=1, source_target_pairs={{0,2},{1,3},{2,0},{3,1},{4,6},{5,7},{6,4},{7,5},{8,10},{9,11},{10,... | collective-permute-start | bytes 786440 | tf_op jit(solution)/shard_map/ppermute | solution.py:360
  278.7 49.4 %collective-permute-start.53 = (bf16[32,32,128]{2,1,0:T(8,128)(2,1)S(1)}, bf16[32,32,128]{2,1,0:T(8,128)(2,1)S(1)}, u32[]{:S(2)}, u32[]{:S(2)}) collective-permute-start(bf16[32,32,128]{2,1,0:T(8,128)(2,1)S(1)} %get-tuple-element.185), channel_id=1, source_target_pairs={{0,3},{1,2},{2,1},{3,0},{4,7},{5,6},{6,5},{7,4},{8,11},{9,10},{10,... | collective-permute-start | bytes 786440 | tf_op jit(solution)/shard_map/ppermute | solution.py:360
  279.2 49.5 %collective-permute-start.54 = (bf16[32,32,128]{2,1,0:T(8,128)(2,1)S(1)}, bf16[32,32,128]{2,1,0:T(8,128)(2,1)S(1)}, u32[]{:S(2)}, u32[]{:S(2)}) collective-permute-start(bf16[32,32,128]{2,1,0:T(8,128)(2,1)S(1)} %get-tuple-element.186), channel_id=1, source_target_pairs={{0,4},{1,5},{2,6},{3,7},{4,0},{5,1},{6,2},{7,3},{8,12},{9,13},{10,... | collective-permute-start | bytes 786440 | tf_op jit(solution)/shard_map/ppermute | solution.py:360
  287.3 41.4 %collective-permute-start.55 = (bf16[32,32,128]{2,1,0:T(8,128)(2,1)S(1)}, bf16[32,32,128]{2,1,0:T(8,128)(2,1)S(1)}, u32[]{:S(2)}, u32[]{:S(2)}) collective-permute-start(bf16[32,32,128]{2,1,0:T(8,128)(2,1)S(1)} %get-tuple-element.187), channel_id=1, source_target_pairs={{0,5},{1,4},{2,7},{3,6},{4,1},{5,0},{6,3},{7,2},{8,13},{9,12},{10,... | collective-permute-start | bytes 786440 | tf_op jit(solution)/shard_map/ppermute | solution.py:360
  317.0 19.0 %collective-permute-start.57 = (bf16[32,32,128]{2,1,0:T(8,128)(2,1)S(1)}, bf16[32,32,128]{2,1,0:T(8,128)(2,1)S(1)}, u32[]{:S(2)}, u32[]{:S(2)}) collective-permute-start(bf16[32,32,128]{2,1,0:T(8,128)(2,1)S(1)} %get-tuple-element.189), channel_id=1, source_target_pairs={{0,7},{1,6},{2,5},{3,4},{4,3},{5,2},{6,1},{7,0},{8,15},{9,14},{10,... | collective-permute-start | bytes 786440 | tf_op jit(solution)/shard_map/ppermute | solution.py:360
  328.2 15.7 %collective-permute-start.72 = (bf16[32,16,128]{2,1,0:T(8,128)(2,1)S(1)}, bf16[32,16,128]{2,1,0:T(8,128)(2,1)S(1)}, u32[]{:S(2)}, u32[]{:S(2)}) collective-permute-start(bf16[32,16,128]{2,1,0:T(8,128)(2,1)S(1)} %get-tuple-element.210), channel_id=1, source_target_pairs={{0,1},{1,0},{2,3},{3,2},{4,5},{5,4},{6,7},{7,6},{8,9},{9,8},{10,11... | collective-permute-start | bytes 393224 | tf_op jit(solution)/shard_map/ppermute | solution.py:360
  328.7 16.2 %collective-permute-start.73 = (bf16[32,16,128]{2,1,0:T(8,128)(2,1)S(1)}, bf16[32,16,128]{2,1,0:T(8,128)(2,1)S(1)}, u32[]{:S(2)}, u32[]{:S(2)}) collective-permute-start(bf16[32,16,128]{2,1,0:T(8,128)(2,1)S(1)} %get-tuple-element.211), channel_id=1, source_target_pairs={{0,2},{1,3},{2,0},{3,1},{4,6},{5,7},{6,4},{7,5},{8,10},{9,11},{10,... | collective-permute-start | bytes 393224 | tf_op jit(solution)/shard_map/ppermute | solution.py:360
  328.7 16.3 %collective-permute-start.74 = (bf16[32,16,128]{2,1,0:T(8,128)(2,1)S(1)}, bf16[32,16,128]{2,1,0:T(8,128)(2,1)S(1)}, u32[]{:S(2)}, u32[]{:S(2)}) collective-permute-start(bf16[32,16,128]{2,1,0:T(8,128)(2,1)S(1)} %get-tuple-element.212), channel_id=1, source_target_pairs={{0,3},{1,2},{2,1},{3,0},{4,7},{5,6},{6,5},{7,4},{8,11},{9,10},{10,... | collective-permute-start | bytes 393224 | tf_op jit(solution)/shard_map/ppermute | solution.py:360
  330.1 27.2 %collective-permute-start.75 = (bf16[32,16,128]{2,1,0:T(8,128)(2,1)S(1)}, bf16[32,16,128]{2,1,0:T(8,128)(2,1)S(1)}, u32[]{:S(2)}, u32[]{:S(2)}) collective-permute-start(bf16[32,16,128]{2,1,0:T(8,128)(2,1)S(1)} %get-tuple-element.213), channel_id=1, source_target_pairs={{0,4},{1,5},{2,6},{3,7},{4,0},{5,1},{6,2},{7,3},{8,12},{9,13},{10,... | collective-permute-start | bytes 393224 | tf_op jit(solution)/shard_map/ppermute | solution.py:360
  336.0 24.8 %collective-permute-start.76 = (bf16[32,16,128]{2,1,0:T(8,128)(2,1)S(1)}, bf16[32,16,128]{2,1,0:T(8,128)(2,1)S(1)}, u32[]{:S(2)}, u32[]{:S(2)}) collective-permute-start(bf16[32,16,128]{2,1,0:T(8,128)(2,1)S(1)} %get-tuple-element.214), channel_id=1, source_target_pairs={{0,5},{1,4},{2,7},{3,6},{4,1},{5,0},{6,3},{7,2},{8,13},{9,12},{10,... | collective-permute-start | bytes 393224 | tf_op jit(solution)/shard_map/ppermute | solution.py:360
  343.9 17.6 %collective-permute-start.77 = (bf16[32,16,128]{2,1,0:T(8,128)(2,1)S(1)}, bf16[32,16,128]{2,1,0:T(8,128)(2,1)S(1)}, u32[]{:S(2)}, u32[]{:S(2)}) collective-permute-start(bf16[32,16,128]{2,1,0:T(8,128)(2,1)S(1)} %get-tuple-element.215), channel_id=1, source_target_pairs={{0,6},{1,7},{2,4},{3,5},{4,2},{5,3},{6,0},{7,1},{8,14},{9,15},{10,... | collective-permute-start | bytes 393224 | tf_op jit(solution)/shard_map/ppermute | solution.py:360
  344.9 27.8 %collective-permute-start.65 = (bf16[32,32,128]{2,1,0:T(8,128)(2,1)S(1)}, bf16[32,32,128]{2,1,0:T(8,128)(2,1)S(1)}, u32[]{:S(2)}, u32[]{:S(2)}) collective-permute-start(bf16[32,32,128]{2,1,0:T(8,128)(2,1)S(1)} %get-tuple-element.201), channel_id=1, source_target_pairs={{0,1},{1,0},{2,3},{3,2},{4,5},{5,4},{6,7},{7,6},{8,9},{9,8},{10,11... | collective-permute-start | bytes 786440 | tf_op jit(solution)/shard_map/ppermute | solution.py:360
  345.7 29.9 %collective-permute-start.66 = (bf16[32,32,128]{2,1,0:T(8,128)(2,1)S(1)}, bf16[32,32,128]{2,1,0:T(8,128)(2,1)S(1)}, u32[]{:S(2)}, u32[]{:S(2)}) collective-permute-start(bf16[32,32,128]{2,1,0:T(8,128)(2,1)S(1)} %get-tuple-element.202), channel_id=1, source_target_pairs={{0,2},{1,3},{2,0},{3,1},{4,6},{5,7},{6,4},{7,5},{8,10},{9,11},{10,... | collective-permute-start | bytes 786440 | tf_op jit(solution)/shard_map/ppermute | solution.py:360
  365.9 21.3 %collective-permute-start.67 = (bf16[32,32,128]{2,1,0:T(8,128)(2,1)}, bf16[32,32,128]{2,1,0:T(8,128)(2,1)S(1)}, u32[]{:S(2)}, u32[]{:S(2)}) collective-permute-start(bf16[32,32,128]{2,1,0:T(8,128)(2,1)} %get-tuple-element.203), channel_id=1, source_target_pairs={{0,3},{1,2},{2,1},{3,0},{4,7},{5,6},{6,5},{7,4},{8,11},{9,10},{10,... | collective-permute-start | bytes 786440 | tf_op jit(solution)/shard_map/ppermute | solution.py:360
  369.7 33.0 %collective-permute-start.68 = (bf16[32,32,128]{2,1,0:T(8,128)(2,1)}, bf16[32,32,128]{2,1,0:T(8,128)(2,1)}, u32[]{:S(2)}, u32[]{:S(2)}) collective-permute-start(bf16[32,32,128]{2,1,0:T(8,128)(2,1)} %get-tuple-element.204), channel_id=1, source_target_pairs={{0,4},{1,5},{2,6},{3,7},{4,0},{5,1},{6,2},{7,3},{8,12},{9,13},{10,... | collective-permute-start | bytes 786440 | tf_op jit(solution)/shard_map/ppermute | solution.py:360
  371.7 37.7 %collective-permute-start.69 = (bf16[32,32,128]{2,1,0:T(8,128)(2,1)}, bf16[32,32,128]{2,1,0:T(8,128)(2,1)}, u32[]{:S(2)}, u32[]{:S(2)}) collective-permute-start(bf16[32,32,128]{2,1,0:T(8,128)(2,1)} %get-tuple-element.205), channel_id=1, source_target_pairs={{0,5},{1,4},{2,7},{3,6},{4,1},{5,0},{6,3},{7,2},{8,13},{9,12},{10,... | collective-permute-start | bytes 786440 | tf_op jit(solution)/shard_map/ppermute | solution.py:360
  372.7 36.6 %collective-permute-start.70 = (bf16[32,32,128]{2,1,0:T(8,128)(2,1)}, bf16[32,32,128]{2,1,0:T(8,128)(2,1)}, u32[]{:S(2)}, u32[]{:S(2)}) collective-permute-start(bf16[32,32,128]{2,1,0:T(8,128)(2,1)} %get-tuple-element.206), channel_id=1, source_target_pairs={{0,6},{1,7},{2,4},{3,5},{4,2},{5,3},{6,0},{7,1},{8,14},{9,15},{10,... | collective-permute-start | bytes 786440 | tf_op jit(solution)/shard_map/ppermute | solution.py:360
  375.5 37.1 %collective-permute-start.71 = (bf16[32,32,128]{2,1,0:T(8,128)(2,1)}, bf16[32,32,128]{2,1,0:T(8,128)(2,1)}, u32[]{:S(2)}, u32[]{:S(2)}) collective-permute-start(bf16[32,32,128]{2,1,0:T(8,128)(2,1)} %get-tuple-element.207), channel_id=1, source_target_pairs={{0,7},{1,6},{2,5},{3,4},{4,3},{5,2},{6,1},{7,0},{8,15},{9,14},{10,... | collective-permute-start | bytes 786440 | tf_op jit(solution)/shard_map/ppermute | solution.py:360
  387.2 34.9 %collective-permute-start.81 = (bf16[32,16,128]{2,1,0:T(8,128)(2,1)}, bf16[32,16,128]{2,1,0:T(8,128)(2,1)S(1)}, u32[]{:S(2)}, u32[]{:S(2)}) collective-permute-start(bf16[32,16,128]{2,1,0:T(8,128)(2,1)} %copy-done.29), channel_id=1, source_target_pairs={{0,3},{1,2},{2,1},{3,0},{4,7},{5,6},{6,5},{7,4},{8,11},{9,10},{10,... | collective-permute-start | bytes 393224 | tf_op jit(solution)/shard_map/ppermute | solution.py:360
  402.7 30.7 %collective-permute-start.82 = (bf16[32,16,128]{2,1,0:T(8,128)(2,1)}, bf16[32,16,128]{2,1,0:T(8,128)(2,1)S(1)}, u32[]{:S(2)}, u32[]{:S(2)}) collective-permute-start(bf16[32,16,128]{2,1,0:T(8,128)(2,1)} %copy-done.28), channel_id=1, source_target_pairs={{0,4},{1,5},{2,6},{3,7},{4,0},{5,1},{6,2},{7,3},{8,12},{9,13},{10,... | collective-permute-start | bytes 393224 | tf_op jit(solution)/shard_map/ppermute | solution.py:360
  409.3 25.2 %collective-permute-start.83 = (bf16[32,16,128]{2,1,0:T(8,128)(2,1)}, bf16[32,16,128]{2,1,0:T(8,128)(2,1)S(1)}, u32[]{:S(2)}, u32[]{:S(2)}) collective-permute-start(bf16[32,16,128]{2,1,0:T(8,128)(2,1)} %copy-done.27), channel_id=1, source_target_pairs={{0,5},{1,4},{2,7},{3,6},{4,1},{5,0},{6,3},{7,2},{8,13},{9,12},{10,... | collective-permute-start | bytes 393224 | tf_op jit(solution)/shard_map/ppermute | solution.py:360
  409.3 25.2 %collective-permute-start.84 = (bf16[32,16,128]{2,1,0:T(8,128)(2,1)}, bf16[32,16,128]{2,1,0:T(8,128)(2,1)S(1)}, u32[]{:S(2)}, u32[]{:S(2)}) collective-permute-start(bf16[32,16,128]{2,1,0:T(8,128)(2,1)} %copy-done.26), channel_id=1, source_target_pairs={{0,6},{1,7},{2,4},{3,5},{4,2},{5,3},{6,0},{7,1},{8,14},{9,15},{10,... | collective-permute-start | bytes 393224 | tf_op jit(solution)/shard_map/ppermute | solution.py:360
  412.6 21.9 %collective-permute-start.85 = (bf16[32,16,128]{2,1,0:T(8,128)(2,1)}, bf16[32,16,128]{2,1,0:T(8,128)(2,1)S(1)}, u32[]{:S(2)}, u32[]{:S(2)}) collective-permute-start(bf16[32,16,128]{2,1,0:T(8,128)(2,1)} %copy-done.25), channel_id=1, source_target_pairs={{0,7},{1,6},{2,5},{3,4},{4,3},{5,2},{6,1},{7,0},{8,15},{9,14},{10,... | collective-permute-start | bytes 393224 | tf_op jit(solution)/shard_map/ppermute | solution.py:360
  (56 other events, 542.7 us)

commit v3 on v2

--- a/solution.py
+++ b/solution.py
@@ -93,7 +93,7 @@
         fill(est32, shot + 2, cut(est_ref, shot))
         return carry
 
-    lax.fori_loop(0, shots, load, 0)
+    lax.fori_loop(0, shots, load, 0, unroll=2)
 
     def residual(place, values):
         shot = first + place - 1
@@ -121,7 +121,7 @@
         energy_ref[pl.ds(shot, 1), :] = jnp.sum(power, axis=0, keepdims=True)
         return carry
 
-    lax.fori_loop(0, shots, middle, 0)
+    lax.fori_loop(0, shots, middle, 0, unroll=2)
 
     def step(shot, carry):
         later, earlier = blended(res32, shot + 1, first + shot)
@@ -135,15 +135,19 @@
             store(shot, column, cell.astype(jnp.bfloat16))
         return carry
 
-    lax.fori_loop(0, shots, step, 0)
+    lax.fori_loop(0, shots, step, 0, unroll=2)
+
+
+def blocks_in(near_ref, far_refs):
+    return [near_ref.at[index] for index in range(near_ref.shape[0])] + list(far_refs)
 
 
 def spectra_kernel(
-    first_ref, delay_ref, est_ref, obs_ref, before_ref, after_ref, table_ref, _, *refs
+    first_ref, delay_ref, est_ref, obs_ref, before_ref, after_ref, table_ref, order_ref, _, *refs
 ):
-    *out_refs, energy_ref, est32, res32, stepped = refs
+    near_ref, *far_refs, energy_ref, est32, res32, stepped, result = refs
     shots, rows, samples = est_ref.shape
-    width = out_refs[0].shape[2]
+    width = near_ref.shape[3]
 
     def store(shot, column, values):
         start = pl.multiple_of(shot * rows, rows)
@@ -152,17 +156,17 @@
     blend_into(
         first_ref, delay_ref, est_ref, obs_ref, before_ref, after_ref, energy_ref, est32, res32, store
     )
-    group = min(shots, max(1, 256 // rows))
+    held = result.shape[0]
+    group = held // rows
 
     def transform(part, carry):
-        start = pl.multiple_of(part * (group * rows), group * rows)
-        result = jnp.dot(
-            stepped[pl.ds(start, group * rows), :], table_ref[...], preferred_element_type=jnp.float32
+        start = pl.multiple_of(part * held, held)
+        result[...] = jnp.dot(
+            stepped[pl.ds(start, held), :], table_ref[...], preferred_element_type=jnp.float32
         ).astype(jnp.bfloat16)
-        for slot, out_ref in enumerate(out_refs):
-            out_ref[pl.ds(part * group, group)] = result[
-                :, slot * width : (slot + 1) * width
-            ].reshape(group, rows, width)
+        for slot, out_ref in enumerate(blocks_in(near_ref, far_refs)):
+            lanes = pl.ds(pl.multiple_of(order_ref[slot] * width, width), width)
+            out_ref[pl.ds(part * group, group)] = result[:, lanes].reshape(group, rows, width)
         return carry
 
     lax.fori_loop(0, shots // group, transform, 0)
@@ -179,16 +183,19 @@
     )
 
 
-def shots_kernel(across_ref, back_ref, level_ref, _, *refs):
-    peers = (len(refs) - 2) // 2
-    spectra_refs, out_refs, (wide, back) = refs[:peers], refs[peers : 2 * peers], refs[2 * peers :]
-    held, rows, width = spectra_refs[0].shape
-    shots = peers * held
+def shots_kernel(order_ref, table_ref, level_ref, _, *refs):
+    *refs, wide, back = refs
+    spectra_refs, out_refs = refs[: len(refs) // 2], refs[len(refs) // 2 :]
+    _, held, rows, width = spectra_refs[0].shape
+    shots = wide.shape[0] // rows
     half = width // 2
-    for slot, ref in enumerate(spectra_refs):
-        wide[pl.ds(slot * held * rows, held * rows), :] = (
-            ref[...].reshape(held * rows, width).astype(jnp.float32)
-        )
+
+    def place(slot):
+        size = held * rows
+        return pl.ds(pl.multiple_of(order_ref[slot] * size, size), size)
+
+    for slot, ref in enumerate(blocks_in(spectra_refs[0], spectra_refs[1:])):
+        wide[place(slot), :] = ref[...].reshape(held * rows, width).astype(jnp.float32)
     level = level_ref[...]
     sign = jnp.where(
         lax.broadcasted_iota(jnp.int32, (1, width), 1) < half, jnp.float32(1.0), jnp.float32(-1.0)
@@ -197,7 +204,7 @@
     def pair(index, carry):
         picks = [pl.ds(index * 2 + turn, shots, stride=rows) for turn in range(2)]
         block = jnp.concatenate([wide[pick, :] for pick in picks], axis=1).astype(jnp.bfloat16)
-        both = jnp.dot(across_ref[...], block, preferred_element_type=jnp.float32)
+        both = jnp.dot(table_ref[...], block, preferred_element_type=jnp.float32)
         kept = []
         for turn in range(2):
             own = both[:, turn * width : (turn + 1) * width]
@@ -206,26 +213,26 @@
             power = power + pltpu.roll(power, half, 1)
             factor = jnp.maximum(1.0 - level * lax.rsqrt(power), 0.0)
             kept.append((wave * factor).astype(jnp.bfloat16))
-        both = jnp.dot(back_ref[...], jnp.concatenate(kept, axis=1), preferred_element_type=jnp.float32)
+        both = jnp.dot(table_ref[...], jnp.concatenate(kept, axis=1), preferred_element_type=jnp.float32)
         for turn in range(2):
             own = both[:, turn * width : (turn + 1) * width]
             back[picks[turn], :] = own[:shots] - sign * pltpu.roll(own[shots:], half, 1)
         return carry
 
-    lax.fori_loop(0, rows // 2, pair, 0)
-    for slot, ref in enumerate(out_refs):
-        ref[...] = (
-            back[pl.ds(slot * held * rows, held * rows), :].astype(jnp.bfloat16).reshape(ref.shape)
-        )
-
-
-def update_kernel(peers, table_ref, _, *refs):
-    restored_refs, (out_ref, turn_ref) = refs[:peers], refs[-2:]
-    held, rows, width = restored_refs[0].shape
-    block = jnp.concatenate(
-        [ref[...].reshape(held * rows, width) for ref in restored_refs], axis=1
-    )
-    out_ref[...] = jnp.dot(block, table_ref[...], preferred_element_type=jnp.float32).reshape(out_ref.shape)
+    lax.fori_loop(0, rows // 2, pair, 0, unroll=2)
+    for slot, ref in enumerate(blocks_in(out_refs[0], out_refs[1:])):
+        ref[...] = back[place(slot), :].astype(jnp.bfloat16).reshape(held, rows, width)
+
+
+def update_kernel(inputs, order_ref, table_ref, _, *refs):
+    restored_refs, (out_ref, turn_ref, whole_rows) = refs[:inputs], refs[-3:]
+    _, held, rows, width = restored_refs[0].shape
+    for slot, ref in enumerate(blocks_in(restored_refs[0], restored_refs[1:])):
+        lanes = pl.ds(pl.multiple_of(order_ref[slot] * width, width), width)
+        whole_rows[:, lanes] = ref[...].reshape(held * rows, width)
+    out_ref[...] = jnp.dot(
+        whole_rows[...], table_ref[...], preferred_element_type=jnp.float32
+    ).reshape(out_ref.shape)
     turn_ref[...] = jnp.zeros_like(turn_ref)
 
 
@@ -233,15 +240,16 @@
     return pl.BlockSpec(shape, lambda *_: (0,) * len(shape))
 
 
-def blend_specs(shots, rows, samples, chunk):
+def blend_specs(shots, rows, samples, chunk, edge_chunk):
     at = lambda *_: (0, chunk, 0)
+    edge = lambda *_: (0, edge_chunk, 0)
     return [
         pl.BlockSpec(memory_space=pltpu.SMEM),
         pl.BlockSpec(memory_space=pltpu.SMEM),
         pl.BlockSpec((shots, rows, samples), at),
         pl.BlockSpec((shots, rows, samples), at),
-        pl.BlockSpec((HALO, rows, samples), at),
-        pl.BlockSpec((HALO, rows, samples), at),
+        pl.BlockSpec((HALO, rows, samples), edge),
+        pl.BlockSpec((HALO, rows, samples), edge),
     ]
 
 
@@ -259,18 +267,28 @@
 ANYWHERE = pl.BlockSpec(memory_space=pl.ANY)
 
 
-def spectra_of(first, delays, fields, table, rows, chunk, peers, after):
+SCALARS = pl.BlockSpec(memory_space=pltpu.SMEM)
+
+
+def spectra_of(first, delays, fields, table, order, rows, chunk, edge_chunk, after):
     shots, _, samples = fields[0].shape
+    peers = order.shape[0]
     block = (shots, rows, 2 * F // peers)
+    blocks = [(peers // 2,) + block] + [block] * (peers - peers // 2)
+    group = min(shots, max(1, 256 // rows))
     *spectra, energy = pl.pallas_call(
         spectra_kernel,
         grid=(1,),
-        in_specs=blend_specs(shots, rows, samples, chunk) + [whole(table.shape), ANYWHERE],
-        out_specs=[whole(block)] * peers + [whole((shots, LANES))],
-        out_shape=[jax.ShapeDtypeStruct(block, jnp.bfloat16)] * peers
+        in_specs=blend_specs(shots, rows, samples, chunk, edge_chunk)
+        + [whole(table.shape), SCALARS, ANYWHERE],
+        out_specs=[whole(shape) for shape in blocks] + [whole((shots, LANES))],
+        out_shape=[jax.ShapeDtypeStruct(shape, jnp.bfloat16) for shape in blocks]
         + [jax.ShapeDtypeStruct((shots, LANES), jnp.float32)],
         scratch_shapes=blend_scratch(shots, rows, samples)
-        + [pltpu.VMEM((shots * rows, samples), jnp.bfloat16)],
+        + [
+            pltpu.VMEM((shots * rows, samples), jnp.bfloat16),
+            pltpu.VMEM((group * rows, 2 * F), jnp.bfloat16),
+        ],
         compiler_params=PARAMS,
         cost_estimate=pl.CostEstimate(
             flops=4 * F * shots * rows * samples,
@@ -278,7 +296,7 @@
             transcendentals=0,
         ),
         name="spectra",
-    )(first, delays, *fields, table, after)
+    )(first, delays, *fields, table, order, after)
     return spectra, energy
 
 
@@ -287,7 +305,7 @@
     return pl.pallas_call(
         step_kernel,
         grid=(1,),
-        in_specs=blend_specs(shots, rows, samples, chunk),
+        in_specs=blend_specs(shots, rows, samples, chunk, chunk),
         out_specs=[whole((shots, rows, samples)), whole((shots, LANES))],
         out_shape=[
             jax.ShapeDtypeStruct((shots, rows, samples), jnp.bfloat16),
@@ -299,40 +317,39 @@
     )(first, delays, *fields)
 
 
-def shrunk_of(spectra, across, back, level, after):
-    held, rows, width = spectra[0].shape
-    peers = len(spectra)
-    shots = peers * held
-    size = spectra[0].size * peers
+def shrunk_of(spectra, table, level, order, after):
+    _, held, rows, width = spectra[0].shape
+    shots = order.shape[0] * held
+    size = shots * rows * width
     return pl.pallas_call(
         shots_kernel,
         grid=(1,),
-        in_specs=[whole(across.shape), whole(back.shape), whole(level.shape), ANYWHERE]
-        + [whole(spectra[0].shape)] * peers,
-        out_specs=[whole(spectra[0].shape)] * peers,
-        out_shape=[jax.ShapeDtypeStruct(spectra[0].shape, jnp.bfloat16)] * peers,
+        in_specs=[SCALARS, whole(table.shape), whole(level.shape), ANYWHERE]
+        + [whole(block.shape) for block in spectra],
+        out_specs=[whole(block.shape) for block in spectra],
+        out_shape=[jax.ShapeDtypeStruct(block.shape, jnp.bfloat16) for block in spectra],
         scratch_shapes=[pltpu.VMEM((shots * rows, width), jnp.float32)] * 2,
         compiler_params=PARAMS,
         cost_estimate=pl.CostEstimate(
-            flops=8 * shots * size, bytes_accessed=4 * size + 4 * across.size, transcendentals=size
+            flops=8 * shots * size, bytes_accessed=4 * size + 2 * table.size, transcendentals=size
         ),
         name="shrink",
-    )(across, back, level, after, *spectra)
-
-
-def updated_of(restored, table, chunk, receivers, onto, after):
-    shots, rows, width = restored[0].shape
-    peers = len(restored)
+    )(order, table, level, after, *spectra)
+
+
+def updated_of(restored, table, order, chunk, receivers, onto, after):
+    near, shots, rows, width = restored[0].shape
     samples = table.shape[1]
     group = min(shots, max(1, 256 // rows))
-    in_specs = [whole(table.shape), ANYWHERE]
-    in_specs += [pl.BlockSpec((group, rows, width), lambda step: (step, 0, 0))] * peers
-    operands = [table, after, *restored]
+    in_specs = [SCALARS, whole(table.shape), ANYWHERE]
+    in_specs += [pl.BlockSpec((near, group, rows, width), lambda step: (0, step, 0, 0))]
+    in_specs += [pl.BlockSpec((group, rows, width), lambda step: (step, 0, 0))] * (len(restored) - 1)
+    operands = [order, table, after, *restored]
     if onto is not None:
         in_specs.append(ANYWHERE)
         operands.append(onto)
     return pl.pallas_call(
-        functools.partial(update_kernel, peers),
+        functools.partial(update_kernel, len(restored)),
         grid=(shots // group,),
         in_specs=in_specs,
         out_specs=[
@@ -343,11 +360,12 @@
             jax.ShapeDtypeStruct((shots, receivers, samples), jnp.float32),
             jax.ShapeDtypeStruct((8, LANES), jnp.float32),
         ],
+        scratch_shapes=[pltpu.VMEM((group * rows, 2 * F), jnp.bfloat16)],
         input_output_aliases={} if onto is None else {len(operands) - 1: 0},
         compiler_params=PARAMS,
         cost_estimate=pl.CostEstimate(
             flops=4 * F * shots * rows * samples,
-            bytes_accessed=2 * restored[0].size * peers + 2 * table.size + 4 * shots * rows * samples,
+            bytes_accessed=4 * F * shots * rows + 2 * table.size + 4 * shots * rows * samples,
             transcendentals=0,
         ),
         name="update",
@@ -355,18 +373,41 @@
 
 
 def exchanged(blocks):
-    peers = len(blocks)
-    return [
-        block if slot == 0 else lax.ppermute(block, "shot", [(i, i ^ slot) for i in range(peers)])
-        for slot, block in enumerate(blocks)
+    near, *far = blocks
+    half = near.shape[0]
+    peers = half + len(far)
+    far = [
+        lax.ppermute(block, "shot", [(i, i ^ (half + slot)) for i in range(peers)])
+        for slot, block in enumerate(far)
     ]
+    groups = [list(range(half)), list(range(half, peers))]
+    near = lax.all_to_all(
+        near, "shot", split_axis=0, concat_axis=0, axis_index_groups=groups, tiled=True
+    )
+    return [near, *far]
+
+
+def peers_of(rank, peers):
+    half = peers // 2
+    near = rank // half * half + jnp.arange(half, dtype=jnp.int32)
+    return jnp.concatenate([near, rank ^ jnp.arange(half, peers, dtype=jnp.int32)])
 
 
 def chunks_of(receivers):
     if receivers == 128:
-        return [(16, 0), (16, 1), (32, 1), (32, 2), (16, 6), (16, 7)]
+        return [(16, 7), (16, 6), (32, 1), (32, 2), (16, 1), (16, 0)]
     rows = min(16, receivers)
-    return [(rows, index) for index in range(receivers // rows)]
+    return [(rows, index) for index in range(receivers // rows)][::-1]
+
+
+def edges(estimate, observed, start, stop):
+    peers = lax.axis_size("shot")
+    up = [(i, i + 1) for i in range(peers - 1)]
+    down = [(j, i) for i, j in up]
+    estimate, observed = estimate[:, start:stop], observed[:, start:stop]
+    tail = jnp.concatenate([estimate[-2:], observed[-1:]])
+    head = jnp.concatenate([estimate[:2], observed[:1]])
+    return lax.ppermute(tail, "shot", up), lax.ppermute(head, "shot", down)
 
 
 def swapped(array):
@@ -411,28 +452,16 @@
     total = random_source_delays.shape[0]
     share = F // peers
     first = jnp.reshape(rank * shots, (1,)).astype(jnp.int32)
-    up = [(i, i + 1) for i in range(peers - 1)]
-    down = [(j, i) for i, j in up]
-    tail = jnp.concatenate([estimate[shots - 2 :], observed[shots - 1 :]])
-    head = jnp.concatenate([estimate[:2], observed[:1]])
-    before = lax.ppermute(tail, "shot", up)
-    after = lax.ppermute(head, "shot", down)
-    fields = (estimate, observed, before, after)
     forward, inverse = (jnp.asarray(table) for table in time_tables(samples, peers))
     table = jnp.asarray(shot_table(total))
     level = lax.dynamic_slice_in_dim(thresholds, rank * share, share)
     chunks = chunks_of(receivers)
+    head_rows = chunks[0][0]
+    early = edges(estimate, observed, receivers - head_rows, receivers)
+    late = edges(estimate, observed, 0, receivers - head_rows) if len(chunks) > 1 else None
     energy = 0.0
     if (2 * share) % LANES == 0 and peers & (peers - 1) == 0:
-        order = rank ^ jnp.arange(peers, dtype=jnp.int32)
-        forward = jnp.take(forward.reshape(samples, peers, 2 * share), order, axis=1)
-        forward = forward.reshape(samples, 2 * F)
-        inverse = jnp.take(inverse.reshape(peers, 2 * share, samples), order, axis=0)
-        inverse = inverse.reshape(2 * F, samples)
-        across = jnp.take(table.reshape(2 * total, peers, shots), order, axis=1)
-        across = across.reshape(2 * total, total)
-        back = jnp.take(table.reshape(2, peers, shots, total), order, axis=1)
-        back = back.reshape(2 * total, total)
+        order = peers_of(rank, peers)
         levels = jnp.tile(level, 2)[None, :]
         updated, last = None, levels
         lag = 2
@@ -440,30 +469,42 @@
         for turn in range(len(chunks) + 2 * lag):
             if turn < len(chunks):
                 rows, index = chunks[turn]
+                sides, edge_index = (late, index) if turn else (early, 0)
                 spectra, power = spectra_of(
-                    first, random_source_delays, fields, forward, rows, index, peers, last
+                    first,
+                    random_source_delays,
+                    (estimate, observed, *sides),
+                    forward,
+                    order,
+                    rows,
+                    index,
+                    edge_index,
+                    last,
                 )
                 last = power
                 energy = energy + power
                 ahead[turn] = exchanged(spectra)
             place = turn - lag
             if place in ahead:
-                shrunk = shrunk_of(ahead.pop(place), across, back, levels, last)
-                last = shrunk[0]
+                shrunk = shrunk_of(ahead.pop(place), table, levels, order, last)
+                last = shrunk[1]
                 behind[place] = exchanged(shrunk)
             place = turn - 2 * lag
             if place in behind:
                 updated, last = updated_of(
-                    behind.pop(place), inverse, chunks[place][1], receivers, updated, last
+                    behind.pop(place), inverse, order, chunks[place][1], receivers, updated, last
                 )
     else:
-        parts = []
+        sides = [jnp.concatenate(pair, axis=1) for pair in zip(late, early)] if late else early
+        parts = {}
         for rows, index in chunks:
-            part, power = stepped_of(first, random_source_delays, fields, rows, index)
+            part, power = stepped_of(
+                first, random_source_delays, (estimate, observed, *sides), rows, index
+            )
             energy = energy + power
-            parts.append(part)
+            parts[index * rows] = part
         updated = spectral_by_einsum(
-            jnp.concatenate(parts, axis=1), forward, inverse, table, level, peers
+            jnp.concatenate([parts[start] for start in sorted(parts)], axis=1), forward, inverse, table, level, peers
         )
     misfit = lax.psum(jnp.sum(energy, axis=1), "patch") / (
         receivers * lax.axis_size("patch") * samples

time: 442 us -> 590 us (1.33)
  blocking collectives: 9.92 us -> 78.3 us
  starting transfers between devices: 149 us -> 211 us
  local copies, waits for them, and re-layouts: 18.8 us -> 62.9 us
  Pallas kernels: 159 us -> 132 us
    all_to_all x0 -> x4, blocking collectives: none -> 68.3 us  [exchanged(): lax.all_to_all(near, 'shot', split_axis=0, concat_axis=0, axis_index_grou...]
    unnamed x68 -> x208, local copies, waits for them, and re-layouts: 7.35 us -> 58.1 us
    all_to_all x0 -> x8, starting transfers between devices: none -> 36.3 us  [exchanged(): lax.all_to_all(near, 'shot', split_axis=0, concat_axis=0, axis_index_grou...]
    ppermute x86 -> x52, starting transfers between devices: 149 us -> 175 us  [the longest x48 165 us: exchanged(): lax.ppermute(block, 'shot', [(i, i ^ half + slot) for i in range(peers)])]
    pallas_call x6, Pallas kernels: 78.3 us -> 61.9 us  [spectra_of(): pl.pallas_call(spectra_kernel, grid=(1,), in_specs=blend_specs(shots, row...]
    pallas_call x12, Pallas kernels: 80.5 us -> 70.4 us  [the longest x6 45.2 us: shrunk_of(): pl.pallas_call(shots_kernel, grid=(1,), in_specs=[SCALARS, whole(table.sh...]
    gather x6 -> x0, local copies, waits for them, and re-layouts: 7.84 us -> none  [the longest x1 3.86 us: local(): jnp.take(forward.reshape(samples, peers, 2 * share), order, axis=1)]
    ppermute x86 -> x52, waiting for transfers between devices: 93.7 us -> 97.6 us  [the longest x48 97.6 us: exchanged(): lax.ppermute(block, 'shot', [(i, i ^ half + slot) for i in range(peers)])]
  transfers between devices with their start and end apart: 86 -> 60, of which waited for: 20 -> 14; matrix products, arithmetic and copies ran while one was open for 3% -> 1% of each run, Pallas kernels for 33% -> 22%
where the time goes in v3:
time: 590 us; the launch traced here: 588 us
  starting transfers between devices  211 us (36%)
  Pallas kernels  132 us (22%)
  waiting for transfers between devices  97.7 us (17%)
  blocking collectives  78.3 us (13%)
  local copies, waits for them, and re-layouts  62.9 us (11%)
    ppermute x48, starting transfers between devices, exchanged(): lax.ppermute(block, 'shot', [(i, i ^ half + slot) for i in range(peers)])  165 us
    ppermute x48, waiting for transfers between devices, exchanged(): lax.ppermute(block, 'shot', [(i, i ^ half + slot) for i in range(peers)])  97.6 us
    all_to_all x4, blocking collectives, exchanged(): lax.all_to_all(near, 'shot', split_axis=0, concat_axis=0, axis_index_grou...  68.3 us
    pallas_call x6, Pallas kernels, spectra_of(): pl.pallas_call(spectra_kernel, grid=(1,), in_specs=blend_specs(shots, row...  61.9 us
    unnamed x208, local copies, waits for them, and re-layouts  58.1 us
    pallas_call x6, Pallas kernels, shrunk_of(): pl.pallas_call(shots_kernel, grid=(1,), in_specs=[SCALARS, whole(table.sh...  45.2 us
    all_to_all x8, starting transfers between devices, exchanged(): lax.all_to_all(near, 'shot', split_axis=0, concat_axis=0, axis_index_grou...  36.3 us
    pallas_call x6, Pallas kernels, updated_of(): pl.pallas_call(functools.partial(update_kernel, len(restored)), grid=(sho...  25.3 us
  transfers between devices with their start and end apart: 60, of which 14 were waited for; matrix products, arithmetic and copies ran while one was open for 1% of the time, Pallas kernels for 22%

profile of v3, /device:TPU:0, one launch (start us, length us, event | category | flops | bytes accessed | tf_op | source)
XLA Modules:
  0.0 587.8 jit_solution(11956565581906050095)
XLA Ops:
  2.3 2.4 collective-permute-start.2
  9.2 5.2 collective-permute-start
  23.0 9.0 %spectra.6 = (bf16[4,32,16,128]{3,2,1,0:T(8,128)(2,1)S(1)}, bf16[32,16,128]{2,1,0:T(8,128)(2,1)S(1)}, bf16[32,16,128]{2,1,0:T(8,128)(2,1)S(1)}, bf16[32,16,128]{...) custom-call(s32[1]{0:T(128)} %bitcast.first_ref, s32[256]{0:T(256)S(1)} %copy-done.46, ...), custom_call_target="tpu_custom_call" | custom-call | flops 1073741824 | bytes 5242880 | tf_op jit(solution)/shard_map/spectra/pallas_call | solution.py:279
  35.4 5.2 all-to-all-start
  40.6 8.8 %spectra.7 = (bf16[4,32,16,128]{3,2,1,0:T(8,128)(2,1)S(1)}, bf16[32,16,128]{2,1,0:T(8,128)(2,1)S(1)}, bf16[32,16,128]{2,1,0:T(8,128)(2,1)S(1)}, bf16[32,16,128]{...) custom-call(s32[1]{0:T(128)} %bitcast.first_ref, s32[256]{0:T(256)S(1)} %copy-done.47, ...), custom_call_target="tpu_custom_call" | custom-call | flops 1073741824 | bytes 5242880 | tf_op jit(solution)/shard_map/spectra/pallas_call | solution.py:279
  52.9 4.2 all-to-all-start.1
  57.0 4.0 collective-permute-start.4
  61.1 3.7 collective-permute-start.6
  65.0 13.2 %spectra.8 = (bf16[4,32,32,128]{3,2,1,0:T(8,128)(2,1)S(1)}, bf16[32,32,128]{2,1,0:T(8,128)(2,1)S(1)}, bf16[32,32,128]{2,1,0:T(8,128)(2,1)S(1)}, bf16[32,32,128]{...) custom-call(s32[1]{0:T(128)} %bitcast.first_ref, s32[256]{0:T(256)S(1)} %copy-done.47, ...), custom_call_target="tpu_custom_call" | custom-call | flops 2147483648 | bytes 8388608 | tf_op jit(solution)/shard_map/spectra/pallas_call | solution.py:279
  82.1 5.3 shrink.6
  91.4 14.2 %all_to_all.60.refs_0_ = bf16[4,32,16,128]{3,2,1,0:T(8,128)(2,1)} all-to-all(bf16[4,32,16,128]{3,2,1,0:T(8,128)(2,1)} %copy-done.19), channel_id=1, replica_groups={{0,1,2,3},{4,5,6,7},{8,9,10,11},{12,13,14,15},{16,17,18,19},{20,21,22,2..., dimensions={0} | all-to-all | bytes 1048576 | tf_op jit(solution)/shard_map/all_to_all | solution.py:384
  105.7 4.2 all-to-all-start.2
  109.9 3.8 collective-permute-start.8
  113.7 3.7 collective-permute-start.10
  118.6 13.2 %spectra.9 = (bf16[4,32,32,128]{3,2,1,0:T(8,128)(2,1)S(1)}, bf16[32,32,128]{2,1,0:T(8,128)(2,1)S(1)}, bf16[32,32,128]{2,1,0:T(8,128)(2,1)S(1)}, bf16[32,32,128]{...) custom-call(s32[1]{0:T(128)} %bitcast.first_ref, s32[256]{0:T(256)S(1)} %copy-done.47, ...), custom_call_target="tpu_custom_call" | custom-call | flops 2147483648 | bytes 8388608 | tf_op jit(solution)/shard_map/spectra/pallas_call | solution.py:279
  138.2 5.3 shrink.7
  146.9 4.1 all-to-all-start.5
  151.9 8.8 %spectra.10 = (bf16[4,32,16,128]{3,2,1,0:T(8,128)(2,1)S(1)}, bf16[32,16,128]{2,1,0:T(8,128)(2,1)S(1)}, bf16[32,16,128]{2,1,0:T(8,128)(2,1)S(1)}, bf16[32,16,128]...) custom-call(s32[1]{0:T(128)} %bitcast.first_ref, s32[256]{0:T(256)S(1)} %copy-done.47, ...), custom_call_target="tpu_custom_call" | custom-call | flops 1073741824 | bytes 5242880 | tf_op jit(solution)/shard_map/spectra/pallas_call | solution.py:279
  164.2 13.0 %all_to_all.61.refs_0_ = bf16[4,32,16,128]{3,2,1,0:T(8,128)(2,1)} all-to-all(bf16[4,32,16,128]{3,2,1,0:T(8,128)(2,1)} %copy-done.20), channel_id=1, replica_groups={{0,1,2,3},{4,5,6,7},{8,9,10,11},{12,13,14,15},{16,17,18,19},{20,21,22,2..., dimensions={0} | all-to-all | bytes 1048576 | tf_op jit(solution)/shard_map/all_to_all | solution.py:384
  177.2 4.4 all-to-all-start.4
  184.2 2.6 collective-permute-start.14
  187.9 11.9 %collective-permute-done.12.refs_1_ = bf16[32,32,128]{2,1,0:T(8,128)(2,1)S(1)} collective-permute-done((bf16[32,32,128]{2,1,0:T(8,128)(2,1)}, bf16[32,32,128]{2,1,0:T(8,128)(2,1)S(1)}, u32[]{:S(2)}, u32[]{:S(2)}) %collective-permute-start.12) | collective-permute-done | bytes 262176 | tf_op jit(solution)/shard_map/ppermute | solution.py:380
  199.8 2.4 collective-permute-start.17
  202.2 3.2 collective-permute-done.13.refs_2_
  205.5 21.3 %collective-permute-start.18 = (bf16[32,16,128]{2,1,0:T(8,128)(2,1)}, bf16[32,16,128]{2,1,0:T(8,128)(2,1)S(1)}, u32[]{:S(2)}, u32[]{:S(2)}) collective-permute-start(bf16[32,16,128]{2,1,0:T(8,128)(2,1)} %copy-done.82), channel_id=1, source_target_pairs={{0,6},{1,7},{2,4},{3,5},{4,2},{5,3},{6,0},{7,1},{8,14},{9,15},{10,... | collective-permute-start | bytes 393224 | tf_op jit(solution)/shard_map/ppermute | solution.py:380
  228.7 14.1 %collective-permute-start.20 = (bf16[32,32,128]{2,1,0:T(8,128)(2,1)}, bf16[32,32,128]{2,1,0:T(8,128)(2,1)}, u32[]{:S(2)}, u32[]{:S(2)}) collective-permute-start(bf16[32,32,128]{2,1,0:T(8,128)(2,1)} %copy-done.65), channel_id=1, source_target_pairs={{0,4},{1,5},{2,6},{3,7},{4,0},{5,1},{6,2},{7,3},{8,12},{9,13},{10,... | collective-permute-start | bytes 786440 | tf_op jit(solution)/shard_map/ppermute | solution.py:380
  243.7 12.2 %shrink.8 = (bf16[4,32,32,128]{3,2,1,0:T(8,128)(2,1)S(1)}, bf16[32,32,128]{2,1,0:T(8,128)(2,1)S(1)}, bf16[32,32,128]{2,1,0:T(8,128)(2,1)S(1)}, bf16[32,32,128]{2,1,0:T(8,128)(2,1)S(1)}, bf16[32,32,128]{2,1,0:T(8,128)(2,1)S(1)}) custom-call(s32[8]{0:T(128)S(1)} %pad_add_fusion.order_ref, bf16[512,256]{1,0:T(8,128)(2,1)S(1)} %copy-done.100, ...), custom_call_target="tpu_custom_call" | custom-call | flops 2147483648 | bytes 4456448 | tf_op jit(solution)/shard_map/shrink/pallas_call | solution.py:324
  260.6 3.2 update.6
  263.9 8.8 %spectra.11 = (bf16[4,32,16,128]{3,2,1,0:T(8,128)(2,1)S(1)}, bf16[32,16,128]{2,1,0:T(8,128)(2,1)S(1)}, bf16[32,16,128]{2,1,0:T(8,128)(2,1)S(1)}, bf16[32,16,128]...) custom-call(s32[1]{0:T(128)} %bitcast.first_ref, s32[256]{0:T(256)S(1)} %copy-done.47, ...), custom_call_target="tpu_custom_call" | custom-call | flops 1073741824 | bytes 5242880 | tf_op jit(solution)/shard_map/spectra/pallas_call | solution.py:279
  276.2 4.3 all-to-all-start.8
  280.5 4.1 collective-permute-start.22
  285.0 2.9 collective-permute-start.26
  288.2 9.3 %collective-permute-done.22.refs_3_ = bf16[32,32,128]{2,1,0:T(8,128)(2,1)S(1)} collective-permute-done((bf16[32,32,128]{2,1,0:T(8,128)(2,1)}, bf16[32,32,128]{2,1,0:T(8,128)(2,1)S(1)}, u32[]{:S(2)}, u32[]{:S(2)}) %collective-permute-start.22) | collective-permute-done | bytes 262176 | tf_op jit(solution)/shard_map/ppermute | solution.py:380
  297.5 14.7 %collective-permute-start.24 = (bf16[32,16,128]{2,1,0:T(8,128)(2,1)}, bf16[32,16,128]{2,1,0:T(8,128)(2,1)S(1)}, u32[]{:S(2)}, u32[]{:S(2)}) collective-permute-start(bf16[32,16,128]{2,1,0:T(8,128)(2,1)} %copy-done.21), channel_id=1, source_target_pairs={{0,4},{1,5},{2,6},{3,7},{4,0},{5,1},{6,2},{7,3},{8,12},{9,13},{10,... | collective-permute-start | bytes 393224 | tf_op jit(solution)/shard_map/ppermute | solution.py:380
  312.2 7.3 %collective-permute-start.28 = (bf16[32,16,128]{2,1,0:T(8,128)(2,1)}, bf16[32,16,128]{2,1,0:T(8,128)(2,1)S(1)}, u32[]{:S(2)}, u32[]{:S(2)}) collective-permute-start(bf16[32,16,128]{2,1,0:T(8,128)(2,1)} %copy-done.73), channel_id=1, source_target_pairs={{0,4},{1,5},{2,6},{3,7},{4,0},{5,1},{6,2},{7,3},{8,12},{9,13},{10,... | collective-permute-start | bytes 393224 | tf_op jit(solution)/shard_map/ppermute | solution.py:380
  320.5 2.7 collective-permute-start.30
  326.1 12.3 %shrink.9 = (bf16[4,32,32,128]{3,2,1,0:T(8,128)(2,1)S(1)}, bf16[32,32,128]{2,1,0:T(8,128)(2,1)S(1)}, bf16[32,32,128]{2,1,0:T(8,128)(2,1)S(1)}, bf16[32,32,128]{2,1,0:T(8,128)(2,1)S(1)}, bf16[32,32,128]{2,1,0:T(8,128)(2,1)S(1)}) custom-call(s32[8]{0:T(128)S(1)} %pad_add_fusion.order_ref, bf16[512,256]{1,0:T(8,128)(2,1)S(1)} %copy-done.101, ...), custom_call_target="tpu_custom_call" | custom-call | flops 2147483648 | bytes 4456448 | tf_op jit(solution)/shard_map/shrink/pallas_call | solution.py:324
  339.4 2.4 collective-permute-done.24.refs_1_
  341.8 3.8 update.7
  346.8 4.8 shrink.10
  354.3 23.5 %all_to_all.62.refs_0_ = bf16[4,32,16,128]{3,2,1,0:T(8,128)(2,1)} all-to-all(bf16[4,32,16,128]{3,2,1,0:T(8,128)(2,1)} %copy-done.18), channel_id=1, replica_groups={{0,1,2,3},{4,5,6,7},{8,9,10,11},{12,13,14,15},{16,17,18,19},{20,21,22,2..., dimensions={0} | all-to-all | bytes 1048576 | tf_op jit(solution)/shard_map/all_to_all | solution.py:384
  377.8 17.6 %all_to_all.63.refs_0_ = bf16[4,32,32,128]{3,2,1,0:T(8,128)(2,1)} all-to-all(bf16[4,32,32,128]{3,2,1,0:T(8,128)(2,1)S(1)} %copy-done.7), channel_id=1, replica_groups={{0,1,2,3},{4,5,6,7},{8,9,10,11},{12,13,14,15},{16,17,18,19},{20,21,22,2..., dimensions={0} | all-to-all | bytes 2097152 | tf_op jit(solution)/shard_map/all_to_all | solution.py:384
  395.4 3.5 all-to-all-start.9
  398.9 2.9 collective-permute-start.33
  405.0 2.9 collective-permute-start.36
  407.9 9.3 %collective-permute-done.33.refs_2_ = bf16[32,32,128]{2,1,0:T(8,128)(2,1)S(1)} collective-permute-done((bf16[32,32,128]{2,1,0:T(8,128)(2,1)}, bf16[32,32,128]{2,1,0:T(8,128)(2,1)S(1)}, u32[]{:S(2)}, u32[]{:S(2)}) %collective-permute-start.33) | collective-permute-done | bytes 262176 | tf_op jit(solution)/shard_map/ppermute | solution.py:380
  417.2 2.8 collective-permute-start.37
  419.9 7.4 %collective-permute-done.34.refs_3_ = bf16[32,32,128]{2,1,0:T(8,128)(2,1)S(1)} collective-permute-done((bf16[32,32,128]{2,1,0:T(8,128)(2,1)}, bf16[32,32,128]{2,1,0:T(8,128)(2,1)S(1)}, u32[]{:S(2)}, u32[]{:S(2)}) %collective-permute-start.34) | collective-permute-done | bytes 262176 | tf_op jit(solution)/shard_map/ppermute | solution.py:380
  427.3 4.7 collective-permute-done.35.refs_4_
  432.1 27.7 %collective-permute-done.32.refs_1_ = bf16[32,32,128]{2,1,0:T(8,128)(2,1)S(1)} collective-permute-done((bf16[32,32,128]{2,1,0:T(8,128)(2,1)}, bf16[32,32,128]{2,1,0:T(8,128)(2,1)S(1)}, u32[]{:S(2)}, u32[]{:S(2)}) %collective-permute-start.32) | collective-permute-done | bytes 262176 | tf_op jit(solution)/shard_map/ppermute | solution.py:380
  461.6 5.1 update.8
  466.8 5.3 shrink.11
  475.5 6.4 %all-to-all-start.11 = ((bf16[4,32,16,128]{3,2,1,0:T(8,128)(2,1)}), bf16[4,32,16,128]{3,2,1,0:T(8,128)(2,1)}, u32[]{:S(2)}, u32[]{:S(2)}) async-start(bf16[4,32,16,128]{3,2,1,0:T(8,128)(2,1)} %copy-done.13), calls=%async_computation.11 | async-start | bytes 1048576 | tf_op jit(solution)/shard_map/all_to_all | solution.py:384
  481.9 4.4 collective-permute-start.45
  489.8 2.7 collective-permute-start.42
  493.1 24.4 %collective-permute-start.43 = (bf16[32,32,128]{2,1,0:T(8,128)(2,1)}, bf16[32,32,128]{2,1,0:T(8,128)(2,1)}, u32[]{:S(2)}, u32[]{:S(2)}) collective-permute-start(bf16[32,32,128]{2,1,0:T(8,128)(2,1)} %copy-done.56), channel_id=1, source_target_pairs={{0,7},{1,6},{2,5},{3,4},{4,3},{5,2},{6,1},{7,0},{8,15},{9,14},{10,... | collective-permute-start | bytes 786440 | tf_op jit(solution)/shard_map/ppermute | solution.py:380
  518.9 10.0 %psum.7 = f32[32]{0:T(128)S(1)} all-reduce(f32[32]{0:T(128)} %add_reduce_fusion), channel_id=1, replica_groups=mesh['patch'=4,'shot'=8] {'patch'}, use_global_device_ids=true, to_apply=%region_1.2 | all-reduce | flops 32 | bytes 256 | tf_op jit(solution)/shard_map/psum | solution.py:509
  529.5 6.4 %collective-permute-done.47.refs_4_ = bf16[32,16,128]{2,1,0:T(8,128)(2,1)S(1)} collective-permute-done((bf16[32,16,128]{2,1,0:T(8,128)(2,1)}, bf16[32,16,128]{2,1,0:T(8,128)(2,1)S(1)}, u32[]{:S(2)}, u32[]{:S(2)}) %collective-permute-start.47) | collective-permute-done | bytes 131104 | tf_op jit(solution)/shard_map/ppermute | solution.py:380
  535.9 16.5 %collective-permute-start.44 = (bf16[32,16,128]{2,1,0:T(8,128)(2,1)S(1)}, bf16[32,16,128]{2,1,0:T(8,128)(2,1)S(1)}, u32[]{:S(2)}, u32[]{:S(2)}) collective-permute-start(bf16[32,16,128]{2,1,0:T(8,128)(2,1)S(1)} %get-tuple-element.125._), channel_id=1, source_target_pairs={{0,4},{1,5},{2,6},{3,7},{4,0},{5,1},{6,2},{7,3},{8,12},{9,13},{10,... | collective-permute-start | bytes 393224 | tf_op jit(solution)/shard_map/ppermute | solution.py:380
  558.3 5.9 %update.9 = (f32[32,128,1024]{2,1,0:T(8,128)}, f32[8,128]{1,0:T(8,128)S(1)}) custom-call(s32[8]{0:T(128)S(1)} %copy-done.44, bf16[1024,1024]{1,0:T(8,128)(2,1)S(1)} %copy-done.3, bf16[32,16,128]{2,1,0:T(8,128)(2,1)S(1)} %copy-done.26, bf16[4,32,32,128]{3,2,1,0:T(8,128)(2,1)S(1)} %all-to-all-done.9.refs_0_, ...), custom_call_target="tpu_custom_call", output_to_operand_aliasing={{0}: (8, {})} | custom-call | flops 2147483648 | bytes 8388608 | tf_op jit(solution)/shard_map/update/pallas_call | solution.py:351
  564.3 6.3 %collective-permute-done.44.refs_1_ = bf16[32,16,128]{2,1,0:T(8,128)(2,1)S(1)} collective-permute-done((bf16[32,16,128]{2,1,0:T(8,128)(2,1)S(1)}, bf16[32,16,128]{2,1,0:T(8,128)(2,1)S(1)}, u32[]{:S(2)}, u32[]{:S(2)}) %collective-permute-start.44) | collective-permute-done | bytes 131104 | tf_op jit(solution)/shard_map/ppermute | solution.py:380
  570.6 3.6 update.10
  576.1 5.4 collective-permute-done.48.refs_1_
  584.2 3.6 update.11
  (302 shorter events, 94.3 us)
Async XLA Ops:
  2.3 15.3 %collective-permute-start.2 = (bf16[3,16,1024]{2,1,0:T(8,128)(2,1)S(1)}, bf16[3,16,1024]{2,1,0:T(8,128)(2,1)S(1)}, u32[]{:S(2)}, u32[]{:S(2)}) collective-permute-start(bf16[3,16,1024]{2,1,0:T(8,128)(2,1)S(1)} %pad_maximum_fusion.2), channel_id=1, source_target_pairs={{0,1},{1,2},{2,3},{3,4},{4,5},{5,6},{6,7},{8,9},{9,10},{10,11},{11... | collective-permute-start | bytes 294920 | tf_op jit(solution)/shard_map/ppermute | solution.py:410
  4.7 13.6 %collective-permute-start.3 = (bf16[3,16,1024]{2,1,0:T(8,128)(2,1)S(1)}, bf16[3,16,1024]{2,1,0:T(8,128)(2,1)S(1)}, u32[]{:S(2)}, u32[]{:S(2)}) collective-permute-start(bf16[3,16,1024]{2,1,0:T(8,128)(2,1)S(1)} %pad_maximum_fusion.3), channel_id=1, source_target_pairs={{1,0},{2,1},{3,2},{4,3},{5,4},{6,5},{7,6},{9,8},{10,9},{11,10},{12... | collective-permute-start | bytes 294920 | tf_op jit(solution)/shard_map/ppermute | solution.py:410
  9.2 31.3 %collective-permute-start = (bf16[3,112,1024]{2,1,0:T(8,128)(2,1)}, bf16[3,112,1024]{2,1,0:T(8,128)(2,1)S(1)}, u32[]{:S(2)}, u32[]{:S(2)}) collective-permute-start(bf16[3,112,1024]{2,1,0:T(8,128)(2,1)} %pad_maximum_fusion), channel_id=1, source_target_pairs={{0,1},{1,2},{2,3},{3,4},{4,5},{5,6},{6,7},{8,9},{9,10},{10,11},{11... | collective-permute-start | bytes 2064392 | tf_op jit(solution)/shard_map/ppermute | solution.py:410
  15.4 25.2 %collective-permute-start.1 = (bf16[3,112,1024]{2,1,0:T(8,128)(2,1)}, bf16[3,112,1024]{2,1,0:T(8,128)(2,1)S(1)}, u32[]{:S(2)}, u32[]{:S(2)}) collective-permute-start(bf16[3,112,1024]{2,1,0:T(8,128)(2,1)} %pad_maximum_fusion.1), channel_id=1, source_target_pairs={{1,0},{2,1},{3,2},{4,3},{5,4},{6,5},{7,6},{9,8},{10,9},{11,10},{12... | collective-permute-start | bytes 2064392 | tf_op jit(solution)/shard_map/ppermute | solution.py:410
  17.6 307.5 %copy-start.52 = (f32[1,128]{1,0:T(1,128)}, f32[1,128]{1,0:T(1,128)S(1)}, u32[]{:S(2)}) copy-start(f32[1,128]{1,0:T(1,128)S(1)} %broadcast_in_dim_tile.3._.level_ref) | copy-start | bytes 1540
  35.4 17.5 %all-to-all-start = ((bf16[4,32,16,128]{3,2,1,0:T(8,128)(2,1)}), bf16[4,32,16,128]{3,2,1,0:T(8,128)(2,1)}, u32[]{:S(2)}, u32[]{:S(2)}) async-start(bf16[4,32,16,128]{3,2,1,0:T(8,128)(2,1)} %copy-done.16), calls=%async_computation | async-start | bytes 1048576 | tf_op jit(solution)/shard_map/all_to_all | solution.py:384
  52.9 38.6 %all-to-all-start.1 = ((bf16[4,32,16,128]{3,2,1,0:T(8,128)(2,1)}), bf16[4,32,16,128]{3,2,1,0:T(8,128)(2,1)}, u32[]{:S(2)}, u32[]{:S(2)}) async-start(bf16[4,32,16,128]{3,2,1,0:T(8,128)(2,1)} %copy-done.15), calls=%async_computation.1 | async-start | bytes 1048576 | tf_op jit(solution)/shard_map/all_to_all | solution.py:384
  57.0 25.1 %collective-permute-start.4 = (bf16[32,16,128]{2,1,0:T(8,128)(2,1)}, bf16[32,16,128]{2,1,0:T(8,128)(2,1)S(1)}, u32[]{:S(2)}, u32[]{:S(2)}) collective-permute-start(bf16[32,16,128]{2,1,0:T(8,128)(2,1)} %copy-done.97), channel_id=1, source_target_pairs={{0,4},{1,5},{2,6},{3,7},{4,0},{5,1},{6,2},{7,3},{8,12},{9,13},{10,... | collective-permute-start | bytes 393224 | tf_op jit(solution)/shard_map/ppermute | solution.py:380
  61.0 21.1 %collective-permute-start.5 = (bf16[32,16,128]{2,1,0:T(8,128)(2,1)}, bf16[32,16,128]{2,1,0:T(8,128)(2,1)S(1)}, u32[]{:S(2)}, u32[]{:S(2)}) collective-permute-start(bf16[32,16,128]{2,1,0:T(8,128)(2,1)} %copy-done.96), channel_id=1, source_target_pairs={{0,5},{1,4},{2,7},{3,6},{4,1},{5,0},{6,3},{7,2},{8,13},{9,12},{10,... | collective-permute-start | bytes 393224 | tf_op jit(solution)/shard_map/ppermute | solution.py:380
  61.1 21.0 %collective-permute-start.6 = (bf16[32,16,128]{2,1,0:T(8,128)(2,1)}, bf16[32,16,128]{2,1,0:T(8,128)(2,1)S(1)}, u32[]{:S(2)}, u32[]{:S(2)}) collective-permute-start(bf16[32,16,128]{2,1,0:T(8,128)(2,1)} %copy-done.95), channel_id=1, source_target_pairs={{0,6},{1,7},{2,4},{3,5},{4,2},{5,3},{6,0},{7,1},{8,14},{9,15},{10,... | collective-permute-start | bytes 393224 | tf_op jit(solution)/shard_map/ppermute | solution.py:380
  64.7 17.3 %collective-permute-start.7 = (bf16[32,16,128]{2,1,0:T(8,128)(2,1)}, bf16[32,16,128]{2,1,0:T(8,128)(2,1)S(1)}, u32[]{:S(2)}, u32[]{:S(2)}) collective-permute-start(bf16[32,16,128]{2,1,0:T(8,128)(2,1)} %copy-done.94), channel_id=1, source_target_pairs={{0,7},{1,6},{2,5},{3,4},{4,3},{5,2},{6,1},{7,0},{8,15},{9,14},{10,... | collective-permute-start | bytes 393224 | tf_op jit(solution)/shard_map/ppermute | solution.py:380
  105.7 41.2 %all-to-all-start.2 = ((bf16[4,32,32,128]{3,2,1,0:T(8,128)(2,1)}), bf16[4,32,32,128]{3,2,1,0:T(8,128)(2,1)}, u32[]{:S(2)}, u32[]{:S(2)}) async-start(bf16[4,32,32,128]{3,2,1,0:T(8,128)(2,1)} %copy-done.10), calls=%async_computation.2 | async-start | bytes 2097152 | tf_op jit(solution)/shard_map/all_to_all | solution.py:384
  109.9 25.8 %collective-permute-start.8 = (bf16[32,16,128]{2,1,0:T(8,128)(2,1)}, bf16[32,16,128]{2,1,0:T(8,128)(2,1)S(1)}, u32[]{:S(2)}, u32[]{:S(2)}) collective-permute-start(bf16[32,16,128]{2,1,0:T(8,128)(2,1)} %copy-done.93), channel_id=1, source_target_pairs={{0,4},{1,5},{2,6},{3,7},{4,0},{5,1},{6,2},{7,3},{8,12},{9,13},{10,... | collective-permute-start | bytes 393224 | tf_op jit(solution)/shard_map/ppermute | solution.py:380
  113.7 22.0 %collective-permute-start.9 = (bf16[32,16,128]{2,1,0:T(8,128)(2,1)}, bf16[32,16,128]{2,1,0:T(8,128)(2,1)S(1)}, u32[]{:S(2)}, u32[]{:S(2)}) collective-permute-start(bf16[32,16,128]{2,1,0:T(8,128)(2,1)} %copy-done.92), channel_id=1, source_target_pairs={{0,5},{1,4},{2,7},{3,6},{4,1},{5,0},{6,3},{7,2},{8,13},{9,12},{10,... | collective-permute-start | bytes 393224 | tf_op jit(solution)/shard_map/ppermute | solution.py:380
  113.7 22.6 %collective-permute-start.10 = (bf16[32,16,128]{2,1,0:T(8,128)(2,1)}, bf16[32,16,128]{2,1,0:T(8,128)(2,1)S(1)}, u32[]{:S(2)}, u32[]{:S(2)}) collective-permute-start(bf16[32,16,128]{2,1,0:T(8,128)(2,1)} %copy-done.91), channel_id=1, source_target_pairs={{0,6},{1,7},{2,4},{3,5},{4,2},{5,3},{6,0},{7,1},{8,14},{9,15},{10,... | collective-permute-start | bytes 393224 | tf_op jit(solution)/shard_map/ppermute | solution.py:380
  117.4 20.8 %collective-permute-start.11 = (bf16[32,16,128]{2,1,0:T(8,128)(2,1)}, bf16[32,16,128]{2,1,0:T(8,128)(2,1)S(1)}, u32[]{:S(2)}, u32[]{:S(2)}) collective-permute-start(bf16[32,16,128]{2,1,0:T(8,128)(2,1)} %copy-done.90), channel_id=1, source_target_pairs={{0,7},{1,6},{2,5},{3,4},{4,3},{5,2},{6,1},{7,0},{8,15},{9,14},{10,... | collective-permute-start | bytes 393224 | tf_op jit(solution)/shard_map/ppermute | solution.py:380
  146.9 17.3 %all-to-all-start.5 = ((bf16[4,32,16,128]{3,2,1,0:T(8,128)(2,1)}), bf16[4,32,16,128]{3,2,1,0:T(8,128)(2,1)}, u32[]{:S(2)}, u32[]{:S(2)}) async-start(bf16[4,32,16,128]{3,2,1,0:T(8,128)(2,1)} %copy-done.17), calls=%async_computation.5 | async-start | bytes 1048576 | tf_op jit(solution)/shard_map/all_to_all | solution.py:384
  164.2 108.6 %copy-start.50 = (f32[32,128]{1,0:T(8,128)}, f32[32,128]{1,0:T(8,128)S(1)}, u32[]{:S(2)}) copy-start(f32[32,128]{1,0:T(8,128)S(1)} %get-tuple-element.95._) | copy-start | bytes 49156
  177.2 99.0 %all-to-all-start.4 = ((bf16[4,32,32,128]{3,2,1,0:T(8,128)(2,1)}), bf16[4,32,32,128]{3,2,1,0:T(8,128)(2,1)}, u32[]{:S(2)}, u32[]{:S(2)}) async-start(bf16[4,32,32,128]{3,2,1,0:T(8,128)(2,1)} %copy-done.8), calls=%async_computation.4 | async-start | bytes 2097152 | tf_op jit(solution)/shard_map/all_to_all | solution.py:384
  181.6 18.2 %collective-permute-start.12 = (bf16[32,32,128]{2,1,0:T(8,128)(2,1)}, bf16[32,32,128]{2,1,0:T(8,128)(2,1)S(1)}, u32[]{:S(2)}, u32[]{:S(2)}) collective-permute-start(bf16[32,32,128]{2,1,0:T(8,128)(2,1)} %copy-done.69), channel_id=1, source_target_pairs={{0,4},{1,5},{2,6},{3,7},{4,0},{5,1},{6,2},{7,3},{8,12},{9,13},{10,... | collective-permute-start | bytes 786440 | tf_op jit(solution)/shard_map/ppermute | solution.py:380
  183.2 22.3 %collective-permute-start.13 = (bf16[32,32,128]{2,1,0:T(8,128)(2,1)}, bf16[32,32,128]{2,1,0:T(8,128)(2,1)S(1)}, u32[]{:S(2)}, u32[]{:S(2)}) collective-permute-start(bf16[32,32,128]{2,1,0:T(8,128)(2,1)} %copy-done.68), channel_id=1, source_target_pairs={{0,5},{1,4},{2,7},{3,6},{4,1},{5,0},{6,3},{7,2},{8,13},{9,12},{10,... | collective-permute-start | bytes 786440 | tf_op jit(solution)/shard_map/ppermute | solution.py:380
  184.2 42.6 %collective-permute-start.14 = (bf16[32,32,128]{2,1,0:T(8,128)(2,1)}, bf16[32,32,128]{2,1,0:T(8,128)(2,1)S(1)}, u32[]{:S(2)}, u32[]{:S(2)}) collective-permute-start(bf16[32,32,128]{2,1,0:T(8,128)(2,1)} %copy-done.67), channel_id=1, source_target_pairs={{0,6},{1,7},{2,4},{3,5},{4,2},{5,3},{6,0},{7,1},{8,14},{9,15},{10,... | collective-permute-start | bytes 786440 | tf_op jit(solution)/shard_map/ppermute | solution.py:380
  186.8 41.9 %collective-permute-start.15 = (bf16[32,32,128]{2,1,0:T(8,128)(2,1)}, bf16[32,32,128]{2,1,0:T(8,128)(2,1)S(1)}, u32[]{:S(2)}, u32[]{:S(2)}) collective-permute-start(bf16[32,32,128]{2,1,0:T(8,128)(2,1)} %copy-done.66), channel_id=1, source_target_pairs={{0,7},{1,6},{2,5},{3,4},{4,3},{5,2},{6,1},{7,0},{8,15},{9,14},{10,... | collective-permute-start | bytes 786440 | tf_op jit(solution)/shard_map/ppermute | solution.py:380
  187.9 70.1 %collective-permute-start.16 = (bf16[32,16,128]{2,1,0:T(8,128)(2,1)}, bf16[32,16,128]{2,1,0:T(8,128)(2,1)S(1)}, u32[]{:S(2)}, u32[]{:S(2)}) collective-permute-start(bf16[32,16,128]{2,1,0:T(8,128)(2,1)} %copy-done.23), channel_id=1, source_target_pairs={{0,4},{1,5},{2,6},{3,7},{4,0},{5,1},{6,2},{7,3},{8,12},{9,13},{10,... | collective-permute-start | bytes 393224 | tf_op jit(solution)/shard_map/ppermute | solution.py:380
  199.8 57.1 %collective-permute-start.17 = (bf16[32,16,128]{2,1,0:T(8,128)(2,1)}, bf16[32,16,128]{2,1,0:T(8,128)(2,1)S(1)}, u32[]{:S(2)}, u32[]{:S(2)}) collective-permute-start(bf16[32,16,128]{2,1,0:T(8,128)(2,1)} %copy-done.84), channel_id=1, source_target_pairs={{0,5},{1,4},{2,7},{3,6},{4,1},{5,0},{6,3},{7,2},{8,13},{9,12},{10,... | collective-permute-start | bytes 393224 | tf_op jit(solution)/shard_map/ppermute | solution.py:380
  205.5 52.5 %collective-permute-start.18 = (bf16[32,16,128]{2,1,0:T(8,128)(2,1)}, bf16[32,16,128]{2,1,0:T(8,128)(2,1)S(1)}, u32[]{:S(2)}, u32[]{:S(2)}) collective-permute-start(bf16[32,16,128]{2,1,0:T(8,128)(2,1)} %copy-done.82), channel_id=1, source_target_pairs={{0,6},{1,7},{2,4},{3,5},{4,2},{5,3},{6,0},{7,1},{8,14},{9,15},{10,... | collective-permute-start | bytes 393224 | tf_op jit(solution)/shard_map/ppermute | solution.py:380
  226.8 31.2 %collective-permute-start.19 = (bf16[32,16,128]{2,1,0:T(8,128)(2,1)}, bf16[32,16,128]{2,1,0:T(8,128)(2,1)S(1)}, u32[]{:S(2)}, u32[]{:S(2)}) collective-permute-start(bf16[32,16,128]{2,1,0:T(8,128)(2,1)} %copy-done.81), channel_id=1, source_target_pairs={{0,7},{1,6},{2,5},{3,4},{4,3},{5,2},{6,1},{7,0},{8,15},{9,14},{10,... | collective-permute-start | bytes 393224 | tf_op jit(solution)/shard_map/ppermute | solution.py:380
  228.7 56.3 %collective-permute-start.20 = (bf16[32,32,128]{2,1,0:T(8,128)(2,1)}, bf16[32,32,128]{2,1,0:T(8,128)(2,1)}, u32[]{:S(2)}, u32[]{:S(2)}) collective-permute-start(bf16[32,32,128]{2,1,0:T(8,128)(2,1)} %copy-done.65), channel_id=1, source_target_pairs={{0,4},{1,5},{2,6},{3,7},{4,0},{5,1},{6,2},{7,3},{8,12},{9,13},{10,... | collective-permute-start | bytes 786440 | tf_op jit(solution)/shard_map/ppermute | solution.py:380
  256.9 30.9 %collective-permute-start.21 = (bf16[32,32,128]{2,1,0:T(8,128)(2,1)}, bf16[32,32,128]{2,1,0:T(8,128)(2,1)}, u32[]{:S(2)}, u32[]{:S(2)}) collective-permute-start(bf16[32,32,128]{2,1,0:T(8,128)(2,1)} %copy-done.64), channel_id=1, source_target_pairs={{0,5},{1,4},{2,7},{3,6},{4,1},{5,0},{6,3},{7,2},{8,13},{9,12},{10,... | collective-permute-start | bytes 786440 | tf_op jit(solution)/shard_map/ppermute | solution.py:380
  276.2 69.4 %copy-start.51 = (f32[32,128]{1,0:T(8,128)}, f32[32,128]{1,0:T(8,128)S(1)}, u32[]{:S(2)}) copy-start(f32[32,128]{1,0:T(8,128)S(1)} %get-tuple-element.107._) | copy-start | bytes 49156
  276.2 65.6 %copy-start.3 = (bf16[1024,1024]{1,0:T(8,128)(2,1)S(1)}, bf16[1024,1024]{1,0:T(8,128)(2,1)}, u32[]{:S(2)}) copy-start(bf16[1024,1024]{1,0:T(8,128)(2,1)} %constant.41.clone.table_ref) | copy-start | bytes 6291460
  276.2 78.2 %all-to-all-start.8 = ((bf16[4,32,16,128]{3,2,1,0:T(8,128)(2,1)}), bf16[4,32,16,128]{3,2,1,0:T(8,128)(2,1)}, u32[]{:S(2)}, u32[]{:S(2)}) async-start(bf16[4,32,16,128]{3,2,1,0:T(8,128)(2,1)} %copy-done.14), calls=%async_computation.8 | async-start | bytes 1048576 | tf_op jit(solution)/shard_map/all_to_all | solution.py:384
  280.5 17.1 %collective-permute-start.22 = (bf16[32,32,128]{2,1,0:T(8,128)(2,1)}, bf16[32,32,128]{2,1,0:T(8,128)(2,1)S(1)}, u32[]{:S(2)}, u32[]{:S(2)}) collective-permute-start(bf16[32,32,128]{2,1,0:T(8,128)(2,1)} %copy-done.63), channel_id=1, source_target_pairs={{0,6},{1,7},{2,4},{3,5},{4,2},{5,3},{6,0},{7,1},{8,14},{9,15},{10,... | collective-permute-start | bytes 786440 | tf_op jit(solution)/shard_map/ppermute | solution.py:380
  284.5 27.7 %collective-permute-start.23 = (bf16[32,32,128]{2,1,0:T(8,128)(2,1)}, bf16[32,32,128]{2,1,0:T(8,128)(2,1)S(1)}, u32[]{:S(2)}, u32[]{:S(2)}) collective-permute-start(bf16[32,32,128]{2,1,0:T(8,128)(2,1)} %copy-done.62), channel_id=1, source_target_pairs={{0,7},{1,6},{2,5},{3,4},{4,3},{5,2},{6,1},{7,0},{8,15},{9,14},{10,... | collective-permute-start | bytes 786440 | tf_op jit(solution)/shard_map/ppermute | solution.py:380
  284.5 36.0 %collective-permute-start.25 = (bf16[32,16,128]{2,1,0:T(8,128)(2,1)}, bf16[32,16,128]{2,1,0:T(8,128)(2,1)S(1)}, u32[]{:S(2)}, u32[]{:S(2)}) collective-permute-start(bf16[32,16,128]{2,1,0:T(8,128)(2,1)} %copy-done.80), channel_id=1, source_target_pairs={{0,5},{1,4},{2,7},{3,6},{4,1},{5,0},{6,3},{7,2},{8,13},{9,12},{10,... | collective-permute-start | bytes 393224 | tf_op jit(solution)/shard_map/ppermute | solution.py:380
  285.0 35.6 %collective-permute-start.26 = (bf16[32,16,128]{2,1,0:T(8,128)(2,1)}, bf16[32,16,128]{2,1,0:T(8,128)(2,1)S(1)}, u32[]{:S(2)}, u32[]{:S(2)}) collective-permute-start(bf16[32,16,128]{2,1,0:T(8,128)(2,1)} %copy-done.79), channel_id=1, source_target_pairs={{0,6},{1,7},{2,4},{3,5},{4,2},{5,3},{6,0},{7,1},{8,14},{9,15},{10,... | collective-permute-start | bytes 393224 | tf_op jit(solution)/shard_map/ppermute | solution.py:380
  287.8 35.4 %collective-permute-start.27 = (bf16[32,16,128]{2,1,0:T(8,128)(2,1)}, bf16[32,16,128]{2,1,0:T(8,128)(2,1)S(1)}, u32[]{:S(2)}, u32[]{:S(2)}) collective-permute-start(bf16[32,16,128]{2,1,0:T(8,128)(2,1)} %copy-done.78), channel_id=1, source_target_pairs={{0,7},{1,6},{2,5},{3,4},{4,3},{5,2},{6,1},{7,0},{8,15},{9,14},{10,... | collective-permute-start | bytes 393224 | tf_op jit(solution)/shard_map/ppermute | solution.py:380
  297.5 44.3 %collective-permute-start.24 = (bf16[32,16,128]{2,1,0:T(8,128)(2,1)}, bf16[32,16,128]{2,1,0:T(8,128)(2,1)S(1)}, u32[]{:S(2)}, u32[]{:S(2)}) collective-permute-start(bf16[32,16,128]{2,1,0:T(8,128)(2,1)} %copy-done.21), channel_id=1, source_target_pairs={{0,4},{1,5},{2,6},{3,7},{4,0},{5,1},{6,2},{7,3},{8,12},{9,13},{10,... | collective-permute-start | bytes 393224 | tf_op jit(solution)/shard_map/ppermute | solution.py:380
  312.2 33.9 %collective-permute-start.28 = (bf16[32,16,128]{2,1,0:T(8,128)(2,1)}, bf16[32,16,128]{2,1,0:T(8,128)(2,1)S(1)}, u32[]{:S(2)}, u32[]{:S(2)}) collective-permute-start(bf16[32,16,128]{2,1,0:T(8,128)(2,1)} %copy-done.73), channel_id=1, source_target_pairs={{0,4},{1,5},{2,6},{3,7},{4,0},{5,1},{6,2},{7,3},{8,12},{9,13},{10,... | collective-permute-start | bytes 393224 | tf_op jit(solution)/shard_map/ppermute | solution.py:380
  320.5 25.6 %collective-permute-start.29 = (bf16[32,16,128]{2,1,0:T(8,128)(2,1)}, bf16[32,16,128]{2,1,0:T(8,128)(2,1)S(1)}, u32[]{:S(2)}, u32[]{:S(2)}) collective-permute-start(bf16[32,16,128]{2,1,0:T(8,128)(2,1)} %copy-done.72), channel_id=1, source_target_pairs={{0,5},{1,4},{2,7},{3,6},{4,1},{5,0},{6,3},{7,2},{8,13},{9,12},{10,... | collective-permute-start | bytes 393224 | tf_op jit(solution)/shard_map/ppermute | solution.py:380
  320.5 25.6 %collective-permute-start.30 = (bf16[32,16,128]{2,1,0:T(8,128)(2,1)}, bf16[32,16,128]{2,1,0:T(8,128)(2,1)S(1)}, u32[]{:S(2)}, u32[]{:S(2)}) collective-permute-start(bf16[32,16,128]{2,1,0:T(8,128)(2,1)} %copy-done.71), channel_id=1, source_target_pairs={{0,6},{1,7},{2,4},{3,5},{4,2},{5,3},{6,0},{7,1},{8,14},{9,15},{10,... | collective-permute-start | bytes 393224 | tf_op jit(solution)/shard_map/ppermute | solution.py:380
  323.2 22.9 %collective-permute-start.31 = (bf16[32,16,128]{2,1,0:T(8,128)(2,1)}, bf16[32,16,128]{2,1,0:T(8,128)(2,1)S(1)}, u32[]{:S(2)}, u32[]{:S(2)}) collective-permute-start(bf16[32,16,128]{2,1,0:T(8,128)(2,1)} %copy-done.70), channel_id=1, source_target_pairs={{0,7},{1,6},{2,5},{3,4},{4,3},{5,2},{6,1},{7,0},{8,15},{9,14},{10,... | collective-permute-start | bytes 393224 | tf_op jit(solution)/shard_map/ppermute | solution.py:380
  395.4 80.1 %all-to-all-start.9 = ((bf16[4,32,32,128]{3,2,1,0:T(8,128)(2,1)}), bf16[4,32,32,128]{3,2,1,0:T(8,128)(2,1)S(1)}, u32[]{:S(2)}, u32[]{:S(2)}) async-start(bf16[4,32,32,128]{3,2,1,0:T(8,128)(2,1)} %copy-done.9), calls=%async_computation.9 | async-start | bytes 2097152 | tf_op jit(solution)/shard_map/all_to_all | solution.py:384
  398.9 18.3 %collective-permute-start.33 = (bf16[32,32,128]{2,1,0:T(8,128)(2,1)}, bf16[32,32,128]{2,1,0:T(8,128)(2,1)S(1)}, u32[]{:S(2)}, u32[]{:S(2)}) collective-permute-start(bf16[32,32,128]{2,1,0:T(8,128)(2,1)} %copy-done.61), channel_id=1, source_target_pairs={{0,5},{1,4},{2,7},{3,6},{4,1},{5,0},{6,3},{7,2},{8,13},{9,12},{10,... | collective-permute-start | bytes 786440 | tf_op jit(solution)/shard_map/ppermute | solution.py:380
  401.8 25.6 %collective-permute-start.34 = (bf16[32,32,128]{2,1,0:T(8,128)(2,1)}, bf16[32,32,128]{2,1,0:T(8,128)(2,1)S(1)}, u32[]{:S(2)}, u32[]{:S(2)}) collective-permute-start(bf16[32,32,128]{2,1,0:T(8,128)(2,1)} %copy-done.59), channel_id=1, source_target_pairs={{0,6},{1,7},{2,4},{3,5},{4,2},{5,3},{6,0},{7,1},{8,14},{9,15},{10,... | collective-permute-start | bytes 786440 | tf_op jit(solution)/shard_map/ppermute | solution.py:380
  403.1 28.9 %collective-permute-start.35 = (bf16[32,32,128]{2,1,0:T(8,128)(2,1)}, bf16[32,32,128]{2,1,0:T(8,128)(2,1)S(1)}, u32[]{:S(2)}, u32[]{:S(2)}) collective-permute-start(bf16[32,32,128]{2,1,0:T(8,128)(2,1)} %copy-done.57), channel_id=1, source_target_pairs={{0,7},{1,6},{2,5},{3,4},{4,3},{5,2},{6,1},{7,0},{8,15},{9,14},{10,... | collective-permute-start | bytes 786440 | tf_op jit(solution)/shard_map/ppermute | solution.py:380
  405.0 54.8 %collective-permute-start.32 = (bf16[32,32,128]{2,1,0:T(8,128)(2,1)}, bf16[32,32,128]{2,1,0:T(8,128)(2,1)S(1)}, u32[]{:S(2)}, u32[]{:S(2)}) collective-permute-start(bf16[32,32,128]{2,1,0:T(8,128)(2,1)} %copy-done.55), channel_id=1, source_target_pairs={{0,4},{1,5},{2,6},{3,7},{4,0},{5,1},{6,2},{7,3},{8,12},{9,13},{10,... | collective-permute-start | bytes 786440 | tf_op jit(solution)/shard_map/ppermute | solution.py:380
  405.0 61.8 %collective-permute-start.36 = (bf16[32,16,128]{2,1,0:T(8,128)(2,1)}, bf16[32,16,128]{2,1,0:T(8,128)(2,1)S(1)}, u32[]{:S(2)}, u32[]{:S(2)}) collective-permute-start(bf16[32,16,128]{2,1,0:T(8,128)(2,1)} %copy-done.77), channel_id=1, source_target_pairs={{0,4},{1,5},{2,6},{3,7},{4,0},{5,1},{6,2},{7,3},{8,12},{9,13},{10,... | collective-permute-start | bytes 393224 | tf_op jit(solution)/shard_map/ppermute | solution.py:380
  417.2 49.6 %collective-permute-start.37 = (bf16[32,16,128]{2,1,0:T(8,128)(2,1)}, bf16[32,16,128]{2,1,0:T(8,128)(2,1)S(1)}, u32[]{:S(2)}, u32[]{:S(2)}) collective-permute-start(bf16[32,16,128]{2,1,0:T(8,128)(2,1)} %copy-done.76), channel_id=1, source_target_pairs={{0,5},{1,4},{2,7},{3,6},{4,1},{5,0},{6,3},{7,2},{8,13},{9,12},{10,... | collective-permute-start | bytes 393224 | tf_op jit(solution)/shard_map/ppermute | solution.py:380
  427.3 39.4 %collective-permute-start.38 = (bf16[32,16,128]{2,1,0:T(8,128)(2,1)}, bf16[32,16,128]{2,1,0:T(8,128)(2,1)S(1)}, u32[]{:S(2)}, u32[]{:S(2)}) collective-permute-start(bf16[32,16,128]{2,1,0:T(8,128)(2,1)} %copy-done.75), channel_id=1, source_target_pairs={{0,6},{1,7},{2,4},{3,5},{4,2},{5,3},{6,0},{7,1},{8,14},{9,15},{10,... | collective-permute-start | bytes 393224 | tf_op jit(solution)/shard_map/ppermute | solution.py:380
  432.0 34.8 %collective-permute-start.39 = (bf16[32,16,128]{2,1,0:T(8,128)(2,1)}, bf16[32,16,128]{2,1,0:T(8,128)(2,1)S(1)}, u32[]{:S(2)}, u32[]{:S(2)}) collective-permute-start(bf16[32,16,128]{2,1,0:T(8,128)(2,1)} %copy-done.74), channel_id=1, source_target_pairs={{0,7},{1,6},{2,5},{3,4},{4,3},{5,2},{6,1},{7,0},{8,15},{9,14},{10,... | collective-permute-start | bytes 393224 | tf_op jit(solution)/shard_map/ppermute | solution.py:380
  475.5 106.0 %all-to-all-start.11 = ((bf16[4,32,16,128]{3,2,1,0:T(8,128)(2,1)}), bf16[4,32,16,128]{3,2,1,0:T(8,128)(2,1)}, u32[]{:S(2)}, u32[]{:S(2)}) async-start(bf16[4,32,16,128]{3,2,1,0:T(8,128)(2,1)} %copy-done.13), calls=%async_computation.11 | async-start | bytes 1048576 | tf_op jit(solution)/shard_map/all_to_all | solution.py:384
  481.9 10.6 %collective-permute-start.45 = (bf16[32,16,128]{2,1,0:T(8,128)(2,1)}, bf16[32,16,128]{2,1,0:T(8,128)(2,1)S(1)}, u32[]{:S(2)}, u32[]{:S(2)}) collective-permute-start(bf16[32,16,128]{2,1,0:T(8,128)(2,1)} %copy-done.86), channel_id=1, source_target_pairs={{0,5},{1,4},{2,7},{3,6},{4,1},{5,0},{6,3},{7,2},{8,13},{9,12},{10,... | collective-permute-start | bytes 393224 | tf_op jit(solution)/shard_map/ppermute | solution.py:380
  486.3 42.6 %collective-permute-start.46 = (bf16[32,16,128]{2,1,0:T(8,128)(2,1)}, bf16[32,16,128]{2,1,0:T(8,128)(2,1)}, u32[]{:S(2)}, u32[]{:S(2)}) collective-permute-start(bf16[32,16,128]{2,1,0:T(8,128)(2,1)} %copy-done.85), channel_id=1, source_target_pairs={{0,6},{1,7},{2,4},{3,5},{4,2},{5,3},{6,0},{7,1},{8,14},{9,15},{10,... | collective-permute-start | bytes 393224 | tf_op jit(solution)/shard_map/ppermute | solution.py:380
  487.6 68.0 %collective-permute-start.40 = (bf16[32,32,128]{2,1,0:T(8,128)(2,1)S(1)}, bf16[32,32,128]{2,1,0:T(8,128)(2,1)}, u32[]{:S(2)}, u32[]{:S(2)}) collective-permute-start(bf16[32,32,128]{2,1,0:T(8,128)(2,1)S(1)} %get-tuple-element.113._), channel_id=1, source_target_pairs={{0,4},{1,5},{2,6},{3,7},{4,0},{5,1},{6,2},{7,3},{8,12},{9,13},{10,... | collective-permute-start | bytes 786440 | tf_op jit(solution)/shard_map/ppermute | solution.py:380
  489.4 62.9 %collective-permute-start.41 = (bf16[32,32,128]{2,1,0:T(8,128)(2,1)}, bf16[32,32,128]{2,1,0:T(8,128)(2,1)}, u32[]{:S(2)}, u32[]{:S(2)}) collective-permute-start(bf16[32,32,128]{2,1,0:T(8,128)(2,1)} %copy-done.60), channel_id=1, source_target_pairs={{0,5},{1,4},{2,7},{3,6},{4,1},{5,0},{6,3},{7,2},{8,13},{9,12},{10,... | collective-permute-start | bytes 786440 | tf_op jit(solution)/shard_map/ppermute | solution.py:380
  489.8 62.6 %collective-permute-start.42 = (bf16[32,32,128]{2,1,0:T(8,128)(2,1)}, bf16[32,32,128]{2,1,0:T(8,128)(2,1)}, u32[]{:S(2)}, u32[]{:S(2)}) collective-permute-start(bf16[32,32,128]{2,1,0:T(8,128)(2,1)} %copy-done.58), channel_id=1, source_target_pairs={{0,6},{1,7},{2,4},{3,5},{4,2},{5,3},{6,0},{7,1},{8,14},{9,15},{10,... | collective-permute-start | bytes 786440 | tf_op jit(solution)/shard_map/ppermute | solution.py:380
  493.1 60.2 %collective-permute-start.43 = (bf16[32,32,128]{2,1,0:T(8,128)(2,1)}, bf16[32,32,128]{2,1,0:T(8,128)(2,1)}, u32[]{:S(2)}, u32[]{:S(2)}) collective-permute-start(bf16[32,32,128]{2,1,0:T(8,128)(2,1)} %copy-done.56), channel_id=1, source_target_pairs={{0,7},{1,6},{2,5},{3,4},{4,3},{5,2},{6,1},{7,0},{8,15},{9,14},{10,... | collective-permute-start | bytes 786440 | tf_op jit(solution)/shard_map/ppermute | solution.py:380
  528.9 7.0 %collective-permute-start.47 = (bf16[32,16,128]{2,1,0:T(8,128)(2,1)}, bf16[32,16,128]{2,1,0:T(8,128)(2,1)S(1)}, u32[]{:S(2)}, u32[]{:S(2)}) collective-permute-start(bf16[32,16,128]{2,1,0:T(8,128)(2,1)} %copy-done.83), channel_id=1, source_target_pairs={{0,7},{1,6},{2,5},{3,4},{4,3},{5,2},{6,1},{7,0},{8,15},{9,14},{10,... | collective-permute-start | bytes 393224 | tf_op jit(solution)/shard_map/ppermute | solution.py:380
  535.9 34.7 %collective-permute-start.44 = (bf16[32,16,128]{2,1,0:T(8,128)(2,1)S(1)}, bf16[32,16,128]{2,1,0:T(8,128)(2,1)S(1)}, u32[]{:S(2)}, u32[]{:S(2)}) collective-permute-start(bf16[32,16,128]{2,1,0:T(8,128)(2,1)S(1)} %get-tuple-element.125._), channel_id=1, source_target_pairs={{0,4},{1,5},{2,6},{3,7},{4,0},{5,1},{6,2},{7,3},{8,12},{9,13},{10,... | collective-permute-start | bytes 393224 | tf_op jit(solution)/shard_map/ppermute | solution.py:380
  552.4 21.8 %collective-permute-start.49 = (bf16[32,16,128]{2,1,0:T(8,128)(2,1)}, bf16[32,16,128]{2,1,0:T(8,128)(2,1)S(1)}, u32[]{:S(2)}, u32[]{:S(2)}) collective-permute-start(bf16[32,16,128]{2,1,0:T(8,128)(2,1)} %copy-done.89), channel_id=1, source_target_pairs={{0,5},{1,4},{2,7},{3,6},{4,1},{5,0},{6,3},{7,2},{8,13},{9,12},{10,... | collective-permute-start | bytes 393224 | tf_op jit(solution)/shard_map/ppermute | solution.py:380
  552.4 22.4 %collective-permute-start.50 = (bf16[32,16,128]{2,1,0:T(8,128)(2,1)}, bf16[32,16,128]{2,1,0:T(8,128)(2,1)S(1)}, u32[]{:S(2)}, u32[]{:S(2)}) collective-permute-start(bf16[32,16,128]{2,1,0:T(8,128)(2,1)} %copy-done.88), channel_id=1, source_target_pairs={{0,6},{1,7},{2,4},{3,5},{4,2},{5,3},{6,0},{7,1},{8,14},{9,15},{10,... | collective-permute-start | bytes 393224 | tf_op jit(solution)/shard_map/ppermute | solution.py:380
  553.3 22.1 %collective-permute-start.51 = (bf16[32,16,128]{2,1,0:T(8,128)(2,1)}, bf16[32,16,128]{2,1,0:T(8,128)(2,1)S(1)}, u32[]{:S(2)}, u32[]{:S(2)}) collective-permute-start(bf16[32,16,128]{2,1,0:T(8,128)(2,1)} %copy-done.87), channel_id=1, source_target_pairs={{0,7},{1,6},{2,5},{3,4},{4,3},{5,2},{6,1},{7,0},{8,15},{9,14},{10,... | collective-permute-start | bytes 393224 | tf_op jit(solution)/shard_map/ppermute | solution.py:380
  555.7 25.8 %collective-permute-start.48 = (bf16[32,16,128]{2,1,0:T(8,128)(2,1)}, bf16[32,16,128]{2,1,0:T(8,128)(2,1)S(1)}, u32[]{:S(2)}, u32[]{:S(2)}) collective-permute-start(bf16[32,16,128]{2,1,0:T(8,128)(2,1)} %copy-done.25), channel_id=1, source_target_pairs={{0,4},{1,5},{2,6},{3,7},{4,0},{5,1},{6,2},{7,3},{8,12},{9,13},{10,... | collective-permute-start | bytes 393224 | tf_op jit(solution)/shard_map/ppermute | solution.py:380
  (100 other events, 327.1 us)

commit v4 on v1

v4 whole, which is shorter than its diff:
```python
import functools

import jax
import jax.numpy as jnp
import ml_dtypes
import numpy as np
from jax import lax
from jax.experimental import pallas as pl
from jax.experimental.pallas import tpu as pltpu
from jax.sharding import PartitionSpec as P

F = 512
SOURCE_SPACING = 512
JITTER = 256
STEP = 0.5
LANES = 128
NEAR = SOURCE_SPACING - JITTER
FAR = SOURCE_SPACING + JITTER
HALO = 3


def time_tables(samples, blocks):
    freq = np.arange(F, dtype=np.int32)
    sample = np.arange(samples, dtype=np.int32)
    phase = (freq[:, None] * sample[None, :] % samples).astype(np.float32)
    angle = np.float32(2.0 * np.pi) * phase / np.float32(samples)
    root = np.sqrt(np.float32(samples))
    weight = np.where(freq == 0, 1.0, 2.0).astype(np.float32)[:, None] / root
    forward = np.stack([np.cos(angle) / root, -np.sin(angle) / root])
    inverse = np.stack([weight * np.cos(angle), -weight * np.sin(angle)])

    def ordered(table):
        table = table.astype(np.float32).astype(ml_dtypes.bfloat16)
        table = table.reshape(2, blocks, F // blocks, samples).transpose(1, 0, 2, 3)
        return table.reshape(2 * F, samples)

    return np.ascontiguousarray(ordered(forward).T), ordered(inverse)


def shot_table(shots):
    index = np.arange(shots, dtype=np.int32)
    phase = (index[:, None] * index[None, :] % shots).astype(np.float32)
    angle = np.float32(2.0 * np.pi) * phase / np.float32(shots)
    root = np.sqrt(np.float32(shots))
    table = np.concatenate([np.cos(angle) / root, np.sin(angle) / root])
    return table.astype(np.float32).astype(ml_dtypes.bfloat16)


def band(meta_ref, chip, width):
    return pl.ds(pl.multiple_of(meta_ref[3 + 2 * chip] // 2 * width, width), width)


def views(refs):
    return [ref.at[index] for ref in refs for index in range(ref.shape[0])]


def blend_into(
    meta_ref, delay_ref, est_ref, obs_ref, before_ref, after_ref, energy_ref, est32, res32, store
):
    shots, rows, samples = est_ref.shape
    columns = samples // LANES
    margin = (FAR - NEAR) // LANES
    inner = (samples - NEAR) // LANES
    skip = NEAR // LANES
    total = delay_ref.shape[0]
    first = meta_ref[0]
    lane = lax.broadcasted_iota(jnp.int32, (1, rows, LANES), 2)

    def ahead(shot):
        shot = jnp.clip(shot, 0, total - 2)
        return jnp.clip(SOURCE_SPACING + delay_ref[shot + 1] - delay_ref[shot], NEAR + 1, FAR - 1)

    def window(field, slot, start):
        column, rest = start // LANES, start % LANES
        wide = field[slot, pl.ds(column, inner + 1)]
        turned = pltpu.roll(
            wide.reshape((inner + 1) * rows, LANES), (LANES - rest) % LANES, 1
        ).reshape(inner + 1, rows, LANES)
        return jnp.where(lane < LANES - rest, turned[:-1], turned[1:])

    def blended(field, slot, shot):
        later = window(field, slot + 1, margin * LANES + NEAR - ahead(shot))
        earlier = window(field, slot - 1, margin * LANES + ahead(shot - 1))
        return later, earlier

    def fill(field, slot, values):
        blank = jnp.zeros((margin, rows, LANES), jnp.float32)
        field[slot, pl.ds(0, margin)] = blank
        field[slot, pl.ds(margin + columns, margin)] = blank
        for column in range(columns):
            field[slot, margin + column] = values(column)

    def cut(ref, shot):
        return lambda column: ref[shot, :, column * LANES : (column + 1) * LANES].astype(jnp.float32)

    for slot in range(2):
        fill(est32, slot, cut(before_ref, slot))
        fill(est32, shots + 2 + slot, cut(after_ref, slot))

    def load(shot, carry):
        fill(est32, shot + 2, cut(est_ref, shot))
        return carry

    lax.fori_loop(0, shots, load, 0, unroll=2)

    def residual(place, values):
        shot = first + place - 1
        inside = jnp.logical_and(shot >= 0, shot < total)
        later, earlier = blended(est32, place + 1, shot)
        power = jnp.zeros((rows, LANES), jnp.float32)
        cells = []
        for column in range(columns):
            cell = est32[place + 1, margin + column]
            if column >= skip:
                cell = cell + later[column - skip]
            if column < inner:
                cell = cell + earlier[column]
            cell = jnp.where(inside, values(column) - cell, 0.0)
            power = power + cell * cell
            cells.append(cell)
        fill(res32, place, lambda column: cells[column])
        return power

    residual(0, cut(before_ref, 2))
    residual(shots + 1, cut(after_ref, 2))

    def middle(shot, carry):
        power = residual(shot + 1, cut(obs_ref, shot))
        energy_ref[pl.ds(shot, 1), :] = jnp.sum(power, axis=0, keepdims=True)
        return carry

    lax.fori_loop(0, shots, middle, 0, unroll=2)

    def step(shot, carry):
        later, earlier = blended(res32, shot + 1, first + shot)
        for column in range(columns):
            cell = res32[shot + 1, margin + column]
            if column >= skip:
                cell = cell + later[column - skip]
            if column < inner:
                cell = cell + earlier[column]
            cell = est32[shot + 2, margin + column] + STEP * cell
            store(shot, column, cell.astype(jnp.bfloat16))
        return carry

    lax.fori_loop(0, shots, step, 0, unroll=2)


def spectra_kernel(outputs, packed, meta_ref, delay_ref, est_ref, obs_ref, before_ref, after_ref, table_ref, _, *refs):
    *refs, energy_ref, est32, res32, stepped, result = refs
    out_refs, partner_refs = refs[-outputs:], refs[:-outputs]
    shots, rows, samples = est_ref.shape
    width = out_refs[0].shape[3]

    def store(shot, column, values):
        start = pl.multiple_of(shot * rows, rows)
        stepped[pl.ds(start, rows), column * LANES : (column + 1) * LANES] = values

    blend_into(
        meta_ref, delay_ref, est_ref, obs_ref, before_ref, after_ref, energy_ref, est32, res32, store
    )
    held = result.shape[0]
    group = held // rows
    if packed:
        targets = [out_refs[0].at[chip] for chip in range(out_refs[0].shape[0])]
    else:
        targets = [ref.at[0] for ref in out_refs]

    def transform(part, carry):
        start = pl.multiple_of(part * held, held)
        result[...] = jnp.dot(
            stepped[pl.ds(start, held), :], table_ref[...], preferred_element_type=jnp.float32
        ).astype(jnp.bfloat16)
        for chip, target in enumerate(targets):
            target[pl.ds(part * group, group)] = result[:, band(meta_ref, chip, width)].reshape(
                group, rows, width
            )
        return carry

    lax.fori_loop(0, shots // group, transform, 0)
    for partner_ref in partner_refs:
        for chip, out_ref in enumerate(out_refs):
            out_ref[1] = partner_ref[chip]


def step_kernel(
    meta_ref, delay_ref, est_ref, obs_ref, before_ref, after_ref, out_ref, energy_ref, est32, res32
):
    def store(shot, column, values):
        out_ref[shot, :, column * LANES : (column + 1) * LANES] = values

    blend_into(
        meta_ref, delay_ref, est_ref, obs_ref, before_ref, after_ref, energy_ref, est32, res32, store
    )


def shots_kernel(inputs, meta_ref, table_ref, level_ref, _, *refs):
    *refs, wide, back = refs
    _, held, rows, width = refs[0].shape
    pieces, size, _ = wide.shape
    shots = size // rows
    half = width // 2

    def place(slot):
        size = held * rows
        return pl.ds(pl.multiple_of(meta_ref[3 + slot] * size, size), size)

    for slot, ref in enumerate(views(refs[:inputs])):
        block = ref[...].reshape(held * rows, width).astype(jnp.float32)
        for piece in range(pieces):
            wide[piece, place(slot), :] = block[:, piece * LANES : (piece + 1) * LANES]
    level = level_ref[...]
    sign = jnp.where(
        lax.broadcasted_iota(jnp.int32, (1, width), 1) < half, jnp.float32(1.0), jnp.float32(-1.0)
    )

    def receiver(index, carry):
        pick = pl.ds(index, shots, stride=rows)
        block = jnp.concatenate([wide.at[piece][pick, :] for piece in range(pieces)], axis=1)
        both = jnp.dot(
            table_ref[...], block.astype(jnp.bfloat16), preferred_element_type=jnp.float32
        )
        wave = both[:shots] + sign * pltpu.roll(both[shots:], half, 1)
        power = wave * wave
        power = power + pltpu.roll(power, half, 1)
        factor = jnp.maximum(1.0 - level * lax.rsqrt(power), 0.0)
        kept = (wave * factor).astype(jnp.bfloat16)
        both = jnp.dot(table_ref[...], kept, preferred_element_type=jnp.float32)
        both = both[:shots] - sign * pltpu.roll(both[shots:], half, 1)
        for piece in range(pieces):
            back.at[piece][pick, :] = both[:, piece * LANES : (piece + 1) * LANES]
        return carry

    lax.fori_loop(0, rows, receiver, 0, unroll=2)
    for slot, ref in enumerate(views(refs[inputs:])):
        block = jnp.concatenate([back[piece, place(slot), :] for piece in range(pieces)], axis=1)
        ref[...] = block.astype(jnp.bfloat16).reshape(held, rows, width)


def update_kernel(inputs, passes, meta_ref, table_ref, _, *refs):
    restored_refs, whole_rows = refs[:inputs], refs[-1]
    outputs = refs[-4:-1] if passes else refs[-3:-1]
    own = [restored_refs[0].at[chip] for chip in range(restored_refs[0].shape[0])]
    if inputs > 1:
        own = [ref.at[0] for ref in restored_refs]
    held, rows, width = own[0].shape
    for chip, ref in enumerate(own):
        whole_rows[:, band(meta_ref, chip, width)] = ref[...].reshape(held * rows, width)
    outputs[0][...] = jnp.dot(
        whole_rows[...], table_ref[...], preferred_element_type=jnp.float32
    ).reshape(outputs[0].shape)
    outputs[1][...] = jnp.zeros_like(outputs[1])
    if passes:
        for chip, ref in enumerate(restored_refs):
            outputs[2][chip] = ref[1]


def whole(shape):
    return pl.BlockSpec(shape, lambda *_: (0,) * len(shape))


def blend_specs(shots, rows, samples, block, edge_block):
    at = lambda step, meta, delays: (0, block(meta), 0)
    edge = lambda step, meta, delays: (0, edge_block(meta), 0)
    return [
        pl.BlockSpec((shots, rows, samples), at),
        pl.BlockSpec((shots, rows, samples), at),
        pl.BlockSpec((HALO, rows, samples), edge),
        pl.BlockSpec((HALO, rows, samples), edge),
    ]


def blend_scratch(shots, rows, samples):
    columns = (samples + 2 * (FAR - NEAR)) // LANES
    return [
        pltpu.VMEM((shots + 4, columns, rows, LANES), jnp.float32),
        pltpu.VMEM((shots + 2, columns, rows, LANES), jnp.float32),
    ]


PARAMS = pltpu.CompilerParams(vmem_limit_bytes=60 * 1024 * 1024)
ANYWHERE = pl.BlockSpec(memory_space=pl.ANY)


def spectra_of(meta, delays, fields, table, block, edge_block, rows, peers, mode, partner, after):
    shots, _, samples = fields[0].shape
    chips = peers // 2
    block_shape = (shots, rows, 2 * F // chips)
    shapes = {
        "apart": [(1, *block_shape)] * chips,
        "packed": [(chips, *block_shape)],
        "joined": [(2, *block_shape)] * chips,
    }[mode]
    group = min(shots, max(1, 256 // rows))
    partners = [] if partner is None else [partner]
    *spectra, energy = pl.pallas_call(
        functools.partial(spectra_kernel, len(shapes), mode == "packed"),
        grid_spec=pltpu.PrefetchScalarGridSpec(
            num_scalar_prefetch=2,
            grid=(1,),
            in_specs=blend_specs(shots, rows, samples, block, edge_block)
            + [whole(table.shape), ANYWHERE]
            + [whole(array.shape) for array in partners],
            out_specs=[whole(shape) for shape in shapes] + [whole((shots, LANES))],
            scratch_shapes=blend_scratch(shots, rows, samples)
            + [
                pltpu.VMEM((shots * rows, samples), jnp.bfloat16),
                pltpu.VMEM((group * rows, 2 * F), jnp.bfloat16),
            ],
        ),
        out_shape=[pltpu.HBM(shape, jnp.bfloat16) for shape in shapes]
        + [pltpu.HBM((shots, LANES), jnp.float32)],
        compiler_params=PARAMS,
        cost_estimate=pl.CostEstimate(
            flops=4 * F * shots * rows * samples,
            bytes_accessed=3 * 2 * shots * rows * samples + table.size * 2,
            transcendentals=0,
        ),
        name="spectra_" + mode,
    )(meta, delays, *fields, table, after, *partners)
    return spectra, energy


def stepped_of(meta, delays, fields, rows, index):
    shots, _, samples = fields[0].shape
    block = lambda meta: index
    return pl.pallas_call(
        step_kernel,
        grid_spec=pltpu.PrefetchScalarGridSpec(
            num_scalar_prefetch=2,
            grid=(1,),
            in_specs=blend_specs(shots, rows, samples, block, block),
            out_specs=[whole((shots, rows, samples)), whole((shots, LANES))],
            scratch_shapes=blend_scratch(shots, rows, samples),
        ),
        out_shape=[
            jax.ShapeDtypeStruct((shots, rows, samples), jnp.bfloat16),
            jax.ShapeDtypeStruct((shots, LANES), jnp.float32),
        ],
        compiler_params=PARAMS,
        name="stepped",
    )(meta, delays, *fields)


def shrunk_of(meta, spectra, table, level, joined, after):
    _, held, rows, width = spectra[0].shape
    shots = table.shape[1]
    peers = shots // held
    size = shots * rows * width
    shapes = [(2, held, rows, width)] * (peers // 2) if joined else [(1, held, rows, width)] * peers
    return pl.pallas_call(
        functools.partial(shots_kernel, len(spectra)),
        grid_spec=pltpu.PrefetchScalarGridSpec(
            num_scalar_prefetch=1,
            grid=(1,),
            in_specs=[whole(table.shape), whole(level.shape), ANYWHERE]
            + [whole(block.shape) for block in spectra],
            out_specs=[whole(shape) for shape in shapes],
            scratch_shapes=[pltpu.VMEM((width // LANES, shots * rows, LANES), jnp.float32)] * 2,
        ),
        out_shape=[pltpu.HBM(shape, jnp.bfloat16) for shape in shapes],
        compiler_params=PARAMS,
        cost_estimate=pl.CostEstimate(
            flops=8 * shots * size, bytes_accessed=4 * size + 2 * table.size, transcendentals=size
        ),
        name="shrink",
    )(meta, table, level, after, *spectra)


def updated_of(meta, restored, table, block, receivers, onto, passes, after):
    _, shots, rows, width = restored[0].shape
    samples = table.shape[1]
    chips = table.shape[0] // width
    group = min(shots, max(1, 256 // rows))
    by_shots = lambda step, meta: (0, step, 0, 0)
    in_specs = [whole(table.shape), ANYWHERE]
    in_specs += [pl.BlockSpec((array.shape[0], group, rows, width), by_shots) for array in restored]
    operands = [meta, table, after, *restored]
    if onto is not None:
        in_specs.append(ANYWHERE)
        operands.append(onto)
    out_specs = [
        pl.BlockSpec((group, rows, samples), lambda step, meta: (step, block(meta), 0)),
        whole((8, LANES)),
    ]
    out_shape = [
        pltpu.HBM((shots, receivers, samples), jnp.float32),
        pltpu.HBM((8, LANES), jnp.float32),
    ]
    if passes:
        out_specs.append(pl.BlockSpec((chips, group, rows, width), by_shots))
        out_shape.append(pltpu.HBM((chips, shots, rows, width), jnp.bfloat16))
    return pl.pallas_call(
        functools.partial(update_kernel, len(restored), passes),
        grid_spec=pltpu.PrefetchScalarGridSpec(
            num_scalar_prefetch=1,
            grid=(shots // group,),
            in_specs=in_specs,
            out_specs=out_specs,
            scratch_shapes=[pltpu.VMEM((group * rows, 2 * F), jnp.bfloat16)],
        ),
        out_shape=out_shape,
        input_output_aliases={} if onto is None else {len(operands) - 1: 0},
        compiler_params=PARAMS,
        cost_estimate=pl.CostEstimate(
            flops=4 * F * shots * rows * samples,
            bytes_accessed=4 * F * shots * rows + 2 * table.size + 4 * shots * rows * samples,
            transcendentals=0,
        ),
        name="update",
    )(*operands)


def swapped(array):
    return lax.all_to_all(array, "shot", split_axis=0, concat_axis=0, tiled=True)


def sent(array, distance):
    peers = lax.axis_size("shot")
    return lax.ppermute(array, "shot", [(i, i ^ distance) for i in range(peers)])


def edges(estimate, observed):
    peers = lax.axis_size("shot")
    up = [(i, i + 1) for i in range(peers - 1)]
    down = [(j, i) for i, j in up]
    tail = jnp.concatenate([estimate[-2:], observed[-1:]])
    head = jnp.concatenate([estimate[:2], observed[:1]])
    return lax.ppermute(tail, "shot", up), lax.ppermute(head, "shot", down)


def part_of_halves(array, start, stop):
    shots, receivers, samples = array.shape
    halves = array.reshape(shots, 2, receivers // 2, samples)[:, :, start:stop]
    return halves.reshape(shots, 2 * (stop - start), samples)


def turns(steps):
    for turn in range(steps + 4):
        if turn == 0:
            yield "own", 0
            yield "other", 0
        if turn + 1 < steps:
            yield "other", turn + 1
        if 0 < turn < steps:
            yield "own", turn
        for name, lag in (("shrink", 1), ("update own", 3), ("update other", 4)):
            if 0 <= turn - lag < steps:
                yield name, turn - lag


def in_pairs(estimate, observed, delays, thresholds, rows):
    shots, receivers, samples = estimate.shape
    peers = lax.axis_size("shot")
    rank = lax.axis_index("shot")
    total = delays.shape[0]
    chips = peers // 2
    share = F // chips
    steps = receivers // 2 // rows
    core = rank % 2
    meta = jnp.concatenate(
        [jnp.stack([rank * shots, core, 1 - core]), rank ^ jnp.arange(peers, dtype=jnp.int32)]
    ).astype(jnp.int32)
    forward, inverse = (jnp.asarray(table) for table in time_tables(samples, chips))
    table = jnp.asarray(shot_table(total))
    levels = jnp.tile(lax.dynamic_slice_in_dim(thresholds, rank // 2 * share, share), 2)[None, :]
    early = edges(part_of_halves(estimate, 0, rows), part_of_halves(observed, 0, rows))
    late = None
    last, updated, energy = levels, None, 0.0
    packed, ahead, behind, passed = {}, {}, {}, {}
    for name, step in turns(steps):
        side = 1 if name.endswith("own") else 2
        block = lambda meta, side=side, step=step: meta[side] * steps + step
        if name in ("own", "other"):
            edge_block = block
            if step == 0:
                edge_block = lambda meta, side=side: meta[side]
            else:
                edge_block = lambda meta, side=side, step=step: meta[side] * (steps - 1) + step - 1
            direct = step == 0
            mode = "apart" if direct else "joined" if name == "own" else "packed"
            spectra, power = spectra_of(
                meta,
                delays,
                (estimate, observed, *(late if step else early)),
                forward,
                block,
                edge_block,
                rows,
                peers,
                mode,
                packed.pop(step) if mode == "joined" else None,
                last,
            )
            last = power
            energy = energy + power
            if mode == "packed":
                packed[step] = sent(spectra[0], 1)
            elif mode == "joined":
                far = [sent(spectra[chip], 2 * chip) for chip in range(1, chips)]
                ahead[step] = [spectra[0], *far]
            elif name == "own":
                far = [sent(spectra[chip], 2 * chip) for chip in range(1, chips)]
                ahead[step] = [spectra[0], *far]
                held_estimate, held_observed, _ = lax.optimization_barrier(
                    (estimate, observed, power)
                )
                if steps > 1:
                    late = edges(
                        part_of_halves(held_estimate, rows, receivers // 2),
                        part_of_halves(held_observed, rows, receivers // 2),
                    )
            else:
                other = [sent(spectra[chip], 2 * chip + 1) for chip in range(chips)]
                ahead[step] = [array for pair in zip(ahead[step], other) for array in pair]
        elif name == "shrink":
            direct = step == steps - 1
            shrunk = shrunk_of(meta, ahead.pop(step), table, levels, not direct, last)
            last = shrunk[0]
            unit = 1 if direct else 2
            behind[step] = [
                sent(array, unit * index) if index else array for index, array in enumerate(shrunk)
            ]
        elif name == "update own":
            direct = step == steps - 1
            restored = behind.pop(step)
            if direct:
                passed[step] = restored[1::2]
                restored = restored[::2]
            updated, last, *partner = updated_of(
                meta, restored, inverse, block, receivers, updated, not direct, last
            )
            if not direct:
                passed[step] = [sent(partner[0], 1)]
        else:
            updated, last = updated_of(
                meta, passed.pop(step), inverse, block, receivers, updated, False, last
            )
    return updated, energy


def spectral_by_einsum(stepped, forward, inverse, table, level, peers):
    shots, receivers, samples = stepped.shape
    total = table.shape[1]
    share = F // peers
    spectra = jnp.einsum(
        "srt,tdpf->dpfsr",
        stepped,
        forward.reshape(samples, peers, 2, share),
        preferred_element_type=jnp.float32,
    ).astype(jnp.bfloat16)
    mixed = swapped(spectra).transpose(1, 2, 0, 3, 4).reshape(2, share, total, receivers)
    cosine, sine = table[:total], table[total:]
    across = jnp.stack([jnp.stack([cosine, sine]), jnp.stack([-sine, cosine])])
    wave = jnp.einsum("pqks,qfsr->pfkr", across, mixed, preferred_element_type=jnp.float32)
    magnitude = jnp.sqrt(wave[0] * wave[0] + wave[1] * wave[1])
    bound = level[:, None, None]
    factor = jnp.maximum(magnitude - bound, 0.0) / jnp.maximum(magnitude, bound)
    shrunk = (wave * factor[None]).astype(jnp.bfloat16)
    back = jnp.stack([jnp.stack([cosine, -sine]), jnp.stack([sine, cosine])])
    restored = jnp.einsum(
        "pqks,qfkr->pfsr", back, shrunk, preferred_element_type=jnp.float32
    ).astype(jnp.bfloat16)
    restored = restored.reshape(2, share, peers, shots, receivers).transpose(2, 0, 1, 3, 4)
    return jnp.einsum(
        "dpft,dpfsr->srt",
        inverse.reshape(peers, 2, share, samples),
        swapped(restored),
        preferred_element_type=jnp.float32,
    )


def by_einsum(estimate, observed, delays, thresholds, rows):
    shots, receivers, samples = estimate.shape
    peers = lax.axis_size("shot")
    rank = lax.axis_index("shot")
    share = F // peers
    meta = jnp.reshape(rank * shots, (1,)).astype(jnp.int32)
    sides = edges(estimate, observed)
    energy = 0.0
    parts = []
    for index in range(receivers // rows):
        part, power = stepped_of(meta, delays, (estimate, observed, *sides), rows, index)
        energy = energy + power
        parts.append(part)
    forward, inverse = (jnp.asarray(table) for table in time_tables(samples, peers))
    table = jnp.asarray(shot_table(delays.shape[0]))
    level = lax.dynamic_slice_in_dim(thresholds, rank * share, share)
    stepped = jnp.concatenate(parts, axis=1)
    return spectral_by_einsum(stepped, forward, inverse, table, level, peers), energy


def local(estimate, observed, random_source_delays, thresholds):
    receivers, samples = estimate.shape[1:]
    peers = lax.axis_size("shot")
    rows = min(16, receivers)
    paired = (
        peers > 1
        and peers & (peers - 1) == 0
        and (4 * F // peers) % LANES == 0
        and receivers % (2 * rows) == 0
    )
    path = in_pairs if paired else by_einsum
    updated, energy = path(estimate, observed, random_source_delays, thresholds, rows)
    misfit = lax.psum(jnp.sum(energy, axis=1), "patch") / (
        receivers * lax.axis_size("patch") * samples
    )
    return updated, misfit


def solution(mesh):
    in_specs = (P("shot", "patch", None), P("shot", "patch", None), P(), P())
    out_specs = (P("shot", "patch", None), P("shot"))
    return jax.shard_map(local, mesh=mesh, in_specs=in_specs, out_specs=out_specs, check_vma=False)
```

time: 542 us -> 464 us (0.86)
  waiting for transfers between devices: 244 us -> 130 us
  starting transfers between devices: 79.3 us -> 121 us
  local copies, waits for them, and re-layouts: 23 us -> 16.4 us
    all_to_all x16 -> x0, waiting for transfers between devices: 239 us -> none  [swapped(): lax.all_to_all(array, 'shot', split_axis=0, concat_axis=0, tiled=True)]
    ppermute x2 -> x42, waiting for transfers between devices: 5.35 us -> 130 us  [the longest x38 127 us: sent(): lax.ppermute(array, 'shot', [(i, i ^ distance) for i in range(peers)])]
    ppermute x2 -> x42, starting transfers between devices: 3.67 us -> 121 us  [the longest x38 110 us: sent(): lax.ppermute(array, 'shot', [(i, i ^ distance) for i in range(peers)])]
    all_to_all x16 -> x0, starting transfers between devices: 75.6 us -> none  [swapped(): lax.all_to_all(array, 'shot', split_axis=0, concat_axis=0, tiled=True)]
    unnamed x46 -> x98, local copies, waits for them, and re-layouts: 19.6 us -> 11 us
    pallas_call x24 -> x20, Pallas kernels: 180 us -> 181 us  [the longest x8 91.8 us: spectra_of(): pl.pallas_call(functools.partial(spectra_kernel, len(shapes), mode == 'pa...]
  transfers between devices with their start and end apart: 18 -> 42, of which waited for: 16 -> 11; matrix products, arithmetic and copies ran while one was open for 0% -> 0% of each run, Pallas kernels for 31% -> 33%
where the time goes in v4:
time: 464 us; the launch traced here: 460 us
  Pallas kernels  181 us (39%)
  waiting for transfers between devices  130 us (28%)
  starting transfers between devices  121 us (26%)
  local copies, waits for them, and re-layouts  16.4 us (4%)
  blocking collectives  9.91 us (2%)
    ppermute x38, waiting for transfers between devices, sent(): lax.ppermute(array, 'shot', [(i, i ^ distance) for i in range(peers)])  127 us
    ppermute x38, starting transfers between devices, sent(): lax.ppermute(array, 'shot', [(i, i ^ distance) for i in range(peers)])  110 us
    pallas_call x8, Pallas kernels, spectra_of(): pl.pallas_call(functools.partial(spectra_kernel, len(shapes), mode == 'pa...  91.8 us
    pallas_call x4, Pallas kernels, shrunk_of(): pl.pallas_call(functools.partial(shots_kernel, len(spectra)), grid_spec=p...  47.4 us
    pallas_call x8, Pallas kernels, updated_of(): pl.pallas_call(functools.partial(update_kernel, len(restored), passes), g...  41.5 us
    ppermute x4, starting transfers between devices, edges(): return (lax.ppermute(tail, 'shot', up), lax.ppermute(head, 'shot', down))  11.2 us
    unnamed x98, local copies, waits for them, and re-layouts  11 us
    psum x1, blocking collectives, local(): lax.psum(jnp.sum(energy, axis=1), 'patch')  9.91 us
  transfers between devices with their start and end apart: 42, of which 11 were waited for; matrix products, arithmetic and copies ran while one was open for 0% of the time, Pallas kernels for 33%

profile of v4, /device:TPU:0, one launch (start us, length us, event | category | flops | bytes accessed | tf_op | source)
XLA Modules:
  0.0 460.2 jit_solution(7229546027523687967)
XLA Ops:
  1.5 1.0 fusion.2
  2.5 2.4 collective-permute-start
  5.0 1.3 collective-permute-start.1
  7.7 2.8 collective-permute-done.1.after_ref
  11.2 11.2 %spectra_apart.2 = (bf16[1,32,16,256]{3,2,1,0:T(8,128)(2,1)}, bf16[1,32,16,256]{3,2,1,0:T(8,128)(2,1)}, bf16[1,32,16,256]{3,2,1,0:T(8,128)(2,1)}, bf16[1,32,16,256]{3,2,1,0:T(8,128)(2,1)}, f32[32,128]{1,0:T(8,128)}) custom-call(s32[11]{0:T(128)} %pad_add_fusion.meta_ref, s32[256]{0:T(256)} %delay_ref.15, bf16[32,128,1024]{2,1,0:T(8,128)(2,1)} %est_ref.15, ...), custom_call_target="tpu_custom_call" | custom-call | flops 1073741824 | bytes 5242880 | tf_op jit(solution)/shard_map/spectra_apart/pallas_call | solution.py:296
  22.4 1.0 fusion.1
  23.4 1.2 fusion
  24.7 6.1 %collective-permute-start.2 = (bf16[3,96,1024]{2,1,0:T(8,128)(2,1)S(1)}, bf16[3,96,1024]{2,1,0:T(8,128)(2,1)S(1)}, u32[]{:S(2)}, u32[]{:S(2)}) collective-permute-start(bf16[3,96,1024]{2,1,0:T(8,128)(2,1)S(1)} %pad_maximum_fusion), channel_id=1, source_target_pairs={{0,1},{1,2},{2,3},{3,4},{4,5},{5,6},{6,7},{8,9},{9,10},{10,11},{11... | collective-permute-start | bytes 1769480 | tf_op jit(solution)/shard_map/ppermute | solution.py:429
  30.9 1.4 collective-permute-start.3
  32.3 11.3 %spectra_apart.3 = (bf16[1,32,16,256]{3,2,1,0:T(8,128)(2,1)}, bf16[1,32,16,256]{3,2,1,0:T(8,128)(2,1)}, bf16[1,32,16,256]{3,2,1,0:T(8,128)(2,1)}, bf16[1,32,16,256]{3,2,1,0:T(8,128)(2,1)}, f32[32,128]{1,0:T(8,128)}) custom-call(s32[11]{0:T(128)} %pad_add_fusion.meta_ref, s32[256]{0:T(256)} %delay_ref.15, bf16[32,128,1024]{2,1,0:T(8,128)(2,1)} %est_ref.15, ...), custom_call_target="tpu_custom_call" | custom-call | flops 1073741824 | bytes 5242880 | tf_op jit(solution)/shard_map/spectra_apart/pallas_call | solution.py:296
  44.6 11.2 %spectra_packed.3 = (bf16[4,32,16,256]{3,2,1,0:T(8,128)(2,1)}, f32[32,128]{1,0:T(8,128)}) custom-call(s32[11]{0:T(128)} %pad_add_fusion.meta_ref, s32[256]{0:T(256)} %delay_ref.15, bf16[32,128,1024]{2,1,0:T(8,128)(2,1)} %est_ref.15, bf16[32,128,1024]{2,1,0:T(8,128)(2,1)} %obs_ref.15, bf16[3,96,1024]{2,1,0:T(8,128)(2,1)} %copy-done, ...), custom_call_target="tpu_custom_call" | custom-call | flops 1073741824 | bytes 5242880 | tf_op jit(solution)/shard_map/spectra_packed/pallas_call | solution.py:296
  55.8 1.1 collective-permute-start.4
  56.9 1.5 collective-permute-start.6
  58.5 2.2 collective-permute-start.8
  61.3 11.1 %spectra_packed.4 = (bf16[4,32,16,256]{3,2,1,0:T(8,128)(2,1)}, f32[32,128]{1,0:T(8,128)}) custom-call(s32[11]{0:T(128)} %pad_add_fusion.meta_ref, s32[256]{0:T(256)} %delay_ref.15, bf16[32,128,1024]{2,1,0:T(8,128)(2,1)} %est_ref.15, bf16[32,128,1024]{2,1,0:T(8,128)(2,1)} %obs_ref.15, bf16[3,96,1024]{2,1,0:T(8,128)(2,1)} %copy-done, ...), custom_call_target="tpu_custom_call" | custom-call | flops 1073741824 | bytes 5242880 | tf_op jit(solution)/shard_map/spectra_packed/pallas_call | solution.py:296
  73.0 6.8 %collective-permute-done.8.refs_4_ = bf16[1,32,16,256]{3,2,1,0:T(8,128)(2,1)S(1)} collective-permute-done((bf16[1,32,16,256]{3,2,1,0:T(8,128)(2,1)S(1)}, bf16[1,32,16,256]{3,2,1,0:T(8,128)(2,1)S(1)}, u32[]{:S(2)}, u32[]{:S(2)}) %collective-permute-start.8) | collective-permute-done | bytes 262176 | tf_op jit(solution)/shard_map/ppermute | solution.py:420
  79.8 4.7 %collective-permute-start.9 = (bf16[1,32,16,256]{3,2,1,0:T(8,128)(2,1)}, bf16[1,32,16,256]{3,2,1,0:T(8,128)(2,1)}, u32[]{:S(2)}, u32[]{:S(2)}) collective-permute-start(bf16[1,32,16,256]{3,2,1,0:T(8,128)(2,1)} %get-tuple-element.86), channel_id=1, source_target_pairs={{0,5},{1,4},{2,7},{3,6},{4,1},{5,0},{6,3},{7,2},{8,13},{9,12},{10,... | collective-permute-start | bytes 786440 | tf_op jit(solution)/shard_map/ppermute | solution.py:420
  84.5 2.5 collective-permute-start.11
  87.0 11.8 %spectra_joined.3 = (bf16[2,32,16,256]{3,2,1,0:T(8,128)(2,1)}, bf16[2,32,16,256]{3,2,1,0:T(8,128)(2,1)}, bf16[2,32,16,256]{3,2,1,0:T(8,128)(2,1)}, bf16[2,32,16,256]{3,2,1,0:T(8,128)(2,1)}, f32[32,128]{1,0:T(8,128)}) custom-call(s32[11]{0:T(128)} %pad_add_fusion.meta_ref, s32[256]{0:T(256)} %delay_ref.15, bf16[32,128,1024]{2,1,0:T(8,128)(2,1)} %est_ref.15, ...), custom_call_target="tpu_custom_call" | custom-call | flops 1073741824 | bytes 5242880 | tf_op jit(solution)/shard_map/spectra_joined/pallas_call | solution.py:296
  99.0 2.4 collective-permute-done.9.refs_5_
  101.3 11.9 %shrink.4 = (bf16[2,32,16,256]{3,2,1,0:T(8,128)(2,1)}, bf16[2,32,16,256]{3,2,1,0:T(8,128)(2,1)}, bf16[2,32,16,256]{3,2,1,0:T(8,128)(2,1)}, bf16[2,32,16,256]{3,2,1,0:T(8,128)(2,1)}) custom-call(s32[11]{0:T(128)} %pad_add_fusion.meta_ref, bf16[512,256]{1,0:T(8,128)(2,1)} %constant.49.clone.table_ref, f32[1,256]{1,0:T(1,128)} %bitcast.29, ...), custom_call_target="tpu_custom_call" | custom-call | flops 2147483648 | bytes 4456448 | tf_op jit(solution)/shard_map/shrink/pallas_call | solution.py:351
  113.2 11.1 %spectra_packed.5 = (bf16[4,32,16,256]{3,2,1,0:T(8,128)(2,1)}, f32[32,128]{1,0:T(8,128)}) custom-call(s32[11]{0:T(128)} %pad_add_fusion.meta_ref, s32[256]{0:T(256)} %delay_ref.15, bf16[32,128,1024]{2,1,0:T(8,128)(2,1)} %est_ref.15, bf16[32,128,1024]{2,1,0:T(8,128)(2,1)} %obs_ref.15, bf16[3,96,1024]{2,1,0:T(8,128)(2,1)} %copy-done, ...), custom_call_target="tpu_custom_call" | custom-call | flops 1073741824 | bytes 5242880 | tf_op jit(solution)/shard_map/spectra_packed/pallas_call | solution.py:296
  124.3 3.1 collective-permute-start.16
  127.5 4.6 %collective-permute-start.14 = (bf16[2,32,16,256]{3,2,1,0:T(8,128)(2,1)S(1)}, bf16[2,32,16,256]{3,2,1,0:T(8,128)(2,1)}, u32[]{:S(2)}, u32[]{:S(2)}) collective-permute-start(bf16[2,32,16,256]{3,2,1,0:T(8,128)(2,1)S(1)} %copy-done.36), channel_id=1, source_target_pairs={{0,4},{1,5},{2,6},{3,7},{4,0},{5,1},{6,2},{7,3},{8,12},{9,13},{10,... | collective-permute-start | bytes 1572872 | tf_op jit(solution)/shard_map/ppermute | solution.py:420
  132.1 2.5 collective-permute-start.15
  134.6 1.0 copy-done.6
  135.5 11.9 %spectra_joined.4 = (bf16[2,32,16,256]{3,2,1,0:T(8,128)(2,1)}, bf16[2,32,16,256]{3,2,1,0:T(8,128)(2,1)}, bf16[2,32,16,256]{3,2,1,0:T(8,128)(2,1)}, bf16[2,32,16,256]{3,2,1,0:T(8,128)(2,1)}, f32[32,128]{1,0:T(8,128)}) custom-call(s32[11]{0:T(128)} %pad_add_fusion.meta_ref, s32[256]{0:T(256)} %delay_ref.15, bf16[32,128,1024]{2,1,0:T(8,128)(2,1)} %est_ref.15, ...), custom_call_target="tpu_custom_call" | custom-call | flops 1073741824 | bytes 5242880 | tf_op jit(solution)/shard_map/spectra_joined/pallas_call | solution.py:296
  147.5 1.9 collective-permute-start.18
  149.4 18.0 %collective-permute-done.14.refs_2_ = bf16[2,32,16,256]{3,2,1,0:T(8,128)(2,1)} collective-permute-done((bf16[2,32,16,256]{3,2,1,0:T(8,128)(2,1)S(1)}, bf16[2,32,16,256]{3,2,1,0:T(8,128)(2,1)}, u32[]{:S(2)}, u32[]{:S(2)}) %collective-permute-start.14) | collective-permute-done | bytes 524320 | tf_op jit(solution)/shard_map/ppermute | solution.py:420
  167.4 2.8 collective-permute-start.19
  170.2 31.5 %collective-permute-start.20 = (bf16[2,32,16,256]{3,2,1,0:T(8,128)(2,1)}, bf16[2,32,16,256]{3,2,1,0:T(8,128)(2,1)S(1)}, u32[]{:S(2)}, u32[]{:S(2)}) collective-permute-start(bf16[2,32,16,256]{3,2,1,0:T(8,128)(2,1)} %get-tuple-element.105), channel_id=1, source_target_pairs={{0,2},{1,3},{2,0},{3,1},{4,6},{5,7},{6,4},{7,5},{8,10},{9,11},{10,... | collective-permute-start | bytes 1572872 | tf_op jit(solution)/shard_map/ppermute | solution.py:420
  201.7 1.1 collective-permute-start.21
  202.8 9.5 %collective-permute-done.18.refs_2_ = bf16[2,32,16,256]{3,2,1,0:T(8,128)(2,1)S(1)} collective-permute-done((bf16[2,32,16,256]{3,2,1,0:T(8,128)(2,1)}, bf16[2,32,16,256]{3,2,1,0:T(8,128)(2,1)S(1)}, u32[]{:S(2)}, u32[]{:S(2)}) %collective-permute-start.18) | collective-permute-done | bytes 524320 | tf_op jit(solution)/shard_map/ppermute | solution.py:420
  213.1 2.8 collective-permute-start.22
  215.9 11.9 %shrink.5 = (bf16[2,32,16,256]{3,2,1,0:T(8,128)(2,1)}, bf16[2,32,16,256]{3,2,1,0:T(8,128)(2,1)}, bf16[2,32,16,256]{3,2,1,0:T(8,128)(2,1)}, bf16[2,32,16,256]{3,2,1,0:T(8,128)(2,1)}) custom-call(s32[11]{0:T(128)} %pad_add_fusion.meta_ref, bf16[512,256]{1,0:T(8,128)(2,1)} %constant.49.clone.table_ref, f32[1,256]{1,0:T(1,128)} %bitcast.30, ...), custom_call_target="tpu_custom_call" | custom-call | flops 2147483648 | bytes 4456448 | tf_op jit(solution)/shard_map/shrink/pallas_call | solution.py:351
  228.7 12.1 %spectra_joined.5 = (bf16[2,32,16,256]{3,2,1,0:T(8,128)(2,1)}, bf16[2,32,16,256]{3,2,1,0:T(8,128)(2,1)}, bf16[2,32,16,256]{3,2,1,0:T(8,128)(2,1)}, bf16[2,32,16,256]{3,2,1,0:T(8,128)(2,1)}, f32[32,128]{1,0:T(8,128)}) custom-call(s32[11]{0:T(128)} %pad_add_fusion.meta_ref, s32[256]{0:T(256)} %delay_ref.15, bf16[32,128,1024]{2,1,0:T(8,128)(2,1)} %est_ref.15, ...), custom_call_target="tpu_custom_call" | custom-call | flops 1073741824 | bytes 5242880 | tf_op jit(solution)/shard_map/spectra_joined/pallas_call | solution.py:296
  241.5 6.8 %collective-permute-start.27 = (bf16[2,32,16,256]{3,2,1,0:T(8,128)(2,1)}, bf16[2,32,16,256]{3,2,1,0:T(8,128)(2,1)S(1)}, u32[]{:S(2)}, u32[]{:S(2)}) collective-permute-start(bf16[2,32,16,256]{3,2,1,0:T(8,128)(2,1)} %get-tuple-element.115), channel_id=1, source_target_pairs={{0,4},{1,5},{2,6},{3,7},{4,0},{5,1},{6,2},{7,3},{8,12},{9,13},{10,... | collective-permute-start | bytes 1572872 | tf_op jit(solution)/shard_map/ppermute | solution.py:420
  248.4 11.8 %shrink.6 = (bf16[2,32,16,256]{3,2,1,0:T(8,128)(2,1)}, bf16[2,32,16,256]{3,2,1,0:T(8,128)(2,1)}, bf16[2,32,16,256]{3,2,1,0:T(8,128)(2,1)}, bf16[2,32,16,256]{3,2,1,0:T(8,128)(2,1)}) custom-call(s32[11]{0:T(128)} %pad_add_fusion.meta_ref, bf16[512,256]{1,0:T(8,128)(2,1)} %constant.49.clone.table_ref, f32[1,256]{1,0:T(1,128)} %bitcast.31, ...), custom_call_target="tpu_custom_call" | custom-call | flops 2147483648 | bytes 4456448 | tf_op jit(solution)/shard_map/shrink/pallas_call | solution.py:351
  260.2 8.3 %collective-permute-done.21.refs_2_ = bf16[2,32,16,256]{3,2,1,0:T(8,128)(2,1)S(1)} collective-permute-done((bf16[2,32,16,256]{3,2,1,0:T(8,128)(2,1)}, bf16[2,32,16,256]{3,2,1,0:T(8,128)(2,1)S(1)}, u32[]{:S(2)}, u32[]{:S(2)}) %collective-permute-start.21) | collective-permute-done | bytes 524320 | tf_op jit(solution)/shard_map/ppermute | solution.py:420
  269.6 5.4 %update.8 = (f32[32,128,1024]{2,1,0:T(8,128)}, f32[8,128]{1,0:T(8,128)}, bf16[4,32,16,256]{3,2,1,0:T(8,128)(2,1)}) custom-call(s32[11]{0:T(128)} %pad_add_fusion.meta_ref, bf16[1024,1024]{1,0:T(8,128)(2,1)} %constant.48.clone.table_ref, bf16[2,32,16,256]{3,2,1,0:T(8,128)(2,1)} %get-tuple-element.104._.refs_0_, ...), custom_call_target="tpu_custom_call" | custom-call | flops 1073741824 | bytes 5242880 | tf_op jit(solution)/shard_map/update/pallas_call | solution.py:393
  275.0 11.6 %collective-permute-start.23 = (bf16[2,32,16,256]{3,2,1,0:T(8,128)(2,1)}, bf16[2,32,16,256]{3,2,1,0:T(8,128)(2,1)S(1)}, u32[]{:S(2)}, u32[]{:S(2)}) collective-permute-start(bf16[2,32,16,256]{3,2,1,0:T(8,128)(2,1)} %get-tuple-element.110), channel_id=1, source_target_pairs={{0,2},{1,3},{2,0},{3,1},{4,6},{5,7},{6,4},{7,5},{8,10},{9,11},{10,... | collective-permute-start | bytes 1572872 | tf_op jit(solution)/shard_map/ppermute | solution.py:420
  286.6 1.1 collective-permute-start.24
  287.7 1.4 collective-permute-start.25
  289.1 1.4 collective-permute-done.27.refs_2_
  290.5 2.5 collective-permute-start.28
  293.0 19.6 %collective-permute-done.23.refs_1_ = bf16[2,32,16,256]{3,2,1,0:T(8,128)(2,1)S(1)} collective-permute-done((bf16[2,32,16,256]{3,2,1,0:T(8,128)(2,1)}, bf16[2,32,16,256]{3,2,1,0:T(8,128)(2,1)S(1)}, u32[]{:S(2)}, u32[]{:S(2)}) %collective-permute-start.23) | collective-permute-done | bytes 524320 | tf_op jit(solution)/shard_map/ppermute | solution.py:420
  312.6 23.7 %collective-permute-done.24.refs_2_ = bf16[2,32,16,256]{3,2,1,0:T(8,128)(2,1)S(1)} collective-permute-done((bf16[2,32,16,256]{3,2,1,0:T(8,128)(2,1)}, bf16[2,32,16,256]{3,2,1,0:T(8,128)(2,1)S(1)}, u32[]{:S(2)}, u32[]{:S(2)}) %collective-permute-start.24) | collective-permute-done | bytes 524320 | tf_op jit(solution)/shard_map/ppermute | solution.py:420
  337.0 2.5 collective-permute-start.32
  339.5 11.8 %shrink.7 = (bf16[1,32,16,256]{3,2,1,0:T(8,128)(2,1)}, bf16[1,32,16,256]{3,2,1,0:T(8,128)(2,1)}, bf16[1,32,16,256]{3,2,1,0:T(8,128)(2,1)}, bf16[1,32,16,256]{3,2...) custom-call(s32[11]{0:T(128)} %pad_add_fusion.meta_ref, ...), custom_call_target="tpu_custom_call" | custom-call | flops 2147483648 | bytes 4456448 | tf_op jit(solution)/shard_map/shrink/pallas_call | solution.py:351
  352.1 5.4 %update.9 = (f32[32,128,1024]{2,1,0:T(8,128)}, f32[8,128]{1,0:T(8,128)}, bf16[4,32,16,256]{3,2,1,0:T(8,128)(2,1)}) custom-call(s32[11]{0:T(128)} %pad_add_fusion.meta_ref, bf16[1024,1024]{1,0:T(8,128)(2,1)} %constant.48.clone.table_ref, bf16[1,32,16,256]{3,2,1,0:T(8,128)(2,1)} %get-tuple-element.113._.refs_0_, ...), custom_call_target="tpu_custom_call", output_to_operand_aliasing={{0}: (7, {})} | custom-call | flops 1073741824 | bytes 5242880 | tf_op jit(solution)/shard_map/update/pallas_call | solution.py:393
  358.6 5.1 %update.10 = (f32[32,128,1024]{2,1,0:T(8,128)}, f32[8,128]{1,0:T(8,128)}) custom-call(s32[11]{0:T(128)} %pad_add_fusion.meta_ref, bf16[1024,1024]{1,0:T(8,128)(2,1)} %constant.48.clone.table_ref, f32[8,128]{1,0:T(8,128)} %get-tuple-element.118._, bf16[4,32,16,256]{3,2,1,0:T(8,128)(2,1)} %copy-done.3, ...), custom_call_target="tpu_custom_call", output_to_operand_aliasing={{0}: (4, {})} | custom-call | flops 1073741824 | bytes 5242880 | tf_op jit(solution)/shard_map/update/pallas_call | solution.py:393
  363.7 28.7 %collective-permute-done.31.refs_2_ = bf16[2,32,16,256]{3,2,1,0:T(8,128)(2,1)S(1)} collective-permute-done((bf16[2,32,16,256]{3,2,1,0:T(8,128)(2,1)}, bf16[2,32,16,256]{3,2,1,0:T(8,128)(2,1)S(1)}, u32[]{:S(2)}, u32[]{:S(2)}) %collective-permute-start.31) | collective-permute-done | bytes 524320 | tf_op jit(solution)/shard_map/ppermute | solution.py:420
  393.2 5.4 %update.11 = (f32[32,128,1024]{2,1,0:T(8,128)}, f32[8,128]{1,0:T(8,128)}, bf16[4,32,16,256]{3,2,1,0:T(8,128)(2,1)}) custom-call(s32[11]{0:T(128)} %pad_add_fusion.meta_ref, bf16[1024,1024]{1,0:T(8,128)(2,1)} %constant.48.clone.table_ref, f32[8,128]{1,0:T(8,128)} %get-tuple-element.121._, ...), custom_call_target="tpu_custom_call", output_to_operand_aliasing={{0}: (7, {})} | custom-call | flops 1073741824 | bytes 5242880 | tf_op jit(solution)/shard_map/update/pallas_call | solution.py:393
  398.6 10.4 %collective-permute-start.34 = (bf16[1,32,16,256]{3,2,1,0:T(8,128)(2,1)}, bf16[1,32,16,256]{3,2,1,0:T(8,128)(2,1)S(1)}, u32[]{:S(2)}, u32[]{:S(2)}) collective-permute-start(bf16[1,32,16,256]{3,2,1,0:T(8,128)(2,1)} %get-tuple-element.130), channel_id=1, source_target_pairs={{0,2},{1,3},{2,0},{3,1},{4,6},{5,7},{6,4},{7,5},{8,10},{9,11},{10,... | collective-permute-start | bytes 786440 | tf_op jit(solution)/shard_map/ppermute | solution.py:420
  409.0 1.1 collective-permute-start.35
  410.1 1.4 collective-permute-start.36
  411.7 9.9 %psum.7 = f32[32]{0:T(128)S(1)} all-reduce(f32[32]{0:T(128)S(1)} %add_reduce_fusion), channel_id=1, replica_groups=mesh['patch'=4,'shot'=8] {'patch'}, use_global_device_ids=true, to_apply=%region_1.2 | all-reduce | flops 32 | bytes 256 | tf_op jit(solution)/shard_map/psum | solution.py:605
  422.1 8.4 %collective-permute-done.35.refs_2_ = bf16[1,32,16,256]{3,2,1,0:T(8,128)(2,1)S(1)} collective-permute-done((bf16[1,32,16,256]{3,2,1,0:T(8,128)(2,1)}, bf16[1,32,16,256]{3,2,1,0:T(8,128)(2,1)S(1)}, u32[]{:S(2)}, u32[]{:S(2)}) %collective-permute-start.35) | collective-permute-done | bytes 262176 | tf_op jit(solution)/shard_map/ppermute | solution.py:420
  430.6 5.3 %collective-permute-start.40 = (bf16[1,32,16,256]{3,2,1,0:T(8,128)(2,1)}, bf16[1,32,16,256]{3,2,1,0:T(8,128)(2,1)S(1)}, u32[]{:S(2)}, u32[]{:S(2)}) collective-permute-start(bf16[1,32,16,256]{3,2,1,0:T(8,128)(2,1)} %get-tuple-element.140), channel_id=1, source_target_pairs={{0,5},{1,4},{2,7},{3,6},{4,1},{5,0},{6,3},{7,2},{8,13},{9,12},{10,... | collective-permute-start | bytes 786440 | tf_op jit(solution)/shard_map/ppermute | solution.py:420
  435.9 2.1 collective-permute-start.41
  438.0 5.0 %update.12 = (f32[32,128,1024]{2,1,0:T(8,128)}, f32[8,128]{1,0:T(8,128)}) custom-call(s32[11]{0:T(128)} %pad_add_fusion.meta_ref, bf16[1024,1024]{1,0:T(8,128)(2,1)} %constant.48.clone.table_ref, f32[8,128]{1,0:T(8,128)} %get-tuple-element.126._, bf16[4,32,16,256]{3,2,1,0:T(8,128)(2,1)} %copy-done.2, ...), custom_call_target="tpu_custom_call", output_to_operand_aliasing={{0}: (4, {})} | custom-call | flops 1073741824 | bytes 5242880 | tf_op jit(solution)/shard_map/update/pallas_call | solution.py:393
  443.0 5.1 %update.13 = (f32[32,128,1024]{2,1,0:T(8,128)}, f32[8,128]{1,0:T(8,128)}) custom-call(s32[11]{0:T(128)} %pad_add_fusion.meta_ref, bf16[1024,1024]{1,0:T(8,128)(2,1)} %constant.48.clone.table_ref, f32[8,128]{1,0:T(8,128)} %get-tuple-element.129._, bf16[1,32,16,256]{3,2,1,0:T(8,128)(2,1)} %get-tuple-element.113._.refs_0_, ...), custom_call_target="tpu_custom_call", output_to_operand_aliasing={{0}: (7, {})} | custom-call | flops 1073741824 | bytes 5242880 | tf_op jit(solution)/shard_map/update/pallas_call | solution.py:393
  449.1 5.0 %update.14 = (f32[32,128,1024]{2,1,0:T(8,128)}, f32[8,128]{1,0:T(8,128)}) custom-call(s32[11]{0:T(128)} %pad_add_fusion.meta_ref, bf16[1024,1024]{1,0:T(8,128)(2,1)} %constant.48.clone.table_ref, f32[8,128]{1,0:T(8,128)} %get-tuple-element.134._, bf16[4,32,16,256]{3,2,1,0:T(8,128)(2,1)} %copy-done.5, ...), custom_call_target="tpu_custom_call", output_to_operand_aliasing={{0}: (4, {})} | custom-call | flops 1073741824 | bytes 5242880 | tf_op jit(solution)/shard_map/update/pallas_call | solution.py:393
  455.1 5.1 %update.15 = (f32[32,128,1024]{2,1,0:T(8,128)}, f32[8,128]{1,0:T(8,128)}) custom-call(s32[11]{0:T(128)} %pad_add_fusion.meta_ref, bf16[1024,1024]{1,0:T(8,128)(2,1)} %constant.48.clone.table_ref, f32[8,128]{1,0:T(8,128)} %get-tuple-element.137._, bf16[1,32,16,256]{3,2,1,0:T(8,128)(2,1)} %copy-done.18, ...), custom_call_target="tpu_custom_call", output_to_operand_aliasing={{0}: (7, {})} | custom-call | flops 1073741824 | bytes 5242880 | tf_op jit(solution)/shard_map/update/pallas_call | solution.py:393
  (153 shorter events, 15.0 us)
Async XLA Ops:
  2.5 5.1 %collective-permute-start = (bf16[3,32,1024]{2,1,0:T(8,128)(2,1)S(1)}, bf16[3,32,1024]{2,1,0:T(8,128)(2,1)S(1)}, u32[]{:S(2)}, u32[]{:S(2)}) collective-permute-start(bf16[3,32,1024]{2,1,0:T(8,128)(2,1)S(1)} %pad_maximum_fusion.2), channel_id=1, source_target_pairs={{0,1},{1,2},{2,3},{3,4},{4,5},{5,6},{6,7},{8,9},{9,10},{10,11},{11... | collective-permute-start | bytes 589832 | tf_op jit(solution)/shard_map/ppermute | solution.py:429
  5.0 5.5 %collective-permute-start.1 = (bf16[3,32,1024]{2,1,0:T(8,128)(2,1)S(1)}, bf16[3,32,1024]{2,1,0:T(8,128)(2,1)S(1)}, u32[]{:S(2)}, u32[]{:S(2)}) collective-permute-start(bf16[3,32,1024]{2,1,0:T(8,128)(2,1)S(1)} %pad_maximum_fusion.3), channel_id=1, source_target_pairs={{1,0},{2,1},{3,2},{4,3},{5,4},{6,5},{7,6},{9,8},{10,9},{11,10},{12... | collective-permute-start | bytes 589832 | tf_op jit(solution)/shard_map/ppermute | solution.py:429
  24.7 18.9 %collective-permute-start.2 = (bf16[3,96,1024]{2,1,0:T(8,128)(2,1)S(1)}, bf16[3,96,1024]{2,1,0:T(8,128)(2,1)S(1)}, u32[]{:S(2)}, u32[]{:S(2)}) collective-permute-start(bf16[3,96,1024]{2,1,0:T(8,128)(2,1)S(1)} %pad_maximum_fusion), channel_id=1, source_target_pairs={{0,1},{1,2},{2,3},{3,4},{4,5},{5,6},{6,7},{8,9},{9,10},{10,11},{11... | collective-permute-start | bytes 1769480 | tf_op jit(solution)/shard_map/ppermute | solution.py:429
  30.8 26.1 %copy-start.48 = (bf16[1,32,16,256]{3,2,1,0:T(8,128)(2,1)S(1)}, bf16[1,32,16,256]{3,2,1,0:T(8,128)(2,1)}, u32[]{:S(2)}) copy-start(bf16[1,32,16,256]{3,2,1,0:T(8,128)(2,1)} %get-tuple-element.83) | copy-start | bytes 786436
  30.8 27.6 %copy-start.47 = (bf16[1,32,16,256]{3,2,1,0:T(8,128)(2,1)S(1)}, bf16[1,32,16,256]{3,2,1,0:T(8,128)(2,1)}, u32[]{:S(2)}) copy-start(bf16[1,32,16,256]{3,2,1,0:T(8,128)(2,1)} %get-tuple-element.85) | copy-start | bytes 786436
  30.8 29.9 %copy-start.43 = (bf16[1,32,16,256]{3,2,1,0:T(8,128)(2,1)S(1)}, bf16[1,32,16,256]{3,2,1,0:T(8,128)(2,1)}, u32[]{:S(2)}) copy-start(bf16[1,32,16,256]{3,2,1,0:T(8,128)(2,1)} %get-tuple-element.87) | copy-start | bytes 786436
  30.9 12.7 %collective-permute-start.3 = (bf16[3,96,1024]{2,1,0:T(8,128)(2,1)S(1)}, bf16[3,96,1024]{2,1,0:T(8,128)(2,1)S(1)}, u32[]{:S(2)}, u32[]{:S(2)}) collective-permute-start(bf16[3,96,1024]{2,1,0:T(8,128)(2,1)S(1)} %pad_maximum_fusion.1), channel_id=1, source_target_pairs={{1,0},{2,1},{3,2},{4,3},{5,4},{6,5},{7,6},{9,8},{10,9},{11,10},{12... | collective-permute-start | bytes 1769480 | tf_op jit(solution)/shard_map/ppermute | solution.py:429
  44.6 40.0 %copy-start.42 = (bf16[1,32,16,256]{3,2,1,0:T(8,128)(2,1)S(1)}, bf16[1,32,16,256]{3,2,1,0:T(8,128)(2,1)}, u32[]{:S(2)}) copy-start(bf16[1,32,16,256]{3,2,1,0:T(8,128)(2,1)} %get-tuple-element.88) | copy-start | bytes 786436
  55.8 28.7 %collective-permute-start.4 = (bf16[4,32,16,256]{3,2,1,0:T(8,128)(2,1)}, bf16[4,32,16,256]{3,2,1,0:T(8,128)(2,1)S(1)}, u32[]{:S(2)}, u32[]{:S(2)}) collective-permute-start(bf16[4,32,16,256]{3,2,1,0:T(8,128)(2,1)} %get-tuple-element.79), channel_id=1, source_target_pairs={{0,1},{1,0},{2,3},{3,2},{4,5},{5,4},{6,7},{7,6},{8,9},{9,8},{10,11... | collective-permute-start | bytes 3145736 | tf_op jit(solution)/shard_map/ppermute | solution.py:420
  56.9 15.5 %collective-permute-start.6 = (bf16[1,32,16,256]{3,2,1,0:T(8,128)(2,1)S(1)}, bf16[1,32,16,256]{3,2,1,0:T(8,128)(2,1)S(1)}, u32[]{:S(2)}, u32[]{:S(2)}) collective-permute-start(bf16[1,32,16,256]{3,2,1,0:T(8,128)(2,1)S(1)} %copy-done.48), channel_id=1, source_target_pairs={{0,2},{1,3},{2,0},{3,1},{4,6},{5,7},{6,4},{7,5},{8,10},{9,11},{10,... | collective-permute-start | bytes 786440 | tf_op jit(solution)/shard_map/ppermute | solution.py:420
  58.5 21.3 %collective-permute-start.8 = (bf16[1,32,16,256]{3,2,1,0:T(8,128)(2,1)S(1)}, bf16[1,32,16,256]{3,2,1,0:T(8,128)(2,1)S(1)}, u32[]{:S(2)}, u32[]{:S(2)}) collective-permute-start(bf16[1,32,16,256]{3,2,1,0:T(8,128)(2,1)S(1)} %copy-done.47), channel_id=1, source_target_pairs={{0,4},{1,5},{2,6},{3,7},{4,0},{5,1},{6,2},{7,3},{8,12},{9,13},{10,... | collective-permute-start | bytes 786440 | tf_op jit(solution)/shard_map/ppermute | solution.py:420
  60.7 19.1 %collective-permute-start.10 = (bf16[1,32,16,256]{3,2,1,0:T(8,128)(2,1)S(1)}, bf16[1,32,16,256]{3,2,1,0:T(8,128)(2,1)S(1)}, u32[]{:S(2)}, u32[]{:S(2)}) collective-permute-start(bf16[1,32,16,256]{3,2,1,0:T(8,128)(2,1)S(1)} %copy-done.43), channel_id=1, source_target_pairs={{0,6},{1,7},{2,4},{3,5},{4,2},{5,3},{6,0},{7,1},{8,14},{9,15},{10,... | collective-permute-start | bytes 786440 | tf_op jit(solution)/shard_map/ppermute | solution.py:420
  72.4 62.1 %collective-permute-start.12 = (bf16[4,32,16,256]{3,2,1,0:T(8,128)(2,1)}, bf16[4,32,16,256]{3,2,1,0:T(8,128)(2,1)S(1)}, u32[]{:S(2)}, u32[]{:S(2)}) collective-permute-start(bf16[4,32,16,256]{3,2,1,0:T(8,128)(2,1)} %get-tuple-element.91), channel_id=1, source_target_pairs={{0,1},{1,0},{2,3},{3,2},{4,5},{5,4},{6,7},{7,6},{8,9},{9,8},{10,11... | collective-permute-start | bytes 3145736 | tf_op jit(solution)/shard_map/ppermute | solution.py:420
  72.5 26.4 %copy-start.44 = (bf16[1,32,16,256]{3,2,1,0:T(8,128)(2,1)}, bf16[1,32,16,256]{3,2,1,0:T(8,128)(2,1)S(1)}, u32[]{:S(2)}) copy-start(bf16[1,32,16,256]{3,2,1,0:T(8,128)(2,1)S(1)} %collective-permute-done.6.refs_2_) | copy-start | bytes 786436
  72.5 26.4 %collective-permute-start.5 = (bf16[1,32,16,256]{3,2,1,0:T(8,128)(2,1)}, bf16[1,32,16,256]{3,2,1,0:T(8,128)(2,1)}, u32[]{:S(2)}, u32[]{:S(2)}) collective-permute-start(bf16[1,32,16,256]{3,2,1,0:T(8,128)(2,1)} %get-tuple-element.82), channel_id=1, source_target_pairs={{0,1},{1,0},{2,3},{3,2},{4,5},{5,4},{6,7},{7,6},{8,9},{9,8},{10,11... | collective-permute-start | bytes 786440 | tf_op jit(solution)/shard_map/ppermute | solution.py:420
  79.8 19.1 %collective-permute-start.7 = (bf16[1,32,16,256]{3,2,1,0:T(8,128)(2,1)}, bf16[1,32,16,256]{3,2,1,0:T(8,128)(2,1)}, u32[]{:S(2)}, u32[]{:S(2)}) collective-permute-start(bf16[1,32,16,256]{3,2,1,0:T(8,128)(2,1)} %get-tuple-element.84), channel_id=1, source_target_pairs={{0,3},{1,2},{2,1},{3,0},{4,7},{5,6},{6,5},{7,4},{8,11},{9,10},{10,... | collective-permute-start | bytes 786440 | tf_op jit(solution)/shard_map/ppermute | solution.py:420
  79.8 21.5 %collective-permute-start.9 = (bf16[1,32,16,256]{3,2,1,0:T(8,128)(2,1)}, bf16[1,32,16,256]{3,2,1,0:T(8,128)(2,1)}, u32[]{:S(2)}, u32[]{:S(2)}) collective-permute-start(bf16[1,32,16,256]{3,2,1,0:T(8,128)(2,1)} %get-tuple-element.86), channel_id=1, source_target_pairs={{0,5},{1,4},{2,7},{3,6},{4,1},{5,0},{6,3},{7,2},{8,13},{9,12},{10,... | collective-permute-start | bytes 786440 | tf_op jit(solution)/shard_map/ppermute | solution.py:420
  84.5 16.8 %collective-permute-start.11 = (bf16[1,32,16,256]{3,2,1,0:T(8,128)(2,1)S(1)}, bf16[1,32,16,256]{3,2,1,0:T(8,128)(2,1)}, u32[]{:S(2)}, u32[]{:S(2)}) collective-permute-start(bf16[1,32,16,256]{3,2,1,0:T(8,128)(2,1)S(1)} %copy-done.42), channel_id=1, source_target_pairs={{0,7},{1,6},{2,5},{3,4},{4,3},{5,2},{6,1},{7,0},{8,15},{9,14},{10,... | collective-permute-start | bytes 786440 | tf_op jit(solution)/shard_map/ppermute | solution.py:420
  98.8 28.6 %copy-start.36 = (bf16[2,32,16,256]{3,2,1,0:T(8,128)(2,1)S(1)}, bf16[2,32,16,256]{3,2,1,0:T(8,128)(2,1)}, u32[]{:S(2)}) copy-start(bf16[2,32,16,256]{3,2,1,0:T(8,128)(2,1)} %get-tuple-element.95) | copy-start | bytes 1572868
  98.8 33.2 %copy-start.34 = (bf16[2,32,16,256]{3,2,1,0:T(8,128)(2,1)S(1)}, bf16[2,32,16,256]{3,2,1,0:T(8,128)(2,1)}, u32[]{:S(2)}) copy-start(bf16[2,32,16,256]{3,2,1,0:T(8,128)(2,1)} %get-tuple-element.96) | copy-start | bytes 1572868
  98.9 48.6 %collective-permute-start.13 = (bf16[2,32,16,256]{3,2,1,0:T(8,128)(2,1)}, bf16[2,32,16,256]{3,2,1,0:T(8,128)(2,1)S(1)}, u32[]{:S(2)}, u32[]{:S(2)}) collective-permute-start(bf16[2,32,16,256]{3,2,1,0:T(8,128)(2,1)} %get-tuple-element.94), channel_id=1, source_target_pairs={{0,2},{1,3},{2,0},{3,1},{4,6},{5,7},{6,4},{7,5},{8,10},{9,11},{10,... | collective-permute-start | bytes 1572872 | tf_op jit(solution)/shard_map/ppermute | solution.py:420
  124.3 103.4 %collective-permute-start.16 = (bf16[4,32,16,256]{3,2,1,0:T(8,128)(2,1)}, bf16[4,32,16,256]{3,2,1,0:T(8,128)(2,1)S(1)}, u32[]{:S(2)}, u32[]{:S(2)}) collective-permute-start(bf16[4,32,16,256]{3,2,1,0:T(8,128)(2,1)} %get-tuple-element.98), channel_id=1, source_target_pairs={{0,1},{1,0},{2,3},{3,2},{4,5},{5,4},{6,7},{7,6},{8,9},{9,8},{10,11... | collective-permute-start | bytes 3145736 | tf_op jit(solution)/shard_map/ppermute | solution.py:420
  127.5 40.0 %collective-permute-start.14 = (bf16[2,32,16,256]{3,2,1,0:T(8,128)(2,1)S(1)}, bf16[2,32,16,256]{3,2,1,0:T(8,128)(2,1)}, u32[]{:S(2)}, u32[]{:S(2)}) collective-permute-start(bf16[2,32,16,256]{3,2,1,0:T(8,128)(2,1)S(1)} %copy-done.36), channel_id=1, source_target_pairs={{0,4},{1,5},{2,6},{3,7},{4,0},{5,1},{6,2},{7,3},{8,12},{9,13},{10,... | collective-permute-start | bytes 1572872 | tf_op jit(solution)/shard_map/ppermute | solution.py:420
  132.1 38.1 %collective-permute-start.15 = (bf16[2,32,16,256]{3,2,1,0:T(8,128)(2,1)S(1)}, bf16[2,32,16,256]{3,2,1,0:T(8,128)(2,1)}, u32[]{:S(2)}, u32[]{:S(2)}) collective-permute-start(bf16[2,32,16,256]{3,2,1,0:T(8,128)(2,1)S(1)} %copy-done.34), channel_id=1, source_target_pairs={{0,6},{1,7},{2,4},{3,5},{4,2},{5,3},{6,0},{7,1},{8,14},{9,15},{10,... | collective-permute-start | bytes 1572872 | tf_op jit(solution)/shard_map/ppermute | solution.py:420
  147.4 54.2 %collective-permute-start.17 = (bf16[2,32,16,256]{3,2,1,0:T(8,128)(2,1)}, bf16[2,32,16,256]{3,2,1,0:T(8,128)(2,1)S(1)}, u32[]{:S(2)}, u32[]{:S(2)}) collective-permute-start(bf16[2,32,16,256]{3,2,1,0:T(8,128)(2,1)} %get-tuple-element.101), channel_id=1, source_target_pairs={{0,2},{1,3},{2,0},{3,1},{4,6},{5,7},{6,4},{7,5},{8,10},{9,11},{10,... | collective-permute-start | bytes 1572872 | tf_op jit(solution)/shard_map/ppermute | solution.py:420
  147.5 22.8 %copy-start.33 = (bf16[2,32,16,256]{3,2,1,0:T(8,128)(2,1)}, bf16[2,32,16,256]{3,2,1,0:T(8,128)(2,1)S(1)}, u32[]{:S(2)}) copy-start(bf16[2,32,16,256]{3,2,1,0:T(8,128)(2,1)S(1)} %collective-permute-done.13.refs_1_) | copy-start | bytes 1572868
  147.5 64.8 %collective-permute-start.18 = (bf16[2,32,16,256]{3,2,1,0:T(8,128)(2,1)}, bf16[2,32,16,256]{3,2,1,0:T(8,128)(2,1)S(1)}, u32[]{:S(2)}, u32[]{:S(2)}) collective-permute-start(bf16[2,32,16,256]{3,2,1,0:T(8,128)(2,1)} %get-tuple-element.102), channel_id=1, source_target_pairs={{0,4},{1,5},{2,6},{3,7},{4,0},{5,1},{6,2},{7,3},{8,12},{9,13},{10,... | collective-permute-start | bytes 1572872 | tf_op jit(solution)/shard_map/ppermute | solution.py:420
  167.4 73.3 %collective-permute-start.19 = (bf16[2,32,16,256]{3,2,1,0:T(8,128)(2,1)}, bf16[2,32,16,256]{3,2,1,0:T(8,128)(2,1)S(1)}, u32[]{:S(2)}, u32[]{:S(2)}) collective-permute-start(bf16[2,32,16,256]{3,2,1,0:T(8,128)(2,1)} %get-tuple-element.103), channel_id=1, source_target_pairs={{0,6},{1,7},{2,4},{3,5},{4,2},{5,3},{6,0},{7,1},{8,14},{9,15},{10,... | collective-permute-start | bytes 1572872 | tf_op jit(solution)/shard_map/ppermute | solution.py:420
  170.2 90.0 %collective-permute-start.20 = (bf16[2,32,16,256]{3,2,1,0:T(8,128)(2,1)}, bf16[2,32,16,256]{3,2,1,0:T(8,128)(2,1)S(1)}, u32[]{:S(2)}, u32[]{:S(2)}) collective-permute-start(bf16[2,32,16,256]{3,2,1,0:T(8,128)(2,1)} %get-tuple-element.105), channel_id=1, source_target_pairs={{0,2},{1,3},{2,0},{3,1},{4,6},{5,7},{6,4},{7,5},{8,10},{9,11},{10,... | collective-permute-start | bytes 1572872 | tf_op jit(solution)/shard_map/ppermute | solution.py:420
  201.7 66.8 %collective-permute-start.21 = (bf16[2,32,16,256]{3,2,1,0:T(8,128)(2,1)}, bf16[2,32,16,256]{3,2,1,0:T(8,128)(2,1)S(1)}, u32[]{:S(2)}, u32[]{:S(2)}) collective-permute-start(bf16[2,32,16,256]{3,2,1,0:T(8,128)(2,1)} %get-tuple-element.106), channel_id=1, source_target_pairs={{0,4},{1,5},{2,6},{3,7},{4,0},{5,1},{6,2},{7,3},{8,12},{9,13},{10,... | collective-permute-start | bytes 1572872 | tf_op jit(solution)/shard_map/ppermute | solution.py:420
  213.1 55.4 %collective-permute-start.22 = (bf16[2,32,16,256]{3,2,1,0:T(8,128)(2,1)}, bf16[2,32,16,256]{3,2,1,0:T(8,128)(2,1)S(1)}, u32[]{:S(2)}, u32[]{:S(2)}) collective-permute-start(bf16[2,32,16,256]{3,2,1,0:T(8,128)(2,1)} %get-tuple-element.107), channel_id=1, source_target_pairs={{0,6},{1,7},{2,4},{3,5},{4,2},{5,3},{6,0},{7,1},{8,14},{9,15},{10,... | collective-permute-start | bytes 1572872 | tf_op jit(solution)/shard_map/ppermute | solution.py:420
  227.7 60.0 %collective-permute-start.26 = (bf16[2,32,16,256]{3,2,1,0:T(8,128)(2,1)}, bf16[2,32,16,256]{3,2,1,0:T(8,128)(2,1)S(1)}, u32[]{:S(2)}, u32[]{:S(2)}) collective-permute-start(bf16[2,32,16,256]{3,2,1,0:T(8,128)(2,1)} %get-tuple-element.114), channel_id=1, source_target_pairs={{0,2},{1,3},{2,0},{3,1},{4,6},{5,7},{6,4},{7,5},{8,10},{9,11},{10,... | collective-permute-start | bytes 1572872 | tf_op jit(solution)/shard_map/ppermute | solution.py:420
  241.5 49.0 %collective-permute-start.27 = (bf16[2,32,16,256]{3,2,1,0:T(8,128)(2,1)}, bf16[2,32,16,256]{3,2,1,0:T(8,128)(2,1)S(1)}, u32[]{:S(2)}, u32[]{:S(2)}) collective-permute-start(bf16[2,32,16,256]{3,2,1,0:T(8,128)(2,1)} %get-tuple-element.115), channel_id=1, source_target_pairs={{0,4},{1,5},{2,6},{3,7},{4,0},{5,1},{6,2},{7,3},{8,12},{9,13},{10,... | collective-permute-start | bytes 1572872 | tf_op jit(solution)/shard_map/ppermute | solution.py:420
  275.0 82.6 %collective-permute-start.29 = (bf16[4,32,16,256]{3,2,1,0:T(8,128)(2,1)}, bf16[4,32,16,256]{3,2,1,0:T(8,128)(2,1)S(1)}, u32[]{:S(2)}, u32[]{:S(2)}) collective-permute-start(bf16[4,32,16,256]{3,2,1,0:T(8,128)(2,1)} %get-tuple-element.119), channel_id=1, source_target_pairs={{0,1},{1,0},{2,3},{3,2},{4,5},{5,4},{6,7},{7,6},{8,9},{9,8},{10,11... | collective-permute-start | bytes 3145736 | tf_op jit(solution)/shard_map/ppermute | solution.py:420
  275.0 37.6 %collective-permute-start.23 = (bf16[2,32,16,256]{3,2,1,0:T(8,128)(2,1)}, bf16[2,32,16,256]{3,2,1,0:T(8,128)(2,1)S(1)}, u32[]{:S(2)}, u32[]{:S(2)}) collective-permute-start(bf16[2,32,16,256]{3,2,1,0:T(8,128)(2,1)} %get-tuple-element.110), channel_id=1, source_target_pairs={{0,2},{1,3},{2,0},{3,1},{4,6},{5,7},{6,4},{7,5},{8,10},{9,11},{10,... | collective-permute-start | bytes 1572872 | tf_op jit(solution)/shard_map/ppermute | solution.py:420
  286.6 49.6 %collective-permute-start.24 = (bf16[2,32,16,256]{3,2,1,0:T(8,128)(2,1)}, bf16[2,32,16,256]{3,2,1,0:T(8,128)(2,1)S(1)}, u32[]{:S(2)}, u32[]{:S(2)}) collective-permute-start(bf16[2,32,16,256]{3,2,1,0:T(8,128)(2,1)} %get-tuple-element.111), channel_id=1, source_target_pairs={{0,4},{1,5},{2,6},{3,7},{4,0},{5,1},{6,2},{7,3},{8,12},{9,13},{10,... | collective-permute-start | bytes 1572872 | tf_op jit(solution)/shard_map/ppermute | solution.py:420
  287.7 63.6 %copy-start.10 = (bf16[2,32,16,256]{3,2,1,0:T(8,128)(2,1)}, bf16[2,32,16,256]{3,2,1,0:T(8,128)(2,1)S(1)}, u32[]{:S(2)}) copy-start(bf16[2,32,16,256]{3,2,1,0:T(8,128)(2,1)S(1)} %collective-permute-done.26.refs_1_) | copy-start | bytes 1572868
  287.7 49.3 %collective-permute-start.25 = (bf16[2,32,16,256]{3,2,1,0:T(8,128)(2,1)}, bf16[2,32,16,256]{3,2,1,0:T(8,128)(2,1)}, u32[]{:S(2)}, u32[]{:S(2)}) collective-permute-start(bf16[2,32,16,256]{3,2,1,0:T(8,128)(2,1)} %get-tuple-element.112), channel_id=1, source_target_pairs={{0,6},{1,7},{2,4},{3,5},{4,2},{5,3},{6,0},{7,1},{8,14},{9,15},{10,... | collective-permute-start | bytes 1572872 | tf_op jit(solution)/shard_map/ppermute | solution.py:420
  290.5 60.8 %copy-start.11 = (bf16[2,32,16,256]{3,2,1,0:T(8,128)(2,1)}, bf16[2,32,16,256]{3,2,1,0:T(8,128)(2,1)S(1)}, u32[]{:S(2)}) copy-start(bf16[2,32,16,256]{3,2,1,0:T(8,128)(2,1)S(1)} %collective-permute-done.27.refs_2_) | copy-start | bytes 1572868
  290.5 60.8 %collective-permute-start.28 = (bf16[2,32,16,256]{3,2,1,0:T(8,128)(2,1)}, bf16[2,32,16,256]{3,2,1,0:T(8,128)(2,1)S(1)}, u32[]{:S(2)}, u32[]{:S(2)}) collective-permute-start(bf16[2,32,16,256]{3,2,1,0:T(8,128)(2,1)} %get-tuple-element.116), channel_id=1, source_target_pairs={{0,6},{1,7},{2,4},{3,5},{4,2},{5,3},{6,0},{7,1},{8,14},{9,15},{10,... | collective-permute-start | bytes 1572872 | tf_op jit(solution)/shard_map/ppermute | solution.py:420
  312.5 23.7 %copy-start.39 = (bf16[2,32,16,256]{3,2,1,0:T(8,128)(2,1)}, bf16[2,32,16,256]{3,2,1,0:T(8,128)(2,1)S(1)}, u32[]{:S(2)}) copy-start(bf16[2,32,16,256]{3,2,1,0:T(8,128)(2,1)S(1)} %collective-permute-done.23.refs_1_) | copy-start | bytes 1572868
  312.6 51.2 %collective-permute-start.30 = (bf16[2,32,16,256]{3,2,1,0:T(8,128)(2,1)}, bf16[2,32,16,256]{3,2,1,0:T(8,128)(2,1)S(1)}, u32[]{:S(2)}, u32[]{:S(2)}) collective-permute-start(bf16[2,32,16,256]{3,2,1,0:T(8,128)(2,1)} %get-tuple-element.122), channel_id=1, source_target_pairs={{0,2},{1,3},{2,0},{3,1},{4,6},{5,7},{6,4},{7,5},{8,10},{9,11},{10,... | collective-permute-start | bytes 1572872 | tf_op jit(solution)/shard_map/ppermute | solution.py:420
  337.0 55.4 %collective-permute-start.31 = (bf16[2,32,16,256]{3,2,1,0:T(8,128)(2,1)}, bf16[2,32,16,256]{3,2,1,0:T(8,128)(2,1)S(1)}, u32[]{:S(2)}, u32[]{:S(2)}) collective-permute-start(bf16[2,32,16,256]{3,2,1,0:T(8,128)(2,1)} %get-tuple-element.123), channel_id=1, source_target_pairs={{0,4},{1,5},{2,6},{3,7},{4,0},{5,1},{6,2},{7,3},{8,12},{9,13},{10,... | collective-permute-start | bytes 1572872 | tf_op jit(solution)/shard_map/ppermute | solution.py:420
  337.0 55.4 %collective-permute-start.32 = (bf16[2,32,16,256]{3,2,1,0:T(8,128)(2,1)}, bf16[2,32,16,256]{3,2,1,0:T(8,128)(2,1)}, u32[]{:S(2)}, u32[]{:S(2)}) collective-permute-start(bf16[2,32,16,256]{3,2,1,0:T(8,128)(2,1)} %get-tuple-element.124), channel_id=1, source_target_pairs={{0,6},{1,7},{2,4},{3,5},{4,2},{5,3},{6,0},{7,1},{8,14},{9,15},{10,... | collective-permute-start | bytes 1572872 | tf_op jit(solution)/shard_map/ppermute | solution.py:420
  357.5 78.4 %collective-permute-start.33 = (bf16[4,32,16,256]{3,2,1,0:T(8,128)(2,1)}, bf16[4,32,16,256]{3,2,1,0:T(8,128)(2,1)S(1)}, u32[]{:S(2)}, u32[]{:S(2)}) collective-permute-start(bf16[4,32,16,256]{3,2,1,0:T(8,128)(2,1)} %get-tuple-element.127), channel_id=1, source_target_pairs={{0,1},{1,0},{2,3},{3,2},{4,5},{5,4},{6,7},{7,6},{8,9},{9,8},{10,11... | collective-permute-start | bytes 3145736 | tf_op jit(solution)/shard_map/ppermute | solution.py:420
  358.5 51.6 %copy-start.41 = (bf16[1,32,16,256]{3,2,1,0:T(8,128)(2,1)S(1)}, bf16[1,32,16,256]{3,2,1,0:T(8,128)(2,1)}, u32[]{:S(2)}) copy-start(bf16[1,32,16,256]{3,2,1,0:T(8,128)(2,1)} %get-tuple-element.132) | copy-start | bytes 786436
  358.5 52.9 %copy-start.25 = (f32[32,128]{1,0:T(8,128)S(1)}, f32[32,128]{1,0:T(8,128)}, u32[]{:S(2)}) copy-start(f32[32,128]{1,0:T(8,128)} %get-tuple-element.73._) | copy-start | bytes 49156
  358.5 52.9 %copy-start.26 = (f32[32,128]{1,0:T(8,128)S(1)}, f32[32,128]{1,0:T(8,128)}, u32[]{:S(2)}) copy-start(f32[32,128]{1,0:T(8,128)} %get-tuple-element.76._) | copy-start | bytes 49156
  358.5 52.9 %copy-start.27 = (f32[32,128]{1,0:T(8,128)S(1)}, f32[32,128]{1,0:T(8,128)}, u32[]{:S(2)}) copy-start(f32[32,128]{1,0:T(8,128)} %get-tuple-element.77._) | copy-start | bytes 49156
  358.5 52.9 %copy-start.28 = (f32[32,128]{1,0:T(8,128)S(1)}, f32[32,128]{1,0:T(8,128)}, u32[]{:S(2)}) copy-start(f32[32,128]{1,0:T(8,128)} %get-tuple-element.78._) | copy-start | bytes 49156
  358.6 52.9 %copy-start.29 = (f32[32,128]{1,0:T(8,128)S(1)}, f32[32,128]{1,0:T(8,128)}, u32[]{:S(2)}) copy-start(f32[32,128]{1,0:T(8,128)} %get-tuple-element.90._) | copy-start | bytes 49156
  358.6 52.9 %copy-start.30 = (f32[32,128]{1,0:T(8,128)S(1)}, f32[32,128]{1,0:T(8,128)}, u32[]{:S(2)}) copy-start(f32[32,128]{1,0:T(8,128)} %get-tuple-element.80._) | copy-start | bytes 49156
  358.6 52.9 %copy-start.31 = (f32[32,128]{1,0:T(8,128)S(1)}, f32[32,128]{1,0:T(8,128)}, u32[]{:S(2)}) copy-start(f32[32,128]{1,0:T(8,128)} %get-tuple-element.92._) | copy-start | bytes 49156
  358.6 52.9 %copy-start.32 = (f32[32,128]{1,0:T(8,128)S(1)}, f32[32,128]{1,0:T(8,128)}, u32[]{:S(2)}) copy-start(f32[32,128]{1,0:T(8,128)} %get-tuple-element.99._) | copy-start | bytes 49156
  363.7 28.7 %copy-start.12 = (bf16[2,32,16,256]{3,2,1,0:T(8,128)(2,1)}, bf16[2,32,16,256]{3,2,1,0:T(8,128)(2,1)S(1)}, u32[]{:S(2)}) copy-start(bf16[2,32,16,256]{3,2,1,0:T(8,128)(2,1)S(1)} %collective-permute-done.30.refs_1_) | copy-start | bytes 1572868
  398.6 49.6 %collective-permute-start.37 = (bf16[4,32,16,256]{3,2,1,0:T(8,128)(2,1)}, bf16[4,32,16,256]{3,2,1,0:T(8,128)(2,1)S(1)}, u32[]{:S(2)}, u32[]{:S(2)}) collective-permute-start(bf16[4,32,16,256]{3,2,1,0:T(8,128)(2,1)} %get-tuple-element.135), channel_id=1, source_target_pairs={{0,1},{1,0},{2,3},{3,2},{4,5},{5,4},{6,7},{7,6},{8,9},{9,8},{10,11... | collective-permute-start | bytes 3145736 | tf_op jit(solution)/shard_map/ppermute | solution.py:420
  398.6 23.5 %collective-permute-start.34 = (bf16[1,32,16,256]{3,2,1,0:T(8,128)(2,1)}, bf16[1,32,16,256]{3,2,1,0:T(8,128)(2,1)S(1)}, u32[]{:S(2)}, u32[]{:S(2)}) collective-permute-start(bf16[1,32,16,256]{3,2,1,0:T(8,128)(2,1)} %get-tuple-element.130), channel_id=1, source_target_pairs={{0,2},{1,3},{2,0},{3,1},{4,6},{5,7},{6,4},{7,5},{8,10},{9,11},{10,... | collective-permute-start | bytes 786440 | tf_op jit(solution)/shard_map/ppermute | solution.py:420
  409.0 21.5 %collective-permute-start.35 = (bf16[1,32,16,256]{3,2,1,0:T(8,128)(2,1)}, bf16[1,32,16,256]{3,2,1,0:T(8,128)(2,1)S(1)}, u32[]{:S(2)}, u32[]{:S(2)}) collective-permute-start(bf16[1,32,16,256]{3,2,1,0:T(8,128)(2,1)} %get-tuple-element.131), channel_id=1, source_target_pairs={{0,4},{1,5},{2,6},{3,7},{4,0},{5,1},{6,2},{7,3},{8,12},{9,13},{10,... | collective-permute-start | bytes 786440 | tf_op jit(solution)/shard_map/ppermute | solution.py:420
  410.1 20.4 %collective-permute-start.36 = (bf16[1,32,16,256]{3,2,1,0:T(8,128)(2,1)S(1)}, bf16[1,32,16,256]{3,2,1,0:T(8,128)(2,1)S(1)}, u32[]{:S(2)}, u32[]{:S(2)}) collective-permute-start(bf16[1,32,16,256]{3,2,1,0:T(8,128)(2,1)S(1)} %copy-done.41), channel_id=1, source_target_pairs={{0,6},{1,7},{2,4},{3,5},{4,2},{5,3},{6,0},{7,1},{8,14},{9,15},{10,... | collective-permute-start | bytes 786440 | tf_op jit(solution)/shard_map/ppermute | solution.py:420
  422.1 20.9 %copy-start.20 = (bf16[1,32,16,256]{3,2,1,0:T(8,128)(2,1)}, bf16[1,32,16,256]{3,2,1,0:T(8,128)(2,1)S(1)}, u32[]{:S(2)}) copy-start(bf16[1,32,16,256]{3,2,1,0:T(8,128)(2,1)S(1)} %collective-permute-done.34.refs_1_) | copy-start | bytes 786436
  422.1 32.0 %collective-permute-start.38 = (bf16[1,32,16,256]{3,2,1,0:T(8,128)(2,1)}, bf16[1,32,16,256]{3,2,1,0:T(8,128)(2,1)S(1)}, u32[]{:S(2)}, u32[]{:S(2)}) collective-permute-start(bf16[1,32,16,256]{3,2,1,0:T(8,128)(2,1)} %get-tuple-element.138), channel_id=1, source_target_pairs={{0,1},{1,0},{2,3},{3,2},{4,5},{5,4},{6,7},{7,6},{8,9},{9,8},{10,11... | collective-permute-start | bytes 786440 | tf_op jit(solution)/shard_map/ppermute | solution.py:420
  430.6 23.6 %collective-permute-start.39 = (bf16[1,32,16,256]{3,2,1,0:T(8,128)(2,1)}, bf16[1,32,16,256]{3,2,1,0:T(8,128)(2,1)S(1)}, u32[]{:S(2)}, u32[]{:S(2)}) collective-permute-start(bf16[1,32,16,256]{3,2,1,0:T(8,128)(2,1)} %get-tuple-element.139), channel_id=1, source_target_pairs={{0,3},{1,2},{2,1},{3,0},{4,7},{5,6},{6,5},{7,4},{8,11},{9,10},{10,... | collective-permute-start | bytes 786440 | tf_op jit(solution)/shard_map/ppermute | solution.py:420
  430.6 23.6 %collective-permute-start.40 = (bf16[1,32,16,256]{3,2,1,0:T(8,128)(2,1)}, bf16[1,32,16,256]{3,2,1,0:T(8,128)(2,1)S(1)}, u32[]{:S(2)}, u32[]{:S(2)}) collective-permute-start(bf16[1,32,16,256]{3,2,1,0:T(8,128)(2,1)} %get-tuple-element.140), channel_id=1, source_target_pairs={{0,5},{1,4},{2,7},{3,6},{4,1},{5,0},{6,3},{7,2},{8,13},{9,12},{10,... | collective-permute-start | bytes 786440 | tf_op jit(solution)/shard_map/ppermute | solution.py:420
  435.9 18.3 %collective-permute-start.41 = (bf16[1,32,16,256]{3,2,1,0:T(8,128)(2,1)}, bf16[1,32,16,256]{3,2,1,0:T(8,128)(2,1)S(1)}, u32[]{:S(2)}, u32[]{:S(2)}) collective-permute-start(bf16[1,32,16,256]{3,2,1,0:T(8,128)(2,1)} %get-tuple-element.141), channel_id=1, source_target_pairs={{0,7},{1,6},{2,5},{3,4},{4,3},{5,2},{6,1},{7,0},{8,15},{9,14},{10,... | collective-permute-start | bytes 786440 | tf_op jit(solution)/shard_map/ppermute | solution.py:420
  (27 other events, 81.8 us)

commit v5 on v4

--- a/solution.py
+++ b/solution.py
@@ -129,7 +129,7 @@
         energy_ref[pl.ds(shot, 1), :] = jnp.sum(power, axis=0, keepdims=True)
         return carry
 
-    lax.fori_loop(0, shots, middle, 0, unroll=2)
+    lax.fori_loop(0, shots, middle, 0, unroll=4)
 
     def step(shot, carry):
         later, earlier = blended(res32, shot + 1, first + shot)
@@ -143,7 +143,7 @@
             store(shot, column, cell.astype(jnp.bfloat16))
         return carry
 
-    lax.fori_loop(0, shots, step, 0, unroll=2)
+    lax.fori_loop(0, shots, step, 0, unroll=4)
 
 
 def spectra_kernel(outputs, packed, meta_ref, delay_ref, est_ref, obs_ref, before_ref, after_ref, table_ref, _, *refs):
@@ -293,6 +293,7 @@
     }[mode]
     group = min(shots, max(1, 256 // rows))
     partners = [] if partner is None else [partner]
+    start = lambda step: (0, 0, 0, 0)
     *spectra, energy = pl.pallas_call(
         functools.partial(spectra_kernel, len(shapes), mode == "packed"),
         grid_spec=pltpu.PrefetchScalarGridSpec(
@@ -300,7 +301,7 @@
             grid=(1,),
             in_specs=blend_specs(shots, rows, samples, block, edge_block)
             + [whole(table.shape), ANYWHERE]
-            + [whole(array.shape) for array in partners],
+            + [read(item, (chips, *block_shape), start) for item in partners],
             out_specs=[whole(shape) for shape in shapes] + [whole((shots, LANES))],
             scratch_shapes=blend_scratch(shots, rows, samples)
             + [
@@ -317,7 +318,7 @@
             transcendentals=0,
         ),
         name="spectra_" + mode,
-    )(meta, delays, *fields, table, after, *partners)
+    )(meta, delays, *fields, table, after, *[array for array, _ in partners])
     return spectra, energy
 
 
@@ -343,18 +344,19 @@
 
 
 def shrunk_of(meta, spectra, table, level, joined, after):
-    _, held, rows, width = spectra[0].shape
+    count, here, rows, width = spectra[0][0].shape[-4:]
     shots = table.shape[1]
-    peers = shots // held
+    peers = shots // here
     size = shots * rows * width
-    shapes = [(2, held, rows, width)] * (peers // 2) if joined else [(1, held, rows, width)] * peers
+    shapes = [(2, here, rows, width)] * (peers // 2) if joined else [(1, here, rows, width)] * peers
+    start = lambda step: (0, 0, 0, 0)
     return pl.pallas_call(
         functools.partial(shots_kernel, len(spectra)),
         grid_spec=pltpu.PrefetchScalarGridSpec(
             num_scalar_prefetch=1,
             grid=(1,),
             in_specs=[whole(table.shape), whole(level.shape), ANYWHERE]
-            + [whole(block.shape) for block in spectra],
+            + [read(item, (count, here, rows, width), start) for item in spectra],
             out_specs=[whole(shape) for shape in shapes],
             scratch_shapes=[pltpu.VMEM((width // LANES, shots * rows, LANES), jnp.float32)] * 2,
         ),
@@ -364,18 +366,20 @@
             flops=8 * shots * size, bytes_accessed=4 * size + 2 * table.size, transcendentals=size
         ),
         name="shrink",
-    )(meta, table, level, after, *spectra)
+    )(meta, table, level, after, *[array for array, _ in spectra])
 
 
 def updated_of(meta, restored, table, block, receivers, onto, passes, after):
-    _, shots, rows, width = restored[0].shape
+    count, shots, rows, width = restored[0][0].shape[-4:]
     samples = table.shape[1]
     chips = table.shape[0] // width
     group = min(shots, max(1, 256 // rows))
     by_shots = lambda step, meta: (0, step, 0, 0)
     in_specs = [whole(table.shape), ANYWHERE]
-    in_specs += [pl.BlockSpec((array.shape[0], group, rows, width), by_shots) for array in restored]
-    operands = [meta, table, after, *restored]
+    in_specs += [
+        read(item, (count, group, rows, width), lambda step: (0, step, 0, 0)) for item in restored
+    ]
+    operands = [meta, table, after, *[array for array, _ in restored]]
     if onto is not None:
         in_specs.append(ANYWHERE)
         operands.append(onto)
@@ -417,7 +421,24 @@
 
 def sent(array, distance):
     peers = lax.axis_size("shot")
-    return lax.ppermute(array, "shot", [(i, i ^ distance) for i in range(peers)])
+    if distance < peers // 2:
+        groups = [[i, i ^ distance] for i in range(peers) if i < i ^ distance]
+        return lax.all_gather(array, "shot", axis_index_groups=groups), distance
+    return lax.ppermute(array, "shot", [(i, i ^ distance) for i in range(peers)]), 0
+
+
+def held(array):
+    return array, 0
+
+
+def read(item, shape, where):
+    _, distance = item
+    if distance == 0:
+        return pl.BlockSpec(shape, lambda step, meta, *_: where(step))
+    return pl.BlockSpec(
+        (None, *shape),
+        lambda step, meta, *_: (jnp.where(meta[3] < meta[3 + distance], 1, 0), *where(step)),
+    )
 
 
 def edges(estimate, observed):
@@ -498,10 +519,10 @@
                 packed[step] = sent(spectra[0], 1)
             elif mode == "joined":
                 far = [sent(spectra[chip], 2 * chip) for chip in range(1, chips)]
-                ahead[step] = [spectra[0], *far]
+                ahead[step] = [held(spectra[0]), *far]
             elif name == "own":
                 far = [sent(spectra[chip], 2 * chip) for chip in range(1, chips)]
-                ahead[step] = [spectra[0], *far]
+                ahead[step] = [held(spectra[0]), *far]
                 held_estimate, held_observed, _ = lax.optimization_barrier(
                     (estimate, observed, power)
                 )
@@ -519,7 +540,8 @@
             last = shrunk[0]
             unit = 1 if direct else 2
             behind[step] = [
-                sent(array, unit * index) if index else array for index, array in enumerate(shrunk)
+                sent(array, unit * index) if index else held(array)
+                for index, array in enumerate(shrunk)
             ]
         elif name == "update own":
             direct = step == steps - 1

time: 464 us -> 575 us (1.24)
  blocking collectives: 9.91 us -> 93 us
  waiting for transfers between devices: 130 us -> 199 us
  starting transfers between devices: 121 us -> 82.6 us
  between operations: 1.13 us -> 14.7 us
  Pallas kernels: 181 us -> 169 us
    all_gather x0 -> x6, blocking collectives: none -> 83.4 us  [sent(): return (lax.all_gather(array, 'shot', axis_index_groups=groups), distance)]
    ppermute x38 -> x20, waiting for transfers between devices: 127 us -> 192 us  [sent(): lax.ppermute(array, 'shot', [(i, i ^ distance) for i in range(peers)])]
    ppermute x38 -> x20, starting transfers between devices: 110 us -> 70.3 us  [sent(): lax.ppermute(array, 'shot', [(i, i ^ distance) for i in range(peers)])]
    pallas_call x8, Pallas kernels: 91.8 us -> 80.2 us  [spectra_of(): pl.pallas_call(functools.partial(spectra_kernel, len(shapes), mode == 'pa...]
  transfers between devices with their start and end apart: 42 -> 36, of which waited for: 11 -> 9; matrix products, arithmetic and copies ran while one was open for 0% -> 0% of each run, Pallas kernels for 33% -> 25%
where the time goes in v5:
time: 575 us; the launch traced here: 574 us
  waiting for transfers between devices  199 us (35%)
  Pallas kernels  169 us (29%)
  blocking collectives  93 us (16%)
  starting transfers between devices  82.6 us (14%)
  between operations  14.7 us (3%)
  local copies, waits for them, and re-layouts  14 us (2%)
    ppermute x20, waiting for transfers between devices, sent(): lax.ppermute(array, 'shot', [(i, i ^ distance) for i in range(peers)])  192 us
    all_gather x6, blocking collectives, sent(): return (lax.all_gather(array, 'shot', axis_index_groups=groups), distance)  83.4 us
    pallas_call x8, Pallas kernels, spectra_of(): pl.pallas_call(functools.partial(spectra_kernel, len(shapes), mode == 'pa...  80.2 us
    ppermute x20, starting transfers between devices, sent(): lax.ppermute(array, 'shot', [(i, i ^ distance) for i in range(peers)])  70.3 us
    pallas_call x4, Pallas kernels, shrunk_of(): pl.pallas_call(functools.partial(shots_kernel, len(spectra)), grid_spec=p...  47.4 us
    pallas_call x8, Pallas kernels, updated_of(): pl.pallas_call(functools.partial(update_kernel, len(restored), passes), g...  41.8 us
    ppermute x4, starting transfers between devices, edges(): return (lax.ppermute(tail, 'shot', up), lax.ppermute(head, 'shot', down))  11.7 us
  transfers between devices with their start and end apart: 36, of which 9 were waited for; matrix products, arithmetic and copies ran while one was open for 0% of the time, Pallas kernels for 25%

profile of v5, /device:TPU:0, one launch (start us, length us, event | category | flops | bytes accessed | tf_op | source)
XLA Modules:
  0.0 574.1 jit_solution(920493687647812101)
XLA Ops:
  7.2 1.0 fusion.2
  8.2 0.9 fusion.3
  9.1 2.4 collective-permute-start
  11.5 1.3 collective-permute-start.1
  14.2 2.9 collective-permute-done.1.after_ref
  17.7 9.8 %spectra_apart.2 = (bf16[1,32,16,256]{3,2,1,0:T(8,128)(2,1)}, bf16[1,32,16,256]{3,2,1,0:T(8,128)(2,1)}, bf16[1,32,16,256]{3,2,1,0:T(8,128)(2,1)}, bf16[1,32,16,256]{3,2,1,0:T(8,128)(2,1)}, f32[32,128]{1,0:T(8,128)}) custom-call(s32[11]{0:T(128)} %pad_add_fusion.meta_ref, s32[256]{0:T(256)} %delay_ref.15, bf16[32,128,1024]{2,1,0:T(8,128)(2,1)} %est_ref.15, ...), custom_call_target="tpu_custom_call" | custom-call | flops 1073741824 | bytes 5242880 | tf_op jit(solution)/shard_map/spectra_apart/pallas_call | solution.py:297
  27.5 1.2 fusion
  28.6 1.1 fusion.1
  29.8 1.3 collective-permute-start.3
  31.1 6.7 %collective-permute-start.2 = (bf16[3,96,1024]{2,1,0:T(8,128)(2,1)S(1)}, bf16[3,96,1024]{2,1,0:T(8,128)(2,1)S(1)}, u32[]{:S(2)}, u32[]{:S(2)}) collective-permute-start(bf16[3,96,1024]{2,1,0:T(8,128)(2,1)S(1)} %pad_maximum_fusion), channel_id=1, source_target_pairs={{0,1},{1,2},{2,3},{3,4},{4,5},{5,6},{6,7},{8,9},{9,10},{10,11},{11... | collective-permute-start | bytes 1769480 | tf_op jit(solution)/shard_map/ppermute | solution.py:450
  37.9 9.7 %spectra_apart.3 = (bf16[1,32,16,256]{3,2,1,0:T(8,128)(2,1)}, bf16[1,32,16,256]{3,2,1,0:T(8,128)(2,1)}, bf16[1,32,16,256]{3,2,1,0:T(8,128)(2,1)}, bf16[1,32,16,256]{3,2,1,0:T(8,128)(2,1)}, f32[32,128]{1,0:T(8,128)}) custom-call(s32[11]{0:T(128)} %pad_add_fusion.meta_ref, s32[256]{0:T(256)} %delay_ref.15, bf16[32,128,1024]{2,1,0:T(8,128)(2,1)} %est_ref.15, ...), custom_call_target="tpu_custom_call" | custom-call | flops 1073741824 | bytes 5242880 | tf_op jit(solution)/shard_map/spectra_apart/pallas_call | solution.py:297
  47.6 0.8 copy-done
  48.6 9.7 %spectra_packed.3 = (bf16[4,32,16,256]{3,2,1,0:T(8,128)(2,1)}, f32[32,128]{1,0:T(8,128)}) custom-call(s32[11]{0:T(128)} %pad_add_fusion.meta_ref, s32[256]{0:T(256)} %delay_ref.15, bf16[32,128,1024]{2,1,0:T(8,128)(2,1)} %est_ref.15, bf16[32,128,1024]{2,1,0:T(8,128)(2,1)} %obs_ref.15, bf16[3,96,1024]{2,1,0:T(8,128)(2,1)} %copy-done.1, ...), custom_call_target="tpu_custom_call" | custom-call | flops 1073741824 | bytes 5242880 | tf_op jit(solution)/shard_map/spectra_packed/pallas_call | solution.py:297
  58.4 9.7 %spectra_packed.4 = (bf16[4,32,16,256]{3,2,1,0:T(8,128)(2,1)}, f32[32,128]{1,0:T(8,128)}) custom-call(s32[11]{0:T(128)} %pad_add_fusion.meta_ref, s32[256]{0:T(256)} %delay_ref.15, bf16[32,128,1024]{2,1,0:T(8,128)(2,1)} %est_ref.15, bf16[32,128,1024]{2,1,0:T(8,128)(2,1)} %obs_ref.15, bf16[3,96,1024]{2,1,0:T(8,128)(2,1)} %copy-done.1, ...), custom_call_target="tpu_custom_call" | custom-call | flops 1073741824 | bytes 5242880 | tf_op jit(solution)/shard_map/spectra_packed/pallas_call | solution.py:297
  68.2 2.5 all-gather.31.cloned.1.call-done
  70.7 10.5 %spectra_joined.3 = (bf16[2,32,16,256]{3,2,1,0:T(8,128)(2,1)}, bf16[2,32,16,256]{3,2,1,0:T(8,128)(2,1)}, bf16[2,32,16,256]{3,2,1,0:T(8,128)(2,1)}, bf16[2,32,16,256]{3,2,1,0:T(8,128)(2,1)}, f32[32,128]{1,0:T(8,128)}) custom-call(s32[11]{0:T(128)} %pad_add_fusion.meta_ref, s32[256]{0:T(256)} %delay_ref.15, bf16[32,128,1024]{2,1,0:T(8,128)(2,1)} %est_ref.15, ...), custom_call_target="tpu_custom_call" | custom-call | flops 1073741824 | bytes 5242880 | tf_op jit(solution)/shard_map/spectra_joined/pallas_call | solution.py:297
  81.3 2.6 collective-permute-start.5
  83.9 1.3 collective-permute-start.7
  85.2 1.5 collective-permute-start.4
  86.7 1.2 collective-permute-start.6
  87.8 2.3 all-gather.1
  90.2 33.8 %all-gather.3 = bf16[2,32,16,256]{3,2,1,0:T(8,128)(2,1)} all-gather(bf16[1,32,16,256]{3,2,1,0:T(8,128)(2,1)S(1)} %copy-done.18), channel_id=5, replica_groups={{0,3},{1,2},{4,7},{5,6},{8,11},{9,10},{12,15},{13,14},{16,19},{17,18},{..., dimensions={0}, use_global_device_ids=true | all-gather | bytes 786432 | tf_op jit(solution)/shard_map/all_gather | solution.py:426
  123.9 12.0 %all-gather.2 = bf16[2,32,16,256]{3,2,1,0:T(8,128)(2,1)} all-gather(bf16[1,32,16,256]{3,2,1,0:T(8,128)(2,1)S(1)} %copy-done.17), channel_id=4, replica_groups={{0,2},{1,3},{4,6},{5,7},{8,10},{9,11},{12,14},{13,15},{16,18},{17,19},{..., dimensions={0}, use_global_device_ids=true | all-gather | bytes 786432 | tf_op jit(solution)/shard_map/all_gather | solution.py:426
  136.9 11.8 %shrink.4 = (bf16[2,32,16,256]{3,2,1,0:T(8,128)(2,1)}, bf16[2,32,16,256]{3,2,1,0:T(8,128)(2,1)}, bf16[2,32,16,256]{3,2,1,0:T(8,128)(2,1)}, bf16[2,32,16,256]{3,2,1,0:T(8,128)(2,1)}) custom-call(s32[11]{0:T(128)} %pad_add_fusion.meta_ref, bf16[512,256]{1,0:T(8,128)(2,1)} %constant.49.clone.table_ref, f32[1,256]{1,0:T(1,128)} %bitcast.62, ...), custom_call_target="tpu_custom_call" | custom-call | flops 2147483648 | bytes 4456448 | tf_op jit(solution)/shard_map/shrink/pallas_call | solution.py:353
  148.7 9.7 %spectra_packed.5 = (bf16[4,32,16,256]{3,2,1,0:T(8,128)(2,1)}, f32[32,128]{1,0:T(8,128)}) custom-call(s32[11]{0:T(128)} %pad_add_fusion.meta_ref, s32[256]{0:T(256)} %delay_ref.15, bf16[32,128,1024]{2,1,0:T(8,128)(2,1)} %est_ref.15, bf16[32,128,1024]{2,1,0:T(8,128)(2,1)} %obs_ref.15, bf16[3,96,1024]{2,1,0:T(8,128)(2,1)} %copy-done.1, ...), custom_call_target="tpu_custom_call" | custom-call | flops 1073741824 | bytes 5242880 | tf_op jit(solution)/shard_map/spectra_packed/pallas_call | solution.py:297
  158.5 10.5 %spectra_joined.4 = (bf16[2,32,16,256]{3,2,1,0:T(8,128)(2,1)}, bf16[2,32,16,256]{3,2,1,0:T(8,128)(2,1)}, bf16[2,32,16,256]{3,2,1,0:T(8,128)(2,1)}, bf16[2,32,16,256]{3,2,1,0:T(8,128)(2,1)}, f32[32,128]{1,0:T(8,128)}) custom-call(s32[11]{0:T(128)} %pad_add_fusion.meta_ref, s32[256]{0:T(256)} %delay_ref.15, bf16[32,128,1024]{2,1,0:T(8,128)(2,1)} %est_ref.15, ...), custom_call_target="tpu_custom_call" | custom-call | flops 1073741824 | bytes 5242880 | tf_op jit(solution)/shard_map/spectra_joined/pallas_call | solution.py:297
  169.7 1.6 collective-permute-start.8
  171.3 2.1 collective-permute-start.9
  173.4 34.5 %collective-permute-done.8.refs_2_ = bf16[2,32,16,256]{3,2,1,0:T(8,128)(2,1)S(1)} collective-permute-done((bf16[2,32,16,256]{3,2,1,0:T(8,128)(2,1)S(1)}, bf16[2,32,16,256]{3,2,1,0:T(8,128)(2,1)S(1)}, u32[]{:S(2)}, u32[]{:S(2)}) %collective-permute-start.8) | collective-permute-done | bytes 524320 | tf_op jit(solution)/shard_map/ppermute | solution.py:427
  208.9 11.8 %shrink.5 = (bf16[2,32,16,256]{3,2,1,0:T(8,128)(2,1)}, bf16[2,32,16,256]{3,2,1,0:T(8,128)(2,1)}, bf16[2,32,16,256]{3,2,1,0:T(8,128)(2,1)}, bf16[2,32,16,256]{3,2,1,0:T(8,128)(2,1)}) custom-call(s32[11]{0:T(128)} %pad_add_fusion.meta_ref, bf16[512,256]{1,0:T(8,128)(2,1)} %constant.49.clone.table_ref, f32[1,256]{1,0:T(1,128)} %bitcast.63, ...), custom_call_target="tpu_custom_call" | custom-call | flops 2147483648 | bytes 4456448 | tf_op jit(solution)/shard_map/shrink/pallas_call | solution.py:353
  220.8 10.6 %spectra_joined.5 = (bf16[2,32,16,256]{3,2,1,0:T(8,128)(2,1)}, bf16[2,32,16,256]{3,2,1,0:T(8,128)(2,1)}, bf16[2,32,16,256]{3,2,1,0:T(8,128)(2,1)}, bf16[2,32,16,256]{3,2,1,0:T(8,128)(2,1)}, f32[32,128]{1,0:T(8,128)}) custom-call(s32[11]{0:T(128)} %pad_add_fusion.meta_ref, s32[256]{0:T(256)} %delay_ref.15, bf16[32,128,1024]{2,1,0:T(8,128)(2,1)} %est_ref.15, ...), custom_call_target="tpu_custom_call" | custom-call | flops 1073741824 | bytes 5242880 | tf_op jit(solution)/shard_map/spectra_joined/pallas_call | solution.py:297
  232.2 11.5 %collective-permute-start.10 = (bf16[2,32,16,256]{3,2,1,0:T(8,128)(2,1)}, bf16[2,32,16,256]{3,2,1,0:T(8,128)(2,1)}, u32[]{:S(2)}, u32[]{:S(2)}) collective-permute-start(bf16[2,32,16,256]{3,2,1,0:T(8,128)(2,1)} %get-tuple-element.102), channel_id=1, source_target_pairs={{0,4},{1,5},{2,6},{3,7},{4,0},{5,1},{6,2},{7,3},{8,12},{9,13},{10,... | collective-permute-start | bytes 1572872 | tf_op jit(solution)/shard_map/ppermute | solution.py:427
  243.7 1.5 collective-permute-start.11
  245.2 2.4 collective-permute-start.13
  247.6 27.6 %collective-permute-done.10.refs_2_ = bf16[2,32,16,256]{3,2,1,0:T(8,128)(2,1)} collective-permute-done((bf16[2,32,16,256]{3,2,1,0:T(8,128)(2,1)}, bf16[2,32,16,256]{3,2,1,0:T(8,128)(2,1)}, u32[]{:S(2)}, u32[]{:S(2)}) %collective-permute-start.10) | collective-permute-done | bytes 524320 | tf_op jit(solution)/shard_map/ppermute | solution.py:427
  275.2 5.6 collective-permute-done.11.refs_3_
  280.9 11.8 %shrink.6 = (bf16[2,32,16,256]{3,2,1,0:T(8,128)(2,1)}, bf16[2,32,16,256]{3,2,1,0:T(8,128)(2,1)}, bf16[2,32,16,256]{3,2,1,0:T(8,128)(2,1)}, bf16[2,32,16,256]{3,2,1,0:T(8,128)(2,1)}) custom-call(s32[11]{0:T(128)} %pad_add_fusion.meta_ref, bf16[512,256]{1,0:T(8,128)(2,1)} %constant.49.clone.table_ref, f32[1,256]{1,0:T(1,128)} %bitcast.64, ...), custom_call_target="tpu_custom_call" | custom-call | flops 2147483648 | bytes 4456448 | tf_op jit(solution)/shard_map/shrink/pallas_call | solution.py:353
  292.7 31.2 %collective-permute-done.12.refs_2_ = bf16[2,32,16,256]{3,2,1,0:T(8,128)(2,1)S(1)} collective-permute-done((bf16[2,32,16,256]{3,2,1,0:T(8,128)(2,1)S(1)}, bf16[2,32,16,256]{3,2,1,0:T(8,128)(2,1)S(1)}, u32[]{:S(2)}, u32[]{:S(2)}) %collective-permute-start.12) | collective-permute-done | bytes 524320 | tf_op jit(solution)/shard_map/ppermute | solution.py:427
  324.9 5.4 update.8
  331.0 10.4 %collective-permute-start.14 = (bf16[2,32,16,256]{3,2,1,0:T(8,128)(2,1)}, bf16[2,32,16,256]{3,2,1,0:T(8,128)(2,1)S(1)}, u32[]{:S(2)}, u32[]{:S(2)}) collective-permute-start(bf16[2,32,16,256]{3,2,1,0:T(8,128)(2,1)} %get-tuple-element.111), channel_id=1, source_target_pairs={{0,4},{1,5},{2,6},{3,7},{4,0},{5,1},{6,2},{7,3},{8,12},{9,13},{10,... | collective-permute-start | bytes 1572872 | tf_op jit(solution)/shard_map/ppermute | solution.py:427
  341.4 3.2 collective-permute-start.15
  345.3 37.4 %collective-permute-done.14.refs_2_ = bf16[2,32,16,256]{3,2,1,0:T(8,128)(2,1)S(1)} collective-permute-done((bf16[2,32,16,256]{3,2,1,0:T(8,128)(2,1)}, bf16[2,32,16,256]{3,2,1,0:T(8,128)(2,1)S(1)}, u32[]{:S(2)}, u32[]{:S(2)}) %collective-permute-start.14) | collective-permute-done | bytes 524320 | tf_op jit(solution)/shard_map/ppermute | solution.py:427
  382.8 0.8 copy-done.36
  383.7 11.9 %shrink.7 = (bf16[1,32,16,256]{3,2,1,0:T(8,128)(2,1)}, bf16[1,32,16,256]{3,2,1,0:T(8,128)(2,1)}, bf16[1,32,16,256]{3,2,1,0:T(8,128)(2,1)}, bf16[1,32,16,256]{3,2...) custom-call(s32[11]{0:T(128)} %pad_add_fusion.meta_ref, ...), custom_call_target="tpu_custom_call" | custom-call | flops 2147483648 | bytes 4456448 | tf_op jit(solution)/shard_map/shrink/pallas_call | solution.py:353
  395.7 26.2 %collective-permute-done.16.refs_2_ = bf16[2,32,16,256]{3,2,1,0:T(8,128)(2,1)S(1)} collective-permute-done((bf16[2,32,16,256]{3,2,1,0:T(8,128)(2,1)S(1)}, bf16[2,32,16,256]{3,2,1,0:T(8,128)(2,1)S(1)}, u32[]{:S(2)}, u32[]{:S(2)}) %collective-permute-start.16) | collective-permute-done | bytes 524320 | tf_op jit(solution)/shard_map/ppermute | solution.py:427
  421.9 0.8 copy-done.4
  422.8 5.6 update.9
  428.5 12.5 %collective-permute-start.18 = (bf16[2,32,16,256]{3,2,1,0:T(8,128)(2,1)S(1)}, bf16[2,32,16,256]{3,2,1,0:T(8,128)(2,1)S(1)}, u32[]{:S(2)}, u32[]{:S(2)}) collective-permute-start(bf16[2,32,16,256]{3,2,1,0:T(8,128)(2,1)S(1)} %copy-done.33), channel_id=1, source_target_pairs={{0,4},{1,5},{2,6},{3,7},{4,0},{5,1},{6,2},{7,3},{8,12},{9,13},{10,... | collective-permute-start | bytes 1572872 | tf_op jit(solution)/shard_map/ppermute | solution.py:427
  441.4 5.0 update.10
  446.4 29.2 %collective-permute-done.18.refs_2_ = bf16[2,32,16,256]{3,2,1,0:T(8,128)(2,1)S(1)} collective-permute-done((bf16[2,32,16,256]{3,2,1,0:T(8,128)(2,1)S(1)}, bf16[2,32,16,256]{3,2,1,0:T(8,128)(2,1)S(1)}, u32[]{:S(2)}, u32[]{:S(2)}) %collective-permute-start.18) | collective-permute-done | bytes 524320 | tf_op jit(solution)/shard_map/ppermute | solution.py:427
  475.7 0.8 copy-done.6
  476.7 5.6 update.11
  482.6 9.5 %psum.7 = f32[32]{0:T(128)S(1)} all-reduce(f32[32]{0:T(128)S(1)} %add_reduce_fusion), channel_id=1, replica_groups=mesh['patch'=4,'shot'=8] {'patch'}, use_global_device_ids=true, to_apply=%region_1.2 | all-reduce | flops 32 | bytes 256 | tf_op jit(solution)/shard_map/psum | solution.py:627
  492.6 10.3 %collective-permute-start.20 = (bf16[1,32,16,256]{3,2,1,0:T(8,128)(2,1)S(1)}, bf16[1,32,16,256]{3,2,1,0:T(8,128)(2,1)S(1)}, u32[]{:S(2)}, u32[]{:S(2)}) collective-permute-start(bf16[1,32,16,256]{3,2,1,0:T(8,128)(2,1)S(1)} %copy-done.43), channel_id=1, source_target_pairs={{0,4},{1,5},{2,6},{3,7},{4,0},{5,1},{6,2},{7,3},{8,12},{9,13},{10,... | collective-permute-start | bytes 786440 | tf_op jit(solution)/shard_map/ppermute | solution.py:427
  503.0 3.4 collective-permute-start.21
  506.3 13.9 %all-gather.14 = bf16[2,32,16,256]{3,2,1,0:T(8,128)(2,1)} all-gather(bf16[1,32,16,256]{3,2,1,0:T(8,128)(2,1)S(1)} %copy-done.16), channel_id=16, replica_groups={{0,2},{1,3},{4,6},{5,7},{8,10},{9,11},{12,14},{13,15},{16,18},{17,19},{..., dimensions={0}, use_global_device_ids=true | all-gather | bytes 786432 | tf_op jit(solution)/shard_map/all_gather | solution.py:426
  520.3 2.3 all-gather.16
  522.6 1.8 collective-permute-start.22
  524.4 1.8 collective-permute-start.23
  526.2 19.2 %all-gather.17 = bf16[2,32,16,256]{3,2,1,0:T(8,128)(2,1)} all-gather(bf16[1,32,16,256]{3,2,1,0:T(8,128)(2,1)S(1)} %copy-done.14), channel_id=19, replica_groups={{0,3},{1,2},{4,7},{5,6},{8,11},{9,10},{12,15},{13,14},{16,19},{17,18},{..., dimensions={0}, use_global_device_ids=true | all-gather | bytes 786432 | tf_op jit(solution)/shard_map/all_gather | solution.py:426
  545.3 5.0 update.12
  551.2 5.1 update.13
  556.3 5.0 update.14
  562.1 5.2 update.15
  (165 shorter events, 11.7 us)
Async XLA Ops:
  7.2 63.5 %all-gather.31.cloned.1.call-start = ((), (), s32[]{:S(2)}) async-start(), calls=%async_computation | async-start | bytes 3145728 | tf_op jit(solution)/shard_map/all_gather | solution.py:426
  9.1 5.1 collective-permute-start
  11.5 5.5 collective-permute-start.1
  29.8 17.8 %collective-permute-start.3 = (bf16[3,96,1024]{2,1,0:T(8,128)(2,1)S(1)}, bf16[3,96,1024]{2,1,0:T(8,128)(2,1)S(1)}, u32[]{:S(2)}, u32[]{:S(2)}) collective-permute-start(bf16[3,96,1024]{2,1,0:T(8,128)(2,1)S(1)} %pad_maximum_fusion.1), channel_id=1, source_target_pairs={{1,0},{2,1},{3,2},{4,3},{5,4},{6,5},{7,6},{9,8},{10,9},{11,10},{12... | collective-permute-start | bytes 1769480 | tf_op jit(solution)/shard_map/ppermute | solution.py:450
  31.1 16.5 %collective-permute-start.2 = (bf16[3,96,1024]{2,1,0:T(8,128)(2,1)S(1)}, bf16[3,96,1024]{2,1,0:T(8,128)(2,1)S(1)}, u32[]{:S(2)}, u32[]{:S(2)}) collective-permute-start(bf16[3,96,1024]{2,1,0:T(8,128)(2,1)S(1)} %pad_maximum_fusion), channel_id=1, source_target_pairs={{0,1},{1,2},{2,3},{3,4},{4,5},{5,6},{6,7},{8,9},{9,10},{10,11},{11... | collective-permute-start | bytes 1769480 | tf_op jit(solution)/shard_map/ppermute | solution.py:450
  58.3 100.1 %all-gather.33.cloned.1.call-start = ((), (), s32[]{:S(2)}) async-start(), calls=%async_computation.1 | async-start | bytes 3145728 | tf_op jit(solution)/shard_map/all_gather | solution.py:426
  68.1 139.8 %all-gather.35.cloned.1.call-start = ((), (), s32[]{:S(2)}) async-start(), calls=%async_computation.2 | async-start | bytes 1572864 | tf_op jit(solution)/shard_map/all_gather | solution.py:426
  70.7 10.6 %copy-start.47 = (bf16[1,32,16,256]{3,2,1,0:T(8,128)(2,1)S(1)}, bf16[1,32,16,256]{3,2,1,0:T(8,128)(2,1)}, u32[]{:S(2)}) copy-start(bf16[1,32,16,256]{3,2,1,0:T(8,128)(2,1)} %get-tuple-element.86) | copy-start | bytes 786436
  70.7 13.3 %copy-start.46 = (bf16[1,32,16,256]{3,2,1,0:T(8,128)(2,1)S(1)}, bf16[1,32,16,256]{3,2,1,0:T(8,128)(2,1)}, u32[]{:S(2)}) copy-start(bf16[1,32,16,256]{3,2,1,0:T(8,128)(2,1)} %get-tuple-element.88) | copy-start | bytes 786436
  70.7 14.5 %copy-start.45 = (bf16[1,32,16,256]{3,2,1,0:T(8,128)(2,1)S(1)}, bf16[1,32,16,256]{3,2,1,0:T(8,128)(2,1)}, u32[]{:S(2)}) copy-start(bf16[1,32,16,256]{3,2,1,0:T(8,128)(2,1)} %get-tuple-element.85) | copy-start | bytes 786436
  70.7 16.0 %copy-start.44 = (bf16[1,32,16,256]{3,2,1,0:T(8,128)(2,1)S(1)}, bf16[1,32,16,256]{3,2,1,0:T(8,128)(2,1)}, u32[]{:S(2)}) copy-start(bf16[1,32,16,256]{3,2,1,0:T(8,128)(2,1)} %get-tuple-element.87) | copy-start | bytes 786436
  70.7 17.2 %copy-start.19 = (bf16[1,32,16,256]{3,2,1,0:T(8,128)(2,1)S(1)}, bf16[1,32,16,256]{3,2,1,0:T(8,128)(2,1)}, u32[]{:S(2)}) copy-start(bf16[1,32,16,256]{3,2,1,0:T(8,128)(2,1)} %get-tuple-element.82) | copy-start | bytes 786436
  70.7 19.5 %copy-start.18 = (bf16[1,32,16,256]{3,2,1,0:T(8,128)(2,1)S(1)}, bf16[1,32,16,256]{3,2,1,0:T(8,128)(2,1)}, u32[]{:S(2)}) copy-start(bf16[1,32,16,256]{3,2,1,0:T(8,128)(2,1)} %get-tuple-element.84) | copy-start | bytes 786436
  70.7 53.2 %copy-start.17 = (bf16[1,32,16,256]{3,2,1,0:T(8,128)(2,1)S(1)}, bf16[1,32,16,256]{3,2,1,0:T(8,128)(2,1)}, u32[]{:S(2)}) copy-start(bf16[1,32,16,256]{3,2,1,0:T(8,128)(2,1)} %get-tuple-element.83) | copy-start | bytes 786436
  81.2 139.5 %all-gather.37.cloned.1.call-start = ((), (), s32[]{:S(2)}) async-start(), calls=%async_computation.3 | async-start | bytes 3145728 | tf_op jit(solution)/shard_map/all_gather | solution.py:426
  81.3 54.6 %collective-permute-start.5 = (bf16[1,32,16,256]{3,2,1,0:T(8,128)(2,1)S(1)}, bf16[1,32,16,256]{3,2,1,0:T(8,128)(2,1)S(1)}, u32[]{:S(2)}, u32[]{:S(2)}) collective-permute-start(bf16[1,32,16,256]{3,2,1,0:T(8,128)(2,1)S(1)} %copy-done.47), channel_id=1, source_target_pairs={{0,5},{1,4},{2,7},{3,6},{4,1},{5,0},{6,3},{7,2},{8,13},{9,12},{10,... | collective-permute-start | bytes 786440 | tf_op jit(solution)/shard_map/ppermute | solution.py:427
  83.9 52.0 %collective-permute-start.7 = (bf16[1,32,16,256]{3,2,1,0:T(8,128)(2,1)S(1)}, bf16[1,32,16,256]{3,2,1,0:T(8,128)(2,1)S(1)}, u32[]{:S(2)}, u32[]{:S(2)}) collective-permute-start(bf16[1,32,16,256]{3,2,1,0:T(8,128)(2,1)S(1)} %copy-done.46), channel_id=1, source_target_pairs={{0,7},{1,6},{2,5},{3,4},{4,3},{5,2},{6,1},{7,0},{8,15},{9,14},{10,... | collective-permute-start | bytes 786440 | tf_op jit(solution)/shard_map/ppermute | solution.py:427
  85.2 50.7 %collective-permute-start.4 = (bf16[1,32,16,256]{3,2,1,0:T(8,128)(2,1)S(1)}, bf16[1,32,16,256]{3,2,1,0:T(8,128)(2,1)S(1)}, u32[]{:S(2)}, u32[]{:S(2)}) collective-permute-start(bf16[1,32,16,256]{3,2,1,0:T(8,128)(2,1)S(1)} %copy-done.45), channel_id=1, source_target_pairs={{0,4},{1,5},{2,6},{3,7},{4,0},{5,1},{6,2},{7,3},{8,12},{9,13},{10,... | collective-permute-start | bytes 786440 | tf_op jit(solution)/shard_map/ppermute | solution.py:427
  86.7 49.3 %collective-permute-start.6 = (bf16[1,32,16,256]{3,2,1,0:T(8,128)(2,1)S(1)}, bf16[1,32,16,256]{3,2,1,0:T(8,128)(2,1)S(1)}, u32[]{:S(2)}, u32[]{:S(2)}) collective-permute-start(bf16[1,32,16,256]{3,2,1,0:T(8,128)(2,1)S(1)} %copy-done.44), channel_id=1, source_target_pairs={{0,6},{1,7},{2,4},{3,5},{4,2},{5,3},{6,0},{7,1},{8,14},{9,15},{10,... | collective-permute-start | bytes 786440 | tf_op jit(solution)/shard_map/ppermute | solution.py:427
  158.4 122.5 %all-gather.39.cloned.1.call-start = ((), (), s32[]{:S(2)}) async-start(), calls=%async_computation.4 | async-start | bytes 1572864 | tf_op jit(solution)/shard_map/all_gather | solution.py:426
  158.5 11.2 %copy-start.35 = (bf16[2,32,16,256]{3,2,1,0:T(8,128)(2,1)S(1)}, bf16[2,32,16,256]{3,2,1,0:T(8,128)(2,1)}, u32[]{:S(2)}) copy-start(bf16[2,32,16,256]{3,2,1,0:T(8,128)(2,1)} %get-tuple-element.95) | copy-start | bytes 1572868
  158.5 12.8 %copy-start.34 = (bf16[2,32,16,256]{3,2,1,0:T(8,128)(2,1)S(1)}, bf16[2,32,16,256]{3,2,1,0:T(8,128)(2,1)}, u32[]{:S(2)}) copy-start(bf16[2,32,16,256]{3,2,1,0:T(8,128)(2,1)} %get-tuple-element.96) | copy-start | bytes 1572868
  169.0 154.9 %all-gather.41.cloned.1.call-start = ((), (), s32[]{:S(2)}) async-start(), calls=%async_computation.5 | async-start | bytes 1572864 | tf_op jit(solution)/shard_map/all_gather | solution.py:426
  169.6 213.2 %all-gather.43.cloned.1.call-start = ((), (), s32[]{:S(2)}) async-start(), calls=%async_computation.6 | async-start | bytes 1572864 | tf_op jit(solution)/shard_map/all_gather | solution.py:426
  169.7 38.3 %collective-permute-start.8 = (bf16[2,32,16,256]{3,2,1,0:T(8,128)(2,1)S(1)}, bf16[2,32,16,256]{3,2,1,0:T(8,128)(2,1)S(1)}, u32[]{:S(2)}, u32[]{:S(2)}) collective-permute-start(bf16[2,32,16,256]{3,2,1,0:T(8,128)(2,1)S(1)} %copy-done.35), channel_id=1, source_target_pairs={{0,4},{1,5},{2,6},{3,7},{4,0},{5,1},{6,2},{7,3},{8,12},{9,13},{10,... | collective-permute-start | bytes 1572872 | tf_op jit(solution)/shard_map/ppermute | solution.py:427
  171.3 36.7 %collective-permute-start.9 = (bf16[2,32,16,256]{3,2,1,0:T(8,128)(2,1)S(1)}, bf16[2,32,16,256]{3,2,1,0:T(8,128)(2,1)S(1)}, u32[]{:S(2)}, u32[]{:S(2)}) collective-permute-start(bf16[2,32,16,256]{3,2,1,0:T(8,128)(2,1)S(1)} %copy-done.34), channel_id=1, source_target_pairs={{0,6},{1,7},{2,4},{3,5},{4,2},{5,3},{6,0},{7,1},{8,14},{9,15},{10,... | collective-permute-start | bytes 1572872 | tf_op jit(solution)/shard_map/ppermute | solution.py:427
  220.8 24.4 %copy-start.31 = (bf16[2,32,16,256]{3,2,1,0:T(8,128)(2,1)S(1)}, bf16[2,32,16,256]{3,2,1,0:T(8,128)(2,1)}, u32[]{:S(2)}) copy-start(bf16[2,32,16,256]{3,2,1,0:T(8,128)(2,1)} %get-tuple-element.106) | copy-start | bytes 1572868
  220.8 24.4 %copy-start.30 = (bf16[2,32,16,256]{3,2,1,0:T(8,128)(2,1)S(1)}, bf16[2,32,16,256]{3,2,1,0:T(8,128)(2,1)}, u32[]{:S(2)}) copy-start(bf16[2,32,16,256]{3,2,1,0:T(8,128)(2,1)} %get-tuple-element.107) | copy-start | bytes 1572868
  231.4 113.3 %copy-start.29 = (bf16[2,32,16,256]{3,2,1,0:T(8,128)(2,1)S(1)}, bf16[2,32,16,256]{3,2,1,0:T(8,128)(2,1)}, u32[]{:S(2)}) copy-start(bf16[2,32,16,256]{3,2,1,0:T(8,128)(2,1)} %get-tuple-element.115) | copy-start | bytes 1572868
  231.4 113.3 %copy-start.28 = (bf16[2,32,16,256]{3,2,1,0:T(8,128)(2,1)S(1)}, bf16[2,32,16,256]{3,2,1,0:T(8,128)(2,1)}, u32[]{:S(2)}) copy-start(bf16[2,32,16,256]{3,2,1,0:T(8,128)(2,1)} %get-tuple-element.116) | copy-start | bytes 1572868
  231.4 190.5 %all-gather.45.cloned.1.call-start = ((), (), s32[]{:S(2)}) async-start(), calls=%async_computation.7 | async-start | bytes 1572864 | tf_op jit(solution)/shard_map/all_gather | solution.py:426
  232.2 209.3 %all-gather.47.cloned.1.call-start = ((), (), s32[]{:S(2)}) async-start(), calls=%async_computation.8 | async-start | bytes 3145728 | tf_op jit(solution)/shard_map/all_gather | solution.py:426
  232.2 43.0 %collective-permute-start.10 = (bf16[2,32,16,256]{3,2,1,0:T(8,128)(2,1)}, bf16[2,32,16,256]{3,2,1,0:T(8,128)(2,1)}, u32[]{:S(2)}, u32[]{:S(2)}) collective-permute-start(bf16[2,32,16,256]{3,2,1,0:T(8,128)(2,1)} %get-tuple-element.102), channel_id=1, source_target_pairs={{0,4},{1,5},{2,6},{3,7},{4,0},{5,1},{6,2},{7,3},{8,12},{9,13},{10,... | collective-permute-start | bytes 1572872 | tf_op jit(solution)/shard_map/ppermute | solution.py:427
  243.7 37.1 %collective-permute-start.11 = (bf16[2,32,16,256]{3,2,1,0:T(8,128)(2,1)}, bf16[2,32,16,256]{3,2,1,0:T(8,128)(2,1)}, u32[]{:S(2)}, u32[]{:S(2)}) collective-permute-start(bf16[2,32,16,256]{3,2,1,0:T(8,128)(2,1)} %get-tuple-element.103), channel_id=1, source_target_pairs={{0,6},{1,7},{2,4},{3,5},{4,2},{5,3},{6,0},{7,1},{8,14},{9,15},{10,... | collective-permute-start | bytes 1572872 | tf_op jit(solution)/shard_map/ppermute | solution.py:427
  245.2 78.7 %collective-permute-start.12 = (bf16[2,32,16,256]{3,2,1,0:T(8,128)(2,1)S(1)}, bf16[2,32,16,256]{3,2,1,0:T(8,128)(2,1)S(1)}, u32[]{:S(2)}, u32[]{:S(2)}) collective-permute-start(bf16[2,32,16,256]{3,2,1,0:T(8,128)(2,1)S(1)} %copy-done.31), channel_id=1, source_target_pairs={{0,4},{1,5},{2,6},{3,7},{4,0},{5,1},{6,2},{7,3},{8,12},{9,13},{10,... | collective-permute-start | bytes 1572872 | tf_op jit(solution)/shard_map/ppermute | solution.py:427
  245.2 78.7 %collective-permute-start.13 = (bf16[2,32,16,256]{3,2,1,0:T(8,128)(2,1)S(1)}, bf16[2,32,16,256]{3,2,1,0:T(8,128)(2,1)S(1)}, u32[]{:S(2)}, u32[]{:S(2)}) collective-permute-start(bf16[2,32,16,256]{3,2,1,0:T(8,128)(2,1)S(1)} %copy-done.30), channel_id=1, source_target_pairs={{0,6},{1,7},{2,4},{3,5},{4,2},{5,3},{6,0},{7,1},{8,14},{9,15},{10,... | collective-permute-start | bytes 1572872 | tf_op jit(solution)/shard_map/ppermute | solution.py:427
  330.3 145.3 %all-gather.49.cloned.1.call-start = ((), (), s32[]{:S(2)}) async-start(), calls=%async_computation.9 | async-start | bytes 1572864 | tf_op jit(solution)/shard_map/all_gather | solution.py:426
  330.9 214.4 %all-gather.51.cloned.1.call-start = ((), (), s32[]{:S(2)}) async-start(), calls=%async_computation.10 | async-start | bytes 3145728 | tf_op jit(solution)/shard_map/all_gather | solution.py:426
  331.0 51.8 %collective-permute-start.14 = (bf16[2,32,16,256]{3,2,1,0:T(8,128)(2,1)}, bf16[2,32,16,256]{3,2,1,0:T(8,128)(2,1)S(1)}, u32[]{:S(2)}, u32[]{:S(2)}) collective-permute-start(bf16[2,32,16,256]{3,2,1,0:T(8,128)(2,1)} %get-tuple-element.111), channel_id=1, source_target_pairs={{0,4},{1,5},{2,6},{3,7},{4,0},{5,1},{6,2},{7,3},{8,12},{9,13},{10,... | collective-permute-start | bytes 1572872 | tf_op jit(solution)/shard_map/ppermute | solution.py:427
  341.4 41.3 %collective-permute-start.15 = (bf16[2,32,16,256]{3,2,1,0:T(8,128)(2,1)}, bf16[2,32,16,256]{3,2,1,0:T(8,128)(2,1)S(1)}, u32[]{:S(2)}, u32[]{:S(2)}) collective-permute-start(bf16[2,32,16,256]{3,2,1,0:T(8,128)(2,1)} %get-tuple-element.112), channel_id=1, source_target_pairs={{0,6},{1,7},{2,4},{3,5},{4,2},{5,3},{6,0},{7,1},{8,14},{9,15},{10,... | collective-permute-start | bytes 1572872 | tf_op jit(solution)/shard_map/ppermute | solution.py:427
  344.6 77.2 %collective-permute-start.16 = (bf16[2,32,16,256]{3,2,1,0:T(8,128)(2,1)S(1)}, bf16[2,32,16,256]{3,2,1,0:T(8,128)(2,1)S(1)}, u32[]{:S(2)}, u32[]{:S(2)}) collective-permute-start(bf16[2,32,16,256]{3,2,1,0:T(8,128)(2,1)S(1)} %copy-done.29), channel_id=1, source_target_pairs={{0,4},{1,5},{2,6},{3,7},{4,0},{5,1},{6,2},{7,3},{8,12},{9,13},{10,... | collective-permute-start | bytes 1572872 | tf_op jit(solution)/shard_map/ppermute | solution.py:427
  344.6 77.2 %collective-permute-start.17 = (bf16[2,32,16,256]{3,2,1,0:T(8,128)(2,1)S(1)}, bf16[2,32,16,256]{3,2,1,0:T(8,128)(2,1)S(1)}, u32[]{:S(2)}, u32[]{:S(2)}) collective-permute-start(bf16[2,32,16,256]{3,2,1,0:T(8,128)(2,1)S(1)} %copy-done.28), channel_id=1, source_target_pairs={{0,6},{1,7},{2,4},{3,5},{4,2},{5,3},{6,0},{7,1},{8,14},{9,15},{10,... | collective-permute-start | bytes 1572872 | tf_op jit(solution)/shard_map/ppermute | solution.py:427
  422.8 18.1 %copy-start.32 = (bf16[2,32,16,256]{3,2,1,0:T(8,128)(2,1)S(1)}, bf16[2,32,16,256]{3,2,1,0:T(8,128)(2,1)}, u32[]{:S(2)}) copy-start(bf16[2,32,16,256]{3,2,1,0:T(8,128)(2,1)} %get-tuple-element.124) | copy-start | bytes 1572868
  428.4 127.9 %all-gather.53.cloned.1.call-start = ((), (), s32[]{:S(2)}) async-start(), calls=%async_computation.11 | async-start | bytes 3145728 | tf_op jit(solution)/shard_map/all_gather | solution.py:426
  428.5 47.2 %collective-permute-start.18 = (bf16[2,32,16,256]{3,2,1,0:T(8,128)(2,1)S(1)}, bf16[2,32,16,256]{3,2,1,0:T(8,128)(2,1)S(1)}, u32[]{:S(2)}, u32[]{:S(2)}) collective-permute-start(bf16[2,32,16,256]{3,2,1,0:T(8,128)(2,1)S(1)} %copy-done.33), channel_id=1, source_target_pairs={{0,4},{1,5},{2,6},{3,7},{4,0},{5,1},{6,2},{7,3},{8,12},{9,13},{10,... | collective-permute-start | bytes 1572872 | tf_op jit(solution)/shard_map/ppermute | solution.py:427
  441.0 34.7 %collective-permute-start.19 = (bf16[2,32,16,256]{3,2,1,0:T(8,128)(2,1)S(1)}, bf16[2,32,16,256]{3,2,1,0:T(8,128)(2,1)S(1)}, u32[]{:S(2)}, u32[]{:S(2)}) collective-permute-start(bf16[2,32,16,256]{3,2,1,0:T(8,128)(2,1)S(1)} %copy-done.32), channel_id=1, source_target_pairs={{0,6},{1,7},{2,4},{3,5},{4,2},{5,3},{6,0},{7,1},{8,14},{9,15},{10,... | collective-permute-start | bytes 1572872 | tf_op jit(solution)/shard_map/ppermute | solution.py:427
  476.6 5.7 %copy-start.21 = (f32[32,128]{1,0:T(8,128)S(1)}, f32[32,128]{1,0:T(8,128)}, u32[]{:S(2)}) copy-start(f32[32,128]{1,0:T(8,128)} %get-tuple-element.76._) | copy-start | bytes 49156
  476.6 5.8 %copy-start.22 = (f32[32,128]{1,0:T(8,128)S(1)}, f32[32,128]{1,0:T(8,128)}, u32[]{:S(2)}) copy-start(f32[32,128]{1,0:T(8,128)} %get-tuple-element.77._) | copy-start | bytes 49156
  476.6 5.8 %copy-start.23 = (f32[32,128]{1,0:T(8,128)S(1)}, f32[32,128]{1,0:T(8,128)}, u32[]{:S(2)}) copy-start(f32[32,128]{1,0:T(8,128)} %get-tuple-element.78._) | copy-start | bytes 49156
  476.6 5.8 %copy-start.24 = (f32[32,128]{1,0:T(8,128)S(1)}, f32[32,128]{1,0:T(8,128)}, u32[]{:S(2)}) copy-start(f32[32,128]{1,0:T(8,128)} %get-tuple-element.90._) | copy-start | bytes 49156
  476.6 5.8 %copy-start.25 = (f32[32,128]{1,0:T(8,128)S(1)}, f32[32,128]{1,0:T(8,128)}, u32[]{:S(2)}) copy-start(f32[32,128]{1,0:T(8,128)} %get-tuple-element.80._) | copy-start | bytes 49156
  476.6 5.8 %copy-start.26 = (f32[32,128]{1,0:T(8,128)S(1)}, f32[32,128]{1,0:T(8,128)}, u32[]{:S(2)}) copy-start(f32[32,128]{1,0:T(8,128)} %get-tuple-element.92._) | copy-start | bytes 49156
  476.7 5.8 %copy-start.27 = (f32[32,128]{1,0:T(8,128)S(1)}, f32[32,128]{1,0:T(8,128)}, u32[]{:S(2)}) copy-start(f32[32,128]{1,0:T(8,128)} %get-tuple-element.99._) | copy-start | bytes 49156
  476.7 15.9 %copy-start.43 = (bf16[1,32,16,256]{3,2,1,0:T(8,128)(2,1)S(1)}, bf16[1,32,16,256]{3,2,1,0:T(8,128)(2,1)}, u32[]{:S(2)}) copy-start(bf16[1,32,16,256]{3,2,1,0:T(8,128)(2,1)} %get-tuple-element.131) | copy-start | bytes 786436
  476.7 26.3 %copy-start.42 = (bf16[1,32,16,256]{3,2,1,0:T(8,128)(2,1)S(1)}, bf16[1,32,16,256]{3,2,1,0:T(8,128)(2,1)}, u32[]{:S(2)}) copy-start(bf16[1,32,16,256]{3,2,1,0:T(8,128)(2,1)} %get-tuple-element.132) | copy-start | bytes 786436
  476.7 29.7 %copy-start.16 = (bf16[1,32,16,256]{3,2,1,0:T(8,128)(2,1)S(1)}, bf16[1,32,16,256]{3,2,1,0:T(8,128)(2,1)}, u32[]{:S(2)}) copy-start(bf16[1,32,16,256]{3,2,1,0:T(8,128)(2,1)} %get-tuple-element.130) | copy-start | bytes 786436
  476.7 43.6 %copy-start.15 = (bf16[1,32,16,256]{3,2,1,0:T(8,128)(2,1)S(1)}, bf16[1,32,16,256]{3,2,1,0:T(8,128)(2,1)}, u32[]{:S(2)}) copy-start(bf16[1,32,16,256]{3,2,1,0:T(8,128)(2,1)} %get-tuple-element.138) | copy-start | bytes 786436
  476.7 45.9 %copy-start.41 = (bf16[1,32,16,256]{3,2,1,0:T(8,128)(2,1)S(1)}, bf16[1,32,16,256]{3,2,1,0:T(8,128)(2,1)}, u32[]{:S(2)}) copy-start(bf16[1,32,16,256]{3,2,1,0:T(8,128)(2,1)} %get-tuple-element.140) | copy-start | bytes 786436
  476.7 47.7 %copy-start.40 = (bf16[1,32,16,256]{3,2,1,0:T(8,128)(2,1)S(1)}, bf16[1,32,16,256]{3,2,1,0:T(8,128)(2,1)}, u32[]{:S(2)}) copy-start(bf16[1,32,16,256]{3,2,1,0:T(8,128)(2,1)} %get-tuple-element.141) | copy-start | bytes 786436
  476.7 49.4 %copy-start.14 = (bf16[1,32,16,256]{3,2,1,0:T(8,128)(2,1)S(1)}, bf16[1,32,16,256]{3,2,1,0:T(8,128)(2,1)}, u32[]{:S(2)}) copy-start(bf16[1,32,16,256]{3,2,1,0:T(8,128)(2,1)} %get-tuple-element.139) | copy-start | bytes 786436
  492.6 57.7 %collective-permute-start.20 = (bf16[1,32,16,256]{3,2,1,0:T(8,128)(2,1)S(1)}, bf16[1,32,16,256]{3,2,1,0:T(8,128)(2,1)S(1)}, u32[]{:S(2)}, u32[]{:S(2)}) collective-permute-start(bf16[1,32,16,256]{3,2,1,0:T(8,128)(2,1)S(1)} %copy-done.43), channel_id=1, source_target_pairs={{0,4},{1,5},{2,6},{3,7},{4,0},{5,1},{6,2},{7,3},{8,12},{9,13},{10,... | collective-permute-start | bytes 786440 | tf_op jit(solution)/shard_map/ppermute | solution.py:427
  503.0 47.4 %collective-permute-start.21 = (bf16[1,32,16,256]{3,2,1,0:T(8,128)(2,1)S(1)}, bf16[1,32,16,256]{3,2,1,0:T(8,128)(2,1)S(1)}, u32[]{:S(2)}, u32[]{:S(2)}) collective-permute-start(bf16[1,32,16,256]{3,2,1,0:T(8,128)(2,1)S(1)} %copy-done.42), channel_id=1, source_target_pairs={{0,6},{1,7},{2,4},{3,5},{4,2},{5,3},{6,0},{7,1},{8,14},{9,15},{10,... | collective-permute-start | bytes 786440 | tf_op jit(solution)/shard_map/ppermute | solution.py:427
  522.6 38.7 %collective-permute-start.22 = (bf16[1,32,16,256]{3,2,1,0:T(8,128)(2,1)S(1)}, bf16[1,32,16,256]{3,2,1,0:T(8,128)(2,1)S(1)}, u32[]{:S(2)}, u32[]{:S(2)}) collective-permute-start(bf16[1,32,16,256]{3,2,1,0:T(8,128)(2,1)S(1)} %copy-done.41), channel_id=1, source_target_pairs={{0,5},{1,4},{2,7},{3,6},{4,1},{5,0},{6,3},{7,2},{8,13},{9,12},{10,... | collective-permute-start | bytes 786440 | tf_op jit(solution)/shard_map/ppermute | solution.py:427
  524.4 36.9 %collective-permute-start.23 = (bf16[1,32,16,256]{3,2,1,0:T(8,128)(2,1)S(1)}, bf16[1,32,16,256]{3,2,1,0:T(8,128)(2,1)S(1)}, u32[]{:S(2)}, u32[]{:S(2)}) collective-permute-start(bf16[1,32,16,256]{3,2,1,0:T(8,128)(2,1)S(1)} %copy-done.40), channel_id=1, source_target_pairs={{0,7},{1,6},{2,5},{3,4},{4,3},{5,2},{6,1},{7,0},{8,15},{9,14},{10,... | collective-permute-start | bytes 786440 | tf_op jit(solution)/shard_map/ppermute | solution.py:427
  (24 other events, 32.7 us)
Sparse Core Ops, SparseCore 0:
  58.5 12.1 all-gather.30
  72.2 11.7 all-gather.32
  85.5 46.9 all-gather.34
  158.5 11.7 all-gather.36
  171.7 43.9 all-gather.38
  217.1 22.1 all-gather.40
  240.8 43.3 all-gather.42
  285.8 38.3 all-gather.44
  330.5 19.3 all-gather.46
  351.3 35.9 all-gather.48
  428.5 20.3 all-gather.50
  482.5 19.2 all-gather.52

commit v6 on v4

--- a/solution.py
+++ b/solution.py
@@ -101,7 +101,7 @@
         fill(est32, shot + 2, cut(est_ref, shot))
         return carry
 
-    lax.fori_loop(0, shots, load, 0, unroll=2)
+    lax.fori_loop(0, shots, load, 0, unroll=4)
 
     def residual(place, values):
         shot = first + place - 1
@@ -129,7 +129,7 @@
         energy_ref[pl.ds(shot, 1), :] = jnp.sum(power, axis=0, keepdims=True)
         return carry
 
-    lax.fori_loop(0, shots, middle, 0, unroll=2)
+    lax.fori_loop(0, shots, middle, 0, unroll=4)
 
     def step(shot, carry):
         later, earlier = blended(res32, shot + 1, first + shot)
@@ -143,7 +143,7 @@
             store(shot, column, cell.astype(jnp.bfloat16))
         return carry
 
-    lax.fori_loop(0, shots, step, 0, unroll=2)
+    lax.fori_loop(0, shots, step, 0, unroll=4)
 
 
 def spectra_kernel(outputs, packed, meta_ref, delay_ref, est_ref, obs_ref, before_ref, after_ref, table_ref, _, *refs):
@@ -279,6 +279,7 @@
 
 
 PARAMS = pltpu.CompilerParams(vmem_limit_bytes=60 * 1024 * 1024)
+SMALL = pl.CostEstimate(flops=1024, bytes_accessed=1024, transcendentals=0)
 ANYWHERE = pl.BlockSpec(memory_space=pl.ANY)
 
 
@@ -287,7 +288,6 @@
     chips = peers // 2
     block_shape = (shots, rows, 2 * F // chips)
     shapes = {
-        "apart": [(1, *block_shape)] * chips,
         "packed": [(chips, *block_shape)],
         "joined": [(2, *block_shape)] * chips,
     }[mode]
@@ -311,11 +311,7 @@
         out_shape=[pltpu.HBM(shape, jnp.bfloat16) for shape in shapes]
         + [pltpu.HBM((shots, LANES), jnp.float32)],
         compiler_params=PARAMS,
-        cost_estimate=pl.CostEstimate(
-            flops=4 * F * shots * rows * samples,
-            bytes_accessed=3 * 2 * shots * rows * samples + table.size * 2,
-            transcendentals=0,
-        ),
+        cost_estimate=SMALL,
         name="spectra_" + mode,
     )(meta, delays, *fields, table, after, *partners)
     return spectra, energy
@@ -360,9 +356,7 @@
         ),
         out_shape=[pltpu.HBM(shape, jnp.bfloat16) for shape in shapes],
         compiler_params=PARAMS,
-        cost_estimate=pl.CostEstimate(
-            flops=8 * shots * size, bytes_accessed=4 * size + 2 * table.size, transcendentals=size
-        ),
+        cost_estimate=SMALL,
         name="shrink",
     )(meta, table, level, after, *spectra)
 
@@ -401,12 +395,8 @@
         ),
         out_shape=out_shape,
         input_output_aliases={} if onto is None else {len(operands) - 1: 0},
-        compiler_params=PARAMS,
-        cost_estimate=pl.CostEstimate(
-            flops=4 * F * shots * rows * samples,
-            bytes_accessed=4 * F * shots * rows + 2 * table.size + 4 * shots * rows * samples,
-            transcendentals=0,
-        ),
+        compiler_params=pltpu.CompilerParams(vmem_limit_bytes=24 * 1024 * 1024),
+        cost_estimate=SMALL,
         name="update",
     )(*operands)
 
@@ -436,17 +426,25 @@
 
 
 def turns(steps):
-    for turn in range(steps + 4):
-        if turn == 0:
-            yield "own", 0
-            yield "other", 0
-        if turn + 1 < steps:
-            yield "other", turn + 1
-        if 0 < turn < steps:
-            yield "own", turn
-        for name, lag in (("shrink", 1), ("update own", 3), ("update other", 4)):
+    lags = (("other", 0), ("own", 0), ("shrink", 1), ("update own", 2), ("update other", 3))
+    for turn in range(steps + 3):
+        for name, lag in lags:
             if 0 <= turn - lag < steps:
                 yield name, turn - lag
+
+
+def to_chips(arrays):
+    far = {chip: sent(arrays[chip], 2 * chip) for chip in range(len(arrays) // 2, len(arrays))}
+    near = {chip: sent(arrays[chip], 2 * chip) for chip in range(1, len(arrays) // 2)}
+    return [arrays[0], *[{**near, **far}[chip] for chip in range(1, len(arrays))]]
+
+
+def to_devices(arrays):
+    count = len(arrays)
+    order = [*range(count // 2, count, 2), *range(count // 2 + 1, count, 2)]
+    order += [*range(2, count // 2, 2), *range(3, count // 2, 2), 1]
+    moved = {slot: sent(arrays[slot], slot) for slot in order}
+    return [arrays[0], *[moved[slot] for slot in range(1, count)]]
 
 
 def in_pairs(estimate, observed, delays, thresholds, rows):
@@ -477,8 +475,7 @@
                 edge_block = lambda meta, side=side: meta[side]
             else:
                 edge_block = lambda meta, side=side, step=step: meta[side] * (steps - 1) + step - 1
-            direct = step == 0
-            mode = "apart" if direct else "joined" if name == "own" else "packed"
+            mode = "joined" if name == "own" else "packed"
             spectra, power = spectra_of(
                 meta,
                 delays,
@@ -494,33 +491,18 @@
             )
             last = power
             energy = energy + power
-            if mode == "packed":
+            if mode == "joined":
+                ahead[step] = to_chips(spectra)
+            else:
                 packed[step] = sent(spectra[0], 1)
-            elif mode == "joined":
-                far = [sent(spectra[chip], 2 * chip) for chip in range(1, chips)]
-                ahead[step] = [spectra[0], *far]
-            elif name == "own":
-                far = [sent(spectra[chip], 2 * chip) for chip in range(1, chips)]
-                ahead[step] = [spectra[0], *far]
-                held_estimate, held_observed, _ = lax.optimization_barrier(
-                    (estimate, observed, power)
-                )
-                if steps > 1:
-                    late = edges(
-                        part_of_halves(held_estimate, rows, receivers // 2),
-                        part_of_halves(held_observed, rows, receivers // 2),
-                    )
-            else:
-                other = [sent(spectra[chip], 2 * chip + 1) for chip in range(chips)]
-                ahead[step] = [array for pair in zip(ahead[step], other) for array in pair]
+            if late is None and steps > 1:
+                later = lax.optimization_barrier((estimate, observed, power))
+                late = edges(*[part_of_halves(array, rows, receivers // 2) for array in later[:2]])
         elif name == "shrink":
             direct = step == steps - 1
             shrunk = shrunk_of(meta, ahead.pop(step), table, levels, not direct, last)
             last = shrunk[0]
-            unit = 1 if direct else 2
-            behind[step] = [
-                sent(array, unit * index) if index else array for index, array in enumerate(shrunk)
-            ]
+            behind[step] = to_devices(shrunk) if direct else to_chips(shrunk)
         elif name == "update own":
             direct = step == steps - 1
             restored = behind.pop(step)
@@ -595,7 +577,7 @@
     peers = lax.axis_size("shot")
     rows = min(16, receivers)
     paired = (
-        peers > 1
+        peers >= 4
         and peers & (peers - 1) == 0
         and (4 * F // peers) % LANES == 0
         and receivers % (2 * rows) == 0

time: 464 us -> 499 us (1.075)
  waiting for transfers between devices: 130 us -> 179 us
  Pallas kernels: 181 us -> 160 us
  starting transfers between devices: 121 us -> 126 us
    ppermute x38 -> x35, waiting for transfers between devices: 127 us -> 176 us  [sent(): lax.ppermute(array, 'shot', [(i, i ^ distance) for i in range(peers)])]
    pallas_call x8, Pallas kernels: 91.8 us -> 80.5 us  [spectra_of(): pl.pallas_call(functools.partial(spectra_kernel, len(shapes), mode == 'pa...]
    pallas_call x8, Pallas kernels: 41.5 us -> 31.6 us  [updated_of(): pl.pallas_call(functools.partial(update_kernel, len(restored), passes), g...]
    ppermute x38 -> x35, starting transfers between devices: 110 us -> 119 us  [sent(): lax.ppermute(array, 'shot', [(i, i ^ distance) for i in range(peers)])]
    unnamed x98 -> x92, local copies, waits for them, and re-layouts: 11 us -> 15.5 us
  transfers between devices with their start and end apart: 42 -> 39, of which waited for: 11 -> 13; matrix products, arithmetic and copies ran while one was open for 0% -> 1% of each run, Pallas kernels for 33% -> 20%
where the time goes in v6:
time: 499 us; the launch traced here: 498 us
  waiting for transfers between devices  179 us (36%)
  Pallas kernels  160 us (32%)
  starting transfers between devices  126 us (25%)
  local copies, waits for them, and re-layouts  21 us (4%)
  blocking collectives  9.91 us (2%)
    ppermute x35, waiting for transfers between devices, sent(): lax.ppermute(array, 'shot', [(i, i ^ distance) for i in range(peers)])  176 us
    ppermute x35, starting transfers between devices, sent(): lax.ppermute(array, 'shot', [(i, i ^ distance) for i in range(peers)])  119 us
    pallas_call x8, Pallas kernels, spectra_of(): pl.pallas_call(functools.partial(spectra_kernel, len(shapes), mode == 'pa...  80.5 us
    pallas_call x4, Pallas kernels, shrunk_of(): pl.pallas_call(functools.partial(shots_kernel, len(spectra)), grid_spec=p...  47.5 us
    pallas_call x8, Pallas kernels, updated_of(): pl.pallas_call(functools.partial(update_kernel, len(restored), passes), g...  31.6 us
    unnamed x92, local copies, waits for them, and re-layouts  15.5 us
  transfers between devices with their start and end apart: 39, of which 13 were waited for; matrix products, arithmetic and copies ran while one was open for 1% of the time, Pallas kernels for 20%

profile of v6, /device:TPU:0, one launch (start us, length us, event | category | flops | bytes accessed | tf_op | source)
XLA Modules:
  0.0 497.5 jit_solution(1580557245426248589)
XLA Ops:
  2.5 2.4 collective-permute-start
  4.9 1.3 collective-permute-start.1
  7.6 2.9 collective-permute-done.1.after_ref
  11.2 9.7 %spectra_packed.4 = (bf16[4,32,16,256]{3,2,1,0:T(8,128)(2,1)}, f32[32,128]{1,0:T(8,128)}) custom-call(s32[11]{0:T(128)} %pad_add_fusion.meta_ref, s32[256]{0:T(256)} %delay_ref.15, bf16[32,128,1024]{2,1,0:T(8,128)(2,1)} %est_ref.15, bf16[32,128,1024]{2,1,0:T(8,128)(2,1)} %obs_ref.15, bf16[3,32,1024]{2,1,0:T(8,128)(2,1)} %copy-done.28, ...), custom_call_target="tpu_custom_call" | custom-call | flops 1024 | bytes 1024 | tf_op jit(solution)/shard_map/spectra_packed/pallas_call | solution.py:296
  20.8 1.2 fusion
  22.0 4.2 collective-permute-start.4
  26.2 1.0 fusion.1
  27.3 2.0 collective-permute-start.2
  29.4 1.3 collective-permute-start.3
  31.6 10.4 %spectra_joined.4 = (bf16[2,32,16,256]{3,2,1,0:T(8,128)(2,1)}, bf16[2,32,16,256]{3,2,1,0:T(8,128)(2,1)}, bf16[2,32,16,256]{3,2,1,0:T(8,128)(2,1)}, bf16[2,32,16,256]{3,2,1,0:T(8,128)(2,1)}, f32[32,128]{1,0:T(8,128)}) custom-call(s32[11]{0:T(128)} %pad_add_fusion.meta_ref, s32[256]{0:T(256)} %delay_ref.15, bf16[32,128,1024]{2,1,0:T(8,128)(2,1)} %est_ref.15, ...), custom_call_target="tpu_custom_call" | custom-call | flops 1024 | bytes 1024 | tf_op jit(solution)/shard_map/spectra_joined/pallas_call | solution.py:296
  43.0 9.7 %spectra_packed.5 = (bf16[4,32,16,256]{3,2,1,0:T(8,128)(2,1)}, f32[32,128]{1,0:T(8,128)}) custom-call(s32[11]{0:T(128)} %pad_add_fusion.meta_ref, s32[256]{0:T(256)} %delay_ref.15, bf16[32,128,1024]{2,1,0:T(8,128)(2,1)} %est_ref.15, bf16[32,128,1024]{2,1,0:T(8,128)(2,1)} %obs_ref.15, bf16[3,96,1024]{2,1,0:T(8,128)(2,1)} %copy-done.24, ...), custom_call_target="tpu_custom_call" | custom-call | flops 1024 | bytes 1024 | tf_op jit(solution)/shard_map/spectra_packed/pallas_call | solution.py:296
  52.7 2.3 collective-permute-start.5
  55.0 1.6 collective-permute-start.6
  56.6 1.1 collective-permute-start.7
  57.7 1.7 collective-permute-start.8
  60.3 10.4 %spectra_joined.5 = (bf16[2,32,16,256]{3,2,1,0:T(8,128)(2,1)}, bf16[2,32,16,256]{3,2,1,0:T(8,128)(2,1)}, bf16[2,32,16,256]{3,2,1,0:T(8,128)(2,1)}, bf16[2,32,16,256]{3,2,1,0:T(8,128)(2,1)}, f32[32,128]{1,0:T(8,128)}) custom-call(s32[11]{0:T(128)} %pad_add_fusion.meta_ref, s32[256]{0:T(256)} %delay_ref.15, bf16[32,128,1024]{2,1,0:T(8,128)(2,1)} %est_ref.15, ...), custom_call_target="tpu_custom_call" | custom-call | flops 1024 | bytes 1024 | tf_op jit(solution)/shard_map/spectra_joined/pallas_call | solution.py:296
  70.7 9.5 %collective-permute-done.6.refs_1_ = bf16[2,32,16,256]{3,2,1,0:T(8,128)(2,1)S(1)} collective-permute-done((bf16[2,32,16,256]{3,2,1,0:T(8,128)(2,1)}, bf16[2,32,16,256]{3,2,1,0:T(8,128)(2,1)S(1)}, u32[]{:S(2)}, u32[]{:S(2)}) %collective-permute-start.6) | collective-permute-done | bytes 524320 | tf_op jit(solution)/shard_map/ppermute | solution.py:410
  80.2 14.8 %collective-permute-done.7.refs_2_ = bf16[2,32,16,256]{3,2,1,0:T(8,128)(2,1)S(1)} collective-permute-done((bf16[2,32,16,256]{3,2,1,0:T(8,128)(2,1)}, bf16[2,32,16,256]{3,2,1,0:T(8,128)(2,1)S(1)}, u32[]{:S(2)}, u32[]{:S(2)}) %collective-permute-start.7) | collective-permute-done | bytes 524320 | tf_op jit(solution)/shard_map/ppermute | solution.py:410
  96.0 11.9 %shrink.4 = (bf16[2,32,16,256]{3,2,1,0:T(8,128)(2,1)}, bf16[2,32,16,256]{3,2,1,0:T(8,128)(2,1)}, bf16[2,32,16,256]{3,2,1,0:T(8,128)(2,1)}, bf16[2,32,16,256]{3,2,1,0:T(8,128)(2,1)}) custom-call(s32[11]{0:T(128)} %pad_add_fusion.meta_ref, bf16[512,256]{1,0:T(8,128)(2,1)} %constant.49.clone.table_ref, f32[1,256]{1,0:T(1,128)} %bitcast.29, ...), custom_call_target="tpu_custom_call" | custom-call | flops 1024 | bytes 1024 | tf_op jit(solution)/shard_map/shrink/pallas_call | solution.py:347
  107.9 9.7 %spectra_packed.6 = (bf16[4,32,16,256]{3,2,1,0:T(8,128)(2,1)}, f32[32,128]{1,0:T(8,128)}) custom-call(s32[11]{0:T(128)} %pad_add_fusion.meta_ref, s32[256]{0:T(256)} %delay_ref.15, bf16[32,128,1024]{2,1,0:T(8,128)(2,1)} %est_ref.15, bf16[32,128,1024]{2,1,0:T(8,128)(2,1)} %obs_ref.15, bf16[3,96,1024]{2,1,0:T(8,128)(2,1)} %copy-done.24, ...), custom_call_target="tpu_custom_call" | custom-call | flops 1024 | bytes 1024 | tf_op jit(solution)/shard_map/spectra_packed/pallas_call | solution.py:296
  117.6 11.0 %collective-permute-start.10 = (bf16[2,32,16,256]{3,2,1,0:T(8,128)(2,1)}, bf16[2,32,16,256]{3,2,1,0:T(8,128)(2,1)S(1)}, u32[]{:S(2)}, u32[]{:S(2)}) collective-permute-start(bf16[2,32,16,256]{3,2,1,0:T(8,128)(2,1)} %get-tuple-element.87), channel_id=1, source_target_pairs={{0,2},{1,3},{2,0},{3,1},{4,6},{5,7},{6,4},{7,5},{8,10},{9,11},{10,... | collective-permute-start | bytes 1572872 | tf_op jit(solution)/shard_map/ppermute | solution.py:410
  128.7 2.9 collective-permute-start.11
  131.6 1.4 collective-permute-start.12
  133.0 19.8 %collective-permute-done.10.refs_1_ = bf16[2,32,16,256]{3,2,1,0:T(8,128)(2,1)S(1)} collective-permute-done((bf16[2,32,16,256]{3,2,1,0:T(8,128)(2,1)}, bf16[2,32,16,256]{3,2,1,0:T(8,128)(2,1)S(1)}, u32[]{:S(2)}, u32[]{:S(2)}) %collective-permute-start.10) | collective-permute-done | bytes 524320 | tf_op jit(solution)/shard_map/ppermute | solution.py:410
  154.3 1.8 collective-permute-start.15
  156.1 10.4 %spectra_joined.6 = (bf16[2,32,16,256]{3,2,1,0:T(8,128)(2,1)}, bf16[2,32,16,256]{3,2,1,0:T(8,128)(2,1)}, bf16[2,32,16,256]{3,2,1,0:T(8,128)(2,1)}, bf16[2,32,16,256]{3,2,1,0:T(8,128)(2,1)}, f32[32,128]{1,0:T(8,128)}) custom-call(s32[11]{0:T(128)} %pad_add_fusion.meta_ref, s32[256]{0:T(256)} %delay_ref.15, bf16[32,128,1024]{2,1,0:T(8,128)(2,1)} %est_ref.15, ...), custom_call_target="tpu_custom_call" | custom-call | flops 1024 | bytes 1024 | tf_op jit(solution)/shard_map/spectra_joined/pallas_call | solution.py:296
  166.5 11.4 %collective-permute-done.12.refs_3_ = bf16[2,32,16,256]{3,2,1,0:T(8,128)(2,1)} collective-permute-done((bf16[2,32,16,256]{3,2,1,0:T(8,128)(2,1)}, bf16[2,32,16,256]{3,2,1,0:T(8,128)(2,1)}, u32[]{:S(2)}, u32[]{:S(2)}) %collective-permute-start.12) | collective-permute-done | bytes 524320 | tf_op jit(solution)/shard_map/ppermute | solution.py:410
  177.9 11.9 %shrink.5 = (bf16[2,32,16,256]{3,2,1,0:T(8,128)(2,1)}, bf16[2,32,16,256]{3,2,1,0:T(8,128)(2,1)}, bf16[2,32,16,256]{3,2,1,0:T(8,128)(2,1)}, bf16[2,32,16,256]{3,2,1,0:T(8,128)(2,1)}) custom-call(s32[11]{0:T(128)} %pad_add_fusion.meta_ref, bf16[512,256]{1,0:T(8,128)(2,1)} %constant.49.clone.table_ref, f32[1,256]{1,0:T(1,128)} %bitcast.30, ...), custom_call_target="tpu_custom_call" | custom-call | flops 1024 | bytes 1024 | tf_op jit(solution)/shard_map/shrink/pallas_call | solution.py:347
  189.7 21.7 %collective-permute-done.14.refs_2_ = bf16[2,32,16,256]{3,2,1,0:T(8,128)(2,1)S(1)} collective-permute-done((bf16[2,32,16,256]{3,2,1,0:T(8,128)(2,1)}, bf16[2,32,16,256]{3,2,1,0:T(8,128)(2,1)S(1)}, u32[]{:S(2)}, u32[]{:S(2)}) %collective-permute-start.14) | collective-permute-done | bytes 524320 | tf_op jit(solution)/shard_map/ppermute | solution.py:410
  212.5 4.4 update.8
  216.9 9.9 %spectra_packed.7 = (bf16[4,32,16,256]{3,2,1,0:T(8,128)(2,1)}, f32[32,128]{1,0:T(8,128)}) custom-call(s32[11]{0:T(128)} %pad_add_fusion.meta_ref, s32[256]{0:T(256)} %delay_ref.15, bf16[32,128,1024]{2,1,0:T(8,128)(2,1)} %est_ref.15, bf16[32,128,1024]{2,1,0:T(8,128)(2,1)} %obs_ref.15, bf16[3,96,1024]{2,1,0:T(8,128)(2,1)} %copy-done.24, ...), custom_call_target="tpu_custom_call" | custom-call | flops 1024 | bytes 1024 | tf_op jit(solution)/shard_map/spectra_packed/pallas_call | solution.py:296
  226.8 11.8 %collective-permute-start.20 = (bf16[2,32,16,256]{3,2,1,0:T(8,128)(2,1)}, bf16[2,32,16,256]{3,2,1,0:T(8,128)(2,1)S(1)}, u32[]{:S(2)}, u32[]{:S(2)}) collective-permute-start(bf16[2,32,16,256]{3,2,1,0:T(8,128)(2,1)} %get-tuple-element.103), channel_id=1, source_target_pairs={{0,2},{1,3},{2,0},{3,1},{4,6},{5,7},{6,4},{7,5},{8,10},{9,11},{10,... | collective-permute-start | bytes 1572872 | tf_op jit(solution)/shard_map/ppermute | solution.py:410
  238.8 2.7 collective-permute-start.18
  241.6 21.3 %collective-permute-done.20.refs_1_ = bf16[2,32,16,256]{3,2,1,0:T(8,128)(2,1)S(1)} collective-permute-done((bf16[2,32,16,256]{3,2,1,0:T(8,128)(2,1)}, bf16[2,32,16,256]{3,2,1,0:T(8,128)(2,1)S(1)}, u32[]{:S(2)}, u32[]{:S(2)}) %collective-permute-start.20) | collective-permute-done | bytes 524320 | tf_op jit(solution)/shard_map/ppermute | solution.py:410
  263.7 2.4 collective-permute-start.19
  266.0 7.9 %collective-permute-done.17.refs_1_ = bf16[2,32,16,256]{3,2,1,0:T(8,128)(2,1)} collective-permute-done((bf16[2,32,16,256]{3,2,1,0:T(8,128)(2,1)}, bf16[2,32,16,256]{3,2,1,0:T(8,128)(2,1)}, u32[]{:S(2)}, u32[]{:S(2)}) %collective-permute-start.17) | collective-permute-done | bytes 524320 | tf_op jit(solution)/shard_map/ppermute | solution.py:410
  274.4 1.9 collective-permute-start.22
  276.3 10.3 %spectra_joined.7 = (bf16[2,32,16,256]{3,2,1,0:T(8,128)(2,1)}, bf16[2,32,16,256]{3,2,1,0:T(8,128)(2,1)}, bf16[2,32,16,256]{3,2,1,0:T(8,128)(2,1)}, bf16[2,32,16,256]{3,2,1,0:T(8,128)(2,1)}, f32[32,128]{1,0:T(8,128)}) custom-call(s32[11]{0:T(128)} %pad_add_fusion.meta_ref, s32[256]{0:T(256)} %delay_ref.15, bf16[32,128,1024]{2,1,0:T(8,128)(2,1)} %est_ref.15, ...), custom_call_target="tpu_custom_call" | custom-call | flops 1024 | bytes 1024 | tf_op jit(solution)/shard_map/spectra_joined/pallas_call | solution.py:296
  286.6 1.1 collective-permute-start.24
  287.8 33.8 %collective-permute-start.25 = (bf16[2,32,16,256]{3,2,1,0:T(8,128)(2,1)}, bf16[2,32,16,256]{3,2,1,0:T(8,128)(2,1)}, u32[]{:S(2)}, u32[]{:S(2)}) collective-permute-start(bf16[2,32,16,256]{3,2,1,0:T(8,128)(2,1)} %get-tuple-element.113), channel_id=1, source_target_pairs={{0,4},{1,5},{2,6},{3,7},{4,0},{5,1},{6,2},{7,3},{8,12},{9,13},{10,... | collective-permute-start | bytes 1572872 | tf_op jit(solution)/shard_map/ppermute | solution.py:410
  321.6 11.8 %shrink.6 = (bf16[2,32,16,256]{3,2,1,0:T(8,128)(2,1)}, bf16[2,32,16,256]{3,2,1,0:T(8,128)(2,1)}, bf16[2,32,16,256]{3,2,1,0:T(8,128)(2,1)}, bf16[2,32,16,256]{3,2,1,0:T(8,128)(2,1)}) custom-call(s32[11]{0:T(128)} %pad_add_fusion.meta_ref, bf16[512,256]{1,0:T(8,128)(2,1)} %constant.49.clone.table_ref, f32[1,256]{1,0:T(1,128)} %bitcast.31, ...), custom_call_target="tpu_custom_call" | custom-call | flops 1024 | bytes 1024 | tf_op jit(solution)/shard_map/shrink/pallas_call | solution.py:347
  333.4 10.1 %collective-permute-done.21.refs_2_ = bf16[2,32,16,256]{3,2,1,0:T(8,128)(2,1)} collective-permute-done((bf16[2,32,16,256]{3,2,1,0:T(8,128)(2,1)}, bf16[2,32,16,256]{3,2,1,0:T(8,128)(2,1)}, u32[]{:S(2)}, u32[]{:S(2)}) %collective-permute-start.21) | collective-permute-done | bytes 524320 | tf_op jit(solution)/shard_map/ppermute | solution.py:410
  343.5 1.5 collective-permute-start.26
  346.0 11.8 %collective-permute-start.28 = (bf16[2,32,16,256]{3,2,1,0:T(8,128)(2,1)}, bf16[2,32,16,256]{3,2,1,0:T(8,128)(2,1)S(1)}, u32[]{:S(2)}, u32[]{:S(2)}) collective-permute-start(bf16[2,32,16,256]{3,2,1,0:T(8,128)(2,1)} %get-tuple-element.117), channel_id=1, source_target_pairs={{0,4},{1,5},{2,6},{3,7},{4,0},{5,1},{6,2},{7,3},{8,12},{9,13},{10,... | collective-permute-start | bytes 1572872 | tf_op jit(solution)/shard_map/ppermute | solution.py:410
  357.8 1.5 collective-permute-start.29
  359.3 1.0 copy-done.3
  360.3 1.0 copy-done.11
  361.3 4.4 update.9
  365.8 34.0 %collective-permute-done.25.refs_2_ = bf16[2,32,16,256]{3,2,1,0:T(8,128)(2,1)} collective-permute-done((bf16[2,32,16,256]{3,2,1,0:T(8,128)(2,1)}, bf16[2,32,16,256]{3,2,1,0:T(8,128)(2,1)}, u32[]{:S(2)}, u32[]{:S(2)}) %collective-permute-start.25) | collective-permute-done | bytes 524320 | tf_op jit(solution)/shard_map/ppermute | solution.py:410
  400.4 3.2 update.10
  403.6 11.9 %shrink.7 = (bf16[1,32,16,256]{3,2,1,0:T(8,128)(2,1)}, bf16[1,32,16,256]{3,2,1,0:T(8,128)(2,1)}, bf16[1,32,16,256]{3,2,1,0:T(8,128)(2,1)}, bf16[1,32,16,256]{3,2...) custom-call(s32[11]{0:T(128)} %pad_add_fusion.meta_ref, ...), custom_call_target="tpu_custom_call" | custom-call | flops 1024 | bytes 1024 | tf_op jit(solution)/shard_map/shrink/pallas_call | solution.py:347
  415.6 6.5 %collective-permute-done.28.refs_2_ = bf16[2,32,16,256]{3,2,1,0:T(8,128)(2,1)S(1)} collective-permute-done((bf16[2,32,16,256]{3,2,1,0:T(8,128)(2,1)}, bf16[2,32,16,256]{3,2,1,0:T(8,128)(2,1)S(1)}, u32[]{:S(2)}, u32[]{:S(2)}) %collective-permute-start.28) | collective-permute-done | bytes 524320 | tf_op jit(solution)/shard_map/ppermute | solution.py:410
  423.1 4.4 update.11
  427.5 11.9 %collective-permute-start.31 = (bf16[1,32,16,256]{3,2,1,0:T(8,128)(2,1)S(1)}, bf16[1,32,16,256]{3,2,1,0:T(8,128)(2,1)S(1)}, u32[]{:S(2)}, u32[]{:S(2)}) collective-permute-start(bf16[1,32,16,256]{3,2,1,0:T(8,128)(2,1)S(1)} %copy-done.45), channel_id=1, source_target_pairs={{0,2},{1,3},{2,0},{3,1},{4,6},{5,7},{6,4},{7,5},{8,10},{9,11},{10,... | collective-permute-start | bytes 786440 | tf_op jit(solution)/shard_map/ppermute | solution.py:410
  439.4 2.4 collective-permute-start.33
  441.8 8.9 %collective-permute-done.31.refs_1_ = bf16[1,32,16,256]{3,2,1,0:T(8,128)(2,1)S(1)} collective-permute-done((bf16[1,32,16,256]{3,2,1,0:T(8,128)(2,1)S(1)}, bf16[1,32,16,256]{3,2,1,0:T(8,128)(2,1)S(1)}, u32[]{:S(2)}, u32[]{:S(2)}) %collective-permute-start.31) | collective-permute-done | bytes 262176 | tf_op jit(solution)/shard_map/ppermute | solution.py:410
  450.7 9.9 %collective-permute-done.32.refs_2_ = bf16[1,32,16,256]{3,2,1,0:T(8,128)(2,1)S(1)} collective-permute-done((bf16[1,32,16,256]{3,2,1,0:T(8,128)(2,1)S(1)}, bf16[1,32,16,256]{3,2,1,0:T(8,128)(2,1)S(1)}, u32[]{:S(2)}, u32[]{:S(2)}) %collective-permute-start.32) | collective-permute-done | bytes 262176 | tf_op jit(solution)/shard_map/ppermute | solution.py:410
  462.1 3.6 collective-permute-start.37
  465.7 3.2 collective-permute-start.38
  469.1 9.9 %psum.7 = f32[32]{0:T(128)S(1)} all-reduce(f32[32]{0:T(128)S(1)} %add_reduce_fusion), channel_id=1, replica_groups=mesh['patch'=4,'shot'=8] {'patch'}, use_global_device_ids=true, to_apply=%region_1.2 | all-reduce | flops 32 | bytes 256 | tf_op jit(solution)/shard_map/psum | solution.py:587
  480.2 4.1 update.12
  485.0 3.1 update.13
  488.7 4.1 update.14
  493.5 4.0 update.15
  (141 shorter events, 19.7 us)
Async XLA Ops:
  2.5 5.1 %collective-permute-start = (bf16[3,32,1024]{2,1,0:T(8,128)(2,1)S(1)}, bf16[3,32,1024]{2,1,0:T(8,128)(2,1)S(1)}, u32[]{:S(2)}, u32[]{:S(2)}) collective-permute-start(bf16[3,32,1024]{2,1,0:T(8,128)(2,1)S(1)} %pad_maximum_fusion.2), channel_id=1, source_target_pairs={{0,1},{1,2},{2,3},{3,4},{4,5},{5,6},{6,7},{8,9},{9,10},{10,11},{11... | collective-permute-start | bytes 589832 | tf_op jit(solution)/shard_map/ppermute | solution.py:419
  4.9 5.5 %collective-permute-start.1 = (bf16[3,32,1024]{2,1,0:T(8,128)(2,1)S(1)}, bf16[3,32,1024]{2,1,0:T(8,128)(2,1)S(1)}, u32[]{:S(2)}, u32[]{:S(2)}) collective-permute-start(bf16[3,32,1024]{2,1,0:T(8,128)(2,1)S(1)} %pad_maximum_fusion.3), channel_id=1, source_target_pairs={{1,0},{2,1},{3,2},{4,3},{5,4},{6,5},{7,6},{9,8},{10,9},{11,10},{12... | collective-permute-start | bytes 589832 | tf_op jit(solution)/shard_map/ppermute | solution.py:419
  7.6 3.5 copy-start.28
  22.0 8.7 %collective-permute-start.4 = (bf16[4,32,16,256]{3,2,1,0:T(8,128)(2,1)}, bf16[4,32,16,256]{3,2,1,0:T(8,128)(2,1)S(1)}, u32[]{:S(2)}, u32[]{:S(2)}) collective-permute-start(bf16[4,32,16,256]{3,2,1,0:T(8,128)(2,1)} %get-tuple-element.73), channel_id=1, source_target_pairs={{0,1},{1,0},{2,3},{3,2},{4,5},{5,4},{6,7},{7,6},{8,9},{9,8},{10,11... | collective-permute-start | bytes 3145736 | tf_op jit(solution)/shard_map/ppermute | solution.py:410
  27.3 14.7 %collective-permute-start.2 = (bf16[3,96,1024]{2,1,0:T(8,128)(2,1)S(1)}, bf16[3,96,1024]{2,1,0:T(8,128)(2,1)S(1)}, u32[]{:S(2)}, u32[]{:S(2)}) collective-permute-start(bf16[3,96,1024]{2,1,0:T(8,128)(2,1)S(1)} %pad_maximum_fusion), channel_id=1, source_target_pairs={{0,1},{1,2},{2,3},{3,4},{4,5},{5,6},{6,7},{8,9},{9,10},{10,11},{11... | collective-permute-start | bytes 1769480 | tf_op jit(solution)/shard_map/ppermute | solution.py:419
  29.4 12.7 %collective-permute-start.3 = (bf16[3,96,1024]{2,1,0:T(8,128)(2,1)S(1)}, bf16[3,96,1024]{2,1,0:T(8,128)(2,1)S(1)}, u32[]{:S(2)}, u32[]{:S(2)}) collective-permute-start(bf16[3,96,1024]{2,1,0:T(8,128)(2,1)S(1)} %pad_maximum_fusion.1), channel_id=1, source_target_pairs={{1,0},{2,1},{3,2},{4,3},{5,4},{6,5},{7,6},{9,8},{10,9},{11,10},{12... | collective-permute-start | bytes 1769480 | tf_op jit(solution)/shard_map/ppermute | solution.py:419
  42.0 15.6 %copy-start.42 = (bf16[2,32,16,256]{3,2,1,0:T(8,128)(2,1)S(1)}, bf16[2,32,16,256]{3,2,1,0:T(8,128)(2,1)}, u32[]{:S(2)}) copy-start(bf16[2,32,16,256]{3,2,1,0:T(8,128)(2,1)} %get-tuple-element.81) | copy-start | bytes 1572868
  52.7 6.7 %collective-permute-start.5 = (bf16[4,32,16,256]{3,2,1,0:T(8,128)(2,1)}, bf16[4,32,16,256]{3,2,1,0:T(8,128)(2,1)S(1)}, u32[]{:S(2)}, u32[]{:S(2)}) collective-permute-start(bf16[4,32,16,256]{3,2,1,0:T(8,128)(2,1)} %get-tuple-element.76), channel_id=1, source_target_pairs={{0,1},{1,0},{2,3},{3,2},{4,5},{5,4},{6,7},{7,6},{8,9},{9,8},{10,11... | collective-permute-start | bytes 3145736 | tf_op jit(solution)/shard_map/ppermute | solution.py:410
  55.0 25.3 %collective-permute-start.6 = (bf16[2,32,16,256]{3,2,1,0:T(8,128)(2,1)}, bf16[2,32,16,256]{3,2,1,0:T(8,128)(2,1)S(1)}, u32[]{:S(2)}, u32[]{:S(2)}) collective-permute-start(bf16[2,32,16,256]{3,2,1,0:T(8,128)(2,1)} %get-tuple-element.79), channel_id=1, source_target_pairs={{0,2},{1,3},{2,0},{3,1},{4,6},{5,7},{6,4},{7,5},{8,10},{9,11},{10,... | collective-permute-start | bytes 1572872 | tf_op jit(solution)/shard_map/ppermute | solution.py:410
  56.6 38.4 %collective-permute-start.7 = (bf16[2,32,16,256]{3,2,1,0:T(8,128)(2,1)}, bf16[2,32,16,256]{3,2,1,0:T(8,128)(2,1)S(1)}, u32[]{:S(2)}, u32[]{:S(2)}) collective-permute-start(bf16[2,32,16,256]{3,2,1,0:T(8,128)(2,1)} %get-tuple-element.80), channel_id=1, source_target_pairs={{0,4},{1,5},{2,6},{3,7},{4,0},{5,1},{6,2},{7,3},{8,12},{9,13},{10,... | collective-permute-start | bytes 1572872 | tf_op jit(solution)/shard_map/ppermute | solution.py:410
  57.7 37.3 %collective-permute-start.8 = (bf16[2,32,16,256]{3,2,1,0:T(8,128)(2,1)S(1)}, bf16[2,32,16,256]{3,2,1,0:T(8,128)(2,1)S(1)}, u32[]{:S(2)}, u32[]{:S(2)}) collective-permute-start(bf16[2,32,16,256]{3,2,1,0:T(8,128)(2,1)S(1)} %copy-done.42), channel_id=1, source_target_pairs={{0,6},{1,7},{2,4},{3,5},{4,2},{5,3},{6,0},{7,1},{8,14},{9,15},{10,... | collective-permute-start | bytes 1572872 | tf_op jit(solution)/shard_map/ppermute | solution.py:410
  80.2 14.8 %copy-start.31 = (bf16[2,32,16,256]{3,2,1,0:T(8,128)(2,1)}, bf16[2,32,16,256]{3,2,1,0:T(8,128)(2,1)S(1)}, u32[]{:S(2)}) copy-start(bf16[2,32,16,256]{3,2,1,0:T(8,128)(2,1)S(1)} %collective-permute-done.6.refs_1_) | copy-start | bytes 1572868
  117.5 93.9 %copy-start = (bf16[1024,1024]{1,0:T(8,128)(2,1)S(1)}, bf16[1024,1024]{1,0:T(8,128)(2,1)}, u32[]{:S(2)}) copy-start(bf16[1024,1024]{1,0:T(8,128)(2,1)} %constant.48.clone.table_ref) | copy-start | bytes 6291460
  117.5 93.9 %copy-start.5 = (bf16[2,32,16,256]{3,2,1,0:T(8,128)(2,1)S(1)}, bf16[2,32,16,256]{3,2,1,0:T(8,128)(2,1)}, u32[]{:S(2)}) copy-start(bf16[2,32,16,256]{3,2,1,0:T(8,128)(2,1)} %get-tuple-element.82._.refs_0_) | copy-start | bytes 1572868
  117.5 93.9 %copy-start.16 = (s32[11]{0:T(128)S(1)}, s32[11]{0:T(128)}, u32[]{:S(2)}) copy-start(s32[11]{0:T(128)} %pad_add_fusion.meta_ref) | copy-start | bytes 136
  117.5 36.7 %collective-permute-start.9 = (bf16[4,32,16,256]{3,2,1,0:T(8,128)(2,1)}, bf16[4,32,16,256]{3,2,1,0:T(8,128)(2,1)}, u32[]{:S(2)}, u32[]{:S(2)}) collective-permute-start(bf16[4,32,16,256]{3,2,1,0:T(8,128)(2,1)} %get-tuple-element.84), channel_id=1, source_target_pairs={{0,1},{1,0},{2,3},{3,2},{4,5},{5,4},{6,7},{7,6},{8,9},{9,8},{10,11... | collective-permute-start | bytes 3145736 | tf_op jit(solution)/shard_map/ppermute | solution.py:410
  117.6 35.2 %collective-permute-start.10 = (bf16[2,32,16,256]{3,2,1,0:T(8,128)(2,1)}, bf16[2,32,16,256]{3,2,1,0:T(8,128)(2,1)S(1)}, u32[]{:S(2)}, u32[]{:S(2)}) collective-permute-start(bf16[2,32,16,256]{3,2,1,0:T(8,128)(2,1)} %get-tuple-element.87), channel_id=1, source_target_pairs={{0,2},{1,3},{2,0},{3,1},{4,6},{5,7},{6,4},{7,5},{8,10},{9,11},{10,... | collective-permute-start | bytes 1572872 | tf_op jit(solution)/shard_map/ppermute | solution.py:410
  128.6 61.1 %collective-permute-start.13 = (bf16[2,32,16,256]{3,2,1,0:T(8,128)(2,1)}, bf16[2,32,16,256]{3,2,1,0:T(8,128)(2,1)S(1)}, u32[]{:S(2)}, u32[]{:S(2)}) collective-permute-start(bf16[2,32,16,256]{3,2,1,0:T(8,128)(2,1)} %get-tuple-element.91), channel_id=1, source_target_pairs={{0,2},{1,3},{2,0},{3,1},{4,6},{5,7},{6,4},{7,5},{8,10},{9,11},{10,... | collective-permute-start | bytes 1572872 | tf_op jit(solution)/shard_map/ppermute | solution.py:410
  128.7 37.8 %collective-permute-start.11 = (bf16[2,32,16,256]{3,2,1,0:T(8,128)(2,1)}, bf16[2,32,16,256]{3,2,1,0:T(8,128)(2,1)}, u32[]{:S(2)}, u32[]{:S(2)}) collective-permute-start(bf16[2,32,16,256]{3,2,1,0:T(8,128)(2,1)} %get-tuple-element.88), channel_id=1, source_target_pairs={{0,4},{1,5},{2,6},{3,7},{4,0},{5,1},{6,2},{7,3},{8,12},{9,13},{10,... | collective-permute-start | bytes 1572872 | tf_op jit(solution)/shard_map/ppermute | solution.py:410
  131.6 46.3 %collective-permute-start.12 = (bf16[2,32,16,256]{3,2,1,0:T(8,128)(2,1)}, bf16[2,32,16,256]{3,2,1,0:T(8,128)(2,1)}, u32[]{:S(2)}, u32[]{:S(2)}) collective-permute-start(bf16[2,32,16,256]{3,2,1,0:T(8,128)(2,1)} %get-tuple-element.89), channel_id=1, source_target_pairs={{0,6},{1,7},{2,4},{3,5},{4,2},{5,3},{6,0},{7,1},{8,14},{9,15},{10,... | collective-permute-start | bytes 1572872 | tf_op jit(solution)/shard_map/ppermute | solution.py:410
  153.6 57.8 %collective-permute-start.14 = (bf16[2,32,16,256]{3,2,1,0:T(8,128)(2,1)}, bf16[2,32,16,256]{3,2,1,0:T(8,128)(2,1)S(1)}, u32[]{:S(2)}, u32[]{:S(2)}) collective-permute-start(bf16[2,32,16,256]{3,2,1,0:T(8,128)(2,1)} %get-tuple-element.92), channel_id=1, source_target_pairs={{0,4},{1,5},{2,6},{3,7},{4,0},{5,1},{6,2},{7,3},{8,12},{9,13},{10,... | collective-permute-start | bytes 1572872 | tf_op jit(solution)/shard_map/ppermute | solution.py:410
  154.3 57.2 %collective-permute-start.15 = (bf16[2,32,16,256]{3,2,1,0:T(8,128)(2,1)}, bf16[2,32,16,256]{3,2,1,0:T(8,128)(2,1)}, u32[]{:S(2)}, u32[]{:S(2)}) collective-permute-start(bf16[2,32,16,256]{3,2,1,0:T(8,128)(2,1)} %get-tuple-element.93), channel_id=1, source_target_pairs={{0,6},{1,7},{2,4},{3,5},{4,2},{5,3},{6,0},{7,1},{8,14},{9,15},{10,... | collective-permute-start | bytes 1572872 | tf_op jit(solution)/shard_map/ppermute | solution.py:410
  226.8 132.4 %copy-start.2 = (bf16[2,32,16,256]{3,2,1,0:T(8,128)(2,1)S(1)}, bf16[2,32,16,256]{3,2,1,0:T(8,128)(2,1)}, u32[]{:S(2)}) copy-start(bf16[2,32,16,256]{3,2,1,0:T(8,128)(2,1)} %get-tuple-element.90._.refs_0_) | copy-start | bytes 1572868
  226.8 132.4 %copy-start.17 = (s32[11]{0:T(128)S(1)}, s32[11]{0:T(128)}, u32[]{:S(2)}) copy-start(s32[11]{0:T(128)} %pad_add_fusion.meta_ref) | copy-start | bytes 136
  226.8 47.6 %collective-permute-start.16 = (bf16[4,32,16,256]{3,2,1,0:T(8,128)(2,1)}, bf16[4,32,16,256]{3,2,1,0:T(8,128)(2,1)}, u32[]{:S(2)}, u32[]{:S(2)}) collective-permute-start(bf16[4,32,16,256]{3,2,1,0:T(8,128)(2,1)} %get-tuple-element.96), channel_id=1, source_target_pairs={{0,1},{1,0},{2,3},{3,2},{4,5},{5,4},{6,7},{7,6},{8,9},{9,8},{10,11... | collective-permute-start | bytes 3145736 | tf_op jit(solution)/shard_map/ppermute | solution.py:410
  226.8 36.0 %collective-permute-start.20 = (bf16[2,32,16,256]{3,2,1,0:T(8,128)(2,1)}, bf16[2,32,16,256]{3,2,1,0:T(8,128)(2,1)S(1)}, u32[]{:S(2)}, u32[]{:S(2)}) collective-permute-start(bf16[2,32,16,256]{3,2,1,0:T(8,128)(2,1)} %get-tuple-element.103), channel_id=1, source_target_pairs={{0,2},{1,3},{2,0},{3,1},{4,6},{5,7},{6,4},{7,5},{8,10},{9,11},{10,... | collective-permute-start | bytes 1572872 | tf_op jit(solution)/shard_map/ppermute | solution.py:410
  238.6 35.3 %collective-permute-start.17 = (bf16[2,32,16,256]{3,2,1,0:T(8,128)(2,1)}, bf16[2,32,16,256]{3,2,1,0:T(8,128)(2,1)}, u32[]{:S(2)}, u32[]{:S(2)}) collective-permute-start(bf16[2,32,16,256]{3,2,1,0:T(8,128)(2,1)} %get-tuple-element.99), channel_id=1, source_target_pairs={{0,2},{1,3},{2,0},{3,1},{4,6},{5,7},{6,4},{7,5},{8,10},{9,11},{10,... | collective-permute-start | bytes 1572872 | tf_op jit(solution)/shard_map/ppermute | solution.py:410
  238.7 106.3 %collective-permute-start.23 = (bf16[4,32,16,256]{3,2,1,0:T(8,128)(2,1)}, bf16[4,32,16,256]{3,2,1,0:T(8,128)(2,1)S(1)}, u32[]{:S(2)}, u32[]{:S(2)}) collective-permute-start(bf16[4,32,16,256]{3,2,1,0:T(8,128)(2,1)} %get-tuple-element.108), channel_id=1, source_target_pairs={{0,1},{1,0},{2,3},{3,2},{4,5},{5,4},{6,7},{7,6},{8,9},{9,8},{10,11... | collective-permute-start | bytes 3145736 | tf_op jit(solution)/shard_map/ppermute | solution.py:410
  238.8 47.8 %collective-permute-start.18 = (bf16[2,32,16,256]{3,2,1,0:T(8,128)(2,1)}, bf16[2,32,16,256]{3,2,1,0:T(8,128)(2,1)}, u32[]{:S(2)}, u32[]{:S(2)}) collective-permute-start(bf16[2,32,16,256]{3,2,1,0:T(8,128)(2,1)} %get-tuple-element.100), channel_id=1, source_target_pairs={{0,4},{1,5},{2,6},{3,7},{4,0},{5,1},{6,2},{7,3},{8,12},{9,13},{10,... | collective-permute-start | bytes 1572872 | tf_op jit(solution)/shard_map/ppermute | solution.py:410
  263.7 24.2 %collective-permute-start.19 = (bf16[2,32,16,256]{3,2,1,0:T(8,128)(2,1)}, bf16[2,32,16,256]{3,2,1,0:T(8,128)(2,1)}, u32[]{:S(2)}, u32[]{:S(2)}) collective-permute-start(bf16[2,32,16,256]{3,2,1,0:T(8,128)(2,1)} %get-tuple-element.101), channel_id=1, source_target_pairs={{0,6},{1,7},{2,4},{3,5},{4,2},{5,3},{6,0},{7,1},{8,14},{9,15},{10,... | collective-permute-start | bytes 1572872 | tf_op jit(solution)/shard_map/ppermute | solution.py:410
  273.9 69.6 %collective-permute-start.21 = (bf16[2,32,16,256]{3,2,1,0:T(8,128)(2,1)}, bf16[2,32,16,256]{3,2,1,0:T(8,128)(2,1)}, u32[]{:S(2)}, u32[]{:S(2)}) collective-permute-start(bf16[2,32,16,256]{3,2,1,0:T(8,128)(2,1)} %get-tuple-element.104), channel_id=1, source_target_pairs={{0,4},{1,5},{2,6},{3,7},{4,0},{5,1},{6,2},{7,3},{8,12},{9,13},{10,... | collective-permute-start | bytes 1572872 | tf_op jit(solution)/shard_map/ppermute | solution.py:410
  274.4 69.1 %collective-permute-start.22 = (bf16[2,32,16,256]{3,2,1,0:T(8,128)(2,1)}, bf16[2,32,16,256]{3,2,1,0:T(8,128)(2,1)}, u32[]{:S(2)}, u32[]{:S(2)}) collective-permute-start(bf16[2,32,16,256]{3,2,1,0:T(8,128)(2,1)} %get-tuple-element.105), channel_id=1, source_target_pairs={{0,6},{1,7},{2,4},{3,5},{4,2},{5,3},{6,0},{7,1},{8,14},{9,15},{10,... | collective-permute-start | bytes 1572872 | tf_op jit(solution)/shard_map/ppermute | solution.py:410
  286.6 71.2 %collective-permute-start.24 = (bf16[2,32,16,256]{3,2,1,0:T(8,128)(2,1)}, bf16[2,32,16,256]{3,2,1,0:T(8,128)(2,1)}, u32[]{:S(2)}, u32[]{:S(2)}) collective-permute-start(bf16[2,32,16,256]{3,2,1,0:T(8,128)(2,1)} %get-tuple-element.112), channel_id=1, source_target_pairs={{0,2},{1,3},{2,0},{3,1},{4,6},{5,7},{6,4},{7,5},{8,10},{9,11},{10,... | collective-permute-start | bytes 1572872 | tf_op jit(solution)/shard_map/ppermute | solution.py:410
  287.8 111.9 %collective-permute-start.25 = (bf16[2,32,16,256]{3,2,1,0:T(8,128)(2,1)}, bf16[2,32,16,256]{3,2,1,0:T(8,128)(2,1)}, u32[]{:S(2)}, u32[]{:S(2)}) collective-permute-start(bf16[2,32,16,256]{3,2,1,0:T(8,128)(2,1)} %get-tuple-element.113), channel_id=1, source_target_pairs={{0,4},{1,5},{2,6},{3,7},{4,0},{5,1},{6,2},{7,3},{8,12},{9,13},{10,... | collective-permute-start | bytes 1572872 | tf_op jit(solution)/shard_map/ppermute | solution.py:410
  343.5 72.1 %collective-permute-start.27 = (bf16[2,32,16,256]{3,2,1,0:T(8,128)(2,1)}, bf16[2,32,16,256]{3,2,1,0:T(8,128)(2,1)}, u32[]{:S(2)}, u32[]{:S(2)}) collective-permute-start(bf16[2,32,16,256]{3,2,1,0:T(8,128)(2,1)} %get-tuple-element.116), channel_id=1, source_target_pairs={{0,2},{1,3},{2,0},{3,1},{4,6},{5,7},{6,4},{7,5},{8,10},{9,11},{10,... | collective-permute-start | bytes 1572872 | tf_op jit(solution)/shard_map/ppermute | solution.py:410
  343.5 60.1 %collective-permute-start.26 = (bf16[2,32,16,256]{3,2,1,0:T(8,128)(2,1)}, bf16[2,32,16,256]{3,2,1,0:T(8,128)(2,1)}, u32[]{:S(2)}, u32[]{:S(2)}) collective-permute-start(bf16[2,32,16,256]{3,2,1,0:T(8,128)(2,1)} %get-tuple-element.114), channel_id=1, source_target_pairs={{0,6},{1,7},{2,4},{3,5},{4,2},{5,3},{6,0},{7,1},{8,14},{9,15},{10,... | collective-permute-start | bytes 1572872 | tf_op jit(solution)/shard_map/ppermute | solution.py:410
  346.0 76.1 %collective-permute-start.28 = (bf16[2,32,16,256]{3,2,1,0:T(8,128)(2,1)}, bf16[2,32,16,256]{3,2,1,0:T(8,128)(2,1)S(1)}, u32[]{:S(2)}, u32[]{:S(2)}) collective-permute-start(bf16[2,32,16,256]{3,2,1,0:T(8,128)(2,1)} %get-tuple-element.117), channel_id=1, source_target_pairs={{0,4},{1,5},{2,6},{3,7},{4,0},{5,1},{6,2},{7,3},{8,12},{9,13},{10,... | collective-permute-start | bytes 1572872 | tf_op jit(solution)/shard_map/ppermute | solution.py:410
  357.8 64.3 %collective-permute-start.29 = (bf16[2,32,16,256]{3,2,1,0:T(8,128)(2,1)}, bf16[2,32,16,256]{3,2,1,0:T(8,128)(2,1)}, u32[]{:S(2)}, u32[]{:S(2)}) collective-permute-start(bf16[2,32,16,256]{3,2,1,0:T(8,128)(2,1)} %get-tuple-element.118), channel_id=1, source_target_pairs={{0,6},{1,7},{2,4},{3,5},{4,2},{5,3},{6,0},{7,1},{8,14},{9,15},{10,... | collective-permute-start | bytes 1572872 | tf_op jit(solution)/shard_map/ppermute | solution.py:410
  361.3 38.4 %copy-start.9 = (bf16[4,32,16,256]{3,2,1,0:T(8,128)(2,1)S(1)}, bf16[4,32,16,256]{3,2,1,0:T(8,128)(2,1)}, u32[]{:S(2)}) copy-start(bf16[4,32,16,256]{3,2,1,0:T(8,128)(2,1)} %copy-done.8) | copy-start | bytes 3145732
  361.3 60.8 %copy-start.4 = (bf16[2,32,16,256]{3,2,1,0:T(8,128)(2,1)S(1)}, bf16[2,32,16,256]{3,2,1,0:T(8,128)(2,1)}, u32[]{:S(2)}) copy-start(bf16[2,32,16,256]{3,2,1,0:T(8,128)(2,1)} %get-tuple-element.102._.refs_0_) | copy-start | bytes 1572868
  361.3 60.8 %copy-start.18 = (s32[11]{0:T(128)S(1)}, s32[11]{0:T(128)}, u32[]{:S(2)}) copy-start(s32[11]{0:T(128)} %pad_add_fusion.meta_ref) | copy-start | bytes 136
  399.7 66.0 %collective-permute-start.30 = (bf16[4,32,16,256]{3,2,1,0:T(8,128)(2,1)}, bf16[4,32,16,256]{3,2,1,0:T(8,128)(2,1)}, u32[]{:S(2)}, u32[]{:S(2)}) collective-permute-start(bf16[4,32,16,256]{3,2,1,0:T(8,128)(2,1)} %get-tuple-element.121), channel_id=1, source_target_pairs={{0,1},{1,0},{2,3},{3,2},{4,5},{5,4},{6,7},{7,6},{8,9},{9,8},{10,11... | collective-permute-start | bytes 3145736 | tf_op jit(solution)/shard_map/ppermute | solution.py:410
  403.6 65.3 %copy-start.34 = (f32[32,128]{1,0:T(8,128)S(1)}, f32[32,128]{1,0:T(8,128)}, u32[]{:S(2)}) copy-start(f32[32,128]{1,0:T(8,128)} %get-tuple-element.74._) | copy-start | bytes 49156
  403.6 65.3 %copy-start.35 = (f32[32,128]{1,0:T(8,128)S(1)}, f32[32,128]{1,0:T(8,128)}, u32[]{:S(2)}) copy-start(f32[32,128]{1,0:T(8,128)} %get-tuple-element.77._) | copy-start | bytes 49156
  403.6 65.3 %copy-start.36 = (f32[32,128]{1,0:T(8,128)S(1)}, f32[32,128]{1,0:T(8,128)}, u32[]{:S(2)}) copy-start(f32[32,128]{1,0:T(8,128)} %get-tuple-element.85._) | copy-start | bytes 49156
  403.6 65.3 %copy-start.37 = (f32[32,128]{1,0:T(8,128)S(1)}, f32[32,128]{1,0:T(8,128)}, u32[]{:S(2)}) copy-start(f32[32,128]{1,0:T(8,128)} %get-tuple-element.97._) | copy-start | bytes 49156
  403.6 65.3 %copy-start.38 = (f32[32,128]{1,0:T(8,128)S(1)}, f32[32,128]{1,0:T(8,128)}, u32[]{:S(2)}) copy-start(f32[32,128]{1,0:T(8,128)} %get-tuple-element.70._) | copy-start | bytes 49156
  403.6 65.3 %copy-start.39 = (f32[32,128]{1,0:T(8,128)S(1)}, f32[32,128]{1,0:T(8,128)}, u32[]{:S(2)}) copy-start(f32[32,128]{1,0:T(8,128)} %get-tuple-element.75._) | copy-start | bytes 49156
  403.6 65.3 %copy-start.40 = (f32[32,128]{1,0:T(8,128)S(1)}, f32[32,128]{1,0:T(8,128)}, u32[]{:S(2)}) copy-start(f32[32,128]{1,0:T(8,128)} %get-tuple-element.83._) | copy-start | bytes 49156
  403.6 65.3 %copy-start.41 = (f32[32,128]{1,0:T(8,128)S(1)}, f32[32,128]{1,0:T(8,128)}, u32[]{:S(2)}) copy-start(f32[32,128]{1,0:T(8,128)} %get-tuple-element.95._) | copy-start | bytes 49156
  423.1 4.4 copy-start.45
  423.1 16.3 %copy-start.44 = (bf16[1,32,16,256]{3,2,1,0:T(8,128)(2,1)S(1)}, bf16[1,32,16,256]{3,2,1,0:T(8,128)(2,1)}, u32[]{:S(2)}) copy-start(bf16[1,32,16,256]{3,2,1,0:T(8,128)(2,1)} %get-tuple-element.125) | copy-start | bytes 786436
  423.1 16.4 %copy-start.43 = (bf16[1,32,16,256]{3,2,1,0:T(8,128)(2,1)S(1)}, bf16[1,32,16,256]{3,2,1,0:T(8,128)(2,1)}, u32[]{:S(2)}) copy-start(bf16[1,32,16,256]{3,2,1,0:T(8,128)(2,1)} %get-tuple-element.126) | copy-start | bytes 786436
  423.1 61.2 %copy-start.7 = (bf16[1,32,16,256]{3,2,1,0:T(8,128)(2,1)S(1)}, bf16[1,32,16,256]{3,2,1,0:T(8,128)(2,1)}, u32[]{:S(2)}) copy-start(bf16[1,32,16,256]{3,2,1,0:T(8,128)(2,1)} %get-tuple-element.115._.refs_0_) | copy-start | bytes 786436
  427.5 60.6 %collective-permute-start.34 = (bf16[4,32,16,256]{3,2,1,0:T(8,128)(2,1)}, bf16[4,32,16,256]{3,2,1,0:T(8,128)(2,1)}, u32[]{:S(2)}, u32[]{:S(2)}) collective-permute-start(bf16[4,32,16,256]{3,2,1,0:T(8,128)(2,1)} %get-tuple-element.129), channel_id=1, source_target_pairs={{0,1},{1,0},{2,3},{3,2},{4,5},{5,4},{6,7},{7,6},{8,9},{9,8},{10,11... | collective-permute-start | bytes 3145736 | tf_op jit(solution)/shard_map/ppermute | solution.py:410
  427.5 23.3 %collective-permute-start.31 = (bf16[1,32,16,256]{3,2,1,0:T(8,128)(2,1)S(1)}, bf16[1,32,16,256]{3,2,1,0:T(8,128)(2,1)S(1)}, u32[]{:S(2)}, u32[]{:S(2)}) collective-permute-start(bf16[1,32,16,256]{3,2,1,0:T(8,128)(2,1)S(1)} %copy-done.45), channel_id=1, source_target_pairs={{0,2},{1,3},{2,0},{3,1},{4,6},{5,7},{6,4},{7,5},{8,10},{9,11},{10,... | collective-permute-start | bytes 786440 | tf_op jit(solution)/shard_map/ppermute | solution.py:410
  439.4 21.3 %collective-permute-start.32 = (bf16[1,32,16,256]{3,2,1,0:T(8,128)(2,1)S(1)}, bf16[1,32,16,256]{3,2,1,0:T(8,128)(2,1)S(1)}, u32[]{:S(2)}, u32[]{:S(2)}) collective-permute-start(bf16[1,32,16,256]{3,2,1,0:T(8,128)(2,1)S(1)} %copy-done.44), channel_id=1, source_target_pairs={{0,4},{1,5},{2,6},{3,7},{4,0},{5,1},{6,2},{7,3},{8,12},{9,13},{10,... | collective-permute-start | bytes 786440 | tf_op jit(solution)/shard_map/ppermute | solution.py:410
  439.4 22.0 %collective-permute-start.33 = (bf16[1,32,16,256]{3,2,1,0:T(8,128)(2,1)S(1)}, bf16[1,32,16,256]{3,2,1,0:T(8,128)(2,1)S(1)}, u32[]{:S(2)}, u32[]{:S(2)}) collective-permute-start(bf16[1,32,16,256]{3,2,1,0:T(8,128)(2,1)S(1)} %copy-done.43), channel_id=1, source_target_pairs={{0,6},{1,7},{2,4},{3,5},{4,2},{5,3},{6,0},{7,1},{8,14},{9,15},{10,... | collective-permute-start | bytes 786440 | tf_op jit(solution)/shard_map/ppermute | solution.py:410
  450.7 42.1 %collective-permute-start.35 = (bf16[1,32,16,256]{3,2,1,0:T(8,128)(2,1)}, bf16[1,32,16,256]{3,2,1,0:T(8,128)(2,1)S(1)}, u32[]{:S(2)}, u32[]{:S(2)}) collective-permute-start(bf16[1,32,16,256]{3,2,1,0:T(8,128)(2,1)} %get-tuple-element.132), channel_id=1, source_target_pairs={{0,1},{1,0},{2,3},{3,2},{4,5},{5,4},{6,7},{7,6},{8,9},{9,8},{10,11... | collective-permute-start | bytes 786440 | tf_op jit(solution)/shard_map/ppermute | solution.py:410
  461.4 31.4 %collective-permute-start.36 = (bf16[1,32,16,256]{3,2,1,0:T(8,128)(2,1)}, bf16[1,32,16,256]{3,2,1,0:T(8,128)(2,1)S(1)}, u32[]{:S(2)}, u32[]{:S(2)}) collective-permute-start(bf16[1,32,16,256]{3,2,1,0:T(8,128)(2,1)} %get-tuple-element.133), channel_id=1, source_target_pairs={{0,3},{1,2},{2,1},{3,0},{4,7},{5,6},{6,5},{7,4},{8,11},{9,10},{10,... | collective-permute-start | bytes 786440 | tf_op jit(solution)/shard_map/ppermute | solution.py:410
  462.1 30.7 %collective-permute-start.37 = (bf16[1,32,16,256]{3,2,1,0:T(8,128)(2,1)}, bf16[1,32,16,256]{3,2,1,0:T(8,128)(2,1)S(1)}, u32[]{:S(2)}, u32[]{:S(2)}) collective-permute-start(bf16[1,32,16,256]{3,2,1,0:T(8,128)(2,1)} %get-tuple-element.134), channel_id=1, source_target_pairs={{0,5},{1,4},{2,7},{3,6},{4,1},{5,0},{6,3},{7,2},{8,13},{9,12},{10,... | collective-permute-start | bytes 786440 | tf_op jit(solution)/shard_map/ppermute | solution.py:410
  465.7 27.1 %collective-permute-start.38 = (bf16[1,32,16,256]{3,2,1,0:T(8,128)(2,1)}, bf16[1,32,16,256]{3,2,1,0:T(8,128)(2,1)}, u32[]{:S(2)}, u32[]{:S(2)}) collective-permute-start(bf16[1,32,16,256]{3,2,1,0:T(8,128)(2,1)} %get-tuple-element.135), channel_id=1, source_target_pairs={{0,7},{1,6},{2,5},{3,4},{4,3},{5,2},{6,1},{7,0},{8,15},{9,14},{10,... | collective-permute-start | bytes 786440 | tf_op jit(solution)/shard_map/ppermute | solution.py:410
  479.0 5.3 %copy-start.13 = (bf16[1,32,16,256]{3,2,1,0:T(8,128)(2,1)S(1)}, bf16[1,32,16,256]{3,2,1,0:T(8,128)(2,1)}, u32[]{:S(2)}) copy-start(bf16[1,32,16,256]{3,2,1,0:T(8,128)(2,1)} %copy-done.12) | copy-start | bytes 786436
  479.0 5.3 %copy-start.15 = (bf16[1,32,16,256]{3,2,1,0:T(8,128)(2,1)S(1)}, bf16[1,32,16,256]{3,2,1,0:T(8,128)(2,1)}, u32[]{:S(2)}) copy-start(bf16[1,32,16,256]{3,2,1,0:T(8,128)(2,1)} %copy-done.14) | copy-start | bytes 786436
  (21 other events, 17.8 us)

commit v7 on v6

v7 whole, which is shorter than its diff:
```python
import functools

import jax
import jax.numpy as jnp
import ml_dtypes
import numpy as np
from jax import lax
from jax.experimental import pallas as pl
from jax.experimental.pallas import tpu as pltpu
from jax.sharding import PartitionSpec as P

F = 512
SOURCE_SPACING = 512
JITTER = 256
STEP = 0.5
LANES = 128
NEAR = SOURCE_SPACING - JITTER
FAR = SOURCE_SPACING + JITTER
HALO = 3


def time_tables(samples, blocks):
    freq = np.arange(F, dtype=np.int32)
    sample = np.arange(samples, dtype=np.int32)
    phase = (freq[:, None] * sample[None, :] % samples).astype(np.float32)
    angle = np.float32(2.0 * np.pi) * phase / np.float32(samples)
    root = np.sqrt(np.float32(samples))
    weight = np.where(freq == 0, 1.0, 2.0).astype(np.float32)[:, None] / root
    forward = np.stack([np.cos(angle) / root, -np.sin(angle) / root])
    inverse = np.stack([weight * np.cos(angle), -weight * np.sin(angle)])

    def ordered(table):
        table = table.astype(np.float32).astype(ml_dtypes.bfloat16)
        table = table.reshape(2, blocks, F // blocks, samples).transpose(1, 0, 2, 3)
        return table.reshape(2 * F, samples)

    return np.ascontiguousarray(ordered(forward).T), ordered(inverse)


def shot_table(shots):
    index = np.arange(shots, dtype=np.int32)
    phase = (index[:, None] * index[None, :] % shots).astype(np.float32)
    angle = np.float32(2.0 * np.pi) * phase / np.float32(shots)
    root = np.sqrt(np.float32(shots))
    table = np.concatenate([np.cos(angle) / root, np.sin(angle) / root])
    return table.astype(np.float32).astype(ml_dtypes.bfloat16)


def band(meta_ref, slot, width):
    return pl.ds(pl.multiple_of(meta_ref[1 + slot] * width, width), width)


def blend_into(
    meta_ref, delay_ref, est_ref, obs_ref, before_ref, after_ref, energy_ref, est32, res32, store
):
    shots, rows, samples = est_ref.shape
    columns = samples // LANES
    margin = (FAR - NEAR) // LANES
    inner = (samples - NEAR) // LANES
    skip = NEAR // LANES
    total = delay_ref.shape[0]
    first = meta_ref[0]
    lane = lax.broadcasted_iota(jnp.int32, (1, rows, LANES), 2)

    def ahead(shot):
        shot = jnp.clip(shot, 0, total - 2)
        return jnp.clip(SOURCE_SPACING + delay_ref[shot + 1] - delay_ref[shot], NEAR + 1, FAR - 1)

    def window(field, slot, start):
        column, rest = start // LANES, start % LANES
        wide = field[slot, pl.ds(column, inner + 1)]
        turned = pltpu.roll(
            wide.reshape((inner + 1) * rows, LANES), (LANES - rest) % LANES, 1
        ).reshape(inner + 1, rows, LANES)
        return jnp.where(lane < LANES - rest, turned[:-1], turned[1:])

    def blended(field, slot, shot):
        later = window(field, slot + 1, margin * LANES + NEAR - ahead(shot))
        earlier = window(field, slot - 1, margin * LANES + ahead(shot - 1))
        return later, earlier

    def fill(field, slot, values):
        blank = jnp.zeros((margin, rows, LANES), jnp.float32)
        field[slot, pl.ds(0, margin)] = blank
        field[slot, pl.ds(margin + columns, margin)] = blank
        for column in range(columns):
            field[slot, margin + column] = values(column)

    def cut(ref, shot):
        return lambda column: ref[shot, :, column * LANES : (column + 1) * LANES].astype(jnp.float32)

    for slot in range(2):
        fill(est32, slot, cut(before_ref, slot))
        fill(est32, shots + 2 + slot, cut(after_ref, slot))

    def load(shot, carry):
        fill(est32, shot + 2, cut(est_ref, shot))
        return carry

    lax.fori_loop(0, shots, load, 0, unroll=2)

    def residual(place, values):
        shot = first + place - 1
        inside = jnp.logical_and(shot >= 0, shot < total)
        later, earlier = blended(est32, place + 1, shot)
        power = jnp.zeros((rows, LANES), jnp.float32)
        cells = []
        for column in range(columns):
            cell = est32[place + 1, margin + column]
            if column >= skip:
                cell = cell + later[column - skip]
            if column < inner:
                cell = cell + earlier[column]
            cell = jnp.where(inside, values(column) - cell, 0.0)
            power = power + cell * cell
            cells.append(cell)
        fill(res32, place, lambda column: cells[column])
        return power

    residual(0, cut(before_ref, 2))
    residual(shots + 1, cut(after_ref, 2))

    def middle(shot, carry):
        power = residual(shot + 1, cut(obs_ref, shot))
        energy_ref[pl.ds(shot, 1), :] = jnp.sum(power, axis=0, keepdims=True)
        return carry

    lax.fori_loop(0, shots, middle, 0, unroll=4)

    def step(shot, carry):
        later, earlier = blended(res32, shot + 1, first + shot)
        for column in range(columns):
            cell = res32[shot + 1, margin + column]
            if column >= skip:
                cell = cell + later[column - skip]
            if column < inner:
                cell = cell + earlier[column]
            cell = est32[shot + 2, margin + column] + STEP * cell
            store(shot, column, cell.astype(jnp.bfloat16))
        return carry

    lax.fori_loop(0, shots, step, 0, unroll=4)


def spectra_kernel(
    meta_ref, delay_ref, est_ref, obs_ref, before_ref, after_ref, table_ref, _, *refs
):
    *out_refs, energy_ref, est32, res32, stepped, result = refs
    shots, rows, samples = est_ref.shape
    width = out_refs[0].shape[2]

    def store(shot, column, values):
        start = pl.multiple_of(shot * rows, rows)
        stepped[pl.ds(start, rows), column * LANES : (column + 1) * LANES] = values

    blend_into(
        meta_ref, delay_ref, est_ref, obs_ref, before_ref, after_ref, energy_ref, est32, res32, store
    )
    held = result.shape[0]
    group = held // rows

    def transform(part, carry):
        start = pl.multiple_of(part * held, held)
        result[...] = jnp.dot(
            stepped[pl.ds(start, held), :], table_ref[...], preferred_element_type=jnp.float32
        ).astype(jnp.bfloat16)
        for slot, ref in enumerate(out_refs):
            ref[pl.ds(part * group, group)] = result[:, band(meta_ref, slot, width)].reshape(
                group, rows, width
            )
        return carry

    lax.fori_loop(0, shots // group, transform, 0)


def step_kernel(
    meta_ref, delay_ref, est_ref, obs_ref, before_ref, after_ref, out_ref, energy_ref, est32, res32
):
    def store(shot, column, values):
        out_ref[shot, :, column * LANES : (column + 1) * LANES] = values

    blend_into(
        meta_ref, delay_ref, est_ref, obs_ref, before_ref, after_ref, energy_ref, est32, res32, store
    )


def shots_kernel(meta_ref, table_ref, level_ref, _, *refs):
    *refs, wide, back = refs
    spectra_refs, out_refs = refs[: len(refs) // 2], refs[len(refs) // 2 :]
    held, rows, width = out_refs[0].shape
    shots = wide.shape[0] // rows
    half = width // 2

    def place(slot):
        size = held * rows
        return pl.ds(pl.multiple_of(meta_ref[1 + slot] * size, size), size)

    for slot, ref in zip(slots_of(len(spectra_refs)), spectra_refs):
        wide[place(slot), :] = ref[...].reshape(held * rows, width).astype(jnp.float32)
    level = level_ref[...]
    sign = jnp.where(
        lax.broadcasted_iota(jnp.int32, (1, width), 1) < half, jnp.float32(1.0), jnp.float32(-1.0)
    )

    def pair(index, carry):
        picks = [pl.ds(index * 2 + turn, shots, stride=rows) for turn in range(2)]
        block = jnp.concatenate([wide[pick, :] for pick in picks], axis=1).astype(jnp.bfloat16)
        both = jnp.dot(table_ref[...], block, preferred_element_type=jnp.float32)
        kept = []
        for turn in range(2):
            own = both[:, turn * width : (turn + 1) * width]
            wave = own[:shots] + sign * pltpu.roll(own[shots:], half, 1)
            power = wave * wave
            power = power + pltpu.roll(power, half, 1)
            factor = jnp.maximum(1.0 - level * lax.rsqrt(power), 0.0)
            kept.append((wave * factor).astype(jnp.bfloat16))
        both = jnp.dot(table_ref[...], jnp.concatenate(kept, axis=1), preferred_element_type=jnp.float32)
        for turn in range(2):
            own = both[:, turn * width : (turn + 1) * width]
            back[picks[turn], :] = own[:shots] - sign * pltpu.roll(own[shots:], half, 1)
        return carry

    lax.fori_loop(0, rows // 2, pair, 0, unroll=2)
    for slot, ref in enumerate(out_refs):
        ref[...] = back[place(slot), :].astype(jnp.bfloat16).reshape(held, rows, width)


def update_kernel(inputs, meta_ref, table_ref, _, *refs):
    restored_refs, (out_ref, turn_ref, whole_rows) = refs[:inputs], refs[-3:]
    held, rows, width = restored_refs[0].shape
    for slot, ref in zip(slots_of(inputs), restored_refs):
        whole_rows[:, band(meta_ref, slot, width)] = ref[...].reshape(held * rows, width)
    out_ref[...] = jnp.dot(
        whole_rows[...], table_ref[...], preferred_element_type=jnp.float32
    ).reshape(out_ref.shape)
    turn_ref[...] = jnp.zeros_like(turn_ref)


def whole(shape):
    return pl.BlockSpec(shape, lambda *_: (0,) * len(shape))


def blend_specs(shots, rows, samples, block, edge_block):
    at = lambda step, meta, delays: (0, block, 0)
    edge = lambda step, meta, delays: (0, edge_block, 0)
    return [
        pl.BlockSpec((shots, rows, samples), at),
        pl.BlockSpec((shots, rows, samples), at),
        pl.BlockSpec((HALO, rows, samples), edge),
        pl.BlockSpec((HALO, rows, samples), edge),
    ]


def blend_scratch(shots, rows, samples):
    columns = (samples + 2 * (FAR - NEAR)) // LANES
    return [
        pltpu.VMEM((shots + 4, columns, rows, LANES), jnp.float32),
        pltpu.VMEM((shots + 2, columns, rows, LANES), jnp.float32),
    ]


PARAMS = pltpu.CompilerParams(vmem_limit_bytes=60 * 1024 * 1024)
SMALL = pl.CostEstimate(flops=1024, bytes_accessed=1024, transcendentals=0)
ANYWHERE = pl.BlockSpec(memory_space=pl.ANY)


def spectra_of(meta, delays, fields, table, rows, block, edge_block, peers, after):
    shots, _, samples = fields[0].shape
    shape = (shots, rows, 2 * F // peers)
    group = min(shots, max(1, 256 // rows))
    *spectra, energy = pl.pallas_call(
        spectra_kernel,
        grid_spec=pltpu.PrefetchScalarGridSpec(
            num_scalar_prefetch=2,
            grid=(1,),
            in_specs=blend_specs(shots, rows, samples, block, edge_block)
            + [whole(table.shape), ANYWHERE],
            out_specs=[whole(shape)] * peers + [whole((shots, LANES))],
            scratch_shapes=blend_scratch(shots, rows, samples)
            + [
                pltpu.VMEM((shots * rows, samples), jnp.bfloat16),
                pltpu.VMEM((group * rows, 2 * F), jnp.bfloat16),
            ],
        ),
        out_shape=[pltpu.HBM(shape, jnp.bfloat16)] * peers + [pltpu.HBM((shots, LANES), jnp.float32)],
        compiler_params=PARAMS,
        cost_estimate=SMALL,
        name="spectra",
    )(meta, delays, *fields, table, after)
    return spectra, energy


def stepped_of(meta, delays, fields, rows, index):
    shots, _, samples = fields[0].shape
    return pl.pallas_call(
        step_kernel,
        grid_spec=pltpu.PrefetchScalarGridSpec(
            num_scalar_prefetch=2,
            grid=(1,),
            in_specs=blend_specs(shots, rows, samples, index, index),
            out_specs=[whole((shots, rows, samples)), whole((shots, LANES))],
            scratch_shapes=blend_scratch(shots, rows, samples),
        ),
        out_shape=[
            jax.ShapeDtypeStruct((shots, rows, samples), jnp.bfloat16),
            jax.ShapeDtypeStruct((shots, LANES), jnp.float32),
        ],
        compiler_params=PARAMS,
        name="stepped",
    )(meta, delays, *fields)


def shrunk_of(meta, spectra, table, level, after):
    shape = spectra[0][0].shape
    held, rows, width = shape
    peers = len(spectra)
    return pl.pallas_call(
        shots_kernel,
        grid_spec=pltpu.PrefetchScalarGridSpec(
            num_scalar_prefetch=1,
            grid=(1,),
            in_specs=[whole(table.shape), whole(level.shape), ANYWHERE]
            + [read(item, shape, lambda step: (0, 0, 0)) for item in spectra],
            out_specs=[whole(shape)] * peers,
            scratch_shapes=[pltpu.VMEM((peers * held * rows, width), jnp.float32)] * 2,
        ),
        out_shape=[pltpu.HBM(shape, jnp.bfloat16)] * peers,
        compiler_params=PARAMS,
        cost_estimate=SMALL,
        name="shrink",
    )(meta, table, level, after, *[array for array, _ in spectra])


def updated_of(meta, restored, table, block, receivers, onto, after):
    shots, rows, width = restored[0][0].shape
    samples = table.shape[1]
    group = min(shots, max(1, 256 // rows))
    in_specs = [whole(table.shape), ANYWHERE]
    in_specs += [read(item, (group, rows, width), lambda step: (step, 0, 0)) for item in restored]
    operands = [meta, table, after, *[array for array, _ in restored]]
    if onto is not None:
        in_specs.append(ANYWHERE)
        operands.append(onto)
    return pl.pallas_call(
        functools.partial(update_kernel, len(restored)),
        grid_spec=pltpu.PrefetchScalarGridSpec(
            num_scalar_prefetch=1,
            grid=(shots // group,),
            in_specs=in_specs,
            out_specs=[
                pl.BlockSpec((group, rows, samples), lambda step, meta: (step, block, 0)),
                whole((8, LANES)),
            ],
            scratch_shapes=[pltpu.VMEM((group * rows, 2 * F), jnp.bfloat16)],
        ),
        out_shape=[
            pltpu.HBM((shots, receivers, samples), jnp.float32),
            pltpu.HBM((8, LANES), jnp.float32),
        ],
        input_output_aliases={} if onto is None else {len(operands) - 1: 0},
        compiler_params=pltpu.CompilerParams(vmem_limit_bytes=24 * 1024 * 1024),
        cost_estimate=SMALL,
        name="update",
    )(*operands)


def swapped(array):
    return lax.all_to_all(array, "shot", split_axis=0, concat_axis=0, tiled=True)


def sent(array, distance):
    peers = lax.axis_size("shot")
    if distance == 1:
        groups = [[i, i ^ 1] for i in range(0, peers, 2)]
        return lax.all_gather(array, "shot", axis_index_groups=groups), distance
    return lax.ppermute(array, "shot", [(i, i ^ distance) for i in range(peers)]), 0


def held(array):
    return array, 0


def read(item, shape, where):
    _, distance = item
    if distance == 0:
        return pl.BlockSpec(shape, lambda step, meta, *_: where(step))
    return pl.BlockSpec(
        (None, *shape),
        lambda step, meta, *_: (jnp.where(meta[1] < meta[1 + distance], 1, 0), *where(step)),
    )


def slots_of(peers):
    far, near = list(range(peers // 2, peers)), list(range(2, peers // 2))
    order = [0, 1]
    while far or near:
        order += far[:2] + near[:1]
        far, near = far[2:], near[1:]
    return order


def exchanged(arrays):
    slots = slots_of(len(arrays))
    return [sent(arrays[slot], slot) if slot else held(arrays[slot]) for slot in slots]


def edges(estimate, observed):
    peers = lax.axis_size("shot")
    up = [(i, i + 1) for i in range(peers - 1)]
    down = [(j, i) for i, j in up]
    tail = jnp.concatenate([estimate[-2:], observed[-1:]])
    head = jnp.concatenate([estimate[:2], observed[:1]])
    return lax.ppermute(tail, "shot", up), lax.ppermute(head, "shot", down)


def chunks_of(receivers):
    if receivers == 128:
        return [(16, 7), (16, 6), (32, 2), (32, 1), (16, 1), (16, 0)]
    rows = min(16, receivers)
    return [(rows, index) for index in range(receivers // rows)][::-1]


def direct(estimate, observed, delays, thresholds):
    shots, receivers, samples = estimate.shape
    peers = lax.axis_size("shot")
    rank = lax.axis_index("shot")
    share = F // peers
    meta = jnp.concatenate(
        [jnp.reshape(rank * shots, (1,)), rank ^ jnp.arange(peers, dtype=jnp.int32)]
    ).astype(jnp.int32)
    forward, inverse = (jnp.asarray(table) for table in time_tables(samples, peers))
    table = jnp.asarray(shot_table(delays.shape[0]))
    levels = jnp.tile(lax.dynamic_slice_in_dim(thresholds, rank * share, share), 2)[None, :]
    chunks = chunks_of(receivers)
    rest = receivers - chunks[0][0]
    early = edges(estimate[:, rest:], observed[:, rest:])
    late = None
    last, updated, energy = levels, None, 0.0
    lag = 2
    ahead, behind = {}, {}
    for turn in range(len(chunks) + 2 * lag):
        if turn < len(chunks):
            rows, index = chunks[turn]
            spectra, power = spectra_of(
                meta,
                delays,
                (estimate, observed, *(late if turn else early)),
                forward,
                rows,
                index,
                index if turn else 0,
                peers,
                last,
            )
            last = power
            energy = energy + power
            ahead[turn] = exchanged(spectra)
            if turn == 0 and rest:
                later = lax.optimization_barrier((estimate, observed, power))
                late = edges(later[0][:, :rest], later[1][:, :rest])
        place = turn - lag
        if place in ahead:
            shrunk = shrunk_of(meta, ahead.pop(place), table, levels, last)
            last = shrunk[0]
            behind[place] = exchanged(shrunk)
        place = turn - 2 * lag
        if place in behind:
            updated, last = updated_of(
                meta, behind.pop(place), inverse, chunks[place][1], receivers, updated, last
            )
    return updated, energy


def spectral_by_einsum(stepped, forward, inverse, table, level, peers):
    shots, receivers, samples = stepped.shape
    total = table.shape[1]
    share = F // peers
    spectra = jnp.einsum(
        "srt,tdpf->dpfsr",
        stepped,
        forward.reshape(samples, peers, 2, share),
        preferred_element_type=jnp.float32,
    ).astype(jnp.bfloat16)
    mixed = swapped(spectra).transpose(1, 2, 0, 3, 4).reshape(2, share, total, receivers)
    cosine, sine = table[:total], table[total:]
    across = jnp.stack([jnp.stack([cosine, sine]), jnp.stack([-sine, cosine])])
    wave = jnp.einsum("pqks,qfsr->pfkr", across, mixed, preferred_element_type=jnp.float32)
    magnitude = jnp.sqrt(wave[0] * wave[0] + wave[1] * wave[1])
    bound = level[:, None, None]
    factor = jnp.maximum(magnitude - bound, 0.0) / jnp.maximum(magnitude, bound)
    shrunk = (wave * factor[None]).astype(jnp.bfloat16)
    back = jnp.stack([jnp.stack([cosine, -sine]), jnp.stack([sine, cosine])])
    restored = jnp.einsum(
        "pqks,qfkr->pfsr", back, shrunk, preferred_element_type=jnp.float32
    ).astype(jnp.bfloat16)
    restored = restored.reshape(2, share, peers, shots, receivers).transpose(2, 0, 1, 3, 4)
    return jnp.einsum(
        "dpft,dpfsr->srt",
        inverse.reshape(peers, 2, share, samples),
        swapped(restored),
        preferred_element_type=jnp.float32,
    )


def by_einsum(estimate, observed, delays, thresholds):
    shots, receivers, samples = estimate.shape
    peers = lax.axis_size("shot")
    rank = lax.axis_index("shot")
    share = F // peers
    rows = min(16, receivers)
    meta = jnp.reshape(rank * shots, (1,)).astype(jnp.int32)
    sides = edges(estimate, observed)
    energy = 0.0
    parts = []
    for index in range(receivers // rows):
        part, power = stepped_of(meta, delays, (estimate, observed, *sides), rows, index)
        energy = energy + power
        parts.append(part)
    forward, inverse = (jnp.asarray(table) for table in time_tables(samples, peers))
    table = jnp.asarray(shot_table(delays.shape[0]))
    level = lax.dynamic_slice_in_dim(thresholds, rank * share, share)
    stepped = jnp.concatenate(parts, axis=1)
    return spectral_by_einsum(stepped, forward, inverse, table, level, peers), energy


def local(estimate, observed, random_source_delays, thresholds):
    receivers, samples = estimate.shape[1:]
    peers = lax.axis_size("shot")
    filled = peers >= 4 and peers & (peers - 1) == 0 and (2 * F // peers) % LANES == 0
    path = direct if filled else by_einsum
    updated, energy = path(estimate, observed, random_source_delays, thresholds)
    misfit = lax.psum(jnp.sum(energy, axis=1), "patch") / (
        receivers * lax.axis_size("patch") * samples
    )
    return updated, misfit


def solution(mesh):
    in_specs = (P("shot", "patch", None), P("shot", "patch", None), P(), P())
    out_specs = (P("shot", "patch", None), P("shot"))
    return jax.shard_map(local, mesh=mesh, in_specs=in_specs, out_specs=out_specs, check_vma=False)
```

time: 499 us -> 480 us (0.962)
  waiting for transfers between devices: 179 us -> 129 us
  blocking collectives: 9.91 us -> 40.8 us
  starting transfers between devices: 126 us -> 135 us
  Pallas kernels: 160 us -> 152 us
    ppermute x35 -> x72, waiting for transfers between devices: 176 us -> 127 us  [sent(): lax.ppermute(array, 'shot', [(i, i ^ distance) for i in range(peers)])]
    all_gather x0 -> x12, blocking collectives: none -> 30.9 us  [sent(): return (lax.all_gather(array, 'shot', axis_index_groups=groups), distance)]
    pallas_call x20 -> x18, Pallas kernels: 160 us -> 152 us  [the longest x6 69.5 us: spectra_of(): pl.pallas_call(spectra_kernel, grid_spec=pltpu.PrefetchScalarGridSpec(num...]
    ppermute x35 -> x72, starting transfers between devices: 119 us -> 124 us  [sent(): lax.ppermute(array, 'shot', [(i, i ^ distance) for i in range(peers)])]
    unnamed x92 -> x156, local copies, waits for them, and re-layouts: 15.5 us -> 13 us
  transfers between devices with their start and end apart: 39 -> 76, of which waited for: 13 -> 17; matrix products, arithmetic and copies ran while one was open for 1% -> 1% of each run, Pallas kernels for 20% -> 29%
where the time goes in v7:
time: 480 us; the launch traced here: 478 us
  Pallas kernels  152 us (32%)
  starting transfers between devices  135 us (28%)
  waiting for transfers between devices  129 us (27%)
  blocking collectives  40.8 us (8%)
  local copies, waits for them, and re-layouts  18.3 us (4%)
    ppermute x72, waiting for transfers between devices, sent(): lax.ppermute(array, 'shot', [(i, i ^ distance) for i in range(peers)])  127 us
    ppermute x72, starting transfers between devices, sent(): lax.ppermute(array, 'shot', [(i, i ^ distance) for i in range(peers)])  124 us
    pallas_call x6, Pallas kernels, spectra_of(): pl.pallas_call(spectra_kernel, grid_spec=pltpu.PrefetchScalarGridSpec(num...  69.5 us
    pallas_call x6, Pallas kernels, shrunk_of(): pl.pallas_call(shots_kernel, grid_spec=pltpu.PrefetchScalarGridSpec(num_s...  58.4 us
    all_gather x12, blocking collectives, sent(): return (lax.all_gather(array, 'shot', axis_index_groups=groups), distance)  30.9 us
    pallas_call x6, Pallas kernels, updated_of(): pl.pallas_call(functools.partial(update_kernel, len(restored)), grid_spec...  24.2 us
    unnamed x156, local copies, waits for them, and re-layouts  13 us
    ppermute x4, starting transfers between devices, edges(): return (lax.ppermute(tail, 'shot', up), lax.ppermute(head, 'shot', down))  10.8 us
  transfers between devices with their start and end apart: 76, of which 17 were waited for; matrix products, arithmetic and copies ran while one was open for 1% of the time, Pallas kernels for 29%

profile of v7, /device:TPU:0, one launch (start us, length us, event | category | flops | bytes accessed | tf_op | source)
XLA Modules:
  0.0 478.4 jit_solution(1892718917532132914)
XLA Ops:
  2.3 2.4 collective-permute-start
  8.0 2.1 collective-permute-done.1.after_ref
  10.7 9.9 %spectra.6 = (bf16[32,16,128]{2,1,0:T(8,128)(2,1)}, bf16[32,16,128]{2,1,0:T(8,128)(2,1)}, bf16[32,16,128]{2,1,0:T(8,128)(2,1)}, bf16[32,16,128]{2,1,0:T(8,128)(2...) custom-call(s32[9]{0:T(128)} %pad_add_fusion.meta_ref, ...), custom_call_target="tpu_custom_call" | custom-call | flops 1024 | bytes 1024 | tf_op jit(solution)/shard_map/spectra/pallas_call | solution.py:271
  24.4 5.8 %collective-permute-start.2 = (bf16[3,112,1024]{2,1,0:T(8,128)(2,1)S(1)}, bf16[3,112,1024]{2,1,0:T(8,128)(2,1)S(1)}, u32[]{:S(2)}, u32[]{:S(2)}) collective-permute-start(bf16[3,112,1024]{2,1,0:T(8,128)(2,1)S(1)} %pad_maximum_fusion), channel_id=1, source_target_pairs={{0,1},{1,2},{2,3},{3,4},{4,5},{5,6},{6,7},{8,9},{9,10},{10,11},{11... | collective-permute-start | bytes 2064392 | tf_op jit(solution)/shard_map/ppermute | solution.py:413
  30.2 2.7 collective-permute-start.4
  35.8 8.4 %collective-permute-start.7 = (bf16[32,16,128]{2,1,0:T(8,128)(2,1)}, bf16[32,16,128]{2,1,0:T(8,128)(2,1)S(1)}, u32[]{:S(2)}, u32[]{:S(2)}) collective-permute-start(bf16[32,16,128]{2,1,0:T(8,128)(2,1)} %get-tuple-element.127), channel_id=1, source_target_pairs={{0,6},{1,7},{2,4},{3,5},{4,2},{5,3},{6,0},{7,1},{8,14},{9,15},{10,... | collective-permute-start | bytes 393224 | tf_op jit(solution)/shard_map/ppermute | solution.py:376
  45.2 10.0 %spectra.7 = (bf16[32,16,128]{2,1,0:T(8,128)(2,1)}, bf16[32,16,128]{2,1,0:T(8,128)(2,1)}, bf16[32,16,128]{2,1,0:T(8,128)(2,1)}, bf16[32,16,128]{2,1,0:T(8,128)(2...) custom-call(s32[9]{0:T(128)} %pad_add_fusion.meta_ref, ...), custom_call_target="tpu_custom_call" | custom-call | flops 1024 | bytes 1024 | tf_op jit(solution)/shard_map/spectra/pallas_call | solution.py:271
  55.4 12.7 %collective-permute-start.9 = (bf16[32,16,128]{2,1,0:T(8,128)(2,1)S(1)}, bf16[32,16,128]{2,1,0:T(8,128)(2,1)S(1)}, u32[]{:S(2)}, u32[]{:S(2)}) collective-permute-start(bf16[32,16,128]{2,1,0:T(8,128)(2,1)S(1)} %copy-done.77), channel_id=1, source_target_pairs={{0,3},{1,2},{2,1},{3,0},{4,7},{5,6},{6,5},{7,4},{8,11},{9,10},{10,... | collective-permute-start | bytes 393224 | tf_op jit(solution)/shard_map/ppermute | solution.py:376
  68.8 2.1 collective-permute-start.12
  74.4 5.5 %collective-permute-done.10.refs_2_ = bf16[32,16,128]{2,1,0:T(8,128)(2,1)S(1)} collective-permute-done((bf16[32,16,128]{2,1,0:T(8,128)(2,1)}, bf16[32,16,128]{2,1,0:T(8,128)(2,1)S(1)}, u32[]{:S(2)}, u32[]{:S(2)}) %collective-permute-start.10) | collective-permute-done | bytes 131104 | tf_op jit(solution)/shard_map/ppermute | solution.py:376
  79.9 2.1 all-gather
  82.1 14.7 %spectra.8 = (bf16[32,32,128]{2,1,0:T(8,128)(2,1)}, bf16[32,32,128]{2,1,0:T(8,128)(2,1)}, bf16[32,32,128]{2,1,0:T(8,128)(2,1)}, bf16[32,32,128]{2,1,0:T(8,128)(2...) custom-call(s32[9]{0:T(128)} %pad_add_fusion.meta_ref, ...), custom_call_target="tpu_custom_call" | custom-call | flops 1024 | bytes 1024 | tf_op jit(solution)/shard_map/spectra/pallas_call | solution.py:271
  96.8 7.3 %shrink.6 = (bf16[32,16,128]{2,1,0:T(8,128)(2,1)}, bf16[32,16,128]{2,1,0:T(8,128)(2,1)}, bf16[32,16,128]{2,1,0:T(8,128)(2,1)}, bf16[32,16,128]{2,1,0:T(8,128)(2,...) custom-call(s32[9]{0:T(128)} %pad_add_fusion.meta_ref, ...), custom_call_target="tpu_custom_call" | custom-call | flops 1024 | bytes 1024 | tf_op jit(solution)/shard_map/shrink/pallas_call | solution.py:317
  104.3 2.3 collective-permute-start.23
  111.0 6.3 %collective-permute-done.22.refs_2_ = bf16[32,16,128]{2,1,0:T(8,128)(2,1)S(1)} collective-permute-done((bf16[32,16,128]{2,1,0:T(8,128)(2,1)}, bf16[32,16,128]{2,1,0:T(8,128)(2,1)S(1)}, u32[]{:S(2)}, u32[]{:S(2)}) %collective-permute-start.22) | collective-permute-done | bytes 131104 | tf_op jit(solution)/shard_map/ppermute | solution.py:376
  117.7 14.8 %collective-permute-done.23.refs_3_ = bf16[32,16,128]{2,1,0:T(8,128)(2,1)S(1)} collective-permute-done((bf16[32,16,128]{2,1,0:T(8,128)(2,1)}, bf16[32,16,128]{2,1,0:T(8,128)(2,1)S(1)}, u32[]{:S(2)}, u32[]{:S(2)}) %collective-permute-start.23) | collective-permute-done | bytes 131104 | tf_op jit(solution)/shard_map/ppermute | solution.py:376
  134.2 15.0 %spectra.9 = (bf16[32,32,128]{2,1,0:T(8,128)(2,1)}, bf16[32,32,128]{2,1,0:T(8,128)(2,1)}, bf16[32,32,128]{2,1,0:T(8,128)(2,1)}, bf16[32,32,128]{2,1,0:T(8,128)(2...) custom-call(s32[9]{0:T(128)} %pad_add_fusion.meta_ref, ...), custom_call_target="tpu_custom_call" | custom-call | flops 1024 | bytes 1024 | tf_op jit(solution)/shard_map/spectra/pallas_call | solution.py:271
  149.2 2.3 collective-permute-start.18
  155.0 2.4 collective-permute-start.28
  158.9 2.3 collective-permute-start.29
  161.2 4.8 collective-permute-done.19.refs_5_
  166.0 7.1 %collective-permute-start.30 = (bf16[32,32,128]{2,1,0:T(8,128)(2,1)}, bf16[32,32,128]{2,1,0:T(8,128)(2,1)S(1)}, u32[]{:S(2)}, u32[]{:S(2)}) collective-permute-start(bf16[32,32,128]{2,1,0:T(8,128)(2,1)} %get-tuple-element.164), channel_id=1, source_target_pairs={{0,2},{1,3},{2,0},{3,1},{4,6},{5,7},{6,4},{7,5},{8,10},{9,11},{10,... | collective-permute-start | bytes 786440 | tf_op jit(solution)/shard_map/ppermute | solution.py:376
  173.1 2.1 collective-permute-start.31
  175.4 2.7 collective-permute-start.32
  178.1 28.2 %collective-permute-done.28.refs_2_ = bf16[32,32,128]{2,1,0:T(8,128)(2,1)S(1)} collective-permute-done((bf16[32,32,128]{2,1,0:T(8,128)(2,1)}, bf16[32,32,128]{2,1,0:T(8,128)(2,1)S(1)}, u32[]{:S(2)}, u32[]{:S(2)}) %collective-permute-start.28) | collective-permute-done | bytes 262176 | tf_op jit(solution)/shard_map/ppermute | solution.py:376
  206.3 2.1 all-gather.1
  208.4 2.2 all-gather.3
  210.6 7.3 %shrink.7 = (bf16[32,16,128]{2,1,0:T(8,128)(2,1)}, bf16[32,16,128]{2,1,0:T(8,128)(2,1)}, bf16[32,16,128]{2,1,0:T(8,128)(2,1)}, bf16[32,16,128]{2,1,0:T(8,128)(2,...) custom-call(s32[9]{0:T(128)} %pad_add_fusion.meta_ref, ...), custom_call_target="tpu_custom_call" | custom-call | flops 1024 | bytes 1024 | tf_op jit(solution)/shard_map/shrink/pallas_call | solution.py:317
  217.9 2.4 collective-permute-start.34
  222.4 2.1 collective-permute-start.37
  225.8 2.6 all-gather.2
  228.4 10.0 %spectra.10 = (bf16[32,16,128]{2,1,0:T(8,128)(2,1)}, bf16[32,16,128]{2,1,0:T(8,128)(2,1)}, bf16[32,16,128]{2,1,0:T(8,128)(2,1)}, bf16[32,16,128]{2,1,0:T(8,128)(...) custom-call(s32[9]{0:T(128)} %pad_add_fusion.meta_ref, ...), custom_call_target="tpu_custom_call" | custom-call | flops 1024 | bytes 1024 | tf_op jit(solution)/shard_map/spectra/pallas_call | solution.py:271
  245.0 5.1 %all-gather.4 = bf16[64,32,128]{2,1,0:T(8,128)(2,1)} all-gather(bf16[32,32,128]{2,1,0:T(8,128)(2,1)} %get-tuple-element.161), channel_id=6, replica_groups={{0,1},{2,3},{4,5},{6,7},{8,9},{10,11},{12,13},{14,15},{16,17},{18,19},{..., dimensions={0}, use_global_device_ids=true | all-gather | bytes 786432 | tf_op jit(solution)/shard_map/all_gather | solution.py:375
  250.1 14.7 %shrink.8 = (bf16[32,32,128]{2,1,0:T(8,128)(2,1)}, bf16[32,32,128]{2,1,0:T(8,128)(2,1)}, bf16[32,32,128]{2,1,0:T(8,128)(2,1)}, bf16[32,32,128]{2,1,0:T(8,128)(2,...) custom-call(s32[9]{0:T(128)} %pad_add_fusion.meta_ref, ...), custom_call_target="tpu_custom_call" | custom-call | flops 1024 | bytes 1024 | tf_op jit(solution)/shard_map/shrink/pallas_call | solution.py:317
  265.8 3.2 update.6
  269.1 10.0 %spectra.11 = (bf16[32,16,128]{2,1,0:T(8,128)(2,1)}, bf16[32,16,128]{2,1,0:T(8,128)(2,1)}, bf16[32,16,128]{2,1,0:T(8,128)(2,1)}, bf16[32,16,128]{2,1,0:T(8,128)(...) custom-call(s32[9]{0:T(128)} %pad_add_fusion.meta_ref, ...), custom_call_target="tpu_custom_call" | custom-call | flops 1024 | bytes 1024 | tf_op jit(solution)/shard_map/spectra/pallas_call | solution.py:271
  279.1 2.2 collective-permute-start.44
  281.3 6.2 %collective-permute-start.45 = (bf16[32,16,128]{2,1,0:T(8,128)(2,1)}, bf16[32,16,128]{2,1,0:T(8,128)(2,1)}, u32[]{:S(2)}, u32[]{:S(2)}) collective-permute-start(bf16[32,16,128]{2,1,0:T(8,128)(2,1)} %get-tuple-element.185), channel_id=1, source_target_pairs={{0,3},{1,2},{2,1},{3,0},{4,7},{5,6},{6,5},{7,4},{8,11},{9,10},{10,... | collective-permute-start | bytes 393224 | tf_op jit(solution)/shard_map/ppermute | solution.py:376
  287.8 2.1 collective-permute-start.53
  292.2 2.3 all-gather.6
  294.5 14.6 %shrink.9 = (bf16[32,32,128]{2,1,0:T(8,128)(2,1)}, bf16[32,32,128]{2,1,0:T(8,128)(2,1)}, bf16[32,32,128]{2,1,0:T(8,128)(2,1)}, bf16[32,32,128]{2,1,0:T(8,128)(2,...) custom-call(s32[9]{0:T(128)} %pad_add_fusion.meta_ref, ...), custom_call_target="tpu_custom_call" | custom-call | flops 1024 | bytes 1024 | tf_op jit(solution)/shard_map/shrink/pallas_call | solution.py:317
  310.1 3.2 update.7
  316.9 7.3 %shrink.10 = (bf16[32,16,128]{2,1,0:T(8,128)(2,1)}, bf16[32,16,128]{2,1,0:T(8,128)(2,1)}, bf16[32,16,128]{2,1,0:T(8,128)(2,1)}, bf16[32,16,128]{2,1,0:T(8,128)(2...) custom-call(s32[9]{0:T(128)} %pad_add_fusion.meta_ref, ...), custom_call_target="tpu_custom_call" | custom-call | flops 1024 | bytes 1024 | tf_op jit(solution)/shard_map/shrink/pallas_call | solution.py:317
  324.3 2.3 collective-permute-start.64
  332.7 5.1 %collective-permute-done.64.refs_2_ = bf16[32,16,128]{2,1,0:T(8,128)(2,1)S(1)} collective-permute-done((bf16[32,16,128]{2,1,0:T(8,128)(2,1)}, bf16[32,16,128]{2,1,0:T(8,128)(2,1)S(1)}, u32[]{:S(2)}, u32[]{:S(2)}) %collective-permute-start.64) | collective-permute-done | bytes 131104 | tf_op jit(solution)/shard_map/ppermute | solution.py:376
  337.8 16.1 %collective-permute-done.65.refs_3_ = bf16[32,16,128]{2,1,0:T(8,128)(2,1)S(1)} collective-permute-done((bf16[32,16,128]{2,1,0:T(8,128)(2,1)}, bf16[32,16,128]{2,1,0:T(8,128)(2,1)S(1)}, u32[]{:S(2)}, u32[]{:S(2)}) %collective-permute-start.65) | collective-permute-done | bytes 131104 | tf_op jit(solution)/shard_map/ppermute | solution.py:376
  359.4 9.9 %psum.7 = f32[32]{0:T(128)S(1)} all-reduce(f32[32]{0:T(128)S(1)} %add_reduce_fusion), channel_id=1, replica_groups=mesh['patch'=4,'shot'=8] {'patch'}, use_global_device_ids=true, to_apply=%region_1.0 | all-reduce | flops 32 | bytes 256 | tf_op jit(solution)/shard_map/psum | solution.py:532
  372.0 13.1 %collective-permute-done.69.refs_7_ = bf16[32,16,128]{2,1,0:T(8,128)(2,1)S(1)} collective-permute-done((bf16[32,16,128]{2,1,0:T(8,128)(2,1)}, bf16[32,16,128]{2,1,0:T(8,128)(2,1)S(1)}, u32[]{:S(2)}, u32[]{:S(2)}) %collective-permute-start.69) | collective-permute-done | bytes 131104 | tf_op jit(solution)/shard_map/ppermute | solution.py:376
  387.9 2.8 collective-permute-start.58
  391.9 3.6 all-gather.8
  395.5 2.1 collective-permute-start.60
  397.6 2.2 collective-permute-start.61
  399.7 3.8 collective-permute-done.51.refs_7_
  403.5 2.5 collective-permute-start.62
  406.0 10.9 %collective-permute-done.58.refs_2_ = bf16[32,32,128]{2,1,0:T(8,128)(2,1)S(1)} collective-permute-done((bf16[32,32,128]{2,1,0:T(8,128)(2,1)}, bf16[32,32,128]{2,1,0:T(8,128)(2,1)S(1)}, u32[]{:S(2)}, u32[]{:S(2)}) %collective-permute-start.58) | collective-permute-done | bytes 262176 | tf_op jit(solution)/shard_map/ppermute | solution.py:376
  416.9 2.4 all-gather.7
  422.1 5.0 %update.8 = (f32[32,128,1024]{2,1,0:T(8,128)}, f32[8,128]{1,0:T(8,128)}) custom-call(s32[9]{0:T(128)S(1)} %copy-done.16, bf16[1024,1024]{1,0:T(8,128)(2,1)S(1)} %copy-done, bf16[32,16,128]{2,1,0:T(8,128)(2,1)S(1)} %copy-done.5, bf16[32,32,128]{2,1,0:T(8,128)(2,1)S(1)} %copy-done.4, ...), custom_call_target="tpu_custom_call", output_to_operand_aliasing={{0}: (11, {})} | custom-call | flops 1024 | bytes 1024 | tf_op jit(solution)/shard_map/update/pallas_call | solution.py:344
  427.2 7.2 %shrink.11 = (bf16[32,16,128]{2,1,0:T(8,128)(2,1)}, bf16[32,16,128]{2,1,0:T(8,128)(2,1)}, bf16[32,16,128]{2,1,0:T(8,128)(2,1)}, bf16[32,16,128]{2,1,0:T(8,128)(2...) custom-call(s32[9]{0:T(128)} %pad_add_fusion.meta_ref, ...), custom_call_target="tpu_custom_call" | custom-call | flops 1024 | bytes 1024 | tf_op jit(solution)/shard_map/shrink/pallas_call | solution.py:317
  436.2 2.4 all-gather.9
  444.6 14.5 %collective-permute-done.70.refs_2_ = bf16[32,16,128]{2,1,0:T(8,128)(2,1)S(1)} collective-permute-done((bf16[32,16,128]{2,1,0:T(8,128)(2,1)}, bf16[32,16,128]{2,1,0:T(8,128)(2,1)S(1)}, u32[]{:S(2)}, u32[]{:S(2)}) %collective-permute-start.70) | collective-permute-done | bytes 131104 | tf_op jit(solution)/shard_map/ppermute | solution.py:376
  459.1 2.2 all-gather.10
  462.2 6.2 %update.9 = (f32[32,128,1024]{2,1,0:T(8,128)}, f32[8,128]{1,0:T(8,128)}) custom-call(s32[9]{0:T(128)S(1)} %copy-done.17, bf16[1024,1024]{1,0:T(8,128)(2,1)S(1)} %copy-done, bf16[32,16,128]{2,1,0:T(8,128)(2,1)S(1)} %copy-done.8, bf16[32,32,128]{2,1,0:T(8,128)(2,1)S(1)} %copy-done.2, ...), custom_call_target="tpu_custom_call", output_to_operand_aliasing={{0}: (11, {})} | custom-call | flops 1024 | bytes 1024 | tf_op jit(solution)/shard_map/update/pallas_call | solution.py:344
  469.2 3.2 update.10
  475.1 3.2 update.11
  (290 shorter events, 80.8 us)
Async XLA Ops:
  24.4 19.8 %collective-permute-start.2 = (bf16[3,112,1024]{2,1,0:T(8,128)(2,1)S(1)}, bf16[3,112,1024]{2,1,0:T(8,128)(2,1)S(1)}, u32[]{:S(2)}, u32[]{:S(2)}) collective-permute-start(bf16[3,112,1024]{2,1,0:T(8,128)(2,1)S(1)} %pad_maximum_fusion), channel_id=1, source_target_pairs={{0,1},{1,2},{2,3},{3,4},{4,5},{5,6},{6,7},{8,9},{9,10},{10,11},{11... | collective-permute-start | bytes 2064392 | tf_op jit(solution)/shard_map/ppermute | solution.py:413
  30.2 25.2 %collective-permute-start.4 = (bf16[32,16,128]{2,1,0:T(8,128)(2,1)}, bf16[32,16,128]{2,1,0:T(8,128)(2,1)S(1)}, u32[]{:S(2)}, u32[]{:S(2)}) collective-permute-start(bf16[32,16,128]{2,1,0:T(8,128)(2,1)} %get-tuple-element.124), channel_id=1, source_target_pairs={{0,4},{1,5},{2,6},{3,7},{4,0},{5,1},{6,2},{7,3},{8,12},{9,13},{10,... | collective-permute-start | bytes 393224 | tf_op jit(solution)/shard_map/ppermute | solution.py:376
  32.8 35.3 %collective-permute-start.5 = (bf16[32,16,128]{2,1,0:T(8,128)(2,1)}, bf16[32,16,128]{2,1,0:T(8,128)(2,1)S(1)}, u32[]{:S(2)}, u32[]{:S(2)}) collective-permute-start(bf16[32,16,128]{2,1,0:T(8,128)(2,1)} %get-tuple-element.125), channel_id=1, source_target_pairs={{0,5},{1,4},{2,7},{3,6},{4,1},{5,0},{6,3},{7,2},{8,13},{9,12},{10,... | collective-permute-start | bytes 393224 | tf_op jit(solution)/shard_map/ppermute | solution.py:376
  34.2 34.6 %collective-permute-start.6 = (bf16[32,16,128]{2,1,0:T(8,128)(2,1)}, bf16[32,16,128]{2,1,0:T(8,128)(2,1)S(1)}, u32[]{:S(2)}, u32[]{:S(2)}) collective-permute-start(bf16[32,16,128]{2,1,0:T(8,128)(2,1)} %get-tuple-element.126), channel_id=1, source_target_pairs={{0,2},{1,3},{2,0},{3,1},{4,6},{5,7},{6,4},{7,5},{8,10},{9,11},{10,... | collective-permute-start | bytes 393224 | tf_op jit(solution)/shard_map/ppermute | solution.py:376
  35.8 33.0 %collective-permute-start.7 = (bf16[32,16,128]{2,1,0:T(8,128)(2,1)}, bf16[32,16,128]{2,1,0:T(8,128)(2,1)S(1)}, u32[]{:S(2)}, u32[]{:S(2)}) collective-permute-start(bf16[32,16,128]{2,1,0:T(8,128)(2,1)} %get-tuple-element.127), channel_id=1, source_target_pairs={{0,6},{1,7},{2,4},{3,5},{4,2},{5,3},{6,0},{7,1},{8,14},{9,15},{10,... | collective-permute-start | bytes 393224 | tf_op jit(solution)/shard_map/ppermute | solution.py:376
  44.2 26.7 %collective-permute-start.8 = (bf16[32,16,128]{2,1,0:T(8,128)(2,1)}, bf16[32,16,128]{2,1,0:T(8,128)(2,1)S(1)}, u32[]{:S(2)}, u32[]{:S(2)}) collective-permute-start(bf16[32,16,128]{2,1,0:T(8,128)(2,1)} %get-tuple-element.128), channel_id=1, source_target_pairs={{0,7},{1,6},{2,5},{3,4},{4,3},{5,2},{6,1},{7,0},{8,15},{9,14},{10,... | collective-permute-start | bytes 393224 | tf_op jit(solution)/shard_map/ppermute | solution.py:376
  55.4 17.2 %collective-permute-start.9 = (bf16[32,16,128]{2,1,0:T(8,128)(2,1)S(1)}, bf16[32,16,128]{2,1,0:T(8,128)(2,1)S(1)}, u32[]{:S(2)}, u32[]{:S(2)}) collective-permute-start(bf16[32,16,128]{2,1,0:T(8,128)(2,1)S(1)} %copy-done.77), channel_id=1, source_target_pairs={{0,3},{1,2},{2,1},{3,0},{4,7},{5,6},{6,5},{7,4},{8,11},{9,10},{10,... | collective-permute-start | bytes 393224 | tf_op jit(solution)/shard_map/ppermute | solution.py:376
  68.8 35.3 %collective-permute-start.11 = (bf16[32,16,128]{2,1,0:T(8,128)(2,1)}, bf16[32,16,128]{2,1,0:T(8,128)(2,1)S(1)}, u32[]{:S(2)}, u32[]{:S(2)}) collective-permute-start(bf16[32,16,128]{2,1,0:T(8,128)(2,1)} %get-tuple-element.135), channel_id=1, source_target_pairs={{0,5},{1,4},{2,7},{3,6},{4,1},{5,0},{6,3},{7,2},{8,13},{9,12},{10,... | collective-permute-start | bytes 393224 | tf_op jit(solution)/shard_map/ppermute | solution.py:376
  68.8 35.5 %collective-permute-start.12 = (bf16[32,16,128]{2,1,0:T(8,128)(2,1)}, bf16[32,16,128]{2,1,0:T(8,128)(2,1)S(1)}, u32[]{:S(2)}, u32[]{:S(2)}) collective-permute-start(bf16[32,16,128]{2,1,0:T(8,128)(2,1)} %get-tuple-element.136), channel_id=1, source_target_pairs={{0,2},{1,3},{2,0},{3,1},{4,6},{5,7},{6,4},{7,5},{8,10},{9,11},{10,... | collective-permute-start | bytes 393224 | tf_op jit(solution)/shard_map/ppermute | solution.py:376
  70.9 35.7 %collective-permute-start.13 = (bf16[32,16,128]{2,1,0:T(8,128)(2,1)}, bf16[32,16,128]{2,1,0:T(8,128)(2,1)S(1)}, u32[]{:S(2)}, u32[]{:S(2)}) collective-permute-start(bf16[32,16,128]{2,1,0:T(8,128)(2,1)} %get-tuple-element.137), channel_id=1, source_target_pairs={{0,6},{1,7},{2,4},{3,5},{4,2},{5,3},{6,0},{7,1},{8,14},{9,15},{10,... | collective-permute-start | bytes 393224 | tf_op jit(solution)/shard_map/ppermute | solution.py:376
  72.6 35.9 %collective-permute-start.14 = (bf16[32,16,128]{2,1,0:T(8,128)(2,1)}, bf16[32,16,128]{2,1,0:T(8,128)(2,1)S(1)}, u32[]{:S(2)}, u32[]{:S(2)}) collective-permute-start(bf16[32,16,128]{2,1,0:T(8,128)(2,1)} %get-tuple-element.138), channel_id=1, source_target_pairs={{0,7},{1,6},{2,5},{3,4},{4,3},{5,2},{6,1},{7,0},{8,15},{9,14},{10,... | collective-permute-start | bytes 393224 | tf_op jit(solution)/shard_map/ppermute | solution.py:376
  79.9 29.1 %collective-permute-start.15 = (bf16[32,16,128]{2,1,0:T(8,128)(2,1)}, bf16[32,16,128]{2,1,0:T(8,128)(2,1)S(1)}, u32[]{:S(2)}, u32[]{:S(2)}) collective-permute-start(bf16[32,16,128]{2,1,0:T(8,128)(2,1)} %get-tuple-element.139), channel_id=1, source_target_pairs={{0,3},{1,2},{2,1},{3,0},{4,7},{5,6},{6,5},{7,4},{8,11},{9,10},{10,... | collective-permute-start | bytes 393224 | tf_op jit(solution)/shard_map/ppermute | solution.py:376
  104.3 28.3 %collective-permute-start.23 = (bf16[32,16,128]{2,1,0:T(8,128)(2,1)}, bf16[32,16,128]{2,1,0:T(8,128)(2,1)S(1)}, u32[]{:S(2)}, u32[]{:S(2)}) collective-permute-start(bf16[32,16,128]{2,1,0:T(8,128)(2,1)} %get-tuple-element.153), channel_id=1, source_target_pairs={{0,5},{1,4},{2,7},{3,6},{4,1},{5,0},{6,3},{7,2},{8,13},{9,12},{10,... | collective-permute-start | bytes 393224 | tf_op jit(solution)/shard_map/ppermute | solution.py:376
  106.6 27.6 %collective-permute-start.24 = (bf16[32,16,128]{2,1,0:T(8,128)(2,1)}, bf16[32,16,128]{2,1,0:T(8,128)(2,1)S(1)}, u32[]{:S(2)}, u32[]{:S(2)}) collective-permute-start(bf16[32,16,128]{2,1,0:T(8,128)(2,1)} %get-tuple-element.154), channel_id=1, source_target_pairs={{0,2},{1,3},{2,0},{3,1},{4,6},{5,7},{6,4},{7,5},{8,10},{9,11},{10,... | collective-permute-start | bytes 393224 | tf_op jit(solution)/shard_map/ppermute | solution.py:376
  108.6 45.7 %collective-permute-start.16 = (bf16[32,32,128]{2,1,0:T(8,128)(2,1)}, bf16[32,32,128]{2,1,0:T(8,128)(2,1)S(1)}, u32[]{:S(2)}, u32[]{:S(2)}) collective-permute-start(bf16[32,32,128]{2,1,0:T(8,128)(2,1)} %get-tuple-element.144), channel_id=1, source_target_pairs={{0,4},{1,5},{2,6},{3,7},{4,0},{5,1},{6,2},{7,3},{8,12},{9,13},{10,... | collective-permute-start | bytes 786440 | tf_op jit(solution)/shard_map/ppermute | solution.py:376
  109.0 45.6 %collective-permute-start.17 = (bf16[32,32,128]{2,1,0:T(8,128)(2,1)}, bf16[32,32,128]{2,1,0:T(8,128)(2,1)S(1)}, u32[]{:S(2)}, u32[]{:S(2)}) collective-permute-start(bf16[32,32,128]{2,1,0:T(8,128)(2,1)} %get-tuple-element.145), channel_id=1, source_target_pairs={{0,5},{1,4},{2,7},{3,6},{4,1},{5,0},{6,3},{7,2},{8,13},{9,12},{10,... | collective-permute-start | bytes 786440 | tf_op jit(solution)/shard_map/ppermute | solution.py:376
  117.2 32.0 %collective-permute-start.25 = (bf16[32,16,128]{2,1,0:T(8,128)(2,1)}, bf16[32,16,128]{2,1,0:T(8,128)(2,1)S(1)}, u32[]{:S(2)}, u32[]{:S(2)}) collective-permute-start(bf16[32,16,128]{2,1,0:T(8,128)(2,1)} %get-tuple-element.155), channel_id=1, source_target_pairs={{0,6},{1,7},{2,4},{3,5},{4,2},{5,3},{6,0},{7,1},{8,14},{9,15},{10,... | collective-permute-start | bytes 393224 | tf_op jit(solution)/shard_map/ppermute | solution.py:376
  132.5 19.0 %collective-permute-start.26 = (bf16[32,16,128]{2,1,0:T(8,128)(2,1)}, bf16[32,16,128]{2,1,0:T(8,128)(2,1)S(1)}, u32[]{:S(2)}, u32[]{:S(2)}) collective-permute-start(bf16[32,16,128]{2,1,0:T(8,128)(2,1)} %get-tuple-element.156), channel_id=1, source_target_pairs={{0,7},{1,6},{2,5},{3,4},{4,3},{5,2},{6,1},{7,0},{8,15},{9,14},{10,... | collective-permute-start | bytes 393224 | tf_op jit(solution)/shard_map/ppermute | solution.py:376
  134.2 19.0 %collective-permute-start.27 = (bf16[32,16,128]{2,1,0:T(8,128)(2,1)}, bf16[32,16,128]{2,1,0:T(8,128)(2,1)S(1)}, u32[]{:S(2)}, u32[]{:S(2)}) collective-permute-start(bf16[32,16,128]{2,1,0:T(8,128)(2,1)} %get-tuple-element.157), channel_id=1, source_target_pairs={{0,3},{1,2},{2,1},{3,0},{4,7},{5,6},{6,5},{7,4},{8,11},{9,10},{10,... | collective-permute-start | bytes 393224 | tf_op jit(solution)/shard_map/ppermute | solution.py:376
  151.6 14.4 %collective-permute-start.19 = (bf16[32,32,128]{2,1,0:T(8,128)(2,1)S(1)}, bf16[32,32,128]{2,1,0:T(8,128)(2,1)S(1)}, u32[]{:S(2)}, u32[]{:S(2)}) collective-permute-start(bf16[32,32,128]{2,1,0:T(8,128)(2,1)S(1)} %copy-done.76), channel_id=1, source_target_pairs={{0,6},{1,7},{2,4},{3,5},{4,2},{5,3},{6,0},{7,1},{8,14},{9,15},{10,... | collective-permute-start | bytes 786440 | tf_op jit(solution)/shard_map/ppermute | solution.py:376
  153.2 19.9 %collective-permute-start.20 = (bf16[32,32,128]{2,1,0:T(8,128)(2,1)}, bf16[32,32,128]{2,1,0:T(8,128)(2,1)S(1)}, u32[]{:S(2)}, u32[]{:S(2)}) collective-permute-start(bf16[32,32,128]{2,1,0:T(8,128)(2,1)} %get-tuple-element.148), channel_id=1, source_target_pairs={{0,7},{1,6},{2,5},{3,4},{4,3},{5,2},{6,1},{7,0},{8,15},{9,14},{10,... | collective-permute-start | bytes 786440 | tf_op jit(solution)/shard_map/ppermute | solution.py:376
  154.3 21.1 %collective-permute-start.21 = (bf16[32,32,128]{2,1,0:T(8,128)(2,1)S(1)}, bf16[32,32,128]{2,1,0:T(8,128)(2,1)S(1)}, u32[]{:S(2)}, u32[]{:S(2)}) collective-permute-start(bf16[32,32,128]{2,1,0:T(8,128)(2,1)S(1)} %copy-done.75), channel_id=1, source_target_pairs={{0,3},{1,2},{2,1},{3,0},{4,7},{5,6},{6,5},{7,4},{8,11},{9,10},{10,... | collective-permute-start | bytes 786440 | tf_op jit(solution)/shard_map/ppermute | solution.py:376
  155.0 51.2 %collective-permute-start.28 = (bf16[32,32,128]{2,1,0:T(8,128)(2,1)}, bf16[32,32,128]{2,1,0:T(8,128)(2,1)S(1)}, u32[]{:S(2)}, u32[]{:S(2)}) collective-permute-start(bf16[32,32,128]{2,1,0:T(8,128)(2,1)} %get-tuple-element.162), channel_id=1, source_target_pairs={{0,4},{1,5},{2,6},{3,7},{4,0},{5,1},{6,2},{7,3},{8,12},{9,13},{10,... | collective-permute-start | bytes 786440 | tf_op jit(solution)/shard_map/ppermute | solution.py:376
  158.9 58.9 %collective-permute-start.29 = (bf16[32,32,128]{2,1,0:T(8,128)(2,1)}, bf16[32,32,128]{2,1,0:T(8,128)(2,1)S(1)}, u32[]{:S(2)}, u32[]{:S(2)}) collective-permute-start(bf16[32,32,128]{2,1,0:T(8,128)(2,1)} %get-tuple-element.163), channel_id=1, source_target_pairs={{0,5},{1,4},{2,7},{3,6},{4,1},{5,0},{6,3},{7,2},{8,13},{9,12},{10,... | collective-permute-start | bytes 786440 | tf_op jit(solution)/shard_map/ppermute | solution.py:376
  166.0 54.3 %collective-permute-start.30 = (bf16[32,32,128]{2,1,0:T(8,128)(2,1)}, bf16[32,32,128]{2,1,0:T(8,128)(2,1)S(1)}, u32[]{:S(2)}, u32[]{:S(2)}) collective-permute-start(bf16[32,32,128]{2,1,0:T(8,128)(2,1)} %get-tuple-element.164), channel_id=1, source_target_pairs={{0,2},{1,3},{2,0},{3,1},{4,6},{5,7},{6,4},{7,5},{8,10},{9,11},{10,... | collective-permute-start | bytes 786440 | tf_op jit(solution)/shard_map/ppermute | solution.py:376
  173.1 47.3 %collective-permute-start.31 = (bf16[32,32,128]{2,1,0:T(8,128)(2,1)}, bf16[32,32,128]{2,1,0:T(8,128)(2,1)S(1)}, u32[]{:S(2)}, u32[]{:S(2)}) collective-permute-start(bf16[32,32,128]{2,1,0:T(8,128)(2,1)} %get-tuple-element.165), channel_id=1, source_target_pairs={{0,6},{1,7},{2,4},{3,5},{4,2},{5,3},{6,0},{7,1},{8,14},{9,15},{10,... | collective-permute-start | bytes 786440 | tf_op jit(solution)/shard_map/ppermute | solution.py:376
  175.4 47.0 %collective-permute-start.32 = (bf16[32,32,128]{2,1,0:T(8,128)(2,1)}, bf16[32,32,128]{2,1,0:T(8,128)(2,1)S(1)}, u32[]{:S(2)}, u32[]{:S(2)}) collective-permute-start(bf16[32,32,128]{2,1,0:T(8,128)(2,1)} %get-tuple-element.166), channel_id=1, source_target_pairs={{0,7},{1,6},{2,5},{3,4},{4,3},{5,2},{6,1},{7,0},{8,15},{9,14},{10,... | collective-permute-start | bytes 786440 | tf_op jit(solution)/shard_map/ppermute | solution.py:376
  206.3 18.2 %collective-permute-start.33 = (bf16[32,32,128]{2,1,0:T(8,128)(2,1)}, bf16[32,32,128]{2,1,0:T(8,128)(2,1)S(1)}, u32[]{:S(2)}, u32[]{:S(2)}) collective-permute-start(bf16[32,32,128]{2,1,0:T(8,128)(2,1)} %get-tuple-element.167), channel_id=1, source_target_pairs={{0,3},{1,2},{2,1},{3,0},{4,7},{5,6},{6,5},{7,4},{8,11},{9,10},{10,... | collective-permute-start | bytes 786440 | tf_op jit(solution)/shard_map/ppermute | solution.py:376
  217.9 20.6 %collective-permute-start.34 = (bf16[32,16,128]{2,1,0:T(8,128)(2,1)}, bf16[32,16,128]{2,1,0:T(8,128)(2,1)S(1)}, u32[]{:S(2)}, u32[]{:S(2)}) collective-permute-start(bf16[32,16,128]{2,1,0:T(8,128)(2,1)} %get-tuple-element.170), channel_id=1, source_target_pairs={{0,4},{1,5},{2,6},{3,7},{4,0},{5,1},{6,2},{7,3},{8,12},{9,13},{10,... | collective-permute-start | bytes 393224 | tf_op jit(solution)/shard_map/ppermute | solution.py:376
  220.3 19.2 %collective-permute-start.35 = (bf16[32,16,128]{2,1,0:T(8,128)(2,1)}, bf16[32,16,128]{2,1,0:T(8,128)(2,1)S(1)}, u32[]{:S(2)}, u32[]{:S(2)}) collective-permute-start(bf16[32,16,128]{2,1,0:T(8,128)(2,1)} %get-tuple-element.171), channel_id=1, source_target_pairs={{0,5},{1,4},{2,7},{3,6},{4,1},{5,0},{6,3},{7,2},{8,13},{9,12},{10,... | collective-permute-start | bytes 393224 | tf_op jit(solution)/shard_map/ppermute | solution.py:376
  220.4 20.6 %collective-permute-start.36 = (bf16[32,16,128]{2,1,0:T(8,128)(2,1)}, bf16[32,16,128]{2,1,0:T(8,128)(2,1)S(1)}, u32[]{:S(2)}, u32[]{:S(2)}) collective-permute-start(bf16[32,16,128]{2,1,0:T(8,128)(2,1)} %get-tuple-element.172), channel_id=1, source_target_pairs={{0,2},{1,3},{2,0},{3,1},{4,6},{5,7},{6,4},{7,5},{8,10},{9,11},{10,... | collective-permute-start | bytes 393224 | tf_op jit(solution)/shard_map/ppermute | solution.py:376
  222.4 19.7 %collective-permute-start.37 = (bf16[32,16,128]{2,1,0:T(8,128)(2,1)}, bf16[32,16,128]{2,1,0:T(8,128)(2,1)S(1)}, u32[]{:S(2)}, u32[]{:S(2)}) collective-permute-start(bf16[32,16,128]{2,1,0:T(8,128)(2,1)} %get-tuple-element.173), channel_id=1, source_target_pairs={{0,6},{1,7},{2,4},{3,5},{4,2},{5,3},{6,0},{7,1},{8,14},{9,15},{10,... | collective-permute-start | bytes 393224 | tf_op jit(solution)/shard_map/ppermute | solution.py:376
  224.5 18.9 %collective-permute-start.38 = (bf16[32,16,128]{2,1,0:T(8,128)(2,1)}, bf16[32,16,128]{2,1,0:T(8,128)(2,1)S(1)}, u32[]{:S(2)}, u32[]{:S(2)}) collective-permute-start(bf16[32,16,128]{2,1,0:T(8,128)(2,1)} %get-tuple-element.174), channel_id=1, source_target_pairs={{0,7},{1,6},{2,5},{3,4},{4,3},{5,2},{6,1},{7,0},{8,15},{9,14},{10,... | collective-permute-start | bytes 393224 | tf_op jit(solution)/shard_map/ppermute | solution.py:376
  238.4 40.7 %collective-permute-start.39 = (bf16[32,16,128]{2,1,0:T(8,128)(2,1)}, bf16[32,16,128]{2,1,0:T(8,128)(2,1)S(1)}, u32[]{:S(2)}, u32[]{:S(2)}) collective-permute-start(bf16[32,16,128]{2,1,0:T(8,128)(2,1)} %get-tuple-element.175), channel_id=1, source_target_pairs={{0,3},{1,2},{2,1},{3,0},{4,7},{5,6},{6,5},{7,4},{8,11},{9,10},{10,... | collective-permute-start | bytes 393224 | tf_op jit(solution)/shard_map/ppermute | solution.py:376
  239.5 41.8 %collective-permute-start.40 = (bf16[32,16,128]{2,1,0:T(8,128)(2,1)}, bf16[32,16,128]{2,1,0:T(8,128)(2,1)}, u32[]{:S(2)}, u32[]{:S(2)}) collective-permute-start(bf16[32,16,128]{2,1,0:T(8,128)(2,1)} %get-tuple-element.180), channel_id=1, source_target_pairs={{0,4},{1,5},{2,6},{3,7},{4,0},{5,1},{6,2},{7,3},{8,12},{9,13},{10,... | collective-permute-start | bytes 393224 | tf_op jit(solution)/shard_map/ppermute | solution.py:376
  241.0 46.4 %collective-permute-start.41 = (bf16[32,16,128]{2,1,0:T(8,128)(2,1)}, bf16[32,16,128]{2,1,0:T(8,128)(2,1)}, u32[]{:S(2)}, u32[]{:S(2)}) collective-permute-start(bf16[32,16,128]{2,1,0:T(8,128)(2,1)} %get-tuple-element.181), channel_id=1, source_target_pairs={{0,5},{1,4},{2,7},{3,6},{4,1},{5,0},{6,3},{7,2},{8,13},{9,12},{10,... | collective-permute-start | bytes 393224 | tf_op jit(solution)/shard_map/ppermute | solution.py:376
  242.1 45.7 %collective-permute-start.42 = (bf16[32,16,128]{2,1,0:T(8,128)(2,1)}, bf16[32,16,128]{2,1,0:T(8,128)(2,1)}, u32[]{:S(2)}, u32[]{:S(2)}) collective-permute-start(bf16[32,16,128]{2,1,0:T(8,128)(2,1)} %get-tuple-element.182), channel_id=1, source_target_pairs={{0,2},{1,3},{2,0},{3,1},{4,6},{5,7},{6,4},{7,5},{8,10},{9,11},{10,... | collective-permute-start | bytes 393224 | tf_op jit(solution)/shard_map/ppermute | solution.py:376
  243.4 46.5 %collective-permute-start.43 = (bf16[32,16,128]{2,1,0:T(8,128)(2,1)}, bf16[32,16,128]{2,1,0:T(8,128)(2,1)}, u32[]{:S(2)}, u32[]{:S(2)}) collective-permute-start(bf16[32,16,128]{2,1,0:T(8,128)(2,1)} %get-tuple-element.183), channel_id=1, source_target_pairs={{0,6},{1,7},{2,4},{3,5},{4,2},{5,3},{6,0},{7,1},{8,14},{9,15},{10,... | collective-permute-start | bytes 393224 | tf_op jit(solution)/shard_map/ppermute | solution.py:376
  279.1 34.3 %collective-permute-start.44 = (bf16[32,16,128]{2,1,0:T(8,128)(2,1)}, bf16[32,16,128]{2,1,0:T(8,128)(2,1)S(1)}, u32[]{:S(2)}, u32[]{:S(2)}) collective-permute-start(bf16[32,16,128]{2,1,0:T(8,128)(2,1)} %get-tuple-element.184), channel_id=1, source_target_pairs={{0,7},{1,6},{2,5},{3,4},{4,3},{5,2},{6,1},{7,0},{8,15},{9,14},{10,... | collective-permute-start | bytes 393224 | tf_op jit(solution)/shard_map/ppermute | solution.py:376
  281.3 33.9 %collective-permute-start.45 = (bf16[32,16,128]{2,1,0:T(8,128)(2,1)}, bf16[32,16,128]{2,1,0:T(8,128)(2,1)}, u32[]{:S(2)}, u32[]{:S(2)}) collective-permute-start(bf16[32,16,128]{2,1,0:T(8,128)(2,1)} %get-tuple-element.185), channel_id=1, source_target_pairs={{0,3},{1,2},{2,1},{3,0},{4,7},{5,6},{6,5},{7,4},{8,11},{9,10},{10,... | collective-permute-start | bytes 393224 | tf_op jit(solution)/shard_map/ppermute | solution.py:376
  287.4 36.8 %collective-permute-start.52 = (bf16[32,16,128]{2,1,0:T(8,128)(2,1)}, bf16[32,16,128]{2,1,0:T(8,128)(2,1)S(1)}, u32[]{:S(2)}, u32[]{:S(2)}) collective-permute-start(bf16[32,16,128]{2,1,0:T(8,128)(2,1)} %get-tuple-element.198), channel_id=1, source_target_pairs={{0,4},{1,5},{2,6},{3,7},{4,0},{5,1},{6,2},{7,3},{8,12},{9,13},{10,... | collective-permute-start | bytes 393224 | tf_op jit(solution)/shard_map/ppermute | solution.py:376
  287.8 36.5 %collective-permute-start.53 = (bf16[32,16,128]{2,1,0:T(8,128)(2,1)}, bf16[32,16,128]{2,1,0:T(8,128)(2,1)S(1)}, u32[]{:S(2)}, u32[]{:S(2)}) collective-permute-start(bf16[32,16,128]{2,1,0:T(8,128)(2,1)} %get-tuple-element.199), channel_id=1, source_target_pairs={{0,5},{1,4},{2,7},{3,6},{4,1},{5,0},{6,3},{7,2},{8,13},{9,12},{10,... | collective-permute-start | bytes 393224 | tf_op jit(solution)/shard_map/ppermute | solution.py:376
  289.9 36.8 %collective-permute-start.54 = (bf16[32,16,128]{2,1,0:T(8,128)(2,1)}, bf16[32,16,128]{2,1,0:T(8,128)(2,1)S(1)}, u32[]{:S(2)}, u32[]{:S(2)}) collective-permute-start(bf16[32,16,128]{2,1,0:T(8,128)(2,1)} %get-tuple-element.200), channel_id=1, source_target_pairs={{0,2},{1,3},{2,0},{3,1},{4,6},{5,7},{6,4},{7,5},{8,10},{9,11},{10,... | collective-permute-start | bytes 393224 | tf_op jit(solution)/shard_map/ppermute | solution.py:376
  326.7 27.2 %collective-permute-start.65 = (bf16[32,16,128]{2,1,0:T(8,128)(2,1)}, bf16[32,16,128]{2,1,0:T(8,128)(2,1)S(1)}, u32[]{:S(2)}, u32[]{:S(2)}) collective-permute-start(bf16[32,16,128]{2,1,0:T(8,128)(2,1)} %get-tuple-element.216), channel_id=1, source_target_pairs={{0,5},{1,4},{2,7},{3,6},{4,1},{5,0},{6,3},{7,2},{8,13},{9,12},{10,... | collective-permute-start | bytes 393224 | tf_op jit(solution)/shard_map/ppermute | solution.py:376
  327.1 27.4 %collective-permute-start.66 = (bf16[32,16,128]{2,1,0:T(8,128)(2,1)}, bf16[32,16,128]{2,1,0:T(8,128)(2,1)S(1)}, u32[]{:S(2)}, u32[]{:S(2)}) collective-permute-start(bf16[32,16,128]{2,1,0:T(8,128)(2,1)} %get-tuple-element.217), channel_id=1, source_target_pairs={{0,2},{1,3},{2,0},{3,1},{4,6},{5,7},{6,4},{7,5},{8,10},{9,11},{10,... | collective-permute-start | bytes 393224 | tf_op jit(solution)/shard_map/ppermute | solution.py:376
  328.8 28.2 %collective-permute-start.67 = (bf16[32,16,128]{2,1,0:T(8,128)(2,1)}, bf16[32,16,128]{2,1,0:T(8,128)(2,1)S(1)}, u32[]{:S(2)}, u32[]{:S(2)}) collective-permute-start(bf16[32,16,128]{2,1,0:T(8,128)(2,1)} %get-tuple-element.218), channel_id=1, source_target_pairs={{0,6},{1,7},{2,4},{3,5},{4,2},{5,3},{6,0},{7,1},{8,14},{9,15},{10,... | collective-permute-start | bytes 393224 | tf_op jit(solution)/shard_map/ppermute | solution.py:376
  331.2 55.9 %collective-permute-start.46 = (bf16[32,32,128]{2,1,0:T(8,128)(2,1)}, bf16[32,32,128]{2,1,0:T(8,128)(2,1)S(1)}, u32[]{:S(2)}, u32[]{:S(2)}) collective-permute-start(bf16[32,32,128]{2,1,0:T(8,128)(2,1)} %get-tuple-element.188), channel_id=1, source_target_pairs={{0,4},{1,5},{2,6},{3,7},{4,0},{5,1},{6,2},{7,3},{8,12},{9,13},{10,... | collective-permute-start | bytes 786440 | tf_op jit(solution)/shard_map/ppermute | solution.py:376
  337.8 49.4 %collective-permute-start.47 = (bf16[32,32,128]{2,1,0:T(8,128)(2,1)}, bf16[32,32,128]{2,1,0:T(8,128)(2,1)S(1)}, u32[]{:S(2)}, u32[]{:S(2)}) collective-permute-start(bf16[32,32,128]{2,1,0:T(8,128)(2,1)} %get-tuple-element.189), channel_id=1, source_target_pairs={{0,5},{1,4},{2,7},{3,6},{4,1},{5,0},{6,3},{7,2},{8,13},{9,12},{10,... | collective-permute-start | bytes 786440 | tf_op jit(solution)/shard_map/ppermute | solution.py:376
  354.5 36.1 %collective-permute-start.48 = (bf16[32,32,128]{2,1,0:T(8,128)(2,1)}, bf16[32,32,128]{2,1,0:T(8,128)(2,1)S(1)}, u32[]{:S(2)}, u32[]{:S(2)}) collective-permute-start(bf16[32,32,128]{2,1,0:T(8,128)(2,1)} %get-tuple-element.190), channel_id=1, source_target_pairs={{0,2},{1,3},{2,0},{3,1},{4,6},{5,7},{6,4},{7,5},{8,10},{9,11},{10,... | collective-permute-start | bytes 786440 | tf_op jit(solution)/shard_map/ppermute | solution.py:376
  357.6 27.5 %collective-permute-start.69 = (bf16[32,16,128]{2,1,0:T(8,128)(2,1)}, bf16[32,16,128]{2,1,0:T(8,128)(2,1)S(1)}, u32[]{:S(2)}, u32[]{:S(2)}) collective-permute-start(bf16[32,16,128]{2,1,0:T(8,128)(2,1)} %get-tuple-element.220), channel_id=1, source_target_pairs={{0,3},{1,2},{2,1},{3,0},{4,7},{5,6},{6,5},{7,4},{8,11},{9,10},{10,... | collective-permute-start | bytes 393224 | tf_op jit(solution)/shard_map/ppermute | solution.py:376
  370.0 25.5 %collective-permute-start.49 = (bf16[32,32,128]{2,1,0:T(8,128)(2,1)}, bf16[32,32,128]{2,1,0:T(8,128)(2,1)S(1)}, u32[]{:S(2)}, u32[]{:S(2)}) collective-permute-start(bf16[32,32,128]{2,1,0:T(8,128)(2,1)} %get-tuple-element.191), channel_id=1, source_target_pairs={{0,6},{1,7},{2,4},{3,5},{4,2},{5,3},{6,0},{7,1},{8,14},{9,15},{10,... | collective-permute-start | bytes 786440 | tf_op jit(solution)/shard_map/ppermute | solution.py:376
  387.2 16.4 %collective-permute-start.51 = (bf16[32,32,128]{2,1,0:T(8,128)(2,1)}, bf16[32,32,128]{2,1,0:T(8,128)(2,1)S(1)}, u32[]{:S(2)}, u32[]{:S(2)}) collective-permute-start(bf16[32,32,128]{2,1,0:T(8,128)(2,1)} %get-tuple-element.193), channel_id=1, source_target_pairs={{0,3},{1,2},{2,1},{3,0},{4,7},{5,6},{6,5},{7,4},{8,11},{9,10},{10,... | collective-permute-start | bytes 786440 | tf_op jit(solution)/shard_map/ppermute | solution.py:376
  387.9 29.0 %collective-permute-start.58 = (bf16[32,32,128]{2,1,0:T(8,128)(2,1)}, bf16[32,32,128]{2,1,0:T(8,128)(2,1)S(1)}, u32[]{:S(2)}, u32[]{:S(2)}) collective-permute-start(bf16[32,32,128]{2,1,0:T(8,128)(2,1)} %get-tuple-element.206), channel_id=1, source_target_pairs={{0,4},{1,5},{2,6},{3,7},{4,0},{5,1},{6,2},{7,3},{8,12},{9,13},{10,... | collective-permute-start | bytes 786440 | tf_op jit(solution)/shard_map/ppermute | solution.py:376
  391.4 43.0 %collective-permute-start.59 = (bf16[32,32,128]{2,1,0:T(8,128)(2,1)}, bf16[32,32,128]{2,1,0:T(8,128)(2,1)S(1)}, u32[]{:S(2)}, u32[]{:S(2)}) collective-permute-start(bf16[32,32,128]{2,1,0:T(8,128)(2,1)} %get-tuple-element.207), channel_id=1, source_target_pairs={{0,5},{1,4},{2,7},{3,6},{4,1},{5,0},{6,3},{7,2},{8,13},{9,12},{10,... | collective-permute-start | bytes 786440 | tf_op jit(solution)/shard_map/ppermute | solution.py:376
  395.5 43.1 %collective-permute-start.60 = (bf16[32,32,128]{2,1,0:T(8,128)(2,1)}, bf16[32,32,128]{2,1,0:T(8,128)(2,1)S(1)}, u32[]{:S(2)}, u32[]{:S(2)}) collective-permute-start(bf16[32,32,128]{2,1,0:T(8,128)(2,1)} %get-tuple-element.208), channel_id=1, source_target_pairs={{0,2},{1,3},{2,0},{3,1},{4,6},{5,7},{6,4},{7,5},{8,10},{9,11},{10,... | collective-permute-start | bytes 786440 | tf_op jit(solution)/shard_map/ppermute | solution.py:376
  397.6 42.0 %collective-permute-start.61 = (bf16[32,32,128]{2,1,0:T(8,128)(2,1)}, bf16[32,32,128]{2,1,0:T(8,128)(2,1)}, u32[]{:S(2)}, u32[]{:S(2)}) collective-permute-start(bf16[32,32,128]{2,1,0:T(8,128)(2,1)} %get-tuple-element.209), channel_id=1, source_target_pairs={{0,6},{1,7},{2,4},{3,5},{4,2},{5,3},{6,0},{7,1},{8,14},{9,15},{10,... | collective-permute-start | bytes 786440 | tf_op jit(solution)/shard_map/ppermute | solution.py:376
  403.5 37.8 %collective-permute-start.62 = (bf16[32,32,128]{2,1,0:T(8,128)(2,1)}, bf16[32,32,128]{2,1,0:T(8,128)(2,1)}, u32[]{:S(2)}, u32[]{:S(2)}) collective-permute-start(bf16[32,32,128]{2,1,0:T(8,128)(2,1)} %get-tuple-element.210), channel_id=1, source_target_pairs={{0,7},{1,6},{2,5},{3,4},{4,3},{5,2},{6,1},{7,0},{8,15},{9,14},{10,... | collective-permute-start | bytes 786440 | tf_op jit(solution)/shard_map/ppermute | solution.py:376
  416.9 25.8 %collective-permute-start.63 = (bf16[32,32,128]{2,1,0:T(8,128)(2,1)}, bf16[32,32,128]{2,1,0:T(8,128)(2,1)}, u32[]{:S(2)}, u32[]{:S(2)}) collective-permute-start(bf16[32,32,128]{2,1,0:T(8,128)(2,1)} %get-tuple-element.211), channel_id=1, source_target_pairs={{0,3},{1,2},{2,1},{3,0},{4,7},{5,6},{6,5},{7,4},{8,11},{9,10},{10,... | collective-permute-start | bytes 786440 | tf_op jit(solution)/shard_map/ppermute | solution.py:376
  434.4 24.7 %collective-permute-start.70 = (bf16[32,16,128]{2,1,0:T(8,128)(2,1)}, bf16[32,16,128]{2,1,0:T(8,128)(2,1)S(1)}, u32[]{:S(2)}, u32[]{:S(2)}) collective-permute-start(bf16[32,16,128]{2,1,0:T(8,128)(2,1)} %get-tuple-element.224), channel_id=1, source_target_pairs={{0,4},{1,5},{2,6},{3,7},{4,0},{5,1},{6,2},{7,3},{8,12},{9,13},{10,... | collective-permute-start | bytes 393224 | tf_op jit(solution)/shard_map/ppermute | solution.py:376
  438.6 35.8 %collective-permute-start.71 = (bf16[32,16,128]{2,1,0:T(8,128)(2,1)}, bf16[32,16,128]{2,1,0:T(8,128)(2,1)S(1)}, u32[]{:S(2)}, u32[]{:S(2)}) collective-permute-start(bf16[32,16,128]{2,1,0:T(8,128)(2,1)} %get-tuple-element.225), channel_id=1, source_target_pairs={{0,5},{1,4},{2,7},{3,6},{4,1},{5,0},{6,3},{7,2},{8,13},{9,12},{10,... | collective-permute-start | bytes 393224 | tf_op jit(solution)/shard_map/ppermute | solution.py:376
  439.5 34.9 %collective-permute-start.72 = (bf16[32,16,128]{2,1,0:T(8,128)(2,1)}, bf16[32,16,128]{2,1,0:T(8,128)(2,1)S(1)}, u32[]{:S(2)}, u32[]{:S(2)}) collective-permute-start(bf16[32,16,128]{2,1,0:T(8,128)(2,1)} %get-tuple-element.226), channel_id=1, source_target_pairs={{0,2},{1,3},{2,0},{3,1},{4,6},{5,7},{6,4},{7,5},{8,10},{9,11},{10,... | collective-permute-start | bytes 393224 | tf_op jit(solution)/shard_map/ppermute | solution.py:376
  441.3 33.1 %collective-permute-start.73 = (bf16[32,16,128]{2,1,0:T(8,128)(2,1)}, bf16[32,16,128]{2,1,0:T(8,128)(2,1)S(1)}, u32[]{:S(2)}, u32[]{:S(2)}) collective-permute-start(bf16[32,16,128]{2,1,0:T(8,128)(2,1)} %get-tuple-element.227), channel_id=1, source_target_pairs={{0,6},{1,7},{2,4},{3,5},{4,2},{5,3},{6,0},{7,1},{8,14},{9,15},{10,... | collective-permute-start | bytes 393224 | tf_op jit(solution)/shard_map/ppermute | solution.py:376
  442.7 31.7 %collective-permute-start.74 = (bf16[32,16,128]{2,1,0:T(8,128)(2,1)}, bf16[32,16,128]{2,1,0:T(8,128)(2,1)S(1)}, u32[]{:S(2)}, u32[]{:S(2)}) collective-permute-start(bf16[32,16,128]{2,1,0:T(8,128)(2,1)} %get-tuple-element.228), channel_id=1, source_target_pairs={{0,7},{1,6},{2,5},{3,4},{4,3},{5,2},{6,1},{7,0},{8,15},{9,14},{10,... | collective-permute-start | bytes 393224 | tf_op jit(solution)/shard_map/ppermute | solution.py:376
  459.1 15.4 %collective-permute-start.75 = (bf16[32,16,128]{2,1,0:T(8,128)(2,1)}, bf16[32,16,128]{2,1,0:T(8,128)(2,1)S(1)}, u32[]{:S(2)}, u32[]{:S(2)}) collective-permute-start(bf16[32,16,128]{2,1,0:T(8,128)(2,1)} %get-tuple-element.229), channel_id=1, source_target_pairs={{0,3},{1,2},{2,1},{3,0},{4,7},{5,6},{6,5},{7,4},{8,11},{9,10},{10,... | collective-permute-start | bytes 393224 | tf_op jit(solution)/shard_map/ppermute | solution.py:376
  (90 other events, 1818.9 us)

commit v8 on v7

--- a/solution.py
+++ b/solution.py
@@ -143,9 +143,9 @@
 
 
 def spectra_kernel(
-    meta_ref, delay_ref, est_ref, obs_ref, before_ref, after_ref, table_ref, _, *refs
+    unused, meta_ref, delay_ref, est_ref, obs_ref, before_ref, after_ref, table_ref, *refs
 ):
-    *out_refs, energy_ref, est32, res32, stepped, result = refs
+    *out_refs, energy_ref, est32, res32, stepped, result = refs[unused:]
     shots, rows, samples = est_ref.shape
     width = out_refs[0].shape[2]
 
@@ -184,8 +184,8 @@
     )
 
 
-def shots_kernel(meta_ref, table_ref, level_ref, _, *refs):
-    *refs, wide, back = refs
+def shots_kernel(unused, meta_ref, table_ref, level_ref, *refs):
+    *refs, wide, back = refs[unused:]
     spectra_refs, out_refs = refs[: len(refs) // 2], refs[len(refs) // 2 :]
     held, rows, width = out_refs[0].shape
     shots = wide.shape[0] // rows
@@ -225,7 +225,8 @@
         ref[...] = back[place(slot), :].astype(jnp.bfloat16).reshape(held, rows, width)
 
 
-def update_kernel(inputs, meta_ref, table_ref, _, *refs):
+def update_kernel(unused, inputs, meta_ref, table_ref, *refs):
+    refs = refs[unused:]
     restored_refs, (out_ref, turn_ref, whole_rows) = refs[:inputs], refs[-3:]
     held, rows, width = restored_refs[0].shape
     for slot, ref in zip(slots_of(inputs), restored_refs):
@@ -269,12 +270,13 @@
     shape = (shots, rows, 2 * F // peers)
     group = min(shots, max(1, 256 // rows))
     *spectra, energy = pl.pallas_call(
-        spectra_kernel,
+        functools.partial(spectra_kernel, len(after)),
         grid_spec=pltpu.PrefetchScalarGridSpec(
             num_scalar_prefetch=2,
             grid=(1,),
             in_specs=blend_specs(shots, rows, samples, block, edge_block)
-            + [whole(table.shape), ANYWHERE],
+            + [whole(table.shape)]
+            + [ANYWHERE] * len(after),
             out_specs=[whole(shape)] * peers + [whole((shots, LANES))],
             scratch_shapes=blend_scratch(shots, rows, samples)
             + [
@@ -286,7 +288,7 @@
         compiler_params=PARAMS,
         cost_estimate=SMALL,
         name="spectra",
-    )(meta, delays, *fields, table, after)
+    )(meta, delays, *fields, table, *after)
     return spectra, energy
 
 
@@ -315,11 +317,12 @@
     held, rows, width = shape
     peers = len(spectra)
     return pl.pallas_call(
-        shots_kernel,
+        functools.partial(shots_kernel, len(after)),
         grid_spec=pltpu.PrefetchScalarGridSpec(
             num_scalar_prefetch=1,
             grid=(1,),
-            in_specs=[whole(table.shape), whole(level.shape), ANYWHERE]
+            in_specs=[whole(table.shape), whole(level.shape)]
+            + [ANYWHERE] * len(after)
             + [read(item, shape, lambda step: (0, 0, 0)) for item in spectra],
             out_specs=[whole(shape)] * peers,
             scratch_shapes=[pltpu.VMEM((peers * held * rows, width), jnp.float32)] * 2,
@@ -328,21 +331,21 @@
         compiler_params=PARAMS,
         cost_estimate=SMALL,
         name="shrink",
-    )(meta, table, level, after, *[array for array, _ in spectra])
+    )(meta, table, level, *after, *[array for array, _ in spectra])
 
 
 def updated_of(meta, restored, table, block, receivers, onto, after):
     shots, rows, width = restored[0][0].shape
     samples = table.shape[1]
     group = min(shots, max(1, 256 // rows))
-    in_specs = [whole(table.shape), ANYWHERE]
+    in_specs = [whole(table.shape)] + [ANYWHERE] * len(after)
     in_specs += [read(item, (group, rows, width), lambda step: (step, 0, 0)) for item in restored]
-    operands = [meta, table, after, *[array for array, _ in restored]]
+    operands = [meta, table, *after, *[array for array, _ in restored]]
     if onto is not None:
         in_specs.append(ANYWHERE)
         operands.append(onto)
     return pl.pallas_call(
-        functools.partial(update_kernel, len(restored)),
+        functools.partial(update_kernel, len(after), len(restored)),
         grid_spec=pltpu.PrefetchScalarGridSpec(
             num_scalar_prefetch=1,
             grid=(shots // group,),
@@ -391,12 +394,7 @@
 
 
 def slots_of(peers):
-    far, near = list(range(peers // 2, peers)), list(range(2, peers // 2))
-    order = [0, 1]
-    while far or near:
-        order += far[:2] + near[:1]
-        far, near = far[2:], near[1:]
-    return order
+    return [0, 1, *range(2, min(3, peers // 2)), *range(peers // 2, peers), *range(3, peers // 2)]
 
 
 def exchanged(arrays):
@@ -415,9 +413,20 @@
 
 def chunks_of(receivers):
     if receivers == 128:
-        return [(16, 7), (16, 6), (32, 2), (32, 1), (16, 1), (16, 0)]
+        return [(16, 96), (32, 64), (32, 32), (32, 0), (16, 112)], 2
     rows = min(16, receivers)
-    return [(rows, index) for index in range(receivers // rows)][::-1]
+    return [(rows, start) for start in range(0, receivers, rows)], 1
+
+
+def edges_of(estimate, observed, chunks):
+    order = sorted(chunks, key=lambda chunk: (-chunk[0], chunk[1]))
+    cut = lambda array: jnp.concatenate([array[:, start : start + rows] for rows, start in order], axis=1)
+    ends = [jnp.concatenate([array[:2], array[-2:]]) for array in (estimate, observed)]
+    places, position = {}, 0
+    for rows, start in order:
+        places[start] = position // rows
+        position += rows
+    return edges(*[cut(array) for array in ends]), places
 
 
 def direct(estimate, observed, delays, thresholds):
@@ -431,42 +440,48 @@
     forward, inverse = (jnp.asarray(table) for table in time_tables(samples, peers))
     table = jnp.asarray(shot_table(delays.shape[0]))
     levels = jnp.tile(lax.dynamic_slice_in_dim(thresholds, rank * share, share), 2)[None, :]
-    chunks = chunks_of(receivers)
-    rest = receivers - chunks[0][0]
-    early = edges(estimate[:, rest:], observed[:, rest:])
-    late = None
+    chunks, ahead = chunks_of(receivers)
+    sides, places = edges_of(estimate, observed, chunks[:ahead])
+    makers = [("spectra", 0)]
+    for chunk in range(len(chunks)):
+        makers += [("spectra", chunk + 1)] if chunk + 1 < len(chunks) and chunk == 0 else []
+        makers += [("shrink", chunk)]
+        makers += [("spectra", chunk + 2)] if chunk + 2 < len(chunks) else []
     last, updated, energy = levels, None, 0.0
-    lag = 2
-    ahead, behind = {}, {}
-    for turn in range(len(chunks) + 2 * lag):
-        if turn < len(chunks):
-            rows, index = chunks[turn]
-            spectra, power = spectra_of(
+    brought, exchanges = {}, []
+    for place, (name, chunk) in enumerate(makers):
+        rows, start = chunks[chunk]
+        after = [last]
+        if place >= 2:
+            after += [array for array, _ in exchanges[place - 2][1:]]
+        if name == "spectra":
+            if chunk == ahead:
+                later = lax.optimization_barrier((estimate, observed, energy))
+                sides, places = edges_of(*later[:2], chunks[ahead:])
+            blocks, power = spectra_of(
                 meta,
                 delays,
-                (estimate, observed, *(late if turn else early)),
+                (estimate, observed, *sides),
                 forward,
                 rows,
-                index,
-                index if turn else 0,
+                start // rows,
+                places[start],
                 peers,
-                last,
+                after,
             )
             last = power
             energy = energy + power
-            ahead[turn] = exchanged(spectra)
-            if turn == 0 and rest:
-                later = lax.optimization_barrier((estimate, observed, power))
-                late = edges(later[0][:, :rest], later[1][:, :rest])
-        place = turn - lag
-        if place in ahead:
-            shrunk = shrunk_of(meta, ahead.pop(place), table, levels, last)
-            last = shrunk[0]
-            behind[place] = exchanged(shrunk)
-        place = turn - 2 * lag
-        if place in behind:
+        else:
+            blocks = shrunk_of(meta, brought.pop(("spectra", chunk)), table, levels, after)
+            last = blocks[0]
+        exchanges.append(exchanged(blocks))
+        brought[name, chunk] = exchanges[-1]
+        ready = [chunk - 1] if name == "shrink" and chunk else []
+        ready += [chunk] if place == len(makers) - 1 else []
+        for done in ready:
+            rows, start = chunks[done]
             updated, last = updated_of(
-                meta, behind.pop(place), inverse, chunks[place][1], receivers, updated, last
+                meta, brought.pop(("shrink", done)), inverse, start // rows, receivers, updated, [last]
             )
     return updated, energy
 

time: 480 us -> 473 us (0.985)
  waiting for transfers between devices: 129 us -> 73.6 us
  starting transfers between devices: 135 us -> 177 us
  local copies, waits for them, and re-layouts: 18.3 us -> 26.6 us
  Pallas kernels: 152 us -> 147 us
    ppermute x72 -> x60, waiting for transfers between devices: 127 us -> 71.3 us  [sent(): lax.ppermute(array, 'shot', [(i, i ^ distance) for i in range(peers)])]
    ppermute x72 -> x60, starting transfers between devices: 124 us -> 170 us  [sent(): lax.ppermute(array, 'shot', [(i, i ^ distance) for i in range(peers)])]
    unnamed x156 -> x180, local copies, waits for them, and re-layouts: 13 us -> 21.3 us
    pallas_call x18 -> x15, Pallas kernels: 152 us -> 147 us  [the longest x5 64.6 us: spectra_of(): pl.pallas_call(functools.partial(spectra_kernel, len(after)), grid_spec=p...]
    all_gather x12 -> x10, blocking collectives: 30.9 us -> 33 us  [sent(): return (lax.all_gather(array, 'shot', axis_index_groups=groups), distance)]
  transfers between devices with their start and end apart: 76 -> 64, of which waited for: 17 -> 10; matrix products, arithmetic and copies ran while one was open for 1% -> 1% of each run, Pallas kernels for 29% -> 28%
where the time goes in v8:
time: 473 us; the launch traced here: 471 us
  starting transfers between devices  177 us (37%)
  Pallas kernels  147 us (31%)
  waiting for transfers between devices  73.6 us (16%)
  blocking collectives  42.9 us (9%)
  local copies, waits for them, and re-layouts  26.6 us (6%)
    ppermute x60, starting transfers between devices, sent(): lax.ppermute(array, 'shot', [(i, i ^ distance) for i in range(peers)])  170 us
    ppermute x60, waiting for transfers between devices, sent(): lax.ppermute(array, 'shot', [(i, i ^ distance) for i in range(peers)])  71.3 us
    pallas_call x5, Pallas kernels, spectra_of(): pl.pallas_call(functools.partial(spectra_kernel, len(after)), grid_spec=p...  64.6 us
    pallas_call x5, Pallas kernels, shrunk_of(): pl.pallas_call(functools.partial(shots_kernel, len(after)), grid_spec=plt...  59.2 us
    all_gather x10, blocking collectives, sent(): return (lax.all_gather(array, 'shot', axis_index_groups=groups), distance)  33 us
    pallas_call x5, Pallas kernels, updated_of(): pl.pallas_call(functools.partial(update_kernel, len(after), len(restored)...  22.8 us
    unnamed x180, local copies, waits for them, and re-layouts  21.3 us
    psum x1, blocking collectives, local(): lax.psum(jnp.sum(energy, axis=1), 'patch')  9.92 us
  transfers between devices with their start and end apart: 64, of which 10 were waited for; matrix products, arithmetic and copies ran while one was open for 1% of the time, Pallas kernels for 28%

profile of v8, /device:TPU:0, one launch (start us, length us, event | category | flops | bytes accessed | tf_op | source)
XLA Modules:
  0.0 471.1 jit_solution(7845563241924279840)
XLA Ops:
  2.7 2.4 collective-permute-start
  8.5 2.2 collective-permute-done.1.after_ref
  11.5 9.9 %spectra.5 = (bf16[32,16,128]{2,1,0:T(8,128)(2,1)}, bf16[32,16,128]{2,1,0:T(8,128)(2,1)}, bf16[32,16,128]{2,1,0:T(8,128)(2,1)}, bf16[32,16,128]{2,1,0:T(8,128)(2...) custom-call(s32[9]{0:T(128)} %pad_add_fusion.meta_ref, ...), custom_call_target="tpu_custom_call" | custom-call | flops 1024 | bytes 1024 | tf_op jit(solution)/shard_map/spectra/pallas_call | solution.py:272
  21.4 4.8 %collective-permute-start.4 = (bf16[32,16,128]{2,1,0:T(8,128)(2,1)}, bf16[32,16,128]{2,1,0:T(8,128)(2,1)S(1)}, u32[]{:S(2)}, u32[]{:S(2)}) collective-permute-start(bf16[32,16,128]{2,1,0:T(8,128)(2,1)} %get-tuple-element.103), channel_id=1, source_target_pairs={{0,2},{1,3},{2,0},{3,1},{4,6},{5,7},{6,4},{7,5},{8,10},{9,11},{10,... | collective-permute-start | bytes 393224 | tf_op jit(solution)/shard_map/ppermute | solution.py:379
  26.2 2.6 collective-permute-start.5
  30.0 2.5 collective-permute-start.7
  32.5 14.9 %spectra.6 = (bf16[32,32,128]{2,1,0:T(8,128)(2,1)}, bf16[32,32,128]{2,1,0:T(8,128)(2,1)}, bf16[32,32,128]{2,1,0:T(8,128)(2,1)}, bf16[32,32,128]{2,1,0:T(8,128)(2...) custom-call(s32[9]{0:T(128)} %pad_add_fusion.meta_ref, ...), custom_call_target="tpu_custom_call" | custom-call | flops 1024 | bytes 1024 | tf_op jit(solution)/shard_map/spectra/pallas_call | solution.py:272
  51.7 3.2 collective-permute-start.10
  56.0 3.7 all-gather
  59.6 2.3 collective-permute-start.2
  62.6 7.4 %shrink.5 = (bf16[32,16,128]{2,1,0:T(8,128)(2,1)}, bf16[32,16,128]{2,1,0:T(8,128)(2,1)}, bf16[32,16,128]{2,1,0:T(8,128)(2,1)}, bf16[32,16,128]{2,1,0:T(8,128)(2,...) custom-call(s32[9]{0:T(128)} %pad_add_fusion.meta_ref, ...), custom_call_target="tpu_custom_call" | custom-call | flops 1024 | bytes 1024 | tf_op jit(solution)/shard_map/shrink/pallas_call | solution.py:319
  70.0 3.4 collective-permute-start.16
  73.4 8.8 %collective-permute-done.16.refs_2_.refs_3_ = bf16[32,16,128]{2,1,0:T(8,128)(2,1)S(1)} collective-permute-done((bf16[32,16,128]{2,1,0:T(8,128)(2,1)}, bf16[32,16,128]{2,1,0:T(8,128)(2,1)S(1)}, u32[]{:S(2)}, u32[]{:S(2)}) %collective-permute-start.16) | collective-permute-done | bytes 131104 | tf_op jit(solution)/shard_map/ppermute | solution.py:379
  83.6 2.9 collective-permute-start.13
  88.1 14.5 %collective-permute-done.13.refs_5_.refs_13_ = bf16[32,32,128]{2,1,0:T(8,128)(2,1)S(1)} collective-permute-done((bf16[32,32,128]{2,1,0:T(8,128)(2,1)}, bf16[32,32,128]{2,1,0:T(8,128)(2,1)S(1)}, u32[]{:S(2)}, u32[]{:S(2)}) %collective-permute-start.13) | collective-permute-done | bytes 262176 | tf_op jit(solution)/shard_map/ppermute | solution.py:379
  102.6 11.8 %collective-permute-start.17 = (bf16[32,16,128]{2,1,0:T(8,128)(2,1)}, bf16[32,16,128]{2,1,0:T(8,128)(2,1)S(1)}, u32[]{:S(2)}, u32[]{:S(2)}) collective-permute-start(bf16[32,16,128]{2,1,0:T(8,128)(2,1)} %get-tuple-element.121), channel_id=1, source_target_pairs={{0,4},{1,5},{2,6},{3,7},{4,0},{5,1},{6,2},{7,3},{8,12},{9,13},{10,... | collective-permute-start | bytes 393224 | tf_op jit(solution)/shard_map/ppermute | solution.py:379
  114.4 5.5 %collective-permute-start.19 = (bf16[32,16,128]{2,1,0:T(8,128)(2,1)}, bf16[32,16,128]{2,1,0:T(8,128)(2,1)S(1)}, u32[]{:S(2)}, u32[]{:S(2)}) collective-permute-start(bf16[32,16,128]{2,1,0:T(8,128)(2,1)} %get-tuple-element.123), channel_id=1, source_target_pairs={{0,6},{1,7},{2,4},{3,5},{4,2},{5,3},{6,0},{7,1},{8,14},{9,15},{10,... | collective-permute-start | bytes 393224 | tf_op jit(solution)/shard_map/ppermute | solution.py:379
  120.4 5.1 %all-gather.1 = bf16[64,32,128]{2,1,0:T(8,128)(2,1)} all-gather(bf16[32,32,128]{2,1,0:T(8,128)(2,1)} %get-tuple-element.111), channel_id=3, replica_groups={{0,1},{2,3},{4,5},{6,7},{8,9},{10,11},{12,13},{14,15},{16,17},{18,19},{..., dimensions={0}, use_global_device_ids=true | all-gather | bytes 786432 | tf_op jit(solution)/shard_map/all_gather | solution.py:378
  126.3 14.9 %spectra.7 = (bf16[32,32,128]{2,1,0:T(8,128)(2,1)}, bf16[32,32,128]{2,1,0:T(8,128)(2,1)}, bf16[32,32,128]{2,1,0:T(8,128)(2,1)}, bf16[32,32,128]{2,1,0:T(8,128)(2...) custom-call(s32[9]{0:T(128)} %pad_add_fusion.meta_ref, ...), custom_call_target="tpu_custom_call" | custom-call | flops 1024 | bytes 1024 | tf_op jit(solution)/shard_map/spectra/pallas_call | solution.py:272
  142.6 2.6 collective-permute-start.23
  145.3 2.9 collective-permute-start.25
  148.9 2.2 all-gather.2
  151.1 14.9 %shrink.6 = (bf16[32,32,128]{2,1,0:T(8,128)(2,1)}, bf16[32,32,128]{2,1,0:T(8,128)(2,1)}, bf16[32,32,128]{2,1,0:T(8,128)(2,1)}, bf16[32,32,128]{2,1,0:T(8,128)(2,...) custom-call(s32[9]{0:T(128)} %pad_add_fusion.meta_ref, ...), custom_call_target="tpu_custom_call" | custom-call | flops 1024 | bytes 1024 | tf_op jit(solution)/shard_map/shrink/pallas_call | solution.py:319
  166.1 9.4 %collective-permute-done.23.refs_3_.refs_11_ = bf16[32,32,128]{2,1,0:T(8,128)(2,1)S(1)} collective-permute-done((bf16[32,32,128]{2,1,0:T(8,128)(2,1)}, bf16[32,32,128]{2,1,0:T(8,128)(2,1)S(1)}, u32[]{:S(2)}, u32[]{:S(2)}) %collective-permute-start.23) | collective-permute-done | bytes 262176 | tf_op jit(solution)/shard_map/ppermute | solution.py:379
  175.8 3.0 collective-permute-done.24.refs_4_.refs_12_
  178.9 1.9 collective-permute-start.29
  180.8 12.0 %collective-permute-start.30 = (bf16[32,32,128]{2,1,0:T(8,128)(2,1)}, bf16[32,32,128]{2,1,0:T(8,128)(2,1)S(1)}, u32[]{:S(2)}, u32[]{:S(2)}) collective-permute-start(bf16[32,32,128]{2,1,0:T(8,128)(2,1)} %get-tuple-element.140), channel_id=1, source_target_pairs={{0,5},{1,4},{2,7},{3,6},{4,1},{5,0},{6,3},{7,2},{8,13},{9,12},{10,... | collective-permute-start | bytes 786440 | tf_op jit(solution)/shard_map/ppermute | solution.py:379
  193.2 7.1 %all-gather.3 = bf16[64,32,128]{2,1,0:T(8,128)(2,1)} all-gather(bf16[32,32,128]{2,1,0:T(8,128)(2,1)} %get-tuple-element.129), channel_id=5, replica_groups={{0,1},{2,3},{4,5},{6,7},{8,9},{10,11},{12,13},{14,15},{16,17},{18,19},{..., dimensions={0}, use_global_device_ids=true | all-gather | bytes 786432 | tf_op jit(solution)/shard_map/all_gather | solution.py:378
  201.1 2.8 collective-permute-start.32
  203.9 19.2 %collective-permute-start.33 = (bf16[32,32,128]{2,1,0:T(8,128)(2,1)}, bf16[32,32,128]{2,1,0:T(8,128)(2,1)S(1)}, u32[]{:S(2)}, u32[]{:S(2)}) collective-permute-start(bf16[32,32,128]{2,1,0:T(8,128)(2,1)} %get-tuple-element.143), channel_id=1, source_target_pairs={{0,3},{1,2},{2,1},{3,0},{4,7},{5,6},{6,5},{7,4},{8,11},{9,10},{10,... | collective-permute-start | bytes 786440 | tf_op jit(solution)/shard_map/ppermute | solution.py:379
  229.4 3.2 update.5
  232.7 14.8 %spectra.8 = (bf16[32,32,128]{2,1,0:T(8,128)(2,1)}, bf16[32,32,128]{2,1,0:T(8,128)(2,1)}, bf16[32,32,128]{2,1,0:T(8,128)(2,1)}, bf16[32,32,128]{2,1,0:T(8,128)(2...) custom-call(s32[9]{0:T(128)} %pad_add_fusion.meta_ref, ...), custom_call_target="tpu_custom_call" | custom-call | flops 1024 | bytes 1024 | tf_op jit(solution)/shard_map/spectra/pallas_call | solution.py:272
  247.8 3.0 collective-permute-start.35
  250.8 2.3 all-gather.4
  253.1 2.2 collective-permute-start.37
  256.6 14.8 %shrink.7 = (bf16[32,32,128]{2,1,0:T(8,128)(2,1)}, bf16[32,32,128]{2,1,0:T(8,128)(2,1)}, bf16[32,32,128]{2,1,0:T(8,128)(2,1)}, bf16[32,32,128]{2,1,0:T(8,128)(2,...) custom-call(s32[9]{0:T(128)} %pad_add_fusion.meta_ref, ...), custom_call_target="tpu_custom_call" | custom-call | flops 1024 | bytes 1024 | tf_op jit(solution)/shard_map/shrink/pallas_call | solution.py:319
  271.7 9.1 %collective-permute-done.35.refs_3_.refs_11_ = bf16[32,32,128]{2,1,0:T(8,128)(2,1)} collective-permute-done((bf16[32,32,128]{2,1,0:T(8,128)(2,1)}, bf16[32,32,128]{2,1,0:T(8,128)(2,1)}, u32[]{:S(2)}, u32[]{:S(2)}) %collective-permute-start.35) | collective-permute-done | bytes 262176 | tf_op jit(solution)/shard_map/ppermute | solution.py:379
  280.9 4.0 collective-permute-done.36.refs_4_.refs_12_
  291.7 5.0 %update.6 = (f32[32,128,1024]{2,1,0:T(8,128)}, f32[8,128]{1,0:T(8,128)}) custom-call(s32[9]{0:T(128)S(1)} %copy-done.49, bf16[1024,1024]{1,0:T(8,128)(2,1)S(1)} %copy-done, bf16[32,32,128]{2,1,0:T(8,128)(2,1)S(1)} %copy-done.4, bf16[32,32,128]{2,1,0:T(8,128)(2,1)S(1)} %copy-done.9, ...), custom_call_target="tpu_custom_call", output_to_operand_aliasing={{0}: (11, {})} | custom-call | flops 1024 | bytes 1024 | tf_op jit(solution)/shard_map/update/pallas_call | solution.py:347
  296.7 2.5 collective-permute-start.42
  299.3 2.5 collective-permute-start.43
  302.6 19.6 %collective-permute-start.45 = (bf16[32,32,128]{2,1,0:T(8,128)(2,1)}, bf16[32,32,128]{2,1,0:T(8,128)(2,1)S(1)}, u32[]{:S(2)}, u32[]{:S(2)}) collective-permute-start(bf16[32,32,128]{2,1,0:T(8,128)(2,1)} %get-tuple-element.162), channel_id=1, source_target_pairs={{0,3},{1,2},{2,1},{3,0},{4,7},{5,6},{6,5},{7,4},{8,11},{9,10},{10,... | collective-permute-start | bytes 786440 | tf_op jit(solution)/shard_map/ppermute | solution.py:379
  322.2 2.3 all-gather.5
  324.5 10.0 %spectra.9 = (bf16[32,16,128]{2,1,0:T(8,128)(2,1)}, bf16[32,16,128]{2,1,0:T(8,128)(2,1)}, bf16[32,16,128]{2,1,0:T(8,128)(2,1)}, bf16[32,16,128]{2,1,0:T(8,128)(2...) custom-call(s32[9]{0:T(128)} %pad_add_fusion.meta_ref, ...), custom_call_target="tpu_custom_call" | custom-call | flops 1024 | bytes 1024 | tf_op jit(solution)/shard_map/spectra/pallas_call | solution.py:272
  334.6 2.6 collective-permute-start.47
  337.2 2.1 collective-permute-start.49
  339.4 2.4 collective-permute-start.50
  341.8 13.5 %collective-permute-start.51 = (bf16[32,16,128]{2,1,0:T(8,128)(2,1)}, bf16[32,16,128]{2,1,0:T(8,128)(2,1)}, u32[]{:S(2)}, u32[]{:S(2)}) collective-permute-start(bf16[32,16,128]{2,1,0:T(8,128)(2,1)} %get-tuple-element.173), channel_id=1, source_target_pairs={{0,3},{1,2},{2,1},{3,0},{4,7},{5,6},{6,5},{7,4},{8,11},{9,10},{10,... | collective-permute-start | bytes 393224 | tf_op jit(solution)/shard_map/ppermute | solution.py:379
  355.3 2.3 all-gather.6
  357.7 14.8 %shrink.8 = (bf16[32,32,128]{2,1,0:T(8,128)(2,1)}, bf16[32,32,128]{2,1,0:T(8,128)(2,1)}, bf16[32,32,128]{2,1,0:T(8,128)(2,1)}, bf16[32,32,128]{2,1,0:T(8,128)(2,...) custom-call(s32[9]{0:T(128)} %pad_add_fusion.meta_ref, ...), custom_call_target="tpu_custom_call" | custom-call | flops 1024 | bytes 1024 | tf_op jit(solution)/shard_map/shrink/pallas_call | solution.py:319
  377.5 5.0 %update.7 = (f32[32,128,1024]{2,1,0:T(8,128)}, f32[8,128]{1,0:T(8,128)}) custom-call(s32[9]{0:T(128)S(1)} %copy-done.50, bf16[1024,1024]{1,0:T(8,128)(2,1)S(1)} %copy-done, bf16[32,32,128]{2,1,0:T(8,128)(2,1)S(1)} %copy-done.6, bf16[32,32,128]{2,1,0:T(8,128)(2,1)S(1)} %copy-done.5, ...), custom_call_target="tpu_custom_call", output_to_operand_aliasing={{0}: (11, {})} | custom-call | flops 1024 | bytes 1024 | tf_op jit(solution)/shard_map/update/pallas_call | solution.py:347
  382.6 2.3 all-gather.7
  385.0 7.4 %shrink.9 = (bf16[32,16,128]{2,1,0:T(8,128)(2,1)}, bf16[32,16,128]{2,1,0:T(8,128)(2,1)}, bf16[32,16,128]{2,1,0:T(8,128)(2,1)}, bf16[32,16,128]{2,1,0:T(8,128)(2,...) custom-call(s32[9]{0:T(128)} %pad_add_fusion.meta_ref, ...), custom_call_target="tpu_custom_call" | custom-call | flops 1024 | bytes 1024 | tf_op jit(solution)/shard_map/shrink/pallas_call | solution.py:319
  396.4 2.5 collective-permute-start.55
  402.2 9.9 %psum.7 = f32[32]{0:T(128)S(1)} all-reduce(f32[32]{0:T(128)S(1)} %add_reduce_fusion), channel_id=1, replica_groups=mesh['patch'=4,'shot'=8] {'patch'}, use_global_device_ids=true, to_apply=%region_1.0 | all-reduce | flops 32 | bytes 256 | tf_op jit(solution)/shard_map/psum | solution.py:547
  412.6 14.4 %collective-permute-done.53.refs_4_ = bf16[32,32,128]{2,1,0:T(8,128)(2,1)S(1)} collective-permute-done((bf16[32,32,128]{2,1,0:T(8,128)(2,1)}, bf16[32,32,128]{2,1,0:T(8,128)(2,1)S(1)}, u32[]{:S(2)}, u32[]{:S(2)}) %collective-permute-start.53) | collective-permute-done | bytes 262176 | tf_op jit(solution)/shard_map/ppermute | solution.py:379
  427.0 6.3 %collective-permute-done.54.refs_5_ = bf16[32,32,128]{2,1,0:T(8,128)(2,1)S(1)} collective-permute-done((bf16[32,32,128]{2,1,0:T(8,128)(2,1)}, bf16[32,32,128]{2,1,0:T(8,128)(2,1)S(1)}, u32[]{:S(2)}, u32[]{:S(2)}) %collective-permute-start.54) | collective-permute-done | bytes 262176 | tf_op jit(solution)/shard_map/ppermute | solution.py:379
  433.3 2.5 collective-permute-start.61
  435.9 2.6 collective-permute-start.62
  438.4 16.8 %collective-permute-start.63 = (bf16[32,16,128]{2,1,0:T(8,128)(2,1)}, bf16[32,16,128]{2,1,0:T(8,128)(2,1)S(1)}, u32[]{:S(2)}, u32[]{:S(2)}) collective-permute-start(bf16[32,16,128]{2,1,0:T(8,128)(2,1)} %get-tuple-element.191), channel_id=1, source_target_pairs={{0,3},{1,2},{2,1},{3,0},{4,7},{5,6},{6,5},{7,4},{8,11},{9,10},{10,... | collective-permute-start | bytes 393224 | tf_op jit(solution)/shard_map/ppermute | solution.py:379
  455.2 3.5 all-gather.8
  458.7 2.2 all-gather.9
  460.9 6.2 %update.8 = (f32[32,128,1024]{2,1,0:T(8,128)}, f32[8,128]{1,0:T(8,128)}) custom-call(s32[9]{0:T(128)S(1)} %copy-done.51, bf16[1024,1024]{1,0:T(8,128)(2,1)S(1)} %copy-done, bf16[32,16,128]{2,1,0:T(8,128)(2,1)S(1)} %copy-done.34, bf16[32,32,128]{2,1,0:T(8,128)(2,1)S(1)} %copy-done.7, ...), custom_call_target="tpu_custom_call", output_to_operand_aliasing={{0}: (11, {})} | custom-call | flops 1024 | bytes 1024 | tf_op jit(solution)/shard_map/update/pallas_call | solution.py:347
  467.9 3.2 update.9
  (291 shorter events, 50.9 us)
Async XLA Ops:
  2.7 5.8 %collective-permute-start = (bf16[3,48,1024]{2,1,0:T(8,128)(2,1)S(1)}, bf16[3,48,1024]{2,1,0:T(8,128)(2,1)S(1)}, u32[]{:S(2)}, u32[]{:S(2)}) collective-permute-start(bf16[3,48,1024]{2,1,0:T(8,128)(2,1)S(1)} %pad_maximum_fusion.2), channel_id=1, source_target_pairs={{0,1},{1,2},{2,3},{3,4},{4,5},{5,6},{6,7},{8,9},{9,10},{10,11},{11... | collective-permute-start | bytes 884744 | tf_op jit(solution)/shard_map/ppermute | solution.py:411
  5.1 5.7 %collective-permute-start.1 = (bf16[3,48,1024]{2,1,0:T(8,128)(2,1)S(1)}, bf16[3,48,1024]{2,1,0:T(8,128)(2,1)S(1)}, u32[]{:S(2)}, u32[]{:S(2)}) collective-permute-start(bf16[3,48,1024]{2,1,0:T(8,128)(2,1)S(1)} %pad_maximum_fusion.3), channel_id=1, source_target_pairs={{1,0},{2,1},{3,2},{4,3},{5,4},{6,5},{7,6},{9,8},{10,9},{11,10},{12... | collective-permute-start | bytes 884744 | tf_op jit(solution)/shard_map/ppermute | solution.py:411
  21.4 29.4 %collective-permute-start.4 = (bf16[32,16,128]{2,1,0:T(8,128)(2,1)}, bf16[32,16,128]{2,1,0:T(8,128)(2,1)S(1)}, u32[]{:S(2)}, u32[]{:S(2)}) collective-permute-start(bf16[32,16,128]{2,1,0:T(8,128)(2,1)} %get-tuple-element.103), channel_id=1, source_target_pairs={{0,2},{1,3},{2,0},{3,1},{4,6},{5,7},{6,4},{7,5},{8,10},{9,11},{10,... | collective-permute-start | bytes 393224 | tf_op jit(solution)/shard_map/ppermute | solution.py:379
  26.2 25.5 %collective-permute-start.5 = (bf16[32,16,128]{2,1,0:T(8,128)(2,1)}, bf16[32,16,128]{2,1,0:T(8,128)(2,1)S(1)}, u32[]{:S(2)}, u32[]{:S(2)}) collective-permute-start(bf16[32,16,128]{2,1,0:T(8,128)(2,1)} %get-tuple-element.104), channel_id=1, source_target_pairs={{0,4},{1,5},{2,6},{3,7},{4,0},{5,1},{6,2},{7,3},{8,12},{9,13},{10,... | collective-permute-start | bytes 393224 | tf_op jit(solution)/shard_map/ppermute | solution.py:379
  28.8 26.1 %collective-permute-start.6 = (bf16[32,16,128]{2,1,0:T(8,128)(2,1)}, bf16[32,16,128]{2,1,0:T(8,128)(2,1)S(1)}, u32[]{:S(2)}, u32[]{:S(2)}) collective-permute-start(bf16[32,16,128]{2,1,0:T(8,128)(2,1)} %get-tuple-element.105), channel_id=1, source_target_pairs={{0,5},{1,4},{2,7},{3,6},{4,1},{5,0},{6,3},{7,2},{8,13},{9,12},{10,... | collective-permute-start | bytes 393224 | tf_op jit(solution)/shard_map/ppermute | solution.py:379
  30.0 26.0 %collective-permute-start.7 = (bf16[32,16,128]{2,1,0:T(8,128)(2,1)}, bf16[32,16,128]{2,1,0:T(8,128)(2,1)S(1)}, u32[]{:S(2)}, u32[]{:S(2)}) collective-permute-start(bf16[32,16,128]{2,1,0:T(8,128)(2,1)} %get-tuple-element.106), channel_id=1, source_target_pairs={{0,6},{1,7},{2,4},{3,5},{4,2},{5,3},{6,0},{7,1},{8,14},{9,15},{10,... | collective-permute-start | bytes 393224 | tf_op jit(solution)/shard_map/ppermute | solution.py:379
  32.5 27.2 %collective-permute-start.8 = (bf16[32,16,128]{2,1,0:T(8,128)(2,1)}, bf16[32,16,128]{2,1,0:T(8,128)(2,1)S(1)}, u32[]{:S(2)}, u32[]{:S(2)}) collective-permute-start(bf16[32,16,128]{2,1,0:T(8,128)(2,1)} %get-tuple-element.107), channel_id=1, source_target_pairs={{0,7},{1,6},{2,5},{3,4},{4,3},{5,2},{6,1},{7,0},{8,15},{9,14},{10,... | collective-permute-start | bytes 393224 | tf_op jit(solution)/shard_map/ppermute | solution.py:379
  51.6 10.3 %collective-permute-start.9 = (bf16[32,16,128]{2,1,0:T(8,128)(2,1)S(1)}, bf16[32,16,128]{2,1,0:T(8,128)(2,1)S(1)}, u32[]{:S(2)}, u32[]{:S(2)}) collective-permute-start(bf16[32,16,128]{2,1,0:T(8,128)(2,1)S(1)} %copy-done.89), channel_id=1, source_target_pairs={{0,3},{1,2},{2,1},{3,0},{4,7},{5,6},{6,5},{7,4},{8,11},{9,10},{10,... | collective-permute-start | bytes 393224 | tf_op jit(solution)/shard_map/ppermute | solution.py:379
  51.7 31.9 %collective-permute-start.10 = (bf16[32,32,128]{2,1,0:T(8,128)(2,1)}, bf16[32,32,128]{2,1,0:T(8,128)(2,1)S(1)}, u32[]{:S(2)}, u32[]{:S(2)}) collective-permute-start(bf16[32,32,128]{2,1,0:T(8,128)(2,1)} %get-tuple-element.112), channel_id=1, source_target_pairs={{0,2},{1,3},{2,0},{3,1},{4,6},{5,7},{6,4},{7,5},{8,10},{9,11},{10,... | collective-permute-start | bytes 786440 | tf_op jit(solution)/shard_map/ppermute | solution.py:379
  54.8 31.7 %collective-permute-start.11 = (bf16[32,32,128]{2,1,0:T(8,128)(2,1)}, bf16[32,32,128]{2,1,0:T(8,128)(2,1)S(1)}, u32[]{:S(2)}, u32[]{:S(2)}) collective-permute-start(bf16[32,32,128]{2,1,0:T(8,128)(2,1)} %get-tuple-element.113), channel_id=1, source_target_pairs={{0,4},{1,5},{2,6},{3,7},{4,0},{5,1},{6,2},{7,3},{8,12},{9,13},{10,... | collective-permute-start | bytes 786440 | tf_op jit(solution)/shard_map/ppermute | solution.py:379
  55.9 32.0 %collective-permute-start.12 = (bf16[32,32,128]{2,1,0:T(8,128)(2,1)}, bf16[32,32,128]{2,1,0:T(8,128)(2,1)S(1)}, u32[]{:S(2)}, u32[]{:S(2)}) collective-permute-start(bf16[32,32,128]{2,1,0:T(8,128)(2,1)} %get-tuple-element.114), channel_id=1, source_target_pairs={{0,5},{1,4},{2,7},{3,6},{4,1},{5,0},{6,3},{7,2},{8,13},{9,12},{10,... | collective-permute-start | bytes 786440 | tf_op jit(solution)/shard_map/ppermute | solution.py:379
  59.6 60.3 %collective-permute-start.2 = (bf16[3,80,1024]{2,1,0:T(8,128)(2,1)S(1)}, bf16[3,80,1024]{2,1,0:T(8,128)(2,1)S(1)}, u32[]{:S(2)}, u32[]{:S(2)}) collective-permute-start(bf16[3,80,1024]{2,1,0:T(8,128)(2,1)S(1)} %pad_maximum_fusion), channel_id=1, source_target_pairs={{0,1},{1,2},{2,3},{3,4},{4,5},{5,6},{6,7},{8,9},{9,10},{10,11},{11... | collective-permute-start | bytes 1474568 | tf_op jit(solution)/shard_map/ppermute | solution.py:411
  70.0 12.2 %collective-permute-start.16 = (bf16[32,16,128]{2,1,0:T(8,128)(2,1)}, bf16[32,16,128]{2,1,0:T(8,128)(2,1)S(1)}, u32[]{:S(2)}, u32[]{:S(2)}) collective-permute-start(bf16[32,16,128]{2,1,0:T(8,128)(2,1)} %get-tuple-element.120), channel_id=1, source_target_pairs={{0,2},{1,3},{2,0},{3,1},{4,6},{5,7},{6,4},{7,5},{8,10},{9,11},{10,... | collective-permute-start | bytes 393224 | tf_op jit(solution)/shard_map/ppermute | solution.py:379
  82.3 43.2 %collective-permute-start.3 = (bf16[3,80,1024]{2,1,0:T(8,128)(2,1)S(1)}, bf16[3,80,1024]{2,1,0:T(8,128)(2,1)S(1)}, u32[]{:S(2)}, u32[]{:S(2)}) collective-permute-start(bf16[3,80,1024]{2,1,0:T(8,128)(2,1)S(1)} %pad_maximum_fusion.1), channel_id=1, source_target_pairs={{1,0},{2,1},{3,2},{4,3},{5,4},{6,5},{7,6},{9,8},{10,9},{11,10},{12... | collective-permute-start | bytes 1474568 | tf_op jit(solution)/shard_map/ppermute | solution.py:411
  83.6 19.0 %collective-permute-start.13 = (bf16[32,32,128]{2,1,0:T(8,128)(2,1)}, bf16[32,32,128]{2,1,0:T(8,128)(2,1)S(1)}, u32[]{:S(2)}, u32[]{:S(2)}) collective-permute-start(bf16[32,32,128]{2,1,0:T(8,128)(2,1)} %get-tuple-element.115), channel_id=1, source_target_pairs={{0,6},{1,7},{2,4},{3,5},{4,2},{5,3},{6,0},{7,1},{8,14},{9,15},{10,... | collective-permute-start | bytes 786440 | tf_op jit(solution)/shard_map/ppermute | solution.py:379
  86.5 27.9 %collective-permute-start.14 = (bf16[32,32,128]{2,1,0:T(8,128)(2,1)S(1)}, bf16[32,32,128]{2,1,0:T(8,128)(2,1)S(1)}, u32[]{:S(2)}, u32[]{:S(2)}) collective-permute-start(bf16[32,32,128]{2,1,0:T(8,128)(2,1)S(1)} %copy-done.87), channel_id=1, source_target_pairs={{0,7},{1,6},{2,5},{3,4},{4,3},{5,2},{6,1},{7,0},{8,15},{9,14},{10,... | collective-permute-start | bytes 786440 | tf_op jit(solution)/shard_map/ppermute | solution.py:379
  88.0 26.4 %collective-permute-start.15 = (bf16[32,32,128]{2,1,0:T(8,128)(2,1)S(1)}, bf16[32,32,128]{2,1,0:T(8,128)(2,1)S(1)}, u32[]{:S(2)}, u32[]{:S(2)}) collective-permute-start(bf16[32,32,128]{2,1,0:T(8,128)(2,1)S(1)} %copy-done.86), channel_id=1, source_target_pairs={{0,3},{1,2},{2,1},{3,0},{4,7},{5,6},{6,5},{7,4},{8,11},{9,10},{10,... | collective-permute-start | bytes 786440 | tf_op jit(solution)/shard_map/ppermute | solution.py:379
  102.6 38.6 %collective-permute-start.17 = (bf16[32,16,128]{2,1,0:T(8,128)(2,1)}, bf16[32,16,128]{2,1,0:T(8,128)(2,1)S(1)}, u32[]{:S(2)}, u32[]{:S(2)}) collective-permute-start(bf16[32,16,128]{2,1,0:T(8,128)(2,1)} %get-tuple-element.121), channel_id=1, source_target_pairs={{0,4},{1,5},{2,6},{3,7},{4,0},{5,1},{6,2},{7,3},{8,12},{9,13},{10,... | collective-permute-start | bytes 393224 | tf_op jit(solution)/shard_map/ppermute | solution.py:379
  114.4 28.2 %collective-permute-start.18 = (bf16[32,16,128]{2,1,0:T(8,128)(2,1)}, bf16[32,16,128]{2,1,0:T(8,128)(2,1)S(1)}, u32[]{:S(2)}, u32[]{:S(2)}) collective-permute-start(bf16[32,16,128]{2,1,0:T(8,128)(2,1)} %get-tuple-element.122), channel_id=1, source_target_pairs={{0,5},{1,4},{2,7},{3,6},{4,1},{5,0},{6,3},{7,2},{8,13},{9,12},{10,... | collective-permute-start | bytes 393224 | tf_op jit(solution)/shard_map/ppermute | solution.py:379
  114.4 30.8 %collective-permute-start.19 = (bf16[32,16,128]{2,1,0:T(8,128)(2,1)}, bf16[32,16,128]{2,1,0:T(8,128)(2,1)S(1)}, u32[]{:S(2)}, u32[]{:S(2)}) collective-permute-start(bf16[32,16,128]{2,1,0:T(8,128)(2,1)} %get-tuple-element.123), channel_id=1, source_target_pairs={{0,6},{1,7},{2,4},{3,5},{4,2},{5,3},{6,0},{7,1},{8,14},{9,15},{10,... | collective-permute-start | bytes 393224 | tf_op jit(solution)/shard_map/ppermute | solution.py:379
  119.9 25.3 %collective-permute-start.20 = (bf16[32,16,128]{2,1,0:T(8,128)(2,1)}, bf16[32,16,128]{2,1,0:T(8,128)(2,1)S(1)}, u32[]{:S(2)}, u32[]{:S(2)}) collective-permute-start(bf16[32,16,128]{2,1,0:T(8,128)(2,1)} %get-tuple-element.124), channel_id=1, source_target_pairs={{0,7},{1,6},{2,5},{3,4},{4,3},{5,2},{6,1},{7,0},{8,15},{9,14},{10,... | collective-permute-start | bytes 393224 | tf_op jit(solution)/shard_map/ppermute | solution.py:379
  125.5 22.7 %collective-permute-start.21 = (bf16[32,16,128]{2,1,0:T(8,128)(2,1)S(1)}, bf16[32,16,128]{2,1,0:T(8,128)(2,1)S(1)}, u32[]{:S(2)}, u32[]{:S(2)}) collective-permute-start(bf16[32,16,128]{2,1,0:T(8,128)(2,1)S(1)} %copy-done.88), channel_id=1, source_target_pairs={{0,3},{1,2},{2,1},{3,0},{4,7},{5,6},{6,5},{7,4},{8,11},{9,10},{10,... | collective-permute-start | bytes 393224 | tf_op jit(solution)/shard_map/ppermute | solution.py:379
  141.2 24.8 %collective-permute-start.22 = (bf16[32,32,128]{2,1,0:T(8,128)(2,1)}, bf16[32,32,128]{2,1,0:T(8,128)(2,1)S(1)}, u32[]{:S(2)}, u32[]{:S(2)}) collective-permute-start(bf16[32,32,128]{2,1,0:T(8,128)(2,1)} %get-tuple-element.130), channel_id=1, source_target_pairs={{0,2},{1,3},{2,0},{3,1},{4,6},{5,7},{6,4},{7,5},{8,10},{9,11},{10,... | collective-permute-start | bytes 786440 | tf_op jit(solution)/shard_map/ppermute | solution.py:379
  142.6 32.8 %collective-permute-start.23 = (bf16[32,32,128]{2,1,0:T(8,128)(2,1)}, bf16[32,32,128]{2,1,0:T(8,128)(2,1)S(1)}, u32[]{:S(2)}, u32[]{:S(2)}) collective-permute-start(bf16[32,32,128]{2,1,0:T(8,128)(2,1)} %get-tuple-element.131), channel_id=1, source_target_pairs={{0,4},{1,5},{2,6},{3,7},{4,0},{5,1},{6,2},{7,3},{8,12},{9,13},{10,... | collective-permute-start | bytes 786440 | tf_op jit(solution)/shard_map/ppermute | solution.py:379
  145.2 33.6 %collective-permute-start.24 = (bf16[32,32,128]{2,1,0:T(8,128)(2,1)}, bf16[32,32,128]{2,1,0:T(8,128)(2,1)S(1)}, u32[]{:S(2)}, u32[]{:S(2)}) collective-permute-start(bf16[32,32,128]{2,1,0:T(8,128)(2,1)} %get-tuple-element.132), channel_id=1, source_target_pairs={{0,5},{1,4},{2,7},{3,6},{4,1},{5,0},{6,3},{7,2},{8,13},{9,12},{10,... | collective-permute-start | bytes 786440 | tf_op jit(solution)/shard_map/ppermute | solution.py:379
  145.3 35.5 %collective-permute-start.25 = (bf16[32,32,128]{2,1,0:T(8,128)(2,1)}, bf16[32,32,128]{2,1,0:T(8,128)(2,1)}, u32[]{:S(2)}, u32[]{:S(2)}) collective-permute-start(bf16[32,32,128]{2,1,0:T(8,128)(2,1)} %get-tuple-element.133), channel_id=1, source_target_pairs={{0,6},{1,7},{2,4},{3,5},{4,2},{5,3},{6,0},{7,1},{8,14},{9,15},{10,... | collective-permute-start | bytes 786440 | tf_op jit(solution)/shard_map/ppermute | solution.py:379
  148.1 44.6 %collective-permute-start.26 = (bf16[32,32,128]{2,1,0:T(8,128)(2,1)}, bf16[32,32,128]{2,1,0:T(8,128)(2,1)}, u32[]{:S(2)}, u32[]{:S(2)}) collective-permute-start(bf16[32,32,128]{2,1,0:T(8,128)(2,1)} %get-tuple-element.134), channel_id=1, source_target_pairs={{0,7},{1,6},{2,5},{3,4},{4,3},{5,2},{6,1},{7,0},{8,15},{9,14},{10,... | collective-permute-start | bytes 786440 | tf_op jit(solution)/shard_map/ppermute | solution.py:379
  166.0 34.4 %collective-permute-start.27 = (bf16[32,32,128]{2,1,0:T(8,128)(2,1)}, bf16[32,32,128]{2,1,0:T(8,128)(2,1)S(1)}, u32[]{:S(2)}, u32[]{:S(2)}) collective-permute-start(bf16[32,32,128]{2,1,0:T(8,128)(2,1)} %get-tuple-element.135), channel_id=1, source_target_pairs={{0,3},{1,2},{2,1},{3,0},{4,7},{5,6},{6,5},{7,4},{8,11},{9,10},{10,... | collective-permute-start | bytes 786440 | tf_op jit(solution)/shard_map/ppermute | solution.py:379
  175.4 28.4 %collective-permute-start.28 = (bf16[32,32,128]{2,1,0:T(8,128)(2,1)}, bf16[32,32,128]{2,1,0:T(8,128)(2,1)S(1)}, u32[]{:S(2)}, u32[]{:S(2)}) collective-permute-start(bf16[32,32,128]{2,1,0:T(8,128)(2,1)} %get-tuple-element.138), channel_id=1, source_target_pairs={{0,2},{1,3},{2,0},{3,1},{4,6},{5,7},{6,4},{7,5},{8,10},{9,11},{10,... | collective-permute-start | bytes 786440 | tf_op jit(solution)/shard_map/ppermute | solution.py:379
  178.9 68.7 %collective-permute-start.29 = (bf16[32,32,128]{2,1,0:T(8,128)(2,1)}, bf16[32,32,128]{2,1,0:T(8,128)(2,1)S(1)}, u32[]{:S(2)}, u32[]{:S(2)}) collective-permute-start(bf16[32,32,128]{2,1,0:T(8,128)(2,1)} %get-tuple-element.139), channel_id=1, source_target_pairs={{0,4},{1,5},{2,6},{3,7},{4,0},{5,1},{6,2},{7,3},{8,12},{9,13},{10,... | collective-permute-start | bytes 786440 | tf_op jit(solution)/shard_map/ppermute | solution.py:379
  180.8 67.0 %collective-permute-start.30 = (bf16[32,32,128]{2,1,0:T(8,128)(2,1)}, bf16[32,32,128]{2,1,0:T(8,128)(2,1)S(1)}, u32[]{:S(2)}, u32[]{:S(2)}) collective-permute-start(bf16[32,32,128]{2,1,0:T(8,128)(2,1)} %get-tuple-element.140), channel_id=1, source_target_pairs={{0,5},{1,4},{2,7},{3,6},{4,1},{5,0},{6,3},{7,2},{8,13},{9,12},{10,... | collective-permute-start | bytes 786440 | tf_op jit(solution)/shard_map/ppermute | solution.py:379
  192.8 58.0 %collective-permute-start.31 = (bf16[32,32,128]{2,1,0:T(8,128)(2,1)}, bf16[32,32,128]{2,1,0:T(8,128)(2,1)S(1)}, u32[]{:S(2)}, u32[]{:S(2)}) collective-permute-start(bf16[32,32,128]{2,1,0:T(8,128)(2,1)} %get-tuple-element.141), channel_id=1, source_target_pairs={{0,6},{1,7},{2,4},{3,5},{4,2},{5,3},{6,0},{7,1},{8,14},{9,15},{10,... | collective-permute-start | bytes 786440 | tf_op jit(solution)/shard_map/ppermute | solution.py:379
  201.1 52.1 %collective-permute-start.32 = (bf16[32,32,128]{2,1,0:T(8,128)(2,1)}, bf16[32,32,128]{2,1,0:T(8,128)(2,1)S(1)}, u32[]{:S(2)}, u32[]{:S(2)}) collective-permute-start(bf16[32,32,128]{2,1,0:T(8,128)(2,1)} %get-tuple-element.142), channel_id=1, source_target_pairs={{0,7},{1,6},{2,5},{3,4},{4,3},{5,2},{6,1},{7,0},{8,15},{9,14},{10,... | collective-permute-start | bytes 786440 | tf_op jit(solution)/shard_map/ppermute | solution.py:379
  203.9 51.5 %collective-permute-start.33 = (bf16[32,32,128]{2,1,0:T(8,128)(2,1)}, bf16[32,32,128]{2,1,0:T(8,128)(2,1)S(1)}, u32[]{:S(2)}, u32[]{:S(2)}) collective-permute-start(bf16[32,32,128]{2,1,0:T(8,128)(2,1)} %get-tuple-element.143), channel_id=1, source_target_pairs={{0,3},{1,2},{2,1},{3,0},{4,7},{5,6},{6,5},{7,4},{8,11},{9,10},{10,... | collective-permute-start | bytes 786440 | tf_op jit(solution)/shard_map/ppermute | solution.py:379
  247.5 23.9 %collective-permute-start.34 = (bf16[32,32,128]{2,1,0:T(8,128)(2,1)}, bf16[32,32,128]{2,1,0:T(8,128)(2,1)}, u32[]{:S(2)}, u32[]{:S(2)}) collective-permute-start(bf16[32,32,128]{2,1,0:T(8,128)(2,1)} %get-tuple-element.149), channel_id=1, source_target_pairs={{0,2},{1,3},{2,0},{3,1},{4,6},{5,7},{6,4},{7,5},{8,10},{9,11},{10,... | collective-permute-start | bytes 786440 | tf_op jit(solution)/shard_map/ppermute | solution.py:379
  247.8 33.1 %collective-permute-start.35 = (bf16[32,32,128]{2,1,0:T(8,128)(2,1)}, bf16[32,32,128]{2,1,0:T(8,128)(2,1)}, u32[]{:S(2)}, u32[]{:S(2)}) collective-permute-start(bf16[32,32,128]{2,1,0:T(8,128)(2,1)} %get-tuple-element.150), channel_id=1, source_target_pairs={{0,4},{1,5},{2,6},{3,7},{4,0},{5,1},{6,2},{7,3},{8,12},{9,13},{10,... | collective-permute-start | bytes 786440 | tf_op jit(solution)/shard_map/ppermute | solution.py:379
  250.8 34.1 %collective-permute-start.36 = (bf16[32,32,128]{2,1,0:T(8,128)(2,1)}, bf16[32,32,128]{2,1,0:T(8,128)(2,1)}, u32[]{:S(2)}, u32[]{:S(2)}) collective-permute-start(bf16[32,32,128]{2,1,0:T(8,128)(2,1)} %get-tuple-element.151), channel_id=1, source_target_pairs={{0,5},{1,4},{2,7},{3,6},{4,1},{5,0},{6,3},{7,2},{8,13},{9,12},{10,... | collective-permute-start | bytes 786440 | tf_op jit(solution)/shard_map/ppermute | solution.py:379
  253.1 43.6 %collective-permute-start.37 = (bf16[32,32,128]{2,1,0:T(8,128)(2,1)}, bf16[32,32,128]{2,1,0:T(8,128)(2,1)}, u32[]{:S(2)}, u32[]{:S(2)}) collective-permute-start(bf16[32,32,128]{2,1,0:T(8,128)(2,1)} %get-tuple-element.152), channel_id=1, source_target_pairs={{0,6},{1,7},{2,4},{3,5},{4,2},{5,3},{6,0},{7,1},{8,14},{9,15},{10,... | collective-permute-start | bytes 786440 | tf_op jit(solution)/shard_map/ppermute | solution.py:379
  255.4 43.9 %collective-permute-start.38 = (bf16[32,32,128]{2,1,0:T(8,128)(2,1)}, bf16[32,32,128]{2,1,0:T(8,128)(2,1)}, u32[]{:S(2)}, u32[]{:S(2)}) collective-permute-start(bf16[32,32,128]{2,1,0:T(8,128)(2,1)} %get-tuple-element.153), channel_id=1, source_target_pairs={{0,7},{1,6},{2,5},{3,4},{4,3},{5,2},{6,1},{7,0},{8,15},{9,14},{10,... | collective-permute-start | bytes 786440 | tf_op jit(solution)/shard_map/ppermute | solution.py:379
  271.4 30.4 %collective-permute-start.39 = (bf16[32,32,128]{2,1,0:T(8,128)(2,1)}, bf16[32,32,128]{2,1,0:T(8,128)(2,1)S(1)}, u32[]{:S(2)}, u32[]{:S(2)}) collective-permute-start(bf16[32,32,128]{2,1,0:T(8,128)(2,1)} %get-tuple-element.154), channel_id=1, source_target_pairs={{0,3},{1,2},{2,1},{3,0},{4,7},{5,6},{6,5},{7,4},{8,11},{9,10},{10,... | collective-permute-start | bytes 786440 | tf_op jit(solution)/shard_map/ppermute | solution.py:379
  280.9 21.7 %collective-permute-start.40 = (bf16[32,32,128]{2,1,0:T(8,128)(2,1)}, bf16[32,32,128]{2,1,0:T(8,128)(2,1)S(1)}, u32[]{:S(2)}, u32[]{:S(2)}) collective-permute-start(bf16[32,32,128]{2,1,0:T(8,128)(2,1)} %get-tuple-element.157), channel_id=1, source_target_pairs={{0,2},{1,3},{2,0},{3,1},{4,6},{5,7},{6,4},{7,5},{8,10},{9,11},{10,... | collective-permute-start | bytes 786440 | tf_op jit(solution)/shard_map/ppermute | solution.py:379
  284.9 49.6 %collective-permute-start.41 = (bf16[32,32,128]{2,1,0:T(8,128)(2,1)}, bf16[32,32,128]{2,1,0:T(8,128)(2,1)S(1)}, u32[]{:S(2)}, u32[]{:S(2)}) collective-permute-start(bf16[32,32,128]{2,1,0:T(8,128)(2,1)} %get-tuple-element.158), channel_id=1, source_target_pairs={{0,4},{1,5},{2,6},{3,7},{4,0},{5,1},{6,2},{7,3},{8,12},{9,13},{10,... | collective-permute-start | bytes 786440 | tf_op jit(solution)/shard_map/ppermute | solution.py:379
  296.7 37.9 %collective-permute-start.42 = (bf16[32,32,128]{2,1,0:T(8,128)(2,1)}, bf16[32,32,128]{2,1,0:T(8,128)(2,1)S(1)}, u32[]{:S(2)}, u32[]{:S(2)}) collective-permute-start(bf16[32,32,128]{2,1,0:T(8,128)(2,1)} %get-tuple-element.159), channel_id=1, source_target_pairs={{0,5},{1,4},{2,7},{3,6},{4,1},{5,0},{6,3},{7,2},{8,13},{9,12},{10,... | collective-permute-start | bytes 786440 | tf_op jit(solution)/shard_map/ppermute | solution.py:379
  299.3 38.0 %collective-permute-start.43 = (bf16[32,32,128]{2,1,0:T(8,128)(2,1)}, bf16[32,32,128]{2,1,0:T(8,128)(2,1)S(1)}, u32[]{:S(2)}, u32[]{:S(2)}) collective-permute-start(bf16[32,32,128]{2,1,0:T(8,128)(2,1)} %get-tuple-element.160), channel_id=1, source_target_pairs={{0,6},{1,7},{2,4},{3,5},{4,2},{5,3},{6,0},{7,1},{8,14},{9,15},{10,... | collective-permute-start | bytes 786440 | tf_op jit(solution)/shard_map/ppermute | solution.py:379
  301.8 35.4 %collective-permute-start.44 = (bf16[32,32,128]{2,1,0:T(8,128)(2,1)}, bf16[32,32,128]{2,1,0:T(8,128)(2,1)S(1)}, u32[]{:S(2)}, u32[]{:S(2)}) collective-permute-start(bf16[32,32,128]{2,1,0:T(8,128)(2,1)} %get-tuple-element.161), channel_id=1, source_target_pairs={{0,7},{1,6},{2,5},{3,4},{4,3},{5,2},{6,1},{7,0},{8,15},{9,14},{10,... | collective-permute-start | bytes 786440 | tf_op jit(solution)/shard_map/ppermute | solution.py:379
  302.6 36.8 %collective-permute-start.45 = (bf16[32,32,128]{2,1,0:T(8,128)(2,1)}, bf16[32,32,128]{2,1,0:T(8,128)(2,1)S(1)}, u32[]{:S(2)}, u32[]{:S(2)}) collective-permute-start(bf16[32,32,128]{2,1,0:T(8,128)(2,1)} %get-tuple-element.162), channel_id=1, source_target_pairs={{0,3},{1,2},{2,1},{3,0},{4,7},{5,6},{6,5},{7,4},{8,11},{9,10},{10,... | collective-permute-start | bytes 786440 | tf_op jit(solution)/shard_map/ppermute | solution.py:379
  334.5 7.3 %collective-permute-start.46 = (bf16[32,16,128]{2,1,0:T(8,128)(2,1)}, bf16[32,16,128]{2,1,0:T(8,128)(2,1)S(1)}, u32[]{:S(2)}, u32[]{:S(2)}) collective-permute-start(bf16[32,16,128]{2,1,0:T(8,128)(2,1)} %get-tuple-element.168), channel_id=1, source_target_pairs={{0,2},{1,3},{2,0},{3,1},{4,6},{5,7},{6,4},{7,5},{8,10},{9,11},{10,... | collective-permute-start | bytes 393224 | tf_op jit(solution)/shard_map/ppermute | solution.py:379
  334.6 37.8 %collective-permute-start.47 = (bf16[32,16,128]{2,1,0:T(8,128)(2,1)}, bf16[32,16,128]{2,1,0:T(8,128)(2,1)}, u32[]{:S(2)}, u32[]{:S(2)}) collective-permute-start(bf16[32,16,128]{2,1,0:T(8,128)(2,1)} %get-tuple-element.169), channel_id=1, source_target_pairs={{0,4},{1,5},{2,6},{3,7},{4,0},{5,1},{6,2},{7,3},{8,12},{9,13},{10,... | collective-permute-start | bytes 393224 | tf_op jit(solution)/shard_map/ppermute | solution.py:379
  337.2 47.7 %collective-permute-start.48 = (bf16[32,16,128]{2,1,0:T(8,128)(2,1)}, bf16[32,16,128]{2,1,0:T(8,128)(2,1)}, u32[]{:S(2)}, u32[]{:S(2)}) collective-permute-start(bf16[32,16,128]{2,1,0:T(8,128)(2,1)} %get-tuple-element.170), channel_id=1, source_target_pairs={{0,5},{1,4},{2,7},{3,6},{4,1},{5,0},{6,3},{7,2},{8,13},{9,12},{10,... | collective-permute-start | bytes 393224 | tf_op jit(solution)/shard_map/ppermute | solution.py:379
  337.2 47.7 %collective-permute-start.49 = (bf16[32,16,128]{2,1,0:T(8,128)(2,1)}, bf16[32,16,128]{2,1,0:T(8,128)(2,1)}, u32[]{:S(2)}, u32[]{:S(2)}) collective-permute-start(bf16[32,16,128]{2,1,0:T(8,128)(2,1)} %get-tuple-element.171), channel_id=1, source_target_pairs={{0,6},{1,7},{2,4},{3,5},{4,2},{5,3},{6,0},{7,1},{8,14},{9,15},{10,... | collective-permute-start | bytes 393224 | tf_op jit(solution)/shard_map/ppermute | solution.py:379
  339.4 45.6 %collective-permute-start.50 = (bf16[32,16,128]{2,1,0:T(8,128)(2,1)}, bf16[32,16,128]{2,1,0:T(8,128)(2,1)}, u32[]{:S(2)}, u32[]{:S(2)}) collective-permute-start(bf16[32,16,128]{2,1,0:T(8,128)(2,1)} %get-tuple-element.172), channel_id=1, source_target_pairs={{0,7},{1,6},{2,5},{3,4},{4,3},{5,2},{6,1},{7,0},{8,15},{9,14},{10,... | collective-permute-start | bytes 393224 | tf_op jit(solution)/shard_map/ppermute | solution.py:379
  341.8 43.2 %collective-permute-start.51 = (bf16[32,16,128]{2,1,0:T(8,128)(2,1)}, bf16[32,16,128]{2,1,0:T(8,128)(2,1)}, u32[]{:S(2)}, u32[]{:S(2)}) collective-permute-start(bf16[32,16,128]{2,1,0:T(8,128)(2,1)} %get-tuple-element.173), channel_id=1, source_target_pairs={{0,3},{1,2},{2,1},{3,0},{4,7},{5,6},{6,5},{7,4},{8,11},{9,10},{10,... | collective-permute-start | bytes 393224 | tf_op jit(solution)/shard_map/ppermute | solution.py:379
  372.5 28.0 %collective-permute-start.52 = (bf16[32,32,128]{2,1,0:T(8,128)(2,1)}, bf16[32,32,128]{2,1,0:T(8,128)(2,1)S(1)}, u32[]{:S(2)}, u32[]{:S(2)}) collective-permute-start(bf16[32,32,128]{2,1,0:T(8,128)(2,1)} %get-tuple-element.177), channel_id=1, source_target_pairs={{0,2},{1,3},{2,0},{3,1},{4,6},{5,7},{6,4},{7,5},{8,10},{9,11},{10,... | collective-permute-start | bytes 786440 | tf_op jit(solution)/shard_map/ppermute | solution.py:379
  392.4 8.1 %collective-permute-start.58 = (bf16[32,16,128]{2,1,0:T(8,128)(2,1)}, bf16[32,16,128]{2,1,0:T(8,128)(2,1)S(1)}, u32[]{:S(2)}, u32[]{:S(2)}) collective-permute-start(bf16[32,16,128]{2,1,0:T(8,128)(2,1)} %get-tuple-element.186), channel_id=1, source_target_pairs={{0,2},{1,3},{2,0},{3,1},{4,6},{5,7},{6,4},{7,5},{8,10},{9,11},{10,... | collective-permute-start | bytes 393224 | tf_op jit(solution)/shard_map/ppermute | solution.py:379
  394.2 32.8 %collective-permute-start.53 = (bf16[32,32,128]{2,1,0:T(8,128)(2,1)}, bf16[32,32,128]{2,1,0:T(8,128)(2,1)S(1)}, u32[]{:S(2)}, u32[]{:S(2)}) collective-permute-start(bf16[32,32,128]{2,1,0:T(8,128)(2,1)} %get-tuple-element.178), channel_id=1, source_target_pairs={{0,4},{1,5},{2,6},{3,7},{4,0},{5,1},{6,2},{7,3},{8,12},{9,13},{10,... | collective-permute-start | bytes 786440 | tf_op jit(solution)/shard_map/ppermute | solution.py:379
  395.5 37.8 %collective-permute-start.54 = (bf16[32,32,128]{2,1,0:T(8,128)(2,1)}, bf16[32,32,128]{2,1,0:T(8,128)(2,1)S(1)}, u32[]{:S(2)}, u32[]{:S(2)}) collective-permute-start(bf16[32,32,128]{2,1,0:T(8,128)(2,1)} %get-tuple-element.179), channel_id=1, source_target_pairs={{0,5},{1,4},{2,7},{3,6},{4,1},{5,0},{6,3},{7,2},{8,13},{9,12},{10,... | collective-permute-start | bytes 786440 | tf_op jit(solution)/shard_map/ppermute | solution.py:379
  396.4 37.0 %collective-permute-start.55 = (bf16[32,32,128]{2,1,0:T(8,128)(2,1)}, bf16[32,32,128]{2,1,0:T(8,128)(2,1)}, u32[]{:S(2)}, u32[]{:S(2)}) collective-permute-start(bf16[32,32,128]{2,1,0:T(8,128)(2,1)} %get-tuple-element.180), channel_id=1, source_target_pairs={{0,6},{1,7},{2,4},{3,5},{4,2},{5,3},{6,0},{7,1},{8,14},{9,15},{10,... | collective-permute-start | bytes 786440 | tf_op jit(solution)/shard_map/ppermute | solution.py:379
  400.4 35.4 %collective-permute-start.56 = (bf16[32,32,128]{2,1,0:T(8,128)(2,1)}, bf16[32,32,128]{2,1,0:T(8,128)(2,1)}, u32[]{:S(2)}, u32[]{:S(2)}) collective-permute-start(bf16[32,32,128]{2,1,0:T(8,128)(2,1)} %get-tuple-element.181), channel_id=1, source_target_pairs={{0,7},{1,6},{2,5},{3,4},{4,3},{5,2},{6,1},{7,0},{8,15},{9,14},{10,... | collective-permute-start | bytes 786440 | tf_op jit(solution)/shard_map/ppermute | solution.py:379
  400.4 38.0 %collective-permute-start.57 = (bf16[32,32,128]{2,1,0:T(8,128)(2,1)}, bf16[32,32,128]{2,1,0:T(8,128)(2,1)}, u32[]{:S(2)}, u32[]{:S(2)}) collective-permute-start(bf16[32,32,128]{2,1,0:T(8,128)(2,1)} %get-tuple-element.182), channel_id=1, source_target_pairs={{0,3},{1,2},{2,1},{3,0},{4,7},{5,6},{6,5},{7,4},{8,11},{9,10},{10,... | collective-permute-start | bytes 786440 | tf_op jit(solution)/shard_map/ppermute | solution.py:379
  427.0 40.1 %collective-permute-start.59 = (bf16[32,16,128]{2,1,0:T(8,128)(2,1)}, bf16[32,16,128]{2,1,0:T(8,128)(2,1)S(1)}, u32[]{:S(2)}, u32[]{:S(2)}) collective-permute-start(bf16[32,16,128]{2,1,0:T(8,128)(2,1)} %get-tuple-element.187), channel_id=1, source_target_pairs={{0,4},{1,5},{2,6},{3,7},{4,0},{5,1},{6,2},{7,3},{8,12},{9,13},{10,... | collective-permute-start | bytes 393224 | tf_op jit(solution)/shard_map/ppermute | solution.py:379
  433.3 33.8 %collective-permute-start.60 = (bf16[32,16,128]{2,1,0:T(8,128)(2,1)}, bf16[32,16,128]{2,1,0:T(8,128)(2,1)S(1)}, u32[]{:S(2)}, u32[]{:S(2)}) collective-permute-start(bf16[32,16,128]{2,1,0:T(8,128)(2,1)} %get-tuple-element.188), channel_id=1, source_target_pairs={{0,5},{1,4},{2,7},{3,6},{4,1},{5,0},{6,3},{7,2},{8,13},{9,12},{10,... | collective-permute-start | bytes 393224 | tf_op jit(solution)/shard_map/ppermute | solution.py:379
  433.3 33.8 %collective-permute-start.61 = (bf16[32,16,128]{2,1,0:T(8,128)(2,1)}, bf16[32,16,128]{2,1,0:T(8,128)(2,1)S(1)}, u32[]{:S(2)}, u32[]{:S(2)}) collective-permute-start(bf16[32,16,128]{2,1,0:T(8,128)(2,1)} %get-tuple-element.189), channel_id=1, source_target_pairs={{0,6},{1,7},{2,4},{3,5},{4,2},{5,3},{6,0},{7,1},{8,14},{9,15},{10,... | collective-permute-start | bytes 393224 | tf_op jit(solution)/shard_map/ppermute | solution.py:379
  435.9 31.3 %collective-permute-start.62 = (bf16[32,16,128]{2,1,0:T(8,128)(2,1)}, bf16[32,16,128]{2,1,0:T(8,128)(2,1)S(1)}, u32[]{:S(2)}, u32[]{:S(2)}) collective-permute-start(bf16[32,16,128]{2,1,0:T(8,128)(2,1)} %get-tuple-element.190), channel_id=1, source_target_pairs={{0,7},{1,6},{2,5},{3,4},{4,3},{5,2},{6,1},{7,0},{8,15},{9,14},{10,... | collective-permute-start | bytes 393224 | tf_op jit(solution)/shard_map/ppermute | solution.py:379
  438.4 28.8 %collective-permute-start.63 = (bf16[32,16,128]{2,1,0:T(8,128)(2,1)}, bf16[32,16,128]{2,1,0:T(8,128)(2,1)S(1)}, u32[]{:S(2)}, u32[]{:S(2)}) collective-permute-start(bf16[32,16,128]{2,1,0:T(8,128)(2,1)} %get-tuple-element.191), channel_id=1, source_target_pairs={{0,3},{1,2},{2,1},{3,0},{4,7},{5,6},{6,5},{7,4},{8,11},{9,10},{10,... | collective-permute-start | bytes 393224 | tf_op jit(solution)/shard_map/ppermute | solution.py:379
  (90 other events, 1580.9 us)

commit v9 on v5

--- a/solution.py
+++ b/solution.py
@@ -279,6 +279,7 @@
 
 
 PARAMS = pltpu.CompilerParams(vmem_limit_bytes=60 * 1024 * 1024)
+SMALL = pl.CostEstimate(flops=1024, bytes_accessed=1024, transcendentals=0)
 ANYWHERE = pl.BlockSpec(memory_space=pl.ANY)
 
 
@@ -312,11 +313,7 @@
         out_shape=[pltpu.HBM(shape, jnp.bfloat16) for shape in shapes]
         + [pltpu.HBM((shots, LANES), jnp.float32)],
         compiler_params=PARAMS,
-        cost_estimate=pl.CostEstimate(
-            flops=4 * F * shots * rows * samples,
-            bytes_accessed=3 * 2 * shots * rows * samples + table.size * 2,
-            transcendentals=0,
-        ),
+        cost_estimate=SMALL,
         name="spectra_" + mode,
     )(meta, delays, *fields, table, after, *[array for array, _ in partners])
     return spectra, energy
@@ -362,9 +359,7 @@
         ),
         out_shape=[pltpu.HBM(shape, jnp.bfloat16) for shape in shapes],
         compiler_params=PARAMS,
-        cost_estimate=pl.CostEstimate(
-            flops=8 * shots * size, bytes_accessed=4 * size + 2 * table.size, transcendentals=size
-        ),
+        cost_estimate=SMALL,
         name="shrink",
     )(meta, table, level, after, *[array for array, _ in spectra])
 
@@ -406,11 +401,7 @@
         out_shape=out_shape,
         input_output_aliases={} if onto is None else {len(operands) - 1: 0},
         compiler_params=PARAMS,
-        cost_estimate=pl.CostEstimate(
-            flops=4 * F * shots * rows * samples,
-            bytes_accessed=4 * F * shots * rows + 2 * table.size + 4 * shots * rows * samples,
-            transcendentals=0,
-        ),
+        cost_estimate=SMALL,
         name="update",
     )(*operands)
 
@@ -421,10 +412,17 @@
 
 def sent(array, distance):
     peers = lax.axis_size("shot")
-    if distance < peers // 2:
-        groups = [[i, i ^ distance] for i in range(peers) if i < i ^ distance]
+    if distance == 1:
+        groups = [[i, i ^ 1] for i in range(0, peers, 2)]
         return lax.all_gather(array, "shot", axis_index_groups=groups), distance
     return lax.ppermute(array, "shot", [(i, i ^ distance) for i in range(peers)]), 0
+
+
+def sent_all(arrays, distances):
+    half = lax.axis_size("shot") // 2
+    order = sorted(range(len(arrays)), key=lambda index: distances[index] < half)
+    moved = {i: sent(arrays[i], distances[i]) if distances[i] else held(arrays[i]) for i in order}
+    return [moved[index] for index in range(len(arrays))]
 
 
 def held(array):
@@ -457,17 +455,21 @@
 
 
 def turns(steps):
-    for turn in range(steps + 4):
-        if turn == 0:
-            yield "own", 0
-            yield "other", 0
-        if turn + 1 < steps:
-            yield "other", turn + 1
-        if 0 < turn < steps:
-            yield "own", turn
-        for name, lag in (("shrink", 1), ("update own", 3), ("update other", 4)):
-            if 0 <= turn - lag < steps:
-                yield name, turn - lag
+    work = [("own", 0), ("other", 0)]
+    work += [("other", 1), ("own", 1)] if steps > 1 else []
+    work += [("shrink", 0)]
+    work += [("other", step) for step in range(2, min(4, steps))]
+    for step in range(2, steps + 1):
+        work += [("own", step)] if step < steps else []
+        work += [("shrink", step - 1)]
+        work += [("update own", step - 2)]
+        work += [("update other", step - 3)] if step > 2 else []
+        work += [("other", step + 2)] if step + 2 < steps else []
+    for step in range(max(0, steps - 1), steps):
+        work += [("update other", step - 1)] if step > 1 else []
+        work += [("update own", step), ("update other", step)]
+    done = {step for name, step in work if name == "update other"}
+    return work + [("update other", step) for step in range(steps) if step not in done]
 
 
 def in_pairs(estimate, observed, delays, thresholds, rows):
@@ -485,7 +487,8 @@
     forward, inverse = (jnp.asarray(table) for table in time_tables(samples, chips))
     table = jnp.asarray(shot_table(total))
     levels = jnp.tile(lax.dynamic_slice_in_dim(thresholds, rank // 2 * share, share), 2)[None, :]
-    early = edges(part_of_halves(estimate, 0, rows), part_of_halves(observed, 0, rows))
+    ahead_steps = min(2, steps)
+    early = edges(*[part_of_halves(array, 0, ahead_steps * rows) for array in (estimate, observed)])
     late = None
     last, updated, energy = levels, None, 0.0
     packed, ahead, behind, passed = {}, {}, {}, {}
@@ -493,17 +496,14 @@
         side = 1 if name.endswith("own") else 2
         block = lambda meta, side=side, step=step: meta[side] * steps + step
         if name in ("own", "other"):
-            edge_block = block
-            if step == 0:
-                edge_block = lambda meta, side=side: meta[side]
-            else:
-                edge_block = lambda meta, side=side, step=step: meta[side] * (steps - 1) + step - 1
-            direct = step == 0
-            mode = "apart" if direct else "joined" if name == "own" else "packed"
+            first, count = (0, ahead_steps) if step < ahead_steps else (ahead_steps, steps - ahead_steps)
+            place = step - first
+            edge_block = lambda meta, side=side, count=count, place=place: meta[side] * count + place
+            mode = "apart" if step == 0 else "joined" if name == "own" else "packed"
             spectra, power = spectra_of(
                 meta,
                 delays,
-                (estimate, observed, *(late if step else early)),
+                (estimate, observed, *(late if step >= ahead_steps else early)),
                 forward,
                 block,
                 edge_block,
@@ -517,32 +517,19 @@
             energy = energy + power
             if mode == "packed":
                 packed[step] = sent(spectra[0], 1)
-            elif mode == "joined":
-                far = [sent(spectra[chip], 2 * chip) for chip in range(1, chips)]
-                ahead[step] = [held(spectra[0]), *far]
             elif name == "own":
-                far = [sent(spectra[chip], 2 * chip) for chip in range(1, chips)]
-                ahead[step] = [held(spectra[0]), *far]
-                held_estimate, held_observed, _ = lax.optimization_barrier(
-                    (estimate, observed, power)
-                )
-                if steps > 1:
-                    late = edges(
-                        part_of_halves(held_estimate, rows, receivers // 2),
-                        part_of_halves(held_observed, rows, receivers // 2),
-                    )
+                ahead[step] = sent_all(spectra, range(0, peers, 2))
             else:
-                other = [sent(spectra[chip], 2 * chip + 1) for chip in range(chips)]
-                ahead[step] = [array for pair in zip(ahead[step], other) for array in pair]
+                other = sent_all(spectra, range(1, peers, 2))
+                ahead[step] = [item for pair in zip(ahead[step], other) for item in pair]
+            if late is None and step == 1 and steps > ahead_steps:
+                later = lax.optimization_barrier((estimate, observed, power))
+                late = edges(*[part_of_halves(a, ahead_steps * rows, receivers // 2) for a in later[:2]])
         elif name == "shrink":
             direct = step == steps - 1
             shrunk = shrunk_of(meta, ahead.pop(step), table, levels, not direct, last)
             last = shrunk[0]
-            unit = 1 if direct else 2
-            behind[step] = [
-                sent(array, unit * index) if index else held(array)
-                for index, array in enumerate(shrunk)
-            ]
+            behind[step] = sent_all(shrunk, range(0, peers, 1 if direct else 2))
         elif name == "update own":
             direct = step == steps - 1
             restored = behind.pop(step)
@@ -617,7 +604,7 @@
     peers = lax.axis_size("shot")
     rows = min(16, receivers)
     paired = (
-        peers > 1
+        peers >= 4
         and peers & (peers - 1) == 0
         and (4 * F // peers) % LANES == 0
         and receivers % (2 * rows) == 0

time: 575 us -> 506 us (0.88)
  blocking collectives: 93 us -> 15.1 us
  starting transfers between devices: 82.6 us -> 109 us
  waiting for transfers between devices: 199 us -> 178 us
    all_gather x6 -> x2, blocking collectives: 83.4 us -> 5.21 us  [sent(): return (lax.all_gather(array, 'shot', axis_index_groups=groups), distance)]
    ppermute x20 -> x30, starting transfers between devices: 70.3 us -> 101 us  [sent(): lax.ppermute(array, 'shot', [(i, i ^ distance) for i in range(peers)])]
    ppermute x20 -> x30, waiting for transfers between devices: 192 us -> 175 us  [sent(): lax.ppermute(array, 'shot', [(i, i ^ distance) for i in range(peers)])]
  transfers between devices with their start and end apart: 36 -> 40, of which waited for: 9 -> 14; matrix products, arithmetic and copies ran while one was open for 0% -> 1% of each run, Pallas kernels for 25% -> 25%
where the time goes in v9:
time: 506 us; the launch traced here: 502 us
  waiting for transfers between devices  178 us (35%)
  Pallas kernels  169 us (33%)
  starting transfers between devices  109 us (22%)
  blocking collectives  15.1 us (3%)
  local copies, waits for them, and re-layouts  14.7 us (3%)
  between operations  14.6 us (3%)
    ppermute x30, waiting for transfers between devices, sent(): lax.ppermute(array, 'shot', [(i, i ^ distance) for i in range(peers)])  175 us
    ppermute x30, starting transfers between devices, sent(): lax.ppermute(array, 'shot', [(i, i ^ distance) for i in range(peers)])  101 us
    pallas_call x8, Pallas kernels, spectra_of(): pl.pallas_call(functools.partial(spectra_kernel, len(shapes), mode == 'pa...  80.1 us
    pallas_call x4, Pallas kernels, shrunk_of(): pl.pallas_call(functools.partial(shots_kernel, len(spectra)), grid_spec=p...  47.3 us
    pallas_call x8, Pallas kernels, updated_of(): pl.pallas_call(functools.partial(update_kernel, len(restored), passes), g...  41.6 us
  transfers between devices with their start and end apart: 40, of which 14 were waited for; matrix products, arithmetic and copies ran while one was open for 1% of the time, Pallas kernels for 25%

profile of v9, /device:TPU:0, one launch (start us, length us, event | category | flops | bytes accessed | tf_op | source)
XLA Modules:
  0.0 502.0 jit_solution(5034550844145179236)
XLA Ops:
  7.2 1.0 fusion.3
  8.2 1.1 fusion.2
  9.3 2.4 collective-permute-start
  11.8 1.3 collective-permute-start.1
  14.5 3.1 collective-permute-done.1.after_ref
  18.3 9.8 %spectra_apart.2 = (bf16[1,32,16,256]{3,2,1,0:T(8,128)(2,1)}, bf16[1,32,16,256]{3,2,1,0:T(8,128)(2,1)}, bf16[1,32,16,256]{3,2,1,0:T(8,128)(2,1)}, bf16[1,32,16,256]{3,2,1,0:T(8,128)(2,1)}, f32[32,128]{1,0:T(8,128)}) custom-call(s32[11]{0:T(128)} %pad_add_fusion.meta_ref, s32[256]{0:T(256)} %delay_ref.15, bf16[32,128,1024]{2,1,0:T(8,128)(2,1)} %est_ref.15, ...), custom_call_target="tpu_custom_call" | custom-call | flops 1024 | bytes 1024 | tf_op jit(solution)/shard_map/spectra_apart/pallas_call | solution.py:298
  28.1 9.8 %spectra_apart.3 = (bf16[1,32,16,256]{3,2,1,0:T(8,128)(2,1)}, bf16[1,32,16,256]{3,2,1,0:T(8,128)(2,1)}, bf16[1,32,16,256]{3,2,1,0:T(8,128)(2,1)}, bf16[1,32,16,256]{3,2,1,0:T(8,128)(2,1)}, f32[32,128]{1,0:T(8,128)}) custom-call(s32[11]{0:T(128)} %pad_add_fusion.meta_ref, s32[256]{0:T(256)} %delay_ref.15, bf16[32,128,1024]{2,1,0:T(8,128)(2,1)} %est_ref.15, ...), custom_call_target="tpu_custom_call" | custom-call | flops 1024 | bytes 1024 | tf_op jit(solution)/shard_map/spectra_apart/pallas_call | solution.py:298
  37.9 9.8 %spectra_packed.3 = (bf16[4,32,16,256]{3,2,1,0:T(8,128)(2,1)}, f32[32,128]{1,0:T(8,128)}) custom-call(s32[11]{0:T(128)} %pad_add_fusion.meta_ref, s32[256]{0:T(256)} %delay_ref.15, bf16[32,128,1024]{2,1,0:T(8,128)(2,1)} %est_ref.15, bf16[32,128,1024]{2,1,0:T(8,128)(2,1)} %obs_ref.15, bf16[3,64,1024]{2,1,0:T(8,128)(2,1)} %copy-done.2, ...), custom_call_target="tpu_custom_call" | custom-call | flops 1024 | bytes 1024 | tf_op jit(solution)/shard_map/spectra_packed/pallas_call | solution.py:298
  47.8 5.8 %collective-permute-start.4 = (bf16[1,32,16,256]{3,2,1,0:T(8,128)(2,1)S(1)}, bf16[1,32,16,256]{3,2,1,0:T(8,128)(2,1)S(1)}, u32[]{:S(2)}, u32[]{:S(2)}) collective-permute-start(bf16[1,32,16,256]{3,2,1,0:T(8,128)(2,1)S(1)} %copy-done.51), channel_id=1, source_target_pairs={{0,2},{1,3},{2,0},{3,1},{4,6},{5,7},{6,4},{7,5},{8,10},{9,11},{10,... | collective-permute-start | bytes 786440 | tf_op jit(solution)/shard_map/ppermute | solution.py:418
  53.6 2.6 collective-permute-start.6
  57.2 1.1 fusion
  58.3 3.2 collective-permute-start.2
  61.5 1.3 collective-permute-start.3
  62.8 1.7 collective-permute-done.4.refs_2_
  65.1 9.3 %collective-permute-start.7 = (bf16[1,32,16,256]{3,2,1,0:T(8,128)(2,1)}, bf16[1,32,16,256]{3,2,1,0:T(8,128)(2,1)S(1)}, u32[]{:S(2)}, u32[]{:S(2)}) collective-permute-start(bf16[1,32,16,256]{3,2,1,0:T(8,128)(2,1)} %get-tuple-element.85), channel_id=1, source_target_pairs={{0,5},{1,4},{2,7},{3,6},{4,1},{5,0},{6,3},{7,2},{8,13},{9,12},{10,... | collective-permute-start | bytes 786440 | tf_op jit(solution)/shard_map/ppermute | solution.py:418
  74.5 3.0 collective-permute-start.9
  77.5 2.3 all-gather.1
  79.8 10.4 %spectra_joined.3 = (bf16[2,32,16,256]{3,2,1,0:T(8,128)(2,1)}, bf16[2,32,16,256]{3,2,1,0:T(8,128)(2,1)}, bf16[2,32,16,256]{3,2,1,0:T(8,128)(2,1)}, bf16[2,32,16,256]{3,2,1,0:T(8,128)(2,1)}, f32[32,128]{1,0:T(8,128)}) custom-call(s32[11]{0:T(128)} %pad_add_fusion.meta_ref, s32[256]{0:T(256)} %delay_ref.15, bf16[32,128,1024]{2,1,0:T(8,128)(2,1)} %est_ref.15, ...), custom_call_target="tpu_custom_call" | custom-call | flops 1024 | bytes 1024 | tf_op jit(solution)/shard_map/spectra_joined/pallas_call | solution.py:298
  90.3 7.7 %collective-permute-done.7.refs_5_ = bf16[1,32,16,256]{3,2,1,0:T(8,128)(2,1)S(1)} collective-permute-done((bf16[1,32,16,256]{3,2,1,0:T(8,128)(2,1)}, bf16[1,32,16,256]{3,2,1,0:T(8,128)(2,1)S(1)}, u32[]{:S(2)}, u32[]{:S(2)}) %collective-permute-start.7) | collective-permute-done | bytes 262176 | tf_op jit(solution)/shard_map/ppermute | solution.py:418
  98.8 11.8 %shrink.4 = (bf16[2,32,16,256]{3,2,1,0:T(8,128)(2,1)}, bf16[2,32,16,256]{3,2,1,0:T(8,128)(2,1)}, bf16[2,32,16,256]{3,2,1,0:T(8,128)(2,1)}, bf16[2,32,16,256]{3,2,1,0:T(8,128)(2,1)}) custom-call(s32[11]{0:T(128)} %pad_add_fusion.meta_ref, bf16[512,256]{1,0:T(8,128)(2,1)} %constant.49.clone.table_ref, f32[1,256]{1,0:T(1,128)} %bitcast.45, ...), custom_call_target="tpu_custom_call" | custom-call | flops 1024 | bytes 1024 | tf_op jit(solution)/shard_map/shrink/pallas_call | solution.py:350
  111.5 9.7 %spectra_packed.4 = (bf16[4,32,16,256]{3,2,1,0:T(8,128)(2,1)}, f32[32,128]{1,0:T(8,128)}) custom-call(s32[11]{0:T(128)} %pad_add_fusion.meta_ref, s32[256]{0:T(256)} %delay_ref.15, bf16[32,128,1024]{2,1,0:T(8,128)(2,1)} %est_ref.15, bf16[32,128,1024]{2,1,0:T(8,128)(2,1)} %obs_ref.15, bf16[3,64,1024]{2,1,0:T(8,128)(2,1)} %copy-done, ...), custom_call_target="tpu_custom_call" | custom-call | flops 1024 | bytes 1024 | tf_op jit(solution)/shard_map/spectra_packed/pallas_call | solution.py:298
  121.3 9.8 %spectra_packed.5 = (bf16[4,32,16,256]{3,2,1,0:T(8,128)(2,1)}, f32[32,128]{1,0:T(8,128)}) custom-call(s32[11]{0:T(128)} %pad_add_fusion.meta_ref, s32[256]{0:T(256)} %delay_ref.15, bf16[32,128,1024]{2,1,0:T(8,128)(2,1)} %est_ref.15, bf16[32,128,1024]{2,1,0:T(8,128)(2,1)} %obs_ref.15, bf16[3,64,1024]{2,1,0:T(8,128)(2,1)} %copy-done, ...), custom_call_target="tpu_custom_call" | custom-call | flops 1024 | bytes 1024 | tf_op jit(solution)/shard_map/spectra_packed/pallas_call | solution.py:298
  131.4 6.2 %collective-permute-start.10 = (bf16[2,32,16,256]{3,2,1,0:T(8,128)(2,1)S(1)}, bf16[2,32,16,256]{3,2,1,0:T(8,128)(2,1)S(1)}, u32[]{:S(2)}, u32[]{:S(2)}) collective-permute-start(bf16[2,32,16,256]{3,2,1,0:T(8,128)(2,1)S(1)} %copy-done.44), channel_id=1, source_target_pairs={{0,2},{1,3},{2,0},{3,1},{4,6},{5,7},{6,4},{7,5},{8,10},{9,11},{10,... | collective-permute-start | bytes 1572872 | tf_op jit(solution)/shard_map/ppermute | solution.py:418
  137.6 4.8 collective-permute-start.11
  142.3 1.4 collective-permute-start.12
  144.3 2.4 collective-permute-start.14
  146.7 4.7 collective-permute-done.10.refs_1_
  151.4 14.6 %collective-permute-start.15 = (bf16[2,32,16,256]{3,2,1,0:T(8,128)(2,1)}, bf16[2,32,16,256]{3,2,1,0:T(8,128)(2,1)S(1)}, u32[]{:S(2)}, u32[]{:S(2)}) collective-permute-start(bf16[2,32,16,256]{3,2,1,0:T(8,128)(2,1)} %get-tuple-element.100), channel_id=1, source_target_pairs={{0,6},{1,7},{2,4},{3,5},{4,2},{5,3},{6,0},{7,1},{8,14},{9,15},{10,... | collective-permute-start | bytes 1572872 | tf_op jit(solution)/shard_map/ppermute | solution.py:418
  166.0 10.4 %spectra_joined.4 = (bf16[2,32,16,256]{3,2,1,0:T(8,128)(2,1)}, bf16[2,32,16,256]{3,2,1,0:T(8,128)(2,1)}, bf16[2,32,16,256]{3,2,1,0:T(8,128)(2,1)}, bf16[2,32,16,256]{3,2,1,0:T(8,128)(2,1)}, f32[32,128]{1,0:T(8,128)}) custom-call(s32[11]{0:T(128)} %pad_add_fusion.meta_ref, s32[256]{0:T(256)} %delay_ref.15, bf16[32,128,1024]{2,1,0:T(8,128)(2,1)} %est_ref.15, ...), custom_call_target="tpu_custom_call" | custom-call | flops 1024 | bytes 1024 | tf_op jit(solution)/shard_map/spectra_joined/pallas_call | solution.py:298
  176.4 2.7 collective-permute-done.12.refs_3_
  179.9 11.8 %shrink.5 = (bf16[2,32,16,256]{3,2,1,0:T(8,128)(2,1)}, bf16[2,32,16,256]{3,2,1,0:T(8,128)(2,1)}, bf16[2,32,16,256]{3,2,1,0:T(8,128)(2,1)}, bf16[2,32,16,256]{3,2,1,0:T(8,128)(2,1)}) custom-call(s32[11]{0:T(128)} %pad_add_fusion.meta_ref, bf16[512,256]{1,0:T(8,128)(2,1)} %constant.49.clone.table_ref, f32[1,256]{1,0:T(1,128)} %bitcast.46, ...), custom_call_target="tpu_custom_call" | custom-call | flops 1024 | bytes 1024 | tf_op jit(solution)/shard_map/shrink/pallas_call | solution.py:350
  191.7 30.8 %collective-permute-done.14.refs_2_ = bf16[2,32,16,256]{3,2,1,0:T(8,128)(2,1)S(1)} collective-permute-done((bf16[2,32,16,256]{3,2,1,0:T(8,128)(2,1)}, bf16[2,32,16,256]{3,2,1,0:T(8,128)(2,1)S(1)}, u32[]{:S(2)}, u32[]{:S(2)}) %collective-permute-start.14) | collective-permute-done | bytes 524320 | tf_op jit(solution)/shard_map/ppermute | solution.py:418
  223.4 5.4 %update.8 = (f32[32,128,1024]{2,1,0:T(8,128)}, f32[8,128]{1,0:T(8,128)}, bf16[4,32,16,256]{3,2,1,0:T(8,128)(2,1)}) custom-call(s32[11]{0:T(128)} %pad_add_fusion.meta_ref, bf16[1024,1024]{1,0:T(8,128)(2,1)} %constant.48.clone.table_ref, bf16[2,32,16,256]{3,2,1,0:T(8,128)(2,1)} %get-tuple-element.97._.refs_0_, ...), custom_call_target="tpu_custom_call" | custom-call | flops 1024 | bytes 1024 | tf_op jit(solution)/shard_map/update/pallas_call | solution.py:392
  228.9 11.7 %collective-permute-start.16 = (bf16[2,32,16,256]{3,2,1,0:T(8,128)(2,1)}, bf16[2,32,16,256]{3,2,1,0:T(8,128)(2,1)S(1)}, u32[]{:S(2)}, u32[]{:S(2)}) collective-permute-start(bf16[2,32,16,256]{3,2,1,0:T(8,128)(2,1)} %get-tuple-element.105), channel_id=1, source_target_pairs={{0,2},{1,3},{2,0},{3,1},{4,6},{5,7},{6,4},{7,5},{8,10},{9,11},{10,... | collective-permute-start | bytes 1572872 | tf_op jit(solution)/shard_map/ppermute | solution.py:418
  240.6 2.4 collective-permute-start.18
  243.0 1.0 collective-permute-start.19
  245.0 18.0 %collective-permute-done.16.refs_1_ = bf16[2,32,16,256]{3,2,1,0:T(8,128)(2,1)S(1)} collective-permute-done((bf16[2,32,16,256]{3,2,1,0:T(8,128)(2,1)}, bf16[2,32,16,256]{3,2,1,0:T(8,128)(2,1)S(1)}, u32[]{:S(2)}, u32[]{:S(2)}) %collective-permute-start.16) | collective-permute-done | bytes 524320 | tf_op jit(solution)/shard_map/ppermute | solution.py:418
  263.0 2.2 collective-permute-start.21
  265.2 10.4 %spectra_joined.5 = (bf16[2,32,16,256]{3,2,1,0:T(8,128)(2,1)}, bf16[2,32,16,256]{3,2,1,0:T(8,128)(2,1)}, bf16[2,32,16,256]{3,2,1,0:T(8,128)(2,1)}, bf16[2,32,16,256]{3,2,1,0:T(8,128)(2,1)}, f32[32,128]{1,0:T(8,128)}) custom-call(s32[11]{0:T(128)} %pad_add_fusion.meta_ref, s32[256]{0:T(256)} %delay_ref.15, bf16[32,128,1024]{2,1,0:T(8,128)(2,1)} %est_ref.15, ...), custom_call_target="tpu_custom_call" | custom-call | flops 1024 | bytes 1024 | tf_op jit(solution)/shard_map/spectra_joined/pallas_call | solution.py:298
  275.6 3.4 collective-permute-done.17.refs_2_
  280.0 11.9 %shrink.6 = (bf16[2,32,16,256]{3,2,1,0:T(8,128)(2,1)}, bf16[2,32,16,256]{3,2,1,0:T(8,128)(2,1)}, bf16[2,32,16,256]{3,2,1,0:T(8,128)(2,1)}, bf16[2,32,16,256]{3,2,1,0:T(8,128)(2,1)}) custom-call(s32[11]{0:T(128)} %pad_add_fusion.meta_ref, bf16[512,256]{1,0:T(8,128)(2,1)} %constant.49.clone.table_ref, f32[1,256]{1,0:T(1,128)} %bitcast.47, ...), custom_call_target="tpu_custom_call" | custom-call | flops 1024 | bytes 1024 | tf_op jit(solution)/shard_map/shrink/pallas_call | solution.py:350
  291.9 32.1 %collective-permute-done.20.refs_2_ = bf16[2,32,16,256]{3,2,1,0:T(8,128)(2,1)S(1)} collective-permute-done((bf16[2,32,16,256]{3,2,1,0:T(8,128)(2,1)}, bf16[2,32,16,256]{3,2,1,0:T(8,128)(2,1)S(1)}, u32[]{:S(2)}, u32[]{:S(2)}) %collective-permute-start.20) | collective-permute-done | bytes 524320 | tf_op jit(solution)/shard_map/ppermute | solution.py:418
  325.0 5.4 %update.9 = (f32[32,128,1024]{2,1,0:T(8,128)}, f32[8,128]{1,0:T(8,128)}, bf16[4,32,16,256]{3,2,1,0:T(8,128)(2,1)}) custom-call(s32[11]{0:T(128)} %pad_add_fusion.meta_ref, bf16[1024,1024]{1,0:T(8,128)(2,1)} %constant.48.clone.table_ref, bf16[2,32,16,256]{3,2,1,0:T(8,128)(2,1)} %get-tuple-element.108._.refs_0_, ...), custom_call_target="tpu_custom_call", output_to_operand_aliasing={{0}: (7, {})} | custom-call | flops 1024 | bytes 1024 | tf_op jit(solution)/shard_map/update/pallas_call | solution.py:392
  330.5 10.6 %collective-permute-start.22 = (bf16[2,32,16,256]{3,2,1,0:T(8,128)(2,1)}, bf16[2,32,16,256]{3,2,1,0:T(8,128)(2,1)S(1)}, u32[]{:S(2)}, u32[]{:S(2)}) collective-permute-start(bf16[2,32,16,256]{3,2,1,0:T(8,128)(2,1)} %get-tuple-element.118), channel_id=1, source_target_pairs={{0,2},{1,3},{2,0},{3,1},{4,6},{5,7},{6,4},{7,5},{8,10},{9,11},{10,... | collective-permute-start | bytes 1572872 | tf_op jit(solution)/shard_map/ppermute | solution.py:418
  341.1 2.4 collective-permute-start.24
  343.5 1.0 collective-permute-start.25
  345.5 19.0 %collective-permute-done.22.refs_1_ = bf16[2,32,16,256]{3,2,1,0:T(8,128)(2,1)S(1)} collective-permute-done((bf16[2,32,16,256]{3,2,1,0:T(8,128)(2,1)}, bf16[2,32,16,256]{3,2,1,0:T(8,128)(2,1)S(1)}, u32[]{:S(2)}, u32[]{:S(2)}) %collective-permute-start.22) | collective-permute-done | bytes 524320 | tf_op jit(solution)/shard_map/ppermute | solution.py:418
  365.3 5.0 update.10
  370.3 9.3 %collective-permute-done.23.refs_2_ = bf16[2,32,16,256]{3,2,1,0:T(8,128)(2,1)S(1)} collective-permute-done((bf16[2,32,16,256]{3,2,1,0:T(8,128)(2,1)}, bf16[2,32,16,256]{3,2,1,0:T(8,128)(2,1)S(1)}, u32[]{:S(2)}, u32[]{:S(2)}) %collective-permute-start.23) | collective-permute-done | bytes 524320 | tf_op jit(solution)/shard_map/ppermute | solution.py:418
  380.5 11.9 %shrink.7 = (bf16[1,32,16,256]{3,2,1,0:T(8,128)(2,1)}, bf16[1,32,16,256]{3,2,1,0:T(8,128)(2,1)}, bf16[1,32,16,256]{3,2,1,0:T(8,128)(2,1)}, bf16[1,32,16,256]{3,2...) custom-call(s32[11]{0:T(128)} %pad_add_fusion.meta_ref, ...), custom_call_target="tpu_custom_call" | custom-call | flops 1024 | bytes 1024 | tf_op jit(solution)/shard_map/shrink/pallas_call | solution.py:350
  392.4 32.1 %collective-permute-done.26.refs_2_ = bf16[2,32,16,256]{3,2,1,0:T(8,128)(2,1)S(1)} collective-permute-done((bf16[2,32,16,256]{3,2,1,0:T(8,128)(2,1)}, bf16[2,32,16,256]{3,2,1,0:T(8,128)(2,1)S(1)}, u32[]{:S(2)}, u32[]{:S(2)}) %collective-permute-start.26) | collective-permute-done | bytes 524320 | tf_op jit(solution)/shard_map/ppermute | solution.py:418
  425.6 5.6 %update.11 = (f32[32,128,1024]{2,1,0:T(8,128)}, f32[8,128]{1,0:T(8,128)}, bf16[4,32,16,256]{3,2,1,0:T(8,128)(2,1)}) custom-call(s32[11]{0:T(128)} %pad_add_fusion.meta_ref, bf16[1024,1024]{1,0:T(8,128)(2,1)} %constant.48.clone.table_ref, bf16[1,32,16,256]{3,2,1,0:T(8,128)(2,1)} %get-tuple-element.121._.refs_0_, ...), custom_call_target="tpu_custom_call", output_to_operand_aliasing={{0}: (7, {})} | custom-call | flops 1024 | bytes 1024 | tf_op jit(solution)/shard_map/update/pallas_call | solution.py:392
  431.2 9.4 %collective-permute-start.28 = (bf16[1,32,16,256]{3,2,1,0:T(8,128)(2,1)}, bf16[1,32,16,256]{3,2,1,0:T(8,128)(2,1)S(1)}, u32[]{:S(2)}, u32[]{:S(2)}) collective-permute-start(bf16[1,32,16,256]{3,2,1,0:T(8,128)(2,1)} %get-tuple-element.133), channel_id=1, source_target_pairs={{0,2},{1,3},{2,0},{3,1},{4,6},{5,7},{6,4},{7,5},{8,10},{9,11},{10,... | collective-permute-start | bytes 786440 | tf_op jit(solution)/shard_map/ppermute | solution.py:418
  440.7 9.9 %psum.7 = f32[32]{0:T(128)S(1)} all-reduce(f32[32]{0:T(128)S(1)} %add_reduce_fusion), channel_id=1, replica_groups=mesh['patch'=4,'shot'=8] {'patch'}, use_global_device_ids=true, to_apply=%region_1.2 | all-reduce | flops 32 | bytes 256 | tf_op jit(solution)/shard_map/psum | solution.py:614
  450.7 2.4 collective-permute-start.30
  453.1 1.8 collective-permute-start.32
  454.9 1.5 collective-permute-start.33
  456.9 2.9 all-gather.7
  459.8 5.0 update.12
  464.8 5.0 update.13
  469.8 8.4 %collective-permute-done.29.refs_2_ = bf16[1,32,16,256]{3,2,1,0:T(8,128)(2,1)S(1)} collective-permute-done((bf16[1,32,16,256]{3,2,1,0:T(8,128)(2,1)}, bf16[1,32,16,256]{3,2,1,0:T(8,128)(2,1)S(1)}, u32[]{:S(2)}, u32[]{:S(2)}) %collective-permute-start.29) | collective-permute-done | bytes 262176 | tf_op jit(solution)/shard_map/ppermute | solution.py:418
  479.1 5.1 %update.14 = (f32[32,128,1024]{2,1,0:T(8,128)}, f32[8,128]{1,0:T(8,128)}) custom-call(s32[11]{0:T(128)} %pad_add_fusion.meta_ref, bf16[1024,1024]{1,0:T(8,128)(2,1)} %constant.48.clone.table_ref, f32[8,128]{1,0:T(8,128)} %get-tuple-element.132._, bf16[1,32,16,256]{3,2,1,0:T(8,128)(2,1)} %get-tuple-element.121._.refs_0_, ...), custom_call_target="tpu_custom_call", output_to_operand_aliasing={{0}: (7, {})} | custom-call | flops 1024 | bytes 1024 | tf_op jit(solution)/shard_map/update/pallas_call | solution.py:392
  484.2 5.0 collective-permute-done.32.refs_2_
  490.0 5.1 %update.15 = (f32[32,128,1024]{2,1,0:T(8,128)}, f32[8,128]{1,0:T(8,128)}) custom-call(s32[11]{0:T(128)} %pad_add_fusion.meta_ref, bf16[1024,1024]{1,0:T(8,128)(2,1)} %constant.48.clone.table_ref, f32[8,128]{1,0:T(8,128)} %get-tuple-element.137._, bf16[2,1,32,16,256]{4,3,2,1,0:T(8,128)(2,1)} %bitcast.31, ...), custom_call_target="tpu_custom_call", output_to_operand_aliasing={{0}: (7, {})} | custom-call | flops 1024 | bytes 1024 | tf_op jit(solution)/shard_map/update/pallas_call | solution.py:392
  (163 shorter events, 17.5 us)
Async XLA Ops:
  7.2 72.7 %all-gather.15.cloned.1.call-start = ((), (), s32[]{:S(2)}) async-start(), calls=%async_computation | async-start | bytes 3145728 | tf_op jit(solution)/shard_map/all_gather | solution.py:417
  9.3 5.1 %collective-permute-start = (bf16[3,64,1024]{2,1,0:T(8,128)(2,1)S(1)}, bf16[3,64,1024]{2,1,0:T(8,128)(2,1)S(1)}, u32[]{:S(2)}, u32[]{:S(2)}) collective-permute-start(bf16[3,64,1024]{2,1,0:T(8,128)(2,1)S(1)} %pad_maximum_fusion), channel_id=1, source_target_pairs={{0,1},{1,2},{2,3},{3,4},{4,5},{5,6},{6,7},{8,9},{9,10},{10,11},{11... | collective-permute-start | bytes 1179656 | tf_op jit(solution)/shard_map/ppermute | solution.py:448
  11.8 5.8 %collective-permute-start.1 = (bf16[3,64,1024]{2,1,0:T(8,128)(2,1)S(1)}, bf16[3,64,1024]{2,1,0:T(8,128)(2,1)S(1)}, u32[]{:S(2)}, u32[]{:S(2)}) collective-permute-start(bf16[3,64,1024]{2,1,0:T(8,128)(2,1)S(1)} %pad_maximum_fusion.1), channel_id=1, source_target_pairs={{1,0},{2,1},{3,2},{4,3},{5,4},{6,5},{7,6},{9,8},{10,9},{11,10},{12... | collective-permute-start | bytes 1179656 | tf_op jit(solution)/shard_map/ppermute | solution.py:448
  37.9 15.7 %copy-start.50 = (bf16[1,32,16,256]{3,2,1,0:T(8,128)(2,1)S(1)}, bf16[1,32,16,256]{3,2,1,0:T(8,128)(2,1)}, u32[]{:S(2)}) copy-start(bf16[1,32,16,256]{3,2,1,0:T(8,128)(2,1)} %get-tuple-element.84) | copy-start | bytes 786436
  37.9 18.3 %copy-start.49 = (bf16[1,32,16,256]{3,2,1,0:T(8,128)(2,1)S(1)}, bf16[1,32,16,256]{3,2,1,0:T(8,128)(2,1)}, u32[]{:S(2)}) copy-start(bf16[1,32,16,256]{3,2,1,0:T(8,128)(2,1)} %get-tuple-element.86) | copy-start | bytes 786436
  37.9 39.6 %copy-start.29 = (bf16[1,32,16,256]{3,2,1,0:T(8,128)(2,1)S(1)}, bf16[1,32,16,256]{3,2,1,0:T(8,128)(2,1)}, u32[]{:S(2)}) copy-start(bf16[1,32,16,256]{3,2,1,0:T(8,128)(2,1)} %get-tuple-element.81) | copy-start | bytes 786436
  47.7 118.3 %all-gather.17.cloned.1.call-start = ((), (), s32[]{:S(2)}) async-start(), calls=%async_computation.1 | async-start | bytes 3145728 | tf_op jit(solution)/shard_map/all_gather | solution.py:417
  47.8 16.7 %collective-permute-start.4 = (bf16[1,32,16,256]{3,2,1,0:T(8,128)(2,1)S(1)}, bf16[1,32,16,256]{3,2,1,0:T(8,128)(2,1)S(1)}, u32[]{:S(2)}, u32[]{:S(2)}) collective-permute-start(bf16[1,32,16,256]{3,2,1,0:T(8,128)(2,1)S(1)} %copy-done.51), channel_id=1, source_target_pairs={{0,2},{1,3},{2,0},{3,1},{4,6},{5,7},{6,4},{7,5},{8,10},{9,11},{10,... | collective-permute-start | bytes 786440 | tf_op jit(solution)/shard_map/ppermute | solution.py:418
  53.6 11.6 %collective-permute-start.6 = (bf16[1,32,16,256]{3,2,1,0:T(8,128)(2,1)S(1)}, bf16[1,32,16,256]{3,2,1,0:T(8,128)(2,1)S(1)}, u32[]{:S(2)}, u32[]{:S(2)}) collective-permute-start(bf16[1,32,16,256]{3,2,1,0:T(8,128)(2,1)S(1)} %copy-done.50), channel_id=1, source_target_pairs={{0,4},{1,5},{2,6},{3,7},{4,0},{5,1},{6,2},{7,3},{8,12},{9,13},{10,... | collective-permute-start | bytes 786440 | tf_op jit(solution)/shard_map/ppermute | solution.py:418
  56.2 18.3 %collective-permute-start.8 = (bf16[1,32,16,256]{3,2,1,0:T(8,128)(2,1)S(1)}, bf16[1,32,16,256]{3,2,1,0:T(8,128)(2,1)S(1)}, u32[]{:S(2)}, u32[]{:S(2)}) collective-permute-start(bf16[1,32,16,256]{3,2,1,0:T(8,128)(2,1)S(1)} %copy-done.49), channel_id=1, source_target_pairs={{0,6},{1,7},{2,4},{3,5},{4,2},{5,3},{6,0},{7,1},{8,14},{9,15},{10,... | collective-permute-start | bytes 786440 | tf_op jit(solution)/shard_map/ppermute | solution.py:418
  58.3 52.3 %collective-permute-start.2 = (bf16[3,64,1024]{2,1,0:T(8,128)(2,1)S(1)}, bf16[3,64,1024]{2,1,0:T(8,128)(2,1)S(1)}, u32[]{:S(2)}, u32[]{:S(2)}) collective-permute-start(bf16[3,64,1024]{2,1,0:T(8,128)(2,1)S(1)} %pad_maximum_fusion.2), channel_id=1, source_target_pairs={{0,1},{1,2},{2,3},{3,4},{4,5},{5,6},{6,7},{8,9},{9,10},{10,11},{11... | collective-permute-start | bytes 1179656 | tf_op jit(solution)/shard_map/ppermute | solution.py:448
  61.5 49.1 %collective-permute-start.3 = (bf16[3,64,1024]{2,1,0:T(8,128)(2,1)S(1)}, bf16[3,64,1024]{2,1,0:T(8,128)(2,1)S(1)}, u32[]{:S(2)}, u32[]{:S(2)}) collective-permute-start(bf16[3,64,1024]{2,1,0:T(8,128)(2,1)S(1)} %pad_maximum_fusion.3), channel_id=1, source_target_pairs={{1,0},{2,1},{3,2},{4,3},{5,4},{6,5},{7,6},{9,8},{10,9},{11,10},{12... | collective-permute-start | bytes 1179656 | tf_op jit(solution)/shard_map/ppermute | solution.py:448
  64.5 25.7 %copy-start.30 = (bf16[1,32,16,256]{3,2,1,0:T(8,128)(2,1)}, bf16[1,32,16,256]{3,2,1,0:T(8,128)(2,1)S(1)}, u32[]{:S(2)}) copy-start(bf16[1,32,16,256]{3,2,1,0:T(8,128)(2,1)S(1)} %collective-permute-done.4.refs_2_) | copy-start | bytes 786436
  64.5 25.8 %collective-permute-start.5 = (bf16[1,32,16,256]{3,2,1,0:T(8,128)(2,1)}, bf16[1,32,16,256]{3,2,1,0:T(8,128)(2,1)S(1)}, u32[]{:S(2)}, u32[]{:S(2)}) collective-permute-start(bf16[1,32,16,256]{3,2,1,0:T(8,128)(2,1)} %get-tuple-element.83), channel_id=1, source_target_pairs={{0,3},{1,2},{2,1},{3,0},{4,7},{5,6},{6,5},{7,4},{8,11},{9,10},{10,... | collective-permute-start | bytes 786440 | tf_op jit(solution)/shard_map/ppermute | solution.py:418
  65.1 25.1 %copy-start.31 = (bf16[1,32,16,256]{3,2,1,0:T(8,128)(2,1)}, bf16[1,32,16,256]{3,2,1,0:T(8,128)(2,1)S(1)}, u32[]{:S(2)}) copy-start(bf16[1,32,16,256]{3,2,1,0:T(8,128)(2,1)S(1)} %collective-permute-done.6.refs_4_) | copy-start | bytes 786436
  65.1 32.9 %collective-permute-start.7 = (bf16[1,32,16,256]{3,2,1,0:T(8,128)(2,1)}, bf16[1,32,16,256]{3,2,1,0:T(8,128)(2,1)S(1)}, u32[]{:S(2)}, u32[]{:S(2)}) collective-permute-start(bf16[1,32,16,256]{3,2,1,0:T(8,128)(2,1)} %get-tuple-element.85), channel_id=1, source_target_pairs={{0,5},{1,4},{2,7},{3,6},{4,1},{5,0},{6,3},{7,2},{8,13},{9,12},{10,... | collective-permute-start | bytes 786440 | tf_op jit(solution)/shard_map/ppermute | solution.py:418
  74.5 15.8 %copy-start.32 = (bf16[1,32,16,256]{3,2,1,0:T(8,128)(2,1)}, bf16[1,32,16,256]{3,2,1,0:T(8,128)(2,1)S(1)}, u32[]{:S(2)}) copy-start(bf16[1,32,16,256]{3,2,1,0:T(8,128)(2,1)S(1)} %collective-permute-done.8.refs_6_) | copy-start | bytes 786436
  74.5 23.6 %collective-permute-start.9 = (bf16[1,32,16,256]{3,2,1,0:T(8,128)(2,1)}, bf16[1,32,16,256]{3,2,1,0:T(8,128)(2,1)S(1)}, u32[]{:S(2)}, u32[]{:S(2)}) collective-permute-start(bf16[1,32,16,256]{3,2,1,0:T(8,128)(2,1)} %get-tuple-element.87), channel_id=1, source_target_pairs={{0,7},{1,6},{2,5},{3,4},{4,3},{5,2},{6,1},{7,0},{8,15},{9,14},{10,... | collective-permute-start | bytes 786440 | tf_op jit(solution)/shard_map/ppermute | solution.py:418
  121.2 144.0 %all-gather.19.cloned.1.call-start = ((), (), s32[]{:S(2)}) async-start(), calls=%async_computation.2 | async-start | bytes 3145728 | tf_op jit(solution)/shard_map/all_gather | solution.py:417
  131.2 234.1 %all-gather.21.cloned.1.call-start = ((), (), s32[]{:S(2)}) async-start(), calls=%async_computation.3 | async-start | bytes 3145728 | tf_op jit(solution)/shard_map/all_gather | solution.py:417
  131.4 20.0 %collective-permute-start.10 = (bf16[2,32,16,256]{3,2,1,0:T(8,128)(2,1)S(1)}, bf16[2,32,16,256]{3,2,1,0:T(8,128)(2,1)S(1)}, u32[]{:S(2)}, u32[]{:S(2)}) collective-permute-start(bf16[2,32,16,256]{3,2,1,0:T(8,128)(2,1)S(1)} %copy-done.44), channel_id=1, source_target_pairs={{0,2},{1,3},{2,0},{3,1},{4,6},{5,7},{6,4},{7,5},{8,10},{9,11},{10,... | collective-permute-start | bytes 1572872 | tf_op jit(solution)/shard_map/ppermute | solution.py:418
  137.6 38.8 %collective-permute-start.11 = (bf16[2,32,16,256]{3,2,1,0:T(8,128)(2,1)}, bf16[2,32,16,256]{3,2,1,0:T(8,128)(2,1)S(1)}, u32[]{:S(2)}, u32[]{:S(2)}) collective-permute-start(bf16[2,32,16,256]{3,2,1,0:T(8,128)(2,1)} %get-tuple-element.95), channel_id=1, source_target_pairs={{0,4},{1,5},{2,6},{3,7},{4,0},{5,1},{6,2},{7,3},{8,12},{9,13},{10,... | collective-permute-start | bytes 1572872 | tf_op jit(solution)/shard_map/ppermute | solution.py:418
  142.3 36.7 %collective-permute-start.12 = (bf16[2,32,16,256]{3,2,1,0:T(8,128)(2,1)}, bf16[2,32,16,256]{3,2,1,0:T(8,128)(2,1)S(1)}, u32[]{:S(2)}, u32[]{:S(2)}) collective-permute-start(bf16[2,32,16,256]{3,2,1,0:T(8,128)(2,1)} %get-tuple-element.96), channel_id=1, source_target_pairs={{0,6},{1,7},{2,4},{3,5},{4,2},{5,3},{6,0},{7,1},{8,14},{9,15},{10,... | collective-permute-start | bytes 1572872 | tf_op jit(solution)/shard_map/ppermute | solution.py:418
  143.7 48.0 %collective-permute-start.13 = (bf16[2,32,16,256]{3,2,1,0:T(8,128)(2,1)}, bf16[2,32,16,256]{3,2,1,0:T(8,128)(2,1)S(1)}, u32[]{:S(2)}, u32[]{:S(2)}) collective-permute-start(bf16[2,32,16,256]{3,2,1,0:T(8,128)(2,1)} %get-tuple-element.98), channel_id=1, source_target_pairs={{0,2},{1,3},{2,0},{3,1},{4,6},{5,7},{6,4},{7,5},{8,10},{9,11},{10,... | collective-permute-start | bytes 1572872 | tf_op jit(solution)/shard_map/ppermute | solution.py:418
  144.3 78.2 %collective-permute-start.14 = (bf16[2,32,16,256]{3,2,1,0:T(8,128)(2,1)}, bf16[2,32,16,256]{3,2,1,0:T(8,128)(2,1)S(1)}, u32[]{:S(2)}, u32[]{:S(2)}) collective-permute-start(bf16[2,32,16,256]{3,2,1,0:T(8,128)(2,1)} %get-tuple-element.99), channel_id=1, source_target_pairs={{0,4},{1,5},{2,6},{3,7},{4,0},{5,1},{6,2},{7,3},{8,12},{9,13},{10,... | collective-permute-start | bytes 1572872 | tf_op jit(solution)/shard_map/ppermute | solution.py:418
  151.4 25.0 %copy-start.15 = (bf16[2,32,16,256]{3,2,1,0:T(8,128)(2,1)}, bf16[2,32,16,256]{3,2,1,0:T(8,128)(2,1)S(1)}, u32[]{:S(2)}) copy-start(bf16[2,32,16,256]{3,2,1,0:T(8,128)(2,1)S(1)} %collective-permute-done.10.refs_1_) | copy-start | bytes 1572868
  151.4 71.1 %collective-permute-start.15 = (bf16[2,32,16,256]{3,2,1,0:T(8,128)(2,1)}, bf16[2,32,16,256]{3,2,1,0:T(8,128)(2,1)S(1)}, u32[]{:S(2)}, u32[]{:S(2)}) collective-permute-start(bf16[2,32,16,256]{3,2,1,0:T(8,128)(2,1)} %get-tuple-element.100), channel_id=1, source_target_pairs={{0,6},{1,7},{2,4},{3,5},{4,2},{5,3},{6,0},{7,1},{8,14},{9,15},{10,... | collective-permute-start | bytes 1572872 | tf_op jit(solution)/shard_map/ppermute | solution.py:418
  191.7 30.8 %copy-start.8 = (bf16[2,32,16,256]{3,2,1,0:T(8,128)(2,1)}, bf16[2,32,16,256]{3,2,1,0:T(8,128)(2,1)S(1)}, u32[]{:S(2)}) copy-start(bf16[2,32,16,256]{3,2,1,0:T(8,128)(2,1)S(1)} %collective-permute-done.13.refs_1_) | copy-start | bytes 1572868
  228.9 231.0 %all-gather.23.cloned.1.call-start = ((), (), s32[]{:S(2)}) async-start(), calls=%async_computation.4 | async-start | bytes 3145728 | tf_op jit(solution)/shard_map/all_gather | solution.py:417
  228.9 34.1 %collective-permute-start.16 = (bf16[2,32,16,256]{3,2,1,0:T(8,128)(2,1)}, bf16[2,32,16,256]{3,2,1,0:T(8,128)(2,1)S(1)}, u32[]{:S(2)}, u32[]{:S(2)}) collective-permute-start(bf16[2,32,16,256]{3,2,1,0:T(8,128)(2,1)} %get-tuple-element.105), channel_id=1, source_target_pairs={{0,2},{1,3},{2,0},{3,1},{4,6},{5,7},{6,4},{7,5},{8,10},{9,11},{10,... | collective-permute-start | bytes 1572872 | tf_op jit(solution)/shard_map/ppermute | solution.py:418
  240.6 38.4 %collective-permute-start.17 = (bf16[2,32,16,256]{3,2,1,0:T(8,128)(2,1)}, bf16[2,32,16,256]{3,2,1,0:T(8,128)(2,1)S(1)}, u32[]{:S(2)}, u32[]{:S(2)}) collective-permute-start(bf16[2,32,16,256]{3,2,1,0:T(8,128)(2,1)} %get-tuple-element.106), channel_id=1, source_target_pairs={{0,4},{1,5},{2,6},{3,7},{4,0},{5,1},{6,2},{7,3},{8,12},{9,13},{10,... | collective-permute-start | bytes 1572872 | tf_op jit(solution)/shard_map/ppermute | solution.py:418
  240.6 38.4 %collective-permute-start.18 = (bf16[2,32,16,256]{3,2,1,0:T(8,128)(2,1)}, bf16[2,32,16,256]{3,2,1,0:T(8,128)(2,1)S(1)}, u32[]{:S(2)}, u32[]{:S(2)}) collective-permute-start(bf16[2,32,16,256]{3,2,1,0:T(8,128)(2,1)} %get-tuple-element.107), channel_id=1, source_target_pairs={{0,6},{1,7},{2,4},{3,5},{4,2},{5,3},{6,0},{7,1},{8,14},{9,15},{10,... | collective-permute-start | bytes 1572872 | tf_op jit(solution)/shard_map/ppermute | solution.py:418
  243.0 48.8 %collective-permute-start.19 = (bf16[2,32,16,256]{3,2,1,0:T(8,128)(2,1)}, bf16[2,32,16,256]{3,2,1,0:T(8,128)(2,1)S(1)}, u32[]{:S(2)}, u32[]{:S(2)}) collective-permute-start(bf16[2,32,16,256]{3,2,1,0:T(8,128)(2,1)} %get-tuple-element.109), channel_id=1, source_target_pairs={{0,2},{1,3},{2,0},{3,1},{4,6},{5,7},{6,4},{7,5},{8,10},{9,11},{10,... | collective-permute-start | bytes 1572872 | tf_op jit(solution)/shard_map/ppermute | solution.py:418
  244.1 79.9 %collective-permute-start.20 = (bf16[2,32,16,256]{3,2,1,0:T(8,128)(2,1)}, bf16[2,32,16,256]{3,2,1,0:T(8,128)(2,1)S(1)}, u32[]{:S(2)}, u32[]{:S(2)}) collective-permute-start(bf16[2,32,16,256]{3,2,1,0:T(8,128)(2,1)} %get-tuple-element.110), channel_id=1, source_target_pairs={{0,4},{1,5},{2,6},{3,7},{4,0},{5,1},{6,2},{7,3},{8,12},{9,13},{10,... | collective-permute-start | bytes 1572872 | tf_op jit(solution)/shard_map/ppermute | solution.py:418
  263.0 12.6 %copy-start.12 = (bf16[2,32,16,256]{3,2,1,0:T(8,128)(2,1)}, bf16[2,32,16,256]{3,2,1,0:T(8,128)(2,1)S(1)}, u32[]{:S(2)}) copy-start(bf16[2,32,16,256]{3,2,1,0:T(8,128)(2,1)S(1)} %collective-permute-done.16.refs_1_) | copy-start | bytes 1572868
  263.0 61.0 %collective-permute-start.21 = (bf16[2,32,16,256]{3,2,1,0:T(8,128)(2,1)}, bf16[2,32,16,256]{3,2,1,0:T(8,128)(2,1)S(1)}, u32[]{:S(2)}, u32[]{:S(2)}) collective-permute-start(bf16[2,32,16,256]{3,2,1,0:T(8,128)(2,1)} %get-tuple-element.111), channel_id=1, source_target_pairs={{0,6},{1,7},{2,4},{3,5},{4,2},{5,3},{6,0},{7,1},{8,14},{9,15},{10,... | collective-permute-start | bytes 1572872 | tf_op jit(solution)/shard_map/ppermute | solution.py:418
  291.9 32.1 %copy-start.5 = (bf16[2,32,16,256]{3,2,1,0:T(8,128)(2,1)}, bf16[2,32,16,256]{3,2,1,0:T(8,128)(2,1)S(1)}, u32[]{:S(2)}) copy-start(bf16[2,32,16,256]{3,2,1,0:T(8,128)(2,1)S(1)} %collective-permute-done.19.refs_1_) | copy-start | bytes 1572868
  330.4 134.4 %all-gather.25.cloned.1.call-start = ((), (), s32[]{:S(2)}) async-start(), calls=%async_computation.5 | async-start | bytes 3145728 | tf_op jit(solution)/shard_map/all_gather | solution.py:417
  330.5 34.0 %collective-permute-start.22 = (bf16[2,32,16,256]{3,2,1,0:T(8,128)(2,1)}, bf16[2,32,16,256]{3,2,1,0:T(8,128)(2,1)S(1)}, u32[]{:S(2)}, u32[]{:S(2)}) collective-permute-start(bf16[2,32,16,256]{3,2,1,0:T(8,128)(2,1)} %get-tuple-element.118), channel_id=1, source_target_pairs={{0,2},{1,3},{2,0},{3,1},{4,6},{5,7},{6,4},{7,5},{8,10},{9,11},{10,... | collective-permute-start | bytes 1572872 | tf_op jit(solution)/shard_map/ppermute | solution.py:418
  341.1 38.5 %collective-permute-start.23 = (bf16[2,32,16,256]{3,2,1,0:T(8,128)(2,1)}, bf16[2,32,16,256]{3,2,1,0:T(8,128)(2,1)S(1)}, u32[]{:S(2)}, u32[]{:S(2)}) collective-permute-start(bf16[2,32,16,256]{3,2,1,0:T(8,128)(2,1)} %get-tuple-element.119), channel_id=1, source_target_pairs={{0,4},{1,5},{2,6},{3,7},{4,0},{5,1},{6,2},{7,3},{8,12},{9,13},{10,... | collective-permute-start | bytes 1572872 | tf_op jit(solution)/shard_map/ppermute | solution.py:418
  341.1 38.5 %collective-permute-start.24 = (bf16[2,32,16,256]{3,2,1,0:T(8,128)(2,1)}, bf16[2,32,16,256]{3,2,1,0:T(8,128)(2,1)S(1)}, u32[]{:S(2)}, u32[]{:S(2)}) collective-permute-start(bf16[2,32,16,256]{3,2,1,0:T(8,128)(2,1)} %get-tuple-element.120), channel_id=1, source_target_pairs={{0,6},{1,7},{2,4},{3,5},{4,2},{5,3},{6,0},{7,1},{8,14},{9,15},{10,... | collective-permute-start | bytes 1572872 | tf_op jit(solution)/shard_map/ppermute | solution.py:418
  343.5 48.9 %collective-permute-start.25 = (bf16[2,32,16,256]{3,2,1,0:T(8,128)(2,1)}, bf16[2,32,16,256]{3,2,1,0:T(8,128)(2,1)S(1)}, u32[]{:S(2)}, u32[]{:S(2)}) collective-permute-start(bf16[2,32,16,256]{3,2,1,0:T(8,128)(2,1)} %get-tuple-element.122), channel_id=1, source_target_pairs={{0,2},{1,3},{2,0},{3,1},{4,6},{5,7},{6,4},{7,5},{8,10},{9,11},{10,... | collective-permute-start | bytes 1572872 | tf_op jit(solution)/shard_map/ppermute | solution.py:418
  344.6 79.9 %collective-permute-start.26 = (bf16[2,32,16,256]{3,2,1,0:T(8,128)(2,1)}, bf16[2,32,16,256]{3,2,1,0:T(8,128)(2,1)S(1)}, u32[]{:S(2)}, u32[]{:S(2)}) collective-permute-start(bf16[2,32,16,256]{3,2,1,0:T(8,128)(2,1)} %get-tuple-element.123), channel_id=1, source_target_pairs={{0,4},{1,5},{2,6},{3,7},{4,0},{5,1},{6,2},{7,3},{8,12},{9,13},{10,... | collective-permute-start | bytes 1572872 | tf_op jit(solution)/shard_map/ppermute | solution.py:418
  364.5 60.1 %collective-permute-start.27 = (bf16[2,32,16,256]{3,2,1,0:T(8,128)(2,1)}, bf16[2,32,16,256]{3,2,1,0:T(8,128)(2,1)S(1)}, u32[]{:S(2)}, u32[]{:S(2)}) collective-permute-start(bf16[2,32,16,256]{3,2,1,0:T(8,128)(2,1)} %get-tuple-element.124), channel_id=1, source_target_pairs={{0,6},{1,7},{2,4},{3,5},{4,2},{5,3},{6,0},{7,1},{8,14},{9,15},{10,... | collective-permute-start | bytes 1572872 | tf_op jit(solution)/shard_map/ppermute | solution.py:418
  392.4 32.1 %copy-start.4 = (bf16[2,32,16,256]{3,2,1,0:T(8,128)(2,1)}, bf16[2,32,16,256]{3,2,1,0:T(8,128)(2,1)S(1)}, u32[]{:S(2)}) copy-start(bf16[2,32,16,256]{3,2,1,0:T(8,128)(2,1)S(1)} %collective-permute-done.25.refs_1_) | copy-start | bytes 1572868
  425.5 15.1 %copy-start.36 = (f32[32,128]{1,0:T(8,128)S(1)}, f32[32,128]{1,0:T(8,128)}, u32[]{:S(2)}) copy-start(f32[32,128]{1,0:T(8,128)} %get-tuple-element.73._) | copy-start | bytes 49156
  425.5 15.1 %copy-start.37 = (f32[32,128]{1,0:T(8,128)S(1)}, f32[32,128]{1,0:T(8,128)}, u32[]{:S(2)}) copy-start(f32[32,128]{1,0:T(8,128)} %get-tuple-element.74._) | copy-start | bytes 49156
  425.5 15.1 %copy-start.38 = (f32[32,128]{1,0:T(8,128)S(1)}, f32[32,128]{1,0:T(8,128)}, u32[]{:S(2)}) copy-start(f32[32,128]{1,0:T(8,128)} %get-tuple-element.79._) | copy-start | bytes 49156
  425.5 15.1 %copy-start.39 = (f32[32,128]{1,0:T(8,128)S(1)}, f32[32,128]{1,0:T(8,128)}, u32[]{:S(2)}) copy-start(f32[32,128]{1,0:T(8,128)} %get-tuple-element.89._) | copy-start | bytes 49156
  425.5 15.1 %copy-start.40 = (f32[32,128]{1,0:T(8,128)S(1)}, f32[32,128]{1,0:T(8,128)}, u32[]{:S(2)}) copy-start(f32[32,128]{1,0:T(8,128)} %get-tuple-element.92._) | copy-start | bytes 49156
  425.5 15.1 %copy-start.41 = (f32[32,128]{1,0:T(8,128)S(1)}, f32[32,128]{1,0:T(8,128)}, u32[]{:S(2)}) copy-start(f32[32,128]{1,0:T(8,128)} %get-tuple-element.103._) | copy-start | bytes 49156
  425.5 15.1 %copy-start.42 = (f32[32,128]{1,0:T(8,128)S(1)}, f32[32,128]{1,0:T(8,128)}, u32[]{:S(2)}) copy-start(f32[32,128]{1,0:T(8,128)} %get-tuple-element.75._) | copy-start | bytes 49156
  425.5 15.1 %copy-start.43 = (f32[32,128]{1,0:T(8,128)S(1)}, f32[32,128]{1,0:T(8,128)}, u32[]{:S(2)}) copy-start(f32[32,128]{1,0:T(8,128)} %get-tuple-element.90._) | copy-start | bytes 49156
  425.5 25.2 %copy-start.48 = (bf16[1,32,16,256]{3,2,1,0:T(8,128)(2,1)S(1)}, bf16[1,32,16,256]{3,2,1,0:T(8,128)(2,1)}, u32[]{:S(2)}) copy-start(bf16[1,32,16,256]{3,2,1,0:T(8,128)(2,1)} %get-tuple-element.135) | copy-start | bytes 786436
  425.5 27.6 %copy-start.47 = (bf16[1,32,16,256]{3,2,1,0:T(8,128)(2,1)S(1)}, bf16[1,32,16,256]{3,2,1,0:T(8,128)(2,1)}, u32[]{:S(2)}) copy-start(bf16[1,32,16,256]{3,2,1,0:T(8,128)(2,1)} %get-tuple-element.139) | copy-start | bytes 786436
  425.6 27.6 %copy-start.46 = (bf16[1,32,16,256]{3,2,1,0:T(8,128)(2,1)S(1)}, bf16[1,32,16,256]{3,2,1,0:T(8,128)(2,1)}, u32[]{:S(2)}) copy-start(bf16[1,32,16,256]{3,2,1,0:T(8,128)(2,1)} %get-tuple-element.140) | copy-start | bytes 786436
  425.6 29.3 %copy-start.45 = (bf16[1,32,16,256]{3,2,1,0:T(8,128)(2,1)S(1)}, bf16[1,32,16,256]{3,2,1,0:T(8,128)(2,1)}, u32[]{:S(2)}) copy-start(bf16[1,32,16,256]{3,2,1,0:T(8,128)(2,1)} %get-tuple-element.141) | copy-start | bytes 786436
  425.6 31.4 %copy-start.28 = (bf16[1,32,16,256]{3,2,1,0:T(8,128)(2,1)S(1)}, bf16[1,32,16,256]{3,2,1,0:T(8,128)(2,1)}, u32[]{:S(2)}) copy-start(bf16[1,32,16,256]{3,2,1,0:T(8,128)(2,1)} %get-tuple-element.138) | copy-start | bytes 786436
  431.2 23.7 %collective-permute-start.28 = (bf16[1,32,16,256]{3,2,1,0:T(8,128)(2,1)}, bf16[1,32,16,256]{3,2,1,0:T(8,128)(2,1)S(1)}, u32[]{:S(2)}, u32[]{:S(2)}) collective-permute-start(bf16[1,32,16,256]{3,2,1,0:T(8,128)(2,1)} %get-tuple-element.133), channel_id=1, source_target_pairs={{0,2},{1,3},{2,0},{3,1},{4,6},{5,7},{6,4},{7,5},{8,10},{9,11},{10,... | collective-permute-start | bytes 786440 | tf_op jit(solution)/shard_map/ppermute | solution.py:418
  450.6 27.6 %collective-permute-start.29 = (bf16[1,32,16,256]{3,2,1,0:T(8,128)(2,1)}, bf16[1,32,16,256]{3,2,1,0:T(8,128)(2,1)S(1)}, u32[]{:S(2)}, u32[]{:S(2)}) collective-permute-start(bf16[1,32,16,256]{3,2,1,0:T(8,128)(2,1)} %get-tuple-element.134), channel_id=1, source_target_pairs={{0,4},{1,5},{2,6},{3,7},{4,0},{5,1},{6,2},{7,3},{8,12},{9,13},{10,... | collective-permute-start | bytes 786440 | tf_op jit(solution)/shard_map/ppermute | solution.py:418
  450.7 27.5 %collective-permute-start.30 = (bf16[1,32,16,256]{3,2,1,0:T(8,128)(2,1)S(1)}, bf16[1,32,16,256]{3,2,1,0:T(8,128)(2,1)S(1)}, u32[]{:S(2)}, u32[]{:S(2)}) collective-permute-start(bf16[1,32,16,256]{3,2,1,0:T(8,128)(2,1)S(1)} %copy-done.48), channel_id=1, source_target_pairs={{0,6},{1,7},{2,4},{3,5},{4,2},{5,3},{6,0},{7,1},{8,14},{9,15},{10,... | collective-permute-start | bytes 786440 | tf_op jit(solution)/shard_map/ppermute | solution.py:418
  453.1 31.1 %collective-permute-start.31 = (bf16[1,32,16,256]{3,2,1,0:T(8,128)(2,1)S(1)}, bf16[1,32,16,256]{3,2,1,0:T(8,128)(2,1)S(1)}, u32[]{:S(2)}, u32[]{:S(2)}) collective-permute-start(bf16[1,32,16,256]{3,2,1,0:T(8,128)(2,1)S(1)} %copy-done.47), channel_id=1, source_target_pairs={{0,3},{1,2},{2,1},{3,0},{4,7},{5,6},{6,5},{7,4},{8,11},{9,10},{10,... | collective-permute-start | bytes 786440 | tf_op jit(solution)/shard_map/ppermute | solution.py:418
  453.1 36.1 %collective-permute-start.32 = (bf16[1,32,16,256]{3,2,1,0:T(8,128)(2,1)S(1)}, bf16[1,32,16,256]{3,2,1,0:T(8,128)(2,1)S(1)}, u32[]{:S(2)}, u32[]{:S(2)}) collective-permute-start(bf16[1,32,16,256]{3,2,1,0:T(8,128)(2,1)S(1)} %copy-done.46), channel_id=1, source_target_pairs={{0,5},{1,4},{2,7},{3,6},{4,1},{5,0},{6,3},{7,2},{8,13},{9,12},{10,... | collective-permute-start | bytes 786440 | tf_op jit(solution)/shard_map/ppermute | solution.py:418
  454.9 34.3 %collective-permute-start.33 = (bf16[1,32,16,256]{3,2,1,0:T(8,128)(2,1)S(1)}, bf16[1,32,16,256]{3,2,1,0:T(8,128)(2,1)S(1)}, u32[]{:S(2)}, u32[]{:S(2)}) collective-permute-start(bf16[1,32,16,256]{3,2,1,0:T(8,128)(2,1)S(1)} %copy-done.45), channel_id=1, source_target_pairs={{0,7},{1,6},{2,5},{3,4},{4,3},{5,2},{6,1},{7,0},{8,15},{9,14},{10,... | collective-permute-start | bytes 786440 | tf_op jit(solution)/shard_map/ppermute | solution.py:418
  (28 other events, 71.5 us)
Sparse Core Ops, SparseCore 0:
  47.9 16.6 all-gather.14
  121.4 19.0 all-gather.16
  142.0 11.7 all-gather.18
  229.0 19.8 all-gather.20
  330.5 18.7 all-gather.22
  431.3 17.5 all-gather.24

commit v10 on v7

--- a/solution.py
+++ b/solution.py
@@ -195,7 +195,7 @@
         size = held * rows
         return pl.ds(pl.multiple_of(meta_ref[1 + slot] * size, size), size)
 
-    for slot, ref in zip(slots_of(len(spectra_refs)), spectra_refs):
+    for slot, ref in enumerate(spectra_refs):
         wide[place(slot), :] = ref[...].reshape(held * rows, width).astype(jnp.float32)
     level = level_ref[...]
     sign = jnp.where(
@@ -228,7 +228,7 @@
 def update_kernel(inputs, meta_ref, table_ref, _, *refs):
     restored_refs, (out_ref, turn_ref, whole_rows) = refs[:inputs], refs[-3:]
     held, rows, width = restored_refs[0].shape
-    for slot, ref in zip(slots_of(inputs), restored_refs):
+    for slot, ref in enumerate(restored_refs):
         whole_rows[:, band(meta_ref, slot, width)] = ref[...].reshape(held * rows, width)
     out_ref[...] = jnp.dot(
         whole_rows[...], table_ref[...], preferred_element_type=jnp.float32
@@ -260,7 +260,6 @@
 
 
 PARAMS = pltpu.CompilerParams(vmem_limit_bytes=60 * 1024 * 1024)
-SMALL = pl.CostEstimate(flops=1024, bytes_accessed=1024, transcendentals=0)
 ANYWHERE = pl.BlockSpec(memory_space=pl.ANY)
 
 
@@ -284,7 +283,11 @@
         ),
         out_shape=[pltpu.HBM(shape, jnp.bfloat16)] * peers + [pltpu.HBM((shots, LANES), jnp.float32)],
         compiler_params=PARAMS,
-        cost_estimate=SMALL,
+        cost_estimate=pl.CostEstimate(
+            flops=4 * F * shots * rows * samples,
+            bytes_accessed=3 * 2 * shots * rows * samples + table.size * 2,
+            transcendentals=0,
+        ),
         name="spectra",
     )(meta, delays, *fields, table, after)
     return spectra, energy
@@ -311,7 +314,7 @@
 
 
 def shrunk_of(meta, spectra, table, level, after):
-    shape = spectra[0][0].shape
+    shape = spectra[0].shape
     held, rows, width = shape
     peers = len(spectra)
     return pl.pallas_call(
@@ -320,24 +323,28 @@
             num_scalar_prefetch=1,
             grid=(1,),
             in_specs=[whole(table.shape), whole(level.shape), ANYWHERE]
-            + [read(item, shape, lambda step: (0, 0, 0)) for item in spectra],
+            + [whole(shape)] * peers,
             out_specs=[whole(shape)] * peers,
             scratch_shapes=[pltpu.VMEM((peers * held * rows, width), jnp.float32)] * 2,
         ),
         out_shape=[pltpu.HBM(shape, jnp.bfloat16)] * peers,
         compiler_params=PARAMS,
-        cost_estimate=SMALL,
+        cost_estimate=pl.CostEstimate(
+            flops=8 * (peers * held) ** 2 * rows * width,
+            bytes_accessed=4 * peers * held * rows * width + 2 * table.size,
+            transcendentals=peers * held * rows * width,
+        ),
         name="shrink",
-    )(meta, table, level, after, *[array for array, _ in spectra])
+    )(meta, table, level, after, *spectra)
 
 
 def updated_of(meta, restored, table, block, receivers, onto, after):
-    shots, rows, width = restored[0][0].shape
+    shots, rows, width = restored[0].shape
     samples = table.shape[1]
     group = min(shots, max(1, 256 // rows))
     in_specs = [whole(table.shape), ANYWHERE]
-    in_specs += [read(item, (group, rows, width), lambda step: (step, 0, 0)) for item in restored]
-    operands = [meta, table, after, *[array for array, _ in restored]]
+    in_specs += [pl.BlockSpec((group, rows, width), lambda step, meta: (step, 0, 0))] * len(restored)
+    operands = [meta, table, after, *restored]
     if onto is not None:
         in_specs.append(ANYWHERE)
         operands.append(onto)
@@ -358,8 +365,12 @@
             pltpu.HBM((8, LANES), jnp.float32),
         ],
         input_output_aliases={} if onto is None else {len(operands) - 1: 0},
-        compiler_params=pltpu.CompilerParams(vmem_limit_bytes=24 * 1024 * 1024),
-        cost_estimate=SMALL,
+        compiler_params=PARAMS,
+        cost_estimate=pl.CostEstimate(
+            flops=4 * F * shots * rows * samples,
+            bytes_accessed=4 * F * shots * rows + 2 * table.size + 4 * shots * rows * samples,
+            transcendentals=0,
+        ),
         name="update",
     )(*operands)
 
@@ -368,40 +379,12 @@
     return lax.all_to_all(array, "shot", split_axis=0, concat_axis=0, tiled=True)
 
 
-def sent(array, distance):
-    peers = lax.axis_size("shot")
-    if distance == 1:
-        groups = [[i, i ^ 1] for i in range(0, peers, 2)]
-        return lax.all_gather(array, "shot", axis_index_groups=groups), distance
-    return lax.ppermute(array, "shot", [(i, i ^ distance) for i in range(peers)]), 0
-
-
-def held(array):
-    return array, 0
-
-
-def read(item, shape, where):
-    _, distance = item
-    if distance == 0:
-        return pl.BlockSpec(shape, lambda step, meta, *_: where(step))
-    return pl.BlockSpec(
-        (None, *shape),
-        lambda step, meta, *_: (jnp.where(meta[1] < meta[1 + distance], 1, 0), *where(step)),
-    )
-
-
-def slots_of(peers):
-    far, near = list(range(peers // 2, peers)), list(range(2, peers // 2))
-    order = [0, 1]
-    while far or near:
-        order += far[:2] + near[:1]
-        far, near = far[2:], near[1:]
-    return order
-
-
 def exchanged(arrays):
-    slots = slots_of(len(arrays))
-    return [sent(arrays[slot], slot) if slot else held(arrays[slot]) for slot in slots]
+    peers = len(arrays)
+    return [
+        lax.ppermute(array, "shot", [(i, i ^ slot) for i in range(peers)]) if slot else array
+        for slot, array in enumerate(arrays)
+    ]
 
 
 def edges(estimate, observed):
@@ -415,9 +398,9 @@
 
 def chunks_of(receivers):
     if receivers == 128:
-        return [(16, 7), (16, 6), (32, 2), (32, 1), (16, 1), (16, 0)]
+        return [(16, 0), (16, 1), (32, 1), (32, 2), (16, 6), (16, 7)]
     rows = min(16, receivers)
-    return [(rows, index) for index in range(receivers // rows)][::-1]
+    return [(rows, index) for index in range(receivers // rows)]
 
 
 def direct(estimate, observed, delays, thresholds):
@@ -432,9 +415,7 @@
     table = jnp.asarray(shot_table(delays.shape[0]))
     levels = jnp.tile(lax.dynamic_slice_in_dim(thresholds, rank * share, share), 2)[None, :]
     chunks = chunks_of(receivers)
-    rest = receivers - chunks[0][0]
-    early = edges(estimate[:, rest:], observed[:, rest:])
-    late = None
+    sides = edges(estimate, observed)
     last, updated, energy = levels, None, 0.0
     lag = 2
     ahead, behind = {}, {}
@@ -444,20 +425,17 @@
             spectra, power = spectra_of(
                 meta,
                 delays,
-                (estimate, observed, *(late if turn else early)),
+                (estimate, observed, *sides),
                 forward,
                 rows,
                 index,
-                index if turn else 0,
+                index,
                 peers,
                 last,
             )
             last = power
             energy = energy + power
             ahead[turn] = exchanged(spectra)
-            if turn == 0 and rest:
-                later = lax.optimization_barrier((estimate, observed, power))
-                late = edges(later[0][:, :rest], later[1][:, :rest])
         place = turn - lag
         if place in ahead:
             shrunk = shrunk_of(meta, ahead.pop(place), table, levels, last)

time: 480 us -> 437 us (0.910); the launches traced: 478 us -> 429 us
  waiting for transfers between devices: 129 us -> 95 us
  blocking collectives: 40.8 us -> 9.99 us
  Pallas kernels: 152 us -> 165 us
  starting transfers between devices: 135 us -> 147 us
  local copies, waits for them, and re-layouts: 18.3 us -> 8.24 us
    ppermute x72 -> x84, waiting for transfers between devices: 127 us -> 92 us  [exchanged(): lax.ppermute(array, 'shot', [(i, i ^ slot) for i in range(peers)])]
    all_gather x12 -> x0, blocking collectives: 30.9 us -> none  [sent(): return (lax.all_gather(array, 'shot', axis_index_groups=groups), distance)]
    ppermute x72 -> x84, starting transfers between devices: 124 us -> 144 us  [exchanged(): lax.ppermute(array, 'shot', [(i, i ^ slot) for i in range(peers)])]
    pallas_call x6, Pallas kernels: 24.2 us -> 36.8 us  [updated_of(): pl.pallas_call(functools.partial(update_kernel, len(restored)), grid_spec...]
    unnamed x156 -> x210, local copies, waits for them, and re-layouts: 13 us -> 4.55 us
    ppermute x4 -> x2, starting transfers between devices: 10.8 us -> 3.7 us  [edges(): return (lax.ppermute(tail, 'shot', up), lax.ppermute(head, 'shot', down))]
  transfers between devices with their start and end apart: 76 -> 86, of which waited for: 17 -> 20; matrix products, arithmetic and copies ran while one was open for 1% -> 1% of each run, Pallas kernels for 29% -> 35%
where the time goes in v10:
time: 437 us; the launch traced here: 429 us
  Pallas kernels  165 us (38%)
  starting transfers between devices  147 us (34%)
  waiting for transfers between devices  95 us (22%)
  blocking collectives  9.99 us (2%)
  local copies, waits for them, and re-layouts  8.24 us (2%)
    ppermute x84, starting transfers between devices, exchanged(): lax.ppermute(array, 'shot', [(i, i ^ slot) for i in range(peers)])  144 us
    ppermute x84, waiting for transfers between devices, exchanged(): lax.ppermute(array, 'shot', [(i, i ^ slot) for i in range(peers)])  92 us
    pallas_call x6, Pallas kernels, spectra_of(): pl.pallas_call(spectra_kernel, grid_spec=pltpu.PrefetchScalarGridSpec(num...  69 us
    pallas_call x6, Pallas kernels, shrunk_of(): pl.pallas_call(shots_kernel, grid_spec=pltpu.PrefetchScalarGridSpec(num_s...  58.8 us
    pallas_call x6, Pallas kernels, updated_of(): pl.pallas_call(functools.partial(update_kernel, len(restored)), grid_spec...  36.8 us
    psum x1, blocking collectives, local(): lax.psum(jnp.sum(energy, axis=1), 'patch')  9.99 us
  transfers between devices with their start and end apart: 86, of which 20 were waited for; matrix products, arithmetic and copies ran while one was open for 1% of the time, Pallas kernels for 35%

profile of v10, /device:TPU:0, one launch (start us, length us, event | category | flops | bytes accessed | tf_op | source)
XLA Modules:
  0.0 428.5 jit_solution(12599927204297499844)
XLA Ops:
  3.1 2.4 collective-permute-start
  8.9 3.0 collective-permute-done.1.after_ref
  12.7 9.8 %spectra.6 = (bf16[32,16,128]{2,1,0:T(8,128)(2,1)}, bf16[32,16,128]{2,1,0:T(8,128)(2,1)}, bf16[32,16,128]{2,1,0:T(8,128)(2,1)}, bf16[32,16,128]{2,1,0:T(8,128)(2...) custom-call(s32[9]{0:T(128)} %pad_add_fusion.meta_ref, ...), custom_call_target="tpu_custom_call" | custom-call | flops 1073741824 | bytes 5242880 | tf_op jit(solution)/shard_map/spectra/pallas_call | solution.py:270
  22.6 9.7 %collective-permute-start.2 = (bf16[32,16,128]{2,1,0:T(8,128)(2,1)}, bf16[32,16,128]{2,1,0:T(8,128)(2,1)S(1)}, u32[]{:S(2)}, u32[]{:S(2)}) collective-permute-start(bf16[32,16,128]{2,1,0:T(8,128)(2,1)} %get-tuple-element.119), channel_id=1, source_target_pairs={{0,1},{1,0},{2,3},{3,2},{4,5},{5,4},{6,7},{7,6},{8,9},{9,8},{10,11... | collective-permute-start | bytes 393224 | tf_op jit(solution)/shard_map/ppermute | solution.py:385
  33.9 2.4 collective-permute-start.5
  36.7 9.9 %spectra.7 = (bf16[32,16,128]{2,1,0:T(8,128)(2,1)}, bf16[32,16,128]{2,1,0:T(8,128)(2,1)}, bf16[32,16,128]{2,1,0:T(8,128)(2,1)}, bf16[32,16,128]{2,1,0:T(8,128)(2...) custom-call(s32[9]{0:T(128)} %pad_add_fusion.meta_ref, ...), custom_call_target="tpu_custom_call" | custom-call | flops 1073741824 | bytes 5242880 | tf_op jit(solution)/shard_map/spectra/pallas_call | solution.py:270
  46.6 2.1 collective-permute-start.7
  52.1 14.7 %spectra.8 = (bf16[32,32,128]{2,1,0:T(8,128)(2,1)}, bf16[32,32,128]{2,1,0:T(8,128)(2,1)}, bf16[32,32,128]{2,1,0:T(8,128)(2,1)}, bf16[32,32,128]{2,1,0:T(8,128)(2...) custom-call(s32[9]{0:T(128)} %pad_add_fusion.meta_ref, ...), custom_call_target="tpu_custom_call" | custom-call | flops 2147483648 | bytes 8388608 | tf_op jit(solution)/shard_map/spectra/pallas_call | solution.py:270
  70.0 2.1 collective-permute-start.14
  72.1 7.3 %shrink.6 = (bf16[32,16,128]{2,1,0:T(8,128)(2,1)}, bf16[32,16,128]{2,1,0:T(8,128)(2,1)}, bf16[32,16,128]{2,1,0:T(8,128)(2,1)}, bf16[32,16,128]{2,1,0:T(8,128)(2,...) custom-call(s32[9]{0:T(128)} %pad_add_fusion.meta_ref, ...), custom_call_target="tpu_custom_call" | custom-call | flops 1073741824 | bytes 2359296 | tf_op jit(solution)/shard_map/shrink/pallas_call | solution.py:320
  81.9 5.7 %collective-permute-done.13.refs_5_ = bf16[32,16,128]{2,1,0:T(8,128)(2,1)S(1)} collective-permute-done((bf16[32,16,128]{2,1,0:T(8,128)(2,1)S(1)}, bf16[32,16,128]{2,1,0:T(8,128)(2,1)S(1)}, u32[]{:S(2)}, u32[]{:S(2)}) %collective-permute-start.13) | collective-permute-done | bytes 131104 | tf_op jit(solution)/shard_map/ppermute | solution.py:385
  87.6 4.1 collective-permute-start.26
  91.7 2.1 collective-permute-start.17
  94.6 2.0 collective-permute-start.28
  96.6 2.6 collective-permute-done.26.refs_4_
  100.7 3.1 collective-permute-done.27.refs_5_
  103.7 2.5 collective-permute-start.18
  106.2 2.9 collective-permute-done.28.refs_6_
  109.1 5.1 %collective-permute-start.19 = (bf16[32,32,128]{2,1,0:T(8,128)(2,1)}, bf16[32,32,128]{2,1,0:T(8,128)(2,1)S(1)}, u32[]{:S(2)}, u32[]{:S(2)}) collective-permute-start(bf16[32,32,128]{2,1,0:T(8,128)(2,1)} %get-tuple-element.142), channel_id=1, source_target_pairs={{0,4},{1,5},{2,6},{3,7},{4,0},{5,1},{6,2},{7,3},{8,12},{9,13},{10,... | collective-permute-start | bytes 786440 | tf_op jit(solution)/shard_map/ppermute | solution.py:385
  114.2 2.4 collective-permute-start.20
  116.6 2.1 collective-permute-start.21
  120.3 14.7 %spectra.9 = (bf16[32,32,128]{2,1,0:T(8,128)(2,1)}, bf16[32,32,128]{2,1,0:T(8,128)(2,1)}, bf16[32,32,128]{2,1,0:T(8,128)(2,1)}, bf16[32,32,128]{2,1,0:T(8,128)(2...) custom-call(s32[9]{0:T(128)} %pad_add_fusion.meta_ref, ...), custom_call_target="tpu_custom_call" | custom-call | flops 2147483648 | bytes 8388608 | tf_op jit(solution)/shard_map/spectra/pallas_call | solution.py:270
  135.1 7.2 %shrink.7 = (bf16[32,16,128]{2,1,0:T(8,128)(2,1)}, bf16[32,16,128]{2,1,0:T(8,128)(2,1)}, bf16[32,16,128]{2,1,0:T(8,128)(2,1)}, bf16[32,16,128]{2,1,0:T(8,128)(2,...) custom-call(s32[9]{0:T(128)} %pad_add_fusion.meta_ref, ...), custom_call_target="tpu_custom_call" | custom-call | flops 1073741824 | bytes 2359296 | tf_op jit(solution)/shard_map/shrink/pallas_call | solution.py:320
  144.1 5.0 %collective-permute-done.20.refs_5_ = bf16[32,32,128]{2,1,0:T(8,128)(2,1)S(1)} collective-permute-done((bf16[32,32,128]{2,1,0:T(8,128)(2,1)}, bf16[32,32,128]{2,1,0:T(8,128)(2,1)S(1)}, u32[]{:S(2)}, u32[]{:S(2)}) %collective-permute-start.20) | collective-permute-done | bytes 262176 | tf_op jit(solution)/shard_map/ppermute | solution.py:385
  149.1 10.1 %spectra.10 = (bf16[32,16,128]{2,1,0:T(8,128)(2,1)}, bf16[32,16,128]{2,1,0:T(8,128)(2,1)}, bf16[32,16,128]{2,1,0:T(8,128)(2,1)}, bf16[32,16,128]{2,1,0:T(8,128)(...) custom-call(s32[9]{0:T(128)} %pad_add_fusion.meta_ref, ...), custom_call_target="tpu_custom_call" | custom-call | flops 1073741824 | bytes 5242880 | tf_op jit(solution)/shard_map/spectra/pallas_call | solution.py:270
  159.3 2.8 collective-permute-start.40
  162.3 2.0 collective-permute-start.42
  166.3 14.7 %shrink.8 = (bf16[32,32,128]{2,1,0:T(8,128)(2,1)}, bf16[32,32,128]{2,1,0:T(8,128)(2,1)}, bf16[32,32,128]{2,1,0:T(8,128)(2,1)}, bf16[32,32,128]{2,1,0:T(8,128)(2,...) custom-call(s32[9]{0:T(128)} %pad_add_fusion.meta_ref, ...), custom_call_target="tpu_custom_call" | custom-call | flops 2147483648 | bytes 4456448 | tf_op jit(solution)/shard_map/shrink/pallas_call | solution.py:320
  182.6 5.4 %update.6 = (f32[32,128,1024]{2,1,0:T(8,128)}, f32[8,128]{1,0:T(8,128)}) custom-call(s32[9]{0:T(128)} %pad_add_fusion.meta_ref, bf16[1024,1024]{1,0:T(8,128)(2,1)} %constant.24.clone.table_ref, bf16[32,32,128]{2,1,0:T(8,128)(2,1)} %get-tuple-element.146._.refs_0_, bf16[32,16,128]{2,1,0:T(8,128)(2,1)} %get-tuple-element.126._.refs_0_, ...), custom_call_target="tpu_custom_call" | custom-call | flops 1073741824 | bytes 5242880 | tf_op jit(solution)/shard_map/update/pallas_call | solution.py:351
  191.0 1.9 collective-permute-start.49
  193.0 9.9 %spectra.11 = (bf16[32,16,128]{2,1,0:T(8,128)(2,1)}, bf16[32,16,128]{2,1,0:T(8,128)(2,1)}, bf16[32,16,128]{2,1,0:T(8,128)(2,1)}, bf16[32,16,128]{2,1,0:T(8,128)(...) custom-call(s32[9]{0:T(128)} %pad_add_fusion.meta_ref, ...), custom_call_target="tpu_custom_call" | custom-call | flops 1073741824 | bytes 5242880 | tf_op jit(solution)/shard_map/spectra/pallas_call | solution.py:270
  206.4 6.7 %collective-permute-start.61 = (bf16[32,16,128]{2,1,0:T(8,128)(2,1)}, bf16[32,16,128]{2,1,0:T(8,128)(2,1)S(1)}, u32[]{:S(2)}, u32[]{:S(2)}) collective-permute-start(bf16[32,16,128]{2,1,0:T(8,128)(2,1)} %get-tuple-element.196), channel_id=1, source_target_pairs={{0,4},{1,5},{2,6},{3,7},{4,0},{5,1},{6,2},{7,3},{8,12},{9,13},{10,... | collective-permute-start | bytes 393224 | tf_op jit(solution)/shard_map/ppermute | solution.py:385
  214.4 2.0 collective-permute-start.31
  217.9 1.9 collective-permute-start.63
  222.0 4.0 collective-permute-done.62.refs_5_
  226.0 2.5 collective-permute-start.32
  228.5 2.8 collective-permute-done.63.refs_6_
  231.4 4.5 %collective-permute-start.33 = (bf16[32,32,128]{2,1,0:T(8,128)(2,1)S(1)}, bf16[32,32,128]{2,1,0:T(8,128)(2,1)S(1)}, u32[]{:S(2)}, u32[]{:S(2)}) collective-permute-start(bf16[32,32,128]{2,1,0:T(8,128)(2,1)S(1)} %copy-done.49), channel_id=1, source_target_pairs={{0,4},{1,5},{2,6},{3,7},{4,0},{5,1},{6,2},{7,3},{8,12},{9,13},{10,... | collective-permute-start | bytes 786440 | tf_op jit(solution)/shard_map/ppermute | solution.py:385
  236.6 2.4 collective-permute-start.34
  243.1 22.5 %collective-permute-done.33.refs_4_ = bf16[32,32,128]{2,1,0:T(8,128)(2,1)S(1)} collective-permute-done((bf16[32,32,128]{2,1,0:T(8,128)(2,1)S(1)}, bf16[32,32,128]{2,1,0:T(8,128)(2,1)S(1)}, u32[]{:S(2)}, u32[]{:S(2)}) %collective-permute-start.33) | collective-permute-done | bytes 262176 | tf_op jit(solution)/shard_map/ppermute | solution.py:385
  265.6 5.3 %collective-permute-done.34.refs_5_ = bf16[32,32,128]{2,1,0:T(8,128)(2,1)S(1)} collective-permute-done((bf16[32,32,128]{2,1,0:T(8,128)(2,1)S(1)}, bf16[32,32,128]{2,1,0:T(8,128)(2,1)S(1)}, u32[]{:S(2)}, u32[]{:S(2)}) %collective-permute-start.34) | collective-permute-done | bytes 262176 | tf_op jit(solution)/shard_map/ppermute | solution.py:385
  271.0 7.0 %collective-permute-start.54 = (bf16[32,32,128]{2,1,0:T(8,128)(2,1)}, bf16[32,32,128]{2,1,0:T(8,128)(2,1)S(1)}, u32[]{:S(2)}, u32[]{:S(2)}) collective-permute-start(bf16[32,32,128]{2,1,0:T(8,128)(2,1)} %get-tuple-element.186), channel_id=1, source_target_pairs={{0,4},{1,5},{2,6},{3,7},{4,0},{5,1},{6,2},{7,3},{8,12},{9,13},{10,... | collective-permute-start | bytes 786440 | tf_op jit(solution)/shard_map/ppermute | solution.py:385
  278.7 10.7 %collective-permute-start.55 = (bf16[32,32,128]{2,1,0:T(8,128)(2,1)S(1)}, bf16[32,32,128]{2,1,0:T(8,128)(2,1)S(1)}, u32[]{:S(2)}, u32[]{:S(2)}) collective-permute-start(bf16[32,32,128]{2,1,0:T(8,128)(2,1)S(1)} %copy-done.47), channel_id=1, source_target_pairs={{0,5},{1,4},{2,7},{3,6},{4,1},{5,0},{6,3},{7,2},{8,13},{9,12},{10,... | collective-permute-start | bytes 786440 | tf_op jit(solution)/shard_map/ppermute | solution.py:385
  289.4 14.7 %shrink.9 = (bf16[32,32,128]{2,1,0:T(8,128)(2,1)}, bf16[32,32,128]{2,1,0:T(8,128)(2,1)}, bf16[32,32,128]{2,1,0:T(8,128)(2,1)}, bf16[32,32,128]{2,1,0:T(8,128)(2,...) custom-call(s32[9]{0:T(128)} %pad_add_fusion.meta_ref, ...), custom_call_target="tpu_custom_call" | custom-call | flops 2147483648 | bytes 4456448 | tf_op jit(solution)/shard_map/shrink/pallas_call | solution.py:320
  304.2 1.9 collective-permute-start.56
  307.9 5.4 %update.7 = (f32[32,128,1024]{2,1,0:T(8,128)}, f32[8,128]{1,0:T(8,128)}) custom-call(s32[9]{0:T(128)} %pad_add_fusion.meta_ref, bf16[1024,1024]{1,0:T(8,128)(2,1)} %constant.24.clone.table_ref, bf16[32,32,128]{2,1,0:T(8,128)(2,1)} %get-tuple-element.164._.refs_0_, ...), custom_call_target="tpu_custom_call", output_to_operand_aliasing={{0}: (11, {})} | custom-call | flops 1073741824 | bytes 5242880 | tf_op jit(solution)/shard_map/update/pallas_call | solution.py:351
  313.3 7.4 %shrink.10 = (bf16[32,16,128]{2,1,0:T(8,128)(2,1)}, bf16[32,16,128]{2,1,0:T(8,128)(2,1)}, bf16[32,16,128]{2,1,0:T(8,128)(2,1)}, bf16[32,16,128]{2,1,0:T(8,128)(2...) custom-call(s32[9]{0:T(128)} %pad_add_fusion.meta_ref, ...), custom_call_target="tpu_custom_call" | custom-call | flops 1073741824 | bytes 2359296 | tf_op jit(solution)/shard_map/shrink/pallas_call | solution.py:320
  322.7 2.3 collective-permute-start.75
  324.9 5.2 %collective-permute-start.76 = (bf16[32,16,128]{2,1,0:T(8,128)(2,1)}, bf16[32,16,128]{2,1,0:T(8,128)(2,1)S(1)}, u32[]{:S(2)}, u32[]{:S(2)}) collective-permute-start(bf16[32,16,128]{2,1,0:T(8,128)(2,1)} %get-tuple-element.214), channel_id=1, source_target_pairs={{0,5},{1,4},{2,7},{3,6},{4,1},{5,0},{6,3},{7,2},{8,13},{9,12},{10,... | collective-permute-start | bytes 393224 | tf_op jit(solution)/shard_map/ppermute | solution.py:385
  331.9 7.7 %update.8 = (f32[32,128,1024]{2,1,0:T(8,128)}, f32[8,128]{1,0:T(8,128)}) custom-call(s32[9]{0:T(128)} %pad_add_fusion.meta_ref, bf16[1024,1024]{1,0:T(8,128)(2,1)} %constant.24.clone.table_ref, bf16[32,16,128]{2,1,0:T(8,128)(2,1)} %get-tuple-element.182._.refs_0_, ...), custom_call_target="tpu_custom_call", output_to_operand_aliasing={{0}: (11, {})} | custom-call | flops 2147483648 | bytes 8388608 | tf_op jit(solution)/shard_map/update/pallas_call | solution.py:351
  339.6 7.5 %shrink.11 = (bf16[32,16,128]{2,1,0:T(8,128)(2,1)}, bf16[32,16,128]{2,1,0:T(8,128)(2,1)}, bf16[32,16,128]{2,1,0:T(8,128)(2,1)}, bf16[32,16,128]{2,1,0:T(8,128)(2...) custom-call(s32[9]{0:T(128)} %pad_add_fusion.meta_ref, ...), custom_call_target="tpu_custom_call" | custom-call | flops 1073741824 | bytes 2359296 | tf_op jit(solution)/shard_map/shrink/pallas_call | solution.py:320
  347.1 2.3 collective-permute-start.78
  350.6 3.8 collective-permute-done.78.refs_7_
  354.4 3.1 collective-permute-start.67
  359.8 2.2 collective-permute-start.70
  363.9 10.0 %psum.7 = f32[32]{0:T(128)S(1)} all-reduce(f32[32]{0:T(128)S(1)} %add_reduce_fusion), channel_id=1, replica_groups=mesh['patch'=4,'shot'=8] {'patch'}, use_global_device_ids=true, to_apply=%region_1.0 | all-reduce | flops 32 | bytes 256 | tf_op jit(solution)/shard_map/psum | solution.py:510
  374.5 15.9 %collective-permute-done.68.refs_4_ = bf16[32,32,128]{2,1,0:T(8,128)(2,1)S(1)} collective-permute-done((bf16[32,32,128]{2,1,0:T(8,128)(2,1)}, bf16[32,32,128]{2,1,0:T(8,128)(2,1)S(1)}, u32[]{:S(2)}, u32[]{:S(2)}) %collective-permute-start.68) | collective-permute-done | bytes 262176 | tf_op jit(solution)/shard_map/ppermute | solution.py:385
  390.4 6.6 %collective-permute-done.69.refs_5_ = bf16[32,32,128]{2,1,0:T(8,128)(2,1)S(1)} collective-permute-done((bf16[32,32,128]{2,1,0:T(8,128)(2,1)}, bf16[32,32,128]{2,1,0:T(8,128)(2,1)S(1)}, u32[]{:S(2)}, u32[]{:S(2)}) %collective-permute-start.69) | collective-permute-done | bytes 262176 | tf_op jit(solution)/shard_map/ppermute | solution.py:385
  397.0 2.7 collective-permute-start.84
  399.7 2.1 collective-permute-start.85
  401.9 7.7 %update.9 = (f32[32,128,1024]{2,1,0:T(8,128)}, f32[8,128]{1,0:T(8,128)}) custom-call(s32[9]{0:T(128)} %pad_add_fusion.meta_ref, bf16[1024,1024]{1,0:T(8,128)(2,1)} %constant.24.clone.table_ref, bf16[32,16,128]{2,1,0:T(8,128)(2,1)} %get-tuple-element.200._.refs_0_, ...), custom_call_target="tpu_custom_call", output_to_operand_aliasing={{0}: (11, {})} | custom-call | flops 2147483648 | bytes 8388608 | tf_op jit(solution)/shard_map/update/pallas_call | solution.py:351
  409.6 5.4 %update.10 = (f32[32,128,1024]{2,1,0:T(8,128)}, f32[8,128]{1,0:T(8,128)}) custom-call(s32[9]{0:T(128)} %pad_add_fusion.meta_ref, bf16[1024,1024]{1,0:T(8,128)(2,1)} %constant.24.clone.table_ref, f32[8,128]{1,0:T(8,128)} %get-tuple-element.209._, bf16[32,16,128]{2,1,0:T(8,128)(2,1)} %get-tuple-element.182._.refs_0_, ...), custom_call_target="tpu_custom_call", output_to_operand_aliasing={{0}: (11, {})} | custom-call | flops 1073741824 | bytes 5242880 | tf_op jit(solution)/shard_map/update/pallas_call | solution.py:351
  415.0 6.2 %collective-permute-done.82.refs_4_ = bf16[32,16,128]{2,1,0:T(8,128)(2,1)S(1)} collective-permute-done((bf16[32,16,128]{2,1,0:T(8,128)(2,1)}, bf16[32,16,128]{2,1,0:T(8,128)(2,1)S(1)}, u32[]{:S(2)}, u32[]{:S(2)}) %collective-permute-start.82) | collective-permute-done | bytes 131104 | tf_op jit(solution)/shard_map/ppermute | solution.py:385
  423.0 5.4 %update.11 = (f32[32,128,1024]{2,1,0:T(8,128)}, f32[8,128]{1,0:T(8,128)}) custom-call(s32[9]{0:T(128)} %pad_add_fusion.meta_ref, bf16[1024,1024]{1,0:T(8,128)(2,1)} %constant.24.clone.table_ref, f32[8,128]{1,0:T(8,128)} %get-tuple-element.218._, bf16[32,16,128]{2,1,0:T(8,128)(2,1)} %get-tuple-element.200._.refs_0_, ...), custom_call_target="tpu_custom_call", output_to_operand_aliasing={{0}: (11, {})} | custom-call | flops 1073741824 | bytes 5242880 | tf_op jit(solution)/shard_map/update/pallas_call | solution.py:351
  (348 shorter events, 57.1 us)
Async XLA Ops:
  22.6 24.0 %collective-permute-start.2 = (bf16[32,16,128]{2,1,0:T(8,128)(2,1)}, bf16[32,16,128]{2,1,0:T(8,128)(2,1)S(1)}, u32[]{:S(2)}, u32[]{:S(2)}) collective-permute-start(bf16[32,16,128]{2,1,0:T(8,128)(2,1)} %get-tuple-element.119), channel_id=1, source_target_pairs={{0,1},{1,0},{2,3},{3,2},{4,5},{5,4},{6,7},{7,6},{8,9},{9,8},{10,11... | collective-permute-start | bytes 393224 | tf_op jit(solution)/shard_map/ppermute | solution.py:385
  32.3 16.5 %collective-permute-start.3 = (bf16[32,16,128]{2,1,0:T(8,128)(2,1)}, bf16[32,16,128]{2,1,0:T(8,128)(2,1)S(1)}, u32[]{:S(2)}, u32[]{:S(2)}) collective-permute-start(bf16[32,16,128]{2,1,0:T(8,128)(2,1)} %get-tuple-element.120), channel_id=1, source_target_pairs={{0,2},{1,3},{2,0},{3,1},{4,6},{5,7},{6,4},{7,5},{8,10},{9,11},{10,... | collective-permute-start | bytes 393224 | tf_op jit(solution)/shard_map/ppermute | solution.py:385
  33.9 16.3 %collective-permute-start.4 = (bf16[32,16,128]{2,1,0:T(8,128)(2,1)}, bf16[32,16,128]{2,1,0:T(8,128)(2,1)S(1)}, u32[]{:S(2)}, u32[]{:S(2)}) collective-permute-start(bf16[32,16,128]{2,1,0:T(8,128)(2,1)} %get-tuple-element.121), channel_id=1, source_target_pairs={{0,3},{1,2},{2,1},{3,0},{4,7},{5,6},{6,5},{7,4},{8,11},{9,10},{10,... | collective-permute-start | bytes 393224 | tf_op jit(solution)/shard_map/ppermute | solution.py:385
  33.9 16.8 %collective-permute-start.5 = (bf16[32,16,128]{2,1,0:T(8,128)(2,1)}, bf16[32,16,128]{2,1,0:T(8,128)(2,1)S(1)}, u32[]{:S(2)}, u32[]{:S(2)}) collective-permute-start(bf16[32,16,128]{2,1,0:T(8,128)(2,1)} %get-tuple-element.122), channel_id=1, source_target_pairs={{0,4},{1,5},{2,6},{3,7},{4,0},{5,1},{6,2},{7,3},{8,12},{9,13},{10,... | collective-permute-start | bytes 393224 | tf_op jit(solution)/shard_map/ppermute | solution.py:385
  46.6 20.2 %collective-permute-start.7 = (bf16[32,16,128]{2,1,0:T(8,128)(2,1)S(1)}, bf16[32,16,128]{2,1,0:T(8,128)(2,1)S(1)}, u32[]{:S(2)}, u32[]{:S(2)}) collective-permute-start(bf16[32,16,128]{2,1,0:T(8,128)(2,1)S(1)} %copy-done.102), channel_id=1, source_target_pairs={{0,6},{1,7},{2,4},{3,5},{4,2},{5,3},{6,0},{7,1},{8,14},{9,15},{10,... | collective-permute-start | bytes 393224 | tf_op jit(solution)/shard_map/ppermute | solution.py:385
  48.8 19.4 %collective-permute-start.8 = (bf16[32,16,128]{2,1,0:T(8,128)(2,1)S(1)}, bf16[32,16,128]{2,1,0:T(8,128)(2,1)S(1)}, u32[]{:S(2)}, u32[]{:S(2)}) collective-permute-start(bf16[32,16,128]{2,1,0:T(8,128)(2,1)S(1)} %copy-done.101), channel_id=1, source_target_pairs={{0,7},{1,6},{2,5},{3,4},{4,3},{5,2},{6,1},{7,0},{8,15},{9,14},{10,... | collective-permute-start | bytes 393224 | tf_op jit(solution)/shard_map/ppermute | solution.py:385
  50.1 19.8 %collective-permute-start.9 = (bf16[32,16,128]{2,1,0:T(8,128)(2,1)}, bf16[32,16,128]{2,1,0:T(8,128)(2,1)S(1)}, u32[]{:S(2)}, u32[]{:S(2)}) collective-permute-start(bf16[32,16,128]{2,1,0:T(8,128)(2,1)} %get-tuple-element.129), channel_id=1, source_target_pairs={{0,1},{1,0},{2,3},{3,2},{4,5},{5,4},{6,7},{7,6},{8,9},{9,8},{10,11... | collective-permute-start | bytes 393224 | tf_op jit(solution)/shard_map/ppermute | solution.py:385
  50.7 28.7 %collective-permute-start.10 = (bf16[32,16,128]{2,1,0:T(8,128)(2,1)}, bf16[32,16,128]{2,1,0:T(8,128)(2,1)S(1)}, u32[]{:S(2)}, u32[]{:S(2)}) collective-permute-start(bf16[32,16,128]{2,1,0:T(8,128)(2,1)} %get-tuple-element.130), channel_id=1, source_target_pairs={{0,2},{1,3},{2,0},{3,1},{4,6},{5,7},{6,4},{7,5},{8,10},{9,11},{10,... | collective-permute-start | bytes 393224 | tf_op jit(solution)/shard_map/ppermute | solution.py:385
  50.7 29.9 %collective-permute-start.11 = (bf16[32,16,128]{2,1,0:T(8,128)(2,1)}, bf16[32,16,128]{2,1,0:T(8,128)(2,1)S(1)}, u32[]{:S(2)}, u32[]{:S(2)}) collective-permute-start(bf16[32,16,128]{2,1,0:T(8,128)(2,1)} %get-tuple-element.131), channel_id=1, source_target_pairs={{0,3},{1,2},{2,1},{3,0},{4,7},{5,6},{6,5},{7,4},{8,11},{9,10},{10,... | collective-permute-start | bytes 393224 | tf_op jit(solution)/shard_map/ppermute | solution.py:385
  66.8 15.0 %collective-permute-start.12 = (bf16[32,16,128]{2,1,0:T(8,128)(2,1)S(1)}, bf16[32,16,128]{2,1,0:T(8,128)(2,1)S(1)}, u32[]{:S(2)}, u32[]{:S(2)}) collective-permute-start(bf16[32,16,128]{2,1,0:T(8,128)(2,1)S(1)} %copy-done.95), channel_id=1, source_target_pairs={{0,4},{1,5},{2,6},{3,7},{4,0},{5,1},{6,2},{7,3},{8,12},{9,13},{10,... | collective-permute-start | bytes 393224 | tf_op jit(solution)/shard_map/ppermute | solution.py:385
  68.2 19.4 %collective-permute-start.13 = (bf16[32,16,128]{2,1,0:T(8,128)(2,1)S(1)}, bf16[32,16,128]{2,1,0:T(8,128)(2,1)S(1)}, u32[]{:S(2)}, u32[]{:S(2)}) collective-permute-start(bf16[32,16,128]{2,1,0:T(8,128)(2,1)S(1)} %copy-done.94), channel_id=1, source_target_pairs={{0,5},{1,4},{2,7},{3,6},{4,1},{5,0},{6,3},{7,2},{8,13},{9,12},{10,... | collective-permute-start | bytes 393224 | tf_op jit(solution)/shard_map/ppermute | solution.py:385
  70.0 17.6 %collective-permute-start.14 = (bf16[32,16,128]{2,1,0:T(8,128)(2,1)S(1)}, bf16[32,16,128]{2,1,0:T(8,128)(2,1)S(1)}, u32[]{:S(2)}, u32[]{:S(2)}) collective-permute-start(bf16[32,16,128]{2,1,0:T(8,128)(2,1)S(1)} %copy-done.93), channel_id=1, source_target_pairs={{0,6},{1,7},{2,4},{3,5},{4,2},{5,3},{6,0},{7,1},{8,14},{9,15},{10,... | collective-permute-start | bytes 393224 | tf_op jit(solution)/shard_map/ppermute | solution.py:385
  91.7 25.0 %collective-permute-start.16 = (bf16[32,32,128]{2,1,0:T(8,128)(2,1)}, bf16[32,32,128]{2,1,0:T(8,128)(2,1)S(1)}, u32[]{:S(2)}, u32[]{:S(2)}) collective-permute-start(bf16[32,32,128]{2,1,0:T(8,128)(2,1)} %get-tuple-element.139), channel_id=1, source_target_pairs={{0,1},{1,0},{2,3},{3,2},{4,5},{5,4},{6,7},{7,6},{8,9},{9,8},{10,11... | collective-permute-start | bytes 786440 | tf_op jit(solution)/shard_map/ppermute | solution.py:385
  91.7 27.0 %collective-permute-start.17 = (bf16[32,32,128]{2,1,0:T(8,128)(2,1)}, bf16[32,32,128]{2,1,0:T(8,128)(2,1)S(1)}, u32[]{:S(2)}, u32[]{:S(2)}) collective-permute-start(bf16[32,32,128]{2,1,0:T(8,128)(2,1)} %get-tuple-element.140), channel_id=1, source_target_pairs={{0,2},{1,3},{2,0},{3,1},{4,6},{5,7},{6,4},{7,5},{8,10},{9,11},{10,... | collective-permute-start | bytes 786440 | tf_op jit(solution)/shard_map/ppermute | solution.py:385
  94.6 14.5 %collective-permute-start.28 = (bf16[32,16,128]{2,1,0:T(8,128)(2,1)}, bf16[32,16,128]{2,1,0:T(8,128)(2,1)S(1)}, u32[]{:S(2)}, u32[]{:S(2)}) collective-permute-start(bf16[32,16,128]{2,1,0:T(8,128)(2,1)} %get-tuple-element.152), channel_id=1, source_target_pairs={{0,6},{1,7},{2,4},{3,5},{4,2},{5,3},{6,0},{7,1},{8,14},{9,15},{10,... | collective-permute-start | bytes 393224 | tf_op jit(solution)/shard_map/ppermute | solution.py:385
  99.2 15.0 %collective-permute-start.29 = (bf16[32,16,128]{2,1,0:T(8,128)(2,1)}, bf16[32,16,128]{2,1,0:T(8,128)(2,1)S(1)}, u32[]{:S(2)}, u32[]{:S(2)}) collective-permute-start(bf16[32,16,128]{2,1,0:T(8,128)(2,1)} %get-tuple-element.153), channel_id=1, source_target_pairs={{0,7},{1,6},{2,5},{3,4},{4,3},{5,2},{6,1},{7,0},{8,15},{9,14},{10,... | collective-permute-start | bytes 393224 | tf_op jit(solution)/shard_map/ppermute | solution.py:385
  103.7 38.6 %collective-permute-start.18 = (bf16[32,32,128]{2,1,0:T(8,128)(2,1)}, bf16[32,32,128]{2,1,0:T(8,128)(2,1)S(1)}, u32[]{:S(2)}, u32[]{:S(2)}) collective-permute-start(bf16[32,32,128]{2,1,0:T(8,128)(2,1)} %get-tuple-element.141), channel_id=1, source_target_pairs={{0,3},{1,2},{2,1},{3,0},{4,7},{5,6},{6,5},{7,4},{8,11},{9,10},{10,... | collective-permute-start | bytes 786440 | tf_op jit(solution)/shard_map/ppermute | solution.py:385
  109.1 35.0 %collective-permute-start.19 = (bf16[32,32,128]{2,1,0:T(8,128)(2,1)}, bf16[32,32,128]{2,1,0:T(8,128)(2,1)S(1)}, u32[]{:S(2)}, u32[]{:S(2)}) collective-permute-start(bf16[32,32,128]{2,1,0:T(8,128)(2,1)} %get-tuple-element.142), channel_id=1, source_target_pairs={{0,4},{1,5},{2,6},{3,7},{4,0},{5,1},{6,2},{7,3},{8,12},{9,13},{10,... | collective-permute-start | bytes 786440 | tf_op jit(solution)/shard_map/ppermute | solution.py:385
  114.2 34.9 %collective-permute-start.20 = (bf16[32,32,128]{2,1,0:T(8,128)(2,1)}, bf16[32,32,128]{2,1,0:T(8,128)(2,1)S(1)}, u32[]{:S(2)}, u32[]{:S(2)}) collective-permute-start(bf16[32,32,128]{2,1,0:T(8,128)(2,1)} %get-tuple-element.143), channel_id=1, source_target_pairs={{0,5},{1,4},{2,7},{3,6},{4,1},{5,0},{6,3},{7,2},{8,13},{9,12},{10,... | collective-permute-start | bytes 786440 | tf_op jit(solution)/shard_map/ppermute | solution.py:385
  116.6 42.7 %collective-permute-start.21 = (bf16[32,32,128]{2,1,0:T(8,128)(2,1)}, bf16[32,32,128]{2,1,0:T(8,128)(2,1)S(1)}, u32[]{:S(2)}, u32[]{:S(2)}) collective-permute-start(bf16[32,32,128]{2,1,0:T(8,128)(2,1)} %get-tuple-element.144), channel_id=1, source_target_pairs={{0,6},{1,7},{2,4},{3,5},{4,2},{5,3},{6,0},{7,1},{8,14},{9,15},{10,... | collective-permute-start | bytes 786440 | tf_op jit(solution)/shard_map/ppermute | solution.py:385
  118.7 43.4 %collective-permute-start.22 = (bf16[32,32,128]{2,1,0:T(8,128)(2,1)}, bf16[32,32,128]{2,1,0:T(8,128)(2,1)}, u32[]{:S(2)}, u32[]{:S(2)}) collective-permute-start(bf16[32,32,128]{2,1,0:T(8,128)(2,1)} %get-tuple-element.145), channel_id=1, source_target_pairs={{0,7},{1,6},{2,5},{3,4},{4,3},{5,2},{6,1},{7,0},{8,15},{9,14},{10,... | collective-permute-start | bytes 786440 | tf_op jit(solution)/shard_map/ppermute | solution.py:385
  142.3 20.0 %collective-permute-start.37 = (bf16[32,16,128]{2,1,0:T(8,128)(2,1)}, bf16[32,16,128]{2,1,0:T(8,128)(2,1)S(1)}, u32[]{:S(2)}, u32[]{:S(2)}) collective-permute-start(bf16[32,16,128]{2,1,0:T(8,128)(2,1)} %get-tuple-element.165), channel_id=1, source_target_pairs={{0,1},{1,0},{2,3},{3,2},{4,5},{5,4},{6,7},{7,6},{8,9},{9,8},{10,11... | collective-permute-start | bytes 393224 | tf_op jit(solution)/shard_map/ppermute | solution.py:385
  144.1 20.2 %collective-permute-start.38 = (bf16[32,16,128]{2,1,0:T(8,128)(2,1)}, bf16[32,16,128]{2,1,0:T(8,128)(2,1)S(1)}, u32[]{:S(2)}, u32[]{:S(2)}) collective-permute-start(bf16[32,16,128]{2,1,0:T(8,128)(2,1)} %get-tuple-element.166), channel_id=1, source_target_pairs={{0,2},{1,3},{2,0},{3,1},{4,6},{5,7},{6,4},{7,5},{8,10},{9,11},{10,... | collective-permute-start | bytes 393224 | tf_op jit(solution)/shard_map/ppermute | solution.py:385
  149.1 16.6 %collective-permute-start.39 = (bf16[32,16,128]{2,1,0:T(8,128)(2,1)}, bf16[32,16,128]{2,1,0:T(8,128)(2,1)S(1)}, u32[]{:S(2)}, u32[]{:S(2)}) collective-permute-start(bf16[32,16,128]{2,1,0:T(8,128)(2,1)} %get-tuple-element.167), channel_id=1, source_target_pairs={{0,3},{1,2},{2,1},{3,0},{4,7},{5,6},{6,5},{7,4},{8,11},{9,10},{10,... | collective-permute-start | bytes 393224 | tf_op jit(solution)/shard_map/ppermute | solution.py:385
  159.3 21.8 %collective-permute-start.40 = (bf16[32,16,128]{2,1,0:T(8,128)(2,1)}, bf16[32,16,128]{2,1,0:T(8,128)(2,1)S(1)}, u32[]{:S(2)}, u32[]{:S(2)}) collective-permute-start(bf16[32,16,128]{2,1,0:T(8,128)(2,1)} %get-tuple-element.168), channel_id=1, source_target_pairs={{0,4},{1,5},{2,6},{3,7},{4,0},{5,1},{6,2},{7,3},{8,12},{9,13},{10,... | collective-permute-start | bytes 393224 | tf_op jit(solution)/shard_map/ppermute | solution.py:385
  162.2 19.1 %collective-permute-start.41 = (bf16[32,16,128]{2,1,0:T(8,128)(2,1)}, bf16[32,16,128]{2,1,0:T(8,128)(2,1)S(1)}, u32[]{:S(2)}, u32[]{:S(2)}) collective-permute-start(bf16[32,16,128]{2,1,0:T(8,128)(2,1)} %get-tuple-element.169), channel_id=1, source_target_pairs={{0,5},{1,4},{2,7},{3,6},{4,1},{5,0},{6,3},{7,2},{8,13},{9,12},{10,... | collective-permute-start | bytes 393224 | tf_op jit(solution)/shard_map/ppermute | solution.py:385
  162.3 25.7 %collective-permute-start.42 = (bf16[32,16,128]{2,1,0:T(8,128)(2,1)}, bf16[32,16,128]{2,1,0:T(8,128)(2,1)S(1)}, u32[]{:S(2)}, u32[]{:S(2)}) collective-permute-start(bf16[32,16,128]{2,1,0:T(8,128)(2,1)} %get-tuple-element.170), channel_id=1, source_target_pairs={{0,6},{1,7},{2,4},{3,5},{4,2},{5,3},{6,0},{7,1},{8,14},{9,15},{10,... | collective-permute-start | bytes 393224 | tf_op jit(solution)/shard_map/ppermute | solution.py:385
  164.3 25.0 %collective-permute-start.43 = (bf16[32,16,128]{2,1,0:T(8,128)(2,1)}, bf16[32,16,128]{2,1,0:T(8,128)(2,1)S(1)}, u32[]{:S(2)}, u32[]{:S(2)}) collective-permute-start(bf16[32,16,128]{2,1,0:T(8,128)(2,1)} %get-tuple-element.171), channel_id=1, source_target_pairs={{0,7},{1,6},{2,5},{3,4},{4,3},{5,2},{6,1},{7,0},{8,15},{9,14},{10,... | collective-permute-start | bytes 393224 | tf_op jit(solution)/shard_map/ppermute | solution.py:385
  165.7 25.4 %collective-permute-start.44 = (bf16[32,16,128]{2,1,0:T(8,128)(2,1)}, bf16[32,16,128]{2,1,0:T(8,128)(2,1)}, u32[]{:S(2)}, u32[]{:S(2)}) collective-permute-start(bf16[32,16,128]{2,1,0:T(8,128)(2,1)} %get-tuple-element.175), channel_id=1, source_target_pairs={{0,1},{1,0},{2,3},{3,2},{4,5},{5,4},{6,7},{7,6},{8,9},{9,8},{10,11... | collective-permute-start | bytes 393224 | tf_op jit(solution)/shard_map/ppermute | solution.py:385
  181.1 21.7 %collective-permute-start.45 = (bf16[32,16,128]{2,1,0:T(8,128)(2,1)}, bf16[32,16,128]{2,1,0:T(8,128)(2,1)}, u32[]{:S(2)}, u32[]{:S(2)}) collective-permute-start(bf16[32,16,128]{2,1,0:T(8,128)(2,1)} %get-tuple-element.176), channel_id=1, source_target_pairs={{0,2},{1,3},{2,0},{3,1},{4,6},{5,7},{6,4},{7,5},{8,10},{9,11},{10,... | collective-permute-start | bytes 393224 | tf_op jit(solution)/shard_map/ppermute | solution.py:385
  181.2 22.9 %collective-permute-start.46 = (bf16[32,16,128]{2,1,0:T(8,128)(2,1)}, bf16[32,16,128]{2,1,0:T(8,128)(2,1)}, u32[]{:S(2)}, u32[]{:S(2)}) collective-permute-start(bf16[32,16,128]{2,1,0:T(8,128)(2,1)} %get-tuple-element.177), channel_id=1, source_target_pairs={{0,3},{1,2},{2,1},{3,0},{4,7},{5,6},{6,5},{7,4},{8,11},{9,10},{10,... | collective-permute-start | bytes 393224 | tf_op jit(solution)/shard_map/ppermute | solution.py:385
  188.0 17.0 %collective-permute-start.47 = (bf16[32,16,128]{2,1,0:T(8,128)(2,1)}, bf16[32,16,128]{2,1,0:T(8,128)(2,1)}, u32[]{:S(2)}, u32[]{:S(2)}) collective-permute-start(bf16[32,16,128]{2,1,0:T(8,128)(2,1)} %get-tuple-element.178), channel_id=1, source_target_pairs={{0,4},{1,5},{2,6},{3,7},{4,0},{5,1},{6,2},{7,3},{8,12},{9,13},{10,... | collective-permute-start | bytes 393224 | tf_op jit(solution)/shard_map/ppermute | solution.py:385
  189.3 16.8 %collective-permute-start.48 = (bf16[32,16,128]{2,1,0:T(8,128)(2,1)}, bf16[32,16,128]{2,1,0:T(8,128)(2,1)}, u32[]{:S(2)}, u32[]{:S(2)}) collective-permute-start(bf16[32,16,128]{2,1,0:T(8,128)(2,1)} %get-tuple-element.179), channel_id=1, source_target_pairs={{0,5},{1,4},{2,7},{3,6},{4,1},{5,0},{6,3},{7,2},{8,13},{9,12},{10,... | collective-permute-start | bytes 393224 | tf_op jit(solution)/shard_map/ppermute | solution.py:385
  191.0 15.3 %collective-permute-start.49 = (bf16[32,16,128]{2,1,0:T(8,128)(2,1)}, bf16[32,16,128]{2,1,0:T(8,128)(2,1)}, u32[]{:S(2)}, u32[]{:S(2)}) collective-permute-start(bf16[32,16,128]{2,1,0:T(8,128)(2,1)} %get-tuple-element.180), channel_id=1, source_target_pairs={{0,6},{1,7},{2,4},{3,5},{4,2},{5,3},{6,0},{7,1},{8,14},{9,15},{10,... | collective-permute-start | bytes 393224 | tf_op jit(solution)/shard_map/ppermute | solution.py:385
  213.1 25.9 %collective-permute-start.30 = (bf16[32,32,128]{2,1,0:T(8,128)(2,1)S(1)}, bf16[32,32,128]{2,1,0:T(8,128)(2,1)S(1)}, u32[]{:S(2)}, u32[]{:S(2)}) collective-permute-start(bf16[32,32,128]{2,1,0:T(8,128)(2,1)S(1)} %copy-done.52), channel_id=1, source_target_pairs={{0,1},{1,0},{2,3},{3,2},{4,5},{5,4},{6,7},{7,6},{8,9},{9,8},{10,11... | collective-permute-start | bytes 786440 | tf_op jit(solution)/shard_map/ppermute | solution.py:385
  214.4 26.3 %collective-permute-start.31 = (bf16[32,32,128]{2,1,0:T(8,128)(2,1)S(1)}, bf16[32,32,128]{2,1,0:T(8,128)(2,1)S(1)}, u32[]{:S(2)}, u32[]{:S(2)}) collective-permute-start(bf16[32,32,128]{2,1,0:T(8,128)(2,1)S(1)} %copy-done.51), channel_id=1, source_target_pairs={{0,2},{1,3},{2,0},{3,1},{4,6},{5,7},{6,4},{7,5},{8,10},{9,11},{10,... | collective-permute-start | bytes 786440 | tf_op jit(solution)/shard_map/ppermute | solution.py:385
  220.3 15.6 %collective-permute-start.64 = (bf16[32,16,128]{2,1,0:T(8,128)(2,1)}, bf16[32,16,128]{2,1,0:T(8,128)(2,1)S(1)}, u32[]{:S(2)}, u32[]{:S(2)}) collective-permute-start(bf16[32,16,128]{2,1,0:T(8,128)(2,1)} %get-tuple-element.199), channel_id=1, source_target_pairs={{0,7},{1,6},{2,5},{3,4},{4,3},{5,2},{6,1},{7,0},{8,15},{9,14},{10,... | collective-permute-start | bytes 393224 | tf_op jit(solution)/shard_map/ppermute | solution.py:385
  226.0 16.5 %collective-permute-start.32 = (bf16[32,32,128]{2,1,0:T(8,128)(2,1)S(1)}, bf16[32,32,128]{2,1,0:T(8,128)(2,1)S(1)}, u32[]{:S(2)}, u32[]{:S(2)}) collective-permute-start(bf16[32,32,128]{2,1,0:T(8,128)(2,1)S(1)} %copy-done.50), channel_id=1, source_target_pairs={{0,3},{1,2},{2,1},{3,0},{4,7},{5,6},{6,5},{7,4},{8,11},{9,10},{10,... | collective-permute-start | bytes 786440 | tf_op jit(solution)/shard_map/ppermute | solution.py:385
  231.4 34.2 %collective-permute-start.33 = (bf16[32,32,128]{2,1,0:T(8,128)(2,1)S(1)}, bf16[32,32,128]{2,1,0:T(8,128)(2,1)S(1)}, u32[]{:S(2)}, u32[]{:S(2)}) collective-permute-start(bf16[32,32,128]{2,1,0:T(8,128)(2,1)S(1)} %copy-done.49), channel_id=1, source_target_pairs={{0,4},{1,5},{2,6},{3,7},{4,0},{5,1},{6,2},{7,3},{8,12},{9,13},{10,... | collective-permute-start | bytes 786440 | tf_op jit(solution)/shard_map/ppermute | solution.py:385
  236.6 34.4 %collective-permute-start.34 = (bf16[32,32,128]{2,1,0:T(8,128)(2,1)S(1)}, bf16[32,32,128]{2,1,0:T(8,128)(2,1)S(1)}, u32[]{:S(2)}, u32[]{:S(2)}) collective-permute-start(bf16[32,32,128]{2,1,0:T(8,128)(2,1)S(1)} %copy-done.48), channel_id=1, source_target_pairs={{0,5},{1,4},{2,7},{3,6},{4,1},{5,0},{6,3},{7,2},{8,13},{9,12},{10,... | collective-permute-start | bytes 786440 | tf_op jit(solution)/shard_map/ppermute | solution.py:385
  239.0 31.9 %collective-permute-start.35 = (bf16[32,32,128]{2,1,0:T(8,128)(2,1)S(1)}, bf16[32,32,128]{2,1,0:T(8,128)(2,1)S(1)}, u32[]{:S(2)}, u32[]{:S(2)}) collective-permute-start(bf16[32,32,128]{2,1,0:T(8,128)(2,1)S(1)} %copy-done.46), channel_id=1, source_target_pairs={{0,6},{1,7},{2,4},{3,5},{4,2},{5,3},{6,0},{7,1},{8,14},{9,15},{10,... | collective-permute-start | bytes 786440 | tf_op jit(solution)/shard_map/ppermute | solution.py:385
  240.7 37.3 %collective-permute-start.36 = (bf16[32,32,128]{2,1,0:T(8,128)(2,1)S(1)}, bf16[32,32,128]{2,1,0:T(8,128)(2,1)S(1)}, u32[]{:S(2)}, u32[]{:S(2)}) collective-permute-start(bf16[32,32,128]{2,1,0:T(8,128)(2,1)S(1)} %copy-done.44), channel_id=1, source_target_pairs={{0,7},{1,6},{2,5},{3,4},{4,3},{5,2},{6,1},{7,0},{8,15},{9,14},{10,... | collective-permute-start | bytes 786440 | tf_op jit(solution)/shard_map/ppermute | solution.py:385
  242.4 61.7 %collective-permute-start.51 = (bf16[32,32,128]{2,1,0:T(8,128)(2,1)S(1)}, bf16[32,32,128]{2,1,0:T(8,128)(2,1)S(1)}, u32[]{:S(2)}, u32[]{:S(2)}) collective-permute-start(bf16[32,32,128]{2,1,0:T(8,128)(2,1)S(1)} %copy-done.55), channel_id=1, source_target_pairs={{0,1},{1,0},{2,3},{3,2},{4,5},{5,4},{6,7},{7,6},{8,9},{9,8},{10,11... | collective-permute-start | bytes 786440 | tf_op jit(solution)/shard_map/ppermute | solution.py:385
  265.6 40.4 %collective-permute-start.52 = (bf16[32,32,128]{2,1,0:T(8,128)(2,1)S(1)}, bf16[32,32,128]{2,1,0:T(8,128)(2,1)S(1)}, u32[]{:S(2)}, u32[]{:S(2)}) collective-permute-start(bf16[32,32,128]{2,1,0:T(8,128)(2,1)S(1)} %copy-done.53), channel_id=1, source_target_pairs={{0,2},{1,3},{2,0},{3,1},{4,6},{5,7},{6,4},{7,5},{8,10},{9,11},{10,... | collective-permute-start | bytes 786440 | tf_op jit(solution)/shard_map/ppermute | solution.py:385
  270.9 49.8 %collective-permute-start.53 = (bf16[32,32,128]{2,1,0:T(8,128)(2,1)}, bf16[32,32,128]{2,1,0:T(8,128)(2,1)S(1)}, u32[]{:S(2)}, u32[]{:S(2)}) collective-permute-start(bf16[32,32,128]{2,1,0:T(8,128)(2,1)} %get-tuple-element.185), channel_id=1, source_target_pairs={{0,3},{1,2},{2,1},{3,0},{4,7},{5,6},{6,5},{7,4},{8,11},{9,10},{10,... | collective-permute-start | bytes 786440 | tf_op jit(solution)/shard_map/ppermute | solution.py:385
  271.0 50.3 %collective-permute-start.54 = (bf16[32,32,128]{2,1,0:T(8,128)(2,1)}, bf16[32,32,128]{2,1,0:T(8,128)(2,1)S(1)}, u32[]{:S(2)}, u32[]{:S(2)}) collective-permute-start(bf16[32,32,128]{2,1,0:T(8,128)(2,1)} %get-tuple-element.186), channel_id=1, source_target_pairs={{0,4},{1,5},{2,6},{3,7},{4,0},{5,1},{6,2},{7,3},{8,12},{9,13},{10,... | collective-permute-start | bytes 786440 | tf_op jit(solution)/shard_map/ppermute | solution.py:385
  278.7 42.5 %collective-permute-start.55 = (bf16[32,32,128]{2,1,0:T(8,128)(2,1)S(1)}, bf16[32,32,128]{2,1,0:T(8,128)(2,1)S(1)}, u32[]{:S(2)}, u32[]{:S(2)}) collective-permute-start(bf16[32,32,128]{2,1,0:T(8,128)(2,1)S(1)} %copy-done.47), channel_id=1, source_target_pairs={{0,5},{1,4},{2,7},{3,6},{4,1},{5,0},{6,3},{7,2},{8,13},{9,12},{10,... | collective-permute-start | bytes 786440 | tf_op jit(solution)/shard_map/ppermute | solution.py:385
  304.2 18.5 %collective-permute-start.56 = (bf16[32,32,128]{2,1,0:T(8,128)(2,1)S(1)}, bf16[32,32,128]{2,1,0:T(8,128)(2,1)S(1)}, u32[]{:S(2)}, u32[]{:S(2)}) collective-permute-start(bf16[32,32,128]{2,1,0:T(8,128)(2,1)S(1)} %copy-done.45), channel_id=1, source_target_pairs={{0,6},{1,7},{2,4},{3,5},{4,2},{5,3},{6,0},{7,1},{8,14},{9,15},{10,... | collective-permute-start | bytes 786440 | tf_op jit(solution)/shard_map/ppermute | solution.py:385
  306.1 18.9 %collective-permute-start.57 = (bf16[32,32,128]{2,1,0:T(8,128)(2,1)S(1)}, bf16[32,32,128]{2,1,0:T(8,128)(2,1)S(1)}, u32[]{:S(2)}, u32[]{:S(2)}) collective-permute-start(bf16[32,32,128]{2,1,0:T(8,128)(2,1)S(1)} %copy-done.43), channel_id=1, source_target_pairs={{0,7},{1,6},{2,5},{3,4},{4,3},{5,2},{6,1},{7,0},{8,15},{9,14},{10,... | collective-permute-start | bytes 786440 | tf_op jit(solution)/shard_map/ppermute | solution.py:385
  322.7 24.4 %collective-permute-start.75 = (bf16[32,16,128]{2,1,0:T(8,128)(2,1)}, bf16[32,16,128]{2,1,0:T(8,128)(2,1)S(1)}, u32[]{:S(2)}, u32[]{:S(2)}) collective-permute-start(bf16[32,16,128]{2,1,0:T(8,128)(2,1)} %get-tuple-element.213), channel_id=1, source_target_pairs={{0,4},{1,5},{2,6},{3,7},{4,0},{5,1},{6,2},{7,3},{8,12},{9,13},{10,... | collective-permute-start | bytes 393224 | tf_op jit(solution)/shard_map/ppermute | solution.py:385
  324.9 24.5 %collective-permute-start.76 = (bf16[32,16,128]{2,1,0:T(8,128)(2,1)}, bf16[32,16,128]{2,1,0:T(8,128)(2,1)S(1)}, u32[]{:S(2)}, u32[]{:S(2)}) collective-permute-start(bf16[32,16,128]{2,1,0:T(8,128)(2,1)} %get-tuple-element.214), channel_id=1, source_target_pairs={{0,5},{1,4},{2,7},{3,6},{4,1},{5,0},{6,3},{7,2},{8,13},{9,12},{10,... | collective-permute-start | bytes 393224 | tf_op jit(solution)/shard_map/ppermute | solution.py:385
  330.2 19.4 %collective-permute-start.77 = (bf16[32,16,128]{2,1,0:T(8,128)(2,1)}, bf16[32,16,128]{2,1,0:T(8,128)(2,1)S(1)}, u32[]{:S(2)}, u32[]{:S(2)}) collective-permute-start(bf16[32,16,128]{2,1,0:T(8,128)(2,1)} %get-tuple-element.215), channel_id=1, source_target_pairs={{0,6},{1,7},{2,4},{3,5},{4,2},{5,3},{6,0},{7,1},{8,14},{9,15},{10,... | collective-permute-start | bytes 393224 | tf_op jit(solution)/shard_map/ppermute | solution.py:385
  331.8 28.1 %collective-permute-start.65 = (bf16[32,32,128]{2,1,0:T(8,128)(2,1)}, bf16[32,32,128]{2,1,0:T(8,128)(2,1)S(1)}, u32[]{:S(2)}, u32[]{:S(2)}) collective-permute-start(bf16[32,32,128]{2,1,0:T(8,128)(2,1)} %get-tuple-element.201), channel_id=1, source_target_pairs={{0,1},{1,0},{2,3},{3,2},{4,5},{5,4},{6,7},{7,6},{8,9},{9,8},{10,11... | collective-permute-start | bytes 786440 | tf_op jit(solution)/shard_map/ppermute | solution.py:385
  331.8 30.3 %collective-permute-start.66 = (bf16[32,32,128]{2,1,0:T(8,128)(2,1)}, bf16[32,32,128]{2,1,0:T(8,128)(2,1)S(1)}, u32[]{:S(2)}, u32[]{:S(2)}) collective-permute-start(bf16[32,32,128]{2,1,0:T(8,128)(2,1)} %get-tuple-element.202), channel_id=1, source_target_pairs={{0,2},{1,3},{2,0},{3,1},{4,6},{5,7},{6,4},{7,5},{8,10},{9,11},{10,... | collective-permute-start | bytes 786440 | tf_op jit(solution)/shard_map/ppermute | solution.py:385
  354.4 20.0 %collective-permute-start.67 = (bf16[32,32,128]{2,1,0:T(8,128)(2,1)}, bf16[32,32,128]{2,1,0:T(8,128)(2,1)S(1)}, u32[]{:S(2)}, u32[]{:S(2)}) collective-permute-start(bf16[32,32,128]{2,1,0:T(8,128)(2,1)} %get-tuple-element.203), channel_id=1, source_target_pairs={{0,3},{1,2},{2,1},{3,0},{4,7},{5,6},{6,5},{7,4},{8,11},{9,10},{10,... | collective-permute-start | bytes 786440 | tf_op jit(solution)/shard_map/ppermute | solution.py:385
  357.5 32.9 %collective-permute-start.68 = (bf16[32,32,128]{2,1,0:T(8,128)(2,1)}, bf16[32,32,128]{2,1,0:T(8,128)(2,1)S(1)}, u32[]{:S(2)}, u32[]{:S(2)}) collective-permute-start(bf16[32,32,128]{2,1,0:T(8,128)(2,1)} %get-tuple-element.204), channel_id=1, source_target_pairs={{0,4},{1,5},{2,6},{3,7},{4,0},{5,1},{6,2},{7,3},{8,12},{9,13},{10,... | collective-permute-start | bytes 786440 | tf_op jit(solution)/shard_map/ppermute | solution.py:385
  358.3 38.7 %collective-permute-start.69 = (bf16[32,32,128]{2,1,0:T(8,128)(2,1)}, bf16[32,32,128]{2,1,0:T(8,128)(2,1)S(1)}, u32[]{:S(2)}, u32[]{:S(2)}) collective-permute-start(bf16[32,32,128]{2,1,0:T(8,128)(2,1)} %get-tuple-element.205), channel_id=1, source_target_pairs={{0,5},{1,4},{2,7},{3,6},{4,1},{5,0},{6,3},{7,2},{8,13},{9,12},{10,... | collective-permute-start | bytes 786440 | tf_op jit(solution)/shard_map/ppermute | solution.py:385
  359.8 37.2 %collective-permute-start.70 = (bf16[32,32,128]{2,1,0:T(8,128)(2,1)}, bf16[32,32,128]{2,1,0:T(8,128)(2,1)S(1)}, u32[]{:S(2)}, u32[]{:S(2)}) collective-permute-start(bf16[32,32,128]{2,1,0:T(8,128)(2,1)} %get-tuple-element.206), channel_id=1, source_target_pairs={{0,6},{1,7},{2,4},{3,5},{4,2},{5,3},{6,0},{7,1},{8,14},{9,15},{10,... | collective-permute-start | bytes 786440 | tf_op jit(solution)/shard_map/ppermute | solution.py:385
  362.1 37.6 %collective-permute-start.71 = (bf16[32,32,128]{2,1,0:T(8,128)(2,1)S(1)}, bf16[32,32,128]{2,1,0:T(8,128)(2,1)S(1)}, u32[]{:S(2)}, u32[]{:S(2)}) collective-permute-start(bf16[32,32,128]{2,1,0:T(8,128)(2,1)S(1)} %copy-done.54), channel_id=1, source_target_pairs={{0,7},{1,6},{2,5},{3,4},{4,3},{5,2},{6,1},{7,0},{8,15},{9,14},{10,... | collective-permute-start | bytes 786440 | tf_op jit(solution)/shard_map/ppermute | solution.py:385
  374.4 40.5 %collective-permute-start.81 = (bf16[32,16,128]{2,1,0:T(8,128)(2,1)}, bf16[32,16,128]{2,1,0:T(8,128)(2,1)S(1)}, u32[]{:S(2)}, u32[]{:S(2)}) collective-permute-start(bf16[32,16,128]{2,1,0:T(8,128)(2,1)} %get-tuple-element.221), channel_id=1, source_target_pairs={{0,3},{1,2},{2,1},{3,0},{4,7},{5,6},{6,5},{7,4},{8,11},{9,10},{10,... | collective-permute-start | bytes 393224 | tf_op jit(solution)/shard_map/ppermute | solution.py:385
  390.4 30.8 %collective-permute-start.82 = (bf16[32,16,128]{2,1,0:T(8,128)(2,1)}, bf16[32,16,128]{2,1,0:T(8,128)(2,1)S(1)}, u32[]{:S(2)}, u32[]{:S(2)}) collective-permute-start(bf16[32,16,128]{2,1,0:T(8,128)(2,1)} %get-tuple-element.222), channel_id=1, source_target_pairs={{0,4},{1,5},{2,6},{3,7},{4,0},{5,1},{6,2},{7,3},{8,12},{9,13},{10,... | collective-permute-start | bytes 393224 | tf_op jit(solution)/shard_map/ppermute | solution.py:385
  397.0 25.3 %collective-permute-start.83 = (bf16[32,16,128]{2,1,0:T(8,128)(2,1)}, bf16[32,16,128]{2,1,0:T(8,128)(2,1)S(1)}, u32[]{:S(2)}, u32[]{:S(2)}) collective-permute-start(bf16[32,16,128]{2,1,0:T(8,128)(2,1)} %get-tuple-element.223), channel_id=1, source_target_pairs={{0,5},{1,4},{2,7},{3,6},{4,1},{5,0},{6,3},{7,2},{8,13},{9,12},{10,... | collective-permute-start | bytes 393224 | tf_op jit(solution)/shard_map/ppermute | solution.py:385
  397.0 25.3 %collective-permute-start.84 = (bf16[32,16,128]{2,1,0:T(8,128)(2,1)}, bf16[32,16,128]{2,1,0:T(8,128)(2,1)S(1)}, u32[]{:S(2)}, u32[]{:S(2)}) collective-permute-start(bf16[32,16,128]{2,1,0:T(8,128)(2,1)} %get-tuple-element.224), channel_id=1, source_target_pairs={{0,6},{1,7},{2,4},{3,5},{4,2},{5,3},{6,0},{7,1},{8,14},{9,15},{10,... | collective-permute-start | bytes 393224 | tf_op jit(solution)/shard_map/ppermute | solution.py:385
  399.7 22.6 %collective-permute-start.85 = (bf16[32,16,128]{2,1,0:T(8,128)(2,1)}, bf16[32,16,128]{2,1,0:T(8,128)(2,1)S(1)}, u32[]{:S(2)}, u32[]{:S(2)}) collective-permute-start(bf16[32,16,128]{2,1,0:T(8,128)(2,1)} %get-tuple-element.225), channel_id=1, source_target_pairs={{0,7},{1,6},{2,5},{3,4},{4,3},{5,2},{6,1},{7,0},{8,15},{9,14},{10,... | collective-permute-start | bytes 393224 | tf_op jit(solution)/shard_map/ppermute | solution.py:385
  (127 other events, 4570.1 us)

commit v11 on v10

--- a/solution.py
+++ b/solution.py
@@ -195,7 +195,7 @@
         size = held * rows
         return pl.ds(pl.multiple_of(meta_ref[1 + slot] * size, size), size)
 
-    for slot, ref in enumerate(spectra_refs):
+    for slot, ref in zip(slots_of(len(spectra_refs)), spectra_refs):
         wide[place(slot), :] = ref[...].reshape(held * rows, width).astype(jnp.float32)
     level = level_ref[...]
     sign = jnp.where(
@@ -228,7 +228,7 @@
 def update_kernel(inputs, meta_ref, table_ref, _, *refs):
     restored_refs, (out_ref, turn_ref, whole_rows) = refs[:inputs], refs[-3:]
     held, rows, width = restored_refs[0].shape
-    for slot, ref in enumerate(restored_refs):
+    for slot, ref in zip(slots_of(inputs), restored_refs):
         whole_rows[:, band(meta_ref, slot, width)] = ref[...].reshape(held * rows, width)
     out_ref[...] = jnp.dot(
         whole_rows[...], table_ref[...], preferred_element_type=jnp.float32
@@ -361,11 +361,11 @@
             scratch_shapes=[pltpu.VMEM((group * rows, 2 * F), jnp.bfloat16)],
         ),
         out_shape=[
-            pltpu.HBM((shots, receivers, samples), jnp.float32),
-            pltpu.HBM((8, LANES), jnp.float32),
+            jax.ShapeDtypeStruct((shots, receivers, samples), jnp.float32),
+            jax.ShapeDtypeStruct((8, LANES), jnp.float32),
         ],
         input_output_aliases={} if onto is None else {len(operands) - 1: 0},
-        compiler_params=PARAMS,
+        compiler_params=pltpu.CompilerParams(vmem_limit_bytes=48 * 1024 * 1024),
         cost_estimate=pl.CostEstimate(
             flops=4 * F * shots * rows * samples,
             bytes_accessed=4 * F * shots * rows + 2 * table.size + 4 * shots * rows * samples,
@@ -379,11 +379,18 @@
     return lax.all_to_all(array, "shot", split_axis=0, concat_axis=0, tiled=True)
 
 
+def slots_of(peers):
+    order = [0]
+    for slot in range(peers // 2):
+        order += [peers // 2 + slot] + ([slot + 1] if slot + 1 < peers // 2 else [])
+    return order
+
+
 def exchanged(arrays):
     peers = len(arrays)
     return [
-        lax.ppermute(array, "shot", [(i, i ^ slot) for i in range(peers)]) if slot else array
-        for slot, array in enumerate(arrays)
+        lax.ppermute(arrays[slot], "shot", [(i, i ^ slot) for i in range(peers)]) if slot else arrays[0]
+        for slot in slots_of(peers)
     ]
 
 

time: 437 us -> 433 us (level); the launches traced: 429 us -> 430 us
  waiting for transfers between devices: 95 us -> 75.1 us
  local copies, waits for them, and re-layouts: 8.24 us -> 26.2 us
  starting transfers between devices: 147 us -> 160 us
  Pallas kernels: 165 us -> 155 us
    ppermute x84, waiting for transfers between devices: 92 us -> 72.1 us  [exchanged(): lax.ppermute(arrays[slot], 'shot', [(i, i ^ slot) for i in range(peers)])]
    unnamed x210 -> x178, local copies, waits for them, and re-layouts: 4.55 us -> 22.5 us
    ppermute x84, starting transfers between devices: 144 us -> 157 us  [exchanged(): lax.ppermute(arrays[slot], 'shot', [(i, i ^ slot) for i in range(peers)])]
    pallas_call x6, Pallas kernels: 36.8 us -> 26.4 us  [updated_of(): pl.pallas_call(functools.partial(update_kernel, len(restored)), grid_spec...]
  transfers between devices with their start and end apart: 86 -> 86, of which waited for: 20 -> 18; matrix products, arithmetic and copies ran while one was open for 1% -> 1% of each run, Pallas kernels for 35% -> 33%
where the time goes in v11:
time: 433 us; the launch traced here: 430 us
  starting transfers between devices  160 us (37%)
  Pallas kernels  155 us (36%)
  waiting for transfers between devices  75.1 us (17%)
  local copies, waits for them, and re-layouts  26.2 us (6%)
  blocking collectives  9.91 us (2%)
    ppermute x84, starting transfers between devices, exchanged(): lax.ppermute(arrays[slot], 'shot', [(i, i ^ slot) for i in range(peers)])  157 us
    ppermute x84, waiting for transfers between devices, exchanged(): lax.ppermute(arrays[slot], 'shot', [(i, i ^ slot) for i in range(peers)])  72.1 us
    pallas_call x6, Pallas kernels, spectra_of(): pl.pallas_call(spectra_kernel, grid_spec=pltpu.PrefetchScalarGridSpec(num...  69.1 us
    pallas_call x6, Pallas kernels, shrunk_of(): pl.pallas_call(shots_kernel, grid_spec=pltpu.PrefetchScalarGridSpec(num_s...  59.1 us
    pallas_call x6, Pallas kernels, updated_of(): pl.pallas_call(functools.partial(update_kernel, len(restored)), grid_spec...  26.4 us
    unnamed x178, local copies, waits for them, and re-layouts  22.5 us
    psum x1, blocking collectives, local(): lax.psum(jnp.sum(energy, axis=1), 'patch')  9.91 us
  transfers between devices with their start and end apart: 86, of which 18 were waited for; matrix products, arithmetic and copies ran while one was open for 1% of the time, Pallas kernels for 33%

profile of v11, /device:TPU:0, one launch (start us, length us, event | category | flops | bytes accessed | tf_op | source)
XLA Modules:
  0.0 429.6 jit_solution(15621798979901165263)
XLA Ops:
  3.1 2.4 collective-permute-start
  8.9 3.0 collective-permute-done.1.after_ref
  12.8 9.8 %spectra.6 = (bf16[32,16,128]{2,1,0:T(8,128)(2,1)}, bf16[32,16,128]{2,1,0:T(8,128)(2,1)}, bf16[32,16,128]{2,1,0:T(8,128)(2,1)}, bf16[32,16,128]{2,1,0:T(8,128)(2...) custom-call(s32[9]{0:T(128)} %pad_add_fusion.meta_ref, ...), custom_call_target="tpu_custom_call" | custom-call | flops 1073741824 | bytes 5242880 | tf_op jit(solution)/shard_map/spectra/pallas_call | solution.py:270
  22.6 10.4 %collective-permute-start.2 = (bf16[32,16,128]{2,1,0:T(8,128)(2,1)}, bf16[32,16,128]{2,1,0:T(8,128)(2,1)S(1)}, u32[]{:S(2)}, u32[]{:S(2)}) collective-permute-start(bf16[32,16,128]{2,1,0:T(8,128)(2,1)} %get-tuple-element.119), channel_id=1, source_target_pairs={{0,4},{1,5},{2,6},{3,7},{4,0},{5,1},{6,2},{7,3},{8,12},{9,13},{10,... | collective-permute-start | bytes 393224 | tf_op jit(solution)/shard_map/ppermute | solution.py:392
  36.1 2.5 collective-permute-start.6
  38.6 9.9 %spectra.7 = (bf16[32,16,128]{2,1,0:T(8,128)(2,1)}, bf16[32,16,128]{2,1,0:T(8,128)(2,1)}, bf16[32,16,128]{2,1,0:T(8,128)(2,1)}, bf16[32,16,128]{2,1,0:T(8,128)(2...) custom-call(s32[9]{0:T(128)} %pad_add_fusion.meta_ref, ...), custom_call_target="tpu_custom_call" | custom-call | flops 1073741824 | bytes 5242880 | tf_op jit(solution)/shard_map/spectra/pallas_call | solution.py:270
  53.1 14.7 %spectra.8 = (bf16[32,32,128]{2,1,0:T(8,128)(2,1)}, bf16[32,32,128]{2,1,0:T(8,128)(2,1)}, bf16[32,32,128]{2,1,0:T(8,128)(2,1)}, bf16[32,32,128]{2,1,0:T(8,128)(2...) custom-call(s32[9]{0:T(128)} %pad_add_fusion.meta_ref, ...), custom_call_target="tpu_custom_call" | custom-call | flops 2147483648 | bytes 8388608 | tf_op jit(solution)/shard_map/spectra/pallas_call | solution.py:270
  68.7 2.5 collective-permute-start.13
  71.4 7.3 %shrink.6 = (bf16[32,16,128]{2,1,0:T(8,128)(2,1)}, bf16[32,16,128]{2,1,0:T(8,128)(2,1)}, bf16[32,16,128]{2,1,0:T(8,128)(2,1)}, bf16[32,16,128]{2,1,0:T(8,128)(2,...) custom-call(s32[9]{0:T(128)} %pad_add_fusion.meta_ref, ...), custom_call_target="tpu_custom_call" | custom-call | flops 1073741824 | bytes 2359296 | tf_op jit(solution)/shard_map/shrink/pallas_call | solution.py:320
  80.1 1.8 collective-permute-start.23
  86.4 7.9 %collective-permute-start.16 = (bf16[32,32,128]{2,1,0:T(8,128)(2,1)}, bf16[32,32,128]{2,1,0:T(8,128)(2,1)}, u32[]{:S(2)}, u32[]{:S(2)}) collective-permute-start(bf16[32,32,128]{2,1,0:T(8,128)(2,1)} %get-tuple-element.139), channel_id=1, source_target_pairs={{0,4},{1,5},{2,6},{3,7},{4,0},{5,1},{6,2},{7,3},{8,12},{9,13},{10,... | collective-permute-start | bytes 786440 | tf_op jit(solution)/shard_map/ppermute | solution.py:392
  94.3 8.9 %collective-permute-done.23.refs_1_ = bf16[32,16,128]{2,1,0:T(8,128)(2,1)S(1)} collective-permute-done((bf16[32,16,128]{2,1,0:T(8,128)(2,1)}, bf16[32,16,128]{2,1,0:T(8,128)(2,1)S(1)}, u32[]{:S(2)}, u32[]{:S(2)}) %collective-permute-start.23) | collective-permute-done | bytes 131104 | tf_op jit(solution)/shard_map/ppermute | solution.py:392
  103.6 3.3 collective-permute-start.29
  106.9 4.8 %collective-permute-done.27.refs_5_ = bf16[32,16,128]{2,1,0:T(8,128)(2,1)S(1)} collective-permute-done((bf16[32,16,128]{2,1,0:T(8,128)(2,1)}, bf16[32,16,128]{2,1,0:T(8,128)(2,1)S(1)}, u32[]{:S(2)}, u32[]{:S(2)}) %collective-permute-start.27) | collective-permute-done | bytes 131104 | tf_op jit(solution)/shard_map/ppermute | solution.py:392
  111.7 7.1 %collective-permute-start.18 = (bf16[32,32,128]{2,1,0:T(8,128)(2,1)}, bf16[32,32,128]{2,1,0:T(8,128)(2,1)S(1)}, u32[]{:S(2)}, u32[]{:S(2)}) collective-permute-start(bf16[32,32,128]{2,1,0:T(8,128)(2,1)} %get-tuple-element.141), channel_id=1, source_target_pairs={{0,5},{1,4},{2,7},{3,6},{4,1},{5,0},{6,3},{7,2},{8,13},{9,12},{10,... | collective-permute-start | bytes 786440 | tf_op jit(solution)/shard_map/ppermute | solution.py:392
  119.4 1.9 collective-permute-start.19
  123.3 4.8 %collective-permute-start.21 = (bf16[32,32,128]{2,1,0:T(8,128)(2,1)}, bf16[32,32,128]{2,1,0:T(8,128)(2,1)}, u32[]{:S(2)}, u32[]{:S(2)}) collective-permute-start(bf16[32,32,128]{2,1,0:T(8,128)(2,1)} %get-tuple-element.144), channel_id=1, source_target_pairs={{0,3},{1,2},{2,1},{3,0},{4,7},{5,6},{6,5},{7,4},{8,11},{9,10},{10,... | collective-permute-start | bytes 786440 | tf_op jit(solution)/shard_map/ppermute | solution.py:392
  128.2 14.7 %spectra.9 = (bf16[32,32,128]{2,1,0:T(8,128)(2,1)}, bf16[32,32,128]{2,1,0:T(8,128)(2,1)}, bf16[32,32,128]{2,1,0:T(8,128)(2,1)}, bf16[32,32,128]{2,1,0:T(8,128)(2...) custom-call(s32[9]{0:T(128)} %pad_add_fusion.meta_ref, ...), custom_call_target="tpu_custom_call" | custom-call | flops 2147483648 | bytes 8388608 | tf_op jit(solution)/shard_map/spectra/pallas_call | solution.py:270
  142.9 7.4 %shrink.7 = (bf16[32,16,128]{2,1,0:T(8,128)(2,1)}, bf16[32,16,128]{2,1,0:T(8,128)(2,1)}, bf16[32,16,128]{2,1,0:T(8,128)(2,1)}, bf16[32,16,128]{2,1,0:T(8,128)(2,...) custom-call(s32[9]{0:T(128)} %pad_add_fusion.meta_ref, ...), custom_call_target="tpu_custom_call" | custom-call | flops 1073741824 | bytes 2359296 | tf_op jit(solution)/shard_map/shrink/pallas_call | solution.py:320
  155.5 10.1 %spectra.10 = (bf16[32,16,128]{2,1,0:T(8,128)(2,1)}, bf16[32,16,128]{2,1,0:T(8,128)(2,1)}, bf16[32,16,128]{2,1,0:T(8,128)(2,1)}, bf16[32,16,128]{2,1,0:T(8,128)(...) custom-call(s32[9]{0:T(128)} %pad_add_fusion.meta_ref, ...), custom_call_target="tpu_custom_call" | custom-call | flops 1073741824 | bytes 5242880 | tf_op jit(solution)/shard_map/spectra/pallas_call | solution.py:270
  165.7 2.3 collective-permute-start.41
  168.0 2.4 collective-permute-start.43
  171.2 14.8 %shrink.8 = (bf16[32,32,128]{2,1,0:T(8,128)(2,1)}, bf16[32,32,128]{2,1,0:T(8,128)(2,1)}, bf16[32,32,128]{2,1,0:T(8,128)(2,1)}, bf16[32,32,128]{2,1,0:T(8,128)(2,...) custom-call(s32[9]{0:T(128)} %pad_add_fusion.meta_ref, ...), custom_call_target="tpu_custom_call" | custom-call | flops 2147483648 | bytes 4456448 | tf_op jit(solution)/shard_map/shrink/pallas_call | solution.py:320
  186.8 2.2 collective-permute-start.46
  191.8 3.2 update.6
  195.1 2.3 collective-permute-start.48
  197.4 9.9 %spectra.11 = (bf16[32,16,128]{2,1,0:T(8,128)(2,1)}, bf16[32,16,128]{2,1,0:T(8,128)(2,1)}, bf16[32,16,128]{2,1,0:T(8,128)(2,1)}, bf16[32,16,128]{2,1,0:T(8,128)(...) custom-call(s32[9]{0:T(128)} %pad_add_fusion.meta_ref, ...), custom_call_target="tpu_custom_call" | custom-call | flops 1073741824 | bytes 5242880 | tf_op jit(solution)/shard_map/spectra/pallas_call | solution.py:270
  207.3 2.4 collective-permute-start.50
  210.6 2.2 collective-permute-start.60
  212.9 2.1 collective-permute-done.50.refs_7_
  214.9 8.3 %collective-permute-start.30 = (bf16[32,32,128]{2,1,0:T(8,128)(2,1)}, bf16[32,32,128]{2,1,0:T(8,128)(2,1)S(1)}, u32[]{:S(2)}, u32[]{:S(2)}) collective-permute-start(bf16[32,32,128]{2,1,0:T(8,128)(2,1)} %get-tuple-element.157), channel_id=1, source_target_pairs={{0,4},{1,5},{2,6},{3,7},{4,0},{5,1},{6,2},{7,3},{8,12},{9,13},{10,... | collective-permute-start | bytes 786440 | tf_op jit(solution)/shard_map/ppermute | solution.py:392
  223.2 3.1 collective-permute-done.58.refs_1_
  228.7 6.4 %collective-permute-done.60.refs_3_ = bf16[32,16,128]{2,1,0:T(8,128)(2,1)S(1)} collective-permute-done((bf16[32,16,128]{2,1,0:T(8,128)(2,1)}, bf16[32,16,128]{2,1,0:T(8,128)(2,1)S(1)}, u32[]{:S(2)}, u32[]{:S(2)}) %collective-permute-start.60) | collective-permute-done | bytes 131104 | tf_op jit(solution)/shard_map/ppermute | solution.py:392
  235.1 3.6 collective-permute-start.64
  238.7 8.8 %collective-permute-start.32 = (bf16[32,32,128]{2,1,0:T(8,128)(2,1)}, bf16[32,32,128]{2,1,0:T(8,128)(2,1)S(1)}, u32[]{:S(2)}, u32[]{:S(2)}) collective-permute-start(bf16[32,32,128]{2,1,0:T(8,128)(2,1)} %get-tuple-element.159), channel_id=1, source_target_pairs={{0,5},{1,4},{2,7},{3,6},{4,1},{5,0},{6,3},{7,2},{8,13},{9,12},{10,... | collective-permute-start | bytes 786440 | tf_op jit(solution)/shard_map/ppermute | solution.py:392
  247.5 2.6 collective-permute-start.33
  252.3 4.9 %collective-permute-start.35 = (bf16[32,32,128]{2,1,0:T(8,128)(2,1)}, bf16[32,32,128]{2,1,0:T(8,128)(2,1)S(1)}, u32[]{:S(2)}, u32[]{:S(2)}) collective-permute-start(bf16[32,32,128]{2,1,0:T(8,128)(2,1)} %get-tuple-element.162), channel_id=1, source_target_pairs={{0,3},{1,2},{2,1},{3,0},{4,7},{5,6},{6,5},{7,4},{8,11},{9,10},{10,... | collective-permute-start | bytes 786440 | tf_op jit(solution)/shard_map/ppermute | solution.py:392
  257.2 3.8 collective-permute-done.32.refs_3_
  261.1 5.2 %collective-permute-start.51 = (bf16[32,32,128]{2,1,0:T(8,128)(2,1)}, bf16[32,32,128]{2,1,0:T(8,128)(2,1)S(1)}, u32[]{:S(2)}, u32[]{:S(2)}) collective-permute-start(bf16[32,32,128]{2,1,0:T(8,128)(2,1)} %get-tuple-element.183), channel_id=1, source_target_pairs={{0,4},{1,5},{2,6},{3,7},{4,0},{5,1},{6,2},{7,3},{8,12},{9,13},{10,... | collective-permute-start | bytes 786440 | tf_op jit(solution)/shard_map/ppermute | solution.py:392
  267.1 5.6 %collective-permute-start.53 = (bf16[32,32,128]{2,1,0:T(8,128)(2,1)}, bf16[32,32,128]{2,1,0:T(8,128)(2,1)S(1)}, u32[]{:S(2)}, u32[]{:S(2)}) collective-permute-start(bf16[32,32,128]{2,1,0:T(8,128)(2,1)} %get-tuple-element.185), channel_id=1, source_target_pairs={{0,5},{1,4},{2,7},{3,6},{4,1},{5,0},{6,3},{7,2},{8,13},{9,12},{10,... | collective-permute-start | bytes 786440 | tf_op jit(solution)/shard_map/ppermute | solution.py:392
  272.7 2.9 collective-permute-done.35.refs_6_
  275.7 13.2 %collective-permute-start.54 = (bf16[32,32,128]{2,1,0:T(8,128)(2,1)}, bf16[32,32,128]{2,1,0:T(8,128)(2,1)S(1)}, u32[]{:S(2)}, u32[]{:S(2)}) collective-permute-start(bf16[32,32,128]{2,1,0:T(8,128)(2,1)} %get-tuple-element.186), channel_id=1, source_target_pairs={{0,2},{1,3},{2,0},{3,1},{4,6},{5,7},{6,4},{7,5},{8,10},{9,11},{10,... | collective-permute-start | bytes 786440 | tf_op jit(solution)/shard_map/ppermute | solution.py:392
  291.2 14.6 %shrink.9 = (bf16[32,32,128]{2,1,0:T(8,128)(2,1)}, bf16[32,32,128]{2,1,0:T(8,128)(2,1)}, bf16[32,32,128]{2,1,0:T(8,128)(2,1)}, bf16[32,32,128]{2,1,0:T(8,128)(2,...) custom-call(s32[9]{0:T(128)} %pad_add_fusion.meta_ref, ...), custom_call_target="tpu_custom_call" | custom-call | flops 2147483648 | bytes 4456448 | tf_op jit(solution)/shard_map/shrink/pallas_call | solution.py:320
  305.8 2.1 collective-permute-done.51.refs_1_
  307.9 4.0 collective-permute-start.56
  316.0 3.2 update.7
  319.8 7.4 %shrink.10 = (bf16[32,16,128]{2,1,0:T(8,128)(2,1)}, bf16[32,16,128]{2,1,0:T(8,128)(2,1)}, bf16[32,16,128]{2,1,0:T(8,128)(2,1)}, bf16[32,16,128]{2,1,0:T(8,128)(2...) custom-call(s32[9]{0:T(128)} %pad_add_fusion.meta_ref, ...), custom_call_target="tpu_custom_call" | custom-call | flops 1073741824 | bytes 2359296 | tf_op jit(solution)/shard_map/shrink/pallas_call | solution.py:320
  330.2 2.2 collective-permute-start.74
  332.6 2.0 collective-permute-start.76
  334.6 6.4 %collective-permute-done.72.refs_1_ = bf16[32,16,128]{2,1,0:T(8,128)(2,1)S(1)} collective-permute-done((bf16[32,16,128]{2,1,0:T(8,128)(2,1)}, bf16[32,16,128]{2,1,0:T(8,128)(2,1)S(1)}, u32[]{:S(2)}, u32[]{:S(2)}) %collective-permute-start.72) | collective-permute-done | bytes 131104 | tf_op jit(solution)/shard_map/ppermute | solution.py:392
  341.0 2.0 collective-permute-start.65
  343.0 3.8 collective-permute-done.74.refs_3_
  350.2 6.2 %update.8 = (f32[32,128,1024]{2,1,0:T(8,128)}, f32[8,128]{1,0:T(8,128)S(1)}) custom-call(s32[9]{0:T(128)S(1)} %copy-done.33, bf16[1024,1024]{1,0:T(8,128)(2,1)S(1)} %copy-done, bf16[32,16,128]{2,1,0:T(8,128)(2,1)S(1)} %copy-done.4, bf16[32,32,128]{2,1,0:T(8,128)(2,1)S(1)} %copy-done.7, ...), custom_call_target="tpu_custom_call", output_to_operand_aliasing={{0}: (11, {})} | custom-call | flops 2147483648 | bytes 8388608 | tf_op jit(solution)/shard_map/update/pallas_call | solution.py:351
  357.0 7.6 %shrink.11 = (bf16[32,16,128]{2,1,0:T(8,128)(2,1)}, bf16[32,16,128]{2,1,0:T(8,128)(2,1)}, bf16[32,16,128]{2,1,0:T(8,128)(2,1)}, bf16[32,16,128]{2,1,0:T(8,128)(2...) custom-call(s32[9]{0:T(128)} %pad_add_fusion.meta_ref, ...), custom_call_target="tpu_custom_call" | custom-call | flops 1073741824 | bytes 2359296 | tf_op jit(solution)/shard_map/shrink/pallas_call | solution.py:320
  365.3 1.9 collective-permute-start.78
  367.2 5.3 %collective-permute-done.78.refs_7_ = bf16[32,16,128]{2,1,0:T(8,128)(2,1)S(1)} collective-permute-done((bf16[32,16,128]{2,1,0:T(8,128)(2,1)}, bf16[32,16,128]{2,1,0:T(8,128)(2,1)S(1)}, u32[]{:S(2)}, u32[]{:S(2)}) %collective-permute-start.78) | collective-permute-done | bytes 131104 | tf_op jit(solution)/shard_map/ppermute | solution.py:392
  373.2 11.2 %collective-permute-done.79.refs_1_ = bf16[32,16,128]{2,1,0:T(8,128)(2,1)S(1)} collective-permute-done((bf16[32,16,128]{2,1,0:T(8,128)(2,1)}, bf16[32,16,128]{2,1,0:T(8,128)(2,1)S(1)}, u32[]{:S(2)}, u32[]{:S(2)}) %collective-permute-start.79) | collective-permute-done | bytes 131104 | tf_op jit(solution)/shard_map/ppermute | solution.py:392
  387.6 2.8 collective-permute-start.71
  391.3 9.9 %psum.7 = f32[32]{0:T(128)S(1)} all-reduce(f32[32]{0:T(128)S(1)} %add_reduce_fusion), channel_id=1, replica_groups=mesh['patch'=4,'shot'=8] {'patch'}, use_global_device_ids=true, to_apply=%region_1.0 | all-reduce | flops 32 | bytes 256 | tf_op jit(solution)/shard_map/psum | solution.py:517
  401.8 2.0 collective-permute-start.83
  403.9 8.6 %collective-permute-done.70.refs_6_ = bf16[32,32,128]{2,1,0:T(8,128)(2,1)} collective-permute-done((bf16[32,32,128]{2,1,0:T(8,128)(2,1)}, bf16[32,32,128]{2,1,0:T(8,128)(2,1)}, u32[]{:S(2)}, u32[]{:S(2)}) %collective-permute-start.70) | collective-permute-done | bytes 262176 | tf_op jit(solution)/shard_map/ppermute | solution.py:392
  414.8 6.4 %update.9 = (f32[32,128,1024]{2,1,0:T(8,128)}, f32[8,128]{1,0:T(8,128)S(1)}) custom-call(s32[9]{0:T(128)S(1)} %copy-done.34, bf16[1024,1024]{1,0:T(8,128)(2,1)S(1)} %copy-done, bf16[32,16,128]{2,1,0:T(8,128)(2,1)S(1)} %copy-done.6, bf16[32,32,128]{2,1,0:T(8,128)(2,1)S(1)} %copy-done.2, ...), custom_call_target="tpu_custom_call", output_to_operand_aliasing={{0}: (11, {})} | custom-call | flops 2147483648 | bytes 8388608 | tf_op jit(solution)/shard_map/update/pallas_call | solution.py:351
  422.1 4.1 update.10
  426.4 3.3 update.11
  (316 shorter events, 63.8 us)
Async XLA Ops:
  22.6 25.9 %collective-permute-start.2 = (bf16[32,16,128]{2,1,0:T(8,128)(2,1)}, bf16[32,16,128]{2,1,0:T(8,128)(2,1)S(1)}, u32[]{:S(2)}, u32[]{:S(2)}) collective-permute-start(bf16[32,16,128]{2,1,0:T(8,128)(2,1)} %get-tuple-element.119), channel_id=1, source_target_pairs={{0,4},{1,5},{2,6},{3,7},{4,0},{5,1},{6,2},{7,3},{8,12},{9,13},{10,... | collective-permute-start | bytes 393224 | tf_op jit(solution)/shard_map/ppermute | solution.py:392
  34.7 17.2 %collective-permute-start.5 = (bf16[32,16,128]{2,1,0:T(8,128)(2,1)}, bf16[32,16,128]{2,1,0:T(8,128)(2,1)S(1)}, u32[]{:S(2)}, u32[]{:S(2)}) collective-permute-start(bf16[32,16,128]{2,1,0:T(8,128)(2,1)} %get-tuple-element.122), channel_id=1, source_target_pairs={{0,2},{1,3},{2,0},{3,1},{4,6},{5,7},{6,4},{7,5},{8,10},{9,11},{10,... | collective-permute-start | bytes 393224 | tf_op jit(solution)/shard_map/ppermute | solution.py:392
  36.1 15.8 %collective-permute-start.6 = (bf16[32,16,128]{2,1,0:T(8,128)(2,1)}, bf16[32,16,128]{2,1,0:T(8,128)(2,1)S(1)}, u32[]{:S(2)}, u32[]{:S(2)}) collective-permute-start(bf16[32,16,128]{2,1,0:T(8,128)(2,1)} %get-tuple-element.123), channel_id=1, source_target_pairs={{0,6},{1,7},{2,4},{3,5},{4,2},{5,3},{6,0},{7,1},{8,14},{9,15},{10,... | collective-permute-start | bytes 393224 | tf_op jit(solution)/shard_map/ppermute | solution.py:392
  48.5 19.3 %collective-permute-start.7 = (bf16[32,16,128]{2,1,0:T(8,128)(2,1)S(1)}, bf16[32,16,128]{2,1,0:T(8,128)(2,1)S(1)}, u32[]{:S(2)}, u32[]{:S(2)}) collective-permute-start(bf16[32,16,128]{2,1,0:T(8,128)(2,1)S(1)} %copy-done.86), channel_id=1, source_target_pairs={{0,3},{1,2},{2,1},{3,0},{4,7},{5,6},{6,5},{7,4},{8,11},{9,10},{10,... | collective-permute-start | bytes 393224 | tf_op jit(solution)/shard_map/ppermute | solution.py:392
  48.6 20.1 %collective-permute-start.8 = (bf16[32,16,128]{2,1,0:T(8,128)(2,1)S(1)}, bf16[32,16,128]{2,1,0:T(8,128)(2,1)S(1)}, u32[]{:S(2)}, u32[]{:S(2)}) collective-permute-start(bf16[32,16,128]{2,1,0:T(8,128)(2,1)S(1)} %copy-done.85), channel_id=1, source_target_pairs={{0,7},{1,6},{2,5},{3,4},{4,3},{5,2},{6,1},{7,0},{8,15},{9,14},{10,... | collective-permute-start | bytes 393224 | tf_op jit(solution)/shard_map/ppermute | solution.py:392
  50.1 21.2 %collective-permute-start.9 = (bf16[32,16,128]{2,1,0:T(8,128)(2,1)}, bf16[32,16,128]{2,1,0:T(8,128)(2,1)S(1)}, u32[]{:S(2)}, u32[]{:S(2)}) collective-permute-start(bf16[32,16,128]{2,1,0:T(8,128)(2,1)} %get-tuple-element.129), channel_id=1, source_target_pairs={{0,4},{1,5},{2,6},{3,7},{4,0},{5,1},{6,2},{7,3},{8,12},{9,13},{10,... | collective-permute-start | bytes 393224 | tf_op jit(solution)/shard_map/ppermute | solution.py:392
  51.9 26.8 %collective-permute-start.10 = (bf16[32,16,128]{2,1,0:T(8,128)(2,1)}, bf16[32,16,128]{2,1,0:T(8,128)(2,1)S(1)}, u32[]{:S(2)}, u32[]{:S(2)}) collective-permute-start(bf16[32,16,128]{2,1,0:T(8,128)(2,1)} %get-tuple-element.130), channel_id=1, source_target_pairs={{0,1},{1,0},{2,3},{3,2},{4,5},{5,4},{6,7},{7,6},{8,9},{9,8},{10,11... | collective-permute-start | bytes 393224 | tf_op jit(solution)/shard_map/ppermute | solution.py:392
  51.9 28.2 %collective-permute-start.11 = (bf16[32,16,128]{2,1,0:T(8,128)(2,1)}, bf16[32,16,128]{2,1,0:T(8,128)(2,1)S(1)}, u32[]{:S(2)}, u32[]{:S(2)}) collective-permute-start(bf16[32,16,128]{2,1,0:T(8,128)(2,1)} %get-tuple-element.131), channel_id=1, source_target_pairs={{0,5},{1,4},{2,7},{3,6},{4,1},{5,0},{6,3},{7,2},{8,13},{9,12},{10,... | collective-permute-start | bytes 393224 | tf_op jit(solution)/shard_map/ppermute | solution.py:392
  80.1 23.0 %collective-permute-start.23 = (bf16[32,16,128]{2,1,0:T(8,128)(2,1)}, bf16[32,16,128]{2,1,0:T(8,128)(2,1)S(1)}, u32[]{:S(2)}, u32[]{:S(2)}) collective-permute-start(bf16[32,16,128]{2,1,0:T(8,128)(2,1)} %get-tuple-element.147), channel_id=1, source_target_pairs={{0,4},{1,5},{2,6},{3,7},{4,0},{5,1},{6,2},{7,3},{8,12},{9,13},{10,... | collective-permute-start | bytes 393224 | tf_op jit(solution)/shard_map/ppermute | solution.py:392
  82.0 21.2 %collective-permute-start.24 = (bf16[32,16,128]{2,1,0:T(8,128)(2,1)}, bf16[32,16,128]{2,1,0:T(8,128)(2,1)S(1)}, u32[]{:S(2)}, u32[]{:S(2)}) collective-permute-start(bf16[32,16,128]{2,1,0:T(8,128)(2,1)} %get-tuple-element.148), channel_id=1, source_target_pairs={{0,1},{1,0},{2,3},{3,2},{4,5},{5,4},{6,7},{7,6},{8,9},{9,8},{10,11... | collective-permute-start | bytes 393224 | tf_op jit(solution)/shard_map/ppermute | solution.py:392
  82.0 21.6 %collective-permute-start.25 = (bf16[32,16,128]{2,1,0:T(8,128)(2,1)}, bf16[32,16,128]{2,1,0:T(8,128)(2,1)S(1)}, u32[]{:S(2)}, u32[]{:S(2)}) collective-permute-start(bf16[32,16,128]{2,1,0:T(8,128)(2,1)} %get-tuple-element.149), channel_id=1, source_target_pairs={{0,5},{1,4},{2,7},{3,6},{4,1},{5,0},{6,3},{7,2},{8,13},{9,12},{10,... | collective-permute-start | bytes 393224 | tf_op jit(solution)/shard_map/ppermute | solution.py:392
  83.9 19.8 %collective-permute-start.26 = (bf16[32,16,128]{2,1,0:T(8,128)(2,1)}, bf16[32,16,128]{2,1,0:T(8,128)(2,1)S(1)}, u32[]{:S(2)}, u32[]{:S(2)}) collective-permute-start(bf16[32,16,128]{2,1,0:T(8,128)(2,1)} %get-tuple-element.150), channel_id=1, source_target_pairs={{0,2},{1,3},{2,0},{3,1},{4,6},{5,7},{6,4},{7,5},{8,10},{9,11},{10,... | collective-permute-start | bytes 393224 | tf_op jit(solution)/shard_map/ppermute | solution.py:392
  86.4 36.9 %collective-permute-start.16 = (bf16[32,32,128]{2,1,0:T(8,128)(2,1)}, bf16[32,32,128]{2,1,0:T(8,128)(2,1)}, u32[]{:S(2)}, u32[]{:S(2)}) collective-permute-start(bf16[32,32,128]{2,1,0:T(8,128)(2,1)} %get-tuple-element.139), channel_id=1, source_target_pairs={{0,4},{1,5},{2,6},{3,7},{4,0},{5,1},{6,2},{7,3},{8,12},{9,13},{10,... | collective-permute-start | bytes 786440 | tf_op jit(solution)/shard_map/ppermute | solution.py:392
  103.2 24.9 %collective-permute-start.17 = (bf16[32,32,128]{2,1,0:T(8,128)(2,1)}, bf16[32,32,128]{2,1,0:T(8,128)(2,1)}, u32[]{:S(2)}, u32[]{:S(2)}) collective-permute-start(bf16[32,32,128]{2,1,0:T(8,128)(2,1)} %get-tuple-element.140), channel_id=1, source_target_pairs={{0,1},{1,0},{2,3},{3,2},{4,5},{5,4},{6,7},{7,6},{8,9},{9,8},{10,11... | collective-permute-start | bytes 786440 | tf_op jit(solution)/shard_map/ppermute | solution.py:392
  103.6 17.7 %collective-permute-start.29 = (bf16[32,16,128]{2,1,0:T(8,128)(2,1)}, bf16[32,16,128]{2,1,0:T(8,128)(2,1)S(1)}, u32[]{:S(2)}, u32[]{:S(2)}) collective-permute-start(bf16[32,16,128]{2,1,0:T(8,128)(2,1)} %get-tuple-element.153), channel_id=1, source_target_pairs={{0,7},{1,6},{2,5},{3,4},{4,3},{5,2},{6,1},{7,0},{8,15},{9,14},{10,... | collective-permute-start | bytes 393224 | tf_op jit(solution)/shard_map/ppermute | solution.py:392
  111.7 38.6 %collective-permute-start.18 = (bf16[32,32,128]{2,1,0:T(8,128)(2,1)}, bf16[32,32,128]{2,1,0:T(8,128)(2,1)S(1)}, u32[]{:S(2)}, u32[]{:S(2)}) collective-permute-start(bf16[32,32,128]{2,1,0:T(8,128)(2,1)} %get-tuple-element.141), channel_id=1, source_target_pairs={{0,5},{1,4},{2,7},{3,6},{4,1},{5,0},{6,3},{7,2},{8,13},{9,12},{10,... | collective-permute-start | bytes 786440 | tf_op jit(solution)/shard_map/ppermute | solution.py:392
  119.4 32.4 %collective-permute-start.19 = (bf16[32,32,128]{2,1,0:T(8,128)(2,1)}, bf16[32,32,128]{2,1,0:T(8,128)(2,1)S(1)}, u32[]{:S(2)}, u32[]{:S(2)}) collective-permute-start(bf16[32,32,128]{2,1,0:T(8,128)(2,1)} %get-tuple-element.142), channel_id=1, source_target_pairs={{0,2},{1,3},{2,0},{3,1},{4,6},{5,7},{6,4},{7,5},{8,10},{9,11},{10,... | collective-permute-start | bytes 786440 | tf_op jit(solution)/shard_map/ppermute | solution.py:392
  122.0 31.7 %collective-permute-start.20 = (bf16[32,32,128]{2,1,0:T(8,128)(2,1)}, bf16[32,32,128]{2,1,0:T(8,128)(2,1)S(1)}, u32[]{:S(2)}, u32[]{:S(2)}) collective-permute-start(bf16[32,32,128]{2,1,0:T(8,128)(2,1)} %get-tuple-element.143), channel_id=1, source_target_pairs={{0,6},{1,7},{2,4},{3,5},{4,2},{5,3},{6,0},{7,1},{8,14},{9,15},{10,... | collective-permute-start | bytes 786440 | tf_op jit(solution)/shard_map/ppermute | solution.py:392
  123.3 42.3 %collective-permute-start.21 = (bf16[32,32,128]{2,1,0:T(8,128)(2,1)}, bf16[32,32,128]{2,1,0:T(8,128)(2,1)}, u32[]{:S(2)}, u32[]{:S(2)}) collective-permute-start(bf16[32,32,128]{2,1,0:T(8,128)(2,1)} %get-tuple-element.144), channel_id=1, source_target_pairs={{0,3},{1,2},{2,1},{3,0},{4,7},{5,6},{6,5},{7,4},{8,11},{9,10},{10,... | collective-permute-start | bytes 786440 | tf_op jit(solution)/shard_map/ppermute | solution.py:392
  128.1 37.6 %collective-permute-start.22 = (bf16[32,32,128]{2,1,0:T(8,128)(2,1)}, bf16[32,32,128]{2,1,0:T(8,128)(2,1)}, u32[]{:S(2)}, u32[]{:S(2)}) collective-permute-start(bf16[32,32,128]{2,1,0:T(8,128)(2,1)} %get-tuple-element.145), channel_id=1, source_target_pairs={{0,7},{1,6},{2,5},{3,4},{4,3},{5,2},{6,1},{7,0},{8,15},{9,14},{10,... | collective-permute-start | bytes 786440 | tf_op jit(solution)/shard_map/ppermute | solution.py:392
  150.3 17.7 %collective-permute-start.37 = (bf16[32,16,128]{2,1,0:T(8,128)(2,1)}, bf16[32,16,128]{2,1,0:T(8,128)(2,1)S(1)}, u32[]{:S(2)}, u32[]{:S(2)}) collective-permute-start(bf16[32,16,128]{2,1,0:T(8,128)(2,1)} %get-tuple-element.165), channel_id=1, source_target_pairs={{0,4},{1,5},{2,6},{3,7},{4,0},{5,1},{6,2},{7,3},{8,12},{9,13},{10,... | collective-permute-start | bytes 393224 | tf_op jit(solution)/shard_map/ppermute | solution.py:392
  151.9 16.2 %collective-permute-start.38 = (bf16[32,16,128]{2,1,0:T(8,128)(2,1)}, bf16[32,16,128]{2,1,0:T(8,128)(2,1)S(1)}, u32[]{:S(2)}, u32[]{:S(2)}) collective-permute-start(bf16[32,16,128]{2,1,0:T(8,128)(2,1)} %get-tuple-element.166), channel_id=1, source_target_pairs={{0,1},{1,0},{2,3},{3,2},{4,5},{5,4},{6,7},{7,6},{8,9},{9,8},{10,11... | collective-permute-start | bytes 393224 | tf_op jit(solution)/shard_map/ppermute | solution.py:392
  153.7 16.7 %collective-permute-start.39 = (bf16[32,16,128]{2,1,0:T(8,128)(2,1)}, bf16[32,16,128]{2,1,0:T(8,128)(2,1)S(1)}, u32[]{:S(2)}, u32[]{:S(2)}) collective-permute-start(bf16[32,16,128]{2,1,0:T(8,128)(2,1)} %get-tuple-element.167), channel_id=1, source_target_pairs={{0,5},{1,4},{2,7},{3,6},{4,1},{5,0},{6,3},{7,2},{8,13},{9,12},{10,... | collective-permute-start | bytes 393224 | tf_op jit(solution)/shard_map/ppermute | solution.py:392
  165.6 20.5 %collective-permute-start.40 = (bf16[32,16,128]{2,1,0:T(8,128)(2,1)}, bf16[32,16,128]{2,1,0:T(8,128)(2,1)S(1)}, u32[]{:S(2)}, u32[]{:S(2)}) collective-permute-start(bf16[32,16,128]{2,1,0:T(8,128)(2,1)} %get-tuple-element.168), channel_id=1, source_target_pairs={{0,2},{1,3},{2,0},{3,1},{4,6},{5,7},{6,4},{7,5},{8,10},{9,11},{10,... | collective-permute-start | bytes 393224 | tf_op jit(solution)/shard_map/ppermute | solution.py:392
  165.7 20.4 %collective-permute-start.41 = (bf16[32,16,128]{2,1,0:T(8,128)(2,1)S(1)}, bf16[32,16,128]{2,1,0:T(8,128)(2,1)S(1)}, u32[]{:S(2)}, u32[]{:S(2)}) collective-permute-start(bf16[32,16,128]{2,1,0:T(8,128)(2,1)S(1)} %copy-done.79), channel_id=1, source_target_pairs={{0,6},{1,7},{2,4},{3,5},{4,2},{5,3},{6,0},{7,1},{8,14},{9,15},{10,... | collective-permute-start | bytes 393224 | tf_op jit(solution)/shard_map/ppermute | solution.py:392
  168.0 27.0 %collective-permute-start.42 = (bf16[32,16,128]{2,1,0:T(8,128)(2,1)}, bf16[32,16,128]{2,1,0:T(8,128)(2,1)S(1)}, u32[]{:S(2)}, u32[]{:S(2)}) collective-permute-start(bf16[32,16,128]{2,1,0:T(8,128)(2,1)} %get-tuple-element.170), channel_id=1, source_target_pairs={{0,3},{1,2},{2,1},{3,0},{4,7},{5,6},{6,5},{7,4},{8,11},{9,10},{10,... | collective-permute-start | bytes 393224 | tf_op jit(solution)/shard_map/ppermute | solution.py:392
  168.0 27.1 %collective-permute-start.43 = (bf16[32,16,128]{2,1,0:T(8,128)(2,1)}, bf16[32,16,128]{2,1,0:T(8,128)(2,1)S(1)}, u32[]{:S(2)}, u32[]{:S(2)}) collective-permute-start(bf16[32,16,128]{2,1,0:T(8,128)(2,1)} %get-tuple-element.171), channel_id=1, source_target_pairs={{0,7},{1,6},{2,5},{3,4},{4,3},{5,2},{6,1},{7,0},{8,15},{9,14},{10,... | collective-permute-start | bytes 393224 | tf_op jit(solution)/shard_map/ppermute | solution.py:392
  170.4 26.9 %collective-permute-start.44 = (bf16[32,16,128]{2,1,0:T(8,128)(2,1)}, bf16[32,16,128]{2,1,0:T(8,128)(2,1)}, u32[]{:S(2)}, u32[]{:S(2)}) collective-permute-start(bf16[32,16,128]{2,1,0:T(8,128)(2,1)} %get-tuple-element.175), channel_id=1, source_target_pairs={{0,4},{1,5},{2,6},{3,7},{4,0},{5,1},{6,2},{7,3},{8,12},{9,13},{10,... | collective-permute-start | bytes 393224 | tf_op jit(solution)/shard_map/ppermute | solution.py:392
  186.1 21.2 %collective-permute-start.45 = (bf16[32,16,128]{2,1,0:T(8,128)(2,1)}, bf16[32,16,128]{2,1,0:T(8,128)(2,1)}, u32[]{:S(2)}, u32[]{:S(2)}) collective-permute-start(bf16[32,16,128]{2,1,0:T(8,128)(2,1)} %get-tuple-element.176), channel_id=1, source_target_pairs={{0,1},{1,0},{2,3},{3,2},{4,5},{5,4},{6,7},{7,6},{8,9},{9,8},{10,11... | collective-permute-start | bytes 393224 | tf_op jit(solution)/shard_map/ppermute | solution.py:392
  186.8 22.9 %collective-permute-start.46 = (bf16[32,16,128]{2,1,0:T(8,128)(2,1)}, bf16[32,16,128]{2,1,0:T(8,128)(2,1)}, u32[]{:S(2)}, u32[]{:S(2)}) collective-permute-start(bf16[32,16,128]{2,1,0:T(8,128)(2,1)} %get-tuple-element.177), channel_id=1, source_target_pairs={{0,5},{1,4},{2,7},{3,6},{4,1},{5,0},{6,3},{7,2},{8,13},{9,12},{10,... | collective-permute-start | bytes 393224 | tf_op jit(solution)/shard_map/ppermute | solution.py:392
  209.7 16.6 %collective-permute-start.58 = (bf16[32,16,128]{2,1,0:T(8,128)(2,1)}, bf16[32,16,128]{2,1,0:T(8,128)(2,1)S(1)}, u32[]{:S(2)}, u32[]{:S(2)}) collective-permute-start(bf16[32,16,128]{2,1,0:T(8,128)(2,1)} %get-tuple-element.193), channel_id=1, source_target_pairs={{0,4},{1,5},{2,6},{3,7},{4,0},{5,1},{6,2},{7,3},{8,12},{9,13},{10,... | collective-permute-start | bytes 393224 | tf_op jit(solution)/shard_map/ppermute | solution.py:392
  210.5 16.5 %collective-permute-start.59 = (bf16[32,16,128]{2,1,0:T(8,128)(2,1)}, bf16[32,16,128]{2,1,0:T(8,128)(2,1)S(1)}, u32[]{:S(2)}, u32[]{:S(2)}) collective-permute-start(bf16[32,16,128]{2,1,0:T(8,128)(2,1)} %get-tuple-element.194), channel_id=1, source_target_pairs={{0,1},{1,0},{2,3},{3,2},{4,5},{5,4},{6,7},{7,6},{8,9},{9,8},{10,11... | collective-permute-start | bytes 393224 | tf_op jit(solution)/shard_map/ppermute | solution.py:392
  210.6 24.5 %collective-permute-start.60 = (bf16[32,16,128]{2,1,0:T(8,128)(2,1)}, bf16[32,16,128]{2,1,0:T(8,128)(2,1)S(1)}, u32[]{:S(2)}, u32[]{:S(2)}) collective-permute-start(bf16[32,16,128]{2,1,0:T(8,128)(2,1)} %get-tuple-element.195), channel_id=1, source_target_pairs={{0,5},{1,4},{2,7},{3,6},{4,1},{5,0},{6,3},{7,2},{8,13},{9,12},{10,... | collective-permute-start | bytes 393224 | tf_op jit(solution)/shard_map/ppermute | solution.py:392
  212.8 22.3 %collective-permute-start.61 = (bf16[32,16,128]{2,1,0:T(8,128)(2,1)}, bf16[32,16,128]{2,1,0:T(8,128)(2,1)S(1)}, u32[]{:S(2)}, u32[]{:S(2)}) collective-permute-start(bf16[32,16,128]{2,1,0:T(8,128)(2,1)} %get-tuple-element.196), channel_id=1, source_target_pairs={{0,2},{1,3},{2,0},{3,1},{4,6},{5,7},{6,4},{7,5},{8,10},{9,11},{10,... | collective-permute-start | bytes 393224 | tf_op jit(solution)/shard_map/ppermute | solution.py:392
  214.9 37.4 %collective-permute-start.30 = (bf16[32,32,128]{2,1,0:T(8,128)(2,1)}, bf16[32,32,128]{2,1,0:T(8,128)(2,1)S(1)}, u32[]{:S(2)}, u32[]{:S(2)}) collective-permute-start(bf16[32,32,128]{2,1,0:T(8,128)(2,1)} %get-tuple-element.157), channel_id=1, source_target_pairs={{0,4},{1,5},{2,6},{3,7},{4,0},{5,1},{6,2},{7,3},{8,12},{9,13},{10,... | collective-permute-start | bytes 786440 | tf_op jit(solution)/shard_map/ppermute | solution.py:392
  227.0 30.2 %collective-permute-start.31 = (bf16[32,32,128]{2,1,0:T(8,128)(2,1)}, bf16[32,32,128]{2,1,0:T(8,128)(2,1)S(1)}, u32[]{:S(2)}, u32[]{:S(2)}) collective-permute-start(bf16[32,32,128]{2,1,0:T(8,128)(2,1)} %get-tuple-element.158), channel_id=1, source_target_pairs={{0,1},{1,0},{2,3},{3,2},{4,5},{5,4},{6,7},{7,6},{8,9},{9,8},{10,11... | collective-permute-start | bytes 786440 | tf_op jit(solution)/shard_map/ppermute | solution.py:392
  238.7 22.4 %collective-permute-start.32 = (bf16[32,32,128]{2,1,0:T(8,128)(2,1)}, bf16[32,32,128]{2,1,0:T(8,128)(2,1)S(1)}, u32[]{:S(2)}, u32[]{:S(2)}) collective-permute-start(bf16[32,32,128]{2,1,0:T(8,128)(2,1)} %get-tuple-element.159), channel_id=1, source_target_pairs={{0,5},{1,4},{2,7},{3,6},{4,1},{5,0},{6,3},{7,2},{8,13},{9,12},{10,... | collective-permute-start | bytes 786440 | tf_op jit(solution)/shard_map/ppermute | solution.py:392
  247.5 18.8 %collective-permute-start.33 = (bf16[32,32,128]{2,1,0:T(8,128)(2,1)}, bf16[32,32,128]{2,1,0:T(8,128)(2,1)S(1)}, u32[]{:S(2)}, u32[]{:S(2)}) collective-permute-start(bf16[32,32,128]{2,1,0:T(8,128)(2,1)} %get-tuple-element.160), channel_id=1, source_target_pairs={{0,2},{1,3},{2,0},{3,1},{4,6},{5,7},{6,4},{7,5},{8,10},{9,11},{10,... | collective-permute-start | bytes 786440 | tf_op jit(solution)/shard_map/ppermute | solution.py:392
  250.7 16.4 %collective-permute-start.34 = (bf16[32,32,128]{2,1,0:T(8,128)(2,1)}, bf16[32,32,128]{2,1,0:T(8,128)(2,1)S(1)}, u32[]{:S(2)}, u32[]{:S(2)}) collective-permute-start(bf16[32,32,128]{2,1,0:T(8,128)(2,1)} %get-tuple-element.161), channel_id=1, source_target_pairs={{0,6},{1,7},{2,4},{3,5},{4,2},{5,3},{6,0},{7,1},{8,14},{9,15},{10,... | collective-permute-start | bytes 786440 | tf_op jit(solution)/shard_map/ppermute | solution.py:392
  252.3 23.3 %collective-permute-start.35 = (bf16[32,32,128]{2,1,0:T(8,128)(2,1)}, bf16[32,32,128]{2,1,0:T(8,128)(2,1)S(1)}, u32[]{:S(2)}, u32[]{:S(2)}) collective-permute-start(bf16[32,32,128]{2,1,0:T(8,128)(2,1)} %get-tuple-element.162), channel_id=1, source_target_pairs={{0,3},{1,2},{2,1},{3,0},{4,7},{5,6},{6,5},{7,4},{8,11},{9,10},{10,... | collective-permute-start | bytes 786440 | tf_op jit(solution)/shard_map/ppermute | solution.py:392
  257.2 31.7 %collective-permute-start.36 = (bf16[32,32,128]{2,1,0:T(8,128)(2,1)}, bf16[32,32,128]{2,1,0:T(8,128)(2,1)S(1)}, u32[]{:S(2)}, u32[]{:S(2)}) collective-permute-start(bf16[32,32,128]{2,1,0:T(8,128)(2,1)} %get-tuple-element.163), channel_id=1, source_target_pairs={{0,7},{1,6},{2,5},{3,4},{4,3},{5,2},{6,1},{7,0},{8,15},{9,14},{10,... | collective-permute-start | bytes 786440 | tf_op jit(solution)/shard_map/ppermute | solution.py:392
  261.1 46.9 %collective-permute-start.51 = (bf16[32,32,128]{2,1,0:T(8,128)(2,1)}, bf16[32,32,128]{2,1,0:T(8,128)(2,1)S(1)}, u32[]{:S(2)}, u32[]{:S(2)}) collective-permute-start(bf16[32,32,128]{2,1,0:T(8,128)(2,1)} %get-tuple-element.183), channel_id=1, source_target_pairs={{0,4},{1,5},{2,6},{3,7},{4,0},{5,1},{6,2},{7,3},{8,12},{9,13},{10,... | collective-permute-start | bytes 786440 | tf_op jit(solution)/shard_map/ppermute | solution.py:392
  266.3 45.7 %collective-permute-start.52 = (bf16[32,32,128]{2,1,0:T(8,128)(2,1)}, bf16[32,32,128]{2,1,0:T(8,128)(2,1)S(1)}, u32[]{:S(2)}, u32[]{:S(2)}) collective-permute-start(bf16[32,32,128]{2,1,0:T(8,128)(2,1)} %get-tuple-element.184), channel_id=1, source_target_pairs={{0,1},{1,0},{2,3},{3,2},{4,5},{5,4},{6,7},{7,6},{8,9},{9,8},{10,11... | collective-permute-start | bytes 786440 | tf_op jit(solution)/shard_map/ppermute | solution.py:392
  267.1 60.1 %collective-permute-start.53 = (bf16[32,32,128]{2,1,0:T(8,128)(2,1)}, bf16[32,32,128]{2,1,0:T(8,128)(2,1)S(1)}, u32[]{:S(2)}, u32[]{:S(2)}) collective-permute-start(bf16[32,32,128]{2,1,0:T(8,128)(2,1)} %get-tuple-element.185), channel_id=1, source_target_pairs={{0,5},{1,4},{2,7},{3,6},{4,1},{5,0},{6,3},{7,2},{8,13},{9,12},{10,... | collective-permute-start | bytes 786440 | tf_op jit(solution)/shard_map/ppermute | solution.py:392
  275.7 53.5 %collective-permute-start.54 = (bf16[32,32,128]{2,1,0:T(8,128)(2,1)}, bf16[32,32,128]{2,1,0:T(8,128)(2,1)S(1)}, u32[]{:S(2)}, u32[]{:S(2)}) collective-permute-start(bf16[32,32,128]{2,1,0:T(8,128)(2,1)} %get-tuple-element.186), channel_id=1, source_target_pairs={{0,2},{1,3},{2,0},{3,1},{4,6},{5,7},{6,4},{7,5},{8,10},{9,11},{10,... | collective-permute-start | bytes 786440 | tf_op jit(solution)/shard_map/ppermute | solution.py:392
  289.6 40.6 %collective-permute-start.55 = (bf16[32,32,128]{2,1,0:T(8,128)(2,1)}, bf16[32,32,128]{2,1,0:T(8,128)(2,1)}, u32[]{:S(2)}, u32[]{:S(2)}) collective-permute-start(bf16[32,32,128]{2,1,0:T(8,128)(2,1)} %get-tuple-element.187), channel_id=1, source_target_pairs={{0,6},{1,7},{2,4},{3,5},{4,2},{5,3},{6,0},{7,1},{8,14},{9,15},{10,... | collective-permute-start | bytes 786440 | tf_op jit(solution)/shard_map/ppermute | solution.py:392
  307.9 24.5 %collective-permute-start.56 = (bf16[32,32,128]{2,1,0:T(8,128)(2,1)}, bf16[32,32,128]{2,1,0:T(8,128)(2,1)}, u32[]{:S(2)}, u32[]{:S(2)}) collective-permute-start(bf16[32,32,128]{2,1,0:T(8,128)(2,1)} %get-tuple-element.188), channel_id=1, source_target_pairs={{0,3},{1,2},{2,1},{3,0},{4,7},{5,6},{6,5},{7,4},{8,11},{9,10},{10,... | collective-permute-start | bytes 786440 | tf_op jit(solution)/shard_map/ppermute | solution.py:392
  312.0 20.7 %collective-permute-start.57 = (bf16[32,32,128]{2,1,0:T(8,128)(2,1)}, bf16[32,32,128]{2,1,0:T(8,128)(2,1)}, u32[]{:S(2)}, u32[]{:S(2)}) collective-permute-start(bf16[32,32,128]{2,1,0:T(8,128)(2,1)} %get-tuple-element.189), channel_id=1, source_target_pairs={{0,7},{1,6},{2,5},{3,4},{4,3},{5,2},{6,1},{7,0},{8,15},{9,14},{10,... | collective-permute-start | bytes 786440 | tf_op jit(solution)/shard_map/ppermute | solution.py:392
  330.2 16.6 %collective-permute-start.74 = (bf16[32,16,128]{2,1,0:T(8,128)(2,1)}, bf16[32,16,128]{2,1,0:T(8,128)(2,1)S(1)}, u32[]{:S(2)}, u32[]{:S(2)}) collective-permute-start(bf16[32,16,128]{2,1,0:T(8,128)(2,1)} %get-tuple-element.212), channel_id=1, source_target_pairs={{0,5},{1,4},{2,7},{3,6},{4,1},{5,0},{6,3},{7,2},{8,13},{9,12},{10,... | collective-permute-start | bytes 393224 | tf_op jit(solution)/shard_map/ppermute | solution.py:392
  332.4 32.2 %collective-permute-start.75 = (bf16[32,16,128]{2,1,0:T(8,128)(2,1)}, bf16[32,16,128]{2,1,0:T(8,128)(2,1)S(1)}, u32[]{:S(2)}, u32[]{:S(2)}) collective-permute-start(bf16[32,16,128]{2,1,0:T(8,128)(2,1)} %get-tuple-element.213), channel_id=1, source_target_pairs={{0,2},{1,3},{2,0},{3,1},{4,6},{5,7},{6,4},{7,5},{8,10},{9,11},{10,... | collective-permute-start | bytes 393224 | tf_op jit(solution)/shard_map/ppermute | solution.py:392
  332.6 34.5 %collective-permute-start.76 = (bf16[32,16,128]{2,1,0:T(8,128)(2,1)}, bf16[32,16,128]{2,1,0:T(8,128)(2,1)}, u32[]{:S(2)}, u32[]{:S(2)}) collective-permute-start(bf16[32,16,128]{2,1,0:T(8,128)(2,1)} %get-tuple-element.214), channel_id=1, source_target_pairs={{0,6},{1,7},{2,4},{3,5},{4,2},{5,3},{6,0},{7,1},{8,14},{9,15},{10,... | collective-permute-start | bytes 393224 | tf_op jit(solution)/shard_map/ppermute | solution.py:392
  341.0 26.2 %collective-permute-start.77 = (bf16[32,16,128]{2,1,0:T(8,128)(2,1)}, bf16[32,16,128]{2,1,0:T(8,128)(2,1)}, u32[]{:S(2)}, u32[]{:S(2)}) collective-permute-start(bf16[32,16,128]{2,1,0:T(8,128)(2,1)} %get-tuple-element.215), channel_id=1, source_target_pairs={{0,3},{1,2},{2,1},{3,0},{4,7},{5,6},{6,5},{7,4},{8,11},{9,10},{10,... | collective-permute-start | bytes 393224 | tf_op jit(solution)/shard_map/ppermute | solution.py:392
  341.0 46.5 %collective-permute-start.65 = (bf16[32,32,128]{2,1,0:T(8,128)(2,1)}, bf16[32,32,128]{2,1,0:T(8,128)(2,1)S(1)}, u32[]{:S(2)}, u32[]{:S(2)}) collective-permute-start(bf16[32,32,128]{2,1,0:T(8,128)(2,1)} %get-tuple-element.201), channel_id=1, source_target_pairs={{0,4},{1,5},{2,6},{3,7},{4,0},{5,1},{6,2},{7,3},{8,12},{9,13},{10,... | collective-permute-start | bytes 786440 | tf_op jit(solution)/shard_map/ppermute | solution.py:392
  347.4 40.2 %collective-permute-start.66 = (bf16[32,32,128]{2,1,0:T(8,128)(2,1)}, bf16[32,32,128]{2,1,0:T(8,128)(2,1)S(1)}, u32[]{:S(2)}, u32[]{:S(2)}) collective-permute-start(bf16[32,32,128]{2,1,0:T(8,128)(2,1)} %get-tuple-element.202), channel_id=1, source_target_pairs={{0,1},{1,0},{2,3},{3,2},{4,5},{5,4},{6,7},{7,6},{8,9},{9,8},{10,11... | collective-permute-start | bytes 786440 | tf_op jit(solution)/shard_map/ppermute | solution.py:392
  367.2 17.2 %collective-permute-start.79 = (bf16[32,16,128]{2,1,0:T(8,128)(2,1)}, bf16[32,16,128]{2,1,0:T(8,128)(2,1)S(1)}, u32[]{:S(2)}, u32[]{:S(2)}) collective-permute-start(bf16[32,16,128]{2,1,0:T(8,128)(2,1)} %get-tuple-element.219), channel_id=1, source_target_pairs={{0,4},{1,5},{2,6},{3,7},{4,0},{5,1},{6,2},{7,3},{8,12},{9,13},{10,... | collective-permute-start | bytes 393224 | tf_op jit(solution)/shard_map/ppermute | solution.py:392
  367.2 17.9 %collective-permute-start.80 = (bf16[32,16,128]{2,1,0:T(8,128)(2,1)}, bf16[32,16,128]{2,1,0:T(8,128)(2,1)S(1)}, u32[]{:S(2)}, u32[]{:S(2)}) collective-permute-start(bf16[32,16,128]{2,1,0:T(8,128)(2,1)} %get-tuple-element.220), channel_id=1, source_target_pairs={{0,1},{1,0},{2,3},{3,2},{4,5},{5,4},{6,7},{7,6},{8,9},{9,8},{10,11... | collective-permute-start | bytes 393224 | tf_op jit(solution)/shard_map/ppermute | solution.py:392
  373.2 28.5 %collective-permute-start.67 = (bf16[32,32,128]{2,1,0:T(8,128)(2,1)}, bf16[32,32,128]{2,1,0:T(8,128)(2,1)S(1)}, u32[]{:S(2)}, u32[]{:S(2)}) collective-permute-start(bf16[32,32,128]{2,1,0:T(8,128)(2,1)} %get-tuple-element.203), channel_id=1, source_target_pairs={{0,5},{1,4},{2,7},{3,6},{4,1},{5,0},{6,3},{7,2},{8,13},{9,12},{10,... | collective-permute-start | bytes 786440 | tf_op jit(solution)/shard_map/ppermute | solution.py:392
  385.0 16.7 %collective-permute-start.68 = (bf16[32,32,128]{2,1,0:T(8,128)(2,1)}, bf16[32,32,128]{2,1,0:T(8,128)(2,1)}, u32[]{:S(2)}, u32[]{:S(2)}) collective-permute-start(bf16[32,32,128]{2,1,0:T(8,128)(2,1)} %get-tuple-element.204), channel_id=1, source_target_pairs={{0,2},{1,3},{2,0},{3,1},{4,6},{5,7},{6,4},{7,5},{8,10},{9,11},{10,... | collective-permute-start | bytes 786440 | tf_op jit(solution)/shard_map/ppermute | solution.py:392
  385.7 16.1 %collective-permute-start.69 = (bf16[32,32,128]{2,1,0:T(8,128)(2,1)}, bf16[32,32,128]{2,1,0:T(8,128)(2,1)}, u32[]{:S(2)}, u32[]{:S(2)}) collective-permute-start(bf16[32,32,128]{2,1,0:T(8,128)(2,1)} %get-tuple-element.205), channel_id=1, source_target_pairs={{0,6},{1,7},{2,4},{3,5},{4,2},{5,3},{6,0},{7,1},{8,14},{9,15},{10,... | collective-permute-start | bytes 786440 | tf_op jit(solution)/shard_map/ppermute | solution.py:392
  387.5 24.9 %collective-permute-start.70 = (bf16[32,32,128]{2,1,0:T(8,128)(2,1)}, bf16[32,32,128]{2,1,0:T(8,128)(2,1)}, u32[]{:S(2)}, u32[]{:S(2)}) collective-permute-start(bf16[32,32,128]{2,1,0:T(8,128)(2,1)} %get-tuple-element.206), channel_id=1, source_target_pairs={{0,3},{1,2},{2,1},{3,0},{4,7},{5,6},{6,5},{7,4},{8,11},{9,10},{10,... | collective-permute-start | bytes 786440 | tf_op jit(solution)/shard_map/ppermute | solution.py:392
  387.6 24.8 %collective-permute-start.71 = (bf16[32,32,128]{2,1,0:T(8,128)(2,1)}, bf16[32,32,128]{2,1,0:T(8,128)(2,1)}, u32[]{:S(2)}, u32[]{:S(2)}) collective-permute-start(bf16[32,32,128]{2,1,0:T(8,128)(2,1)} %get-tuple-element.207), channel_id=1, source_target_pairs={{0,7},{1,6},{2,5},{3,4},{4,3},{5,2},{6,1},{7,0},{8,15},{9,14},{10,... | collective-permute-start | bytes 786440 | tf_op jit(solution)/shard_map/ppermute | solution.py:392
  401.7 24.5 %collective-permute-start.81 = (bf16[32,16,128]{2,1,0:T(8,128)(2,1)}, bf16[32,16,128]{2,1,0:T(8,128)(2,1)S(1)}, u32[]{:S(2)}, u32[]{:S(2)}) collective-permute-start(bf16[32,16,128]{2,1,0:T(8,128)(2,1)} %get-tuple-element.221), channel_id=1, source_target_pairs={{0,5},{1,4},{2,7},{3,6},{4,1},{5,0},{6,3},{7,2},{8,13},{9,12},{10,... | collective-permute-start | bytes 393224 | tf_op jit(solution)/shard_map/ppermute | solution.py:392
  401.7 24.5 %collective-permute-start.82 = (bf16[32,16,128]{2,1,0:T(8,128)(2,1)}, bf16[32,16,128]{2,1,0:T(8,128)(2,1)S(1)}, u32[]{:S(2)}, u32[]{:S(2)}) collective-permute-start(bf16[32,16,128]{2,1,0:T(8,128)(2,1)} %get-tuple-element.222), channel_id=1, source_target_pairs={{0,2},{1,3},{2,0},{3,1},{4,6},{5,7},{6,4},{7,5},{8,10},{9,11},{10,... | collective-permute-start | bytes 393224 | tf_op jit(solution)/shard_map/ppermute | solution.py:392
  401.8 24.4 %collective-permute-start.83 = (bf16[32,16,128]{2,1,0:T(8,128)(2,1)}, bf16[32,16,128]{2,1,0:T(8,128)(2,1)S(1)}, u32[]{:S(2)}, u32[]{:S(2)}) collective-permute-start(bf16[32,16,128]{2,1,0:T(8,128)(2,1)} %get-tuple-element.223), channel_id=1, source_target_pairs={{0,6},{1,7},{2,4},{3,5},{4,2},{5,3},{6,0},{7,1},{8,14},{9,15},{10,... | collective-permute-start | bytes 393224 | tf_op jit(solution)/shard_map/ppermute | solution.py:392
  (111 other events, 2277.2 us)

commit v12 on v11

--- a/solution.py
+++ b/solution.py
@@ -405,7 +405,7 @@
 
 def chunks_of(receivers):
     if receivers == 128:
-        return [(16, 0), (16, 1), (32, 1), (32, 2), (16, 6), (16, 7)]
+        return [(16, 0), (32, 1), (32, 2), (32, 3), (16, 1)]
     rows = min(16, receivers)
     return [(rows, index) for index in range(receivers // rows)]
 
@@ -424,7 +424,7 @@
     chunks = chunks_of(receivers)
     sides = edges(estimate, observed)
     last, updated, energy = levels, None, 0.0
-    lag = 2
+    lag = 1
     ahead, behind = {}, {}
     for turn in range(len(chunks) + 2 * lag):
         if turn < len(chunks):

time: 433 us -> 433 us (level)
  waiting for transfers between devices: 75.1 us -> 150 us
  starting transfers between devices: 160 us -> 95.6 us
  Pallas kernels: 155 us -> 148 us
    ppermute x84 -> x70, waiting for transfers between devices: 72.1 us -> 147 us  [exchanged(): lax.ppermute(arrays[slot], 'shot', [(i, i ^ slot) for i in range(peers)])]
    ppermute x84 -> x70, starting transfers between devices: 157 us -> 91.9 us  [exchanged(): lax.ppermute(arrays[slot], 'shot', [(i, i ^ slot) for i in range(peers)])]
    pallas_call x6 -> x5, Pallas kernels: 69.1 us -> 64.5 us  [spectra_of(): pl.pallas_call(spectra_kernel, grid_spec=pltpu.PrefetchScalarGridSpec(num...]
    unnamed x178 -> x114, local copies, waits for them, and re-layouts: 22.5 us -> 19.5 us
    pallas_call x6 -> x5, Pallas kernels: 26.4 us -> 24.5 us  [updated_of(): pl.pallas_call(functools.partial(update_kernel, len(restored)), grid_spec...]
    pallas_call x6 -> x5, Pallas kernels: 59.1 us -> 58.6 us  [shrunk_of(): pl.pallas_call(shots_kernel, grid_spec=pltpu.PrefetchScalarGridSpec(num_s...]
  transfers between devices with their start and end apart: 86 -> 72, of which waited for: 18 -> 20; matrix products, arithmetic and copies ran while one was open for 1% -> 1% of each run, Pallas kernels for 33% -> 30%
where the time goes in v12:
time: 433 us; the launch traced here: 431 us
  waiting for transfers between devices  150 us (35%)
  Pallas kernels  148 us (34%)
  starting transfers between devices  95.6 us (22%)
  local copies, waits for them, and re-layouts  23.2 us (5%)
  blocking collectives  9.91 us (2%)
    ppermute x70, waiting for transfers between devices, exchanged(): lax.ppermute(arrays[slot], 'shot', [(i, i ^ slot) for i in range(peers)])  147 us
    ppermute x70, starting transfers between devices, exchanged(): lax.ppermute(arrays[slot], 'shot', [(i, i ^ slot) for i in range(peers)])  91.9 us
    pallas_call x5, Pallas kernels, spectra_of(): pl.pallas_call(spectra_kernel, grid_spec=pltpu.PrefetchScalarGridSpec(num...  64.5 us
    pallas_call x5, Pallas kernels, shrunk_of(): pl.pallas_call(shots_kernel, grid_spec=pltpu.PrefetchScalarGridSpec(num_s...  58.6 us
    pallas_call x5, Pallas kernels, updated_of(): pl.pallas_call(functools.partial(update_kernel, len(restored)), grid_spec...  24.5 us
    unnamed x114, local copies, waits for them, and re-layouts  19.5 us
    psum x1, blocking collectives, local(): lax.psum(jnp.sum(energy, axis=1), 'patch')  9.91 us
  transfers between devices with their start and end apart: 72, of which 20 were waited for; matrix products, arithmetic and copies ran while one was open for 1% of the time, Pallas kernels for 30%

profile of v12, /device:TPU:0, one launch (start us, length us, event | category | flops | bytes accessed | tf_op | source)
XLA Modules:
  0.0 430.8 jit_solution(11425824653313860558)
XLA Ops:
  3.1 2.4 collective-permute-start
  9.8 3.1 collective-permute-done.1.after_ref
  13.8 9.8 %spectra.5 = (bf16[32,16,128]{2,1,0:T(8,128)(2,1)}, bf16[32,16,128]{2,1,0:T(8,128)(2,1)}, bf16[32,16,128]{2,1,0:T(8,128)(2,1)}, bf16[32,16,128]{2,1,0:T(8,128)(2...) custom-call(s32[9]{0:T(128)} %pad_add_fusion.meta_ref, ...), custom_call_target="tpu_custom_call" | custom-call | flops 1073741824 | bytes 5242880 | tf_op jit(solution)/shard_map/spectra/pallas_call | solution.py:270
  23.7 10.5 %collective-permute-start.2 = (bf16[32,16,128]{2,1,0:T(8,128)(2,1)}, bf16[32,16,128]{2,1,0:T(8,128)(2,1)S(1)}, u32[]{:S(2)}, u32[]{:S(2)}) collective-permute-start(bf16[32,16,128]{2,1,0:T(8,128)(2,1)} %get-tuple-element.99), channel_id=1, source_target_pairs={{0,4},{1,5},{2,6},{3,7},{4,0},{5,1},{6,2},{7,3},{8,12},{9,13},{10,... | collective-permute-start | bytes 393224 | tf_op jit(solution)/shard_map/ppermute | solution.py:392
  34.2 1.5 collective-permute-start.3
  35.7 1.5 collective-permute-start.5
  37.1 2.5 collective-permute-start.6
  39.6 3.6 collective-permute-done.2.refs_1_
  43.3 14.7 %spectra.6 = (bf16[32,32,128]{2,1,0:T(8,128)(2,1)}, bf16[32,32,128]{2,1,0:T(8,128)(2,1)}, bf16[32,32,128]{2,1,0:T(8,128)(2,1)}, bf16[32,32,128]{2,1,0:T(8,128)(2...) custom-call(s32[9]{0:T(128)} %pad_add_fusion.meta_ref, ...), custom_call_target="tpu_custom_call" | custom-call | flops 2147483648 | bytes 8388608 | tf_op jit(solution)/shard_map/spectra/pallas_call | solution.py:270
  58.9 7.3 %shrink.5 = (bf16[32,16,128]{2,1,0:T(8,128)(2,1)}, bf16[32,16,128]{2,1,0:T(8,128)(2,1)}, bf16[32,16,128]{2,1,0:T(8,128)(2,1)}, bf16[32,16,128]{2,1,0:T(8,128)(2,...) custom-call(s32[9]{0:T(128)} %pad_add_fusion.meta_ref, ...), custom_call_target="tpu_custom_call" | custom-call | flops 1073741824 | bytes 2359296 | tf_op jit(solution)/shard_map/shrink/pallas_call | solution.py:320
  66.2 3.2 collective-permute-start.16
  69.4 2.8 collective-permute-start.17
  72.1 2.0 collective-permute-start.18
  74.2 1.4 collective-permute-start.19
  76.1 1.5 collective-permute-start.9
  77.7 3.6 collective-permute-start.10
  81.2 14.7 %collective-permute-done.18.refs_3_ = bf16[32,16,128]{2,1,0:T(8,128)(2,1)S(1)} collective-permute-done((bf16[32,16,128]{2,1,0:T(8,128)(2,1)}, bf16[32,16,128]{2,1,0:T(8,128)(2,1)S(1)}, u32[]{:S(2)}, u32[]{:S(2)}) %collective-permute-start.18) | collective-permute-done | bytes 131104 | tf_op jit(solution)/shard_map/ppermute | solution.py:392
  96.3 14.9 %spectra.7 = (bf16[32,32,128]{2,1,0:T(8,128)(2,1)}, bf16[32,32,128]{2,1,0:T(8,128)(2,1)}, bf16[32,32,128]{2,1,0:T(8,128)(2,1)}, bf16[32,32,128]{2,1,0:T(8,128)(2...) custom-call(s32[9]{0:T(128)} %pad_add_fusion.meta_ref, ...), custom_call_target="tpu_custom_call" | custom-call | flops 2147483648 | bytes 8388608 | tf_op jit(solution)/shard_map/spectra/pallas_call | solution.py:270
  111.2 3.6 collective-permute-done.21.refs_6_
  114.8 1.6 collective-permute-start.12
  116.5 3.3 collective-permute-start.13
  121.1 1.9 collective-permute-start.23
  123.0 3.8 collective-permute-done.12.refs_4_
  126.9 5.8 %collective-permute-done.13.refs_5_ = bf16[32,32,128]{2,1,0:T(8,128)(2,1)S(1)} collective-permute-done((bf16[32,32,128]{2,1,0:T(8,128)(2,1)}, bf16[32,32,128]{2,1,0:T(8,128)(2,1)S(1)}, u32[]{:S(2)}, u32[]{:S(2)}) %collective-permute-start.13) | collective-permute-done | bytes 262176 | tf_op jit(solution)/shard_map/ppermute | solution.py:392
  132.7 4.2 collective-permute-done.14.refs_6_
  136.9 3.5 collective-permute-done.15.refs_7_
  140.4 4.0 collective-permute-start.27
  144.3 22.2 %collective-permute-done.23.refs_1_ = bf16[32,32,128]{2,1,0:T(8,128)(2,1)S(1)} collective-permute-done((bf16[32,32,128]{2,1,0:T(8,128)(2,1)}, bf16[32,32,128]{2,1,0:T(8,128)(2,1)S(1)}, u32[]{:S(2)}, u32[]{:S(2)}) %collective-permute-start.23) | collective-permute-done | bytes 262176 | tf_op jit(solution)/shard_map/ppermute | solution.py:392
  166.7 14.7 %shrink.6 = (bf16[32,32,128]{2,1,0:T(8,128)(2,1)}, bf16[32,32,128]{2,1,0:T(8,128)(2,1)}, bf16[32,32,128]{2,1,0:T(8,128)(2,1)}, bf16[32,32,128]{2,1,0:T(8,128)(2,...) custom-call(s32[9]{0:T(128)} %pad_add_fusion.meta_ref, ...), custom_call_target="tpu_custom_call" | custom-call | flops 2147483648 | bytes 4456448 | tf_op jit(solution)/shard_map/shrink/pallas_call | solution.py:320
  182.2 2.4 collective-permute-start.30
  188.7 3.2 update.5
  192.6 15.1 %spectra.8 = (bf16[32,32,128]{2,1,0:T(8,128)(2,1)}, bf16[32,32,128]{2,1,0:T(8,128)(2,1)}, bf16[32,32,128]{2,1,0:T(8,128)(2,1)}, bf16[32,32,128]{2,1,0:T(8,128)(2...) custom-call(s32[9]{0:T(128)} %pad_add_fusion.meta_ref, ...), custom_call_target="tpu_custom_call" | custom-call | flops 2147483648 | bytes 8388608 | tf_op jit(solution)/shard_map/spectra/pallas_call | solution.py:270
  207.6 2.4 collective-permute-start.34
  210.0 9.3 %collective-permute-done.30.refs_1_ = bf16[32,32,128]{2,1,0:T(8,128)(2,1)S(1)} collective-permute-done((bf16[32,32,128]{2,1,0:T(8,128)(2,1)}, bf16[32,32,128]{2,1,0:T(8,128)(2,1)S(1)}, u32[]{:S(2)}, u32[]{:S(2)}) %collective-permute-start.30) | collective-permute-done | bytes 262176 | tf_op jit(solution)/shard_map/ppermute | solution.py:392
  220.2 3.0 collective-permute-done.32.refs_3_
  223.2 1.5 collective-permute-start.37
  224.8 14.7 %shrink.7 = (bf16[32,32,128]{2,1,0:T(8,128)(2,1)}, bf16[32,32,128]{2,1,0:T(8,128)(2,1)}, bf16[32,32,128]{2,1,0:T(8,128)(2,1)}, bf16[32,32,128]{2,1,0:T(8,128)(2,...) custom-call(s32[9]{0:T(128)} %pad_add_fusion.meta_ref, ...), custom_call_target="tpu_custom_call" | custom-call | flops 2147483648 | bytes 4456448 | tf_op jit(solution)/shard_map/shrink/pallas_call | solution.py:320
  239.5 2.3 collective-permute-start.39
  242.4 2.2 collective-permute-start.41
  244.6 19.8 %collective-permute-done.37.refs_1_ = bf16[32,32,128]{2,1,0:T(8,128)(2,1)} collective-permute-done((bf16[32,32,128]{2,1,0:T(8,128)(2,1)}, bf16[32,32,128]{2,1,0:T(8,128)(2,1)}, u32[]{:S(2)}, u32[]{:S(2)}) %collective-permute-start.37) | collective-permute-done | bytes 262176 | tf_op jit(solution)/shard_map/ppermute | solution.py:392
  266.1 5.9 %update.6 = (f32[32,128,1024]{2,1,0:T(8,128)}, f32[8,128]{1,0:T(8,128)S(1)}) custom-call(s32[9]{0:T(128)S(1)} %copy-done.20, bf16[1024,1024]{1,0:T(8,128)(2,1)S(1)} %copy-done, bf16[32,32,128]{2,1,0:T(8,128)(2,1)S(1)} %copy-done.1, bf16[32,32,128]{2,1,0:T(8,128)(2,1)S(1)} %copy-done.7, ...), custom_call_target="tpu_custom_call", output_to_operand_aliasing={{0}: (11, {})} | custom-call | flops 2147483648 | bytes 8388608 | tf_op jit(solution)/shard_map/update/pallas_call | solution.py:351
  272.6 10.0 %spectra.9 = (bf16[32,16,128]{2,1,0:T(8,128)(2,1)}, bf16[32,16,128]{2,1,0:T(8,128)(2,1)}, bf16[32,16,128]{2,1,0:T(8,128)(2,1)}, bf16[32,16,128]{2,1,0:T(8,128)(2...) custom-call(s32[9]{0:T(128)} %pad_add_fusion.meta_ref, ...), custom_call_target="tpu_custom_call" | custom-call | flops 1073741824 | bytes 5242880 | tf_op jit(solution)/shard_map/spectra/pallas_call | solution.py:270
  282.7 2.6 collective-permute-start.51
  286.8 1.6 collective-permute-start.53
  288.3 12.9 %collective-permute-done.51.refs_1_ = bf16[32,16,128]{2,1,0:T(8,128)(2,1)S(1)} collective-permute-done((bf16[32,16,128]{2,1,0:T(8,128)(2,1)}, bf16[32,16,128]{2,1,0:T(8,128)(2,1)S(1)}, u32[]{:S(2)}, u32[]{:S(2)}) %collective-permute-start.51) | collective-permute-done | bytes 131104 | tf_op jit(solution)/shard_map/ppermute | solution.py:392
  302.0 2.2 collective-permute-start.46
  304.2 11.3 %collective-permute-done.53.refs_3_ = bf16[32,16,128]{2,1,0:T(8,128)(2,1)S(1)} collective-permute-done((bf16[32,16,128]{2,1,0:T(8,128)(2,1)}, bf16[32,16,128]{2,1,0:T(8,128)(2,1)S(1)}, u32[]{:S(2)}, u32[]{:S(2)}) %collective-permute-start.53) | collective-permute-done | bytes 131104 | tf_op jit(solution)/shard_map/ppermute | solution.py:392
  316.8 2.2 collective-permute-start.48
  319.2 2.2 collective-permute-start.50
  321.5 14.6 %shrink.8 = (bf16[32,32,128]{2,1,0:T(8,128)(2,1)}, bf16[32,32,128]{2,1,0:T(8,128)(2,1)}, bf16[32,32,128]{2,1,0:T(8,128)(2,1)}, bf16[32,32,128]{2,1,0:T(8,128)(2,...) custom-call(s32[9]{0:T(128)} %pad_add_fusion.meta_ref, ...), custom_call_target="tpu_custom_call" | custom-call | flops 2147483648 | bytes 4456448 | tf_op jit(solution)/shard_map/shrink/pallas_call | solution.py:320
  336.8 2.2 collective-permute-start.55
  340.9 5.3 %collective-permute-done.49.refs_6_ = bf16[32,32,128]{2,1,0:T(8,128)(2,1)S(1)} collective-permute-done((bf16[32,32,128]{2,1,0:T(8,128)(2,1)}, bf16[32,32,128]{2,1,0:T(8,128)(2,1)S(1)}, u32[]{:S(2)}, u32[]{:S(2)}) %collective-permute-start.49) | collective-permute-done | bytes 262176 | tf_op jit(solution)/shard_map/ppermute | solution.py:392
  352.3 5.9 %update.7 = (f32[32,128,1024]{2,1,0:T(8,128)}, f32[8,128]{1,0:T(8,128)S(1)}) custom-call(s32[9]{0:T(128)S(1)} %copy-done.21, bf16[1024,1024]{1,0:T(8,128)(2,1)S(1)} %copy-done, bf16[32,32,128]{2,1,0:T(8,128)(2,1)S(1)} %copy-done.3, bf16[32,32,128]{2,1,0:T(8,128)(2,1)S(1)} %copy-done.2, ...), custom_call_target="tpu_custom_call", output_to_operand_aliasing={{0}: (11, {})} | custom-call | flops 2147483648 | bytes 8388608 | tf_op jit(solution)/shard_map/update/pallas_call | solution.py:351
  360.8 7.3 %shrink.9 = (bf16[32,16,128]{2,1,0:T(8,128)(2,1)}, bf16[32,16,128]{2,1,0:T(8,128)(2,1)}, bf16[32,16,128]{2,1,0:T(8,128)(2,1)}, bf16[32,16,128]{2,1,0:T(8,128)(2,...) custom-call(s32[9]{0:T(128)} %pad_add_fusion.meta_ref, ...), custom_call_target="tpu_custom_call" | custom-call | flops 1073741824 | bytes 2359296 | tf_op jit(solution)/shard_map/shrink/pallas_call | solution.py:320
  368.1 9.6 %collective-permute-start.65 = (bf16[32,16,128]{2,1,0:T(8,128)(2,1)}, bf16[32,16,128]{2,1,0:T(8,128)(2,1)S(1)}, u32[]{:S(2)}, u32[]{:S(2)}) collective-permute-start(bf16[32,16,128]{2,1,0:T(8,128)(2,1)} %get-tuple-element.181), channel_id=1, source_target_pairs={{0,4},{1,5},{2,6},{3,7},{4,0},{5,1},{6,2},{7,3},{8,12},{9,13},{10,... | collective-permute-start | bytes 393224 | tf_op jit(solution)/shard_map/ppermute | solution.py:392
  377.8 7.8 %collective-permute-done.65.refs_1_ = bf16[32,16,128]{2,1,0:T(8,128)(2,1)S(1)} collective-permute-done((bf16[32,16,128]{2,1,0:T(8,128)(2,1)}, bf16[32,16,128]{2,1,0:T(8,128)(2,1)S(1)}, u32[]{:S(2)}, u32[]{:S(2)}) %collective-permute-start.65) | collective-permute-done | bytes 131104 | tf_op jit(solution)/shard_map/ppermute | solution.py:392
  387.6 3.3 collective-permute-start.64
  391.8 9.9 %psum.7 = f32[32]{0:T(128)S(1)} all-reduce(f32[32]{0:T(128)S(1)} %add_reduce_fusion), channel_id=1, replica_groups=mesh['patch'=4,'shot'=8] {'patch'}, use_global_device_ids=true, to_apply=%region_1.0 | all-reduce | flops 32 | bytes 256 | tf_op jit(solution)/shard_map/psum | solution.py:517
  402.5 1.9 collective-permute-start.69
  404.4 9.2 %collective-permute-done.63.refs_6_ = bf16[32,32,128]{2,1,0:T(8,128)(2,1)} collective-permute-done((bf16[32,32,128]{2,1,0:T(8,128)(2,1)}, bf16[32,32,128]{2,1,0:T(8,128)(2,1)}, u32[]{:S(2)}, u32[]{:S(2)}) %collective-permute-start.63) | collective-permute-done | bytes 262176 | tf_op jit(solution)/shard_map/ppermute | solution.py:392
  414.6 6.2 %update.8 = (f32[32,128,1024]{2,1,0:T(8,128)}, f32[8,128]{1,0:T(8,128)S(1)}) custom-call(s32[9]{0:T(128)S(1)} %copy-done.22, bf16[1024,1024]{1,0:T(8,128)(2,1)S(1)} %copy-done, bf16[32,16,128]{2,1,0:T(8,128)(2,1)S(1)} %copy-done.5, bf16[32,32,128]{2,1,0:T(8,128)(2,1)S(1)} %copy-done.4, ...), custom_call_target="tpu_custom_call", output_to_operand_aliasing={{0}: (11, {})} | custom-call | flops 2147483648 | bytes 8388608 | tf_op jit(solution)/shard_map/update/pallas_call | solution.py:351
  420.8 3.8 collective-permute-done.67.refs_3_
  424.6 3.0 collective-permute-done.70.refs_6_
  427.6 3.2 update.9
  (221 shorter events, 40.1 us)
Async XLA Ops:
  23.7 19.5 %collective-permute-start.2 = (bf16[32,16,128]{2,1,0:T(8,128)(2,1)}, bf16[32,16,128]{2,1,0:T(8,128)(2,1)S(1)}, u32[]{:S(2)}, u32[]{:S(2)}) collective-permute-start(bf16[32,16,128]{2,1,0:T(8,128)(2,1)} %get-tuple-element.99), channel_id=1, source_target_pairs={{0,4},{1,5},{2,6},{3,7},{4,0},{5,1},{6,2},{7,3},{8,12},{9,13},{10,... | collective-permute-start | bytes 393224 | tf_op jit(solution)/shard_map/ppermute | solution.py:392
  35.6 22.4 %collective-permute-start.4 = (bf16[32,16,128]{2,1,0:T(8,128)(2,1)}, bf16[32,16,128]{2,1,0:T(8,128)(2,1)S(1)}, u32[]{:S(2)}, u32[]{:S(2)}) collective-permute-start(bf16[32,16,128]{2,1,0:T(8,128)(2,1)} %get-tuple-element.101), channel_id=1, source_target_pairs={{0,5},{1,4},{2,7},{3,6},{4,1},{5,0},{6,3},{7,2},{8,13},{9,12},{10,... | collective-permute-start | bytes 393224 | tf_op jit(solution)/shard_map/ppermute | solution.py:392
  35.7 22.4 %collective-permute-start.5 = (bf16[32,16,128]{2,1,0:T(8,128)(2,1)}, bf16[32,16,128]{2,1,0:T(8,128)(2,1)S(1)}, u32[]{:S(2)}, u32[]{:S(2)}) collective-permute-start(bf16[32,16,128]{2,1,0:T(8,128)(2,1)} %get-tuple-element.102), channel_id=1, source_target_pairs={{0,2},{1,3},{2,0},{3,1},{4,6},{5,7},{6,4},{7,5},{8,10},{9,11},{10,... | collective-permute-start | bytes 393224 | tf_op jit(solution)/shard_map/ppermute | solution.py:392
  37.1 20.9 %collective-permute-start.6 = (bf16[32,16,128]{2,1,0:T(8,128)(2,1)}, bf16[32,16,128]{2,1,0:T(8,128)(2,1)S(1)}, u32[]{:S(2)}, u32[]{:S(2)}) collective-permute-start(bf16[32,16,128]{2,1,0:T(8,128)(2,1)} %get-tuple-element.103), channel_id=1, source_target_pairs={{0,6},{1,7},{2,4},{3,5},{4,2},{5,3},{6,0},{7,1},{8,14},{9,15},{10,... | collective-permute-start | bytes 393224 | tf_op jit(solution)/shard_map/ppermute | solution.py:392
  43.2 14.9 %collective-permute-start.7 = (bf16[32,16,128]{2,1,0:T(8,128)(2,1)}, bf16[32,16,128]{2,1,0:T(8,128)(2,1)S(1)}, u32[]{:S(2)}, u32[]{:S(2)}) collective-permute-start(bf16[32,16,128]{2,1,0:T(8,128)(2,1)} %get-tuple-element.104), channel_id=1, source_target_pairs={{0,3},{1,2},{2,1},{3,0},{4,7},{5,6},{6,5},{7,4},{8,11},{9,10},{10,... | collective-permute-start | bytes 393224 | tf_op jit(solution)/shard_map/ppermute | solution.py:392
  43.2 14.9 %collective-permute-start.8 = (bf16[32,16,128]{2,1,0:T(8,128)(2,1)}, bf16[32,16,128]{2,1,0:T(8,128)(2,1)S(1)}, u32[]{:S(2)}, u32[]{:S(2)}) collective-permute-start(bf16[32,16,128]{2,1,0:T(8,128)(2,1)} %get-tuple-element.105), channel_id=1, source_target_pairs={{0,7},{1,6},{2,5},{3,4},{4,3},{5,2},{6,1},{7,0},{8,15},{9,14},{10,... | collective-permute-start | bytes 393224 | tf_op jit(solution)/shard_map/ppermute | solution.py:392
  72.1 23.8 %collective-permute-start.18 = (bf16[32,16,128]{2,1,0:T(8,128)(2,1)}, bf16[32,16,128]{2,1,0:T(8,128)(2,1)S(1)}, u32[]{:S(2)}, u32[]{:S(2)}) collective-permute-start(bf16[32,16,128]{2,1,0:T(8,128)(2,1)} %get-tuple-element.119), channel_id=1, source_target_pairs={{0,5},{1,4},{2,7},{3,6},{4,1},{5,0},{6,3},{7,2},{8,13},{9,12},{10,... | collective-permute-start | bytes 393224 | tf_op jit(solution)/shard_map/ppermute | solution.py:392
  74.2 21.8 %collective-permute-start.19 = (bf16[32,16,128]{2,1,0:T(8,128)(2,1)}, bf16[32,16,128]{2,1,0:T(8,128)(2,1)S(1)}, u32[]{:S(2)}, u32[]{:S(2)}) collective-permute-start(bf16[32,16,128]{2,1,0:T(8,128)(2,1)} %get-tuple-element.120), channel_id=1, source_target_pairs={{0,2},{1,3},{2,0},{3,1},{4,6},{5,7},{6,4},{7,5},{8,10},{9,11},{10,... | collective-permute-start | bytes 393224 | tf_op jit(solution)/shard_map/ppermute | solution.py:392
  75.6 20.3 %collective-permute-start.20 = (bf16[32,16,128]{2,1,0:T(8,128)(2,1)}, bf16[32,16,128]{2,1,0:T(8,128)(2,1)S(1)}, u32[]{:S(2)}, u32[]{:S(2)}) collective-permute-start(bf16[32,16,128]{2,1,0:T(8,128)(2,1)} %get-tuple-element.121), channel_id=1, source_target_pairs={{0,6},{1,7},{2,4},{3,5},{4,2},{5,3},{6,0},{7,1},{8,14},{9,15},{10,... | collective-permute-start | bytes 393224 | tf_op jit(solution)/shard_map/ppermute | solution.py:392
  76.1 43.6 %collective-permute-start.9 = (bf16[32,32,128]{2,1,0:T(8,128)(2,1)}, bf16[32,32,128]{2,1,0:T(8,128)(2,1)S(1)}, u32[]{:S(2)}, u32[]{:S(2)}) collective-permute-start(bf16[32,32,128]{2,1,0:T(8,128)(2,1)} %get-tuple-element.109), channel_id=1, source_target_pairs={{0,4},{1,5},{2,6},{3,7},{4,0},{5,1},{6,2},{7,3},{8,12},{9,13},{10,... | collective-permute-start | bytes 786440 | tf_op jit(solution)/shard_map/ppermute | solution.py:392
  77.7 42.2 %collective-permute-start.10 = (bf16[32,32,128]{2,1,0:T(8,128)(2,1)}, bf16[32,32,128]{2,1,0:T(8,128)(2,1)}, u32[]{:S(2)}, u32[]{:S(2)}) collective-permute-start(bf16[32,32,128]{2,1,0:T(8,128)(2,1)} %get-tuple-element.110), channel_id=1, source_target_pairs={{0,1},{1,0},{2,3},{3,2},{4,5},{5,4},{6,7},{7,6},{8,9},{9,8},{10,11... | collective-permute-start | bytes 786440 | tf_op jit(solution)/shard_map/ppermute | solution.py:392
  95.9 25.2 %collective-permute-start.11 = (bf16[32,32,128]{2,1,0:T(8,128)(2,1)}, bf16[32,32,128]{2,1,0:T(8,128)(2,1)}, u32[]{:S(2)}, u32[]{:S(2)}) collective-permute-start(bf16[32,32,128]{2,1,0:T(8,128)(2,1)} %get-tuple-element.111), channel_id=1, source_target_pairs={{0,5},{1,4},{2,7},{3,6},{4,1},{5,0},{6,3},{7,2},{8,13},{9,12},{10,... | collective-permute-start | bytes 786440 | tf_op jit(solution)/shard_map/ppermute | solution.py:392
  95.9 18.9 %collective-permute-start.21 = (bf16[32,16,128]{2,1,0:T(8,128)(2,1)}, bf16[32,16,128]{2,1,0:T(8,128)(2,1)S(1)}, u32[]{:S(2)}, u32[]{:S(2)}) collective-permute-start(bf16[32,16,128]{2,1,0:T(8,128)(2,1)} %get-tuple-element.122), channel_id=1, source_target_pairs={{0,3},{1,2},{2,1},{3,0},{4,7},{5,6},{6,5},{7,4},{8,11},{9,10},{10,... | collective-permute-start | bytes 393224 | tf_op jit(solution)/shard_map/ppermute | solution.py:392
  96.0 20.5 %collective-permute-start.22 = (bf16[32,16,128]{2,1,0:T(8,128)(2,1)}, bf16[32,16,128]{2,1,0:T(8,128)(2,1)S(1)}, u32[]{:S(2)}, u32[]{:S(2)}) collective-permute-start(bf16[32,16,128]{2,1,0:T(8,128)(2,1)} %get-tuple-element.123), channel_id=1, source_target_pairs={{0,7},{1,6},{2,5},{3,4},{4,3},{5,2},{6,1},{7,0},{8,15},{9,14},{10,... | collective-permute-start | bytes 393224 | tf_op jit(solution)/shard_map/ppermute | solution.py:392
  116.5 16.2 %collective-permute-start.13 = (bf16[32,32,128]{2,1,0:T(8,128)(2,1)}, bf16[32,32,128]{2,1,0:T(8,128)(2,1)S(1)}, u32[]{:S(2)}, u32[]{:S(2)}) collective-permute-start(bf16[32,32,128]{2,1,0:T(8,128)(2,1)} %get-tuple-element.113), channel_id=1, source_target_pairs={{0,6},{1,7},{2,4},{3,5},{4,2},{5,3},{6,0},{7,1},{8,14},{9,15},{10,... | collective-permute-start | bytes 786440 | tf_op jit(solution)/shard_map/ppermute | solution.py:392
  119.8 17.1 %collective-permute-start.14 = (bf16[32,32,128]{2,1,0:T(8,128)(2,1)S(1)}, bf16[32,32,128]{2,1,0:T(8,128)(2,1)S(1)}, u32[]{:S(2)}, u32[]{:S(2)}) collective-permute-start(bf16[32,32,128]{2,1,0:T(8,128)(2,1)S(1)} %copy-done.35), channel_id=1, source_target_pairs={{0,3},{1,2},{2,1},{3,0},{4,7},{5,6},{6,5},{7,4},{8,11},{9,10},{10,... | collective-permute-start | bytes 786440 | tf_op jit(solution)/shard_map/ppermute | solution.py:392
  119.8 20.5 %collective-permute-start.15 = (bf16[32,32,128]{2,1,0:T(8,128)(2,1)S(1)}, bf16[32,32,128]{2,1,0:T(8,128)(2,1)S(1)}, u32[]{:S(2)}, u32[]{:S(2)}) collective-permute-start(bf16[32,32,128]{2,1,0:T(8,128)(2,1)S(1)} %copy-done.33), channel_id=1, source_target_pairs={{0,7},{1,6},{2,5},{3,4},{4,3},{5,2},{6,1},{7,0},{8,15},{9,14},{10,... | collective-permute-start | bytes 786440 | tf_op jit(solution)/shard_map/ppermute | solution.py:392
  121.1 45.5 %collective-permute-start.23 = (bf16[32,32,128]{2,1,0:T(8,128)(2,1)}, bf16[32,32,128]{2,1,0:T(8,128)(2,1)S(1)}, u32[]{:S(2)}, u32[]{:S(2)}) collective-permute-start(bf16[32,32,128]{2,1,0:T(8,128)(2,1)} %get-tuple-element.127), channel_id=1, source_target_pairs={{0,4},{1,5},{2,6},{3,7},{4,0},{5,1},{6,2},{7,3},{8,12},{9,13},{10,... | collective-permute-start | bytes 786440 | tf_op jit(solution)/shard_map/ppermute | solution.py:392
  126.8 54.5 %collective-permute-start.24 = (bf16[32,32,128]{2,1,0:T(8,128)(2,1)}, bf16[32,32,128]{2,1,0:T(8,128)(2,1)}, u32[]{:S(2)}, u32[]{:S(2)}) collective-permute-start(bf16[32,32,128]{2,1,0:T(8,128)(2,1)} %get-tuple-element.128), channel_id=1, source_target_pairs={{0,1},{1,0},{2,3},{3,2},{4,5},{5,4},{6,7},{7,6},{8,9},{9,8},{10,11... | collective-permute-start | bytes 786440 | tf_op jit(solution)/shard_map/ppermute | solution.py:392
  132.7 49.5 %collective-permute-start.25 = (bf16[32,32,128]{2,1,0:T(8,128)(2,1)}, bf16[32,32,128]{2,1,0:T(8,128)(2,1)}, u32[]{:S(2)}, u32[]{:S(2)}) collective-permute-start(bf16[32,32,128]{2,1,0:T(8,128)(2,1)} %get-tuple-element.129), channel_id=1, source_target_pairs={{0,5},{1,4},{2,7},{3,6},{4,1},{5,0},{6,3},{7,2},{8,13},{9,12},{10,... | collective-permute-start | bytes 786440 | tf_op jit(solution)/shard_map/ppermute | solution.py:392
  136.9 47.8 %collective-permute-start.26 = (bf16[32,32,128]{2,1,0:T(8,128)(2,1)}, bf16[32,32,128]{2,1,0:T(8,128)(2,1)S(1)}, u32[]{:S(2)}, u32[]{:S(2)}) collective-permute-start(bf16[32,32,128]{2,1,0:T(8,128)(2,1)} %get-tuple-element.130), channel_id=1, source_target_pairs={{0,2},{1,3},{2,0},{3,1},{4,6},{5,7},{6,4},{7,5},{8,10},{9,11},{10,... | collective-permute-start | bytes 786440 | tf_op jit(solution)/shard_map/ppermute | solution.py:392
  140.4 44.3 %collective-permute-start.27 = (bf16[32,32,128]{2,1,0:T(8,128)(2,1)}, bf16[32,32,128]{2,1,0:T(8,128)(2,1)}, u32[]{:S(2)}, u32[]{:S(2)}) collective-permute-start(bf16[32,32,128]{2,1,0:T(8,128)(2,1)} %get-tuple-element.131), channel_id=1, source_target_pairs={{0,6},{1,7},{2,4},{3,5},{4,2},{5,3},{6,0},{7,1},{8,14},{9,15},{10,... | collective-permute-start | bytes 786440 | tf_op jit(solution)/shard_map/ppermute | solution.py:392
  166.6 18.9 %collective-permute-start.28 = (bf16[32,32,128]{2,1,0:T(8,128)(2,1)}, bf16[32,32,128]{2,1,0:T(8,128)(2,1)}, u32[]{:S(2)}, u32[]{:S(2)}) collective-permute-start(bf16[32,32,128]{2,1,0:T(8,128)(2,1)} %get-tuple-element.132), channel_id=1, source_target_pairs={{0,3},{1,2},{2,1},{3,0},{4,7},{5,6},{6,5},{7,4},{8,11},{9,10},{10,... | collective-permute-start | bytes 786440 | tf_op jit(solution)/shard_map/ppermute | solution.py:392
  181.4 26.2 %collective-permute-start.29 = (bf16[32,32,128]{2,1,0:T(8,128)(2,1)}, bf16[32,32,128]{2,1,0:T(8,128)(2,1)}, u32[]{:S(2)}, u32[]{:S(2)}) collective-permute-start(bf16[32,32,128]{2,1,0:T(8,128)(2,1)} %get-tuple-element.133), channel_id=1, source_target_pairs={{0,7},{1,6},{2,5},{3,4},{4,3},{5,2},{6,1},{7,0},{8,15},{9,14},{10,... | collective-permute-start | bytes 786440 | tf_op jit(solution)/shard_map/ppermute | solution.py:392
  182.2 37.1 %collective-permute-start.30 = (bf16[32,32,128]{2,1,0:T(8,128)(2,1)}, bf16[32,32,128]{2,1,0:T(8,128)(2,1)S(1)}, u32[]{:S(2)}, u32[]{:S(2)}) collective-permute-start(bf16[32,32,128]{2,1,0:T(8,128)(2,1)} %get-tuple-element.135), channel_id=1, source_target_pairs={{0,4},{1,5},{2,6},{3,7},{4,0},{5,1},{6,2},{7,3},{8,12},{9,13},{10,... | collective-permute-start | bytes 786440 | tf_op jit(solution)/shard_map/ppermute | solution.py:392
  184.6 34.7 %collective-permute-start.31 = (bf16[32,32,128]{2,1,0:T(8,128)(2,1)}, bf16[32,32,128]{2,1,0:T(8,128)(2,1)S(1)}, u32[]{:S(2)}, u32[]{:S(2)}) collective-permute-start(bf16[32,32,128]{2,1,0:T(8,128)(2,1)} %get-tuple-element.136), channel_id=1, source_target_pairs={{0,1},{1,0},{2,3},{3,2},{4,5},{5,4},{6,7},{7,6},{8,9},{9,8},{10,11... | collective-permute-start | bytes 786440 | tf_op jit(solution)/shard_map/ppermute | solution.py:392
  184.7 38.5 %collective-permute-start.32 = (bf16[32,32,128]{2,1,0:T(8,128)(2,1)}, bf16[32,32,128]{2,1,0:T(8,128)(2,1)S(1)}, u32[]{:S(2)}, u32[]{:S(2)}) collective-permute-start(bf16[32,32,128]{2,1,0:T(8,128)(2,1)} %get-tuple-element.137), channel_id=1, source_target_pairs={{0,5},{1,4},{2,7},{3,6},{4,1},{5,0},{6,3},{7,2},{8,13},{9,12},{10,... | collective-permute-start | bytes 786440 | tf_op jit(solution)/shard_map/ppermute | solution.py:392
  185.5 39.2 %collective-permute-start.33 = (bf16[32,32,128]{2,1,0:T(8,128)(2,1)}, bf16[32,32,128]{2,1,0:T(8,128)(2,1)S(1)}, u32[]{:S(2)}, u32[]{:S(2)}) collective-permute-start(bf16[32,32,128]{2,1,0:T(8,128)(2,1)} %get-tuple-element.138), channel_id=1, source_target_pairs={{0,2},{1,3},{2,0},{3,1},{4,6},{5,7},{6,4},{7,5},{8,10},{9,11},{10,... | collective-permute-start | bytes 786440 | tf_op jit(solution)/shard_map/ppermute | solution.py:392
  207.6 31.9 %collective-permute-start.34 = (bf16[32,32,128]{2,1,0:T(8,128)(2,1)}, bf16[32,32,128]{2,1,0:T(8,128)(2,1)S(1)}, u32[]{:S(2)}, u32[]{:S(2)}) collective-permute-start(bf16[32,32,128]{2,1,0:T(8,128)(2,1)} %get-tuple-element.139), channel_id=1, source_target_pairs={{0,6},{1,7},{2,4},{3,5},{4,2},{5,3},{6,0},{7,1},{8,14},{9,15},{10,... | collective-permute-start | bytes 786440 | tf_op jit(solution)/shard_map/ppermute | solution.py:392
  219.3 22.5 %collective-permute-start.35 = (bf16[32,32,128]{2,1,0:T(8,128)(2,1)}, bf16[32,32,128]{2,1,0:T(8,128)(2,1)S(1)}, u32[]{:S(2)}, u32[]{:S(2)}) collective-permute-start(bf16[32,32,128]{2,1,0:T(8,128)(2,1)} %get-tuple-element.140), channel_id=1, source_target_pairs={{0,3},{1,2},{2,1},{3,0},{4,7},{5,6},{6,5},{7,4},{8,11},{9,10},{10,... | collective-permute-start | bytes 786440 | tf_op jit(solution)/shard_map/ppermute | solution.py:392
  219.3 23.1 %collective-permute-start.36 = (bf16[32,32,128]{2,1,0:T(8,128)(2,1)}, bf16[32,32,128]{2,1,0:T(8,128)(2,1)}, u32[]{:S(2)}, u32[]{:S(2)}) collective-permute-start(bf16[32,32,128]{2,1,0:T(8,128)(2,1)} %get-tuple-element.141), channel_id=1, source_target_pairs={{0,7},{1,6},{2,5},{3,4},{4,3},{5,2},{6,1},{7,0},{8,15},{9,14},{10,... | collective-permute-start | bytes 786440 | tf_op jit(solution)/shard_map/ppermute | solution.py:392
  223.2 41.3 %collective-permute-start.37 = (bf16[32,32,128]{2,1,0:T(8,128)(2,1)}, bf16[32,32,128]{2,1,0:T(8,128)(2,1)}, u32[]{:S(2)}, u32[]{:S(2)}) collective-permute-start(bf16[32,32,128]{2,1,0:T(8,128)(2,1)} %get-tuple-element.146), channel_id=1, source_target_pairs={{0,4},{1,5},{2,6},{3,7},{4,0},{5,1},{6,2},{7,3},{8,12},{9,13},{10,... | collective-permute-start | bytes 786440 | tf_op jit(solution)/shard_map/ppermute | solution.py:392
  224.7 39.8 %collective-permute-start.38 = (bf16[32,32,128]{2,1,0:T(8,128)(2,1)}, bf16[32,32,128]{2,1,0:T(8,128)(2,1)}, u32[]{:S(2)}, u32[]{:S(2)}) collective-permute-start(bf16[32,32,128]{2,1,0:T(8,128)(2,1)} %get-tuple-element.147), channel_id=1, source_target_pairs={{0,1},{1,0},{2,3},{3,2},{4,5},{5,4},{6,7},{7,6},{8,9},{9,8},{10,11... | collective-permute-start | bytes 786440 | tf_op jit(solution)/shard_map/ppermute | solution.py:392
  239.5 43.2 %collective-permute-start.39 = (bf16[32,32,128]{2,1,0:T(8,128)(2,1)}, bf16[32,32,128]{2,1,0:T(8,128)(2,1)}, u32[]{:S(2)}, u32[]{:S(2)}) collective-permute-start(bf16[32,32,128]{2,1,0:T(8,128)(2,1)} %get-tuple-element.148), channel_id=1, source_target_pairs={{0,5},{1,4},{2,7},{3,6},{4,1},{5,0},{6,3},{7,2},{8,13},{9,12},{10,... | collective-permute-start | bytes 786440 | tf_op jit(solution)/shard_map/ppermute | solution.py:392
  241.8 43.4 %collective-permute-start.40 = (bf16[32,32,128]{2,1,0:T(8,128)(2,1)}, bf16[32,32,128]{2,1,0:T(8,128)(2,1)}, u32[]{:S(2)}, u32[]{:S(2)}) collective-permute-start(bf16[32,32,128]{2,1,0:T(8,128)(2,1)} %get-tuple-element.149), channel_id=1, source_target_pairs={{0,2},{1,3},{2,0},{3,1},{4,6},{5,7},{6,4},{7,5},{8,10},{9,11},{10,... | collective-permute-start | bytes 786440 | tf_op jit(solution)/shard_map/ppermute | solution.py:392
  242.4 43.2 %collective-permute-start.41 = (bf16[32,32,128]{2,1,0:T(8,128)(2,1)}, bf16[32,32,128]{2,1,0:T(8,128)(2,1)}, u32[]{:S(2)}, u32[]{:S(2)}) collective-permute-start(bf16[32,32,128]{2,1,0:T(8,128)(2,1)} %get-tuple-element.150), channel_id=1, source_target_pairs={{0,6},{1,7},{2,4},{3,5},{4,2},{5,3},{6,0},{7,1},{8,14},{9,15},{10,... | collective-permute-start | bytes 786440 | tf_op jit(solution)/shard_map/ppermute | solution.py:392
  264.4 22.3 %collective-permute-start.42 = (bf16[32,32,128]{2,1,0:T(8,128)(2,1)}, bf16[32,32,128]{2,1,0:T(8,128)(2,1)}, u32[]{:S(2)}, u32[]{:S(2)}) collective-permute-start(bf16[32,32,128]{2,1,0:T(8,128)(2,1)} %get-tuple-element.151), channel_id=1, source_target_pairs={{0,3},{1,2},{2,1},{3,0},{4,7},{5,6},{6,5},{7,4},{8,11},{9,10},{10,... | collective-permute-start | bytes 786440 | tf_op jit(solution)/shard_map/ppermute | solution.py:392
  264.4 22.3 %collective-permute-start.43 = (bf16[32,32,128]{2,1,0:T(8,128)(2,1)}, bf16[32,32,128]{2,1,0:T(8,128)(2,1)}, u32[]{:S(2)}, u32[]{:S(2)}) collective-permute-start(bf16[32,32,128]{2,1,0:T(8,128)(2,1)} %get-tuple-element.152), channel_id=1, source_target_pairs={{0,7},{1,6},{2,5},{3,4},{4,3},{5,2},{6,1},{7,0},{8,15},{9,14},{10,... | collective-permute-start | bytes 786440 | tf_op jit(solution)/shard_map/ppermute | solution.py:392
  282.7 18.6 %collective-permute-start.51 = (bf16[32,16,128]{2,1,0:T(8,128)(2,1)}, bf16[32,16,128]{2,1,0:T(8,128)(2,1)S(1)}, u32[]{:S(2)}, u32[]{:S(2)}) collective-permute-start(bf16[32,16,128]{2,1,0:T(8,128)(2,1)} %get-tuple-element.164), channel_id=1, source_target_pairs={{0,4},{1,5},{2,6},{3,7},{4,0},{5,1},{6,2},{7,3},{8,12},{9,13},{10,... | collective-permute-start | bytes 393224 | tf_op jit(solution)/shard_map/ppermute | solution.py:392
  285.2 33.7 %collective-permute-start.44 = (bf16[32,32,128]{2,1,0:T(8,128)(2,1)S(1)}, bf16[32,32,128]{2,1,0:T(8,128)(2,1)S(1)}, u32[]{:S(2)}, u32[]{:S(2)}) collective-permute-start(bf16[32,32,128]{2,1,0:T(8,128)(2,1)S(1)} %copy-done.36), channel_id=1, source_target_pairs={{0,4},{1,5},{2,6},{3,7},{4,0},{5,1},{6,2},{7,3},{8,12},{9,13},{10,... | collective-permute-start | bytes 786440 | tf_op jit(solution)/shard_map/ppermute | solution.py:392
  285.7 33.6 %collective-permute-start.45 = (bf16[32,32,128]{2,1,0:T(8,128)(2,1)}, bf16[32,32,128]{2,1,0:T(8,128)(2,1)S(1)}, u32[]{:S(2)}, u32[]{:S(2)}) collective-permute-start(bf16[32,32,128]{2,1,0:T(8,128)(2,1)} %get-tuple-element.155), channel_id=1, source_target_pairs={{0,1},{1,0},{2,3},{3,2},{4,5},{5,4},{6,7},{7,6},{8,9},{9,8},{10,11... | collective-permute-start | bytes 786440 | tf_op jit(solution)/shard_map/ppermute | solution.py:392
  286.7 14.6 %collective-permute-start.52 = (bf16[32,16,128]{2,1,0:T(8,128)(2,1)}, bf16[32,16,128]{2,1,0:T(8,128)(2,1)S(1)}, u32[]{:S(2)}, u32[]{:S(2)}) collective-permute-start(bf16[32,16,128]{2,1,0:T(8,128)(2,1)} %get-tuple-element.165), channel_id=1, source_target_pairs={{0,1},{1,0},{2,3},{3,2},{4,5},{5,4},{6,7},{7,6},{8,9},{9,8},{10,11... | collective-permute-start | bytes 393224 | tf_op jit(solution)/shard_map/ppermute | solution.py:392
  286.8 28.7 %collective-permute-start.53 = (bf16[32,16,128]{2,1,0:T(8,128)(2,1)}, bf16[32,16,128]{2,1,0:T(8,128)(2,1)S(1)}, u32[]{:S(2)}, u32[]{:S(2)}) collective-permute-start(bf16[32,16,128]{2,1,0:T(8,128)(2,1)} %get-tuple-element.166), channel_id=1, source_target_pairs={{0,5},{1,4},{2,7},{3,6},{4,1},{5,0},{6,3},{7,2},{8,13},{9,12},{10,... | collective-permute-start | bytes 393224 | tf_op jit(solution)/shard_map/ppermute | solution.py:392
  301.3 14.9 %collective-permute-start.54 = (bf16[32,16,128]{2,1,0:T(8,128)(2,1)}, bf16[32,16,128]{2,1,0:T(8,128)(2,1)S(1)}, u32[]{:S(2)}, u32[]{:S(2)}) collective-permute-start(bf16[32,16,128]{2,1,0:T(8,128)(2,1)} %get-tuple-element.167), channel_id=1, source_target_pairs={{0,2},{1,3},{2,0},{3,1},{4,6},{5,7},{6,4},{7,5},{8,10},{9,11},{10,... | collective-permute-start | bytes 393224 | tf_op jit(solution)/shard_map/ppermute | solution.py:392
  302.0 34.1 %collective-permute-start.46 = (bf16[32,32,128]{2,1,0:T(8,128)(2,1)}, bf16[32,32,128]{2,1,0:T(8,128)(2,1)S(1)}, u32[]{:S(2)}, u32[]{:S(2)}) collective-permute-start(bf16[32,32,128]{2,1,0:T(8,128)(2,1)} %get-tuple-element.156), channel_id=1, source_target_pairs={{0,5},{1,4},{2,7},{3,6},{4,1},{5,0},{6,3},{7,2},{8,13},{9,12},{10,... | collective-permute-start | bytes 786440 | tf_op jit(solution)/shard_map/ppermute | solution.py:392
  316.1 22.9 %collective-permute-start.47 = (bf16[32,32,128]{2,1,0:T(8,128)(2,1)}, bf16[32,32,128]{2,1,0:T(8,128)(2,1)S(1)}, u32[]{:S(2)}, u32[]{:S(2)}) collective-permute-start(bf16[32,32,128]{2,1,0:T(8,128)(2,1)} %get-tuple-element.157), channel_id=1, source_target_pairs={{0,2},{1,3},{2,0},{3,1},{4,6},{5,7},{6,4},{7,5},{8,10},{9,11},{10,... | collective-permute-start | bytes 786440 | tf_op jit(solution)/shard_map/ppermute | solution.py:392
  316.8 22.9 %collective-permute-start.48 = (bf16[32,32,128]{2,1,0:T(8,128)(2,1)}, bf16[32,32,128]{2,1,0:T(8,128)(2,1)S(1)}, u32[]{:S(2)}, u32[]{:S(2)}) collective-permute-start(bf16[32,32,128]{2,1,0:T(8,128)(2,1)} %get-tuple-element.158), channel_id=1, source_target_pairs={{0,6},{1,7},{2,4},{3,5},{4,2},{5,3},{6,0},{7,1},{8,14},{9,15},{10,... | collective-permute-start | bytes 786440 | tf_op jit(solution)/shard_map/ppermute | solution.py:392
  319.0 27.3 %collective-permute-start.49 = (bf16[32,32,128]{2,1,0:T(8,128)(2,1)}, bf16[32,32,128]{2,1,0:T(8,128)(2,1)S(1)}, u32[]{:S(2)}, u32[]{:S(2)}) collective-permute-start(bf16[32,32,128]{2,1,0:T(8,128)(2,1)} %get-tuple-element.159), channel_id=1, source_target_pairs={{0,3},{1,2},{2,1},{3,0},{4,7},{5,6},{6,5},{7,4},{8,11},{9,10},{10,... | collective-permute-start | bytes 786440 | tf_op jit(solution)/shard_map/ppermute | solution.py:392
  319.2 28.3 %collective-permute-start.50 = (bf16[32,32,128]{2,1,0:T(8,128)(2,1)}, bf16[32,32,128]{2,1,0:T(8,128)(2,1)}, u32[]{:S(2)}, u32[]{:S(2)}) collective-permute-start(bf16[32,32,128]{2,1,0:T(8,128)(2,1)} %get-tuple-element.160), channel_id=1, source_target_pairs={{0,7},{1,6},{2,5},{3,4},{4,3},{5,2},{6,1},{7,0},{8,15},{9,14},{10,... | collective-permute-start | bytes 786440 | tf_op jit(solution)/shard_map/ppermute | solution.py:392
  336.8 22.0 %collective-permute-start.55 = (bf16[32,16,128]{2,1,0:T(8,128)(2,1)}, bf16[32,16,128]{2,1,0:T(8,128)(2,1)S(1)}, u32[]{:S(2)}, u32[]{:S(2)}) collective-permute-start(bf16[32,16,128]{2,1,0:T(8,128)(2,1)} %get-tuple-element.168), channel_id=1, source_target_pairs={{0,6},{1,7},{2,4},{3,5},{4,2},{5,3},{6,0},{7,1},{8,14},{9,15},{10,... | collective-permute-start | bytes 393224 | tf_op jit(solution)/shard_map/ppermute | solution.py:392
  339.7 19.7 %collective-permute-start.56 = (bf16[32,16,128]{2,1,0:T(8,128)(2,1)}, bf16[32,16,128]{2,1,0:T(8,128)(2,1)S(1)}, u32[]{:S(2)}, u32[]{:S(2)}) collective-permute-start(bf16[32,16,128]{2,1,0:T(8,128)(2,1)} %get-tuple-element.169), channel_id=1, source_target_pairs={{0,3},{1,2},{2,1},{3,0},{4,7},{5,6},{6,5},{7,4},{8,11},{9,10},{10,... | collective-permute-start | bytes 393224 | tf_op jit(solution)/shard_map/ppermute | solution.py:392
  340.4 19.7 %collective-permute-start.57 = (bf16[32,16,128]{2,1,0:T(8,128)(2,1)}, bf16[32,16,128]{2,1,0:T(8,128)(2,1)S(1)}, u32[]{:S(2)}, u32[]{:S(2)}) collective-permute-start(bf16[32,16,128]{2,1,0:T(8,128)(2,1)} %get-tuple-element.170), channel_id=1, source_target_pairs={{0,7},{1,6},{2,5},{3,4},{4,3},{5,2},{6,1},{7,0},{8,15},{9,14},{10,... | collective-permute-start | bytes 393224 | tf_op jit(solution)/shard_map/ppermute | solution.py:392
  347.0 40.4 %collective-permute-start.58 = (bf16[32,32,128]{2,1,0:T(8,128)(2,1)}, bf16[32,32,128]{2,1,0:T(8,128)(2,1)S(1)}, u32[]{:S(2)}, u32[]{:S(2)}) collective-permute-start(bf16[32,32,128]{2,1,0:T(8,128)(2,1)} %get-tuple-element.172), channel_id=1, source_target_pairs={{0,4},{1,5},{2,6},{3,7},{4,0},{5,1},{6,2},{7,3},{8,12},{9,13},{10,... | collective-permute-start | bytes 786440 | tf_op jit(solution)/shard_map/ppermute | solution.py:392
  347.5 40.1 %collective-permute-start.59 = (bf16[32,32,128]{2,1,0:T(8,128)(2,1)}, bf16[32,32,128]{2,1,0:T(8,128)(2,1)S(1)}, u32[]{:S(2)}, u32[]{:S(2)}) collective-permute-start(bf16[32,32,128]{2,1,0:T(8,128)(2,1)} %get-tuple-element.173), channel_id=1, source_target_pairs={{0,1},{1,0},{2,3},{3,2},{4,5},{5,4},{6,7},{7,6},{8,9},{9,8},{10,11... | collective-permute-start | bytes 786440 | tf_op jit(solution)/shard_map/ppermute | solution.py:392
  368.1 17.6 %collective-permute-start.65 = (bf16[32,16,128]{2,1,0:T(8,128)(2,1)}, bf16[32,16,128]{2,1,0:T(8,128)(2,1)S(1)}, u32[]{:S(2)}, u32[]{:S(2)}) collective-permute-start(bf16[32,16,128]{2,1,0:T(8,128)(2,1)} %get-tuple-element.181), channel_id=1, source_target_pairs={{0,4},{1,5},{2,6},{3,7},{4,0},{5,1},{6,2},{7,3},{8,12},{9,13},{10,... | collective-permute-start | bytes 393224 | tf_op jit(solution)/shard_map/ppermute | solution.py:392
  377.6 24.6 %collective-permute-start.60 = (bf16[32,32,128]{2,1,0:T(8,128)(2,1)}, bf16[32,32,128]{2,1,0:T(8,128)(2,1)S(1)}, u32[]{:S(2)}, u32[]{:S(2)}) collective-permute-start(bf16[32,32,128]{2,1,0:T(8,128)(2,1)} %get-tuple-element.174), channel_id=1, source_target_pairs={{0,5},{1,4},{2,7},{3,6},{4,1},{5,0},{6,3},{7,2},{8,13},{9,12},{10,... | collective-permute-start | bytes 786440 | tf_op jit(solution)/shard_map/ppermute | solution.py:392
  385.6 16.9 %collective-permute-start.61 = (bf16[32,32,128]{2,1,0:T(8,128)(2,1)}, bf16[32,32,128]{2,1,0:T(8,128)(2,1)S(1)}, u32[]{:S(2)}, u32[]{:S(2)}) collective-permute-start(bf16[32,32,128]{2,1,0:T(8,128)(2,1)} %get-tuple-element.175), channel_id=1, source_target_pairs={{0,2},{1,3},{2,0},{3,1},{4,6},{5,7},{6,4},{7,5},{8,10},{9,11},{10,... | collective-permute-start | bytes 786440 | tf_op jit(solution)/shard_map/ppermute | solution.py:392
  386.3 16.2 %collective-permute-start.62 = (bf16[32,32,128]{2,1,0:T(8,128)(2,1)}, bf16[32,32,128]{2,1,0:T(8,128)(2,1)}, u32[]{:S(2)}, u32[]{:S(2)}) collective-permute-start(bf16[32,32,128]{2,1,0:T(8,128)(2,1)} %get-tuple-element.176), channel_id=1, source_target_pairs={{0,6},{1,7},{2,4},{3,5},{4,2},{5,3},{6,0},{7,1},{8,14},{9,15},{10,... | collective-permute-start | bytes 786440 | tf_op jit(solution)/shard_map/ppermute | solution.py:392
  387.4 26.3 %collective-permute-start.63 = (bf16[32,32,128]{2,1,0:T(8,128)(2,1)}, bf16[32,32,128]{2,1,0:T(8,128)(2,1)}, u32[]{:S(2)}, u32[]{:S(2)}) collective-permute-start(bf16[32,32,128]{2,1,0:T(8,128)(2,1)} %get-tuple-element.177), channel_id=1, source_target_pairs={{0,3},{1,2},{2,1},{3,0},{4,7},{5,6},{6,5},{7,4},{8,11},{9,10},{10,... | collective-permute-start | bytes 786440 | tf_op jit(solution)/shard_map/ppermute | solution.py:392
  387.6 26.0 %collective-permute-start.64 = (bf16[32,32,128]{2,1,0:T(8,128)(2,1)}, bf16[32,32,128]{2,1,0:T(8,128)(2,1)}, u32[]{:S(2)}, u32[]{:S(2)}) collective-permute-start(bf16[32,32,128]{2,1,0:T(8,128)(2,1)} %get-tuple-element.178), channel_id=1, source_target_pairs={{0,7},{1,6},{2,5},{3,4},{4,3},{5,2},{6,1},{7,0},{8,15},{9,14},{10,... | collective-permute-start | bytes 786440 | tf_op jit(solution)/shard_map/ppermute | solution.py:392
  402.2 22.4 %collective-permute-start.67 = (bf16[32,16,128]{2,1,0:T(8,128)(2,1)}, bf16[32,16,128]{2,1,0:T(8,128)(2,1)S(1)}, u32[]{:S(2)}, u32[]{:S(2)}) collective-permute-start(bf16[32,16,128]{2,1,0:T(8,128)(2,1)} %get-tuple-element.183), channel_id=1, source_target_pairs={{0,5},{1,4},{2,7},{3,6},{4,1},{5,0},{6,3},{7,2},{8,13},{9,12},{10,... | collective-permute-start | bytes 393224 | tf_op jit(solution)/shard_map/ppermute | solution.py:392
  402.5 22.1 %collective-permute-start.68 = (bf16[32,16,128]{2,1,0:T(8,128)(2,1)}, bf16[32,16,128]{2,1,0:T(8,128)(2,1)S(1)}, u32[]{:S(2)}, u32[]{:S(2)}) collective-permute-start(bf16[32,16,128]{2,1,0:T(8,128)(2,1)} %get-tuple-element.184), channel_id=1, source_target_pairs={{0,2},{1,3},{2,0},{3,1},{4,6},{5,7},{6,4},{7,5},{8,10},{9,11},{10,... | collective-permute-start | bytes 393224 | tf_op jit(solution)/shard_map/ppermute | solution.py:392
  402.5 22.1 %collective-permute-start.69 = (bf16[32,16,128]{2,1,0:T(8,128)(2,1)}, bf16[32,16,128]{2,1,0:T(8,128)(2,1)S(1)}, u32[]{:S(2)}, u32[]{:S(2)}) collective-permute-start(bf16[32,16,128]{2,1,0:T(8,128)(2,1)} %get-tuple-element.185), channel_id=1, source_target_pairs={{0,6},{1,7},{2,4},{3,5},{4,2},{5,3},{6,0},{7,1},{8,14},{9,15},{10,... | collective-permute-start | bytes 393224 | tf_op jit(solution)/shard_map/ppermute | solution.py:392
  413.6 13.9 %collective-permute-start.70 = (bf16[32,16,128]{2,1,0:T(8,128)(2,1)}, bf16[32,16,128]{2,1,0:T(8,128)(2,1)S(1)}, u32[]{:S(2)}, u32[]{:S(2)}) collective-permute-start(bf16[32,16,128]{2,1,0:T(8,128)(2,1)} %get-tuple-element.186), channel_id=1, source_target_pairs={{0,3},{1,2},{2,1},{3,0},{4,7},{5,6},{6,5},{7,4},{8,11},{9,10},{10,... | collective-permute-start | bytes 393224 | tf_op jit(solution)/shard_map/ppermute | solution.py:392
  (65 other events, 1280.2 us)

commit v13 on v12

--- a/solution.py
+++ b/solution.py
@@ -145,9 +145,9 @@
 def spectra_kernel(
     meta_ref, delay_ref, est_ref, obs_ref, before_ref, after_ref, table_ref, _, *refs
 ):
-    *out_refs, energy_ref, est32, res32, stepped, result = refs
+    out_ref, energy_ref, est32, res32, stepped = refs
     shots, rows, samples = est_ref.shape
-    width = out_refs[0].shape[2]
+    peers, _, _, width = out_ref.shape
 
     def store(shot, column, values):
         start = pl.multiple_of(shot * rows, rows)
@@ -156,18 +156,17 @@
     blend_into(
         meta_ref, delay_ref, est_ref, obs_ref, before_ref, after_ref, energy_ref, est32, res32, store
     )
-    held = result.shape[0]
-    group = held // rows
+    group = min(shots, max(1, 256 // rows))
 
     def transform(part, carry):
-        start = pl.multiple_of(part * held, held)
-        result[...] = jnp.dot(
-            stepped[pl.ds(start, held), :], table_ref[...], preferred_element_type=jnp.float32
+        start = pl.multiple_of(part * (group * rows), group * rows)
+        result = jnp.dot(
+            stepped[pl.ds(start, group * rows), :], table_ref[...], preferred_element_type=jnp.float32
         ).astype(jnp.bfloat16)
-        for slot, ref in enumerate(out_refs):
-            ref[pl.ds(part * group, group)] = result[:, band(meta_ref, slot, width)].reshape(
-                group, rows, width
-            )
+        for peer in range(peers):
+            out_ref[peer, pl.ds(part * group, group)] = result[
+                :, peer * width : (peer + 1) * width
+            ].reshape(group, rows, width)
         return carry
 
     lax.fori_loop(0, shots // group, transform, 0)
@@ -186,7 +185,7 @@
 
 def shots_kernel(meta_ref, table_ref, level_ref, _, *refs):
     *refs, wide, back = refs
-    spectra_refs, out_refs = refs[: len(refs) // 2], refs[len(refs) // 2 :]
+    spectra_ref, *out_refs = refs
     held, rows, width = out_refs[0].shape
     shots = wide.shape[0] // rows
     half = width // 2
@@ -195,8 +194,7 @@
         size = held * rows
         return pl.ds(pl.multiple_of(meta_ref[1 + slot] * size, size), size)
 
-    for slot, ref in zip(slots_of(len(spectra_refs)), spectra_refs):
-        wide[place(slot), :] = ref[...].reshape(held * rows, width).astype(jnp.float32)
+    wide[...] = spectra_ref[...].reshape(shots * rows, width).astype(jnp.float32)
     level = level_ref[...]
     sign = jnp.where(
         lax.broadcasted_iota(jnp.int32, (1, width), 1) < half, jnp.float32(1.0), jnp.float32(-1.0)
@@ -265,23 +263,19 @@
 
 def spectra_of(meta, delays, fields, table, rows, block, edge_block, peers, after):
     shots, _, samples = fields[0].shape
-    shape = (shots, rows, 2 * F // peers)
-    group = min(shots, max(1, 256 // rows))
-    *spectra, energy = pl.pallas_call(
+    shape = (peers, shots, rows, 2 * F // peers)
+    return pl.pallas_call(
         spectra_kernel,
         grid_spec=pltpu.PrefetchScalarGridSpec(
             num_scalar_prefetch=2,
             grid=(1,),
             in_specs=blend_specs(shots, rows, samples, block, edge_block)
             + [whole(table.shape), ANYWHERE],
-            out_specs=[whole(shape)] * peers + [whole((shots, LANES))],
+            out_specs=[whole(shape), whole((shots, LANES))],
             scratch_shapes=blend_scratch(shots, rows, samples)
-            + [
-                pltpu.VMEM((shots * rows, samples), jnp.bfloat16),
-                pltpu.VMEM((group * rows, 2 * F), jnp.bfloat16),
-            ],
-        ),
-        out_shape=[pltpu.HBM(shape, jnp.bfloat16)] * peers + [pltpu.HBM((shots, LANES), jnp.float32)],
+            + [pltpu.VMEM((shots * rows, samples), jnp.bfloat16)],
+        ),
+        out_shape=[pltpu.HBM(shape, jnp.bfloat16), pltpu.HBM((shots, LANES), jnp.float32)],
         compiler_params=PARAMS,
         cost_estimate=pl.CostEstimate(
             flops=4 * F * shots * rows * samples,
@@ -290,7 +284,6 @@
         ),
         name="spectra",
     )(meta, delays, *fields, table, after)
-    return spectra, energy
 
 
 def stepped_of(meta, delays, fields, rows, index):
@@ -314,16 +307,15 @@
 
 
 def shrunk_of(meta, spectra, table, level, after):
-    shape = spectra[0].shape
-    held, rows, width = shape
-    peers = len(spectra)
+    peers, held, rows, width = spectra.shape
+    shape = (held, rows, width)
     return pl.pallas_call(
         shots_kernel,
         grid_spec=pltpu.PrefetchScalarGridSpec(
             num_scalar_prefetch=1,
             grid=(1,),
             in_specs=[whole(table.shape), whole(level.shape), ANYWHERE]
-            + [whole(shape)] * peers,
+            + [whole(spectra.shape)],
             out_specs=[whole(shape)] * peers,
             scratch_shapes=[pltpu.VMEM((peers * held * rows, width), jnp.float32)] * 2,
         ),
@@ -335,7 +327,7 @@
             transcendentals=peers * held * rows * width,
         ),
         name="shrink",
-    )(meta, table, level, after, *spectra)
+    )(meta, table, level, after, spectra)
 
 
 def updated_of(meta, restored, table, block, receivers, onto, after):
@@ -442,7 +434,7 @@
             )
             last = power
             energy = energy + power
-            ahead[turn] = exchanged(spectra)
+            ahead[turn] = swapped(spectra)
         place = turn - lag
         if place in ahead:
             shrunk = shrunk_of(meta, ahead.pop(place), table, levels, last)

time: 433 us -> 487 us (1.12)
  waiting for transfers between devices: 150 us -> 229 us
  starting transfers between devices: 95.6 us -> 83.5 us
  local copies, waits for them, and re-layouts: 23.2 us -> 12.5 us
    ppermute x70 -> x35, starting transfers between devices: 91.9 us -> 45.9 us  [exchanged(): lax.ppermute(arrays[slot], 'shot', [(i, i ^ slot) for i in range(peers)])]
    all_to_all x0 -> x5, waiting for transfers between devices: none -> 39.9 us  [swapped(): lax.all_to_all(array, 'shot', split_axis=0, concat_axis=0, tiled=True)]
    ppermute x70 -> x35, waiting for transfers between devices: 147 us -> 186 us  [exchanged(): lax.ppermute(arrays[slot], 'shot', [(i, i ^ slot) for i in range(peers)])]
    all_to_all x0 -> x5, starting transfers between devices: none -> 33.9 us  [swapped(): lax.all_to_all(array, 'shot', split_axis=0, concat_axis=0, tiled=True)]
    unnamed x114 -> x66, local copies, waits for them, and re-layouts: 19.5 us -> 8.79 us
  transfers between devices with their start and end apart: 72 -> 42, of which waited for: 20 -> 11; matrix products, arithmetic and copies ran while one was open for 1% -> 1% of each run, Pallas kernels for 30% -> 27%
where the time goes in v13:
time: 487 us; the launch traced here: 485 us
  waiting for transfers between devices  229 us (47%)
  Pallas kernels  145 us (30%)
  starting transfers between devices  83.5 us (17%)
  local copies, waits for them, and re-layouts  12.5 us (3%)
  blocking collectives  9.91 us (2%)
    ppermute x35, waiting for transfers between devices, exchanged(): lax.ppermute(arrays[slot], 'shot', [(i, i ^ slot) for i in range(peers)])  186 us
    pallas_call x5, Pallas kernels, spectra_of(): pl.pallas_call(spectra_kernel, grid_spec=pltpu.PrefetchScalarGridSpec(num...  61.9 us
    pallas_call x5, Pallas kernels, shrunk_of(): pl.pallas_call(shots_kernel, grid_spec=pltpu.PrefetchScalarGridSpec(num_s...  58.8 us
    ppermute x35, starting transfers between devices, exchanged(): lax.ppermute(arrays[slot], 'shot', [(i, i ^ slot) for i in range(peers)])  45.9 us
    all_to_all x5, waiting for transfers between devices, swapped(): lax.all_to_all(array, 'shot', split_axis=0, concat_axis=0, tiled=True)  39.9 us
    all_to_all x5, starting transfers between devices, swapped(): lax.all_to_all(array, 'shot', split_axis=0, concat_axis=0, tiled=True)  33.9 us
    pallas_call x5, Pallas kernels, updated_of(): pl.pallas_call(functools.partial(update_kernel, len(restored)), grid_spec...  24.8 us
    psum x1, blocking collectives, local(): lax.psum(jnp.sum(energy, axis=1), 'patch')  9.91 us
  transfers between devices with their start and end apart: 42, of which 11 were waited for; matrix products, arithmetic and copies ran while one was open for 1% of the time, Pallas kernels for 27%

profile of v13, /device:TPU:0, one launch (start us, length us, event | category | flops | bytes accessed | tf_op | source)
XLA Modules:
  0.0 484.8 jit_solution(16776169081836892861)
XLA Ops:
  0.6 1.1 fusion.1
  1.7 1.3 fusion
  3.1 2.4 collective-permute-start
  5.5 0.9 pad_maximum_fusion.1
  6.4 1.3 collective-permute-start.1
  7.7 0.8 dynamic_slice.3
  9.6 3.3 collective-permute-done.1.after_ref
  12.9 0.9 copy-done.21
  13.8 9.5 %spectra.5 = (bf16[8,32,16,128]{3,2,1,0:T(8,128)(2,1)}, f32[32,128]{1,0:T(8,128)}) custom-call(s32[9]{0:T(128)} %pad_add_fusion.meta_ref, s32[256]{0:T(256)} %delay_ref.9, bf16[32,128,1024]{2,1,0:T(8,128)(2,1)} %est_ref.9, bf16[32,128,1024]{2,1,0:T(8,128)(2,1)} %obs_ref.9, bf16[3,128,1024]{2,1,0:T(8,128)(2,1)} %copy-done.20, ...), custom_call_target="tpu_custom_call" | custom-call | flops 1073741824 | bytes 5242880 | tf_op jit(solution)/shard_map/spectra/pallas_call | solution.py:267
  23.4 13.1 %all-to-all-start = ((bf16[8,32,16,128]{3,2,1,0:T(8,128)(2,1)}), bf16[8,32,16,128]{3,2,1,0:T(8,128)(2,1)S(1)}, u32[]{:S(2)}, u32[]{:S(2)}) async-start(bf16[8,32,16,128]{3,2,1,0:T(8,128)(2,1)} %get-tuple-element.63), calls=%async_computation | async-start | bytes 2097152 | tf_op jit(solution)/shard_map/all_to_all | solution.py:371
  36.5 14.1 %spectra.6 = (bf16[8,32,32,128]{3,2,1,0:T(8,128)(2,1)}, f32[32,128]{1,0:T(8,128)}) custom-call(s32[9]{0:T(128)} %pad_add_fusion.meta_ref, s32[256]{0:T(256)} %delay_ref.9, bf16[32,128,1024]{2,1,0:T(8,128)(2,1)} %est_ref.9, bf16[32,128,1024]{2,1,0:T(8,128)(2,1)} %obs_ref.9, bf16[3,128,1024]{2,1,0:T(8,128)(2,1)} %copy-done.20, ...), custom_call_target="tpu_custom_call" | custom-call | flops 2147483648 | bytes 8388608 | tf_op jit(solution)/shard_map/spectra/pallas_call | solution.py:267
  50.6 12.5 %all-to-all-done.refs_0_ = bf16[8,32,16,128]{3,2,1,0:T(8,128)(2,1)S(1)} async-done(((bf16[8,32,16,128]{3,2,1,0:T(8,128)(2,1)}), bf16[8,32,16,128]{3,2,1,0:T(8,128)(2,1)S(1)}, u32[]{:S(2)}, u32[]{:S(2)}) %all-to-all-start) | async-done | bytes 1048608 | tf_op jit(solution)/shard_map/all_to_all | solution.py:371
  63.0 4.3 all-to-all-start.1
  67.4 7.2 %shrink.5 = (bf16[32,16,128]{2,1,0:T(8,128)(2,1)}, bf16[32,16,128]{2,1,0:T(8,128)(2,1)}, bf16[32,16,128]{2,1,0:T(8,128)(2,1)}, bf16[32,16,128]{2,1,0:T(8,128)(2,...) custom-call(s32[9]{0:T(128)} %pad_add_fusion.meta_ref, ...), custom_call_target="tpu_custom_call" | custom-call | flops 1073741824 | bytes 2359296 | tf_op jit(solution)/shard_map/shrink/pallas_call | solution.py:312
  74.7 14.3 %spectra.7 = (bf16[8,32,32,128]{3,2,1,0:T(8,128)(2,1)}, f32[32,128]{1,0:T(8,128)}) custom-call(s32[9]{0:T(128)} %pad_add_fusion.meta_ref, s32[256]{0:T(256)} %delay_ref.9, bf16[32,128,1024]{2,1,0:T(8,128)(2,1)} %est_ref.9, bf16[32,128,1024]{2,1,0:T(8,128)(2,1)} %obs_ref.9, bf16[3,128,1024]{2,1,0:T(8,128)(2,1)} %copy-done.20, ...), custom_call_target="tpu_custom_call" | custom-call | flops 2147483648 | bytes 8388608 | tf_op jit(solution)/shard_map/spectra/pallas_call | solution.py:267
  89.0 27.4 %all-to-all-done.1.refs_0_ = bf16[8,32,32,128]{3,2,1,0:T(8,128)(2,1)} async-done(((bf16[8,32,32,128]{3,2,1,0:T(8,128)(2,1)}), bf16[8,32,32,128]{3,2,1,0:T(8,128)(2,1)}, u32[]{:S(2)}, u32[]{:S(2)}) %all-to-all-start.1) | async-done | bytes 2097184 | tf_op jit(solution)/shard_map/all_to_all | solution.py:371
  116.5 4.4 all-to-all-start.2
  120.8 2.8 collective-permute-start.2
  124.0 1.8 collective-permute-start.5
  125.8 2.4 collective-permute-start.6
  128.2 53.3 %collective-permute-done.2.refs_1_ = bf16[32,16,128]{2,1,0:T(8,128)(2,1)S(1)} collective-permute-done((bf16[32,16,128]{2,1,0:T(8,128)(2,1)S(1)}, bf16[32,16,128]{2,1,0:T(8,128)(2,1)S(1)}, u32[]{:S(2)}, u32[]{:S(2)}) %collective-permute-start.2) | collective-permute-done | bytes 131104 | tf_op jit(solution)/shard_map/ppermute | solution.py:384
  181.5 0.7 collective-permute-start.8
  182.2 14.8 %shrink.6 = (bf16[32,32,128]{2,1,0:T(8,128)(2,1)}, bf16[32,32,128]{2,1,0:T(8,128)(2,1)}, bf16[32,32,128]{2,1,0:T(8,128)(2,1)}, bf16[32,32,128]{2,1,0:T(8,128)(2,...) custom-call(s32[9]{0:T(128)} %pad_add_fusion.meta_ref, ...), custom_call_target="tpu_custom_call" | custom-call | flops 2147483648 | bytes 4456448 | tf_op jit(solution)/shard_map/shrink/pallas_call | solution.py:312
  197.1 0.9 copy-done.6
  198.1 3.2 update.5
  201.9 14.2 %spectra.8 = (bf16[8,32,32,128]{3,2,1,0:T(8,128)(2,1)}, f32[32,128]{1,0:T(8,128)}) custom-call(s32[9]{0:T(128)} %pad_add_fusion.meta_ref, s32[256]{0:T(256)} %delay_ref.9, bf16[32,128,1024]{2,1,0:T(8,128)(2,1)} %est_ref.9, bf16[32,128,1024]{2,1,0:T(8,128)(2,1)} %obs_ref.9, bf16[3,128,1024]{2,1,0:T(8,128)(2,1)} %copy-done.20, ...), custom_call_target="tpu_custom_call" | custom-call | flops 2147483648 | bytes 8388608 | tf_op jit(solution)/shard_map/spectra/pallas_call | solution.py:267
  216.1 4.7 all-to-all-start.3
  220.8 2.6 collective-permute-start.9
  223.9 1.6 collective-permute-start.12
  225.6 2.4 collective-permute-start.13
  228.0 64.6 %collective-permute-done.9.refs_1_ = bf16[32,32,128]{2,1,0:T(8,128)(2,1)S(1)} collective-permute-done((bf16[32,32,128]{2,1,0:T(8,128)(2,1)S(1)}, bf16[32,32,128]{2,1,0:T(8,128)(2,1)S(1)}, u32[]{:S(2)}, u32[]{:S(2)}) %collective-permute-start.9) | collective-permute-done | bytes 262176 | tf_op jit(solution)/shard_map/ppermute | solution.py:384
  292.5 0.7 collective-permute-start.15
  293.3 14.8 %shrink.7 = (bf16[32,32,128]{2,1,0:T(8,128)(2,1)}, bf16[32,32,128]{2,1,0:T(8,128)(2,1)}, bf16[32,32,128]{2,1,0:T(8,128)(2,1)}, bf16[32,32,128]{2,1,0:T(8,128)(2,...) custom-call(s32[9]{0:T(128)} %pad_add_fusion.meta_ref, ...), custom_call_target="tpu_custom_call" | custom-call | flops 2147483648 | bytes 4456448 | tf_op jit(solution)/shard_map/shrink/pallas_call | solution.py:312
  308.1 0.9 collective-permute-done.14.refs_6_
  308.9 0.9 copy-done.3
  309.9 5.9 %update.6 = (f32[32,128,1024]{2,1,0:T(8,128)}, f32[8,128]{1,0:T(8,128)S(1)}) custom-call(s32[9]{0:T(128)S(1)} %copy-done.14, bf16[1024,1024]{1,0:T(8,128)(2,1)S(1)} %copy-done, bf16[32,32,128]{2,1,0:T(8,128)(2,1)S(1)} %copy-done.3, bf16[32,32,128]{2,1,0:T(8,128)(2,1)S(1)} %copy-done.7, ...), custom_call_target="tpu_custom_call", output_to_operand_aliasing={{0}: (11, {})} | custom-call | flops 2147483648 | bytes 8388608 | tf_op jit(solution)/shard_map/update/pallas_call | solution.py:343
  316.4 9.7 %spectra.9 = (bf16[8,32,16,128]{3,2,1,0:T(8,128)(2,1)}, f32[32,128]{1,0:T(8,128)}) custom-call(s32[9]{0:T(128)} %pad_add_fusion.meta_ref, s32[256]{0:T(256)} %delay_ref.9, bf16[32,128,1024]{2,1,0:T(8,128)(2,1)} %est_ref.9, bf16[32,128,1024]{2,1,0:T(8,128)(2,1)} %obs_ref.9, bf16[3,128,1024]{2,1,0:T(8,128)(2,1)} %copy-done.20, ...), custom_call_target="tpu_custom_call" | custom-call | flops 1073741824 | bytes 5242880 | tf_op jit(solution)/shard_map/spectra/pallas_call | solution.py:267
  326.1 7.5 %all-to-all-start.4 = ((bf16[8,32,16,128]{3,2,1,0:T(8,128)(2,1)}), bf16[8,32,16,128]{3,2,1,0:T(8,128)(2,1)}, u32[]{:S(2)}, u32[]{:S(2)}) async-start(bf16[8,32,16,128]{3,2,1,0:T(8,128)(2,1)} %get-tuple-element.100), calls=%async_computation.4 | async-start | bytes 2097152 | tf_op jit(solution)/shard_map/all_to_all | solution.py:371
  333.6 3.0 collective-permute-start.16
  336.8 2.6 collective-permute-start.19
  339.4 1.7 collective-permute-start.20
  341.1 42.0 %collective-permute-done.16.refs_1_ = bf16[32,32,128]{2,1,0:T(8,128)(2,1)S(1)} collective-permute-done((bf16[32,32,128]{2,1,0:T(8,128)(2,1)}, bf16[32,32,128]{2,1,0:T(8,128)(2,1)S(1)}, u32[]{:S(2)}, u32[]{:S(2)}) %collective-permute-start.16) | collective-permute-done | bytes 262176 | tf_op jit(solution)/shard_map/ppermute | solution.py:384
  383.1 0.8 collective-permute-start.22
  384.0 14.8 %shrink.8 = (bf16[32,32,128]{2,1,0:T(8,128)(2,1)}, bf16[32,32,128]{2,1,0:T(8,128)(2,1)}, bf16[32,32,128]{2,1,0:T(8,128)(2,1)}, bf16[32,32,128]{2,1,0:T(8,128)(2,...) custom-call(s32[9]{0:T(128)} %pad_add_fusion.meta_ref, ...), custom_call_target="tpu_custom_call" | custom-call | flops 2147483648 | bytes 4456448 | tf_op jit(solution)/shard_map/shrink/pallas_call | solution.py:312
  398.7 2.4 collective-permute-start.23
  401.1 0.7 copy-done.8
  401.9 0.9 copy-done.1
  402.8 0.9 copy-done.9
  403.8 6.2 %update.7 = (f32[32,128,1024]{2,1,0:T(8,128)}, f32[8,128]{1,0:T(8,128)S(1)}) custom-call(s32[9]{0:T(128)S(1)} %copy-done.15, bf16[1024,1024]{1,0:T(8,128)(2,1)S(1)} %copy-done, bf16[32,32,128]{2,1,0:T(8,128)(2,1)S(1)} %copy-done.1, bf16[32,32,128]{2,1,0:T(8,128)(2,1)S(1)} %copy-done.4, ...), custom_call_target="tpu_custom_call", output_to_operand_aliasing={{0}: (11, {})} | custom-call | flops 2147483648 | bytes 8388608 | tf_op jit(solution)/shard_map/update/pallas_call | solution.py:343
  410.6 7.2 %shrink.9 = (bf16[32,16,128]{2,1,0:T(8,128)(2,1)}, bf16[32,16,128]{2,1,0:T(8,128)(2,1)}, bf16[32,16,128]{2,1,0:T(8,128)(2,1)}, bf16[32,16,128]{2,1,0:T(8,128)(2,...) custom-call(s32[9]{0:T(128)} %pad_add_fusion.meta_ref, ...), custom_call_target="tpu_custom_call" | custom-call | flops 1073741824 | bytes 2359296 | tf_op jit(solution)/shard_map/shrink/pallas_call | solution.py:312
  417.8 9.4 %collective-permute-start.30 = (bf16[32,16,128]{2,1,0:T(8,128)(2,1)}, bf16[32,16,128]{2,1,0:T(8,128)(2,1)S(1)}, u32[]{:S(2)}, u32[]{:S(2)}) collective-permute-start(bf16[32,16,128]{2,1,0:T(8,128)(2,1)} %get-tuple-element.111), channel_id=1, source_target_pairs={{0,4},{1,5},{2,6},{3,7},{4,0},{5,1},{6,2},{7,3},{8,12},{9,13},{10,... | collective-permute-start | bytes 393224 | tf_op jit(solution)/shard_map/ppermute | solution.py:384
  427.3 12.4 %collective-permute-done.30.refs_1_ = bf16[32,16,128]{2,1,0:T(8,128)(2,1)S(1)} collective-permute-done((bf16[32,16,128]{2,1,0:T(8,128)(2,1)}, bf16[32,16,128]{2,1,0:T(8,128)(2,1)S(1)}, u32[]{:S(2)}, u32[]{:S(2)}) %collective-permute-start.30) | collective-permute-done | bytes 131104 | tf_op jit(solution)/shard_map/ppermute | solution.py:384
  440.4 2.5 collective-permute-start.27
  443.1 1.9 collective-permute-start.29
  445.0 0.9 add_reduce_fusion
  445.9 9.9 %psum.7 = f32[32]{0:T(128)S(1)} all-reduce(f32[32]{0:T(128)S(1)} %add_reduce_fusion), channel_id=1, replica_groups=mesh['patch'=4,'shot'=8] {'patch'}, use_global_device_ids=true, to_apply=%region_1.0 | all-reduce | flops 32 | bytes 256 | tf_op jit(solution)/shard_map/psum | solution.py:509
  456.5 0.8 collective-permute-start.33
  457.3 1.8 collective-permute-start.34
  459.2 8.5 %collective-permute-done.28.refs_6_ = bf16[32,32,128]{2,1,0:T(8,128)(2,1)} collective-permute-done((bf16[32,32,128]{2,1,0:T(8,128)(2,1)}, bf16[32,32,128]{2,1,0:T(8,128)(2,1)}, u32[]{:S(2)}, u32[]{:S(2)}) %collective-permute-start.28) | collective-permute-done | bytes 262176 | tf_op jit(solution)/shard_map/ppermute | solution.py:384
  467.7 2.4 collective-permute-start.36
  470.1 0.9 copy-done.5
  471.0 6.2 %update.8 = (f32[32,128,1024]{2,1,0:T(8,128)}, f32[8,128]{1,0:T(8,128)S(1)}) custom-call(s32[9]{0:T(128)S(1)} %copy-done.16, bf16[1024,1024]{1,0:T(8,128)(2,1)S(1)} %copy-done, bf16[32,16,128]{2,1,0:T(8,128)(2,1)S(1)} %copy-done.5, bf16[32,32,128]{2,1,0:T(8,128)(2,1)S(1)} %copy-done.2, ...), custom_call_target="tpu_custom_call", output_to_operand_aliasing={{0}: (11, {})} | custom-call | flops 2147483648 | bytes 8388608 | tf_op jit(solution)/shard_map/update/pallas_call | solution.py:343
  477.2 4.3 collective-permute-done.35.refs_6_
  481.6 3.2 update.9
  (113 shorter events, 5.9 us)
Async XLA Ops:
  3.1 6.6 %collective-permute-start = (bf16[3,128,1024]{2,1,0:T(8,128)(2,1)S(1)}, bf16[3,128,1024]{2,1,0:T(8,128)(2,1)S(1)}, u32[]{:S(2)}, u32[]{:S(2)}) collective-permute-start(bf16[3,128,1024]{2,1,0:T(8,128)(2,1)S(1)} %pad_maximum_fusion), channel_id=1, source_target_pairs={{0,1},{1,2},{2,3},{3,4},{4,5},{5,6},{6,7},{8,9},{9,10},{10,11},{11... | collective-permute-start | bytes 2359304 | tf_op jit(solution)/shard_map/ppermute | solution.py:395
  6.4 6.5 %collective-permute-start.1 = (bf16[3,128,1024]{2,1,0:T(8,128)(2,1)}, bf16[3,128,1024]{2,1,0:T(8,128)(2,1)S(1)}, u32[]{:S(2)}, u32[]{:S(2)}) collective-permute-start(bf16[3,128,1024]{2,1,0:T(8,128)(2,1)} %pad_maximum_fusion.1), channel_id=1, source_target_pairs={{1,0},{2,1},{3,2},{4,3},{5,4},{6,5},{7,6},{9,8},{10,9},{11,10},{12... | collective-permute-start | bytes 2359304 | tf_op jit(solution)/shard_map/ppermute | solution.py:395
  9.6 3.3 copy-start.20
  23.4 39.7 %all-to-all-start = ((bf16[8,32,16,128]{3,2,1,0:T(8,128)(2,1)}), bf16[8,32,16,128]{3,2,1,0:T(8,128)(2,1)S(1)}, u32[]{:S(2)}, u32[]{:S(2)}) async-start(bf16[8,32,16,128]{3,2,1,0:T(8,128)(2,1)} %get-tuple-element.63), calls=%async_computation | async-start | bytes 2097152 | tf_op jit(solution)/shard_map/all_to_all | solution.py:371
  63.0 4.4 copy-start.22
  63.0 53.4 %all-to-all-start.1 = ((bf16[8,32,32,128]{3,2,1,0:T(8,128)(2,1)}), bf16[8,32,32,128]{3,2,1,0:T(8,128)(2,1)}, u32[]{:S(2)}, u32[]{:S(2)}) async-start(bf16[8,32,32,128]{3,2,1,0:T(8,128)(2,1)} %get-tuple-element.66), calls=%async_computation.1 | async-start | bytes 4194304 | tf_op jit(solution)/shard_map/all_to_all | solution.py:371
  74.6 46.2 %copy-start.32 = (bf16[32,16,128]{2,1,0:T(8,128)(2,1)S(1)}, bf16[32,16,128]{2,1,0:T(8,128)(2,1)}, u32[]{:S(2)}) copy-start(bf16[32,16,128]{2,1,0:T(8,128)(2,1)} %get-tuple-element.68) | copy-start | bytes 393220
  74.6 49.0 %copy-start.31 = (bf16[32,16,128]{2,1,0:T(8,128)(2,1)S(1)}, bf16[32,16,128]{2,1,0:T(8,128)(2,1)}, u32[]{:S(2)}) copy-start(bf16[32,16,128]{2,1,0:T(8,128)(2,1)} %get-tuple-element.69) | copy-start | bytes 393220
  74.6 49.0 %copy-start.30 = (bf16[32,16,128]{2,1,0:T(8,128)(2,1)S(1)}, bf16[32,16,128]{2,1,0:T(8,128)(2,1)}, u32[]{:S(2)}) copy-start(bf16[32,16,128]{2,1,0:T(8,128)(2,1)} %get-tuple-element.70) | copy-start | bytes 393220
  74.6 49.3 %copy-start.29 = (bf16[32,16,128]{2,1,0:T(8,128)(2,1)S(1)}, bf16[32,16,128]{2,1,0:T(8,128)(2,1)}, u32[]{:S(2)}) copy-start(bf16[32,16,128]{2,1,0:T(8,128)(2,1)} %get-tuple-element.71) | copy-start | bytes 393220
  74.6 51.2 %copy-start.28 = (bf16[32,16,128]{2,1,0:T(8,128)(2,1)S(1)}, bf16[32,16,128]{2,1,0:T(8,128)(2,1)}, u32[]{:S(2)}) copy-start(bf16[32,16,128]{2,1,0:T(8,128)(2,1)} %get-tuple-element.72) | copy-start | bytes 393220
  74.6 106.9 %copy-start.27 = (bf16[32,16,128]{2,1,0:T(8,128)(2,1)S(1)}, bf16[32,16,128]{2,1,0:T(8,128)(2,1)}, u32[]{:S(2)}) copy-start(bf16[32,16,128]{2,1,0:T(8,128)(2,1)} %get-tuple-element.73) | copy-start | bytes 393220
  74.7 106.9 %copy-start.26 = (bf16[32,16,128]{2,1,0:T(8,128)(2,1)S(1)}, bf16[32,16,128]{2,1,0:T(8,128)(2,1)}, u32[]{:S(2)}) copy-start(bf16[32,16,128]{2,1,0:T(8,128)(2,1)} %get-tuple-element.74) | copy-start | bytes 393220
  89.0 108.1 %copy-start = (bf16[1024,1024]{1,0:T(8,128)(2,1)S(1)}, bf16[1024,1024]{1,0:T(8,128)(2,1)}, u32[]{:S(2)}) copy-start(bf16[1024,1024]{1,0:T(8,128)(2,1)} %constant.24.clone.table_ref) | copy-start | bytes 6291460
  89.0 108.1 %copy-start.12 = (bf16[32,16,128]{2,1,0:T(8,128)(2,1)S(1)}, bf16[32,16,128]{2,1,0:T(8,128)(2,1)}, u32[]{:S(2)}) copy-start(bf16[32,16,128]{2,1,0:T(8,128)(2,1)} %get-tuple-element.64._.refs_0_) | copy-start | bytes 393220
  89.0 108.1 %copy-start.13 = (s32[9]{0:T(128)S(1)}, s32[9]{0:T(128)}, u32[]{:S(2)}) copy-start(s32[9]{0:T(128)} %pad_add_fusion.meta_ref) | copy-start | bytes 112
  116.5 99.7 %all-to-all-start.2 = ((bf16[8,32,32,128]{3,2,1,0:T(8,128)(2,1)}), bf16[8,32,32,128]{3,2,1,0:T(8,128)(2,1)}, u32[]{:S(2)}, u32[]{:S(2)}) async-start(bf16[8,32,32,128]{3,2,1,0:T(8,128)(2,1)} %get-tuple-element.77), calls=%async_computation.2 | async-start | bytes 4194304 | tf_op jit(solution)/shard_map/all_to_all | solution.py:371
  120.8 60.7 %collective-permute-start.2 = (bf16[32,16,128]{2,1,0:T(8,128)(2,1)S(1)}, bf16[32,16,128]{2,1,0:T(8,128)(2,1)S(1)}, u32[]{:S(2)}, u32[]{:S(2)}) collective-permute-start(bf16[32,16,128]{2,1,0:T(8,128)(2,1)S(1)} %copy-done.32), channel_id=1, source_target_pairs={{0,4},{1,5},{2,6},{3,7},{4,0},{5,1},{6,2},{7,3},{8,12},{9,13},{10,... | collective-permute-start | bytes 393224 | tf_op jit(solution)/shard_map/ppermute | solution.py:384
  123.7 57.9 %collective-permute-start.3 = (bf16[32,16,128]{2,1,0:T(8,128)(2,1)S(1)}, bf16[32,16,128]{2,1,0:T(8,128)(2,1)S(1)}, u32[]{:S(2)}, u32[]{:S(2)}) collective-permute-start(bf16[32,16,128]{2,1,0:T(8,128)(2,1)S(1)} %copy-done.31), channel_id=1, source_target_pairs={{0,1},{1,0},{2,3},{3,2},{4,5},{5,4},{6,7},{7,6},{8,9},{9,8},{10,11... | collective-permute-start | bytes 393224 | tf_op jit(solution)/shard_map/ppermute | solution.py:384
  123.7 73.4 %collective-permute-start.4 = (bf16[32,16,128]{2,1,0:T(8,128)(2,1)S(1)}, bf16[32,16,128]{2,1,0:T(8,128)(2,1)S(1)}, u32[]{:S(2)}, u32[]{:S(2)}) collective-permute-start(bf16[32,16,128]{2,1,0:T(8,128)(2,1)S(1)} %copy-done.30), channel_id=1, source_target_pairs={{0,5},{1,4},{2,7},{3,6},{4,1},{5,0},{6,3},{7,2},{8,13},{9,12},{10,... | collective-permute-start | bytes 393224 | tf_op jit(solution)/shard_map/ppermute | solution.py:384
  124.0 73.1 %collective-permute-start.5 = (bf16[32,16,128]{2,1,0:T(8,128)(2,1)S(1)}, bf16[32,16,128]{2,1,0:T(8,128)(2,1)S(1)}, u32[]{:S(2)}, u32[]{:S(2)}) collective-permute-start(bf16[32,16,128]{2,1,0:T(8,128)(2,1)S(1)} %copy-done.29), channel_id=1, source_target_pairs={{0,2},{1,3},{2,0},{3,1},{4,6},{5,7},{6,4},{7,5},{8,10},{9,11},{10,... | collective-permute-start | bytes 393224 | tf_op jit(solution)/shard_map/ppermute | solution.py:384
  125.8 71.3 %collective-permute-start.6 = (bf16[32,16,128]{2,1,0:T(8,128)(2,1)S(1)}, bf16[32,16,128]{2,1,0:T(8,128)(2,1)S(1)}, u32[]{:S(2)}, u32[]{:S(2)}) collective-permute-start(bf16[32,16,128]{2,1,0:T(8,128)(2,1)S(1)} %copy-done.28), channel_id=1, source_target_pairs={{0,6},{1,7},{2,4},{3,5},{4,2},{5,3},{6,0},{7,1},{8,14},{9,15},{10,... | collective-permute-start | bytes 393224 | tf_op jit(solution)/shard_map/ppermute | solution.py:384
  181.5 15.6 %collective-permute-start.7 = (bf16[32,16,128]{2,1,0:T(8,128)(2,1)S(1)}, bf16[32,16,128]{2,1,0:T(8,128)(2,1)S(1)}, u32[]{:S(2)}, u32[]{:S(2)}) collective-permute-start(bf16[32,16,128]{2,1,0:T(8,128)(2,1)S(1)} %copy-done.27), channel_id=1, source_target_pairs={{0,3},{1,2},{2,1},{3,0},{4,7},{5,6},{6,5},{7,4},{8,11},{9,10},{10,... | collective-permute-start | bytes 393224 | tf_op jit(solution)/shard_map/ppermute | solution.py:384
  181.5 15.6 %collective-permute-start.8 = (bf16[32,16,128]{2,1,0:T(8,128)(2,1)S(1)}, bf16[32,16,128]{2,1,0:T(8,128)(2,1)S(1)}, u32[]{:S(2)}, u32[]{:S(2)}) collective-permute-start(bf16[32,16,128]{2,1,0:T(8,128)(2,1)S(1)} %copy-done.26), channel_id=1, source_target_pairs={{0,7},{1,6},{2,5},{3,4},{4,3},{5,2},{6,1},{7,0},{8,15},{9,14},{10,... | collective-permute-start | bytes 393224 | tf_op jit(solution)/shard_map/ppermute | solution.py:384
  201.9 18.9 %copy-start.25 = (bf16[32,32,128]{2,1,0:T(8,128)(2,1)S(1)}, bf16[32,32,128]{2,1,0:T(8,128)(2,1)}, u32[]{:S(2)}) copy-start(bf16[32,32,128]{2,1,0:T(8,128)(2,1)} %get-tuple-element.79) | copy-start | bytes 786436
  216.1 92.8 %copy-start.7 = (bf16[32,32,128]{2,1,0:T(8,128)(2,1)S(1)}, bf16[32,32,128]{2,1,0:T(8,128)(2,1)}, u32[]{:S(2)}) copy-start(bf16[32,32,128]{2,1,0:T(8,128)(2,1)} %get-tuple-element.67._.refs_0_) | copy-start | bytes 786436
  216.1 92.8 %copy-start.14 = (s32[9]{0:T(128)S(1)}, s32[9]{0:T(128)}, u32[]{:S(2)}) copy-start(s32[9]{0:T(128)} %pad_add_fusion.meta_ref) | copy-start | bytes 112
  216.1 110.0 %all-to-all-start.3 = ((bf16[8,32,32,128]{3,2,1,0:T(8,128)(2,1)}), bf16[8,32,32,128]{3,2,1,0:T(8,128)(2,1)}, u32[]{:S(2)}, u32[]{:S(2)}) async-start(bf16[8,32,32,128]{3,2,1,0:T(8,128)(2,1)} %get-tuple-element.89), calls=%async_computation.3 | async-start | bytes 4194304 | tf_op jit(solution)/shard_map/all_to_all | solution.py:371
  220.8 71.7 %collective-permute-start.9 = (bf16[32,32,128]{2,1,0:T(8,128)(2,1)S(1)}, bf16[32,32,128]{2,1,0:T(8,128)(2,1)S(1)}, u32[]{:S(2)}, u32[]{:S(2)}) collective-permute-start(bf16[32,32,128]{2,1,0:T(8,128)(2,1)S(1)} %copy-done.25), channel_id=1, source_target_pairs={{0,4},{1,5},{2,6},{3,7},{4,0},{5,1},{6,2},{7,3},{8,12},{9,13},{10,... | collective-permute-start | bytes 786440 | tf_op jit(solution)/shard_map/ppermute | solution.py:384
  223.5 69.1 %collective-permute-start.10 = (bf16[32,32,128]{2,1,0:T(8,128)(2,1)}, bf16[32,32,128]{2,1,0:T(8,128)(2,1)S(1)}, u32[]{:S(2)}, u32[]{:S(2)}) collective-permute-start(bf16[32,32,128]{2,1,0:T(8,128)(2,1)} %get-tuple-element.80), channel_id=1, source_target_pairs={{0,1},{1,0},{2,3},{3,2},{4,5},{5,4},{6,7},{7,6},{8,9},{9,8},{10,11... | collective-permute-start | bytes 786440 | tf_op jit(solution)/shard_map/ppermute | solution.py:384
  223.5 84.6 %collective-permute-start.11 = (bf16[32,32,128]{2,1,0:T(8,128)(2,1)}, bf16[32,32,128]{2,1,0:T(8,128)(2,1)S(1)}, u32[]{:S(2)}, u32[]{:S(2)}) collective-permute-start(bf16[32,32,128]{2,1,0:T(8,128)(2,1)} %get-tuple-element.81), channel_id=1, source_target_pairs={{0,5},{1,4},{2,7},{3,6},{4,1},{5,0},{6,3},{7,2},{8,13},{9,12},{10,... | collective-permute-start | bytes 786440 | tf_op jit(solution)/shard_map/ppermute | solution.py:384
  223.9 84.1 %collective-permute-start.12 = (bf16[32,32,128]{2,1,0:T(8,128)(2,1)}, bf16[32,32,128]{2,1,0:T(8,128)(2,1)S(1)}, u32[]{:S(2)}, u32[]{:S(2)}) collective-permute-start(bf16[32,32,128]{2,1,0:T(8,128)(2,1)} %get-tuple-element.82), channel_id=1, source_target_pairs={{0,2},{1,3},{2,0},{3,1},{4,6},{5,7},{6,4},{7,5},{8,10},{9,11},{10,... | collective-permute-start | bytes 786440 | tf_op jit(solution)/shard_map/ppermute | solution.py:384
  225.6 82.5 %collective-permute-start.13 = (bf16[32,32,128]{2,1,0:T(8,128)(2,1)}, bf16[32,32,128]{2,1,0:T(8,128)(2,1)S(1)}, u32[]{:S(2)}, u32[]{:S(2)}) collective-permute-start(bf16[32,32,128]{2,1,0:T(8,128)(2,1)} %get-tuple-element.83), channel_id=1, source_target_pairs={{0,6},{1,7},{2,4},{3,5},{4,2},{5,3},{6,0},{7,1},{8,14},{9,15},{10,... | collective-permute-start | bytes 786440 | tf_op jit(solution)/shard_map/ppermute | solution.py:384
  292.5 16.4 %collective-permute-start.14 = (bf16[32,32,128]{2,1,0:T(8,128)(2,1)}, bf16[32,32,128]{2,1,0:T(8,128)(2,1)S(1)}, u32[]{:S(2)}, u32[]{:S(2)}) collective-permute-start(bf16[32,32,128]{2,1,0:T(8,128)(2,1)} %get-tuple-element.84), channel_id=1, source_target_pairs={{0,3},{1,2},{2,1},{3,0},{4,7},{5,6},{6,5},{7,4},{8,11},{9,10},{10,... | collective-permute-start | bytes 786440 | tf_op jit(solution)/shard_map/ppermute | solution.py:384
  292.5 16.4 %collective-permute-start.15 = (bf16[32,32,128]{2,1,0:T(8,128)(2,1)}, bf16[32,32,128]{2,1,0:T(8,128)(2,1)}, u32[]{:S(2)}, u32[]{:S(2)}) collective-permute-start(bf16[32,32,128]{2,1,0:T(8,128)(2,1)} %get-tuple-element.85), channel_id=1, source_target_pairs={{0,7},{1,6},{2,5},{3,4},{4,3},{5,2},{6,1},{7,0},{8,15},{9,14},{10,... | collective-permute-start | bytes 786440 | tf_op jit(solution)/shard_map/ppermute | solution.py:384
  316.4 20.2 %copy-start.24 = (bf16[32,32,128]{2,1,0:T(8,128)(2,1)S(1)}, bf16[32,32,128]{2,1,0:T(8,128)(2,1)}, u32[]{:S(2)}) copy-start(bf16[32,32,128]{2,1,0:T(8,128)(2,1)} %get-tuple-element.93) | copy-start | bytes 786436
  316.4 66.7 %copy-start.23 = (bf16[32,32,128]{2,1,0:T(8,128)(2,1)S(1)}, bf16[32,32,128]{2,1,0:T(8,128)(2,1)}, u32[]{:S(2)}) copy-start(bf16[32,32,128]{2,1,0:T(8,128)(2,1)} %get-tuple-element.97) | copy-start | bytes 786436
  326.1 75.8 %copy-start.4 = (bf16[32,32,128]{2,1,0:T(8,128)(2,1)S(1)}, bf16[32,32,128]{2,1,0:T(8,128)(2,1)}, u32[]{:S(2)}) copy-start(bf16[32,32,128]{2,1,0:T(8,128)(2,1)} %get-tuple-element.78._.refs_0_) | copy-start | bytes 786436
  326.1 75.8 %copy-start.15 = (s32[9]{0:T(128)S(1)}, s32[9]{0:T(128)}, u32[]{:S(2)}) copy-start(s32[9]{0:T(128)} %pad_add_fusion.meta_ref) | copy-start | bytes 112
  326.1 84.5 %all-to-all-start.4 = ((bf16[8,32,16,128]{3,2,1,0:T(8,128)(2,1)}), bf16[8,32,16,128]{3,2,1,0:T(8,128)(2,1)}, u32[]{:S(2)}, u32[]{:S(2)}) async-start(bf16[8,32,16,128]{3,2,1,0:T(8,128)(2,1)} %get-tuple-element.100), calls=%async_computation.4 | async-start | bytes 2097152 | tf_op jit(solution)/shard_map/all_to_all | solution.py:371
  333.6 49.5 %collective-permute-start.16 = (bf16[32,32,128]{2,1,0:T(8,128)(2,1)}, bf16[32,32,128]{2,1,0:T(8,128)(2,1)S(1)}, u32[]{:S(2)}, u32[]{:S(2)}) collective-permute-start(bf16[32,32,128]{2,1,0:T(8,128)(2,1)} %get-tuple-element.91), channel_id=1, source_target_pairs={{0,4},{1,5},{2,6},{3,7},{4,0},{5,1},{6,2},{7,3},{8,12},{9,13},{10,... | collective-permute-start | bytes 786440 | tf_op jit(solution)/shard_map/ppermute | solution.py:384
  336.6 46.6 %collective-permute-start.17 = (bf16[32,32,128]{2,1,0:T(8,128)(2,1)}, bf16[32,32,128]{2,1,0:T(8,128)(2,1)S(1)}, u32[]{:S(2)}, u32[]{:S(2)}) collective-permute-start(bf16[32,32,128]{2,1,0:T(8,128)(2,1)} %get-tuple-element.92), channel_id=1, source_target_pairs={{0,1},{1,0},{2,3},{3,2},{4,5},{5,4},{6,7},{7,6},{8,9},{9,8},{10,11... | collective-permute-start | bytes 786440 | tf_op jit(solution)/shard_map/ppermute | solution.py:384
  336.6 62.1 %collective-permute-start.18 = (bf16[32,32,128]{2,1,0:T(8,128)(2,1)S(1)}, bf16[32,32,128]{2,1,0:T(8,128)(2,1)S(1)}, u32[]{:S(2)}, u32[]{:S(2)}) collective-permute-start(bf16[32,32,128]{2,1,0:T(8,128)(2,1)S(1)} %copy-done.24), channel_id=1, source_target_pairs={{0,5},{1,4},{2,7},{3,6},{4,1},{5,0},{6,3},{7,2},{8,13},{9,12},{10,... | collective-permute-start | bytes 786440 | tf_op jit(solution)/shard_map/ppermute | solution.py:384
  336.8 64.3 %collective-permute-start.19 = (bf16[32,32,128]{2,1,0:T(8,128)(2,1)}, bf16[32,32,128]{2,1,0:T(8,128)(2,1)S(1)}, u32[]{:S(2)}, u32[]{:S(2)}) collective-permute-start(bf16[32,32,128]{2,1,0:T(8,128)(2,1)} %get-tuple-element.94), channel_id=1, source_target_pairs={{0,2},{1,3},{2,0},{3,1},{4,6},{5,7},{6,4},{7,5},{8,10},{9,11},{10,... | collective-permute-start | bytes 786440 | tf_op jit(solution)/shard_map/ppermute | solution.py:384
  339.4 62.4 %collective-permute-start.20 = (bf16[32,32,128]{2,1,0:T(8,128)(2,1)}, bf16[32,32,128]{2,1,0:T(8,128)(2,1)}, u32[]{:S(2)}, u32[]{:S(2)}) collective-permute-start(bf16[32,32,128]{2,1,0:T(8,128)(2,1)} %get-tuple-element.95), channel_id=1, source_target_pairs={{0,6},{1,7},{2,4},{3,5},{4,2},{5,3},{6,0},{7,1},{8,14},{9,15},{10,... | collective-permute-start | bytes 786440 | tf_op jit(solution)/shard_map/ppermute | solution.py:384
  383.1 18.7 %collective-permute-start.21 = (bf16[32,32,128]{2,1,0:T(8,128)(2,1)}, bf16[32,32,128]{2,1,0:T(8,128)(2,1)}, u32[]{:S(2)}, u32[]{:S(2)}) collective-permute-start(bf16[32,32,128]{2,1,0:T(8,128)(2,1)} %get-tuple-element.96), channel_id=1, source_target_pairs={{0,3},{1,2},{2,1},{3,0},{4,7},{5,6},{6,5},{7,4},{8,11},{9,10},{10,... | collective-permute-start | bytes 786440 | tf_op jit(solution)/shard_map/ppermute | solution.py:384
  383.1 18.7 %collective-permute-start.22 = (bf16[32,32,128]{2,1,0:T(8,128)(2,1)S(1)}, bf16[32,32,128]{2,1,0:T(8,128)(2,1)}, u32[]{:S(2)}, u32[]{:S(2)}) collective-permute-start(bf16[32,32,128]{2,1,0:T(8,128)(2,1)S(1)} %copy-done.23), channel_id=1, source_target_pairs={{0,7},{1,6},{2,5},{3,4},{4,3},{5,2},{6,1},{7,0},{8,15},{9,14},{10,... | collective-permute-start | bytes 786440 | tf_op jit(solution)/shard_map/ppermute | solution.py:384
  398.7 44.1 %collective-permute-start.23 = (bf16[32,32,128]{2,1,0:T(8,128)(2,1)}, bf16[32,32,128]{2,1,0:T(8,128)(2,1)S(1)}, u32[]{:S(2)}, u32[]{:S(2)}) collective-permute-start(bf16[32,32,128]{2,1,0:T(8,128)(2,1)} %get-tuple-element.102), channel_id=1, source_target_pairs={{0,4},{1,5},{2,6},{3,7},{4,0},{5,1},{6,2},{7,3},{8,12},{9,13},{10,... | collective-permute-start | bytes 786440 | tf_op jit(solution)/shard_map/ppermute | solution.py:384
  401.8 41.3 %collective-permute-start.24 = (bf16[32,32,128]{2,1,0:T(8,128)(2,1)}, bf16[32,32,128]{2,1,0:T(8,128)(2,1)S(1)}, u32[]{:S(2)}, u32[]{:S(2)}) collective-permute-start(bf16[32,32,128]{2,1,0:T(8,128)(2,1)} %get-tuple-element.103), channel_id=1, source_target_pairs={{0,1},{1,0},{2,3},{3,2},{4,5},{5,4},{6,7},{7,6},{8,9},{9,8},{10,11... | collective-permute-start | bytes 786440 | tf_op jit(solution)/shard_map/ppermute | solution.py:384
  403.8 66.3 %copy-start.2 = (bf16[32,32,128]{2,1,0:T(8,128)(2,1)S(1)}, bf16[32,32,128]{2,1,0:T(8,128)(2,1)}, u32[]{:S(2)}) copy-start(bf16[32,32,128]{2,1,0:T(8,128)(2,1)} %get-tuple-element.90._.refs_0_) | copy-start | bytes 786436
  403.8 66.3 %copy-start.16 = (s32[9]{0:T(128)S(1)}, s32[9]{0:T(128)}, u32[]{:S(2)}) copy-start(s32[9]{0:T(128)} %pad_add_fusion.meta_ref) | copy-start | bytes 112
  417.8 21.9 %collective-permute-start.30 = (bf16[32,16,128]{2,1,0:T(8,128)(2,1)}, bf16[32,16,128]{2,1,0:T(8,128)(2,1)S(1)}, u32[]{:S(2)}, u32[]{:S(2)}) collective-permute-start(bf16[32,16,128]{2,1,0:T(8,128)(2,1)} %get-tuple-element.111), channel_id=1, source_target_pairs={{0,4},{1,5},{2,6},{3,7},{4,0},{5,1},{6,2},{7,3},{8,12},{9,13},{10,... | collective-permute-start | bytes 393224 | tf_op jit(solution)/shard_map/ppermute | solution.py:384
  427.1 12.6 %collective-permute-start.31 = (bf16[32,16,128]{2,1,0:T(8,128)(2,1)}, bf16[32,16,128]{2,1,0:T(8,128)(2,1)S(1)}, u32[]{:S(2)}, u32[]{:S(2)}) collective-permute-start(bf16[32,16,128]{2,1,0:T(8,128)(2,1)} %get-tuple-element.112), channel_id=1, source_target_pairs={{0,1},{1,0},{2,3},{3,2},{4,5},{5,4},{6,7},{7,6},{8,9},{9,8},{10,11... | collective-permute-start | bytes 393224 | tf_op jit(solution)/shard_map/ppermute | solution.py:384
  427.2 29.2 %collective-permute-start.25 = (bf16[32,32,128]{2,1,0:T(8,128)(2,1)}, bf16[32,32,128]{2,1,0:T(8,128)(2,1)S(1)}, u32[]{:S(2)}, u32[]{:S(2)}) collective-permute-start(bf16[32,32,128]{2,1,0:T(8,128)(2,1)} %get-tuple-element.104), channel_id=1, source_target_pairs={{0,5},{1,4},{2,7},{3,6},{4,1},{5,0},{6,3},{7,2},{8,13},{9,12},{10,... | collective-permute-start | bytes 786440 | tf_op jit(solution)/shard_map/ppermute | solution.py:384
  439.7 16.8 %collective-permute-start.26 = (bf16[32,32,128]{2,1,0:T(8,128)(2,1)}, bf16[32,32,128]{2,1,0:T(8,128)(2,1)S(1)}, u32[]{:S(2)}, u32[]{:S(2)}) collective-permute-start(bf16[32,32,128]{2,1,0:T(8,128)(2,1)} %get-tuple-element.105), channel_id=1, source_target_pairs={{0,2},{1,3},{2,0},{3,1},{4,6},{5,7},{6,4},{7,5},{8,10},{9,11},{10,... | collective-permute-start | bytes 786440 | tf_op jit(solution)/shard_map/ppermute | solution.py:384
  440.4 17.0 %collective-permute-start.27 = (bf16[32,32,128]{2,1,0:T(8,128)(2,1)}, bf16[32,32,128]{2,1,0:T(8,128)(2,1)}, u32[]{:S(2)}, u32[]{:S(2)}) collective-permute-start(bf16[32,32,128]{2,1,0:T(8,128)(2,1)} %get-tuple-element.106), channel_id=1, source_target_pairs={{0,6},{1,7},{2,4},{3,5},{4,2},{5,3},{6,0},{7,1},{8,14},{9,15},{10,... | collective-permute-start | bytes 786440 | tf_op jit(solution)/shard_map/ppermute | solution.py:384
  442.8 24.8 %collective-permute-start.28 = (bf16[32,32,128]{2,1,0:T(8,128)(2,1)}, bf16[32,32,128]{2,1,0:T(8,128)(2,1)}, u32[]{:S(2)}, u32[]{:S(2)}) collective-permute-start(bf16[32,32,128]{2,1,0:T(8,128)(2,1)} %get-tuple-element.107), channel_id=1, source_target_pairs={{0,3},{1,2},{2,1},{3,0},{4,7},{5,6},{6,5},{7,4},{8,11},{9,10},{10,... | collective-permute-start | bytes 786440 | tf_op jit(solution)/shard_map/ppermute | solution.py:384
  443.1 24.5 %collective-permute-start.29 = (bf16[32,32,128]{2,1,0:T(8,128)(2,1)}, bf16[32,32,128]{2,1,0:T(8,128)(2,1)}, u32[]{:S(2)}, u32[]{:S(2)}) collective-permute-start(bf16[32,32,128]{2,1,0:T(8,128)(2,1)} %get-tuple-element.108), channel_id=1, source_target_pairs={{0,7},{1,6},{2,5},{3,4},{4,3},{5,2},{6,1},{7,0},{8,15},{9,14},{10,... | collective-permute-start | bytes 786440 | tf_op jit(solution)/shard_map/ppermute | solution.py:384
  456.4 20.8 %collective-permute-start.32 = (bf16[32,16,128]{2,1,0:T(8,128)(2,1)}, bf16[32,16,128]{2,1,0:T(8,128)(2,1)S(1)}, u32[]{:S(2)}, u32[]{:S(2)}) collective-permute-start(bf16[32,16,128]{2,1,0:T(8,128)(2,1)} %get-tuple-element.113), channel_id=1, source_target_pairs={{0,5},{1,4},{2,7},{3,6},{4,1},{5,0},{6,3},{7,2},{8,13},{9,12},{10,... | collective-permute-start | bytes 393224 | tf_op jit(solution)/shard_map/ppermute | solution.py:384
  456.5 20.7 %collective-permute-start.33 = (bf16[32,16,128]{2,1,0:T(8,128)(2,1)}, bf16[32,16,128]{2,1,0:T(8,128)(2,1)S(1)}, u32[]{:S(2)}, u32[]{:S(2)}) collective-permute-start(bf16[32,16,128]{2,1,0:T(8,128)(2,1)} %get-tuple-element.114), channel_id=1, source_target_pairs={{0,2},{1,3},{2,0},{3,1},{4,6},{5,7},{6,4},{7,5},{8,10},{9,11},{10,... | collective-permute-start | bytes 393224 | tf_op jit(solution)/shard_map/ppermute | solution.py:384
  457.3 19.9 %collective-permute-start.34 = (bf16[32,16,128]{2,1,0:T(8,128)(2,1)}, bf16[32,16,128]{2,1,0:T(8,128)(2,1)S(1)}, u32[]{:S(2)}, u32[]{:S(2)}) collective-permute-start(bf16[32,16,128]{2,1,0:T(8,128)(2,1)} %get-tuple-element.115), channel_id=1, source_target_pairs={{0,6},{1,7},{2,4},{3,5},{4,2},{5,3},{6,0},{7,1},{8,14},{9,15},{10,... | collective-permute-start | bytes 393224 | tf_op jit(solution)/shard_map/ppermute | solution.py:384
  467.7 13.9 %collective-permute-start.35 = (bf16[32,16,128]{2,1,0:T(8,128)(2,1)}, bf16[32,16,128]{2,1,0:T(8,128)(2,1)S(1)}, u32[]{:S(2)}, u32[]{:S(2)}) collective-permute-start(bf16[32,16,128]{2,1,0:T(8,128)(2,1)} %get-tuple-element.116), channel_id=1, source_target_pairs={{0,3},{1,2},{2,1},{3,0},{4,7},{5,6},{6,5},{7,4},{8,11},{9,10},{10,... | collective-permute-start | bytes 393224 | tf_op jit(solution)/shard_map/ppermute | solution.py:384
  467.7 13.9 %collective-permute-start.36 = (bf16[32,16,128]{2,1,0:T(8,128)(2,1)}, bf16[32,16,128]{2,1,0:T(8,128)(2,1)S(1)}, u32[]{:S(2)}, u32[]{:S(2)}) collective-permute-start(bf16[32,16,128]{2,1,0:T(8,128)(2,1)} %get-tuple-element.117), channel_id=1, source_target_pairs={{0,7},{1,6},{2,5},{3,4},{4,3},{5,2},{6,1},{7,0},{8,15},{9,14},{10,... | collective-permute-start | bytes 393224 | tf_op jit(solution)/shard_map/ppermute | solution.py:384
  471.0 10.6 %copy-start.11 = (bf16[32,16,128]{2,1,0:T(8,128)(2,1)S(1)}, bf16[32,16,128]{2,1,0:T(8,128)(2,1)}, u32[]{:S(2)}) copy-start(bf16[32,16,128]{2,1,0:T(8,128)(2,1)} %copy-done.10) | copy-start | bytes 393220
  (11 other events, 8.7 us)

commit v14 on v12

--- a/solution.py
+++ b/solution.py
@@ -405,9 +405,13 @@
 
 def chunks_of(receivers):
     if receivers == 128:
-        return [(16, 0), (32, 1), (32, 2), (32, 3), (16, 1)]
+        return [(16, 0), (16, 1), (32, 1), (32, 2), (16, 6), (16, 7)]
     rows = min(16, receivers)
     return [(rows, index) for index in range(receivers // rows)]
+
+
+def summed(energy):
+    return lax.psum(jnp.sum(energy, axis=1), "patch")
 
 
 def direct(estimate, observed, delays, thresholds):
@@ -443,6 +447,8 @@
             last = power
             energy = energy + power
             ahead[turn] = exchanged(spectra)
+            if turn == len(chunks) - 1:
+                energy = last = summed(energy)
         place = turn - lag
         if place in ahead:
             shrunk = shrunk_of(meta, ahead.pop(place), table, levels, last)
@@ -505,7 +511,7 @@
     table = jnp.asarray(shot_table(delays.shape[0]))
     level = lax.dynamic_slice_in_dim(thresholds, rank * share, share)
     stepped = jnp.concatenate(parts, axis=1)
-    return spectral_by_einsum(stepped, forward, inverse, table, level, peers), energy
+    return spectral_by_einsum(stepped, forward, inverse, table, level, peers), summed(energy)
 
 
 def local(estimate, observed, random_source_delays, thresholds):
@@ -514,10 +520,7 @@
     filled = peers >= 4 and peers & (peers - 1) == 0 and (2 * F // peers) % LANES == 0
     path = direct if filled else by_einsum
     updated, energy = path(estimate, observed, random_source_delays, thresholds)
-    misfit = lax.psum(jnp.sum(energy, axis=1), "patch") / (
-        receivers * lax.axis_size("patch") * samples
-    )
-    return updated, misfit
+    return updated, energy / (receivers * lax.axis_size("patch") * samples)
 
 
 def solution(mesh):

time: 433 us -> 439 us (1.014)
  starting transfers between devices: 95.6 us -> 140 us
  waiting for transfers between devices: 150 us -> 112 us
  Pallas kernels: 148 us -> 153 us
  local copies, waits for them, and re-layouts: 23.2 us -> 18.8 us
    ppermute x70 -> x84, starting transfers between devices: 91.9 us -> 136 us  [exchanged(): lax.ppermute(arrays[slot], 'shot', [(i, i ^ slot) for i in range(peers)])]
    ppermute x70 -> x84, waiting for transfers between devices: 147 us -> 108 us  [exchanged(): lax.ppermute(arrays[slot], 'shot', [(i, i ^ slot) for i in range(peers)])]
    pallas_call x5 -> x6, Pallas kernels: 64.5 us -> 69.4 us  [spectra_of(): pl.pallas_call(spectra_kernel, grid_spec=pltpu.PrefetchScalarGridSpec(num...]
    unnamed x114 -> x132, local copies, waits for them, and re-layouts: 19.5 us -> 15.1 us
    pallas_call x5 -> x6, Pallas kernels: 24.5 us -> 25.1 us  [updated_of(): pl.pallas_call(functools.partial(update_kernel, len(restored)), grid_spec...]
    pallas_call x5 -> x6, Pallas kernels: 58.6 us -> 58.5 us  [shrunk_of(): pl.pallas_call(shots_kernel, grid_spec=pltpu.PrefetchScalarGridSpec(num_s...]
  transfers between devices with their start and end apart: 72 -> 86, of which waited for: 20 -> 14; matrix products, arithmetic and copies ran while one was open for 1% -> 1% of each run, Pallas kernels for 30% -> 32%
where the time goes in v14:
time: 439 us; the launch traced here: 438 us
  Pallas kernels  153 us (35%)
  starting transfers between devices  140 us (32%)
  waiting for transfers between devices  112 us (26%)
  local copies, waits for them, and re-layouts  18.8 us (4%)
  blocking collectives  10.4 us (2%)
    ppermute x84, starting transfers between devices, exchanged(): lax.ppermute(arrays[slot], 'shot', [(i, i ^ slot) for i in range(peers)])  136 us
    ppermute x84, waiting for transfers between devices, exchanged(): lax.ppermute(arrays[slot], 'shot', [(i, i ^ slot) for i in range(peers)])  108 us
    pallas_call x6, Pallas kernels, spectra_of(): pl.pallas_call(spectra_kernel, grid_spec=pltpu.PrefetchScalarGridSpec(num...  69.4 us
    pallas_call x6, Pallas kernels, shrunk_of(): pl.pallas_call(shots_kernel, grid_spec=pltpu.PrefetchScalarGridSpec(num_s...  58.5 us
    pallas_call x6, Pallas kernels, updated_of(): pl.pallas_call(functools.partial(update_kernel, len(restored)), grid_spec...  25.1 us
    unnamed x132, local copies, waits for them, and re-layouts  15.1 us
    psum x1, blocking collectives, summed(): return lax.psum(jnp.sum(energy, axis=1), 'patch')  10.4 us
  transfers between devices with their start and end apart: 86, of which 14 were waited for; matrix products, arithmetic and copies ran while one was open for 1% of the time, Pallas kernels for 32%

profile of v14, /device:TPU:0, one launch (start us, length us, event | category | flops | bytes accessed | tf_op | source)
XLA Modules:
  0.0 438.0 jit_solution(3595976305102341836)
XLA Ops:
  3.1 2.4 collective-permute-start
  9.7 3.2 collective-permute-done.1.after_ref
  13.8 9.8 %spectra.6 = (bf16[32,16,128]{2,1,0:T(8,128)(2,1)}, bf16[32,16,128]{2,1,0:T(8,128)(2,1)}, bf16[32,16,128]{2,1,0:T(8,128)(2,1)}, bf16[32,16,128]{2,1,0:T(8,128)(2...) custom-call(s32[9]{0:T(128)} %pad_add_fusion.meta_ref, ...), custom_call_target="tpu_custom_call" | custom-call | flops 1073741824 | bytes 5242880 | tf_op jit(solution)/shard_map/spectra/pallas_call | solution.py:270
  23.7 10.5 %collective-permute-start.2 = (bf16[32,16,128]{2,1,0:T(8,128)(2,1)}, bf16[32,16,128]{2,1,0:T(8,128)(2,1)S(1)}, u32[]{:S(2)}, u32[]{:S(2)}) collective-permute-start(bf16[32,16,128]{2,1,0:T(8,128)(2,1)} %get-tuple-element.118), channel_id=1, source_target_pairs={{0,4},{1,5},{2,6},{3,7},{4,0},{5,1},{6,2},{7,3},{8,12},{9,13},{10,... | collective-permute-start | bytes 393224 | tf_op jit(solution)/shard_map/ppermute | solution.py:392
  37.1 2.5 collective-permute-start.6
  39.6 3.6 collective-permute-done.2.refs_1_
  43.3 9.9 %spectra.7 = (bf16[32,16,128]{2,1,0:T(8,128)(2,1)}, bf16[32,16,128]{2,1,0:T(8,128)(2,1)}, bf16[32,16,128]{2,1,0:T(8,128)(2,1)}, bf16[32,16,128]{2,1,0:T(8,128)(2...) custom-call(s32[9]{0:T(128)} %pad_add_fusion.meta_ref, ...), custom_call_target="tpu_custom_call" | custom-call | flops 1073741824 | bytes 5242880 | tf_op jit(solution)/shard_map/spectra/pallas_call | solution.py:270
  53.2 3.2 collective-permute-start.9
  56.4 2.8 collective-permute-start.10
  59.2 2.1 collective-permute-start.11
  63.4 7.3 %shrink.6 = (bf16[32,16,128]{2,1,0:T(8,128)(2,1)}, bf16[32,16,128]{2,1,0:T(8,128)(2,1)}, bf16[32,16,128]{2,1,0:T(8,128)(2,1)}, bf16[32,16,128]{2,1,0:T(8,128)(2,...) custom-call(s32[9]{0:T(128)} %pad_add_fusion.meta_ref, ...), custom_call_target="tpu_custom_call" | custom-call | flops 1073741824 | bytes 2359296 | tf_op jit(solution)/shard_map/shrink/pallas_call | solution.py:320
  71.2 2.3 collective-permute-start.15
  74.5 2.9 collective-permute-start.18
  77.5 14.7 %spectra.8 = (bf16[32,32,128]{2,1,0:T(8,128)(2,1)}, bf16[32,32,128]{2,1,0:T(8,128)(2,1)}, bf16[32,32,128]{2,1,0:T(8,128)(2,1)}, bf16[32,32,128]{2,1,0:T(8,128)(2...) custom-call(s32[9]{0:T(128)} %pad_add_fusion.meta_ref, ...), custom_call_target="tpu_custom_call" | custom-call | flops 2147483648 | bytes 8388608 | tf_op jit(solution)/shard_map/spectra/pallas_call | solution.py:270
  93.9 2.0 collective-permute-start.20
  96.1 7.3 %shrink.7 = (bf16[32,16,128]{2,1,0:T(8,128)(2,1)}, bf16[32,16,128]{2,1,0:T(8,128)(2,1)}, bf16[32,16,128]{2,1,0:T(8,128)(2,1)}, bf16[32,16,128]{2,1,0:T(8,128)(2,...) custom-call(s32[9]{0:T(128)} %pad_add_fusion.meta_ref, ...), custom_call_target="tpu_custom_call" | custom-call | flops 1073741824 | bytes 2359296 | tf_op jit(solution)/shard_map/shrink/pallas_call | solution.py:320
  103.4 2.3 collective-permute-start.22
  106.6 2.1 collective-permute-start.32
  110.3 13.7 %collective-permute-start.33 = (bf16[32,16,128]{2,1,0:T(8,128)(2,1)}, bf16[32,16,128]{2,1,0:T(8,128)(2,1)S(1)}, u32[]{:S(2)}, u32[]{:S(2)}) collective-permute-start(bf16[32,16,128]{2,1,0:T(8,128)(2,1)} %get-tuple-element.157), channel_id=1, source_target_pairs={{0,2},{1,3},{2,0},{3,1},{4,6},{5,7},{6,4},{7,5},{8,10},{9,11},{10,... | collective-permute-start | bytes 393224 | tf_op jit(solution)/shard_map/ppermute | solution.py:392
  124.0 3.9 collective-permute-done.30.refs_1_
  127.9 1.8 collective-permute-start.34
  129.7 2.2 collective-permute-start.36
  132.0 11.5 %collective-permute-done.33.refs_4_ = bf16[32,16,128]{2,1,0:T(8,128)(2,1)S(1)} collective-permute-done((bf16[32,16,128]{2,1,0:T(8,128)(2,1)}, bf16[32,16,128]{2,1,0:T(8,128)(2,1)S(1)}, u32[]{:S(2)}, u32[]{:S(2)}) %collective-permute-start.33) | collective-permute-done | bytes 131104 | tf_op jit(solution)/shard_map/ppermute | solution.py:392
  145.4 3.2 update.6
  148.6 2.4 collective-permute-start.26
  151.1 2.0 collective-permute-start.27
  153.1 15.0 %spectra.9 = (bf16[32,32,128]{2,1,0:T(8,128)(2,1)}, bf16[32,32,128]{2,1,0:T(8,128)(2,1)}, bf16[32,32,128]{2,1,0:T(8,128)(2,1)}, bf16[32,32,128]{2,1,0:T(8,128)(2...) custom-call(s32[9]{0:T(128)} %pad_add_fusion.meta_ref, ...), custom_call_target="tpu_custom_call" | custom-call | flops 2147483648 | bytes 8388608 | tf_op jit(solution)/shard_map/spectra/pallas_call | solution.py:270
  169.2 2.2 collective-permute-start.37
  173.0 7.9 %collective-permute-done.28.refs_6_ = bf16[32,32,128]{2,1,0:T(8,128)(2,1)} collective-permute-done((bf16[32,32,128]{2,1,0:T(8,128)(2,1)}, bf16[32,32,128]{2,1,0:T(8,128)(2,1)}, u32[]{:S(2)}, u32[]{:S(2)}) %collective-permute-start.28) | collective-permute-done | bytes 262176 | tf_op jit(solution)/shard_map/ppermute | solution.py:392
  180.9 2.1 collective-permute-start.41
  183.0 23.5 %collective-permute-done.37.refs_1_ = bf16[32,32,128]{2,1,0:T(8,128)(2,1)S(1)} collective-permute-done((bf16[32,32,128]{2,1,0:T(8,128)(2,1)}, bf16[32,32,128]{2,1,0:T(8,128)(2,1)S(1)}, u32[]{:S(2)}, u32[]{:S(2)}) %collective-permute-start.37) | collective-permute-done | bytes 262176 | tf_op jit(solution)/shard_map/ppermute | solution.py:392
  206.5 14.7 %shrink.8 = (bf16[32,32,128]{2,1,0:T(8,128)(2,1)}, bf16[32,32,128]{2,1,0:T(8,128)(2,1)}, bf16[32,32,128]{2,1,0:T(8,128)(2,1)}, bf16[32,32,128]{2,1,0:T(8,128)(2,...) custom-call(s32[9]{0:T(128)} %pad_add_fusion.meta_ref, ...), custom_call_target="tpu_custom_call" | custom-call | flops 2147483648 | bytes 4456448 | tf_op jit(solution)/shard_map/shrink/pallas_call | solution.py:320
  222.1 2.4 collective-permute-start.44
  225.5 3.2 update.7
  229.3 10.0 %spectra.10 = (bf16[32,16,128]{2,1,0:T(8,128)(2,1)}, bf16[32,16,128]{2,1,0:T(8,128)(2,1)}, bf16[32,16,128]{2,1,0:T(8,128)(2,1)}, bf16[32,16,128]{2,1,0:T(8,128)(...) custom-call(s32[9]{0:T(128)} %pad_add_fusion.meta_ref, ...), custom_call_target="tpu_custom_call" | custom-call | flops 1073741824 | bytes 5242880 | tf_op jit(solution)/shard_map/spectra/pallas_call | solution.py:270
  240.8 2.5 collective-permute-start.46
  243.3 16.2 %collective-permute-done.51.refs_1_ = bf16[32,16,128]{2,1,0:T(8,128)(2,1)S(1)} collective-permute-done((bf16[32,16,128]{2,1,0:T(8,128)(2,1)}, bf16[32,16,128]{2,1,0:T(8,128)(2,1)S(1)}, u32[]{:S(2)}, u32[]{:S(2)}) %collective-permute-start.51) | collective-permute-done | bytes 131104 | tf_op jit(solution)/shard_map/ppermute | solution.py:392
  260.8 2.0 collective-permute-start.48
  262.8 2.7 collective-permute-start.50
  265.5 14.7 %shrink.9 = (bf16[32,32,128]{2,1,0:T(8,128)(2,1)}, bf16[32,32,128]{2,1,0:T(8,128)(2,1)}, bf16[32,32,128]{2,1,0:T(8,128)(2,1)}, bf16[32,32,128]{2,1,0:T(8,128)(2,...) custom-call(s32[9]{0:T(128)} %pad_add_fusion.meta_ref, ...), custom_call_target="tpu_custom_call" | custom-call | flops 2147483648 | bytes 4456448 | tf_op jit(solution)/shard_map/shrink/pallas_call | solution.py:320
  281.8 1.8 collective-permute-start.55
  283.6 2.5 collective-permute-done.49.refs_6_
  286.1 2.4 collective-permute-start.57
  289.5 5.9 %update.8 = (f32[32,128,1024]{2,1,0:T(8,128)}, f32[8,128]{1,0:T(8,128)S(1)}) custom-call(s32[9]{0:T(128)S(1)} %copy-done.15, bf16[1024,1024]{1,0:T(8,128)(2,1)S(1)} %copy-done, bf16[32,32,128]{2,1,0:T(8,128)(2,1)S(1)} %copy-done.1, bf16[32,32,128]{2,1,0:T(8,128)(2,1)S(1)} %copy-done.4, ...), custom_call_target="tpu_custom_call", output_to_operand_aliasing={{0}: (11, {})} | custom-call | flops 2147483648 | bytes 8388608 | tf_op jit(solution)/shard_map/update/pallas_call | solution.py:351
  296.0 10.0 %spectra.11 = (bf16[32,16,128]{2,1,0:T(8,128)(2,1)}, bf16[32,16,128]{2,1,0:T(8,128)(2,1)}, bf16[32,16,128]{2,1,0:T(8,128)(2,1)}, bf16[32,16,128]{2,1,0:T(8,128)(...) custom-call(s32[9]{0:T(128)} %pad_add_fusion.meta_ref, ...), custom_call_target="tpu_custom_call" | custom-call | flops 1073741824 | bytes 5242880 | tf_op jit(solution)/shard_map/spectra/pallas_call | solution.py:270
  306.0 6.8 %collective-permute-start.65 = (bf16[32,16,128]{2,1,0:T(8,128)(2,1)}, bf16[32,16,128]{2,1,0:T(8,128)(2,1)S(1)}, u32[]{:S(2)}, u32[]{:S(2)}) collective-permute-start(bf16[32,16,128]{2,1,0:T(8,128)(2,1)} %get-tuple-element.202), channel_id=1, source_target_pairs={{0,4},{1,5},{2,6},{3,7},{4,0},{5,1},{6,2},{7,3},{8,12},{9,13},{10,... | collective-permute-start | bytes 393224 | tf_op jit(solution)/shard_map/ppermute | solution.py:392
  313.1 2.8 collective-permute-start.58
  315.9 13.7 %collective-permute-done.65.refs_1_ = bf16[32,16,128]{2,1,0:T(8,128)(2,1)S(1)} collective-permute-done((bf16[32,16,128]{2,1,0:T(8,128)(2,1)}, bf16[32,16,128]{2,1,0:T(8,128)(2,1)S(1)}, u32[]{:S(2)}, u32[]{:S(2)}) %collective-permute-start.65) | collective-permute-done | bytes 131104 | tf_op jit(solution)/shard_map/ppermute | solution.py:392
  329.6 2.3 collective-permute-start.69
  331.9 9.3 %collective-permute-done.68.refs_4_ = bf16[32,16,128]{2,1,0:T(8,128)(2,1)S(1)} collective-permute-done((bf16[32,16,128]{2,1,0:T(8,128)(2,1)}, bf16[32,16,128]{2,1,0:T(8,128)(2,1)S(1)}, u32[]{:S(2)}, u32[]{:S(2)}) %collective-permute-start.68) | collective-permute-done | bytes 131104 | tf_op jit(solution)/shard_map/ppermute | solution.py:392
  342.0 2.0 collective-permute-start.62
  344.4 2.6 collective-permute-start.64
  347.9 10.4 %psum.7._ = f32[32]{0:T(128)} all-reduce(f32[32]{0:T(128)S(1)} %add_reduce_fusion), channel_id=1, replica_groups=mesh['patch'=4,'shot'=8] {'patch'}, use_global_device_ids=true, to_apply=%region_1.0 | all-reduce | flops 32 | bytes 256 | tf_op jit(solution)/shard_map/psum | solution.py:414
  358.3 7.4 %shrink.10 = (bf16[32,16,128]{2,1,0:T(8,128)(2,1)}, bf16[32,16,128]{2,1,0:T(8,128)(2,1)}, bf16[32,16,128]{2,1,0:T(8,128)(2,1)}, bf16[32,16,128]{2,1,0:T(8,128)(2...) custom-call(s32[9]{0:T(128)} %pad_add_fusion.meta_ref, ...), custom_call_target="tpu_custom_call" | custom-call | flops 1073741824 | bytes 2359296 | tf_op jit(solution)/shard_map/shrink/pallas_call | solution.py:320
  367.8 11.3 %collective-permute-start.74 = (bf16[32,16,128]{2,1,0:T(8,128)(2,1)}, bf16[32,16,128]{2,1,0:T(8,128)(2,1)S(1)}, u32[]{:S(2)}, u32[]{:S(2)}) collective-permute-start(bf16[32,16,128]{2,1,0:T(8,128)(2,1)} %get-tuple-element.212), channel_id=1, source_target_pairs={{0,5},{1,4},{2,7},{3,6},{4,1},{5,0},{6,3},{7,2},{8,13},{9,12},{10,... | collective-permute-start | bytes 393224 | tf_op jit(solution)/shard_map/ppermute | solution.py:392
  379.1 8.3 %collective-permute-start.75 = (bf16[32,16,128]{2,1,0:T(8,128)(2,1)}, bf16[32,16,128]{2,1,0:T(8,128)(2,1)S(1)}, u32[]{:S(2)}, u32[]{:S(2)}) collective-permute-start(bf16[32,16,128]{2,1,0:T(8,128)(2,1)} %get-tuple-element.213), channel_id=1, source_target_pairs={{0,2},{1,3},{2,0},{3,1},{4,6},{5,7},{6,4},{7,5},{8,10},{9,11},{10,... | collective-permute-start | bytes 393224 | tf_op jit(solution)/shard_map/ppermute | solution.py:392
  388.3 6.2 %update.9 = (f32[32,128,1024]{2,1,0:T(8,128)}, f32[8,128]{1,0:T(8,128)S(1)}) custom-call(s32[9]{0:T(128)S(1)} %copy-done.16, bf16[1024,1024]{1,0:T(8,128)(2,1)S(1)} %copy-done, bf16[32,16,128]{2,1,0:T(8,128)(2,1)S(1)} %copy-done.5, bf16[32,32,128]{2,1,0:T(8,128)(2,1)S(1)} %copy-done.2, ...), custom_call_target="tpu_custom_call", output_to_operand_aliasing={{0}: (11, {})} | custom-call | flops 2147483648 | bytes 8388608 | tf_op jit(solution)/shard_map/update/pallas_call | solution.py:351
  395.8 2.0 collective-permute-start.76
  397.8 7.2 %shrink.11 = (bf16[32,16,128]{2,1,0:T(8,128)(2,1)}, bf16[32,16,128]{2,1,0:T(8,128)(2,1)}, bf16[32,16,128]{2,1,0:T(8,128)(2,1)}, bf16[32,16,128]{2,1,0:T(8,128)(2...) custom-call(s32[9]{0:T(128)} %pad_add_fusion.meta_ref, ...), custom_call_target="tpu_custom_call" | custom-call | flops 1073741824 | bytes 2359296 | tf_op jit(solution)/shard_map/shrink/pallas_call | solution.py:320
  405.8 2.6 collective-permute-start.79
  413.2 1.8 collective-permute-start.83
  415.0 11.9 %collective-permute-done.79.refs_1_ = bf16[32,16,128]{2,1,0:T(8,128)(2,1)S(1)} collective-permute-done((bf16[32,16,128]{2,1,0:T(8,128)(2,1)}, bf16[32,16,128]{2,1,0:T(8,128)(2,1)S(1)}, u32[]{:S(2)}, u32[]{:S(2)}) %collective-permute-start.79) | collective-permute-done | bytes 131104 | tf_op jit(solution)/shard_map/ppermute | solution.py:392
  430.0 3.2 update.10
  434.8 3.2 update.11
  (270 shorter events, 48.4 us)
Async XLA Ops:
  23.7 19.5 %collective-permute-start.2 = (bf16[32,16,128]{2,1,0:T(8,128)(2,1)}, bf16[32,16,128]{2,1,0:T(8,128)(2,1)S(1)}, u32[]{:S(2)}, u32[]{:S(2)}) collective-permute-start(bf16[32,16,128]{2,1,0:T(8,128)(2,1)} %get-tuple-element.118), channel_id=1, source_target_pairs={{0,4},{1,5},{2,6},{3,7},{4,0},{5,1},{6,2},{7,3},{8,12},{9,13},{10,... | collective-permute-start | bytes 393224 | tf_op jit(solution)/shard_map/ppermute | solution.py:392
  35.6 17.6 %collective-permute-start.4 = (bf16[32,16,128]{2,1,0:T(8,128)(2,1)}, bf16[32,16,128]{2,1,0:T(8,128)(2,1)S(1)}, u32[]{:S(2)}, u32[]{:S(2)}) collective-permute-start(bf16[32,16,128]{2,1,0:T(8,128)(2,1)} %get-tuple-element.120), channel_id=1, source_target_pairs={{0,5},{1,4},{2,7},{3,6},{4,1},{5,0},{6,3},{7,2},{8,13},{9,12},{10,... | collective-permute-start | bytes 393224 | tf_op jit(solution)/shard_map/ppermute | solution.py:392
  35.7 20.7 %collective-permute-start.5 = (bf16[32,16,128]{2,1,0:T(8,128)(2,1)}, bf16[32,16,128]{2,1,0:T(8,128)(2,1)S(1)}, u32[]{:S(2)}, u32[]{:S(2)}) collective-permute-start(bf16[32,16,128]{2,1,0:T(8,128)(2,1)} %get-tuple-element.121), channel_id=1, source_target_pairs={{0,2},{1,3},{2,0},{3,1},{4,6},{5,7},{6,4},{7,5},{8,10},{9,11},{10,... | collective-permute-start | bytes 393224 | tf_op jit(solution)/shard_map/ppermute | solution.py:392
  37.1 22.1 %collective-permute-start.6 = (bf16[32,16,128]{2,1,0:T(8,128)(2,1)}, bf16[32,16,128]{2,1,0:T(8,128)(2,1)S(1)}, u32[]{:S(2)}, u32[]{:S(2)}) collective-permute-start(bf16[32,16,128]{2,1,0:T(8,128)(2,1)} %get-tuple-element.122), channel_id=1, source_target_pairs={{0,6},{1,7},{2,4},{3,5},{4,2},{5,3},{6,0},{7,1},{8,14},{9,15},{10,... | collective-permute-start | bytes 393224 | tf_op jit(solution)/shard_map/ppermute | solution.py:392
  43.2 18.1 %collective-permute-start.7 = (bf16[32,16,128]{2,1,0:T(8,128)(2,1)}, bf16[32,16,128]{2,1,0:T(8,128)(2,1)S(1)}, u32[]{:S(2)}, u32[]{:S(2)}) collective-permute-start(bf16[32,16,128]{2,1,0:T(8,128)(2,1)} %get-tuple-element.123), channel_id=1, source_target_pairs={{0,3},{1,2},{2,1},{3,0},{4,7},{5,6},{6,5},{7,4},{8,11},{9,10},{10,... | collective-permute-start | bytes 393224 | tf_op jit(solution)/shard_map/ppermute | solution.py:392
  43.2 19.5 %collective-permute-start.8 = (bf16[32,16,128]{2,1,0:T(8,128)(2,1)}, bf16[32,16,128]{2,1,0:T(8,128)(2,1)S(1)}, u32[]{:S(2)}, u32[]{:S(2)}) collective-permute-start(bf16[32,16,128]{2,1,0:T(8,128)(2,1)} %get-tuple-element.124), channel_id=1, source_target_pairs={{0,7},{1,6},{2,5},{3,4},{4,3},{5,2},{6,1},{7,0},{8,15},{9,14},{10,... | collective-permute-start | bytes 393224 | tf_op jit(solution)/shard_map/ppermute | solution.py:392
  53.2 17.5 %collective-permute-start.9 = (bf16[32,16,128]{2,1,0:T(8,128)(2,1)}, bf16[32,16,128]{2,1,0:T(8,128)(2,1)S(1)}, u32[]{:S(2)}, u32[]{:S(2)}) collective-permute-start(bf16[32,16,128]{2,1,0:T(8,128)(2,1)} %get-tuple-element.128), channel_id=1, source_target_pairs={{0,4},{1,5},{2,6},{3,7},{4,0},{5,1},{6,2},{7,3},{8,12},{9,13},{10,... | collective-permute-start | bytes 393224 | tf_op jit(solution)/shard_map/ppermute | solution.py:392
  70.7 21.5 %collective-permute-start.14 = (bf16[32,16,128]{2,1,0:T(8,128)(2,1)}, bf16[32,16,128]{2,1,0:T(8,128)(2,1)S(1)}, u32[]{:S(2)}, u32[]{:S(2)}) collective-permute-start(bf16[32,16,128]{2,1,0:T(8,128)(2,1)} %get-tuple-element.133), channel_id=1, source_target_pairs={{0,3},{1,2},{2,1},{3,0},{4,7},{5,6},{6,5},{7,4},{8,11},{9,10},{10,... | collective-permute-start | bytes 393224 | tf_op jit(solution)/shard_map/ppermute | solution.py:392
  71.2 22.1 %collective-permute-start.15 = (bf16[32,16,128]{2,1,0:T(8,128)(2,1)}, bf16[32,16,128]{2,1,0:T(8,128)(2,1)S(1)}, u32[]{:S(2)}, u32[]{:S(2)}) collective-permute-start(bf16[32,16,128]{2,1,0:T(8,128)(2,1)} %get-tuple-element.134), channel_id=1, source_target_pairs={{0,7},{1,6},{2,5},{3,4},{4,3},{5,2},{6,1},{7,0},{8,15},{9,14},{10,... | collective-permute-start | bytes 393224 | tf_op jit(solution)/shard_map/ppermute | solution.py:392
  74.4 21.5 %collective-permute-start.16 = (bf16[32,16,128]{2,1,0:T(8,128)(2,1)}, bf16[32,16,128]{2,1,0:T(8,128)(2,1)S(1)}, u32[]{:S(2)}, u32[]{:S(2)}) collective-permute-start(bf16[32,16,128]{2,1,0:T(8,128)(2,1)} %get-tuple-element.136), channel_id=1, source_target_pairs={{0,4},{1,5},{2,6},{3,7},{4,0},{5,1},{6,2},{7,3},{8,12},{9,13},{10,... | collective-permute-start | bytes 393224 | tf_op jit(solution)/shard_map/ppermute | solution.py:392
  74.4 28.9 %collective-permute-start.17 = (bf16[32,16,128]{2,1,0:T(8,128)(2,1)}, bf16[32,16,128]{2,1,0:T(8,128)(2,1)S(1)}, u32[]{:S(2)}, u32[]{:S(2)}) collective-permute-start(bf16[32,16,128]{2,1,0:T(8,128)(2,1)} %get-tuple-element.137), channel_id=1, source_target_pairs={{0,1},{1,0},{2,3},{3,2},{4,5},{5,4},{6,7},{7,6},{8,9},{9,8},{10,11... | collective-permute-start | bytes 393224 | tf_op jit(solution)/shard_map/ppermute | solution.py:392
  74.5 31.1 %collective-permute-start.18 = (bf16[32,16,128]{2,1,0:T(8,128)(2,1)}, bf16[32,16,128]{2,1,0:T(8,128)(2,1)S(1)}, u32[]{:S(2)}, u32[]{:S(2)}) collective-permute-start(bf16[32,16,128]{2,1,0:T(8,128)(2,1)} %get-tuple-element.138), channel_id=1, source_target_pairs={{0,5},{1,4},{2,7},{3,6},{4,1},{5,0},{6,3},{7,2},{8,13},{9,12},{10,... | collective-permute-start | bytes 393224 | tf_op jit(solution)/shard_map/ppermute | solution.py:392
  105.7 22.3 %collective-permute-start.30 = (bf16[32,16,128]{2,1,0:T(8,128)(2,1)}, bf16[32,16,128]{2,1,0:T(8,128)(2,1)S(1)}, u32[]{:S(2)}, u32[]{:S(2)}) collective-permute-start(bf16[32,16,128]{2,1,0:T(8,128)(2,1)} %get-tuple-element.154), channel_id=1, source_target_pairs={{0,4},{1,5},{2,6},{3,7},{4,0},{5,1},{6,2},{7,3},{8,12},{9,13},{10,... | collective-permute-start | bytes 393224 | tf_op jit(solution)/shard_map/ppermute | solution.py:392
  106.6 23.1 %collective-permute-start.31 = (bf16[32,16,128]{2,1,0:T(8,128)(2,1)}, bf16[32,16,128]{2,1,0:T(8,128)(2,1)S(1)}, u32[]{:S(2)}, u32[]{:S(2)}) collective-permute-start(bf16[32,16,128]{2,1,0:T(8,128)(2,1)} %get-tuple-element.155), channel_id=1, source_target_pairs={{0,1},{1,0},{2,3},{3,2},{4,5},{5,4},{6,7},{7,6},{8,9},{9,8},{10,11... | collective-permute-start | bytes 393224 | tf_op jit(solution)/shard_map/ppermute | solution.py:392
  106.6 23.1 %collective-permute-start.32 = (bf16[32,16,128]{2,1,0:T(8,128)(2,1)}, bf16[32,16,128]{2,1,0:T(8,128)(2,1)S(1)}, u32[]{:S(2)}, u32[]{:S(2)}) collective-permute-start(bf16[32,16,128]{2,1,0:T(8,128)(2,1)} %get-tuple-element.156), channel_id=1, source_target_pairs={{0,5},{1,4},{2,7},{3,6},{4,1},{5,0},{6,3},{7,2},{8,13},{9,12},{10,... | collective-permute-start | bytes 393224 | tf_op jit(solution)/shard_map/ppermute | solution.py:392
  109.4 43.7 %collective-permute-start.23 = (bf16[32,32,128]{2,1,0:T(8,128)(2,1)}, bf16[32,32,128]{2,1,0:T(8,128)(2,1)}, u32[]{:S(2)}, u32[]{:S(2)}) collective-permute-start(bf16[32,32,128]{2,1,0:T(8,128)(2,1)} %get-tuple-element.146), channel_id=1, source_target_pairs={{0,4},{1,5},{2,6},{3,7},{4,0},{5,1},{6,2},{7,3},{8,12},{9,13},{10,... | collective-permute-start | bytes 786440 | tf_op jit(solution)/shard_map/ppermute | solution.py:392
  110.3 33.1 %collective-permute-start.33 = (bf16[32,16,128]{2,1,0:T(8,128)(2,1)}, bf16[32,16,128]{2,1,0:T(8,128)(2,1)S(1)}, u32[]{:S(2)}, u32[]{:S(2)}) collective-permute-start(bf16[32,16,128]{2,1,0:T(8,128)(2,1)} %get-tuple-element.157), channel_id=1, source_target_pairs={{0,2},{1,3},{2,0},{3,1},{4,6},{5,7},{6,4},{7,5},{8,10},{9,11},{10,... | collective-permute-start | bytes 393224 | tf_op jit(solution)/shard_map/ppermute | solution.py:392
  129.7 18.9 %collective-permute-start.35 = (bf16[32,16,128]{2,1,0:T(8,128)(2,1)}, bf16[32,16,128]{2,1,0:T(8,128)(2,1)S(1)}, u32[]{:S(2)}, u32[]{:S(2)}) collective-permute-start(bf16[32,16,128]{2,1,0:T(8,128)(2,1)} %get-tuple-element.159), channel_id=1, source_target_pairs={{0,3},{1,2},{2,1},{3,0},{4,7},{5,6},{6,5},{7,4},{8,11},{9,10},{10,... | collective-permute-start | bytes 393224 | tf_op jit(solution)/shard_map/ppermute | solution.py:392
  129.7 21.3 %collective-permute-start.36 = (bf16[32,16,128]{2,1,0:T(8,128)(2,1)}, bf16[32,16,128]{2,1,0:T(8,128)(2,1)S(1)}, u32[]{:S(2)}, u32[]{:S(2)}) collective-permute-start(bf16[32,16,128]{2,1,0:T(8,128)(2,1)} %get-tuple-element.160), channel_id=1, source_target_pairs={{0,7},{1,6},{2,5},{3,4},{4,3},{5,2},{6,1},{7,0},{8,15},{9,14},{10,... | collective-permute-start | bytes 393224 | tf_op jit(solution)/shard_map/ppermute | solution.py:392
  143.4 24.6 %collective-permute-start.24 = (bf16[32,32,128]{2,1,0:T(8,128)(2,1)}, bf16[32,32,128]{2,1,0:T(8,128)(2,1)}, u32[]{:S(2)}, u32[]{:S(2)}) collective-permute-start(bf16[32,32,128]{2,1,0:T(8,128)(2,1)} %get-tuple-element.147), channel_id=1, source_target_pairs={{0,1},{1,0},{2,3},{3,2},{4,5},{5,4},{6,7},{7,6},{8,9},{9,8},{10,11... | collective-permute-start | bytes 786440 | tf_op jit(solution)/shard_map/ppermute | solution.py:392
  143.6 25.6 %collective-permute-start.25 = (bf16[32,32,128]{2,1,0:T(8,128)(2,1)}, bf16[32,32,128]{2,1,0:T(8,128)(2,1)}, u32[]{:S(2)}, u32[]{:S(2)}) collective-permute-start(bf16[32,32,128]{2,1,0:T(8,128)(2,1)} %get-tuple-element.148), channel_id=1, source_target_pairs={{0,5},{1,4},{2,7},{3,6},{4,1},{5,0},{6,3},{7,2},{8,13},{9,12},{10,... | collective-permute-start | bytes 786440 | tf_op jit(solution)/shard_map/ppermute | solution.py:392
  148.6 22.7 %collective-permute-start.26 = (bf16[32,32,128]{2,1,0:T(8,128)(2,1)}, bf16[32,32,128]{2,1,0:T(8,128)(2,1)S(1)}, u32[]{:S(2)}, u32[]{:S(2)}) collective-permute-start(bf16[32,32,128]{2,1,0:T(8,128)(2,1)} %get-tuple-element.149), channel_id=1, source_target_pairs={{0,2},{1,3},{2,0},{3,1},{4,6},{5,7},{6,4},{7,5},{8,10},{9,11},{10,... | collective-permute-start | bytes 786440 | tf_op jit(solution)/shard_map/ppermute | solution.py:392
  151.1 21.0 %collective-permute-start.27 = (bf16[32,32,128]{2,1,0:T(8,128)(2,1)}, bf16[32,32,128]{2,1,0:T(8,128)(2,1)}, u32[]{:S(2)}, u32[]{:S(2)}) collective-permute-start(bf16[32,32,128]{2,1,0:T(8,128)(2,1)} %get-tuple-element.150), channel_id=1, source_target_pairs={{0,6},{1,7},{2,4},{3,5},{4,2},{5,3},{6,0},{7,1},{8,14},{9,15},{10,... | collective-permute-start | bytes 786440 | tf_op jit(solution)/shard_map/ppermute | solution.py:392
  153.1 27.8 %collective-permute-start.28 = (bf16[32,32,128]{2,1,0:T(8,128)(2,1)}, bf16[32,32,128]{2,1,0:T(8,128)(2,1)}, u32[]{:S(2)}, u32[]{:S(2)}) collective-permute-start(bf16[32,32,128]{2,1,0:T(8,128)(2,1)} %get-tuple-element.151), channel_id=1, source_target_pairs={{0,3},{1,2},{2,1},{3,0},{4,7},{5,6},{6,5},{7,4},{8,11},{9,10},{10,... | collective-permute-start | bytes 786440 | tf_op jit(solution)/shard_map/ppermute | solution.py:392
  169.2 37.4 %collective-permute-start.37 = (bf16[32,32,128]{2,1,0:T(8,128)(2,1)}, bf16[32,32,128]{2,1,0:T(8,128)(2,1)S(1)}, u32[]{:S(2)}, u32[]{:S(2)}) collective-permute-start(bf16[32,32,128]{2,1,0:T(8,128)(2,1)} %get-tuple-element.165), channel_id=1, source_target_pairs={{0,4},{1,5},{2,6},{3,7},{4,0},{5,1},{6,2},{7,3},{8,12},{9,13},{10,... | collective-permute-start | bytes 786440 | tf_op jit(solution)/shard_map/ppermute | solution.py:392
  172.0 49.2 %collective-permute-start.38 = (bf16[32,32,128]{2,1,0:T(8,128)(2,1)}, bf16[32,32,128]{2,1,0:T(8,128)(2,1)S(1)}, u32[]{:S(2)}, u32[]{:S(2)}) collective-permute-start(bf16[32,32,128]{2,1,0:T(8,128)(2,1)} %get-tuple-element.166), channel_id=1, source_target_pairs={{0,1},{1,0},{2,3},{3,2},{4,5},{5,4},{6,7},{7,6},{8,9},{9,8},{10,11... | collective-permute-start | bytes 786440 | tf_op jit(solution)/shard_map/ppermute | solution.py:392
  172.1 50.0 %collective-permute-start.39 = (bf16[32,32,128]{2,1,0:T(8,128)(2,1)}, bf16[32,32,128]{2,1,0:T(8,128)(2,1)}, u32[]{:S(2)}, u32[]{:S(2)}) collective-permute-start(bf16[32,32,128]{2,1,0:T(8,128)(2,1)} %get-tuple-element.167), channel_id=1, source_target_pairs={{0,5},{1,4},{2,7},{3,6},{4,1},{5,0},{6,3},{7,2},{8,13},{9,12},{10,... | collective-permute-start | bytes 786440 | tf_op jit(solution)/shard_map/ppermute | solution.py:392
  180.9 43.6 %collective-permute-start.40 = (bf16[32,32,128]{2,1,0:T(8,128)(2,1)}, bf16[32,32,128]{2,1,0:T(8,128)(2,1)}, u32[]{:S(2)}, u32[]{:S(2)}) collective-permute-start(bf16[32,32,128]{2,1,0:T(8,128)(2,1)} %get-tuple-element.168), channel_id=1, source_target_pairs={{0,2},{1,3},{2,0},{3,1},{4,6},{5,7},{6,4},{7,5},{8,10},{9,11},{10,... | collective-permute-start | bytes 786440 | tf_op jit(solution)/shard_map/ppermute | solution.py:392
  180.9 58.4 %collective-permute-start.41 = (bf16[32,32,128]{2,1,0:T(8,128)(2,1)}, bf16[32,32,128]{2,1,0:T(8,128)(2,1)}, u32[]{:S(2)}, u32[]{:S(2)}) collective-permute-start(bf16[32,32,128]{2,1,0:T(8,128)(2,1)} %get-tuple-element.169), channel_id=1, source_target_pairs={{0,6},{1,7},{2,4},{3,5},{4,2},{5,3},{6,0},{7,1},{8,14},{9,15},{10,... | collective-permute-start | bytes 786440 | tf_op jit(solution)/shard_map/ppermute | solution.py:392
  206.5 34.2 %collective-permute-start.42 = (bf16[32,32,128]{2,1,0:T(8,128)(2,1)}, bf16[32,32,128]{2,1,0:T(8,128)(2,1)}, u32[]{:S(2)}, u32[]{:S(2)}) collective-permute-start(bf16[32,32,128]{2,1,0:T(8,128)(2,1)} %get-tuple-element.170), channel_id=1, source_target_pairs={{0,3},{1,2},{2,1},{3,0},{4,7},{5,6},{6,5},{7,4},{8,11},{9,10},{10,... | collective-permute-start | bytes 786440 | tf_op jit(solution)/shard_map/ppermute | solution.py:392
  221.2 19.5 %collective-permute-start.43 = (bf16[32,32,128]{2,1,0:T(8,128)(2,1)}, bf16[32,32,128]{2,1,0:T(8,128)(2,1)}, u32[]{:S(2)}, u32[]{:S(2)}) collective-permute-start(bf16[32,32,128]{2,1,0:T(8,128)(2,1)} %get-tuple-element.171), channel_id=1, source_target_pairs={{0,7},{1,6},{2,5},{3,4},{4,3},{5,2},{6,1},{7,0},{8,15},{9,14},{10,... | collective-permute-start | bytes 786440 | tf_op jit(solution)/shard_map/ppermute | solution.py:392
  222.1 40.7 %collective-permute-start.44 = (bf16[32,32,128]{2,1,0:T(8,128)(2,1)}, bf16[32,32,128]{2,1,0:T(8,128)(2,1)S(1)}, u32[]{:S(2)}, u32[]{:S(2)}) collective-permute-start(bf16[32,32,128]{2,1,0:T(8,128)(2,1)} %get-tuple-element.173), channel_id=1, source_target_pairs={{0,4},{1,5},{2,6},{3,7},{4,0},{5,1},{6,2},{7,3},{8,12},{9,13},{10,... | collective-permute-start | bytes 786440 | tf_op jit(solution)/shard_map/ppermute | solution.py:392
  224.5 38.3 %collective-permute-start.45 = (bf16[32,32,128]{2,1,0:T(8,128)(2,1)}, bf16[32,32,128]{2,1,0:T(8,128)(2,1)S(1)}, u32[]{:S(2)}, u32[]{:S(2)}) collective-permute-start(bf16[32,32,128]{2,1,0:T(8,128)(2,1)} %get-tuple-element.174), channel_id=1, source_target_pairs={{0,1},{1,0},{2,3},{3,2},{4,5},{5,4},{6,7},{7,6},{8,9},{9,8},{10,11... | collective-permute-start | bytes 786440 | tf_op jit(solution)/shard_map/ppermute | solution.py:392
  239.3 20.2 %collective-permute-start.51 = (bf16[32,16,128]{2,1,0:T(8,128)(2,1)}, bf16[32,16,128]{2,1,0:T(8,128)(2,1)S(1)}, u32[]{:S(2)}, u32[]{:S(2)}) collective-permute-start(bf16[32,16,128]{2,1,0:T(8,128)(2,1)} %get-tuple-element.184), channel_id=1, source_target_pairs={{0,4},{1,5},{2,6},{3,7},{4,0},{5,1},{6,2},{7,3},{8,12},{9,13},{10,... | collective-permute-start | bytes 393224 | tf_op jit(solution)/shard_map/ppermute | solution.py:392
  240.8 19.4 %collective-permute-start.52 = (bf16[32,16,128]{2,1,0:T(8,128)(2,1)}, bf16[32,16,128]{2,1,0:T(8,128)(2,1)S(1)}, u32[]{:S(2)}, u32[]{:S(2)}) collective-permute-start(bf16[32,16,128]{2,1,0:T(8,128)(2,1)} %get-tuple-element.185), channel_id=1, source_target_pairs={{0,1},{1,0},{2,3},{3,2},{4,5},{5,4},{6,7},{7,6},{8,9},{9,8},{10,11... | collective-permute-start | bytes 393224 | tf_op jit(solution)/shard_map/ppermute | solution.py:392
  240.8 39.5 %collective-permute-start.46 = (bf16[32,32,128]{2,1,0:T(8,128)(2,1)}, bf16[32,32,128]{2,1,0:T(8,128)(2,1)S(1)}, u32[]{:S(2)}, u32[]{:S(2)}) collective-permute-start(bf16[32,32,128]{2,1,0:T(8,128)(2,1)} %get-tuple-element.175), channel_id=1, source_target_pairs={{0,5},{1,4},{2,7},{3,6},{4,1},{5,0},{6,3},{7,2},{8,13},{9,12},{10,... | collective-permute-start | bytes 786440 | tf_op jit(solution)/shard_map/ppermute | solution.py:392
  260.2 20.1 %collective-permute-start.47 = (bf16[32,32,128]{2,1,0:T(8,128)(2,1)}, bf16[32,32,128]{2,1,0:T(8,128)(2,1)S(1)}, u32[]{:S(2)}, u32[]{:S(2)}) collective-permute-start(bf16[32,32,128]{2,1,0:T(8,128)(2,1)} %get-tuple-element.176), channel_id=1, source_target_pairs={{0,2},{1,3},{2,0},{3,1},{4,6},{5,7},{6,4},{7,5},{8,10},{9,11},{10,... | collective-permute-start | bytes 786440 | tf_op jit(solution)/shard_map/ppermute | solution.py:392
  260.8 21.0 %collective-permute-start.48 = (bf16[32,32,128]{2,1,0:T(8,128)(2,1)}, bf16[32,32,128]{2,1,0:T(8,128)(2,1)S(1)}, u32[]{:S(2)}, u32[]{:S(2)}) collective-permute-start(bf16[32,32,128]{2,1,0:T(8,128)(2,1)} %get-tuple-element.177), channel_id=1, source_target_pairs={{0,6},{1,7},{2,4},{3,5},{4,2},{5,3},{6,0},{7,1},{8,14},{9,15},{10,... | collective-permute-start | bytes 786440 | tf_op jit(solution)/shard_map/ppermute | solution.py:392
  262.8 23.3 %collective-permute-start.49 = (bf16[32,32,128]{2,1,0:T(8,128)(2,1)}, bf16[32,32,128]{2,1,0:T(8,128)(2,1)S(1)}, u32[]{:S(2)}, u32[]{:S(2)}) collective-permute-start(bf16[32,32,128]{2,1,0:T(8,128)(2,1)} %get-tuple-element.178), channel_id=1, source_target_pairs={{0,3},{1,2},{2,1},{3,0},{4,7},{5,6},{6,5},{7,4},{8,11},{9,10},{10,... | collective-permute-start | bytes 786440 | tf_op jit(solution)/shard_map/ppermute | solution.py:392
  262.8 23.3 %collective-permute-start.50 = (bf16[32,32,128]{2,1,0:T(8,128)(2,1)}, bf16[32,32,128]{2,1,0:T(8,128)(2,1)}, u32[]{:S(2)}, u32[]{:S(2)}) collective-permute-start(bf16[32,32,128]{2,1,0:T(8,128)(2,1)} %get-tuple-element.179), channel_id=1, source_target_pairs={{0,7},{1,6},{2,5},{3,4},{4,3},{5,2},{6,1},{7,0},{8,15},{9,14},{10,... | collective-permute-start | bytes 786440 | tf_op jit(solution)/shard_map/ppermute | solution.py:392
  280.2 25.8 %collective-permute-start.53 = (bf16[32,16,128]{2,1,0:T(8,128)(2,1)}, bf16[32,16,128]{2,1,0:T(8,128)(2,1)}, u32[]{:S(2)}, u32[]{:S(2)}) collective-permute-start(bf16[32,16,128]{2,1,0:T(8,128)(2,1)} %get-tuple-element.186), channel_id=1, source_target_pairs={{0,5},{1,4},{2,7},{3,6},{4,1},{5,0},{6,3},{7,2},{8,13},{9,12},{10,... | collective-permute-start | bytes 393224 | tf_op jit(solution)/shard_map/ppermute | solution.py:392
  280.3 32.6 %collective-permute-start.54 = (bf16[32,16,128]{2,1,0:T(8,128)(2,1)}, bf16[32,16,128]{2,1,0:T(8,128)(2,1)}, u32[]{:S(2)}, u32[]{:S(2)}) collective-permute-start(bf16[32,16,128]{2,1,0:T(8,128)(2,1)} %get-tuple-element.187), channel_id=1, source_target_pairs={{0,2},{1,3},{2,0},{3,1},{4,6},{5,7},{6,4},{7,5},{8,10},{9,11},{10,... | collective-permute-start | bytes 393224 | tf_op jit(solution)/shard_map/ppermute | solution.py:392
  281.8 31.1 %collective-permute-start.55 = (bf16[32,16,128]{2,1,0:T(8,128)(2,1)}, bf16[32,16,128]{2,1,0:T(8,128)(2,1)}, u32[]{:S(2)}, u32[]{:S(2)}) collective-permute-start(bf16[32,16,128]{2,1,0:T(8,128)(2,1)} %get-tuple-element.188), channel_id=1, source_target_pairs={{0,6},{1,7},{2,4},{3,5},{4,2},{5,3},{6,0},{7,1},{8,14},{9,15},{10,... | collective-permute-start | bytes 393224 | tf_op jit(solution)/shard_map/ppermute | solution.py:392
  286.1 27.0 %collective-permute-start.56 = (bf16[32,16,128]{2,1,0:T(8,128)(2,1)}, bf16[32,16,128]{2,1,0:T(8,128)(2,1)}, u32[]{:S(2)}, u32[]{:S(2)}) collective-permute-start(bf16[32,16,128]{2,1,0:T(8,128)(2,1)} %get-tuple-element.189), channel_id=1, source_target_pairs={{0,3},{1,2},{2,1},{3,0},{4,7},{5,6},{6,5},{7,4},{8,11},{9,10},{10,... | collective-permute-start | bytes 393224 | tf_op jit(solution)/shard_map/ppermute | solution.py:392
  286.1 29.8 %collective-permute-start.57 = (bf16[32,16,128]{2,1,0:T(8,128)(2,1)}, bf16[32,16,128]{2,1,0:T(8,128)(2,1)}, u32[]{:S(2)}, u32[]{:S(2)}) collective-permute-start(bf16[32,16,128]{2,1,0:T(8,128)(2,1)} %get-tuple-element.190), channel_id=1, source_target_pairs={{0,7},{1,6},{2,5},{3,4},{4,3},{5,2},{6,1},{7,0},{8,15},{9,14},{10,... | collective-permute-start | bytes 393224 | tf_op jit(solution)/shard_map/ppermute | solution.py:392
  306.0 23.6 %collective-permute-start.65 = (bf16[32,16,128]{2,1,0:T(8,128)(2,1)}, bf16[32,16,128]{2,1,0:T(8,128)(2,1)S(1)}, u32[]{:S(2)}, u32[]{:S(2)}) collective-permute-start(bf16[32,16,128]{2,1,0:T(8,128)(2,1)} %get-tuple-element.202), channel_id=1, source_target_pairs={{0,4},{1,5},{2,6},{3,7},{4,0},{5,1},{6,2},{7,3},{8,12},{9,13},{10,... | collective-permute-start | bytes 393224 | tf_op jit(solution)/shard_map/ppermute | solution.py:392
  312.9 19.1 %collective-permute-start.67 = (bf16[32,16,128]{2,1,0:T(8,128)(2,1)}, bf16[32,16,128]{2,1,0:T(8,128)(2,1)S(1)}, u32[]{:S(2)}, u32[]{:S(2)}) collective-permute-start(bf16[32,16,128]{2,1,0:T(8,128)(2,1)} %get-tuple-element.204), channel_id=1, source_target_pairs={{0,5},{1,4},{2,7},{3,6},{4,1},{5,0},{6,3},{7,2},{8,13},{9,12},{10,... | collective-permute-start | bytes 393224 | tf_op jit(solution)/shard_map/ppermute | solution.py:392
  313.1 30.9 %collective-permute-start.58 = (bf16[32,32,128]{2,1,0:T(8,128)(2,1)S(1)}, bf16[32,32,128]{2,1,0:T(8,128)(2,1)S(1)}, u32[]{:S(2)}, u32[]{:S(2)}) collective-permute-start(bf16[32,32,128]{2,1,0:T(8,128)(2,1)S(1)} %copy-done.34), channel_id=1, source_target_pairs={{0,4},{1,5},{2,6},{3,7},{4,0},{5,1},{6,2},{7,3},{8,12},{9,13},{10,... | collective-permute-start | bytes 786440 | tf_op jit(solution)/shard_map/ppermute | solution.py:392
  315.9 28.5 %collective-permute-start.59 = (bf16[32,32,128]{2,1,0:T(8,128)(2,1)S(1)}, bf16[32,32,128]{2,1,0:T(8,128)(2,1)S(1)}, u32[]{:S(2)}, u32[]{:S(2)}) collective-permute-start(bf16[32,32,128]{2,1,0:T(8,128)(2,1)S(1)} %copy-done.32), channel_id=1, source_target_pairs={{0,1},{1,0},{2,3},{3,2},{4,5},{5,4},{6,7},{7,6},{8,9},{9,8},{10,11... | collective-permute-start | bytes 786440 | tf_op jit(solution)/shard_map/ppermute | solution.py:392
  341.2 24.5 %collective-permute-start.60 = (bf16[32,32,128]{2,1,0:T(8,128)(2,1)}, bf16[32,32,128]{2,1,0:T(8,128)(2,1)S(1)}, u32[]{:S(2)}, u32[]{:S(2)}) collective-permute-start(bf16[32,32,128]{2,1,0:T(8,128)(2,1)} %get-tuple-element.194), channel_id=1, source_target_pairs={{0,5},{1,4},{2,7},{3,6},{4,1},{5,0},{6,3},{7,2},{8,13},{9,12},{10,... | collective-permute-start | bytes 786440 | tf_op jit(solution)/shard_map/ppermute | solution.py:392
  341.9 23.9 %collective-permute-start.61 = (bf16[32,32,128]{2,1,0:T(8,128)(2,1)}, bf16[32,32,128]{2,1,0:T(8,128)(2,1)S(1)}, u32[]{:S(2)}, u32[]{:S(2)}) collective-permute-start(bf16[32,32,128]{2,1,0:T(8,128)(2,1)} %get-tuple-element.195), channel_id=1, source_target_pairs={{0,2},{1,3},{2,0},{3,1},{4,6},{5,7},{6,4},{7,5},{8,10},{9,11},{10,... | collective-permute-start | bytes 786440 | tf_op jit(solution)/shard_map/ppermute | solution.py:392
  342.0 24.4 %collective-permute-start.62 = (bf16[32,32,128]{2,1,0:T(8,128)(2,1)}, bf16[32,32,128]{2,1,0:T(8,128)(2,1)}, u32[]{:S(2)}, u32[]{:S(2)}) collective-permute-start(bf16[32,32,128]{2,1,0:T(8,128)(2,1)} %get-tuple-element.196), channel_id=1, source_target_pairs={{0,6},{1,7},{2,4},{3,5},{4,2},{5,3},{6,0},{7,1},{8,14},{9,15},{10,... | collective-permute-start | bytes 786440 | tf_op jit(solution)/shard_map/ppermute | solution.py:392
  344.0 23.8 %collective-permute-start.63 = (bf16[32,32,128]{2,1,0:T(8,128)(2,1)}, bf16[32,32,128]{2,1,0:T(8,128)(2,1)}, u32[]{:S(2)}, u32[]{:S(2)}) collective-permute-start(bf16[32,32,128]{2,1,0:T(8,128)(2,1)} %get-tuple-element.197), channel_id=1, source_target_pairs={{0,3},{1,2},{2,1},{3,0},{4,7},{5,6},{6,5},{7,4},{8,11},{9,10},{10,... | collective-permute-start | bytes 786440 | tf_op jit(solution)/shard_map/ppermute | solution.py:392
  344.4 34.7 %collective-permute-start.64 = (bf16[32,32,128]{2,1,0:T(8,128)(2,1)}, bf16[32,32,128]{2,1,0:T(8,128)(2,1)}, u32[]{:S(2)}, u32[]{:S(2)}) collective-permute-start(bf16[32,32,128]{2,1,0:T(8,128)(2,1)} %get-tuple-element.198), channel_id=1, source_target_pairs={{0,7},{1,6},{2,5},{3,4},{4,3},{5,2},{6,1},{7,0},{8,15},{9,14},{10,... | collective-permute-start | bytes 786440 | tf_op jit(solution)/shard_map/ppermute | solution.py:392
  365.7 29.4 %collective-permute-start.71 = (bf16[32,16,128]{2,1,0:T(8,128)(2,1)}, bf16[32,16,128]{2,1,0:T(8,128)(2,1)S(1)}, u32[]{:S(2)}, u32[]{:S(2)}) collective-permute-start(bf16[32,16,128]{2,1,0:T(8,128)(2,1)} %get-tuple-element.208), channel_id=1, source_target_pairs={{0,7},{1,6},{2,5},{3,4},{4,3},{5,2},{6,1},{7,0},{8,15},{9,14},{10,... | collective-permute-start | bytes 393224 | tf_op jit(solution)/shard_map/ppermute | solution.py:392
  365.8 39.3 %collective-permute-start.72 = (bf16[32,16,128]{2,1,0:T(8,128)(2,1)}, bf16[32,16,128]{2,1,0:T(8,128)(2,1)S(1)}, u32[]{:S(2)}, u32[]{:S(2)}) collective-permute-start(bf16[32,16,128]{2,1,0:T(8,128)(2,1)} %get-tuple-element.210), channel_id=1, source_target_pairs={{0,4},{1,5},{2,6},{3,7},{4,0},{5,1},{6,2},{7,3},{8,12},{9,13},{10,... | collective-permute-start | bytes 393224 | tf_op jit(solution)/shard_map/ppermute | solution.py:392
  366.4 38.7 %collective-permute-start.73 = (bf16[32,16,128]{2,1,0:T(8,128)(2,1)}, bf16[32,16,128]{2,1,0:T(8,128)(2,1)S(1)}, u32[]{:S(2)}, u32[]{:S(2)}) collective-permute-start(bf16[32,16,128]{2,1,0:T(8,128)(2,1)} %get-tuple-element.211), channel_id=1, source_target_pairs={{0,1},{1,0},{2,3},{3,2},{4,5},{5,4},{6,7},{7,6},{8,9},{9,8},{10,11... | collective-permute-start | bytes 393224 | tf_op jit(solution)/shard_map/ppermute | solution.py:392
  367.8 38.0 %collective-permute-start.74 = (bf16[32,16,128]{2,1,0:T(8,128)(2,1)}, bf16[32,16,128]{2,1,0:T(8,128)(2,1)S(1)}, u32[]{:S(2)}, u32[]{:S(2)}) collective-permute-start(bf16[32,16,128]{2,1,0:T(8,128)(2,1)} %get-tuple-element.212), channel_id=1, source_target_pairs={{0,5},{1,4},{2,7},{3,6},{4,1},{5,0},{6,3},{7,2},{8,13},{9,12},{10,... | collective-permute-start | bytes 393224 | tf_op jit(solution)/shard_map/ppermute | solution.py:392
  379.1 29.2 %collective-permute-start.75 = (bf16[32,16,128]{2,1,0:T(8,128)(2,1)}, bf16[32,16,128]{2,1,0:T(8,128)(2,1)S(1)}, u32[]{:S(2)}, u32[]{:S(2)}) collective-permute-start(bf16[32,16,128]{2,1,0:T(8,128)(2,1)} %get-tuple-element.213), channel_id=1, source_target_pairs={{0,2},{1,3},{2,0},{3,1},{4,6},{5,7},{6,4},{7,5},{8,10},{9,11},{10,... | collective-permute-start | bytes 393224 | tf_op jit(solution)/shard_map/ppermute | solution.py:392
  405.8 21.1 %collective-permute-start.79 = (bf16[32,16,128]{2,1,0:T(8,128)(2,1)}, bf16[32,16,128]{2,1,0:T(8,128)(2,1)S(1)}, u32[]{:S(2)}, u32[]{:S(2)}) collective-permute-start(bf16[32,16,128]{2,1,0:T(8,128)(2,1)} %get-tuple-element.219), channel_id=1, source_target_pairs={{0,4},{1,5},{2,6},{3,7},{4,0},{5,1},{6,2},{7,3},{8,12},{9,13},{10,... | collective-permute-start | bytes 393224 | tf_op jit(solution)/shard_map/ppermute | solution.py:392
  409.0 17.9 %collective-permute-start.80 = (bf16[32,16,128]{2,1,0:T(8,128)(2,1)}, bf16[32,16,128]{2,1,0:T(8,128)(2,1)S(1)}, u32[]{:S(2)}, u32[]{:S(2)}) collective-permute-start(bf16[32,16,128]{2,1,0:T(8,128)(2,1)} %get-tuple-element.220), channel_id=1, source_target_pairs={{0,1},{1,0},{2,3},{3,2},{4,5},{5,4},{6,7},{7,6},{8,9},{9,8},{10,11... | collective-permute-start | bytes 393224 | tf_op jit(solution)/shard_map/ppermute | solution.py:392
  409.0 24.2 %collective-permute-start.81 = (bf16[32,16,128]{2,1,0:T(8,128)(2,1)}, bf16[32,16,128]{2,1,0:T(8,128)(2,1)S(1)}, u32[]{:S(2)}, u32[]{:S(2)}) collective-permute-start(bf16[32,16,128]{2,1,0:T(8,128)(2,1)} %get-tuple-element.221), channel_id=1, source_target_pairs={{0,5},{1,4},{2,7},{3,6},{4,1},{5,0},{6,3},{7,2},{8,13},{9,12},{10,... | collective-permute-start | bytes 393224 | tf_op jit(solution)/shard_map/ppermute | solution.py:392
  410.1 23.2 %collective-permute-start.82 = (bf16[32,16,128]{2,1,0:T(8,128)(2,1)}, bf16[32,16,128]{2,1,0:T(8,128)(2,1)S(1)}, u32[]{:S(2)}, u32[]{:S(2)}) collective-permute-start(bf16[32,16,128]{2,1,0:T(8,128)(2,1)} %get-tuple-element.222), channel_id=1, source_target_pairs={{0,2},{1,3},{2,0},{3,1},{4,6},{5,7},{6,4},{7,5},{8,10},{9,11},{10,... | collective-permute-start | bytes 393224 | tf_op jit(solution)/shard_map/ppermute | solution.py:392
  413.2 20.1 %collective-permute-start.83 = (bf16[32,16,128]{2,1,0:T(8,128)(2,1)}, bf16[32,16,128]{2,1,0:T(8,128)(2,1)S(1)}, u32[]{:S(2)}, u32[]{:S(2)}) collective-permute-start(bf16[32,16,128]{2,1,0:T(8,128)(2,1)} %get-tuple-element.223), channel_id=1, source_target_pairs={{0,6},{1,7},{2,4},{3,5},{4,2},{5,3},{6,0},{7,1},{8,14},{9,15},{10,... | collective-permute-start | bytes 393224 | tf_op jit(solution)/shard_map/ppermute | solution.py:392
  (88 other events, 1982.8 us)

commit v15 on v11

--- a/solution.py
+++ b/solution.py
@@ -380,10 +380,8 @@
 
 
 def slots_of(peers):
-    order = [0]
-    for slot in range(peers // 2):
-        order += [peers // 2 + slot] + ([slot + 1] if slot + 1 < peers // 2 else [])
-    return order
+    half = peers // 2
+    return [0, *range(1, min(3, half)), *range(half, peers), *range(3, half)]
 
 
 def exchanged(arrays):
@@ -426,7 +424,7 @@
     last, updated, energy = levels, None, 0.0
     lag = 2
     ahead, behind = {}, {}
-    for turn in range(len(chunks) + 2 * lag):
+    for turn in range(len(chunks) + lag + 1):
         if turn < len(chunks):
             rows, index = chunks[turn]
             spectra, power = spectra_of(
@@ -448,7 +446,7 @@
             shrunk = shrunk_of(meta, ahead.pop(place), table, levels, last)
             last = shrunk[0]
             behind[place] = exchanged(shrunk)
-        place = turn - 2 * lag
+        place = turn - lag - 1
         if place in behind:
             updated, last = updated_of(
                 meta, behind.pop(place), inverse, chunks[place][1], receivers, updated, last

time: 433 us -> 459 us (1.060)
  starting transfers between devices: 160 us -> 188 us
  waiting for transfers between devices: 75.1 us -> 88.5 us
  local copies, waits for them, and re-layouts: 26.2 us -> 15.8 us
    ppermute x84, starting transfers between devices: 157 us -> 184 us  [exchanged(): lax.ppermute(arrays[slot], 'shot', [(i, i ^ slot) for i in range(peers)])]
    ppermute x84, waiting for transfers between devices: 72.1 us -> 85.5 us  [exchanged(): lax.ppermute(arrays[slot], 'shot', [(i, i ^ slot) for i in range(peers)])]
    unnamed x178 -> x158, local copies, waits for them, and re-layouts: 22.5 us -> 12.1 us
  transfers between devices with their start and end apart: 86 -> 86, of which waited for: 18 -> 18; matrix products, arithmetic and copies ran while one was open for 1% -> 1% of each run, Pallas kernels for 33% -> 28%
where the time goes in v15:
time: 459 us; the launch traced here: 457 us
  starting transfers between devices  188 us (41%)
  Pallas kernels  153 us (33%)
  waiting for transfers between devices  88.5 us (19%)
  local copies, waits for them, and re-layouts  15.8 us (3%)
  blocking collectives  9.9 us (2%)
    ppermute x84, starting transfers between devices, exchanged(): lax.ppermute(arrays[slot], 'shot', [(i, i ^ slot) for i in range(peers)])  184 us
    ppermute x84, waiting for transfers between devices, exchanged(): lax.ppermute(arrays[slot], 'shot', [(i, i ^ slot) for i in range(peers)])  85.5 us
    pallas_call x6, Pallas kernels, spectra_of(): pl.pallas_call(spectra_kernel, grid_spec=pltpu.PrefetchScalarGridSpec(num...  69.4 us
    pallas_call x6, Pallas kernels, shrunk_of(): pl.pallas_call(shots_kernel, grid_spec=pltpu.PrefetchScalarGridSpec(num_s...  58.5 us
    pallas_call x6, Pallas kernels, updated_of(): pl.pallas_call(functools.partial(update_kernel, len(restored)), grid_spec...  24.7 us
    unnamed x158, local copies, waits for them, and re-layouts  12.1 us
    psum x1, blocking collectives, local(): lax.psum(jnp.sum(energy, axis=1), 'patch')  9.9 us
  transfers between devices with their start and end apart: 86, of which 18 were waited for; matrix products, arithmetic and copies ran while one was open for 1% of the time, Pallas kernels for 28%

profile of v15, /device:TPU:0, one launch (start us, length us, event | category | flops | bytes accessed | tf_op | source)
XLA Modules:
  0.0 457.1 jit_solution(4379152113064950503)
XLA Ops:
  3.1 2.4 collective-permute-start
  8.9 3.0 collective-permute-done.1.after_ref
  12.8 9.8 %spectra.6 = (bf16[32,16,128]{2,1,0:T(8,128)(2,1)}, bf16[32,16,128]{2,1,0:T(8,128)(2,1)}, bf16[32,16,128]{2,1,0:T(8,128)(2,1)}, bf16[32,16,128]{2,1,0:T(8,128)(2...) custom-call(s32[9]{0:T(128)} %pad_add_fusion.meta_ref, ...), custom_call_target="tpu_custom_call" | custom-call | flops 1073741824 | bytes 5242880 | tf_op jit(solution)/shard_map/spectra/pallas_call | solution.py:270
  22.6 9.7 %collective-permute-start.2 = (bf16[32,16,128]{2,1,0:T(8,128)(2,1)}, bf16[32,16,128]{2,1,0:T(8,128)(2,1)S(1)}, u32[]{:S(2)}, u32[]{:S(2)}) collective-permute-start(bf16[32,16,128]{2,1,0:T(8,128)(2,1)} %get-tuple-element.119), channel_id=1, source_target_pairs={{0,1},{1,0},{2,3},{3,2},{4,5},{5,4},{6,7},{7,6},{8,9},{9,8},{10,11... | collective-permute-start | bytes 393224 | tf_op jit(solution)/shard_map/ppermute | solution.py:390
  35.9 2.5 collective-permute-start.6
  38.4 9.9 %spectra.7 = (bf16[32,16,128]{2,1,0:T(8,128)(2,1)}, bf16[32,16,128]{2,1,0:T(8,128)(2,1)}, bf16[32,16,128]{2,1,0:T(8,128)(2,1)}, bf16[32,16,128]{2,1,0:T(8,128)(2...) custom-call(s32[9]{0:T(128)} %pad_add_fusion.meta_ref, ...), custom_call_target="tpu_custom_call" | custom-call | flops 1073741824 | bytes 5242880 | tf_op jit(solution)/shard_map/spectra/pallas_call | solution.py:270
  50.3 2.0 collective-permute-start.10
  52.3 7.2 %collective-permute-start.11 = (bf16[32,16,128]{2,1,0:T(8,128)(2,1)}, bf16[32,16,128]{2,1,0:T(8,128)(2,1)S(1)}, u32[]{:S(2)}, u32[]{:S(2)}) collective-permute-start(bf16[32,16,128]{2,1,0:T(8,128)(2,1)} %get-tuple-element.131), channel_id=1, source_target_pairs={{0,4},{1,5},{2,6},{3,7},{4,0},{5,1},{6,2},{7,3},{8,12},{9,13},{10,... | collective-permute-start | bytes 393224 | tf_op jit(solution)/shard_map/ppermute | solution.py:390
  59.5 14.7 %spectra.8 = (bf16[32,32,128]{2,1,0:T(8,128)(2,1)}, bf16[32,32,128]{2,1,0:T(8,128)(2,1)}, bf16[32,32,128]{2,1,0:T(8,128)(2,1)}, bf16[32,32,128]{2,1,0:T(8,128)(2...) custom-call(s32[9]{0:T(128)} %pad_add_fusion.meta_ref, ...), custom_call_target="tpu_custom_call" | custom-call | flops 2147483648 | bytes 8388608 | tf_op jit(solution)/shard_map/spectra/pallas_call | solution.py:270
  76.0 7.3 %shrink.6 = (bf16[32,16,128]{2,1,0:T(8,128)(2,1)}, bf16[32,16,128]{2,1,0:T(8,128)(2,1)}, bf16[32,16,128]{2,1,0:T(8,128)(2,1)}, bf16[32,16,128]{2,1,0:T(8,128)(2,...) custom-call(s32[9]{0:T(128)} %pad_add_fusion.meta_ref, ...), custom_call_target="tpu_custom_call" | custom-call | flops 1073741824 | bytes 2359296 | tf_op jit(solution)/shard_map/shrink/pallas_call | solution.py:320
  88.3 2.8 collective-permute-done.14.refs_6_
  91.7 2.7 collective-permute-start.19
  95.0 2.2 collective-permute-start.20
  97.3 3.9 collective-permute-start.21
  101.3 9.0 %collective-permute-done.19.refs_4_ = bf16[32,16,128]{2,1,0:T(8,128)(2,1)S(1)} collective-permute-done((bf16[32,16,128]{2,1,0:T(8,128)(2,1)}, bf16[32,16,128]{2,1,0:T(8,128)(2,1)S(1)}, u32[]{:S(2)}, u32[]{:S(2)}) %collective-permute-start.19) | collective-permute-done | bytes 131104 | tf_op jit(solution)/shard_map/ppermute | solution.py:390
  110.3 3.0 collective-permute-start.26
  113.3 14.0 %collective-permute-start.22 = (bf16[32,16,128]{2,1,0:T(8,128)(2,1)}, bf16[32,16,128]{2,1,0:T(8,128)(2,1)S(1)}, u32[]{:S(2)}, u32[]{:S(2)}) collective-permute-start(bf16[32,16,128]{2,1,0:T(8,128)(2,1)} %get-tuple-element.143), channel_id=1, source_target_pairs={{0,3},{1,2},{2,1},{3,0},{4,7},{5,6},{6,5},{7,4},{8,11},{9,10},{10,... | collective-permute-start | bytes 393224 | tf_op jit(solution)/shard_map/ppermute | solution.py:390
  127.4 14.8 %spectra.9 = (bf16[32,32,128]{2,1,0:T(8,128)(2,1)}, bf16[32,32,128]{2,1,0:T(8,128)(2,1)}, bf16[32,32,128]{2,1,0:T(8,128)(2,1)}, bf16[32,32,128]{2,1,0:T(8,128)(2...) custom-call(s32[9]{0:T(128)} %pad_add_fusion.meta_ref, ...), custom_call_target="tpu_custom_call" | custom-call | flops 2147483648 | bytes 8388608 | tf_op jit(solution)/shard_map/spectra/pallas_call | solution.py:270
  142.2 2.2 collective-permute-start.27
  145.9 7.2 %shrink.7 = (bf16[32,16,128]{2,1,0:T(8,128)(2,1)}, bf16[32,16,128]{2,1,0:T(8,128)(2,1)}, bf16[32,16,128]{2,1,0:T(8,128)(2,1)}, bf16[32,16,128]{2,1,0:T(8,128)(2,...) custom-call(s32[9]{0:T(128)} %pad_add_fusion.meta_ref, ...), custom_call_target="tpu_custom_call" | custom-call | flops 1073741824 | bytes 2359296 | tf_op jit(solution)/shard_map/shrink/pallas_call | solution.py:320
  153.6 1.8 collective-permute-start.31
  156.2 3.2 update.6
  160.1 10.2 %spectra.10 = (bf16[32,16,128]{2,1,0:T(8,128)(2,1)}, bf16[32,16,128]{2,1,0:T(8,128)(2,1)}, bf16[32,16,128]{2,1,0:T(8,128)(2,1)}, bf16[32,16,128]{2,1,0:T(8,128)(...) custom-call(s32[9]{0:T(128)} %pad_add_fusion.meta_ref, ...), custom_call_target="tpu_custom_call" | custom-call | flops 1073741824 | bytes 5242880 | tf_op jit(solution)/shard_map/spectra/pallas_call | solution.py:270
  172.7 2.1 collective-permute-start.34
  174.8 1.8 collective-permute-start.35
  176.6 14.6 %shrink.8 = (bf16[32,32,128]{2,1,0:T(8,128)(2,1)}, bf16[32,32,128]{2,1,0:T(8,128)(2,1)}, bf16[32,32,128]{2,1,0:T(8,128)(2,1)}, bf16[32,32,128]{2,1,0:T(8,128)(2,...) custom-call(s32[9]{0:T(128)} %pad_add_fusion.meta_ref, ...), custom_call_target="tpu_custom_call" | custom-call | flops 2147483648 | bytes 4456448 | tf_op jit(solution)/shard_map/shrink/pallas_call | solution.py:320
  191.2 2.0 collective-permute-done.36.refs_7_
  194.2 3.2 update.7
  198.1 10.0 %spectra.11 = (bf16[32,16,128]{2,1,0:T(8,128)(2,1)}, bf16[32,16,128]{2,1,0:T(8,128)(2,1)}, bf16[32,16,128]{2,1,0:T(8,128)(2,1)}, bf16[32,16,128]{2,1,0:T(8,128)(...) custom-call(s32[9]{0:T(128)} %pad_add_fusion.meta_ref, ...), custom_call_target="tpu_custom_call" | custom-call | flops 1073741824 | bytes 5242880 | tf_op jit(solution)/shard_map/spectra/pallas_call | solution.py:270
  208.3 3.3 collective-permute-start.66
  214.0 2.1 collective-permute-start.69
  218.0 12.3 %collective-permute-done.67.refs_3_ = bf16[32,16,128]{2,1,0:T(8,128)(2,1)S(1)} collective-permute-done((bf16[32,16,128]{2,1,0:T(8,128)(2,1)}, bf16[32,16,128]{2,1,0:T(8,128)(2,1)S(1)}, u32[]{:S(2)}, u32[]{:S(2)}) %collective-permute-start.67) | collective-permute-done | bytes 131104 | tf_op jit(solution)/shard_map/ppermute | solution.py:390
  233.7 7.4 %collective-permute-start.38 = (bf16[32,32,128]{2,1,0:T(8,128)(2,1)S(1)}, bf16[32,32,128]{2,1,0:T(8,128)(2,1)S(1)}, u32[]{:S(2)}, u32[]{:S(2)}) collective-permute-start(bf16[32,32,128]{2,1,0:T(8,128)(2,1)S(1)} %copy-done.33), channel_id=1, source_target_pairs={{0,2},{1,3},{2,0},{3,1},{4,6},{5,7},{6,4},{7,5},{8,10},{9,11},{10,... | collective-permute-start | bytes 786440 | tf_op jit(solution)/shard_map/ppermute | solution.py:390
  245.0 5.7 %collective-permute-done.54.refs_4_ = bf16[32,16,128]{2,1,0:T(8,128)(2,1)S(1)} collective-permute-done((bf16[32,16,128]{2,1,0:T(8,128)(2,1)}, bf16[32,16,128]{2,1,0:T(8,128)(2,1)S(1)}, u32[]{:S(2)}, u32[]{:S(2)}) %collective-permute-start.54) | collective-permute-done | bytes 131104 | tf_op jit(solution)/shard_map/ppermute | solution.py:390
  250.8 3.4 collective-permute-start.39
  255.4 3.4 collective-permute-done.56.refs_6_
  258.8 1.8 collective-permute-start.41
  260.7 15.5 %collective-permute-start.42 = (bf16[32,32,128]{2,1,0:T(8,128)(2,1)S(1)}, bf16[32,32,128]{2,1,0:T(8,128)(2,1)S(1)}, u32[]{:S(2)}, u32[]{:S(2)}) collective-permute-start(bf16[32,32,128]{2,1,0:T(8,128)(2,1)S(1)} %copy-done.29), channel_id=1, source_target_pairs={{0,7},{1,6},{2,5},{3,4},{4,3},{5,2},{6,1},{7,0},{8,15},{9,14},{10,... | collective-permute-start | bytes 786440 | tf_op jit(solution)/shard_map/ppermute | solution.py:390
  276.2 14.9 %collective-permute-done.39.refs_3_ = bf16[32,32,128]{2,1,0:T(8,128)(2,1)S(1)} collective-permute-done((bf16[32,32,128]{2,1,0:T(8,128)(2,1)S(1)}, bf16[32,32,128]{2,1,0:T(8,128)(2,1)S(1)}, u32[]{:S(2)}, u32[]{:S(2)}) %collective-permute-start.39) | collective-permute-done | bytes 262176 | tf_op jit(solution)/shard_map/ppermute | solution.py:390
  291.1 3.9 collective-permute-done.40.refs_4_
  296.0 7.5 %collective-permute-start.46 = (bf16[32,32,128]{2,1,0:T(8,128)(2,1)}, bf16[32,32,128]{2,1,0:T(8,128)(2,1)S(1)}, u32[]{:S(2)}, u32[]{:S(2)}) collective-permute-start(bf16[32,32,128]{2,1,0:T(8,128)(2,1)} %get-tuple-element.176), channel_id=1, source_target_pairs={{0,4},{1,5},{2,6},{3,7},{4,0},{5,1},{6,2},{7,3},{8,12},{9,13},{10,... | collective-permute-start | bytes 786440 | tf_op jit(solution)/shard_map/ppermute | solution.py:390
  303.6 10.7 %collective-permute-start.47 = (bf16[32,32,128]{2,1,0:T(8,128)(2,1)}, bf16[32,32,128]{2,1,0:T(8,128)(2,1)S(1)}, u32[]{:S(2)}, u32[]{:S(2)}) collective-permute-start(bf16[32,32,128]{2,1,0:T(8,128)(2,1)} %get-tuple-element.177), channel_id=1, source_target_pairs={{0,5},{1,4},{2,7},{3,6},{4,1},{5,0},{6,3},{7,2},{8,13},{9,12},{10,... | collective-permute-start | bytes 786440 | tf_op jit(solution)/shard_map/ppermute | solution.py:390
  315.0 14.7 %shrink.9 = (bf16[32,32,128]{2,1,0:T(8,128)(2,1)}, bf16[32,32,128]{2,1,0:T(8,128)(2,1)}, bf16[32,32,128]{2,1,0:T(8,128)(2,1)}, bf16[32,32,128]{2,1,0:T(8,128)(2,...) custom-call(s32[9]{0:T(128)} %pad_add_fusion.meta_ref, ...), custom_call_target="tpu_custom_call" | custom-call | flops 2147483648 | bytes 4456448 | tf_op jit(solution)/shard_map/shrink/pallas_call | solution.py:320
  329.7 1.7 collective-permute-start.48
  331.9 1.9 collective-permute-start.58
  336.0 5.1 %collective-permute-done.48.refs_5_ = bf16[32,32,128]{2,1,0:T(8,128)(2,1)S(1)} collective-permute-done((bf16[32,32,128]{2,1,0:T(8,128)(2,1)}, bf16[32,32,128]{2,1,0:T(8,128)(2,1)S(1)}, u32[]{:S(2)}, u32[]{:S(2)}) %collective-permute-start.48) | collective-permute-done | bytes 262176 | tf_op jit(solution)/shard_map/ppermute | solution.py:390
  341.1 9.8 %collective-permute-start.60 = (bf16[32,32,128]{2,1,0:T(8,128)(2,1)}, bf16[32,32,128]{2,1,0:T(8,128)(2,1)}, u32[]{:S(2)}, u32[]{:S(2)}) collective-permute-start(bf16[32,32,128]{2,1,0:T(8,128)(2,1)} %get-tuple-element.194), channel_id=1, source_target_pairs={{0,4},{1,5},{2,6},{3,7},{4,0},{5,1},{6,2},{7,3},{8,12},{9,13},{10,... | collective-permute-start | bytes 786440 | tf_op jit(solution)/shard_map/ppermute | solution.py:390
  351.0 6.3 %collective-permute-start.61 = (bf16[32,32,128]{2,1,0:T(8,128)(2,1)}, bf16[32,32,128]{2,1,0:T(8,128)(2,1)}, u32[]{:S(2)}, u32[]{:S(2)}) collective-permute-start(bf16[32,32,128]{2,1,0:T(8,128)(2,1)} %get-tuple-element.195), channel_id=1, source_target_pairs={{0,5},{1,4},{2,7},{3,6},{4,1},{5,0},{6,3},{7,2},{8,13},{9,12},{10,... | collective-permute-start | bytes 786440 | tf_op jit(solution)/shard_map/ppermute | solution.py:390
  358.8 2.4 collective-permute-start.63
  363.1 5.0 %update.8 = (f32[32,128,1024]{2,1,0:T(8,128)}, f32[8,128]{1,0:T(8,128)S(1)}) custom-call(s32[9]{0:T(128)S(1)} %copy-done.13, bf16[1024,1024]{1,0:T(8,128)(2,1)S(1)} %copy-done, bf16[32,32,128]{2,1,0:T(8,128)(2,1)S(1)} %copy-done.3, bf16[32,32,128]{2,1,0:T(8,128)(2,1)S(1)} %copy-done.2, ...), custom_call_target="tpu_custom_call", output_to_operand_aliasing={{0}: (11, {})} | custom-call | flops 2147483648 | bytes 8388608 | tf_op jit(solution)/shard_map/update/pallas_call | solution.py:351
  368.8 7.4 %shrink.10 = (bf16[32,16,128]{2,1,0:T(8,128)(2,1)}, bf16[32,16,128]{2,1,0:T(8,128)(2,1)}, bf16[32,16,128]{2,1,0:T(8,128)(2,1)}, bf16[32,16,128]{2,1,0:T(8,128)(2...) custom-call(s32[9]{0:T(128)} %pad_add_fusion.meta_ref, ...), custom_call_target="tpu_custom_call" | custom-call | flops 1073741824 | bytes 2359296 | tf_op jit(solution)/shard_map/shrink/pallas_call | solution.py:320
  376.2 7.1 %collective-permute-done.60.refs_3_ = bf16[32,32,128]{2,1,0:T(8,128)(2,1)} collective-permute-done((bf16[32,32,128]{2,1,0:T(8,128)(2,1)}, bf16[32,32,128]{2,1,0:T(8,128)(2,1)}, u32[]{:S(2)}, u32[]{:S(2)}) %collective-permute-start.60) | collective-permute-done | bytes 262176 | tf_op jit(solution)/shard_map/ppermute | solution.py:390
  383.3 6.4 %collective-permute-done.61.refs_4_ = bf16[32,32,128]{2,1,0:T(8,128)(2,1)} collective-permute-done((bf16[32,32,128]{2,1,0:T(8,128)(2,1)}, bf16[32,32,128]{2,1,0:T(8,128)(2,1)}, u32[]{:S(2)}, u32[]{:S(2)}) %collective-permute-start.61) | collective-permute-done | bytes 262176 | tf_op jit(solution)/shard_map/ppermute | solution.py:390
  389.7 5.4 %collective-permute-start.73 = (bf16[32,16,128]{2,1,0:T(8,128)(2,1)}, bf16[32,16,128]{2,1,0:T(8,128)(2,1)S(1)}, u32[]{:S(2)}, u32[]{:S(2)}) collective-permute-start(bf16[32,16,128]{2,1,0:T(8,128)(2,1)} %get-tuple-element.211), channel_id=1, source_target_pairs={{0,2},{1,3},{2,0},{3,1},{4,6},{5,7},{6,4},{7,5},{8,10},{9,11},{10,... | collective-permute-start | bytes 393224 | tf_op jit(solution)/shard_map/ppermute | solution.py:390
  395.0 6.7 %collective-permute-start.74 = (bf16[32,16,128]{2,1,0:T(8,128)(2,1)}, bf16[32,16,128]{2,1,0:T(8,128)(2,1)S(1)}, u32[]{:S(2)}, u32[]{:S(2)}) collective-permute-start(bf16[32,16,128]{2,1,0:T(8,128)(2,1)} %get-tuple-element.212), channel_id=1, source_target_pairs={{0,4},{1,5},{2,6},{3,7},{4,0},{5,1},{6,2},{7,3},{8,12},{9,13},{10,... | collective-permute-start | bytes 393224 | tf_op jit(solution)/shard_map/ppermute | solution.py:390
  402.7 6.7 %update.9 = (f32[32,128,1024]{2,1,0:T(8,128)}, f32[8,128]{1,0:T(8,128)S(1)}) custom-call(s32[9]{0:T(128)S(1)} %copy-done.14, bf16[1024,1024]{1,0:T(8,128)(2,1)S(1)} %copy-done, bf16[32,16,128]{2,1,0:T(8,128)(2,1)S(1)} %copy-done.4, bf16[32,32,128]{2,1,0:T(8,128)(2,1)S(1)} %copy-done.3, ...), custom_call_target="tpu_custom_call", output_to_operand_aliasing={{0}: (11, {})} | custom-call | flops 2147483648 | bytes 8388608 | tf_op jit(solution)/shard_map/update/pallas_call | solution.py:351
  411.6 7.3 %shrink.11 = (bf16[32,16,128]{2,1,0:T(8,128)(2,1)}, bf16[32,16,128]{2,1,0:T(8,128)(2,1)}, bf16[32,16,128]{2,1,0:T(8,128)(2,1)}, bf16[32,16,128]{2,1,0:T(8,128)(2...) custom-call(s32[9]{0:T(128)} %pad_add_fusion.meta_ref, ...), custom_call_target="tpu_custom_call" | custom-call | flops 1073741824 | bytes 2359296 | tf_op jit(solution)/shard_map/shrink/pallas_call | solution.py:320
  423.1 9.9 %psum.7 = f32[32]{0:T(128)S(1)} all-reduce(f32[32]{0:T(128)S(1)} %add_reduce_fusion), channel_id=1, replica_groups=mesh['patch'=4,'shot'=8] {'patch'}, use_global_device_ids=true, to_apply=%region_1.0 | all-reduce | flops 32 | bytes 256 | tf_op jit(solution)/shard_map/psum | solution.py:515
  433.9 1.9 collective-permute-start.83
  435.9 3.4 collective-permute-start.84
  440.7 3.2 update.10
  443.9 6.3 %collective-permute-done.81.refs_3_ = bf16[32,16,128]{2,1,0:T(8,128)(2,1)S(1)} collective-permute-done((bf16[32,16,128]{2,1,0:T(8,128)(2,1)}, bf16[32,16,128]{2,1,0:T(8,128)(2,1)S(1)}, u32[]{:S(2)}, u32[]{:S(2)}) %collective-permute-start.81) | collective-permute-done | bytes 131104 | tf_op jit(solution)/shard_map/ppermute | solution.py:390
  450.3 3.5 collective-permute-done.85.refs_7_
  453.9 3.2 update.11
  (296 shorter events, 59.1 us)
Async XLA Ops:
  22.6 25.7 %collective-permute-start.2 = (bf16[32,16,128]{2,1,0:T(8,128)(2,1)}, bf16[32,16,128]{2,1,0:T(8,128)(2,1)S(1)}, u32[]{:S(2)}, u32[]{:S(2)}) collective-permute-start(bf16[32,16,128]{2,1,0:T(8,128)(2,1)} %get-tuple-element.119), channel_id=1, source_target_pairs={{0,1},{1,0},{2,3},{3,2},{4,5},{5,4},{6,7},{7,6},{8,9},{9,8},{10,11... | collective-permute-start | bytes 393224 | tf_op jit(solution)/shard_map/ppermute | solution.py:390
  32.3 17.8 %collective-permute-start.3 = (bf16[32,16,128]{2,1,0:T(8,128)(2,1)}, bf16[32,16,128]{2,1,0:T(8,128)(2,1)S(1)}, u32[]{:S(2)}, u32[]{:S(2)}) collective-permute-start(bf16[32,16,128]{2,1,0:T(8,128)(2,1)} %get-tuple-element.120), channel_id=1, source_target_pairs={{0,2},{1,3},{2,0},{3,1},{4,6},{5,7},{6,4},{7,5},{8,10},{9,11},{10,... | collective-permute-start | bytes 393224 | tf_op jit(solution)/shard_map/ppermute | solution.py:390
  33.9 16.3 %collective-permute-start.4 = (bf16[32,16,128]{2,1,0:T(8,128)(2,1)}, bf16[32,16,128]{2,1,0:T(8,128)(2,1)S(1)}, u32[]{:S(2)}, u32[]{:S(2)}) collective-permute-start(bf16[32,16,128]{2,1,0:T(8,128)(2,1)} %get-tuple-element.121), channel_id=1, source_target_pairs={{0,4},{1,5},{2,6},{3,7},{4,0},{5,1},{6,2},{7,3},{8,12},{9,13},{10,... | collective-permute-start | bytes 393224 | tf_op jit(solution)/shard_map/ppermute | solution.py:390
  34.9 15.4 %collective-permute-start.5 = (bf16[32,16,128]{2,1,0:T(8,128)(2,1)}, bf16[32,16,128]{2,1,0:T(8,128)(2,1)S(1)}, u32[]{:S(2)}, u32[]{:S(2)}) collective-permute-start(bf16[32,16,128]{2,1,0:T(8,128)(2,1)} %get-tuple-element.122), channel_id=1, source_target_pairs={{0,5},{1,4},{2,7},{3,6},{4,1},{5,0},{6,3},{7,2},{8,13},{9,12},{10,... | collective-permute-start | bytes 393224 | tf_op jit(solution)/shard_map/ppermute | solution.py:390
  35.9 16.4 %collective-permute-start.6 = (bf16[32,16,128]{2,1,0:T(8,128)(2,1)}, bf16[32,16,128]{2,1,0:T(8,128)(2,1)S(1)}, u32[]{:S(2)}, u32[]{:S(2)}) collective-permute-start(bf16[32,16,128]{2,1,0:T(8,128)(2,1)} %get-tuple-element.123), channel_id=1, source_target_pairs={{0,6},{1,7},{2,4},{3,5},{4,2},{5,3},{6,0},{7,1},{8,14},{9,15},{10,... | collective-permute-start | bytes 393224 | tf_op jit(solution)/shard_map/ppermute | solution.py:390
  48.3 25.9 %collective-permute-start.7 = (bf16[32,16,128]{2,1,0:T(8,128)(2,1)}, bf16[32,16,128]{2,1,0:T(8,128)(2,1)}, u32[]{:S(2)}, u32[]{:S(2)}) collective-permute-start(bf16[32,16,128]{2,1,0:T(8,128)(2,1)} %get-tuple-element.124), channel_id=1, source_target_pairs={{0,7},{1,6},{2,5},{3,4},{4,3},{5,2},{6,1},{7,0},{8,15},{9,14},{10,... | collective-permute-start | bytes 393224 | tf_op jit(solution)/shard_map/ppermute | solution.py:390
  50.1 24.3 %collective-permute-start.8 = (bf16[32,16,128]{2,1,0:T(8,128)(2,1)S(1)}, bf16[32,16,128]{2,1,0:T(8,128)(2,1)}, u32[]{:S(2)}, u32[]{:S(2)}) collective-permute-start(bf16[32,16,128]{2,1,0:T(8,128)(2,1)S(1)} %copy-done.76), channel_id=1, source_target_pairs={{0,3},{1,2},{2,1},{3,0},{4,7},{5,6},{6,5},{7,4},{8,11},{9,10},{10,... | collective-permute-start | bytes 393224 | tf_op jit(solution)/shard_map/ppermute | solution.py:390
  50.2 33.2 %collective-permute-start.9 = (bf16[32,16,128]{2,1,0:T(8,128)(2,1)}, bf16[32,16,128]{2,1,0:T(8,128)(2,1)S(1)}, u32[]{:S(2)}, u32[]{:S(2)}) collective-permute-start(bf16[32,16,128]{2,1,0:T(8,128)(2,1)} %get-tuple-element.129), channel_id=1, source_target_pairs={{0,1},{1,0},{2,3},{3,2},{4,5},{5,4},{6,7},{7,6},{8,9},{9,8},{10,11... | collective-permute-start | bytes 393224 | tf_op jit(solution)/shard_map/ppermute | solution.py:390
  50.3 34.7 %collective-permute-start.10 = (bf16[32,16,128]{2,1,0:T(8,128)(2,1)}, bf16[32,16,128]{2,1,0:T(8,128)(2,1)S(1)}, u32[]{:S(2)}, u32[]{:S(2)}) collective-permute-start(bf16[32,16,128]{2,1,0:T(8,128)(2,1)} %get-tuple-element.130), channel_id=1, source_target_pairs={{0,2},{1,3},{2,0},{3,1},{4,6},{5,7},{6,4},{7,5},{8,10},{9,11},{10,... | collective-permute-start | bytes 393224 | tf_op jit(solution)/shard_map/ppermute | solution.py:390
  52.3 32.8 %collective-permute-start.11 = (bf16[32,16,128]{2,1,0:T(8,128)(2,1)}, bf16[32,16,128]{2,1,0:T(8,128)(2,1)S(1)}, u32[]{:S(2)}, u32[]{:S(2)}) collective-permute-start(bf16[32,16,128]{2,1,0:T(8,128)(2,1)} %get-tuple-element.131), channel_id=1, source_target_pairs={{0,4},{1,5},{2,6},{3,7},{4,0},{5,1},{6,2},{7,3},{8,12},{9,13},{10,... | collective-permute-start | bytes 393224 | tf_op jit(solution)/shard_map/ppermute | solution.py:390
  91.7 18.6 %collective-permute-start.19 = (bf16[32,16,128]{2,1,0:T(8,128)(2,1)}, bf16[32,16,128]{2,1,0:T(8,128)(2,1)S(1)}, u32[]{:S(2)}, u32[]{:S(2)}) collective-permute-start(bf16[32,16,128]{2,1,0:T(8,128)(2,1)} %get-tuple-element.140), channel_id=1, source_target_pairs={{0,5},{1,4},{2,7},{3,6},{4,1},{5,0},{6,3},{7,2},{8,13},{9,12},{10,... | collective-permute-start | bytes 393224 | tf_op jit(solution)/shard_map/ppermute | solution.py:390
  97.3 16.1 %collective-permute-start.21 = (bf16[32,16,128]{2,1,0:T(8,128)(2,1)}, bf16[32,16,128]{2,1,0:T(8,128)(2,1)S(1)}, u32[]{:S(2)}, u32[]{:S(2)}) collective-permute-start(bf16[32,16,128]{2,1,0:T(8,128)(2,1)} %get-tuple-element.142), channel_id=1, source_target_pairs={{0,7},{1,6},{2,5},{3,4},{4,3},{5,2},{6,1},{7,0},{8,15},{9,14},{10,... | collective-permute-start | bytes 393224 | tf_op jit(solution)/shard_map/ppermute | solution.py:390
  101.2 43.2 %collective-permute-start.23 = (bf16[32,32,128]{2,1,0:T(8,128)(2,1)}, bf16[32,32,128]{2,1,0:T(8,128)(2,1)S(1)}, u32[]{:S(2)}, u32[]{:S(2)}) collective-permute-start(bf16[32,32,128]{2,1,0:T(8,128)(2,1)} %get-tuple-element.147), channel_id=1, source_target_pairs={{0,1},{1,0},{2,3},{3,2},{4,5},{5,4},{6,7},{7,6},{8,9},{9,8},{10,11... | collective-permute-start | bytes 786440 | tf_op jit(solution)/shard_map/ppermute | solution.py:390
  101.2 44.6 %collective-permute-start.24 = (bf16[32,32,128]{2,1,0:T(8,128)(2,1)}, bf16[32,32,128]{2,1,0:T(8,128)(2,1)}, u32[]{:S(2)}, u32[]{:S(2)}) collective-permute-start(bf16[32,32,128]{2,1,0:T(8,128)(2,1)} %get-tuple-element.148), channel_id=1, source_target_pairs={{0,2},{1,3},{2,0},{3,1},{4,6},{5,7},{6,4},{7,5},{8,10},{9,11},{10,... | collective-permute-start | bytes 786440 | tf_op jit(solution)/shard_map/ppermute | solution.py:390
  110.3 42.8 %collective-permute-start.25 = (bf16[32,32,128]{2,1,0:T(8,128)(2,1)}, bf16[32,32,128]{2,1,0:T(8,128)(2,1)}, u32[]{:S(2)}, u32[]{:S(2)}) collective-permute-start(bf16[32,32,128]{2,1,0:T(8,128)(2,1)} %get-tuple-element.149), channel_id=1, source_target_pairs={{0,4},{1,5},{2,6},{3,7},{4,0},{5,1},{6,2},{7,3},{8,12},{9,13},{10,... | collective-permute-start | bytes 786440 | tf_op jit(solution)/shard_map/ppermute | solution.py:390
  110.3 43.2 %collective-permute-start.26 = (bf16[32,32,128]{2,1,0:T(8,128)(2,1)}, bf16[32,32,128]{2,1,0:T(8,128)(2,1)}, u32[]{:S(2)}, u32[]{:S(2)}) collective-permute-start(bf16[32,32,128]{2,1,0:T(8,128)(2,1)} %get-tuple-element.150), channel_id=1, source_target_pairs={{0,5},{1,4},{2,7},{3,6},{4,1},{5,0},{6,3},{7,2},{8,13},{9,12},{10,... | collective-permute-start | bytes 786440 | tf_op jit(solution)/shard_map/ppermute | solution.py:390
  113.3 28.8 %collective-permute-start.22 = (bf16[32,16,128]{2,1,0:T(8,128)(2,1)}, bf16[32,16,128]{2,1,0:T(8,128)(2,1)S(1)}, u32[]{:S(2)}, u32[]{:S(2)}) collective-permute-start(bf16[32,16,128]{2,1,0:T(8,128)(2,1)} %get-tuple-element.143), channel_id=1, source_target_pairs={{0,3},{1,2},{2,1},{3,0},{4,7},{5,6},{6,5},{7,4},{8,11},{9,10},{10,... | collective-permute-start | bytes 393224 | tf_op jit(solution)/shard_map/ppermute | solution.py:390
  142.2 28.1 %collective-permute-start.27 = (bf16[32,32,128]{2,1,0:T(8,128)(2,1)}, bf16[32,32,128]{2,1,0:T(8,128)(2,1)}, u32[]{:S(2)}, u32[]{:S(2)}) collective-permute-start(bf16[32,32,128]{2,1,0:T(8,128)(2,1)} %get-tuple-element.151), channel_id=1, source_target_pairs={{0,6},{1,7},{2,4},{3,5},{4,2},{5,3},{6,0},{7,1},{8,14},{9,15},{10,... | collective-permute-start | bytes 786440 | tf_op jit(solution)/shard_map/ppermute | solution.py:390
  144.4 26.9 %collective-permute-start.28 = (bf16[32,32,128]{2,1,0:T(8,128)(2,1)}, bf16[32,32,128]{2,1,0:T(8,128)(2,1)}, u32[]{:S(2)}, u32[]{:S(2)}) collective-permute-start(bf16[32,32,128]{2,1,0:T(8,128)(2,1)} %get-tuple-element.152), channel_id=1, source_target_pairs={{0,7},{1,6},{2,5},{3,4},{4,3},{5,2},{6,1},{7,0},{8,15},{9,14},{10,... | collective-permute-start | bytes 786440 | tf_op jit(solution)/shard_map/ppermute | solution.py:390
  145.8 26.8 %collective-permute-start.29 = (bf16[32,32,128]{2,1,0:T(8,128)(2,1)S(1)}, bf16[32,32,128]{2,1,0:T(8,128)(2,1)}, u32[]{:S(2)}, u32[]{:S(2)}) collective-permute-start(bf16[32,32,128]{2,1,0:T(8,128)(2,1)S(1)} %copy-done.34), channel_id=1, source_target_pairs={{0,3},{1,2},{2,1},{3,0},{4,7},{5,6},{6,5},{7,4},{8,11},{9,10},{10,... | collective-permute-start | bytes 786440 | tf_op jit(solution)/shard_map/ppermute | solution.py:390
  153.1 21.7 %collective-permute-start.30 = (bf16[32,16,128]{2,1,0:T(8,128)(2,1)}, bf16[32,16,128]{2,1,0:T(8,128)(2,1)S(1)}, u32[]{:S(2)}, u32[]{:S(2)}) collective-permute-start(bf16[32,16,128]{2,1,0:T(8,128)(2,1)} %get-tuple-element.155), channel_id=1, source_target_pairs={{0,1},{1,0},{2,3},{3,2},{4,5},{5,4},{6,7},{7,6},{8,9},{9,8},{10,11... | collective-permute-start | bytes 393224 | tf_op jit(solution)/shard_map/ppermute | solution.py:390
  153.6 23.0 %collective-permute-start.31 = (bf16[32,16,128]{2,1,0:T(8,128)(2,1)}, bf16[32,16,128]{2,1,0:T(8,128)(2,1)S(1)}, u32[]{:S(2)}, u32[]{:S(2)}) collective-permute-start(bf16[32,16,128]{2,1,0:T(8,128)(2,1)} %get-tuple-element.156), channel_id=1, source_target_pairs={{0,2},{1,3},{2,0},{3,1},{4,6},{5,7},{6,4},{7,5},{8,10},{9,11},{10,... | collective-permute-start | bytes 393224 | tf_op jit(solution)/shard_map/ppermute | solution.py:390
  170.3 20.9 %collective-permute-start.32 = (bf16[32,16,128]{2,1,0:T(8,128)(2,1)S(1)}, bf16[32,16,128]{2,1,0:T(8,128)(2,1)S(1)}, u32[]{:S(2)}, u32[]{:S(2)}) collective-permute-start(bf16[32,16,128]{2,1,0:T(8,128)(2,1)S(1)} %copy-done.71), channel_id=1, source_target_pairs={{0,4},{1,5},{2,6},{3,7},{4,0},{5,1},{6,2},{7,3},{8,12},{9,13},{10,... | collective-permute-start | bytes 393224 | tf_op jit(solution)/shard_map/ppermute | solution.py:390
  171.2 20.0 %collective-permute-start.33 = (bf16[32,16,128]{2,1,0:T(8,128)(2,1)S(1)}, bf16[32,16,128]{2,1,0:T(8,128)(2,1)S(1)}, u32[]{:S(2)}, u32[]{:S(2)}) collective-permute-start(bf16[32,16,128]{2,1,0:T(8,128)(2,1)S(1)} %copy-done.70), channel_id=1, source_target_pairs={{0,5},{1,4},{2,7},{3,6},{4,1},{5,0},{6,3},{7,2},{8,13},{9,12},{10,... | collective-permute-start | bytes 393224 | tf_op jit(solution)/shard_map/ppermute | solution.py:390
  172.7 18.6 %collective-permute-start.34 = (bf16[32,16,128]{2,1,0:T(8,128)(2,1)S(1)}, bf16[32,16,128]{2,1,0:T(8,128)(2,1)S(1)}, u32[]{:S(2)}, u32[]{:S(2)}) collective-permute-start(bf16[32,16,128]{2,1,0:T(8,128)(2,1)S(1)} %copy-done.68), channel_id=1, source_target_pairs={{0,6},{1,7},{2,4},{3,5},{4,2},{5,3},{6,0},{7,1},{8,14},{9,15},{10,... | collective-permute-start | bytes 393224 | tf_op jit(solution)/shard_map/ppermute | solution.py:390
  174.8 16.4 %collective-permute-start.35 = (bf16[32,16,128]{2,1,0:T(8,128)(2,1)S(1)}, bf16[32,16,128]{2,1,0:T(8,128)(2,1)S(1)}, u32[]{:S(2)}, u32[]{:S(2)}) collective-permute-start(bf16[32,16,128]{2,1,0:T(8,128)(2,1)S(1)} %copy-done.67), channel_id=1, source_target_pairs={{0,7},{1,6},{2,5},{3,4},{4,3},{5,2},{6,1},{7,0},{8,15},{9,14},{10,... | collective-permute-start | bytes 393224 | tf_op jit(solution)/shard_map/ppermute | solution.py:390
  176.5 16.7 %collective-permute-start.36 = (bf16[32,16,128]{2,1,0:T(8,128)(2,1)S(1)}, bf16[32,16,128]{2,1,0:T(8,128)(2,1)S(1)}, u32[]{:S(2)}, u32[]{:S(2)}) collective-permute-start(bf16[32,16,128]{2,1,0:T(8,128)(2,1)S(1)} %copy-done.65), channel_id=1, source_target_pairs={{0,3},{1,2},{2,1},{3,0},{4,7},{5,6},{6,5},{7,4},{8,11},{9,10},{10,... | collective-permute-start | bytes 393224 | tf_op jit(solution)/shard_map/ppermute | solution.py:390
  211.6 18.7 %collective-permute-start.67 = (bf16[32,16,128]{2,1,0:T(8,128)(2,1)}, bf16[32,16,128]{2,1,0:T(8,128)(2,1)S(1)}, u32[]{:S(2)}, u32[]{:S(2)}) collective-permute-start(bf16[32,16,128]{2,1,0:T(8,128)(2,1)} %get-tuple-element.204), channel_id=1, source_target_pairs={{0,4},{1,5},{2,6},{3,7},{4,0},{5,1},{6,2},{7,3},{8,12},{9,13},{10,... | collective-permute-start | bytes 393224 | tf_op jit(solution)/shard_map/ppermute | solution.py:390
  212.3 19.2 %collective-permute-start.68 = (bf16[32,16,128]{2,1,0:T(8,128)(2,1)}, bf16[32,16,128]{2,1,0:T(8,128)(2,1)S(1)}, u32[]{:S(2)}, u32[]{:S(2)}) collective-permute-start(bf16[32,16,128]{2,1,0:T(8,128)(2,1)} %get-tuple-element.205), channel_id=1, source_target_pairs={{0,5},{1,4},{2,7},{3,6},{4,1},{5,0},{6,3},{7,2},{8,13},{9,12},{10,... | collective-permute-start | bytes 393224 | tf_op jit(solution)/shard_map/ppermute | solution.py:390
  214.0 19.0 %collective-permute-start.69 = (bf16[32,16,128]{2,1,0:T(8,128)(2,1)}, bf16[32,16,128]{2,1,0:T(8,128)(2,1)S(1)}, u32[]{:S(2)}, u32[]{:S(2)}) collective-permute-start(bf16[32,16,128]{2,1,0:T(8,128)(2,1)} %get-tuple-element.206), channel_id=1, source_target_pairs={{0,6},{1,7},{2,4},{3,5},{4,2},{5,3},{6,0},{7,1},{8,14},{9,15},{10,... | collective-permute-start | bytes 393224 | tf_op jit(solution)/shard_map/ppermute | solution.py:390
  216.2 17.0 %collective-permute-start.70 = (bf16[32,16,128]{2,1,0:T(8,128)(2,1)}, bf16[32,16,128]{2,1,0:T(8,128)(2,1)S(1)}, u32[]{:S(2)}, u32[]{:S(2)}) collective-permute-start(bf16[32,16,128]{2,1,0:T(8,128)(2,1)} %get-tuple-element.207), channel_id=1, source_target_pairs={{0,7},{1,6},{2,5},{3,4},{4,3},{5,2},{6,1},{7,0},{8,15},{9,14},{10,... | collective-permute-start | bytes 393224 | tf_op jit(solution)/shard_map/ppermute | solution.py:390
  218.0 23.1 %collective-permute-start.51 = (bf16[32,16,128]{2,1,0:T(8,128)(2,1)}, bf16[32,16,128]{2,1,0:T(8,128)(2,1)S(1)}, u32[]{:S(2)}, u32[]{:S(2)}) collective-permute-start(bf16[32,16,128]{2,1,0:T(8,128)(2,1)} %get-tuple-element.184), channel_id=1, source_target_pairs={{0,1},{1,0},{2,3},{3,2},{4,5},{5,4},{6,7},{7,6},{8,9},{9,8},{10,11... | collective-permute-start | bytes 393224 | tf_op jit(solution)/shard_map/ppermute | solution.py:390
  233.1 27.6 %collective-permute-start.37 = (bf16[32,32,128]{2,1,0:T(8,128)(2,1)}, bf16[32,32,128]{2,1,0:T(8,128)(2,1)S(1)}, u32[]{:S(2)}, u32[]{:S(2)}) collective-permute-start(bf16[32,32,128]{2,1,0:T(8,128)(2,1)} %get-tuple-element.166), channel_id=1, source_target_pairs={{0,1},{1,0},{2,3},{3,2},{4,5},{5,4},{6,7},{7,6},{8,9},{9,8},{10,11... | collective-permute-start | bytes 786440 | tf_op jit(solution)/shard_map/ppermute | solution.py:390
  233.7 42.4 %collective-permute-start.38 = (bf16[32,32,128]{2,1,0:T(8,128)(2,1)S(1)}, bf16[32,32,128]{2,1,0:T(8,128)(2,1)S(1)}, u32[]{:S(2)}, u32[]{:S(2)}) collective-permute-start(bf16[32,32,128]{2,1,0:T(8,128)(2,1)S(1)} %copy-done.33), channel_id=1, source_target_pairs={{0,2},{1,3},{2,0},{3,1},{4,6},{5,7},{6,4},{7,5},{8,10},{9,11},{10,... | collective-permute-start | bytes 786440 | tf_op jit(solution)/shard_map/ppermute | solution.py:390
  250.8 40.4 %collective-permute-start.39 = (bf16[32,32,128]{2,1,0:T(8,128)(2,1)S(1)}, bf16[32,32,128]{2,1,0:T(8,128)(2,1)S(1)}, u32[]{:S(2)}, u32[]{:S(2)}) collective-permute-start(bf16[32,32,128]{2,1,0:T(8,128)(2,1)S(1)} %copy-done.32), channel_id=1, source_target_pairs={{0,4},{1,5},{2,6},{3,7},{4,0},{5,1},{6,2},{7,3},{8,12},{9,13},{10,... | collective-permute-start | bytes 786440 | tf_op jit(solution)/shard_map/ppermute | solution.py:390
  255.3 39.8 %collective-permute-start.40 = (bf16[32,32,128]{2,1,0:T(8,128)(2,1)S(1)}, bf16[32,32,128]{2,1,0:T(8,128)(2,1)S(1)}, u32[]{:S(2)}, u32[]{:S(2)}) collective-permute-start(bf16[32,32,128]{2,1,0:T(8,128)(2,1)S(1)} %copy-done.31), channel_id=1, source_target_pairs={{0,5},{1,4},{2,7},{3,6},{4,1},{5,0},{6,3},{7,2},{8,13},{9,12},{10,... | collective-permute-start | bytes 786440 | tf_op jit(solution)/shard_map/ppermute | solution.py:390
  258.8 37.2 %collective-permute-start.41 = (bf16[32,32,128]{2,1,0:T(8,128)(2,1)S(1)}, bf16[32,32,128]{2,1,0:T(8,128)(2,1)S(1)}, u32[]{:S(2)}, u32[]{:S(2)}) collective-permute-start(bf16[32,32,128]{2,1,0:T(8,128)(2,1)S(1)} %copy-done.30), channel_id=1, source_target_pairs={{0,6},{1,7},{2,4},{3,5},{4,2},{5,3},{6,0},{7,1},{8,14},{9,15},{10,... | collective-permute-start | bytes 786440 | tf_op jit(solution)/shard_map/ppermute | solution.py:390
  260.7 42.9 %collective-permute-start.42 = (bf16[32,32,128]{2,1,0:T(8,128)(2,1)S(1)}, bf16[32,32,128]{2,1,0:T(8,128)(2,1)S(1)}, u32[]{:S(2)}, u32[]{:S(2)}) collective-permute-start(bf16[32,32,128]{2,1,0:T(8,128)(2,1)S(1)} %copy-done.29), channel_id=1, source_target_pairs={{0,7},{1,6},{2,5},{3,4},{4,3},{5,2},{6,1},{7,0},{8,15},{9,14},{10,... | collective-permute-start | bytes 786440 | tf_op jit(solution)/shard_map/ppermute | solution.py:390
  276.1 38.1 %collective-permute-start.43 = (bf16[32,32,128]{2,1,0:T(8,128)(2,1)S(1)}, bf16[32,32,128]{2,1,0:T(8,128)(2,1)S(1)}, u32[]{:S(2)}, u32[]{:S(2)}) collective-permute-start(bf16[32,32,128]{2,1,0:T(8,128)(2,1)S(1)} %copy-done.28), channel_id=1, source_target_pairs={{0,3},{1,2},{2,1},{3,0},{4,7},{5,6},{6,5},{7,4},{8,11},{9,10},{10,... | collective-permute-start | bytes 786440 | tf_op jit(solution)/shard_map/ppermute | solution.py:390
  291.1 40.3 %collective-permute-start.44 = (bf16[32,32,128]{2,1,0:T(8,128)(2,1)}, bf16[32,32,128]{2,1,0:T(8,128)(2,1)S(1)}, u32[]{:S(2)}, u32[]{:S(2)}) collective-permute-start(bf16[32,32,128]{2,1,0:T(8,128)(2,1)} %get-tuple-element.174), channel_id=1, source_target_pairs={{0,1},{1,0},{2,3},{3,2},{4,5},{5,4},{6,7},{7,6},{8,9},{9,8},{10,11... | collective-permute-start | bytes 786440 | tf_op jit(solution)/shard_map/ppermute | solution.py:390
  295.1 36.8 %collective-permute-start.45 = (bf16[32,32,128]{2,1,0:T(8,128)(2,1)}, bf16[32,32,128]{2,1,0:T(8,128)(2,1)S(1)}, u32[]{:S(2)}, u32[]{:S(2)}) collective-permute-start(bf16[32,32,128]{2,1,0:T(8,128)(2,1)} %get-tuple-element.175), channel_id=1, source_target_pairs={{0,2},{1,3},{2,0},{3,1},{4,6},{5,7},{6,4},{7,5},{8,10},{9,11},{10,... | collective-permute-start | bytes 786440 | tf_op jit(solution)/shard_map/ppermute | solution.py:390
  296.0 35.8 %collective-permute-start.46 = (bf16[32,32,128]{2,1,0:T(8,128)(2,1)}, bf16[32,32,128]{2,1,0:T(8,128)(2,1)S(1)}, u32[]{:S(2)}, u32[]{:S(2)}) collective-permute-start(bf16[32,32,128]{2,1,0:T(8,128)(2,1)} %get-tuple-element.176), channel_id=1, source_target_pairs={{0,4},{1,5},{2,6},{3,7},{4,0},{5,1},{6,2},{7,3},{8,12},{9,13},{10,... | collective-permute-start | bytes 786440 | tf_op jit(solution)/shard_map/ppermute | solution.py:390
  303.6 30.2 %collective-permute-start.47 = (bf16[32,32,128]{2,1,0:T(8,128)(2,1)}, bf16[32,32,128]{2,1,0:T(8,128)(2,1)S(1)}, u32[]{:S(2)}, u32[]{:S(2)}) collective-permute-start(bf16[32,32,128]{2,1,0:T(8,128)(2,1)} %get-tuple-element.177), channel_id=1, source_target_pairs={{0,5},{1,4},{2,7},{3,6},{4,1},{5,0},{6,3},{7,2},{8,13},{9,12},{10,... | collective-permute-start | bytes 786440 | tf_op jit(solution)/shard_map/ppermute | solution.py:390
  314.2 15.4 %collective-permute-start.57 = (bf16[32,16,128]{2,1,0:T(8,128)(2,1)}, bf16[32,16,128]{2,1,0:T(8,128)(2,1)S(1)}, u32[]{:S(2)}, u32[]{:S(2)}) collective-permute-start(bf16[32,16,128]{2,1,0:T(8,128)(2,1)} %get-tuple-element.190), channel_id=1, source_target_pairs={{0,3},{1,2},{2,1},{3,0},{4,7},{5,6},{6,5},{7,4},{8,11},{9,10},{10,... | collective-permute-start | bytes 393224 | tf_op jit(solution)/shard_map/ppermute | solution.py:390
  331.4 19.6 %collective-permute-start.49 = (bf16[32,32,128]{2,1,0:T(8,128)(2,1)}, bf16[32,32,128]{2,1,0:T(8,128)(2,1)S(1)}, u32[]{:S(2)}, u32[]{:S(2)}) collective-permute-start(bf16[32,32,128]{2,1,0:T(8,128)(2,1)} %get-tuple-element.179), channel_id=1, source_target_pairs={{0,7},{1,6},{2,5},{3,4},{4,3},{5,2},{6,1},{7,0},{8,15},{9,14},{10,... | collective-permute-start | bytes 786440 | tf_op jit(solution)/shard_map/ppermute | solution.py:390
  331.9 25.4 %collective-permute-start.50 = (bf16[32,32,128]{2,1,0:T(8,128)(2,1)}, bf16[32,32,128]{2,1,0:T(8,128)(2,1)S(1)}, u32[]{:S(2)}, u32[]{:S(2)}) collective-permute-start(bf16[32,32,128]{2,1,0:T(8,128)(2,1)} %get-tuple-element.180), channel_id=1, source_target_pairs={{0,3},{1,2},{2,1},{3,0},{4,7},{5,6},{6,5},{7,4},{8,11},{9,10},{10,... | collective-permute-start | bytes 786440 | tf_op jit(solution)/shard_map/ppermute | solution.py:390
  331.9 26.9 %collective-permute-start.58 = (bf16[32,32,128]{2,1,0:T(8,128)(2,1)}, bf16[32,32,128]{2,1,0:T(8,128)(2,1)S(1)}, u32[]{:S(2)}, u32[]{:S(2)}) collective-permute-start(bf16[32,32,128]{2,1,0:T(8,128)(2,1)} %get-tuple-element.192), channel_id=1, source_target_pairs={{0,1},{1,0},{2,3},{3,2},{4,5},{5,4},{6,7},{7,6},{8,9},{9,8},{10,11... | collective-permute-start | bytes 786440 | tf_op jit(solution)/shard_map/ppermute | solution.py:390
  334.5 26.7 %collective-permute-start.59 = (bf16[32,32,128]{2,1,0:T(8,128)(2,1)}, bf16[32,32,128]{2,1,0:T(8,128)(2,1)S(1)}, u32[]{:S(2)}, u32[]{:S(2)}) collective-permute-start(bf16[32,32,128]{2,1,0:T(8,128)(2,1)} %get-tuple-element.193), channel_id=1, source_target_pairs={{0,2},{1,3},{2,0},{3,1},{4,6},{5,7},{6,4},{7,5},{8,10},{9,11},{10,... | collective-permute-start | bytes 786440 | tf_op jit(solution)/shard_map/ppermute | solution.py:390
  341.1 42.2 %collective-permute-start.60 = (bf16[32,32,128]{2,1,0:T(8,128)(2,1)}, bf16[32,32,128]{2,1,0:T(8,128)(2,1)}, u32[]{:S(2)}, u32[]{:S(2)}) collective-permute-start(bf16[32,32,128]{2,1,0:T(8,128)(2,1)} %get-tuple-element.194), channel_id=1, source_target_pairs={{0,4},{1,5},{2,6},{3,7},{4,0},{5,1},{6,2},{7,3},{8,12},{9,13},{10,... | collective-permute-start | bytes 786440 | tf_op jit(solution)/shard_map/ppermute | solution.py:390
  351.0 38.7 %collective-permute-start.61 = (bf16[32,32,128]{2,1,0:T(8,128)(2,1)}, bf16[32,32,128]{2,1,0:T(8,128)(2,1)}, u32[]{:S(2)}, u32[]{:S(2)}) collective-permute-start(bf16[32,32,128]{2,1,0:T(8,128)(2,1)} %get-tuple-element.195), channel_id=1, source_target_pairs={{0,5},{1,4},{2,7},{3,6},{4,1},{5,0},{6,3},{7,2},{8,13},{9,12},{10,... | collective-permute-start | bytes 786440 | tf_op jit(solution)/shard_map/ppermute | solution.py:390
  357.3 32.4 %collective-permute-start.62 = (bf16[32,32,128]{2,1,0:T(8,128)(2,1)}, bf16[32,32,128]{2,1,0:T(8,128)(2,1)}, u32[]{:S(2)}, u32[]{:S(2)}) collective-permute-start(bf16[32,32,128]{2,1,0:T(8,128)(2,1)} %get-tuple-element.196), channel_id=1, source_target_pairs={{0,6},{1,7},{2,4},{3,5},{4,2},{5,3},{6,0},{7,1},{8,14},{9,15},{10,... | collective-permute-start | bytes 786440 | tf_op jit(solution)/shard_map/ppermute | solution.py:390
  358.8 36.3 %collective-permute-start.63 = (bf16[32,32,128]{2,1,0:T(8,128)(2,1)}, bf16[32,32,128]{2,1,0:T(8,128)(2,1)}, u32[]{:S(2)}, u32[]{:S(2)}) collective-permute-start(bf16[32,32,128]{2,1,0:T(8,128)(2,1)} %get-tuple-element.197), channel_id=1, source_target_pairs={{0,7},{1,6},{2,5},{3,4},{4,3},{5,2},{6,1},{7,0},{8,15},{9,14},{10,... | collective-permute-start | bytes 786440 | tf_op jit(solution)/shard_map/ppermute | solution.py:390
  361.2 40.6 %collective-permute-start.64 = (bf16[32,32,128]{2,1,0:T(8,128)(2,1)}, bf16[32,32,128]{2,1,0:T(8,128)(2,1)}, u32[]{:S(2)}, u32[]{:S(2)}) collective-permute-start(bf16[32,32,128]{2,1,0:T(8,128)(2,1)} %get-tuple-element.198), channel_id=1, source_target_pairs={{0,3},{1,2},{2,1},{3,0},{4,7},{5,6},{6,5},{7,4},{8,11},{9,10},{10,... | collective-permute-start | bytes 786440 | tf_op jit(solution)/shard_map/ppermute | solution.py:390
  383.3 26.6 %collective-permute-start.71 = (bf16[32,16,128]{2,1,0:T(8,128)(2,1)}, bf16[32,16,128]{2,1,0:T(8,128)(2,1)S(1)}, u32[]{:S(2)}, u32[]{:S(2)}) collective-permute-start(bf16[32,16,128]{2,1,0:T(8,128)(2,1)} %get-tuple-element.208), channel_id=1, source_target_pairs={{0,3},{1,2},{2,1},{3,0},{4,7},{5,6},{6,5},{7,4},{8,11},{9,10},{10,... | collective-permute-start | bytes 393224 | tf_op jit(solution)/shard_map/ppermute | solution.py:390
  389.7 29.2 %collective-permute-start.72 = (bf16[32,16,128]{2,1,0:T(8,128)(2,1)}, bf16[32,16,128]{2,1,0:T(8,128)(2,1)S(1)}, u32[]{:S(2)}, u32[]{:S(2)}) collective-permute-start(bf16[32,16,128]{2,1,0:T(8,128)(2,1)} %get-tuple-element.210), channel_id=1, source_target_pairs={{0,1},{1,0},{2,3},{3,2},{4,5},{5,4},{6,7},{7,6},{8,9},{9,8},{10,11... | collective-permute-start | bytes 393224 | tf_op jit(solution)/shard_map/ppermute | solution.py:390
  389.7 30.9 %collective-permute-start.73 = (bf16[32,16,128]{2,1,0:T(8,128)(2,1)}, bf16[32,16,128]{2,1,0:T(8,128)(2,1)S(1)}, u32[]{:S(2)}, u32[]{:S(2)}) collective-permute-start(bf16[32,16,128]{2,1,0:T(8,128)(2,1)} %get-tuple-element.211), channel_id=1, source_target_pairs={{0,2},{1,3},{2,0},{3,1},{4,6},{5,7},{6,4},{7,5},{8,10},{9,11},{10,... | collective-permute-start | bytes 393224 | tf_op jit(solution)/shard_map/ppermute | solution.py:390
  395.0 25.5 %collective-permute-start.74 = (bf16[32,16,128]{2,1,0:T(8,128)(2,1)}, bf16[32,16,128]{2,1,0:T(8,128)(2,1)S(1)}, u32[]{:S(2)}, u32[]{:S(2)}) collective-permute-start(bf16[32,16,128]{2,1,0:T(8,128)(2,1)} %get-tuple-element.212), channel_id=1, source_target_pairs={{0,4},{1,5},{2,6},{3,7},{4,0},{5,1},{6,2},{7,3},{8,12},{9,13},{10,... | collective-permute-start | bytes 393224 | tf_op jit(solution)/shard_map/ppermute | solution.py:390
  401.8 19.5 %collective-permute-start.75 = (bf16[32,16,128]{2,1,0:T(8,128)(2,1)}, bf16[32,16,128]{2,1,0:T(8,128)(2,1)S(1)}, u32[]{:S(2)}, u32[]{:S(2)}) collective-permute-start(bf16[32,16,128]{2,1,0:T(8,128)(2,1)} %get-tuple-element.213), channel_id=1, source_target_pairs={{0,5},{1,4},{2,7},{3,6},{4,1},{5,0},{6,3},{7,2},{8,13},{9,12},{10,... | collective-permute-start | bytes 393224 | tf_op jit(solution)/shard_map/ppermute | solution.py:390
  409.9 23.1 %collective-permute-start.76 = (bf16[32,16,128]{2,1,0:T(8,128)(2,1)}, bf16[32,16,128]{2,1,0:T(8,128)(2,1)S(1)}, u32[]{:S(2)}, u32[]{:S(2)}) collective-permute-start(bf16[32,16,128]{2,1,0:T(8,128)(2,1)} %get-tuple-element.214), channel_id=1, source_target_pairs={{0,6},{1,7},{2,4},{3,5},{4,2},{5,3},{6,0},{7,1},{8,14},{9,15},{10,... | collective-permute-start | bytes 393224 | tf_op jit(solution)/shard_map/ppermute | solution.py:390
  420.6 15.3 %collective-permute-start.79 = (bf16[32,16,128]{2,1,0:T(8,128)(2,1)}, bf16[32,16,128]{2,1,0:T(8,128)(2,1)S(1)}, u32[]{:S(2)}, u32[]{:S(2)}) collective-permute-start(bf16[32,16,128]{2,1,0:T(8,128)(2,1)} %get-tuple-element.219), channel_id=1, source_target_pairs={{0,1},{1,0},{2,3},{3,2},{4,5},{5,4},{6,7},{7,6},{8,9},{9,8},{10,11... | collective-permute-start | bytes 393224 | tf_op jit(solution)/shard_map/ppermute | solution.py:390
  421.3 17.9 %collective-permute-start.80 = (bf16[32,16,128]{2,1,0:T(8,128)(2,1)}, bf16[32,16,128]{2,1,0:T(8,128)(2,1)S(1)}, u32[]{:S(2)}, u32[]{:S(2)}) collective-permute-start(bf16[32,16,128]{2,1,0:T(8,128)(2,1)} %get-tuple-element.220), channel_id=1, source_target_pairs={{0,2},{1,3},{2,0},{3,1},{4,6},{5,7},{6,4},{7,5},{8,10},{9,11},{10,... | collective-permute-start | bytes 393224 | tf_op jit(solution)/shard_map/ppermute | solution.py:390
  433.0 17.3 %collective-permute-start.81 = (bf16[32,16,128]{2,1,0:T(8,128)(2,1)}, bf16[32,16,128]{2,1,0:T(8,128)(2,1)S(1)}, u32[]{:S(2)}, u32[]{:S(2)}) collective-permute-start(bf16[32,16,128]{2,1,0:T(8,128)(2,1)} %get-tuple-element.221), channel_id=1, source_target_pairs={{0,4},{1,5},{2,6},{3,7},{4,0},{5,1},{6,2},{7,3},{8,12},{9,13},{10,... | collective-permute-start | bytes 393224 | tf_op jit(solution)/shard_map/ppermute | solution.py:390
  433.9 16.4 %collective-permute-start.82 = (bf16[32,16,128]{2,1,0:T(8,128)(2,1)}, bf16[32,16,128]{2,1,0:T(8,128)(2,1)S(1)}, u32[]{:S(2)}, u32[]{:S(2)}) collective-permute-start(bf16[32,16,128]{2,1,0:T(8,128)(2,1)} %get-tuple-element.222), channel_id=1, source_target_pairs={{0,5},{1,4},{2,7},{3,6},{4,1},{5,0},{6,3},{7,2},{8,13},{9,12},{10,... | collective-permute-start | bytes 393224 | tf_op jit(solution)/shard_map/ppermute | solution.py:390
  433.9 16.4 %collective-permute-start.83 = (bf16[32,16,128]{2,1,0:T(8,128)(2,1)}, bf16[32,16,128]{2,1,0:T(8,128)(2,1)S(1)}, u32[]{:S(2)}, u32[]{:S(2)}) collective-permute-start(bf16[32,16,128]{2,1,0:T(8,128)(2,1)} %get-tuple-element.223), channel_id=1, source_target_pairs={{0,6},{1,7},{2,4},{3,5},{4,2},{5,3},{6,0},{7,1},{8,14},{9,15},{10,... | collective-permute-start | bytes 393224 | tf_op jit(solution)/shard_map/ppermute | solution.py:390
  (101 other events, 2951.5 us)

commit v16 on v12

--- a/solution.py
+++ b/solution.py
@@ -424,7 +424,7 @@
     chunks = chunks_of(receivers)
     sides = edges(estimate, observed)
     last, updated, energy = levels, None, 0.0
-    lag = 1
+    lag = 2
     ahead, behind = {}, {}
     for turn in range(len(chunks) + 2 * lag):
         if turn < len(chunks):

time: 433 us -> 423 us (0.977)
  waiting for transfers between devices: 150 us -> 108 us
  starting transfers between devices: 95.6 us -> 130 us
    ppermute x70, waiting for transfers between devices: 147 us -> 105 us  [exchanged(): lax.ppermute(arrays[slot], 'shot', [(i, i ^ slot) for i in range(peers)])]
    ppermute x70, starting transfers between devices: 91.9 us -> 126 us  [exchanged(): lax.ppermute(arrays[slot], 'shot', [(i, i ^ slot) for i in range(peers)])]
    unnamed x114 -> x154, local copies, waits for them, and re-layouts: 19.5 us -> 16.7 us
  transfers between devices with their start and end apart: 72 -> 72, of which waited for: 20 -> 18; matrix products, arithmetic and copies ran while one was open for 1% -> 1% of each run, Pallas kernels for 30% -> 32%
where the time goes in v16:
time: 423 us; the launch traced here: 421 us
  Pallas kernels  149 us (35%)
  starting transfers between devices  130 us (31%)
  waiting for transfers between devices  108 us (26%)
  local copies, waits for them, and re-layouts  20.4 us (5%)
  blocking collectives  9.91 us (2%)
    ppermute x70, starting transfers between devices, exchanged(): lax.ppermute(arrays[slot], 'shot', [(i, i ^ slot) for i in range(peers)])  126 us
    ppermute x70, waiting for transfers between devices, exchanged(): lax.ppermute(arrays[slot], 'shot', [(i, i ^ slot) for i in range(peers)])  105 us
    pallas_call x5, Pallas kernels, spectra_of(): pl.pallas_call(spectra_kernel, grid_spec=pltpu.PrefetchScalarGridSpec(num...  64.6 us
    pallas_call x5, Pallas kernels, shrunk_of(): pl.pallas_call(shots_kernel, grid_spec=pltpu.PrefetchScalarGridSpec(num_s...  58.6 us
    pallas_call x5, Pallas kernels, updated_of(): pl.pallas_call(functools.partial(update_kernel, len(restored)), grid_spec...  26 us
    unnamed x154, local copies, waits for them, and re-layouts  16.7 us
    psum x1, blocking collectives, local(): lax.psum(jnp.sum(energy, axis=1), 'patch')  9.91 us
  transfers between devices with their start and end apart: 72, of which 18 were waited for; matrix products, arithmetic and copies ran while one was open for 1% of the time, Pallas kernels for 32%

profile of v16, /device:TPU:0, one launch (start us, length us, event | category | flops | bytes accessed | tf_op | source)
XLA Modules:
  0.0 421.1 jit_solution(17591101273273869995)
XLA Ops:
  1.7 1.3 fusion
  3.1 2.4 collective-permute-start
  6.4 1.3 collective-permute-start.1
  9.8 3.2 collective-permute-done.1.after_ref
  13.8 9.9 %spectra.5 = (bf16[32,16,128]{2,1,0:T(8,128)(2,1)}, bf16[32,16,128]{2,1,0:T(8,128)(2,1)}, bf16[32,16,128]{2,1,0:T(8,128)(2,1)}, bf16[32,16,128]{2,1,0:T(8,128)(2...) custom-call(s32[9]{0:T(128)} %pad_add_fusion.meta_ref, ...), custom_call_target="tpu_custom_call" | custom-call | flops 1073741824 | bytes 5242880 | tf_op jit(solution)/shard_map/spectra/pallas_call | solution.py:270
  23.7 10.5 %collective-permute-start.2 = (bf16[32,16,128]{2,1,0:T(8,128)(2,1)}, bf16[32,16,128]{2,1,0:T(8,128)(2,1)S(1)}, u32[]{:S(2)}, u32[]{:S(2)}) collective-permute-start(bf16[32,16,128]{2,1,0:T(8,128)(2,1)} %get-tuple-element.100), channel_id=1, source_target_pairs={{0,4},{1,5},{2,6},{3,7},{4,0},{5,1},{6,2},{7,3},{8,12},{9,13},{10,... | collective-permute-start | bytes 393224 | tf_op jit(solution)/shard_map/ppermute | solution.py:392
  34.2 1.5 collective-permute-start.3
  35.7 1.5 collective-permute-start.5
  37.2 14.9 %spectra.6 = (bf16[32,32,128]{2,1,0:T(8,128)(2,1)}, bf16[32,32,128]{2,1,0:T(8,128)(2,1)}, bf16[32,32,128]{2,1,0:T(8,128)(2,1)}, bf16[32,32,128]{2,1,0:T(8,128)(2...) custom-call(s32[9]{0:T(128)} %pad_add_fusion.meta_ref, ...), custom_call_target="tpu_custom_call" | custom-call | flops 2147483648 | bytes 8388608 | tf_op jit(solution)/shard_map/spectra/pallas_call | solution.py:270
  52.1 1.6 collective-permute-start.9
  53.8 1.3 collective-permute-start.6
  55.6 2.4 collective-permute-start.8
  58.0 7.2 %collective-permute-done.6.refs_5_ = bf16[32,16,128]{2,1,0:T(8,128)(2,1)S(1)} collective-permute-done((bf16[32,16,128]{2,1,0:T(8,128)(2,1)S(1)}, bf16[32,16,128]{2,1,0:T(8,128)(2,1)S(1)}, u32[]{:S(2)}, u32[]{:S(2)}) %collective-permute-start.6) | collective-permute-done | bytes 131104 | tf_op jit(solution)/shard_map/ppermute | solution.py:392
  65.2 11.5 %collective-permute-start.11 = (bf16[32,32,128]{2,1,0:T(8,128)(2,1)}, bf16[32,32,128]{2,1,0:T(8,128)(2,1)S(1)}, u32[]{:S(2)}, u32[]{:S(2)}) collective-permute-start(bf16[32,32,128]{2,1,0:T(8,128)(2,1)} %get-tuple-element.112), channel_id=1, source_target_pairs={{0,5},{1,4},{2,7},{3,6},{4,1},{5,0},{6,3},{7,2},{8,13},{9,12},{10,... | collective-permute-start | bytes 786440 | tf_op jit(solution)/shard_map/ppermute | solution.py:392
  76.7 1.9 collective-permute-start.13
  79.8 1.8 collective-permute-start.15
  81.6 14.7 %spectra.7 = (bf16[32,32,128]{2,1,0:T(8,128)(2,1)}, bf16[32,32,128]{2,1,0:T(8,128)(2,1)}, bf16[32,32,128]{2,1,0:T(8,128)(2,1)}, bf16[32,32,128]{2,1,0:T(8,128)(2...) custom-call(s32[9]{0:T(128)} %pad_add_fusion.meta_ref, ...), custom_call_target="tpu_custom_call" | custom-call | flops 2147483648 | bytes 8388608 | tf_op jit(solution)/shard_map/spectra/pallas_call | solution.py:270
  96.4 7.2 %shrink.5 = (bf16[32,16,128]{2,1,0:T(8,128)(2,1)}, bf16[32,16,128]{2,1,0:T(8,128)(2,1)}, bf16[32,16,128]{2,1,0:T(8,128)(2,1)}, bf16[32,16,128]{2,1,0:T(8,128)(2,...) custom-call(s32[9]{0:T(128)} %pad_add_fusion.meta_ref, ...), custom_call_target="tpu_custom_call" | custom-call | flops 1073741824 | bytes 2359296 | tf_op jit(solution)/shard_map/shrink/pallas_call | solution.py:320
  104.0 2.8 collective-permute-start.25
  107.9 11.2 %collective-permute-start.16 = (bf16[32,32,128]{2,1,0:T(8,128)(2,1)}, bf16[32,32,128]{2,1,0:T(8,128)(2,1)S(1)}, u32[]{:S(2)}, u32[]{:S(2)}) collective-permute-start(bf16[32,32,128]{2,1,0:T(8,128)(2,1)} %get-tuple-element.120), channel_id=1, source_target_pairs={{0,4},{1,5},{2,6},{3,7},{4,0},{5,1},{6,2},{7,3},{8,12},{9,13},{10,... | collective-permute-start | bytes 786440 | tf_op jit(solution)/shard_map/ppermute | solution.py:392
  119.1 2.0 collective-permute-done.23.refs_1_
  122.4 1.9 collective-permute-start.27
  124.3 7.1 %collective-permute-done.25.refs_3_ = bf16[32,16,128]{2,1,0:T(8,128)(2,1)S(1)} collective-permute-done((bf16[32,16,128]{2,1,0:T(8,128)(2,1)}, bf16[32,16,128]{2,1,0:T(8,128)(2,1)S(1)}, u32[]{:S(2)}, u32[]{:S(2)}) %collective-permute-start.25) | collective-permute-done | bytes 131104 | tf_op jit(solution)/shard_map/ppermute | solution.py:392
  132.7 2.4 collective-permute-start.29
  135.1 14.7 %spectra.8 = (bf16[32,32,128]{2,1,0:T(8,128)(2,1)}, bf16[32,32,128]{2,1,0:T(8,128)(2,1)}, bf16[32,32,128]{2,1,0:T(8,128)(2,1)}, bf16[32,32,128]{2,1,0:T(8,128)(2...) custom-call(s32[9]{0:T(128)} %pad_add_fusion.meta_ref, ...), custom_call_target="tpu_custom_call" | custom-call | flops 2147483648 | bytes 8388608 | tf_op jit(solution)/shard_map/spectra/pallas_call | solution.py:270
  151.6 2.7 collective-permute-start.20
  154.4 1.4 collective-permute-start.22
  155.8 14.7 %shrink.6 = (bf16[32,32,128]{2,1,0:T(8,128)(2,1)}, bf16[32,32,128]{2,1,0:T(8,128)(2,1)}, bf16[32,32,128]{2,1,0:T(8,128)(2,1)}, bf16[32,32,128]{2,1,0:T(8,128)(2,...) custom-call(s32[9]{0:T(128)} %pad_add_fusion.meta_ref, ...), custom_call_target="tpu_custom_call" | custom-call | flops 2147483648 | bytes 4456448 | tf_op jit(solution)/shard_map/shrink/pallas_call | solution.py:320
  170.6 10.4 %spectra.9 = (bf16[32,16,128]{2,1,0:T(8,128)(2,1)}, bf16[32,16,128]{2,1,0:T(8,128)(2,1)}, bf16[32,16,128]{2,1,0:T(8,128)(2,1)}, bf16[32,16,128]{2,1,0:T(8,128)(2...) custom-call(s32[9]{0:T(128)} %pad_add_fusion.meta_ref, ...), custom_call_target="tpu_custom_call" | custom-call | flops 1073741824 | bytes 5242880 | tf_op jit(solution)/shard_map/spectra/pallas_call | solution.py:270
  181.1 1.9 collective-permute-start.44
  184.7 2.7 collective-permute-start.48
  187.4 12.1 %collective-permute-done.44.refs_1_ = bf16[32,16,128]{2,1,0:T(8,128)(2,1)S(1)} collective-permute-done((bf16[32,16,128]{2,1,0:T(8,128)(2,1)}, bf16[32,16,128]{2,1,0:T(8,128)(2,1)S(1)}, u32[]{:S(2)}, u32[]{:S(2)}) %collective-permute-start.44) | collective-permute-done | bytes 131104 | tf_op jit(solution)/shard_map/ppermute | solution.py:392
  199.6 1.6 collective-permute-done.46.refs_3_
  201.3 1.4 collective-permute-start.32
  203.8 13.3 %collective-permute-start.50 = (bf16[32,16,128]{2,1,0:T(8,128)(2,1)}, bf16[32,16,128]{2,1,0:T(8,128)(2,1)}, u32[]{:S(2)}, u32[]{:S(2)}) collective-permute-start(bf16[32,16,128]{2,1,0:T(8,128)(2,1)} %get-tuple-element.161), channel_id=1, source_target_pairs={{0,7},{1,6},{2,5},{3,4},{4,3},{5,2},{6,1},{7,0},{8,15},{9,14},{10,... | collective-permute-start | bytes 393224 | tf_op jit(solution)/shard_map/ppermute | solution.py:392
  217.2 14.8 %shrink.7 = (bf16[32,32,128]{2,1,0:T(8,128)(2,1)}, bf16[32,32,128]{2,1,0:T(8,128)(2,1)}, bf16[32,32,128]{2,1,0:T(8,128)(2,1)}, bf16[32,32,128]{2,1,0:T(8,128)(2,...) custom-call(s32[9]{0:T(128)} %pad_add_fusion.meta_ref, ...), custom_call_target="tpu_custom_call" | custom-call | flops 2147483648 | bytes 4456448 | tf_op jit(solution)/shard_map/shrink/pallas_call | solution.py:320
  233.6 3.1 collective-permute-start.36
  236.8 10.2 %collective-permute-done.33.refs_4_ = bf16[32,32,128]{2,1,0:T(8,128)(2,1)S(1)} collective-permute-done((bf16[32,32,128]{2,1,0:T(8,128)(2,1)S(1)}, bf16[32,32,128]{2,1,0:T(8,128)(2,1)S(1)}, u32[]{:S(2)}, u32[]{:S(2)}) %collective-permute-start.33) | collective-permute-done | bytes 262176 | tf_op jit(solution)/shard_map/ppermute | solution.py:392
  247.0 3.5 collective-permute-done.35.refs_6_
  250.5 7.5 %collective-permute-done.36.refs_7_ = bf16[32,32,128]{2,1,0:T(8,128)(2,1)S(1)} collective-permute-done((bf16[32,32,128]{2,1,0:T(8,128)(2,1)S(1)}, bf16[32,32,128]{2,1,0:T(8,128)(2,1)S(1)}, u32[]{:S(2)}, u32[]{:S(2)}) %collective-permute-start.36) | collective-permute-done | bytes 262176 | tf_op jit(solution)/shard_map/ppermute | solution.py:392
  258.1 12.4 %collective-permute-start.37 = (bf16[32,32,128]{2,1,0:T(8,128)(2,1)}, bf16[32,32,128]{2,1,0:T(8,128)(2,1)S(1)}, u32[]{:S(2)}, u32[]{:S(2)}) collective-permute-start(bf16[32,32,128]{2,1,0:T(8,128)(2,1)} %get-tuple-element.145), channel_id=1, source_target_pairs={{0,4},{1,5},{2,6},{3,7},{4,0},{5,1},{6,2},{7,3},{8,12},{9,13},{10,... | collective-permute-start | bytes 786440 | tf_op jit(solution)/shard_map/ppermute | solution.py:392
  270.4 11.7 %collective-permute-done.51.refs_1_ = bf16[32,32,128]{2,1,0:T(8,128)(2,1)S(1)} collective-permute-done((bf16[32,32,128]{2,1,0:T(8,128)(2,1)}, bf16[32,32,128]{2,1,0:T(8,128)(2,1)S(1)}, u32[]{:S(2)}, u32[]{:S(2)}) %collective-permute-start.51) | collective-permute-done | bytes 262176 | tf_op jit(solution)/shard_map/ppermute | solution.py:392
  282.2 1.8 collective-permute-done.53.refs_3_
  284.0 7.5 %collective-permute-start.40 = (bf16[32,32,128]{2,1,0:T(8,128)(2,1)}, bf16[32,32,128]{2,1,0:T(8,128)(2,1)}, u32[]{:S(2)}, u32[]{:S(2)}) collective-permute-start(bf16[32,32,128]{2,1,0:T(8,128)(2,1)} %get-tuple-element.148), channel_id=1, source_target_pairs={{0,2},{1,3},{2,0},{3,1},{4,6},{5,7},{6,4},{7,5},{8,10},{9,11},{10,... | collective-permute-start | bytes 786440 | tf_op jit(solution)/shard_map/ppermute | solution.py:392
  291.5 3.0 collective-permute-start.41
  294.5 4.6 %collective-permute-done.37.refs_1_ = bf16[32,32,128]{2,1,0:T(8,128)(2,1)S(1)} collective-permute-done((bf16[32,32,128]{2,1,0:T(8,128)(2,1)}, bf16[32,32,128]{2,1,0:T(8,128)(2,1)S(1)}, u32[]{:S(2)}, u32[]{:S(2)}) %collective-permute-start.37) | collective-permute-done | bytes 262176 | tf_op jit(solution)/shard_map/ppermute | solution.py:392
  307.9 3.2 update.5
  311.7 14.7 %shrink.8 = (bf16[32,32,128]{2,1,0:T(8,128)(2,1)}, bf16[32,32,128]{2,1,0:T(8,128)(2,1)}, bf16[32,32,128]{2,1,0:T(8,128)(2,1)}, bf16[32,32,128]{2,1,0:T(8,128)(2,...) custom-call(s32[9]{0:T(128)} %pad_add_fusion.meta_ref, ...), custom_call_target="tpu_custom_call" | custom-call | flops 2147483648 | bytes 4456448 | tf_op jit(solution)/shard_map/shrink/pallas_call | solution.py:320
  327.5 2.6 collective-permute-start.57
  330.5 1.8 collective-permute-start.59
  335.2 6.5 %update.6 = (f32[32,128,1024]{2,1,0:T(8,128)}, f32[8,128]{1,0:T(8,128)S(1)}) custom-call(s32[9]{0:T(128)S(1)} %copy-done.13, bf16[1024,1024]{1,0:T(8,128)(2,1)S(1)} %copy-done, bf16[32,32,128]{2,1,0:T(8,128)(2,1)S(1)} %copy-done.2, bf16[32,32,128]{2,1,0:T(8,128)(2,1)S(1)} %copy-done.1, ...), custom_call_target="tpu_custom_call", output_to_operand_aliasing={{0}: (11, {})} | custom-call | flops 2147483648 | bytes 8388608 | tf_op jit(solution)/shard_map/update/pallas_call | solution.py:351
  342.3 7.2 %shrink.9 = (bf16[32,16,128]{2,1,0:T(8,128)(2,1)}, bf16[32,16,128]{2,1,0:T(8,128)(2,1)}, bf16[32,16,128]{2,1,0:T(8,128)(2,1)}, bf16[32,16,128]{2,1,0:T(8,128)(2,...) custom-call(s32[9]{0:T(128)} %pad_add_fusion.meta_ref, ...), custom_call_target="tpu_custom_call" | custom-call | flops 1073741824 | bytes 2359296 | tf_op jit(solution)/shard_map/shrink/pallas_call | solution.py:320
  350.7 9.9 %psum.7 = f32[32]{0:T(128)S(1)} all-reduce(f32[32]{0:T(128)S(1)} %add_reduce_fusion), channel_id=1, replica_groups=mesh['patch'=4,'shot'=8] {'patch'}, use_global_device_ids=true, to_apply=%region_1.0 | all-reduce | flops 32 | bytes 256 | tf_op jit(solution)/shard_map/psum | solution.py:517
  360.7 1.9 collective-permute-start.60
  362.6 13.0 %collective-permute-done.65.refs_1_ = bf16[32,16,128]{2,1,0:T(8,128)(2,1)S(1)} collective-permute-done((bf16[32,16,128]{2,1,0:T(8,128)(2,1)}, bf16[32,16,128]{2,1,0:T(8,128)(2,1)S(1)}, u32[]{:S(2)}, u32[]{:S(2)}) %collective-permute-start.65) | collective-permute-done | bytes 131104 | tf_op jit(solution)/shard_map/ppermute | solution.py:392
  375.5 2.5 collective-permute-start.62
  378.1 2.1 collective-permute-start.64
  381.7 6.2 %update.7 = (f32[32,128,1024]{2,1,0:T(8,128)}, f32[8,128]{1,0:T(8,128)S(1)}) custom-call(s32[9]{0:T(128)S(1)} %copy-done.14, bf16[1024,1024]{1,0:T(8,128)(2,1)S(1)} %copy-done, bf16[32,16,128]{2,1,0:T(8,128)(2,1)S(1)} %copy-done.4, bf16[32,32,128]{2,1,0:T(8,128)(2,1)S(1)} %copy-done.6, ...), custom_call_target="tpu_custom_call", output_to_operand_aliasing={{0}: (11, {})} | custom-call | flops 2147483648 | bytes 8388608 | tf_op jit(solution)/shard_map/update/pallas_call | solution.py:351
  388.2 5.7 %collective-permute-done.61.refs_4_ = bf16[32,32,128]{2,1,0:T(8,128)(2,1)S(1)} collective-permute-done((bf16[32,32,128]{2,1,0:T(8,128)(2,1)}, bf16[32,32,128]{2,1,0:T(8,128)(2,1)S(1)}, u32[]{:S(2)}, u32[]{:S(2)}) %collective-permute-start.61) | collective-permute-done | bytes 262176 | tf_op jit(solution)/shard_map/ppermute | solution.py:392
  394.1 10.3 %collective-permute-done.63.refs_6_ = bf16[32,32,128]{2,1,0:T(8,128)(2,1)S(1)} collective-permute-done((bf16[32,32,128]{2,1,0:T(8,128)(2,1)}, bf16[32,32,128]{2,1,0:T(8,128)(2,1)S(1)}, u32[]{:S(2)}, u32[]{:S(2)}) %collective-permute-start.63) | collective-permute-done | bytes 262176 | tf_op jit(solution)/shard_map/ppermute | solution.py:392
  405.4 6.1 %update.8 = (f32[32,128,1024]{2,1,0:T(8,128)}, f32[8,128]{1,0:T(8,128)S(1)}) custom-call(s32[9]{0:T(128)S(1)} %copy-done.14, bf16[1024,1024]{1,0:T(8,128)(2,1)S(1)} %copy-done, f32[8,128]{1,0:T(8,128)S(1)} %get-tuple-element.171._, bf16[32,32,128]{2,1,0:T(8,128)(2,1)S(1)} %copy-done.3, ...), custom_call_target="tpu_custom_call", output_to_operand_aliasing={{0}: (11, {})} | custom-call | flops 2147483648 | bytes 8388608 | tf_op jit(solution)/shard_map/update/pallas_call | solution.py:351
  411.5 2.4 collective-permute-done.67.refs_3_
  413.9 3.1 collective-permute-done.70.refs_6_
  417.1 4.1 update.9
  (261 shorter events, 36.1 us)
Async XLA Ops:
  23.7 30.0 %collective-permute-start.2 = (bf16[32,16,128]{2,1,0:T(8,128)(2,1)}, bf16[32,16,128]{2,1,0:T(8,128)(2,1)S(1)}, u32[]{:S(2)}, u32[]{:S(2)}) collective-permute-start(bf16[32,16,128]{2,1,0:T(8,128)(2,1)} %get-tuple-element.100), channel_id=1, source_target_pairs={{0,4},{1,5},{2,6},{3,7},{4,0},{5,1},{6,2},{7,3},{8,12},{9,13},{10,... | collective-permute-start | bytes 393224 | tf_op jit(solution)/shard_map/ppermute | solution.py:392
  34.2 19.5 %collective-permute-start.3 = (bf16[32,16,128]{2,1,0:T(8,128)(2,1)}, bf16[32,16,128]{2,1,0:T(8,128)(2,1)S(1)}, u32[]{:S(2)}, u32[]{:S(2)}) collective-permute-start(bf16[32,16,128]{2,1,0:T(8,128)(2,1)} %get-tuple-element.101), channel_id=1, source_target_pairs={{0,1},{1,0},{2,3},{3,2},{4,5},{5,4},{6,7},{7,6},{8,9},{9,8},{10,11... | collective-permute-start | bytes 393224 | tf_op jit(solution)/shard_map/ppermute | solution.py:392
  35.7 19.4 %collective-permute-start.4 = (bf16[32,16,128]{2,1,0:T(8,128)(2,1)}, bf16[32,16,128]{2,1,0:T(8,128)(2,1)S(1)}, u32[]{:S(2)}, u32[]{:S(2)}) collective-permute-start(bf16[32,16,128]{2,1,0:T(8,128)(2,1)} %get-tuple-element.102), channel_id=1, source_target_pairs={{0,5},{1,4},{2,7},{3,6},{4,1},{5,0},{6,3},{7,2},{8,13},{9,12},{10,... | collective-permute-start | bytes 393224 | tf_op jit(solution)/shard_map/ppermute | solution.py:392
  35.7 19.9 %collective-permute-start.5 = (bf16[32,16,128]{2,1,0:T(8,128)(2,1)}, bf16[32,16,128]{2,1,0:T(8,128)(2,1)S(1)}, u32[]{:S(2)}, u32[]{:S(2)}) collective-permute-start(bf16[32,16,128]{2,1,0:T(8,128)(2,1)} %get-tuple-element.103), channel_id=1, source_target_pairs={{0,2},{1,3},{2,0},{3,1},{4,6},{5,7},{6,4},{7,5},{8,10},{9,11},{10,... | collective-permute-start | bytes 393224 | tf_op jit(solution)/shard_map/ppermute | solution.py:392
  52.1 26.5 %collective-permute-start.9 = (bf16[32,32,128]{2,1,0:T(8,128)(2,1)}, bf16[32,32,128]{2,1,0:T(8,128)(2,1)S(1)}, u32[]{:S(2)}, u32[]{:S(2)}) collective-permute-start(bf16[32,32,128]{2,1,0:T(8,128)(2,1)} %get-tuple-element.110), channel_id=1, source_target_pairs={{0,4},{1,5},{2,6},{3,7},{4,0},{5,1},{6,2},{7,3},{8,12},{9,13},{10,... | collective-permute-start | bytes 786440 | tf_op jit(solution)/shard_map/ppermute | solution.py:392
  53.8 26.0 %collective-permute-start.10 = (bf16[32,32,128]{2,1,0:T(8,128)(2,1)}, bf16[32,32,128]{2,1,0:T(8,128)(2,1)S(1)}, u32[]{:S(2)}, u32[]{:S(2)}) collective-permute-start(bf16[32,32,128]{2,1,0:T(8,128)(2,1)} %get-tuple-element.111), channel_id=1, source_target_pairs={{0,1},{1,0},{2,3},{3,2},{4,5},{5,4},{6,7},{7,6},{8,9},{9,8},{10,11... | collective-permute-start | bytes 786440 | tf_op jit(solution)/shard_map/ppermute | solution.py:392
  55.1 21.5 %collective-permute-start.7 = (bf16[32,16,128]{2,1,0:T(8,128)(2,1)S(1)}, bf16[32,16,128]{2,1,0:T(8,128)(2,1)S(1)}, u32[]{:S(2)}, u32[]{:S(2)}) collective-permute-start(bf16[32,16,128]{2,1,0:T(8,128)(2,1)S(1)} %copy-done.73), channel_id=1, source_target_pairs={{0,3},{1,2},{2,1},{3,0},{4,7},{5,6},{6,5},{7,4},{8,11},{9,10},{10,... | collective-permute-start | bytes 393224 | tf_op jit(solution)/shard_map/ppermute | solution.py:392
  55.6 21.1 %collective-permute-start.8 = (bf16[32,16,128]{2,1,0:T(8,128)(2,1)S(1)}, bf16[32,16,128]{2,1,0:T(8,128)(2,1)S(1)}, u32[]{:S(2)}, u32[]{:S(2)}) collective-permute-start(bf16[32,16,128]{2,1,0:T(8,128)(2,1)S(1)} %copy-done.71), channel_id=1, source_target_pairs={{0,7},{1,6},{2,5},{3,4},{4,3},{5,2},{6,1},{7,0},{8,15},{9,14},{10,... | collective-permute-start | bytes 393224 | tf_op jit(solution)/shard_map/ppermute | solution.py:392
  65.2 38.4 %collective-permute-start.11 = (bf16[32,32,128]{2,1,0:T(8,128)(2,1)}, bf16[32,32,128]{2,1,0:T(8,128)(2,1)S(1)}, u32[]{:S(2)}, u32[]{:S(2)}) collective-permute-start(bf16[32,32,128]{2,1,0:T(8,128)(2,1)} %get-tuple-element.112), channel_id=1, source_target_pairs={{0,5},{1,4},{2,7},{3,6},{4,1},{5,0},{6,3},{7,2},{8,13},{9,12},{10,... | collective-permute-start | bytes 786440 | tf_op jit(solution)/shard_map/ppermute | solution.py:392
  76.7 27.3 %collective-permute-start.12 = (bf16[32,32,128]{2,1,0:T(8,128)(2,1)}, bf16[32,32,128]{2,1,0:T(8,128)(2,1)S(1)}, u32[]{:S(2)}, u32[]{:S(2)}) collective-permute-start(bf16[32,32,128]{2,1,0:T(8,128)(2,1)} %get-tuple-element.113), channel_id=1, source_target_pairs={{0,2},{1,3},{2,0},{3,1},{4,6},{5,7},{6,4},{7,5},{8,10},{9,11},{10,... | collective-permute-start | bytes 786440 | tf_op jit(solution)/shard_map/ppermute | solution.py:392
  76.7 27.3 %collective-permute-start.13 = (bf16[32,32,128]{2,1,0:T(8,128)(2,1)}, bf16[32,32,128]{2,1,0:T(8,128)(2,1)S(1)}, u32[]{:S(2)}, u32[]{:S(2)}) collective-permute-start(bf16[32,32,128]{2,1,0:T(8,128)(2,1)} %get-tuple-element.114), channel_id=1, source_target_pairs={{0,6},{1,7},{2,4},{3,5},{4,2},{5,3},{6,0},{7,1},{8,14},{9,15},{10,... | collective-permute-start | bytes 786440 | tf_op jit(solution)/shard_map/ppermute | solution.py:392
  78.6 28.1 %collective-permute-start.14 = (bf16[32,32,128]{2,1,0:T(8,128)(2,1)}, bf16[32,32,128]{2,1,0:T(8,128)(2,1)S(1)}, u32[]{:S(2)}, u32[]{:S(2)}) collective-permute-start(bf16[32,32,128]{2,1,0:T(8,128)(2,1)} %get-tuple-element.115), channel_id=1, source_target_pairs={{0,3},{1,2},{2,1},{3,0},{4,7},{5,6},{6,5},{7,4},{8,11},{9,10},{10,... | collective-permute-start | bytes 786440 | tf_op jit(solution)/shard_map/ppermute | solution.py:392
  79.8 28.1 %collective-permute-start.15 = (bf16[32,32,128]{2,1,0:T(8,128)(2,1)}, bf16[32,32,128]{2,1,0:T(8,128)(2,1)S(1)}, u32[]{:S(2)}, u32[]{:S(2)}) collective-permute-start(bf16[32,32,128]{2,1,0:T(8,128)(2,1)} %get-tuple-element.116), channel_id=1, source_target_pairs={{0,7},{1,6},{2,5},{3,4},{4,3},{5,2},{6,1},{7,0},{8,15},{9,14},{10,... | collective-permute-start | bytes 786440 | tf_op jit(solution)/shard_map/ppermute | solution.py:392
  103.6 17.5 %collective-permute-start.23 = (bf16[32,16,128]{2,1,0:T(8,128)(2,1)}, bf16[32,16,128]{2,1,0:T(8,128)(2,1)S(1)}, u32[]{:S(2)}, u32[]{:S(2)}) collective-permute-start(bf16[32,16,128]{2,1,0:T(8,128)(2,1)} %get-tuple-element.128), channel_id=1, source_target_pairs={{0,4},{1,5},{2,6},{3,7},{4,0},{5,1},{6,2},{7,3},{8,12},{9,13},{10,... | collective-permute-start | bytes 393224 | tf_op jit(solution)/shard_map/ppermute | solution.py:392
  104.0 17.8 %collective-permute-start.24 = (bf16[32,16,128]{2,1,0:T(8,128)(2,1)}, bf16[32,16,128]{2,1,0:T(8,128)(2,1)S(1)}, u32[]{:S(2)}, u32[]{:S(2)}) collective-permute-start(bf16[32,16,128]{2,1,0:T(8,128)(2,1)} %get-tuple-element.129), channel_id=1, source_target_pairs={{0,1},{1,0},{2,3},{3,2},{4,5},{5,4},{6,7},{7,6},{8,9},{9,8},{10,11... | collective-permute-start | bytes 393224 | tf_op jit(solution)/shard_map/ppermute | solution.py:392
  104.0 27.4 %collective-permute-start.25 = (bf16[32,16,128]{2,1,0:T(8,128)(2,1)}, bf16[32,16,128]{2,1,0:T(8,128)(2,1)S(1)}, u32[]{:S(2)}, u32[]{:S(2)}) collective-permute-start(bf16[32,16,128]{2,1,0:T(8,128)(2,1)} %get-tuple-element.130), channel_id=1, source_target_pairs={{0,5},{1,4},{2,7},{3,6},{4,1},{5,0},{6,3},{7,2},{8,13},{9,12},{10,... | collective-permute-start | bytes 393224 | tf_op jit(solution)/shard_map/ppermute | solution.py:392
  106.8 25.3 %collective-permute-start.26 = (bf16[32,16,128]{2,1,0:T(8,128)(2,1)}, bf16[32,16,128]{2,1,0:T(8,128)(2,1)S(1)}, u32[]{:S(2)}, u32[]{:S(2)}) collective-permute-start(bf16[32,16,128]{2,1,0:T(8,128)(2,1)} %get-tuple-element.131), channel_id=1, source_target_pairs={{0,2},{1,3},{2,0},{3,1},{4,6},{5,7},{6,4},{7,5},{8,10},{9,11},{10,... | collective-permute-start | bytes 393224 | tf_op jit(solution)/shard_map/ppermute | solution.py:392
  107.9 46.4 %collective-permute-start.16 = (bf16[32,32,128]{2,1,0:T(8,128)(2,1)}, bf16[32,32,128]{2,1,0:T(8,128)(2,1)S(1)}, u32[]{:S(2)}, u32[]{:S(2)}) collective-permute-start(bf16[32,32,128]{2,1,0:T(8,128)(2,1)} %get-tuple-element.120), channel_id=1, source_target_pairs={{0,4},{1,5},{2,6},{3,7},{4,0},{5,1},{6,2},{7,3},{8,12},{9,13},{10,... | collective-permute-start | bytes 786440 | tf_op jit(solution)/shard_map/ppermute | solution.py:392
  121.7 32.6 %collective-permute-start.17 = (bf16[32,32,128]{2,1,0:T(8,128)(2,1)}, bf16[32,32,128]{2,1,0:T(8,128)(2,1)S(1)}, u32[]{:S(2)}, u32[]{:S(2)}) collective-permute-start(bf16[32,32,128]{2,1,0:T(8,128)(2,1)} %get-tuple-element.121), channel_id=1, source_target_pairs={{0,1},{1,0},{2,3},{3,2},{4,5},{5,4},{6,7},{7,6},{8,9},{9,8},{10,11... | collective-permute-start | bytes 786440 | tf_op jit(solution)/shard_map/ppermute | solution.py:392
  122.4 27.4 %collective-permute-start.27 = (bf16[32,16,128]{2,1,0:T(8,128)(2,1)}, bf16[32,16,128]{2,1,0:T(8,128)(2,1)S(1)}, u32[]{:S(2)}, u32[]{:S(2)}) collective-permute-start(bf16[32,16,128]{2,1,0:T(8,128)(2,1)} %get-tuple-element.132), channel_id=1, source_target_pairs={{0,6},{1,7},{2,4},{3,5},{4,2},{5,3},{6,0},{7,1},{8,14},{9,15},{10,... | collective-permute-start | bytes 393224 | tf_op jit(solution)/shard_map/ppermute | solution.py:392
  132.0 19.1 %collective-permute-start.28 = (bf16[32,16,128]{2,1,0:T(8,128)(2,1)}, bf16[32,16,128]{2,1,0:T(8,128)(2,1)S(1)}, u32[]{:S(2)}, u32[]{:S(2)}) collective-permute-start(bf16[32,16,128]{2,1,0:T(8,128)(2,1)} %get-tuple-element.133), channel_id=1, source_target_pairs={{0,3},{1,2},{2,1},{3,0},{4,7},{5,6},{6,5},{7,4},{8,11},{9,10},{10,... | collective-permute-start | bytes 393224 | tf_op jit(solution)/shard_map/ppermute | solution.py:392
  132.7 18.9 %collective-permute-start.29 = (bf16[32,16,128]{2,1,0:T(8,128)(2,1)}, bf16[32,16,128]{2,1,0:T(8,128)(2,1)S(1)}, u32[]{:S(2)}, u32[]{:S(2)}) collective-permute-start(bf16[32,16,128]{2,1,0:T(8,128)(2,1)} %get-tuple-element.134), channel_id=1, source_target_pairs={{0,7},{1,6},{2,5},{3,4},{4,3},{5,2},{6,1},{7,0},{8,15},{9,14},{10,... | collective-permute-start | bytes 393224 | tf_op jit(solution)/shard_map/ppermute | solution.py:392
  149.9 31.2 %collective-permute-start.18 = (bf16[32,32,128]{2,1,0:T(8,128)(2,1)}, bf16[32,32,128]{2,1,0:T(8,128)(2,1)}, u32[]{:S(2)}, u32[]{:S(2)}) collective-permute-start(bf16[32,32,128]{2,1,0:T(8,128)(2,1)} %get-tuple-element.122), channel_id=1, source_target_pairs={{0,5},{1,4},{2,7},{3,6},{4,1},{5,0},{6,3},{7,2},{8,13},{9,12},{10,... | collective-permute-start | bytes 786440 | tf_op jit(solution)/shard_map/ppermute | solution.py:392
  151.1 31.8 %collective-permute-start.19 = (bf16[32,32,128]{2,1,0:T(8,128)(2,1)}, bf16[32,32,128]{2,1,0:T(8,128)(2,1)}, u32[]{:S(2)}, u32[]{:S(2)}) collective-permute-start(bf16[32,32,128]{2,1,0:T(8,128)(2,1)} %get-tuple-element.123), channel_id=1, source_target_pairs={{0,2},{1,3},{2,0},{3,1},{4,6},{5,7},{6,4},{7,5},{8,10},{9,11},{10,... | collective-permute-start | bytes 786440 | tf_op jit(solution)/shard_map/ppermute | solution.py:392
  151.6 31.3 %collective-permute-start.20 = (bf16[32,32,128]{2,1,0:T(8,128)(2,1)}, bf16[32,32,128]{2,1,0:T(8,128)(2,1)}, u32[]{:S(2)}, u32[]{:S(2)}) collective-permute-start(bf16[32,32,128]{2,1,0:T(8,128)(2,1)} %get-tuple-element.124), channel_id=1, source_target_pairs={{0,6},{1,7},{2,4},{3,5},{4,2},{5,3},{6,0},{7,1},{8,14},{9,15},{10,... | collective-permute-start | bytes 786440 | tf_op jit(solution)/shard_map/ppermute | solution.py:392
  154.4 29.8 %collective-permute-start.21 = (bf16[32,32,128]{2,1,0:T(8,128)(2,1)}, bf16[32,32,128]{2,1,0:T(8,128)(2,1)}, u32[]{:S(2)}, u32[]{:S(2)}) collective-permute-start(bf16[32,32,128]{2,1,0:T(8,128)(2,1)} %get-tuple-element.125), channel_id=1, source_target_pairs={{0,3},{1,2},{2,1},{3,0},{4,7},{5,6},{6,5},{7,4},{8,11},{9,10},{10,... | collective-permute-start | bytes 786440 | tf_op jit(solution)/shard_map/ppermute | solution.py:392
  154.4 30.3 %collective-permute-start.22 = (bf16[32,32,128]{2,1,0:T(8,128)(2,1)}, bf16[32,32,128]{2,1,0:T(8,128)(2,1)}, u32[]{:S(2)}, u32[]{:S(2)}) collective-permute-start(bf16[32,32,128]{2,1,0:T(8,128)(2,1)} %get-tuple-element.126), channel_id=1, source_target_pairs={{0,7},{1,6},{2,5},{3,4},{4,3},{5,2},{6,1},{7,0},{8,15},{9,14},{10,... | collective-permute-start | bytes 786440 | tf_op jit(solution)/shard_map/ppermute | solution.py:392
  181.1 18.5 %collective-permute-start.44 = (bf16[32,16,128]{2,1,0:T(8,128)(2,1)}, bf16[32,16,128]{2,1,0:T(8,128)(2,1)S(1)}, u32[]{:S(2)}, u32[]{:S(2)}) collective-permute-start(bf16[32,16,128]{2,1,0:T(8,128)(2,1)} %get-tuple-element.155), channel_id=1, source_target_pairs={{0,4},{1,5},{2,6},{3,7},{4,0},{5,1},{6,2},{7,3},{8,12},{9,13},{10,... | collective-permute-start | bytes 393224 | tf_op jit(solution)/shard_map/ppermute | solution.py:392
  182.9 18.3 %collective-permute-start.46 = (bf16[32,16,128]{2,1,0:T(8,128)(2,1)}, bf16[32,16,128]{2,1,0:T(8,128)(2,1)S(1)}, u32[]{:S(2)}, u32[]{:S(2)}) collective-permute-start(bf16[32,16,128]{2,1,0:T(8,128)(2,1)} %get-tuple-element.157), channel_id=1, source_target_pairs={{0,5},{1,4},{2,7},{3,6},{4,1},{5,0},{6,3},{7,2},{8,13},{9,12},{10,... | collective-permute-start | bytes 393224 | tf_op jit(solution)/shard_map/ppermute | solution.py:392
  184.2 18.5 %collective-permute-start.47 = (bf16[32,16,128]{2,1,0:T(8,128)(2,1)}, bf16[32,16,128]{2,1,0:T(8,128)(2,1)S(1)}, u32[]{:S(2)}, u32[]{:S(2)}) collective-permute-start(bf16[32,16,128]{2,1,0:T(8,128)(2,1)} %get-tuple-element.158), channel_id=1, source_target_pairs={{0,2},{1,3},{2,0},{3,1},{4,6},{5,7},{6,4},{7,5},{8,10},{9,11},{10,... | collective-permute-start | bytes 393224 | tf_op jit(solution)/shard_map/ppermute | solution.py:392
  184.7 19.1 %collective-permute-start.48 = (bf16[32,16,128]{2,1,0:T(8,128)(2,1)}, bf16[32,16,128]{2,1,0:T(8,128)(2,1)S(1)}, u32[]{:S(2)}, u32[]{:S(2)}) collective-permute-start(bf16[32,16,128]{2,1,0:T(8,128)(2,1)} %get-tuple-element.159), channel_id=1, source_target_pairs={{0,6},{1,7},{2,4},{3,5},{4,2},{5,3},{6,0},{7,1},{8,14},{9,15},{10,... | collective-permute-start | bytes 393224 | tf_op jit(solution)/shard_map/ppermute | solution.py:392
  199.5 33.9 %collective-permute-start.30 = (bf16[32,32,128]{2,1,0:T(8,128)(2,1)}, bf16[32,32,128]{2,1,0:T(8,128)(2,1)}, u32[]{:S(2)}, u32[]{:S(2)}) collective-permute-start(bf16[32,32,128]{2,1,0:T(8,128)(2,1)} %get-tuple-element.137), channel_id=1, source_target_pairs={{0,4},{1,5},{2,6},{3,7},{4,0},{5,1},{6,2},{7,3},{8,12},{9,13},{10,... | collective-permute-start | bytes 786440 | tf_op jit(solution)/shard_map/ppermute | solution.py:392
  199.6 34.0 %collective-permute-start.31 = (bf16[32,32,128]{2,1,0:T(8,128)(2,1)}, bf16[32,32,128]{2,1,0:T(8,128)(2,1)}, u32[]{:S(2)}, u32[]{:S(2)}) collective-permute-start(bf16[32,32,128]{2,1,0:T(8,128)(2,1)} %get-tuple-element.138), channel_id=1, source_target_pairs={{0,1},{1,0},{2,3},{3,2},{4,5},{5,4},{6,7},{7,6},{8,9},{9,8},{10,11... | collective-permute-start | bytes 786440 | tf_op jit(solution)/shard_map/ppermute | solution.py:392
  201.3 35.5 %collective-permute-start.32 = (bf16[32,32,128]{2,1,0:T(8,128)(2,1)S(1)}, bf16[32,32,128]{2,1,0:T(8,128)(2,1)}, u32[]{:S(2)}, u32[]{:S(2)}) collective-permute-start(bf16[32,32,128]{2,1,0:T(8,128)(2,1)S(1)} %copy-done.44), channel_id=1, source_target_pairs={{0,5},{1,4},{2,7},{3,6},{4,1},{5,0},{6,3},{7,2},{8,13},{9,12},{10,... | collective-permute-start | bytes 786440 | tf_op jit(solution)/shard_map/ppermute | solution.py:392
  202.7 29.3 %collective-permute-start.49 = (bf16[32,16,128]{2,1,0:T(8,128)(2,1)}, bf16[32,16,128]{2,1,0:T(8,128)(2,1)S(1)}, u32[]{:S(2)}, u32[]{:S(2)}) collective-permute-start(bf16[32,16,128]{2,1,0:T(8,128)(2,1)} %get-tuple-element.160), channel_id=1, source_target_pairs={{0,3},{1,2},{2,1},{3,0},{4,7},{5,6},{6,5},{7,4},{8,11},{9,10},{10,... | collective-permute-start | bytes 393224 | tf_op jit(solution)/shard_map/ppermute | solution.py:392
  203.8 28.7 %collective-permute-start.50 = (bf16[32,16,128]{2,1,0:T(8,128)(2,1)}, bf16[32,16,128]{2,1,0:T(8,128)(2,1)}, u32[]{:S(2)}, u32[]{:S(2)}) collective-permute-start(bf16[32,16,128]{2,1,0:T(8,128)(2,1)} %get-tuple-element.161), channel_id=1, source_target_pairs={{0,7},{1,6},{2,5},{3,4},{4,3},{5,2},{6,1},{7,0},{8,15},{9,14},{10,... | collective-permute-start | bytes 393224 | tf_op jit(solution)/shard_map/ppermute | solution.py:392
  233.5 17.1 %collective-permute-start.35 = (bf16[32,32,128]{2,1,0:T(8,128)(2,1)S(1)}, bf16[32,32,128]{2,1,0:T(8,128)(2,1)S(1)}, u32[]{:S(2)}, u32[]{:S(2)}) collective-permute-start(bf16[32,32,128]{2,1,0:T(8,128)(2,1)S(1)} %copy-done.40), channel_id=1, source_target_pairs={{0,3},{1,2},{2,1},{3,0},{4,7},{5,6},{6,5},{7,4},{8,11},{9,10},{10,... | collective-permute-start | bytes 786440 | tf_op jit(solution)/shard_map/ppermute | solution.py:392
  233.6 24.5 %collective-permute-start.36 = (bf16[32,32,128]{2,1,0:T(8,128)(2,1)S(1)}, bf16[32,32,128]{2,1,0:T(8,128)(2,1)S(1)}, u32[]{:S(2)}, u32[]{:S(2)}) collective-permute-start(bf16[32,32,128]{2,1,0:T(8,128)(2,1)S(1)} %copy-done.38), channel_id=1, source_target_pairs={{0,7},{1,6},{2,5},{3,4},{4,3},{5,2},{6,1},{7,0},{8,15},{9,14},{10,... | collective-permute-start | bytes 786440 | tf_op jit(solution)/shard_map/ppermute | solution.py:392
  236.8 45.4 %collective-permute-start.51 = (bf16[32,32,128]{2,1,0:T(8,128)(2,1)}, bf16[32,32,128]{2,1,0:T(8,128)(2,1)S(1)}, u32[]{:S(2)}, u32[]{:S(2)}) collective-permute-start(bf16[32,32,128]{2,1,0:T(8,128)(2,1)} %get-tuple-element.163), channel_id=1, source_target_pairs={{0,4},{1,5},{2,6},{3,7},{4,0},{5,1},{6,2},{7,3},{8,12},{9,13},{10,... | collective-permute-start | bytes 786440 | tf_op jit(solution)/shard_map/ppermute | solution.py:392
  246.9 35.2 %collective-permute-start.52 = (bf16[32,32,128]{2,1,0:T(8,128)(2,1)}, bf16[32,32,128]{2,1,0:T(8,128)(2,1)S(1)}, u32[]{:S(2)}, u32[]{:S(2)}) collective-permute-start(bf16[32,32,128]{2,1,0:T(8,128)(2,1)} %get-tuple-element.164), channel_id=1, source_target_pairs={{0,1},{1,0},{2,3},{3,2},{4,5},{5,4},{6,7},{7,6},{8,9},{9,8},{10,11... | collective-permute-start | bytes 786440 | tf_op jit(solution)/shard_map/ppermute | solution.py:392
  246.9 37.0 %collective-permute-start.53 = (bf16[32,32,128]{2,1,0:T(8,128)(2,1)}, bf16[32,32,128]{2,1,0:T(8,128)(2,1)S(1)}, u32[]{:S(2)}, u32[]{:S(2)}) collective-permute-start(bf16[32,32,128]{2,1,0:T(8,128)(2,1)} %get-tuple-element.165), channel_id=1, source_target_pairs={{0,5},{1,4},{2,7},{3,6},{4,1},{5,0},{6,3},{7,2},{8,13},{9,12},{10,... | collective-permute-start | bytes 786440 | tf_op jit(solution)/shard_map/ppermute | solution.py:392
  250.5 41.0 %collective-permute-start.54 = (bf16[32,32,128]{2,1,0:T(8,128)(2,1)}, bf16[32,32,128]{2,1,0:T(8,128)(2,1)S(1)}, u32[]{:S(2)}, u32[]{:S(2)}) collective-permute-start(bf16[32,32,128]{2,1,0:T(8,128)(2,1)} %get-tuple-element.166), channel_id=1, source_target_pairs={{0,2},{1,3},{2,0},{3,1},{4,6},{5,7},{6,4},{7,5},{8,10},{9,11},{10,... | collective-permute-start | bytes 786440 | tf_op jit(solution)/shard_map/ppermute | solution.py:392
  258.1 41.0 %collective-permute-start.37 = (bf16[32,32,128]{2,1,0:T(8,128)(2,1)}, bf16[32,32,128]{2,1,0:T(8,128)(2,1)S(1)}, u32[]{:S(2)}, u32[]{:S(2)}) collective-permute-start(bf16[32,32,128]{2,1,0:T(8,128)(2,1)} %get-tuple-element.145), channel_id=1, source_target_pairs={{0,4},{1,5},{2,6},{3,7},{4,0},{5,1},{6,2},{7,3},{8,12},{9,13},{10,... | collective-permute-start | bytes 786440 | tf_op jit(solution)/shard_map/ppermute | solution.py:392
  282.1 17.0 %collective-permute-start.38 = (bf16[32,32,128]{2,1,0:T(8,128)(2,1)}, bf16[32,32,128]{2,1,0:T(8,128)(2,1)S(1)}, u32[]{:S(2)}, u32[]{:S(2)}) collective-permute-start(bf16[32,32,128]{2,1,0:T(8,128)(2,1)} %get-tuple-element.146), channel_id=1, source_target_pairs={{0,1},{1,0},{2,3},{3,2},{4,5},{5,4},{6,7},{7,6},{8,9},{9,8},{10,11... | collective-permute-start | bytes 786440 | tf_op jit(solution)/shard_map/ppermute | solution.py:392
  282.1 44.2 %collective-permute-start.39 = (bf16[32,32,128]{2,1,0:T(8,128)(2,1)}, bf16[32,32,128]{2,1,0:T(8,128)(2,1)}, u32[]{:S(2)}, u32[]{:S(2)}) collective-permute-start(bf16[32,32,128]{2,1,0:T(8,128)(2,1)} %get-tuple-element.147), channel_id=1, source_target_pairs={{0,5},{1,4},{2,7},{3,6},{4,1},{5,0},{6,3},{7,2},{8,13},{9,12},{10,... | collective-permute-start | bytes 786440 | tf_op jit(solution)/shard_map/ppermute | solution.py:392
  284.0 43.3 %collective-permute-start.40 = (bf16[32,32,128]{2,1,0:T(8,128)(2,1)}, bf16[32,32,128]{2,1,0:T(8,128)(2,1)}, u32[]{:S(2)}, u32[]{:S(2)}) collective-permute-start(bf16[32,32,128]{2,1,0:T(8,128)(2,1)} %get-tuple-element.148), channel_id=1, source_target_pairs={{0,2},{1,3},{2,0},{3,1},{4,6},{5,7},{6,4},{7,5},{8,10},{9,11},{10,... | collective-permute-start | bytes 786440 | tf_op jit(solution)/shard_map/ppermute | solution.py:392
  291.5 36.0 %collective-permute-start.41 = (bf16[32,32,128]{2,1,0:T(8,128)(2,1)}, bf16[32,32,128]{2,1,0:T(8,128)(2,1)}, u32[]{:S(2)}, u32[]{:S(2)}) collective-permute-start(bf16[32,32,128]{2,1,0:T(8,128)(2,1)} %get-tuple-element.149), channel_id=1, source_target_pairs={{0,6},{1,7},{2,4},{3,5},{4,2},{5,3},{6,0},{7,1},{8,14},{9,15},{10,... | collective-permute-start | bytes 786440 | tf_op jit(solution)/shard_map/ppermute | solution.py:392
  299.1 31.1 %collective-permute-start.42 = (bf16[32,32,128]{2,1,0:T(8,128)(2,1)}, bf16[32,32,128]{2,1,0:T(8,128)(2,1)}, u32[]{:S(2)}, u32[]{:S(2)}) collective-permute-start(bf16[32,32,128]{2,1,0:T(8,128)(2,1)} %get-tuple-element.150), channel_id=1, source_target_pairs={{0,3},{1,2},{2,1},{3,0},{4,7},{5,6},{6,5},{7,4},{8,11},{9,10},{10,... | collective-permute-start | bytes 786440 | tf_op jit(solution)/shard_map/ppermute | solution.py:392
  299.8 30.7 %collective-permute-start.43 = (bf16[32,32,128]{2,1,0:T(8,128)(2,1)}, bf16[32,32,128]{2,1,0:T(8,128)(2,1)}, u32[]{:S(2)}, u32[]{:S(2)}) collective-permute-start(bf16[32,32,128]{2,1,0:T(8,128)(2,1)} %get-tuple-element.151), channel_id=1, source_target_pairs={{0,7},{1,6},{2,5},{3,4},{4,3},{5,2},{6,1},{7,0},{8,15},{9,14},{10,... | collective-permute-start | bytes 786440 | tf_op jit(solution)/shard_map/ppermute | solution.py:392
  326.4 23.1 %collective-permute-start.55 = (bf16[32,32,128]{2,1,0:T(8,128)(2,1)}, bf16[32,32,128]{2,1,0:T(8,128)(2,1)}, u32[]{:S(2)}, u32[]{:S(2)}) collective-permute-start(bf16[32,32,128]{2,1,0:T(8,128)(2,1)} %get-tuple-element.167), channel_id=1, source_target_pairs={{0,6},{1,7},{2,4},{3,5},{4,2},{5,3},{6,0},{7,1},{8,14},{9,15},{10,... | collective-permute-start | bytes 786440 | tf_op jit(solution)/shard_map/ppermute | solution.py:392
  327.3 23.1 %collective-permute-start.56 = (bf16[32,32,128]{2,1,0:T(8,128)(2,1)}, bf16[32,32,128]{2,1,0:T(8,128)(2,1)}, u32[]{:S(2)}, u32[]{:S(2)}) collective-permute-start(bf16[32,32,128]{2,1,0:T(8,128)(2,1)} %get-tuple-element.168), channel_id=1, source_target_pairs={{0,3},{1,2},{2,1},{3,0},{4,7},{5,6},{6,5},{7,4},{8,11},{9,10},{10,... | collective-permute-start | bytes 786440 | tf_op jit(solution)/shard_map/ppermute | solution.py:392
  327.5 33.1 %collective-permute-start.57 = (bf16[32,32,128]{2,1,0:T(8,128)(2,1)}, bf16[32,32,128]{2,1,0:T(8,128)(2,1)}, u32[]{:S(2)}, u32[]{:S(2)}) collective-permute-start(bf16[32,32,128]{2,1,0:T(8,128)(2,1)} %get-tuple-element.169), channel_id=1, source_target_pairs={{0,7},{1,6},{2,5},{3,4},{4,3},{5,2},{6,1},{7,0},{8,15},{9,14},{10,... | collective-permute-start | bytes 786440 | tf_op jit(solution)/shard_map/ppermute | solution.py:392
  330.2 47.9 %collective-permute-start.58 = (bf16[32,32,128]{2,1,0:T(8,128)(2,1)}, bf16[32,32,128]{2,1,0:T(8,128)(2,1)}, u32[]{:S(2)}, u32[]{:S(2)}) collective-permute-start(bf16[32,32,128]{2,1,0:T(8,128)(2,1)} %get-tuple-element.172), channel_id=1, source_target_pairs={{0,4},{1,5},{2,6},{3,7},{4,0},{5,1},{6,2},{7,3},{8,12},{9,13},{10,... | collective-permute-start | bytes 786440 | tf_op jit(solution)/shard_map/ppermute | solution.py:392
  330.5 47.5 %collective-permute-start.59 = (bf16[32,32,128]{2,1,0:T(8,128)(2,1)}, bf16[32,32,128]{2,1,0:T(8,128)(2,1)}, u32[]{:S(2)}, u32[]{:S(2)}) collective-permute-start(bf16[32,32,128]{2,1,0:T(8,128)(2,1)} %get-tuple-element.173), channel_id=1, source_target_pairs={{0,1},{1,0},{2,3},{3,2},{4,5},{5,4},{6,7},{7,6},{8,9},{9,8},{10,11... | collective-permute-start | bytes 786440 | tf_op jit(solution)/shard_map/ppermute | solution.py:392
  349.5 26.0 %collective-permute-start.65 = (bf16[32,16,128]{2,1,0:T(8,128)(2,1)}, bf16[32,16,128]{2,1,0:T(8,128)(2,1)S(1)}, u32[]{:S(2)}, u32[]{:S(2)}) collective-permute-start(bf16[32,16,128]{2,1,0:T(8,128)(2,1)} %get-tuple-element.181), channel_id=1, source_target_pairs={{0,4},{1,5},{2,6},{3,7},{4,0},{5,1},{6,2},{7,3},{8,12},{9,13},{10,... | collective-permute-start | bytes 393224 | tf_op jit(solution)/shard_map/ppermute | solution.py:392
  350.4 25.1 %collective-permute-start.66 = (bf16[32,16,128]{2,1,0:T(8,128)(2,1)}, bf16[32,16,128]{2,1,0:T(8,128)(2,1)}, u32[]{:S(2)}, u32[]{:S(2)}) collective-permute-start(bf16[32,16,128]{2,1,0:T(8,128)(2,1)} %get-tuple-element.182), channel_id=1, source_target_pairs={{0,1},{1,0},{2,3},{3,2},{4,5},{5,4},{6,7},{7,6},{8,9},{9,8},{10,11... | collective-permute-start | bytes 393224 | tf_op jit(solution)/shard_map/ppermute | solution.py:392
  360.7 27.2 %collective-permute-start.60 = (bf16[32,32,128]{2,1,0:T(8,128)(2,1)}, bf16[32,32,128]{2,1,0:T(8,128)(2,1)S(1)}, u32[]{:S(2)}, u32[]{:S(2)}) collective-permute-start(bf16[32,32,128]{2,1,0:T(8,128)(2,1)} %get-tuple-element.174), channel_id=1, source_target_pairs={{0,5},{1,4},{2,7},{3,6},{4,1},{5,0},{6,3},{7,2},{8,13},{9,12},{10,... | collective-permute-start | bytes 786440 | tf_op jit(solution)/shard_map/ppermute | solution.py:392
  375.5 18.3 %collective-permute-start.61 = (bf16[32,32,128]{2,1,0:T(8,128)(2,1)}, bf16[32,32,128]{2,1,0:T(8,128)(2,1)S(1)}, u32[]{:S(2)}, u32[]{:S(2)}) collective-permute-start(bf16[32,32,128]{2,1,0:T(8,128)(2,1)} %get-tuple-element.175), channel_id=1, source_target_pairs={{0,2},{1,3},{2,0},{3,1},{4,6},{5,7},{6,4},{7,5},{8,10},{9,11},{10,... | collective-permute-start | bytes 786440 | tf_op jit(solution)/shard_map/ppermute | solution.py:392
  375.5 18.3 %collective-permute-start.62 = (bf16[32,32,128]{2,1,0:T(8,128)(2,1)}, bf16[32,32,128]{2,1,0:T(8,128)(2,1)S(1)}, u32[]{:S(2)}, u32[]{:S(2)}) collective-permute-start(bf16[32,32,128]{2,1,0:T(8,128)(2,1)} %get-tuple-element.176), channel_id=1, source_target_pairs={{0,6},{1,7},{2,4},{3,5},{4,2},{5,3},{6,0},{7,1},{8,14},{9,15},{10,... | collective-permute-start | bytes 786440 | tf_op jit(solution)/shard_map/ppermute | solution.py:392
  378.0 26.4 %collective-permute-start.63 = (bf16[32,32,128]{2,1,0:T(8,128)(2,1)}, bf16[32,32,128]{2,1,0:T(8,128)(2,1)S(1)}, u32[]{:S(2)}, u32[]{:S(2)}) collective-permute-start(bf16[32,32,128]{2,1,0:T(8,128)(2,1)} %get-tuple-element.177), channel_id=1, source_target_pairs={{0,3},{1,2},{2,1},{3,0},{4,7},{5,6},{6,5},{7,4},{8,11},{9,10},{10,... | collective-permute-start | bytes 786440 | tf_op jit(solution)/shard_map/ppermute | solution.py:392
  378.1 26.4 %collective-permute-start.64 = (bf16[32,32,128]{2,1,0:T(8,128)(2,1)}, bf16[32,32,128]{2,1,0:T(8,128)(2,1)S(1)}, u32[]{:S(2)}, u32[]{:S(2)}) collective-permute-start(bf16[32,32,128]{2,1,0:T(8,128)(2,1)} %get-tuple-element.178), channel_id=1, source_target_pairs={{0,7},{1,6},{2,5},{3,4},{4,3},{5,2},{6,1},{7,0},{8,15},{9,14},{10,... | collective-permute-start | bytes 786440 | tf_op jit(solution)/shard_map/ppermute | solution.py:392
  387.9 26.0 %collective-permute-start.67 = (bf16[32,16,128]{2,1,0:T(8,128)(2,1)S(1)}, bf16[32,16,128]{2,1,0:T(8,128)(2,1)S(1)}, u32[]{:S(2)}, u32[]{:S(2)}) collective-permute-start(bf16[32,16,128]{2,1,0:T(8,128)(2,1)S(1)} %copy-done.66), channel_id=1, source_target_pairs={{0,5},{1,4},{2,7},{3,6},{4,1},{5,0},{6,3},{7,2},{8,13},{9,12},{10,... | collective-permute-start | bytes 393224 | tf_op jit(solution)/shard_map/ppermute | solution.py:392
  393.8 20.1 %collective-permute-start.68 = (bf16[32,16,128]{2,1,0:T(8,128)(2,1)S(1)}, bf16[32,16,128]{2,1,0:T(8,128)(2,1)S(1)}, u32[]{:S(2)}, u32[]{:S(2)}) collective-permute-start(bf16[32,16,128]{2,1,0:T(8,128)(2,1)S(1)} %copy-done.65), channel_id=1, source_target_pairs={{0,2},{1,3},{2,0},{3,1},{4,6},{5,7},{6,4},{7,5},{8,10},{9,11},{10,... | collective-permute-start | bytes 393224 | tf_op jit(solution)/shard_map/ppermute | solution.py:392
  393.9 20.1 %collective-permute-start.69 = (bf16[32,16,128]{2,1,0:T(8,128)(2,1)S(1)}, bf16[32,16,128]{2,1,0:T(8,128)(2,1)S(1)}, u32[]{:S(2)}, u32[]{:S(2)}) collective-permute-start(bf16[32,16,128]{2,1,0:T(8,128)(2,1)S(1)} %copy-done.64), channel_id=1, source_target_pairs={{0,6},{1,7},{2,4},{3,5},{4,2},{5,3},{6,0},{7,1},{8,14},{9,15},{10,... | collective-permute-start | bytes 393224 | tf_op jit(solution)/shard_map/ppermute | solution.py:392
  (85 other events, 2377.9 us)

commit v17 on v16

--- a/solution.py
+++ b/solution.py
@@ -48,6 +48,13 @@
 
 def band(meta_ref, slot, width):
     return pl.ds(pl.multiple_of(meta_ref[1 + slot] * width, width), width)
+
+
+def group_of(shots, rows):
+    group = 1
+    while shots % (2 * group) == 0 and 2 * group * rows <= 256:
+        group *= 2
+    return group
 
 
 def blend_into(
@@ -266,7 +273,7 @@
 def spectra_of(meta, delays, fields, table, rows, block, edge_block, peers, after):
     shots, _, samples = fields[0].shape
     shape = (shots, rows, 2 * F // peers)
-    group = min(shots, max(1, 256 // rows))
+    group = group_of(shots, rows)
     *spectra, energy = pl.pallas_call(
         spectra_kernel,
         grid_spec=pltpu.PrefetchScalarGridSpec(
@@ -341,7 +348,7 @@
 def updated_of(meta, restored, table, block, receivers, onto, after):
     shots, rows, width = restored[0].shape
     samples = table.shape[1]
-    group = min(shots, max(1, 256 // rows))
+    group = group_of(shots, rows)
     in_specs = [whole(table.shape), ANYWHERE]
     in_specs += [pl.BlockSpec((group, rows, width), lambda step, meta: (step, 0, 0))] * len(restored)
     operands = [meta, table, after, *restored]
@@ -405,7 +412,7 @@
 
 def chunks_of(receivers):
     if receivers == 128:
-        return [(16, 0), (32, 1), (32, 2), (32, 3), (16, 1)]
+        return [(16, 6), (48, 0), (48, 1), (16, 7)]
     rows = min(16, receivers)
     return [(rows, index) for index in range(receivers // rows)]
 

time: 423 us -> 452 us (1.069); the launches traced: 421 us -> 445 us
  waiting for transfers between devices: 108 us -> 172 us
  starting transfers between devices: 130 us -> 110 us
  Pallas kernels: 149 us -> 134 us
    ppermute x70 -> x56, waiting for transfers between devices: 105 us -> 169 us  [exchanged(): lax.ppermute(arrays[slot], 'shot', [(i, i ^ slot) for i in range(peers)])]
    ppermute x70 -> x56, starting transfers between devices: 126 us -> 106 us  [exchanged(): lax.ppermute(arrays[slot], 'shot', [(i, i ^ slot) for i in range(peers)])]
    pallas_call x5 -> x4, Pallas kernels: 58.6 us -> 48.6 us  [shrunk_of(): pl.pallas_call(shots_kernel, grid_spec=pltpu.PrefetchScalarGridSpec(num_s...]
    pallas_call x5 -> x4, Pallas kernels: 64.6 us -> 61 us  [spectra_of(): pl.pallas_call(spectra_kernel, grid_spec=pltpu.PrefetchScalarGridSpec(num...]
    unnamed x154 -> x116, local copies, waits for them, and re-layouts: 16.7 us -> 13.3 us
    pallas_call x5 -> x4, Pallas kernels: 26 us -> 24.5 us  [updated_of(): pl.pallas_call(functools.partial(update_kernel, len(restored)), grid_spec...]
  transfers between devices with their start and end apart: 72 -> 58, of which waited for: 18 -> 17; matrix products, arithmetic and copies ran while one was open for 1% -> 1% of each run, Pallas kernels for 32% -> 26%
where the time goes in v17:
time: 452 us; the launch traced here: 445 us
  waiting for transfers between devices  172 us (38%)
  Pallas kernels  134 us (30%)
  starting transfers between devices  110 us (24%)
  local copies, waits for them, and re-layouts  17 us (4%)
  blocking collectives  9.9 us (2%)
    ppermute x56, waiting for transfers between devices, exchanged(): lax.ppermute(arrays[slot], 'shot', [(i, i ^ slot) for i in range(peers)])  169 us
    ppermute x56, starting transfers between devices, exchanged(): lax.ppermute(arrays[slot], 'shot', [(i, i ^ slot) for i in range(peers)])  106 us
    pallas_call x4, Pallas kernels, spectra_of(): pl.pallas_call(spectra_kernel, grid_spec=pltpu.PrefetchScalarGridSpec(num...  61 us
    pallas_call x4, Pallas kernels, shrunk_of(): pl.pallas_call(shots_kernel, grid_spec=pltpu.PrefetchScalarGridSpec(num_s...  48.6 us
    pallas_call x4, Pallas kernels, updated_of(): pl.pallas_call(functools.partial(update_kernel, len(restored)), grid_spec...  24.5 us
    unnamed x116, local copies, waits for them, and re-layouts  13.3 us
    psum x1, blocking collectives, local(): lax.psum(jnp.sum(energy, axis=1), 'patch')  9.9 us
  transfers between devices with their start and end apart: 58, of which 17 were waited for; matrix products, arithmetic and copies ran while one was open for 1% of the time, Pallas kernels for 26%

profile of v17, /device:TPU:0, one launch (start us, length us, event | category | flops | bytes accessed | tf_op | source)
XLA Modules:
  0.0 445.4 jit_solution(15767900178854895465)
XLA Ops:
  0.6 1.1 fusion.1
  1.7 1.3 fusion
  3.1 2.4 collective-permute-start
  5.5 1.3 collective-permute-start.1
  8.9 3.0 collective-permute-done.1.after_ref
  12.8 9.9 %spectra.4 = (bf16[32,16,128]{2,1,0:T(8,128)(2,1)}, bf16[32,16,128]{2,1,0:T(8,128)(2,1)}, bf16[32,16,128]{2,1,0:T(8,128)(2,1)}, bf16[32,16,128]{2,1,0:T(8,128)(2...) custom-call(s32[9]{0:T(128)} %pad_add_fusion.meta_ref, ...), custom_call_target="tpu_custom_call" | custom-call | flops 1073741824 | bytes 5242880 | tf_op jit(solution)/shard_map/spectra/pallas_call | solution.py:277
  22.7 10.4 %collective-permute-start.2 = (bf16[32,16,128]{2,1,0:T(8,128)(2,1)}, bf16[32,16,128]{2,1,0:T(8,128)(2,1)S(1)}, u32[]{:S(2)}, u32[]{:S(2)}) collective-permute-start(bf16[32,16,128]{2,1,0:T(8,128)(2,1)} %get-tuple-element.81), channel_id=1, source_target_pairs={{0,4},{1,5},{2,6},{3,7},{4,0},{5,1},{6,2},{7,3},{8,12},{9,13},{10,... | collective-permute-start | bytes 393224 | tf_op jit(solution)/shard_map/ppermute | solution.py:399
  33.0 1.6 collective-permute-start.3
  34.7 1.5 collective-permute-start.5
  36.1 2.5 collective-permute-start.6
  38.6 20.5 %spectra.5 = (bf16[32,48,128]{2,1,0:T(8,128)(2,1)}, bf16[32,48,128]{2,1,0:T(8,128)(2,1)}, bf16[32,48,128]{2,1,0:T(8,128)(2,1)}, bf16[32,48,128]{2,1,0:T(8,128)(2...) custom-call(s32[9]{0:T(128)} %pad_add_fusion.meta_ref, ...), custom_call_target="tpu_custom_call" | custom-call | flops 3221225472 | bytes 11534336 | tf_op jit(solution)/shard_map/spectra/pallas_call | solution.py:277
  60.2 20.5 %spectra.6 = (bf16[32,48,128]{2,1,0:T(8,128)(2,1)}, bf16[32,48,128]{2,1,0:T(8,128)(2,1)}, bf16[32,48,128]{2,1,0:T(8,128)(2,1)}, bf16[32,48,128]{2,1,0:T(8,128)(2...) custom-call(s32[9]{0:T(128)} %pad_add_fusion.meta_ref, ...), custom_call_target="tpu_custom_call" | custom-call | flops 3221225472 | bytes 11534336 | tf_op jit(solution)/shard_map/spectra/pallas_call | solution.py:277
  81.6 7.3 %shrink.4 = (bf16[32,16,128]{2,1,0:T(8,128)(2,1)}, bf16[32,16,128]{2,1,0:T(8,128)(2,1)}, bf16[32,16,128]{2,1,0:T(8,128)(2,1)}, bf16[32,16,128]{2,1,0:T(8,128)(2,...) custom-call(s32[9]{0:T(128)} %pad_add_fusion.meta_ref, ...), custom_call_target="tpu_custom_call" | custom-call | flops 1073741824 | bytes 2359296 | tf_op jit(solution)/shard_map/shrink/pallas_call | solution.py:327
  88.9 2.3 collective-permute-start.23
  92.0 1.2 collective-permute-start.26
  93.2 2.5 collective-permute-start.27
  95.7 6.4 %collective-permute-done.23.refs_1_ = bf16[32,16,128]{2,1,0:T(8,128)(2,1)S(1)} collective-permute-done((bf16[32,16,128]{2,1,0:T(8,128)(2,1)}, bf16[32,16,128]{2,1,0:T(8,128)(2,1)S(1)}, u32[]{:S(2)}, u32[]{:S(2)}) %collective-permute-start.23) | collective-permute-done | bytes 131104 | tf_op jit(solution)/shard_map/ppermute | solution.py:399
  102.1 2.3 collective-permute-start.29
  104.4 2.7 collective-permute-done.25.refs_3_
  109.2 13.8 %collective-permute-start.11 = (bf16[32,48,128]{2,1,0:T(8,128)(2,1)}, bf16[32,48,128]{2,1,0:T(8,128)(2,1)}, u32[]{:S(2)}, u32[]{:S(2)}) collective-permute-start(bf16[32,48,128]{2,1,0:T(8,128)(2,1)} %get-tuple-element.93), channel_id=1, source_target_pairs={{0,5},{1,4},{2,7},{3,6},{4,1},{5,0},{6,3},{7,2},{8,13},{9,12},{10,... | collective-permute-start | bytes 1179656 | tf_op jit(solution)/shard_map/ppermute | solution.py:399
  123.8 10.1 %spectra.7 = (bf16[32,16,128]{2,1,0:T(8,128)(2,1)}, bf16[32,16,128]{2,1,0:T(8,128)(2,1)}, bf16[32,16,128]{2,1,0:T(8,128)(2,1)}, bf16[32,16,128]{2,1,0:T(8,128)(2...) custom-call(s32[9]{0:T(128)} %pad_add_fusion.meta_ref, ...), custom_call_target="tpu_custom_call" | custom-call | flops 1073741824 | bytes 5242880 | tf_op jit(solution)/shard_map/spectra/pallas_call | solution.py:277
  133.9 1.9 collective-permute-start.30
  135.8 19.2 %collective-permute-done.30.refs_1_ = bf16[32,16,128]{2,1,0:T(8,128)(2,1)S(1)} collective-permute-done((bf16[32,16,128]{2,1,0:T(8,128)(2,1)}, bf16[32,16,128]{2,1,0:T(8,128)(2,1)S(1)}, u32[]{:S(2)}, u32[]{:S(2)}) %collective-permute-start.30) | collective-permute-done | bytes 131104 | tf_op jit(solution)/shard_map/ppermute | solution.py:399
  155.0 1.6 collective-permute-done.31.refs_2_
  156.6 2.4 collective-permute-start.13
  160.0 2.3 collective-permute-start.16
  162.3 8.1 %collective-permute-done.13.refs_5_ = bf16[32,48,128]{2,1,0:T(8,128)(2,1)S(1)} collective-permute-done((bf16[32,48,128]{2,1,0:T(8,128)(2,1)S(1)}, bf16[32,48,128]{2,1,0:T(8,128)(2,1)S(1)}, u32[]{:S(2)}, u32[]{:S(2)}) %collective-permute-start.13) | collective-permute-done | bytes 393248 | tf_op jit(solution)/shard_map/ppermute | solution.py:399
  170.5 4.3 collective-permute-start.18
  174.8 4.1 collective-permute-done.14.refs_6_
  178.9 7.0 %collective-permute-done.15.refs_7_ = bf16[32,48,128]{2,1,0:T(8,128)(2,1)S(1)} collective-permute-done((bf16[32,48,128]{2,1,0:T(8,128)(2,1)S(1)}, bf16[32,48,128]{2,1,0:T(8,128)(2,1)S(1)}, u32[]{:S(2)}, u32[]{:S(2)}) %collective-permute-start.15) | collective-permute-done | bytes 393248 | tf_op jit(solution)/shard_map/ppermute | solution.py:399
  185.9 2.4 collective-permute-start.20
  188.4 38.3 %collective-permute-done.16.refs_1_ = bf16[32,48,128]{2,1,0:T(8,128)(2,1)S(1)} collective-permute-done((bf16[32,48,128]{2,1,0:T(8,128)(2,1)S(1)}, bf16[32,48,128]{2,1,0:T(8,128)(2,1)S(1)}, u32[]{:S(2)}, u32[]{:S(2)}) %collective-permute-start.16) | collective-permute-done | bytes 393248 | tf_op jit(solution)/shard_map/ppermute | solution.py:399
  227.6 17.1 %shrink.5 = (bf16[32,48,128]{2,1,0:T(8,128)(2,1)}, bf16[32,48,128]{2,1,0:T(8,128)(2,1)}, bf16[32,48,128]{2,1,0:T(8,128)(2,1)}, bf16[32,48,128]{2,1,0:T(8,128)(2,...) custom-call(s32[9]{0:T(128)} %pad_add_fusion.meta_ref, ...), custom_call_target="tpu_custom_call" | custom-call | flops 3221225472 | bytes 6553600 | tf_op jit(solution)/shard_map/shrink/pallas_call | solution.py:327
  244.7 1.6 collective-permute-start.32
  246.3 1.8 collective-permute-start.33
  248.1 1.4 collective-permute-start.34
  249.5 1.8 collective-permute-done.21.refs_6_
  251.4 2.3 collective-permute-start.35
  253.6 4.5 %collective-permute-start.36 = (bf16[32,16,128]{2,1,0:T(8,128)(2,1)}, bf16[32,16,128]{2,1,0:T(8,128)(2,1)}, u32[]{:S(2)}, u32[]{:S(2)}) collective-permute-start(bf16[32,16,128]{2,1,0:T(8,128)(2,1)} %get-tuple-element.123), channel_id=1, source_target_pairs={{0,7},{1,6},{2,5},{3,4},{4,3},{5,2},{6,1},{7,0},{8,15},{9,14},{10,... | collective-permute-start | bytes 393224 | tf_op jit(solution)/shard_map/ppermute | solution.py:399
  258.2 17.1 %shrink.6 = (bf16[32,48,128]{2,1,0:T(8,128)(2,1)}, bf16[32,48,128]{2,1,0:T(8,128)(2,1)}, bf16[32,48,128]{2,1,0:T(8,128)(2,1)}, bf16[32,48,128]{2,1,0:T(8,128)(2,...) custom-call(s32[9]{0:T(128)} %pad_add_fusion.meta_ref, ...), custom_call_target="tpu_custom_call" | custom-call | flops 3221225472 | bytes 6553600 | tf_op jit(solution)/shard_map/shrink/pallas_call | solution.py:327
  275.3 12.3 %collective-permute-start.37 = (bf16[32,48,128]{2,1,0:T(8,128)(2,1)}, bf16[32,48,128]{2,1,0:T(8,128)(2,1)S(1)}, u32[]{:S(2)}, u32[]{:S(2)}) collective-permute-start(bf16[32,48,128]{2,1,0:T(8,128)(2,1)} %get-tuple-element.125), channel_id=1, source_target_pairs={{0,4},{1,5},{2,6},{3,7},{4,0},{5,1},{6,2},{7,3},{8,12},{9,13},{10,... | collective-permute-start | bytes 1179656 | tf_op jit(solution)/shard_map/ppermute | solution.py:399
  287.8 1.9 collective-permute-start.40
  295.2 3.2 update.4
  299.0 7.2 %shrink.7 = (bf16[32,16,128]{2,1,0:T(8,128)(2,1)}, bf16[32,16,128]{2,1,0:T(8,128)(2,1)}, bf16[32,16,128]{2,1,0:T(8,128)(2,1)}, bf16[32,16,128]{2,1,0:T(8,128)(2,...) custom-call(s32[9]{0:T(128)} %pad_add_fusion.meta_ref, ...), custom_call_target="tpu_custom_call" | custom-call | flops 1073741824 | bytes 2359296 | tf_op jit(solution)/shard_map/shrink/pallas_call | solution.py:327
  307.3 19.7 %collective-permute-done.51.refs_1_ = bf16[32,16,128]{2,1,0:T(8,128)(2,1)S(1)} collective-permute-done((bf16[32,16,128]{2,1,0:T(8,128)(2,1)}, bf16[32,16,128]{2,1,0:T(8,128)(2,1)S(1)}, u32[]{:S(2)}, u32[]{:S(2)}) %collective-permute-start.51) | collective-permute-done | bytes 131104 | tf_op jit(solution)/shard_map/ppermute | solution.py:399
  327.1 1.6 collective-permute-done.52.refs_2_
  328.6 2.2 collective-permute-start.41
  330.8 1.2 collective-permute-start.43
  332.8 2.0 collective-permute-start.44
  335.7 9.9 %psum.7 = f32[32]{0:T(128)S(1)} all-reduce(f32[32]{0:T(128)S(1)} %add_reduce_fusion), channel_id=1, replica_groups=mesh['patch'=4,'shot'=8] {'patch'}, use_global_device_ids=true, to_apply=%region_1.0 | all-reduce | flops 32 | bytes 256 | tf_op jit(solution)/shard_map/psum | solution.py:524
  345.6 1.5 collective-permute-start.46
  347.1 4.1 collective-permute-done.42.refs_6_
  351.2 7.0 %collective-permute-done.43.refs_7_ = bf16[32,48,128]{2,1,0:T(8,128)(2,1)} collective-permute-done((bf16[32,48,128]{2,1,0:T(8,128)(2,1)}, bf16[32,48,128]{2,1,0:T(8,128)(2,1)}, u32[]{:S(2)}, u32[]{:S(2)}) %collective-permute-start.43) | collective-permute-done | bytes 393248 | tf_op jit(solution)/shard_map/ppermute | solution.py:399
  358.2 2.2 collective-permute-start.48
  360.5 38.4 %collective-permute-done.44.refs_1_ = bf16[32,48,128]{2,1,0:T(8,128)(2,1)} collective-permute-done((bf16[32,48,128]{2,1,0:T(8,128)(2,1)}, bf16[32,48,128]{2,1,0:T(8,128)(2,1)}, u32[]{:S(2)}, u32[]{:S(2)}) %collective-permute-start.44) | collective-permute-done | bytes 393248 | tf_op jit(solution)/shard_map/ppermute | solution.py:399
  402.0 9.3 %update.5 = (f32[32,128,1024]{2,1,0:T(8,128)}, f32[8,128]{1,0:T(8,128)S(1)}) custom-call(s32[9]{0:T(128)S(1)} %copy-done.9, bf16[1024,1024]{1,0:T(8,128)(2,1)S(1)} %copy-done, bf16[32,16,128]{2,1,0:T(8,128)(2,1)S(1)} %copy-done.1, bf16[32,48,128]{2,1,0:T(8,128)(2,1)S(1)} %copy-done.2, ...), custom_call_target="tpu_custom_call", output_to_operand_aliasing={{0}: (11, {})} | custom-call | flops 3221225472 | bytes 11534336 | tf_op jit(solution)/shard_map/update/pallas_call | solution.py:358
  411.3 1.2 collective-permute-start.53
  412.5 2.2 collective-permute-start.54
  414.8 1.6 collective-permute-start.55
  416.4 7.9 %collective-permute-done.49.refs_6_ = bf16[32,48,128]{2,1,0:T(8,128)(2,1)S(1)} collective-permute-done((bf16[32,48,128]{2,1,0:T(8,128)(2,1)}, bf16[32,48,128]{2,1,0:T(8,128)(2,1)S(1)}, u32[]{:S(2)}, u32[]{:S(2)}) %collective-permute-start.49) | collective-permute-done | bytes 393248 | tf_op jit(solution)/shard_map/ppermute | solution.py:399
  424.3 4.5 %collective-permute-start.56 = (bf16[32,16,128]{2,1,0:T(8,128)(2,1)S(1)}, bf16[32,16,128]{2,1,0:T(8,128)(2,1)S(1)}, u32[]{:S(2)}, u32[]{:S(2)}) collective-permute-start(bf16[32,16,128]{2,1,0:T(8,128)(2,1)S(1)} %copy-done.44), channel_id=1, source_target_pairs={{0,3},{1,2},{2,1},{3,0},{4,7},{5,6},{6,5},{7,4},{8,11},{9,10},{10,... | collective-permute-start | bytes 393224 | tf_op jit(solution)/shard_map/ppermute | solution.py:399
  428.8 4.1 collective-permute-start.57
  432.9 8.7 %update.6 = (f32[32,128,1024]{2,1,0:T(8,128)}, f32[8,128]{1,0:T(8,128)S(1)}) custom-call(s32[9]{0:T(128)S(1)} %copy-done.9, bf16[1024,1024]{1,0:T(8,128)(2,1)S(1)} %copy-done, f32[8,128]{1,0:T(8,128)S(1)} %get-tuple-element.133._, bf16[32,48,128]{2,1,0:T(8,128)(2,1)S(1)} %copy-done.6, ...), custom_call_target="tpu_custom_call", output_to_operand_aliasing={{0}: (11, {})} | custom-call | flops 3221225472 | bytes 11534336 | tf_op jit(solution)/shard_map/update/pallas_call | solution.py:358
  442.1 3.2 update.7
  (192 shorter events, 23.1 us)
Async XLA Ops:
  3.1 5.8 %collective-permute-start = (bf16[3,128,1024]{2,1,0:T(8,128)(2,1)S(1)}, bf16[3,128,1024]{2,1,0:T(8,128)(2,1)S(1)}, u32[]{:S(2)}, u32[]{:S(2)}) collective-permute-start(bf16[3,128,1024]{2,1,0:T(8,128)(2,1)S(1)} %pad_maximum_fusion), channel_id=1, source_target_pairs={{0,1},{1,2},{2,3},{3,4},{4,5},{5,6},{6,7},{8,9},{9,10},{10,11},{11... | collective-permute-start | bytes 2359304 | tf_op jit(solution)/shard_map/ppermute | solution.py:410
  5.5 6.3 %collective-permute-start.1 = (bf16[3,128,1024]{2,1,0:T(8,128)(2,1)S(1)}, bf16[3,128,1024]{2,1,0:T(8,128)(2,1)S(1)}, u32[]{:S(2)}, u32[]{:S(2)}) collective-permute-start(bf16[3,128,1024]{2,1,0:T(8,128)(2,1)S(1)} %pad_maximum_fusion.1), channel_id=1, source_target_pairs={{1,0},{2,1},{3,2},{4,3},{5,4},{6,5},{7,6},{9,8},{10,9},{11,10},{12... | collective-permute-start | bytes 2359304 | tf_op jit(solution)/shard_map/ppermute | solution.py:410
  22.7 36.5 %collective-permute-start.2 = (bf16[32,16,128]{2,1,0:T(8,128)(2,1)}, bf16[32,16,128]{2,1,0:T(8,128)(2,1)S(1)}, u32[]{:S(2)}, u32[]{:S(2)}) collective-permute-start(bf16[32,16,128]{2,1,0:T(8,128)(2,1)} %get-tuple-element.81), channel_id=1, source_target_pairs={{0,4},{1,5},{2,6},{3,7},{4,0},{5,1},{6,2},{7,3},{8,12},{9,13},{10,... | collective-permute-start | bytes 393224 | tf_op jit(solution)/shard_map/ppermute | solution.py:399
  33.0 26.2 %collective-permute-start.3 = (bf16[32,16,128]{2,1,0:T(8,128)(2,1)}, bf16[32,16,128]{2,1,0:T(8,128)(2,1)S(1)}, u32[]{:S(2)}, u32[]{:S(2)}) collective-permute-start(bf16[32,16,128]{2,1,0:T(8,128)(2,1)} %get-tuple-element.82), channel_id=1, source_target_pairs={{0,1},{1,0},{2,3},{3,2},{4,5},{5,4},{6,7},{7,6},{8,9},{9,8},{10,11... | collective-permute-start | bytes 393224 | tf_op jit(solution)/shard_map/ppermute | solution.py:399
  34.6 46.1 %collective-permute-start.4 = (bf16[32,16,128]{2,1,0:T(8,128)(2,1)}, bf16[32,16,128]{2,1,0:T(8,128)(2,1)S(1)}, u32[]{:S(2)}, u32[]{:S(2)}) collective-permute-start(bf16[32,16,128]{2,1,0:T(8,128)(2,1)} %get-tuple-element.83), channel_id=1, source_target_pairs={{0,5},{1,4},{2,7},{3,6},{4,1},{5,0},{6,3},{7,2},{8,13},{9,12},{10,... | collective-permute-start | bytes 393224 | tf_op jit(solution)/shard_map/ppermute | solution.py:399
  34.7 46.1 %collective-permute-start.5 = (bf16[32,16,128]{2,1,0:T(8,128)(2,1)}, bf16[32,16,128]{2,1,0:T(8,128)(2,1)S(1)}, u32[]{:S(2)}, u32[]{:S(2)}) collective-permute-start(bf16[32,16,128]{2,1,0:T(8,128)(2,1)} %get-tuple-element.84), channel_id=1, source_target_pairs={{0,2},{1,3},{2,0},{3,1},{4,6},{5,7},{6,4},{7,5},{8,10},{9,11},{10,... | collective-permute-start | bytes 393224 | tf_op jit(solution)/shard_map/ppermute | solution.py:399
  36.1 44.6 %collective-permute-start.6 = (bf16[32,16,128]{2,1,0:T(8,128)(2,1)}, bf16[32,16,128]{2,1,0:T(8,128)(2,1)S(1)}, u32[]{:S(2)}, u32[]{:S(2)}) collective-permute-start(bf16[32,16,128]{2,1,0:T(8,128)(2,1)} %get-tuple-element.85), channel_id=1, source_target_pairs={{0,6},{1,7},{2,4},{3,5},{4,2},{5,3},{6,0},{7,1},{8,14},{9,15},{10,... | collective-permute-start | bytes 393224 | tf_op jit(solution)/shard_map/ppermute | solution.py:399
  59.2 21.6 %collective-permute-start.7 = (bf16[32,16,128]{2,1,0:T(8,128)(2,1)S(1)}, bf16[32,16,128]{2,1,0:T(8,128)(2,1)S(1)}, u32[]{:S(2)}, u32[]{:S(2)}) collective-permute-start(bf16[32,16,128]{2,1,0:T(8,128)(2,1)S(1)} %copy-done.54), channel_id=1, source_target_pairs={{0,3},{1,2},{2,1},{3,0},{4,7},{5,6},{6,5},{7,4},{8,11},{9,10},{10,... | collective-permute-start | bytes 393224 | tf_op jit(solution)/shard_map/ppermute | solution.py:399
  59.3 21.5 %collective-permute-start.8 = (bf16[32,16,128]{2,1,0:T(8,128)(2,1)S(1)}, bf16[32,16,128]{2,1,0:T(8,128)(2,1)S(1)}, u32[]{:S(2)}, u32[]{:S(2)}) collective-permute-start(bf16[32,16,128]{2,1,0:T(8,128)(2,1)S(1)} %copy-done.52), channel_id=1, source_target_pairs={{0,7},{1,6},{2,5},{3,4},{4,3},{5,2},{6,1},{7,0},{8,15},{9,14},{10,... | collective-permute-start | bytes 393224 | tf_op jit(solution)/shard_map/ppermute | solution.py:399
  88.9 13.2 %collective-permute-start.23 = (bf16[32,16,128]{2,1,0:T(8,128)(2,1)}, bf16[32,16,128]{2,1,0:T(8,128)(2,1)S(1)}, u32[]{:S(2)}, u32[]{:S(2)}) collective-permute-start(bf16[32,16,128]{2,1,0:T(8,128)(2,1)} %get-tuple-element.108), channel_id=1, source_target_pairs={{0,4},{1,5},{2,6},{3,7},{4,0},{5,1},{6,2},{7,3},{8,12},{9,13},{10,... | collective-permute-start | bytes 393224 | tf_op jit(solution)/shard_map/ppermute | solution.py:399
  91.2 10.9 %collective-permute-start.24 = (bf16[32,16,128]{2,1,0:T(8,128)(2,1)}, bf16[32,16,128]{2,1,0:T(8,128)(2,1)S(1)}, u32[]{:S(2)}, u32[]{:S(2)}) collective-permute-start(bf16[32,16,128]{2,1,0:T(8,128)(2,1)} %get-tuple-element.109), channel_id=1, source_target_pairs={{0,1},{1,0},{2,3},{3,2},{4,5},{5,4},{6,7},{7,6},{8,9},{9,8},{10,11... | collective-permute-start | bytes 393224 | tf_op jit(solution)/shard_map/ppermute | solution.py:399
  91.2 15.9 %collective-permute-start.25 = (bf16[32,16,128]{2,1,0:T(8,128)(2,1)}, bf16[32,16,128]{2,1,0:T(8,128)(2,1)S(1)}, u32[]{:S(2)}, u32[]{:S(2)}) collective-permute-start(bf16[32,16,128]{2,1,0:T(8,128)(2,1)} %get-tuple-element.110), channel_id=1, source_target_pairs={{0,5},{1,4},{2,7},{3,6},{4,1},{5,0},{6,3},{7,2},{8,13},{9,12},{10,... | collective-permute-start | bytes 393224 | tf_op jit(solution)/shard_map/ppermute | solution.py:399
  92.0 15.8 %collective-permute-start.26 = (bf16[32,16,128]{2,1,0:T(8,128)(2,1)}, bf16[32,16,128]{2,1,0:T(8,128)(2,1)S(1)}, u32[]{:S(2)}, u32[]{:S(2)}) collective-permute-start(bf16[32,16,128]{2,1,0:T(8,128)(2,1)} %get-tuple-element.111), channel_id=1, source_target_pairs={{0,2},{1,3},{2,0},{3,1},{4,6},{5,7},{6,4},{7,5},{8,10},{9,11},{10,... | collective-permute-start | bytes 393224 | tf_op jit(solution)/shard_map/ppermute | solution.py:399
  93.2 15.4 %collective-permute-start.27 = (bf16[32,16,128]{2,1,0:T(8,128)(2,1)}, bf16[32,16,128]{2,1,0:T(8,128)(2,1)S(1)}, u32[]{:S(2)}, u32[]{:S(2)}) collective-permute-start(bf16[32,16,128]{2,1,0:T(8,128)(2,1)} %get-tuple-element.112), channel_id=1, source_target_pairs={{0,6},{1,7},{2,4},{3,5},{4,2},{5,3},{6,0},{7,1},{8,14},{9,15},{10,... | collective-permute-start | bytes 393224 | tf_op jit(solution)/shard_map/ppermute | solution.py:399
  102.1 21.0 %collective-permute-start.28 = (bf16[32,16,128]{2,1,0:T(8,128)(2,1)}, bf16[32,16,128]{2,1,0:T(8,128)(2,1)S(1)}, u32[]{:S(2)}, u32[]{:S(2)}) collective-permute-start(bf16[32,16,128]{2,1,0:T(8,128)(2,1)} %get-tuple-element.113), channel_id=1, source_target_pairs={{0,3},{1,2},{2,1},{3,0},{4,7},{5,6},{6,5},{7,4},{8,11},{9,10},{10,... | collective-permute-start | bytes 393224 | tf_op jit(solution)/shard_map/ppermute | solution.py:399
  102.1 31.8 %collective-permute-start.29 = (bf16[32,16,128]{2,1,0:T(8,128)(2,1)}, bf16[32,16,128]{2,1,0:T(8,128)(2,1)S(1)}, u32[]{:S(2)}, u32[]{:S(2)}) collective-permute-start(bf16[32,16,128]{2,1,0:T(8,128)(2,1)} %get-tuple-element.114), channel_id=1, source_target_pairs={{0,7},{1,6},{2,5},{3,4},{4,3},{5,2},{6,1},{7,0},{8,15},{9,14},{10,... | collective-permute-start | bytes 393224 | tf_op jit(solution)/shard_map/ppermute | solution.py:399
  107.8 51.3 %collective-permute-start.9 = (bf16[32,48,128]{2,1,0:T(8,128)(2,1)}, bf16[32,48,128]{2,1,0:T(8,128)(2,1)}, u32[]{:S(2)}, u32[]{:S(2)}) collective-permute-start(bf16[32,48,128]{2,1,0:T(8,128)(2,1)} %get-tuple-element.91), channel_id=1, source_target_pairs={{0,4},{1,5},{2,6},{3,7},{4,0},{5,1},{6,2},{7,3},{8,12},{9,13},{10,... | collective-permute-start | bytes 1179656 | tf_op jit(solution)/shard_map/ppermute | solution.py:399
  108.4 50.6 %collective-permute-start.10 = (bf16[32,48,128]{2,1,0:T(8,128)(2,1)}, bf16[32,48,128]{2,1,0:T(8,128)(2,1)}, u32[]{:S(2)}, u32[]{:S(2)}) collective-permute-start(bf16[32,48,128]{2,1,0:T(8,128)(2,1)} %get-tuple-element.92), channel_id=1, source_target_pairs={{0,1},{1,0},{2,3},{3,2},{4,5},{5,4},{6,7},{7,6},{8,9},{9,8},{10,11... | collective-permute-start | bytes 1179656 | tf_op jit(solution)/shard_map/ppermute | solution.py:399
  109.2 50.8 %collective-permute-start.11 = (bf16[32,48,128]{2,1,0:T(8,128)(2,1)}, bf16[32,48,128]{2,1,0:T(8,128)(2,1)}, u32[]{:S(2)}, u32[]{:S(2)}) collective-permute-start(bf16[32,48,128]{2,1,0:T(8,128)(2,1)} %get-tuple-element.93), channel_id=1, source_target_pairs={{0,5},{1,4},{2,7},{3,6},{4,1},{5,0},{6,3},{7,2},{8,13},{9,12},{10,... | collective-permute-start | bytes 1179656 | tf_op jit(solution)/shard_map/ppermute | solution.py:399
  123.7 38.6 %collective-permute-start.12 = (bf16[32,48,128]{2,1,0:T(8,128)(2,1)S(1)}, bf16[32,48,128]{2,1,0:T(8,128)(2,1)}, u32[]{:S(2)}, u32[]{:S(2)}) collective-permute-start(bf16[32,48,128]{2,1,0:T(8,128)(2,1)S(1)} %copy-done.34), channel_id=1, source_target_pairs={{0,2},{1,3},{2,0},{3,1},{4,6},{5,7},{6,4},{7,5},{8,10},{9,11},{10,... | collective-permute-start | bytes 1179656 | tf_op jit(solution)/shard_map/ppermute | solution.py:399
  123.8 102.9 %copy-start.27 = (bf16[32,48,128]{2,1,0:T(8,128)(2,1)S(1)}, bf16[32,48,128]{2,1,0:T(8,128)(2,1)}, u32[]{:S(2)}) copy-start(bf16[32,48,128]{2,1,0:T(8,128)(2,1)} %get-tuple-element.105) | copy-start | bytes 1179652
  123.8 102.9 %copy-start.26 = (bf16[32,48,128]{2,1,0:T(8,128)(2,1)S(1)}, bf16[32,48,128]{2,1,0:T(8,128)(2,1)}, u32[]{:S(2)}) copy-start(bf16[32,48,128]{2,1,0:T(8,128)(2,1)} %get-tuple-element.106) | copy-start | bytes 1179652
  133.9 141.4 %copy-start.18 = (bf16[32,16,128]{2,1,0:T(8,128)(2,1)}, bf16[32,16,128]{2,1,0:T(8,128)(2,1)S(1)}, u32[]{:S(2)}) copy-start(bf16[32,16,128]{2,1,0:T(8,128)(2,1)S(1)} %collective-permute-done.29.refs_7_) | copy-start | bytes 393220
  133.9 21.2 %collective-permute-start.30 = (bf16[32,16,128]{2,1,0:T(8,128)(2,1)}, bf16[32,16,128]{2,1,0:T(8,128)(2,1)S(1)}, u32[]{:S(2)}, u32[]{:S(2)}) collective-permute-start(bf16[32,16,128]{2,1,0:T(8,128)(2,1)} %get-tuple-element.117), channel_id=1, source_target_pairs={{0,4},{1,5},{2,6},{3,7},{4,0},{5,1},{6,2},{7,3},{8,12},{9,13},{10,... | collective-permute-start | bytes 393224 | tf_op jit(solution)/shard_map/ppermute | solution.py:399
  155.0 1.6 collective-permute-start.31
  156.6 13.8 %collective-permute-start.13 = (bf16[32,48,128]{2,1,0:T(8,128)(2,1)S(1)}, bf16[32,48,128]{2,1,0:T(8,128)(2,1)S(1)}, u32[]{:S(2)}, u32[]{:S(2)}) collective-permute-start(bf16[32,48,128]{2,1,0:T(8,128)(2,1)S(1)} %copy-done.33), channel_id=1, source_target_pairs={{0,6},{1,7},{2,4},{3,5},{4,2},{5,3},{6,0},{7,1},{8,14},{9,15},{10,... | collective-permute-start | bytes 1179656 | tf_op jit(solution)/shard_map/ppermute | solution.py:399
  159.0 19.9 %collective-permute-start.14 = (bf16[32,48,128]{2,1,0:T(8,128)(2,1)S(1)}, bf16[32,48,128]{2,1,0:T(8,128)(2,1)S(1)}, u32[]{:S(2)}, u32[]{:S(2)}) collective-permute-start(bf16[32,48,128]{2,1,0:T(8,128)(2,1)S(1)} %copy-done.31), channel_id=1, source_target_pairs={{0,3},{1,2},{2,1},{3,0},{4,7},{5,6},{6,5},{7,4},{8,11},{9,10},{10,... | collective-permute-start | bytes 1179656 | tf_op jit(solution)/shard_map/ppermute | solution.py:399
  159.0 26.9 %collective-permute-start.15 = (bf16[32,48,128]{2,1,0:T(8,128)(2,1)S(1)}, bf16[32,48,128]{2,1,0:T(8,128)(2,1)S(1)}, u32[]{:S(2)}, u32[]{:S(2)}) collective-permute-start(bf16[32,48,128]{2,1,0:T(8,128)(2,1)S(1)} %copy-done.29), channel_id=1, source_target_pairs={{0,7},{1,6},{2,5},{3,4},{4,3},{5,2},{6,1},{7,0},{8,15},{9,14},{10,... | collective-permute-start | bytes 1179656 | tf_op jit(solution)/shard_map/ppermute | solution.py:399
  160.0 66.7 %collective-permute-start.16 = (bf16[32,48,128]{2,1,0:T(8,128)(2,1)S(1)}, bf16[32,48,128]{2,1,0:T(8,128)(2,1)S(1)}, u32[]{:S(2)}, u32[]{:S(2)}) collective-permute-start(bf16[32,48,128]{2,1,0:T(8,128)(2,1)S(1)} %copy-done.32), channel_id=1, source_target_pairs={{0,4},{1,5},{2,6},{3,7},{4,0},{5,1},{6,2},{7,3},{8,12},{9,13},{10,... | collective-permute-start | bytes 1179656 | tf_op jit(solution)/shard_map/ppermute | solution.py:399
  162.3 64.4 %collective-permute-start.17 = (bf16[32,48,128]{2,1,0:T(8,128)(2,1)S(1)}, bf16[32,48,128]{2,1,0:T(8,128)(2,1)S(1)}, u32[]{:S(2)}, u32[]{:S(2)}) collective-permute-start(bf16[32,48,128]{2,1,0:T(8,128)(2,1)S(1)} %copy-done.30), channel_id=1, source_target_pairs={{0,1},{1,0},{2,3},{3,2},{4,5},{5,4},{6,7},{7,6},{8,9},{9,8},{10,11... | collective-permute-start | bytes 1179656 | tf_op jit(solution)/shard_map/ppermute | solution.py:399
  170.5 74.2 %collective-permute-start.18 = (bf16[32,48,128]{2,1,0:T(8,128)(2,1)}, bf16[32,48,128]{2,1,0:T(8,128)(2,1)}, u32[]{:S(2)}, u32[]{:S(2)}) collective-permute-start(bf16[32,48,128]{2,1,0:T(8,128)(2,1)} %get-tuple-element.102), channel_id=1, source_target_pairs={{0,5},{1,4},{2,7},{3,6},{4,1},{5,0},{6,3},{7,2},{8,13},{9,12},{10,... | collective-permute-start | bytes 1179656 | tf_op jit(solution)/shard_map/ppermute | solution.py:399
  178.9 67.4 %collective-permute-start.19 = (bf16[32,48,128]{2,1,0:T(8,128)(2,1)}, bf16[32,48,128]{2,1,0:T(8,128)(2,1)}, u32[]{:S(2)}, u32[]{:S(2)}) collective-permute-start(bf16[32,48,128]{2,1,0:T(8,128)(2,1)} %get-tuple-element.103), channel_id=1, source_target_pairs={{0,2},{1,3},{2,0},{3,1},{4,6},{5,7},{6,4},{7,5},{8,10},{9,11},{10,... | collective-permute-start | bytes 1179656 | tf_op jit(solution)/shard_map/ppermute | solution.py:399
  185.9 62.2 %collective-permute-start.20 = (bf16[32,48,128]{2,1,0:T(8,128)(2,1)S(1)}, bf16[32,48,128]{2,1,0:T(8,128)(2,1)}, u32[]{:S(2)}, u32[]{:S(2)}) collective-permute-start(bf16[32,48,128]{2,1,0:T(8,128)(2,1)S(1)} %copy-done.28), channel_id=1, source_target_pairs={{0,6},{1,7},{2,4},{3,5},{4,2},{5,3},{6,0},{7,1},{8,14},{9,15},{10,... | collective-permute-start | bytes 1179656 | tf_op jit(solution)/shard_map/ppermute | solution.py:399
  226.7 24.7 %collective-permute-start.21 = (bf16[32,48,128]{2,1,0:T(8,128)(2,1)S(1)}, bf16[32,48,128]{2,1,0:T(8,128)(2,1)}, u32[]{:S(2)}, u32[]{:S(2)}) collective-permute-start(bf16[32,48,128]{2,1,0:T(8,128)(2,1)S(1)} %copy-done.27), channel_id=1, source_target_pairs={{0,3},{1,2},{2,1},{3,0},{4,7},{5,6},{6,5},{7,4},{8,11},{9,10},{10,... | collective-permute-start | bytes 1179656 | tf_op jit(solution)/shard_map/ppermute | solution.py:399
  226.7 26.9 %collective-permute-start.22 = (bf16[32,48,128]{2,1,0:T(8,128)(2,1)S(1)}, bf16[32,48,128]{2,1,0:T(8,128)(2,1)}, u32[]{:S(2)}, u32[]{:S(2)}) collective-permute-start(bf16[32,48,128]{2,1,0:T(8,128)(2,1)S(1)} %copy-done.26), channel_id=1, source_target_pairs={{0,7},{1,6},{2,5},{3,4},{4,3},{5,2},{6,1},{7,0},{8,15},{9,14},{10,... | collective-permute-start | bytes 1179656 | tf_op jit(solution)/shard_map/ppermute | solution.py:399
  244.7 30.6 %collective-permute-start.32 = (bf16[32,16,128]{2,1,0:T(8,128)(2,1)}, bf16[32,16,128]{2,1,0:T(8,128)(2,1)}, u32[]{:S(2)}, u32[]{:S(2)}) collective-permute-start(bf16[32,16,128]{2,1,0:T(8,128)(2,1)} %get-tuple-element.119), channel_id=1, source_target_pairs={{0,5},{1,4},{2,7},{3,6},{4,1},{5,0},{6,3},{7,2},{8,13},{9,12},{10,... | collective-permute-start | bytes 393224 | tf_op jit(solution)/shard_map/ppermute | solution.py:399
  246.3 41.3 %collective-permute-start.33 = (bf16[32,16,128]{2,1,0:T(8,128)(2,1)S(1)}, bf16[32,16,128]{2,1,0:T(8,128)(2,1)}, u32[]{:S(2)}, u32[]{:S(2)}) collective-permute-start(bf16[32,16,128]{2,1,0:T(8,128)(2,1)S(1)} %copy-done.47), channel_id=1, source_target_pairs={{0,2},{1,3},{2,0},{3,1},{4,6},{5,7},{6,4},{7,5},{8,10},{9,11},{10,... | collective-permute-start | bytes 393224 | tf_op jit(solution)/shard_map/ppermute | solution.py:399
  248.1 39.5 %collective-permute-start.34 = (bf16[32,16,128]{2,1,0:T(8,128)(2,1)S(1)}, bf16[32,16,128]{2,1,0:T(8,128)(2,1)}, u32[]{:S(2)}, u32[]{:S(2)}) collective-permute-start(bf16[32,16,128]{2,1,0:T(8,128)(2,1)S(1)} %copy-done.43), channel_id=1, source_target_pairs={{0,6},{1,7},{2,4},{3,5},{4,2},{5,3},{6,0},{7,1},{8,14},{9,15},{10,... | collective-permute-start | bytes 393224 | tf_op jit(solution)/shard_map/ppermute | solution.py:399
  251.4 36.4 %collective-permute-start.35 = (bf16[32,16,128]{2,1,0:T(8,128)(2,1)}, bf16[32,16,128]{2,1,0:T(8,128)(2,1)}, u32[]{:S(2)}, u32[]{:S(2)}) collective-permute-start(bf16[32,16,128]{2,1,0:T(8,128)(2,1)} %get-tuple-element.122), channel_id=1, source_target_pairs={{0,3},{1,2},{2,1},{3,0},{4,7},{5,6},{6,5},{7,4},{8,11},{9,10},{10,... | collective-permute-start | bytes 393224 | tf_op jit(solution)/shard_map/ppermute | solution.py:399
  253.6 45.4 %collective-permute-start.36 = (bf16[32,16,128]{2,1,0:T(8,128)(2,1)}, bf16[32,16,128]{2,1,0:T(8,128)(2,1)}, u32[]{:S(2)}, u32[]{:S(2)}) collective-permute-start(bf16[32,16,128]{2,1,0:T(8,128)(2,1)} %get-tuple-element.123), channel_id=1, source_target_pairs={{0,7},{1,6},{2,5},{3,4},{4,3},{5,2},{6,1},{7,0},{8,15},{9,14},{10,... | collective-permute-start | bytes 393224 | tf_op jit(solution)/shard_map/ppermute | solution.py:399
  258.2 76.7 %copy-start.25 = (f32[32,128]{1,0:T(8,128)S(1)}, f32[32,128]{1,0:T(8,128)}, u32[]{:S(2)}) copy-start(f32[32,128]{1,0:T(8,128)} %get-tuple-element.79._) | copy-start | bytes 49156
  258.2 141.9 %copy-start.2 = (bf16[32,48,128]{2,1,0:T(8,128)(2,1)S(1)}, bf16[32,48,128]{2,1,0:T(8,128)(2,1)}, u32[]{:S(2)}) copy-start(bf16[32,48,128]{2,1,0:T(8,128)(2,1)} %get-tuple-element.98._.refs_0_) | copy-start | bytes 1179652
  258.2 141.9 %copy-start.9 = (s32[9]{0:T(128)S(1)}, s32[9]{0:T(128)}, u32[]{:S(2)}) copy-start(s32[9]{0:T(128)} %pad_add_fusion.meta_ref) | copy-start | bytes 112
  275.3 55.6 %collective-permute-start.37 = (bf16[32,48,128]{2,1,0:T(8,128)(2,1)}, bf16[32,48,128]{2,1,0:T(8,128)(2,1)S(1)}, u32[]{:S(2)}, u32[]{:S(2)}) collective-permute-start(bf16[32,48,128]{2,1,0:T(8,128)(2,1)} %get-tuple-element.125), channel_id=1, source_target_pairs={{0,4},{1,5},{2,6},{3,7},{4,0},{5,1},{6,2},{7,3},{8,12},{9,13},{10,... | collective-permute-start | bytes 1179656 | tf_op jit(solution)/shard_map/ppermute | solution.py:399
  287.6 43.3 %collective-permute-start.38 = (bf16[32,48,128]{2,1,0:T(8,128)(2,1)}, bf16[32,48,128]{2,1,0:T(8,128)(2,1)S(1)}, u32[]{:S(2)}, u32[]{:S(2)}) collective-permute-start(bf16[32,48,128]{2,1,0:T(8,128)(2,1)} %get-tuple-element.126), channel_id=1, source_target_pairs={{0,1},{1,0},{2,3},{3,2},{4,5},{5,4},{6,7},{7,6},{8,9},{9,8},{10,11... | collective-permute-start | bytes 1179656 | tf_op jit(solution)/shard_map/ppermute | solution.py:399
  287.6 44.4 %collective-permute-start.39 = (bf16[32,48,128]{2,1,0:T(8,128)(2,1)}, bf16[32,48,128]{2,1,0:T(8,128)(2,1)S(1)}, u32[]{:S(2)}, u32[]{:S(2)}) collective-permute-start(bf16[32,48,128]{2,1,0:T(8,128)(2,1)} %get-tuple-element.127), channel_id=1, source_target_pairs={{0,5},{1,4},{2,7},{3,6},{4,1},{5,0},{6,3},{7,2},{8,13},{9,12},{10,... | collective-permute-start | bytes 1179656 | tf_op jit(solution)/shard_map/ppermute | solution.py:399
  287.8 47.0 %collective-permute-start.40 = (bf16[32,48,128]{2,1,0:T(8,128)(2,1)}, bf16[32,48,128]{2,1,0:T(8,128)(2,1)}, u32[]{:S(2)}, u32[]{:S(2)}) collective-permute-start(bf16[32,48,128]{2,1,0:T(8,128)(2,1)} %get-tuple-element.128), channel_id=1, source_target_pairs={{0,2},{1,3},{2,0},{3,1},{4,6},{5,7},{6,4},{7,5},{8,10},{9,11},{10,... | collective-permute-start | bytes 1179656 | tf_op jit(solution)/shard_map/ppermute | solution.py:399
  306.3 20.8 %collective-permute-start.51 = (bf16[32,16,128]{2,1,0:T(8,128)(2,1)}, bf16[32,16,128]{2,1,0:T(8,128)(2,1)S(1)}, u32[]{:S(2)}, u32[]{:S(2)}) collective-permute-start(bf16[32,16,128]{2,1,0:T(8,128)(2,1)} %get-tuple-element.143), channel_id=1, source_target_pairs={{0,4},{1,5},{2,6},{3,7},{4,0},{5,1},{6,2},{7,3},{8,12},{9,13},{10,... | collective-permute-start | bytes 393224 | tf_op jit(solution)/shard_map/ppermute | solution.py:399
  327.1 1.6 collective-permute-start.52
  328.6 17.0 %collective-permute-start.41 = (bf16[32,48,128]{2,1,0:T(8,128)(2,1)}, bf16[32,48,128]{2,1,0:T(8,128)(2,1)}, u32[]{:S(2)}, u32[]{:S(2)}) collective-permute-start(bf16[32,48,128]{2,1,0:T(8,128)(2,1)} %get-tuple-element.129), channel_id=1, source_target_pairs={{0,6},{1,7},{2,4},{3,5},{4,2},{5,3},{6,0},{7,1},{8,14},{9,15},{10,... | collective-permute-start | bytes 1179656 | tf_op jit(solution)/shard_map/ppermute | solution.py:399
  330.8 20.4 %collective-permute-start.42 = (bf16[32,48,128]{2,1,0:T(8,128)(2,1)}, bf16[32,48,128]{2,1,0:T(8,128)(2,1)}, u32[]{:S(2)}, u32[]{:S(2)}) collective-permute-start(bf16[32,48,128]{2,1,0:T(8,128)(2,1)} %get-tuple-element.130), channel_id=1, source_target_pairs={{0,3},{1,2},{2,1},{3,0},{4,7},{5,6},{6,5},{7,4},{8,11},{9,10},{10,... | collective-permute-start | bytes 1179656 | tf_op jit(solution)/shard_map/ppermute | solution.py:399
  330.8 27.4 %collective-permute-start.43 = (bf16[32,48,128]{2,1,0:T(8,128)(2,1)}, bf16[32,48,128]{2,1,0:T(8,128)(2,1)}, u32[]{:S(2)}, u32[]{:S(2)}) collective-permute-start(bf16[32,48,128]{2,1,0:T(8,128)(2,1)} %get-tuple-element.131), channel_id=1, source_target_pairs={{0,7},{1,6},{2,5},{3,4},{4,3},{5,2},{6,1},{7,0},{8,15},{9,14},{10,... | collective-permute-start | bytes 1179656 | tf_op jit(solution)/shard_map/ppermute | solution.py:399
  332.8 66.0 %collective-permute-start.44 = (bf16[32,48,128]{2,1,0:T(8,128)(2,1)}, bf16[32,48,128]{2,1,0:T(8,128)(2,1)}, u32[]{:S(2)}, u32[]{:S(2)}) collective-permute-start(bf16[32,48,128]{2,1,0:T(8,128)(2,1)} %get-tuple-element.134), channel_id=1, source_target_pairs={{0,4},{1,5},{2,6},{3,7},{4,0},{5,1},{6,2},{7,3},{8,12},{9,13},{10,... | collective-permute-start | bytes 1179656 | tf_op jit(solution)/shard_map/ppermute | solution.py:399
  334.8 64.0 %collective-permute-start.45 = (bf16[32,48,128]{2,1,0:T(8,128)(2,1)}, bf16[32,48,128]{2,1,0:T(8,128)(2,1)}, u32[]{:S(2)}, u32[]{:S(2)}) collective-permute-start(bf16[32,48,128]{2,1,0:T(8,128)(2,1)} %get-tuple-element.135), channel_id=1, source_target_pairs={{0,1},{1,0},{2,3},{3,2},{4,5},{5,4},{6,7},{7,6},{8,9},{9,8},{10,11... | collective-permute-start | bytes 1179656 | tf_op jit(solution)/shard_map/ppermute | solution.py:399
  345.6 65.7 %collective-permute-start.46 = (bf16[32,48,128]{2,1,0:T(8,128)(2,1)}, bf16[32,48,128]{2,1,0:T(8,128)(2,1)S(1)}, u32[]{:S(2)}, u32[]{:S(2)}) collective-permute-start(bf16[32,48,128]{2,1,0:T(8,128)(2,1)} %get-tuple-element.136), channel_id=1, source_target_pairs={{0,5},{1,4},{2,7},{3,6},{4,1},{5,0},{6,3},{7,2},{8,13},{9,12},{10,... | collective-permute-start | bytes 1179656 | tf_op jit(solution)/shard_map/ppermute | solution.py:399
  351.2 61.3 %collective-permute-start.47 = (bf16[32,48,128]{2,1,0:T(8,128)(2,1)}, bf16[32,48,128]{2,1,0:T(8,128)(2,1)S(1)}, u32[]{:S(2)}, u32[]{:S(2)}) collective-permute-start(bf16[32,48,128]{2,1,0:T(8,128)(2,1)} %get-tuple-element.137), channel_id=1, source_target_pairs={{0,2},{1,3},{2,0},{3,1},{4,6},{5,7},{6,4},{7,5},{8,10},{9,11},{10,... | collective-permute-start | bytes 1179656 | tf_op jit(solution)/shard_map/ppermute | solution.py:399
  358.2 56.5 %collective-permute-start.48 = (bf16[32,48,128]{2,1,0:T(8,128)(2,1)}, bf16[32,48,128]{2,1,0:T(8,128)(2,1)S(1)}, u32[]{:S(2)}, u32[]{:S(2)}) collective-permute-start(bf16[32,48,128]{2,1,0:T(8,128)(2,1)} %get-tuple-element.138), channel_id=1, source_target_pairs={{0,6},{1,7},{2,4},{3,5},{4,2},{5,3},{6,0},{7,1},{8,14},{9,15},{10,... | collective-permute-start | bytes 1179656 | tf_op jit(solution)/shard_map/ppermute | solution.py:399
  398.8 25.5 %collective-permute-start.49 = (bf16[32,48,128]{2,1,0:T(8,128)(2,1)}, bf16[32,48,128]{2,1,0:T(8,128)(2,1)S(1)}, u32[]{:S(2)}, u32[]{:S(2)}) collective-permute-start(bf16[32,48,128]{2,1,0:T(8,128)(2,1)} %get-tuple-element.139), channel_id=1, source_target_pairs={{0,3},{1,2},{2,1},{3,0},{4,7},{5,6},{6,5},{7,4},{8,11},{9,10},{10,... | collective-permute-start | bytes 1179656 | tf_op jit(solution)/shard_map/ppermute | solution.py:399
  398.8 30.0 %collective-permute-start.50 = (bf16[32,48,128]{2,1,0:T(8,128)(2,1)}, bf16[32,48,128]{2,1,0:T(8,128)(2,1)S(1)}, u32[]{:S(2)}, u32[]{:S(2)}) collective-permute-start(bf16[32,48,128]{2,1,0:T(8,128)(2,1)} %get-tuple-element.140), channel_id=1, source_target_pairs={{0,7},{1,6},{2,5},{3,4},{4,3},{5,2},{6,1},{7,0},{8,15},{9,14},{10,... | collective-permute-start | bytes 1179656 | tf_op jit(solution)/shard_map/ppermute | solution.py:399
  411.3 30.8 %collective-permute-start.53 = (bf16[32,16,128]{2,1,0:T(8,128)(2,1)S(1)}, bf16[32,16,128]{2,1,0:T(8,128)(2,1)S(1)}, u32[]{:S(2)}, u32[]{:S(2)}) collective-permute-start(bf16[32,16,128]{2,1,0:T(8,128)(2,1)S(1)} %copy-done.48), channel_id=1, source_target_pairs={{0,5},{1,4},{2,7},{3,6},{4,1},{5,0},{6,3},{7,2},{8,13},{9,12},{10,... | collective-permute-start | bytes 393224 | tf_op jit(solution)/shard_map/ppermute | solution.py:399
  412.5 29.6 %collective-permute-start.54 = (bf16[32,16,128]{2,1,0:T(8,128)(2,1)S(1)}, bf16[32,16,128]{2,1,0:T(8,128)(2,1)S(1)}, u32[]{:S(2)}, u32[]{:S(2)}) collective-permute-start(bf16[32,16,128]{2,1,0:T(8,128)(2,1)S(1)} %copy-done.46), channel_id=1, source_target_pairs={{0,2},{1,3},{2,0},{3,1},{4,6},{5,7},{6,4},{7,5},{8,10},{9,11},{10,... | collective-permute-start | bytes 393224 | tf_op jit(solution)/shard_map/ppermute | solution.py:399
  414.8 27.3 %collective-permute-start.55 = (bf16[32,16,128]{2,1,0:T(8,128)(2,1)S(1)}, bf16[32,16,128]{2,1,0:T(8,128)(2,1)S(1)}, u32[]{:S(2)}, u32[]{:S(2)}) collective-permute-start(bf16[32,16,128]{2,1,0:T(8,128)(2,1)S(1)} %copy-done.45), channel_id=1, source_target_pairs={{0,6},{1,7},{2,4},{3,5},{4,2},{5,3},{6,0},{7,1},{8,14},{9,15},{10,... | collective-permute-start | bytes 393224 | tf_op jit(solution)/shard_map/ppermute | solution.py:399
  424.3 17.8 %collective-permute-start.56 = (bf16[32,16,128]{2,1,0:T(8,128)(2,1)S(1)}, bf16[32,16,128]{2,1,0:T(8,128)(2,1)S(1)}, u32[]{:S(2)}, u32[]{:S(2)}) collective-permute-start(bf16[32,16,128]{2,1,0:T(8,128)(2,1)S(1)} %copy-done.44), channel_id=1, source_target_pairs={{0,3},{1,2},{2,1},{3,0},{4,7},{5,6},{6,5},{7,4},{8,11},{9,10},{10,... | collective-permute-start | bytes 393224 | tf_op jit(solution)/shard_map/ppermute | solution.py:399
  428.8 13.3 %collective-permute-start.57 = (bf16[32,16,128]{2,1,0:T(8,128)(2,1)S(1)}, bf16[32,16,128]{2,1,0:T(8,128)(2,1)S(1)}, u32[]{:S(2)}, u32[]{:S(2)}) collective-permute-start(bf16[32,16,128]{2,1,0:T(8,128)(2,1)S(1)} %copy-done.42), channel_id=1, source_target_pairs={{0,7},{1,6},{2,5},{3,4},{4,3},{5,2},{6,1},{7,0},{8,15},{9,14},{10,... | collective-permute-start | bytes 393224 | tf_op jit(solution)/shard_map/ppermute | solution.py:399
  (52 other events, 1155.6 us)

commit v18 on v16

--- a/solution.py
+++ b/solution.py
@@ -380,10 +380,7 @@
 
 
 def slots_of(peers):
-    order = [0]
-    for slot in range(peers // 2):
-        order += [peers // 2 + slot] + ([slot + 1] if slot + 1 < peers // 2 else [])
-    return order
+    return [0, 1, *range(peers // 2, peers), *range(2, peers // 2)]
 
 
 def exchanged(arrays):

time: 423 us -> 445 us (1.052)
  starting transfers between devices: 130 us -> 162 us
  waiting for transfers between devices: 108 us -> 99 us
    ppermute x70, starting transfers between devices: 126 us -> 158 us  [exchanged(): lax.ppermute(arrays[slot], 'shot', [(i, i ^ slot) for i in range(peers)])]
    ppermute x70, waiting for transfers between devices: 105 us -> 95.9 us  [exchanged(): lax.ppermute(arrays[slot], 'shot', [(i, i ^ slot) for i in range(peers)])]
  transfers between devices with their start and end apart: 72 -> 72, of which waited for: 18 -> 12; matrix products, arithmetic and copies ran while one was open for 1% -> 1% of each run, Pallas kernels for 32% -> 30%
where the time goes in v18:
time: 445 us; the launch traced here: 444 us
  starting transfers between devices  162 us (36%)
  Pallas kernels  149 us (33%)
  waiting for transfers between devices  99 us (22%)
  local copies, waits for them, and re-layouts  20.4 us (5%)
  blocking collectives  9.92 us (2%)
    ppermute x70, starting transfers between devices, exchanged(): lax.ppermute(arrays[slot], 'shot', [(i, i ^ slot) for i in range(peers)])  158 us
    ppermute x70, waiting for transfers between devices, exchanged(): lax.ppermute(arrays[slot], 'shot', [(i, i ^ slot) for i in range(peers)])  95.9 us
    pallas_call x5, Pallas kernels, spectra_of(): pl.pallas_call(spectra_kernel, grid_spec=pltpu.PrefetchScalarGridSpec(num...  64.6 us
    pallas_call x5, Pallas kernels, shrunk_of(): pl.pallas_call(shots_kernel, grid_spec=pltpu.PrefetchScalarGridSpec(num_s...  58.6 us
    pallas_call x5, Pallas kernels, updated_of(): pl.pallas_call(functools.partial(update_kernel, len(restored)), grid_spec...  26 us
    unnamed x154, local copies, waits for them, and re-layouts  16.7 us
    psum x1, blocking collectives, local(): lax.psum(jnp.sum(energy, axis=1), 'patch')  9.92 us
  transfers between devices with their start and end apart: 72, of which 12 were waited for; matrix products, arithmetic and copies ran while one was open for 1% of the time, Pallas kernels for 30%

profile of v18, /device:TPU:0, one launch (start us, length us, event | category | flops | bytes accessed | tf_op | source)
XLA Modules:
  0.0 444.0 jit_solution(11914435734740607123)
XLA Ops:
  3.1 2.4 collective-permute-start
  6.4 1.3 collective-permute-start.1
  9.8 3.2 collective-permute-done.1.after_ref
  13.8 9.9 %spectra.5 = (bf16[32,16,128]{2,1,0:T(8,128)(2,1)}, bf16[32,16,128]{2,1,0:T(8,128)(2,1)}, bf16[32,16,128]{2,1,0:T(8,128)(2,1)}, bf16[32,16,128]{2,1,0:T(8,128)(2...) custom-call(s32[9]{0:T(128)} %pad_add_fusion.meta_ref, ...), custom_call_target="tpu_custom_call" | custom-call | flops 1073741824 | bytes 5242880 | tf_op jit(solution)/shard_map/spectra/pallas_call | solution.py:270
  23.8 9.6 %collective-permute-start.2 = (bf16[32,16,128]{2,1,0:T(8,128)(2,1)}, bf16[32,16,128]{2,1,0:T(8,128)(2,1)S(1)}, u32[]{:S(2)}, u32[]{:S(2)}) collective-permute-start(bf16[32,16,128]{2,1,0:T(8,128)(2,1)} %get-tuple-element.100), channel_id=1, source_target_pairs={{0,1},{1,0},{2,3},{3,2},{4,5},{5,4},{6,7},{7,6},{8,9},{9,8},{10,11... | collective-permute-start | bytes 393224 | tf_op jit(solution)/shard_map/ppermute | solution.py:389
  33.4 2.6 collective-permute-start.3
  36.0 2.0 collective-permute-start.5
  38.0 14.9 %spectra.6 = (bf16[32,32,128]{2,1,0:T(8,128)(2,1)}, bf16[32,32,128]{2,1,0:T(8,128)(2,1)}, bf16[32,32,128]{2,1,0:T(8,128)(2,1)}, bf16[32,32,128]{2,1,0:T(8,128)(2...) custom-call(s32[9]{0:T(128)} %pad_add_fusion.meta_ref, ...), custom_call_target="tpu_custom_call" | custom-call | flops 2147483648 | bytes 8388608 | tf_op jit(solution)/shard_map/spectra/pallas_call | solution.py:270
  54.1 1.9 collective-permute-start.6
  56.4 1.9 collective-permute-start.8
  58.2 6.9 %collective-permute-done.6.refs_5_ = bf16[32,16,128]{2,1,0:T(8,128)(2,1)S(1)} collective-permute-done((bf16[32,16,128]{2,1,0:T(8,128)(2,1)S(1)}, bf16[32,16,128]{2,1,0:T(8,128)(2,1)S(1)}, u32[]{:S(2)}, u32[]{:S(2)}) %collective-permute-start.6) | collective-permute-done | bytes 131104 | tf_op jit(solution)/shard_map/ppermute | solution.py:389
  65.2 9.2 %collective-permute-start.11 = (bf16[32,32,128]{2,1,0:T(8,128)(2,1)}, bf16[32,32,128]{2,1,0:T(8,128)(2,1)S(1)}, u32[]{:S(2)}, u32[]{:S(2)}) collective-permute-start(bf16[32,32,128]{2,1,0:T(8,128)(2,1)} %get-tuple-element.112), channel_id=1, source_target_pairs={{0,5},{1,4},{2,7},{3,6},{4,1},{5,0},{6,3},{7,2},{8,13},{9,12},{10,... | collective-permute-start | bytes 786440 | tf_op jit(solution)/shard_map/ppermute | solution.py:389
  74.4 1.9 collective-permute-start.12
  76.4 1.6 collective-permute-start.13
  78.1 1.7 collective-permute-start.15
  79.7 14.7 %spectra.7 = (bf16[32,32,128]{2,1,0:T(8,128)(2,1)}, bf16[32,32,128]{2,1,0:T(8,128)(2,1)}, bf16[32,32,128]{2,1,0:T(8,128)(2,1)}, bf16[32,32,128]{2,1,0:T(8,128)(2...) custom-call(s32[9]{0:T(128)} %pad_add_fusion.meta_ref, ...), custom_call_target="tpu_custom_call" | custom-call | flops 2147483648 | bytes 8388608 | tf_op jit(solution)/shard_map/spectra/pallas_call | solution.py:270
  94.5 7.3 %shrink.5 = (bf16[32,16,128]{2,1,0:T(8,128)(2,1)}, bf16[32,16,128]{2,1,0:T(8,128)(2,1)}, bf16[32,16,128]{2,1,0:T(8,128)(2,1)}, bf16[32,16,128]{2,1,0:T(8,128)(2,...) custom-call(s32[9]{0:T(128)} %pad_add_fusion.meta_ref, ...), custom_call_target="tpu_custom_call" | custom-call | flops 1073741824 | bytes 2359296 | tf_op jit(solution)/shard_map/shrink/pallas_call | solution.py:320
  102.3 3.2 collective-permute-start.24
  105.5 7.8 %collective-permute-start.25 = (bf16[32,16,128]{2,1,0:T(8,128)(2,1)}, bf16[32,16,128]{2,1,0:T(8,128)(2,1)S(1)}, u32[]{:S(2)}, u32[]{:S(2)}) collective-permute-start(bf16[32,16,128]{2,1,0:T(8,128)(2,1)} %get-tuple-element.130), channel_id=1, source_target_pairs={{0,5},{1,4},{2,7},{3,6},{4,1},{5,0},{6,3},{7,2},{8,13},{9,12},{10,... | collective-permute-start | bytes 393224 | tf_op jit(solution)/shard_map/ppermute | solution.py:389
  113.4 1.9 collective-permute-start.26
  116.7 1.9 collective-permute-start.27
  118.7 13.1 %collective-permute-done.25.refs_3_ = bf16[32,16,128]{2,1,0:T(8,128)(2,1)S(1)} collective-permute-done((bf16[32,16,128]{2,1,0:T(8,128)(2,1)}, bf16[32,16,128]{2,1,0:T(8,128)(2,1)S(1)}, u32[]{:S(2)}, u32[]{:S(2)}) %collective-permute-start.25) | collective-permute-done | bytes 131104 | tf_op jit(solution)/shard_map/ppermute | solution.py:389
  133.1 2.4 collective-permute-start.29
  135.5 14.7 %spectra.8 = (bf16[32,32,128]{2,1,0:T(8,128)(2,1)}, bf16[32,32,128]{2,1,0:T(8,128)(2,1)}, bf16[32,32,128]{2,1,0:T(8,128)(2,1)}, bf16[32,32,128]{2,1,0:T(8,128)(2...) custom-call(s32[9]{0:T(128)} %pad_add_fusion.meta_ref, ...), custom_call_target="tpu_custom_call" | custom-call | flops 2147483648 | bytes 8388608 | tf_op jit(solution)/shard_map/spectra/pallas_call | solution.py:270
  150.8 1.9 collective-permute-start.19
  152.7 2.4 collective-permute-start.20
  156.1 14.7 %shrink.6 = (bf16[32,32,128]{2,1,0:T(8,128)(2,1)}, bf16[32,32,128]{2,1,0:T(8,128)(2,1)}, bf16[32,32,128]{2,1,0:T(8,128)(2,1)}, bf16[32,32,128]{2,1,0:T(8,128)(2,...) custom-call(s32[9]{0:T(128)} %pad_add_fusion.meta_ref, ...), custom_call_target="tpu_custom_call" | custom-call | flops 2147483648 | bytes 4456448 | tf_op jit(solution)/shard_map/shrink/pallas_call | solution.py:320
  170.9 10.4 %spectra.9 = (bf16[32,16,128]{2,1,0:T(8,128)(2,1)}, bf16[32,16,128]{2,1,0:T(8,128)(2,1)}, bf16[32,16,128]{2,1,0:T(8,128)(2,1)}, bf16[32,16,128]{2,1,0:T(8,128)(2...) custom-call(s32[9]{0:T(128)} %pad_add_fusion.meta_ref, ...), custom_call_target="tpu_custom_call" | custom-call | flops 1073741824 | bytes 5242880 | tf_op jit(solution)/shard_map/spectra/pallas_call | solution.py:270
  183.8 7.9 %collective-permute-start.46 = (bf16[32,16,128]{2,1,0:T(8,128)(2,1)}, bf16[32,16,128]{2,1,0:T(8,128)(2,1)S(1)}, u32[]{:S(2)}, u32[]{:S(2)}) collective-permute-start(bf16[32,16,128]{2,1,0:T(8,128)(2,1)} %get-tuple-element.157), channel_id=1, source_target_pairs={{0,5},{1,4},{2,7},{3,6},{4,1},{5,0},{6,3},{7,2},{8,13},{9,12},{10,... | collective-permute-start | bytes 393224 | tf_op jit(solution)/shard_map/ppermute | solution.py:389
  191.7 1.9 collective-permute-start.47
  193.6 1.7 collective-permute-start.48
  195.7 14.8 %collective-permute-done.46.refs_3_ = bf16[32,16,128]{2,1,0:T(8,128)(2,1)S(1)} collective-permute-done((bf16[32,16,128]{2,1,0:T(8,128)(2,1)}, bf16[32,16,128]{2,1,0:T(8,128)(2,1)S(1)}, u32[]{:S(2)}, u32[]{:S(2)}) %collective-permute-start.46) | collective-permute-done | bytes 131104 | tf_op jit(solution)/shard_map/ppermute | solution.py:389
  210.6 8.8 %collective-permute-start.49 = (bf16[32,16,128]{2,1,0:T(8,128)(2,1)}, bf16[32,16,128]{2,1,0:T(8,128)(2,1)S(1)}, u32[]{:S(2)}, u32[]{:S(2)}) collective-permute-start(bf16[32,16,128]{2,1,0:T(8,128)(2,1)} %get-tuple-element.160), channel_id=1, source_target_pairs={{0,2},{1,3},{2,0},{3,1},{4,6},{5,7},{6,4},{7,5},{8,10},{9,11},{10,... | collective-permute-start | bytes 393224 | tf_op jit(solution)/shard_map/ppermute | solution.py:389
  219.3 2.7 collective-permute-start.50
  222.1 14.8 %shrink.7 = (bf16[32,32,128]{2,1,0:T(8,128)(2,1)}, bf16[32,32,128]{2,1,0:T(8,128)(2,1)}, bf16[32,32,128]{2,1,0:T(8,128)(2,1)}, bf16[32,32,128]{2,1,0:T(8,128)(2,...) custom-call(s32[9]{0:T(128)} %pad_add_fusion.meta_ref, ...), custom_call_target="tpu_custom_call" | custom-call | flops 2147483648 | bytes 4456448 | tf_op jit(solution)/shard_map/shrink/pallas_call | solution.py:320
  236.9 2.0 collective-permute-start.33
  238.9 1.6 collective-permute-start.34
  240.6 1.8 collective-permute-start.36
  242.7 5.4 %collective-permute-done.33.refs_4_ = bf16[32,32,128]{2,1,0:T(8,128)(2,1)S(1)} collective-permute-done((bf16[32,32,128]{2,1,0:T(8,128)(2,1)S(1)}, bf16[32,32,128]{2,1,0:T(8,128)(2,1)S(1)}, u32[]{:S(2)}, u32[]{:S(2)}) %collective-permute-start.33) | collective-permute-done | bytes 262176 | tf_op jit(solution)/shard_map/ppermute | solution.py:389
  248.1 10.6 %collective-permute-start.52 = (bf16[32,32,128]{2,1,0:T(8,128)(2,1)}, bf16[32,32,128]{2,1,0:T(8,128)(2,1)S(1)}, u32[]{:S(2)}, u32[]{:S(2)}) collective-permute-start(bf16[32,32,128]{2,1,0:T(8,128)(2,1)} %get-tuple-element.164), channel_id=1, source_target_pairs={{0,4},{1,5},{2,6},{3,7},{4,0},{5,1},{6,2},{7,3},{8,12},{9,13},{10,... | collective-permute-start | bytes 786440 | tf_op jit(solution)/shard_map/ppermute | solution.py:389
  258.7 5.3 %collective-permute-start.53 = (bf16[32,32,128]{2,1,0:T(8,128)(2,1)}, bf16[32,32,128]{2,1,0:T(8,128)(2,1)S(1)}, u32[]{:S(2)}, u32[]{:S(2)}) collective-permute-start(bf16[32,32,128]{2,1,0:T(8,128)(2,1)} %get-tuple-element.165), channel_id=1, source_target_pairs={{0,5},{1,4},{2,7},{3,6},{4,1},{5,0},{6,3},{7,2},{8,13},{9,12},{10,... | collective-permute-start | bytes 786440 | tf_op jit(solution)/shard_map/ppermute | solution.py:389
  264.0 1.9 collective-permute-start.54
  266.4 24.9 %collective-permute-done.52.refs_2_ = bf16[32,32,128]{2,1,0:T(8,128)(2,1)S(1)} collective-permute-done((bf16[32,32,128]{2,1,0:T(8,128)(2,1)}, bf16[32,32,128]{2,1,0:T(8,128)(2,1)S(1)}, u32[]{:S(2)}, u32[]{:S(2)}) %collective-permute-start.52) | collective-permute-done | bytes 262176 | tf_op jit(solution)/shard_map/ppermute | solution.py:389
  291.4 9.6 %collective-permute-done.53.refs_3_ = bf16[32,32,128]{2,1,0:T(8,128)(2,1)S(1)} collective-permute-done((bf16[32,32,128]{2,1,0:T(8,128)(2,1)}, bf16[32,32,128]{2,1,0:T(8,128)(2,1)S(1)}, u32[]{:S(2)}, u32[]{:S(2)}) %collective-permute-start.53) | collective-permute-done | bytes 262176 | tf_op jit(solution)/shard_map/ppermute | solution.py:389
  301.0 1.9 collective-permute-start.40
  302.9 2.7 collective-permute-start.41
  305.6 14.5 %collective-permute-start.42 = (bf16[32,32,128]{2,1,0:T(8,128)(2,1)}, bf16[32,32,128]{2,1,0:T(8,128)(2,1)}, u32[]{:S(2)}, u32[]{:S(2)}) collective-permute-start(bf16[32,32,128]{2,1,0:T(8,128)(2,1)} %get-tuple-element.150), channel_id=1, source_target_pairs={{0,2},{1,3},{2,0},{3,1},{4,6},{5,7},{6,4},{7,5},{8,10},{9,11},{10,... | collective-permute-start | bytes 786440 | tf_op jit(solution)/shard_map/ppermute | solution.py:389
  320.1 5.1 %collective-permute-done.38.refs_2_ = bf16[32,32,128]{2,1,0:T(8,128)(2,1)S(1)} collective-permute-done((bf16[32,32,128]{2,1,0:T(8,128)(2,1)}, bf16[32,32,128]{2,1,0:T(8,128)(2,1)S(1)}, u32[]{:S(2)}, u32[]{:S(2)}) %collective-permute-start.38) | collective-permute-done | bytes 262176 | tf_op jit(solution)/shard_map/ppermute | solution.py:389
  333.2 3.2 update.5
  337.1 14.6 %shrink.8 = (bf16[32,32,128]{2,1,0:T(8,128)(2,1)}, bf16[32,32,128]{2,1,0:T(8,128)(2,1)}, bf16[32,32,128]{2,1,0:T(8,128)(2,1)}, bf16[32,32,128]{2,1,0:T(8,128)(2,...) custom-call(s32[9]{0:T(128)} %pad_add_fusion.meta_ref, ...), custom_call_target="tpu_custom_call" | custom-call | flops 2147483648 | bytes 4456448 | tf_op jit(solution)/shard_map/shrink/pallas_call | solution.py:320
  352.6 2.0 collective-permute-start.56
  355.2 1.9 collective-permute-start.59
  360.1 6.5 %update.6 = (f32[32,128,1024]{2,1,0:T(8,128)}, f32[8,128]{1,0:T(8,128)S(1)}) custom-call(s32[9]{0:T(128)S(1)} %copy-done.13, bf16[1024,1024]{1,0:T(8,128)(2,1)S(1)} %copy-done, bf16[32,32,128]{2,1,0:T(8,128)(2,1)S(1)} %copy-done.2, bf16[32,32,128]{2,1,0:T(8,128)(2,1)S(1)} %copy-done.1, ...), custom_call_target="tpu_custom_call", output_to_operand_aliasing={{0}: (11, {})} | custom-call | flops 2147483648 | bytes 8388608 | tf_op jit(solution)/shard_map/update/pallas_call | solution.py:351
  367.1 7.3 %shrink.9 = (bf16[32,16,128]{2,1,0:T(8,128)(2,1)}, bf16[32,16,128]{2,1,0:T(8,128)(2,1)}, bf16[32,16,128]{2,1,0:T(8,128)(2,1)}, bf16[32,16,128]{2,1,0:T(8,128)(2,...) custom-call(s32[9]{0:T(128)} %pad_add_fusion.meta_ref, ...), custom_call_target="tpu_custom_call" | custom-call | flops 1073741824 | bytes 2359296 | tf_op jit(solution)/shard_map/shrink/pallas_call | solution.py:320
  375.8 9.9 %psum.7 = f32[32]{0:T(128)S(1)} all-reduce(f32[32]{0:T(128)S(1)} %add_reduce_fusion), channel_id=1, replica_groups=mesh['patch'=4,'shot'=8] {'patch'}, use_global_device_ids=true, to_apply=%region_1.0 | all-reduce | flops 32 | bytes 256 | tf_op jit(solution)/shard_map/psum | solution.py:514
  385.8 2.0 collective-permute-start.61
  387.8 3.1 collective-permute-start.62
  392.6 6.2 %update.7 = (f32[32,128,1024]{2,1,0:T(8,128)}, f32[8,128]{1,0:T(8,128)S(1)}) custom-call(s32[9]{0:T(128)S(1)} %copy-done.14, bf16[1024,1024]{1,0:T(8,128)(2,1)S(1)} %copy-done, bf16[32,16,128]{2,1,0:T(8,128)(2,1)S(1)} %copy-done.4, bf16[32,32,128]{2,1,0:T(8,128)(2,1)S(1)} %copy-done.6, ...), custom_call_target="tpu_custom_call", output_to_operand_aliasing={{0}: (11, {})} | custom-call | flops 2147483648 | bytes 8388608 | tf_op jit(solution)/shard_map/update/pallas_call | solution.py:351
  398.8 13.2 %collective-permute-done.60.refs_3_ = bf16[32,32,128]{2,1,0:T(8,128)(2,1)S(1)} collective-permute-done((bf16[32,32,128]{2,1,0:T(8,128)(2,1)}, bf16[32,32,128]{2,1,0:T(8,128)(2,1)S(1)}, u32[]{:S(2)}, u32[]{:S(2)}) %collective-permute-start.60) | collective-permute-done | bytes 262176 | tf_op jit(solution)/shard_map/ppermute | solution.py:389
  412.1 2.0 collective-permute-start.68
  415.0 1.6 collective-permute-done.63.refs_6_
  416.6 16.0 %collective-permute-start.70 = (bf16[32,16,128]{2,1,0:T(8,128)(2,1)S(1)}, bf16[32,16,128]{2,1,0:T(8,128)(2,1)S(1)}, u32[]{:S(2)}, u32[]{:S(2)}) collective-permute-start(bf16[32,16,128]{2,1,0:T(8,128)(2,1)S(1)} %copy-done.63), channel_id=1, source_target_pairs={{0,2},{1,3},{2,0},{3,1},{4,6},{5,7},{6,4},{7,5},{8,10},{9,11},{10,... | collective-permute-start | bytes 393224 | tf_op jit(solution)/shard_map/ppermute | solution.py:389
  433.1 6.1 %update.8 = (f32[32,128,1024]{2,1,0:T(8,128)}, f32[8,128]{1,0:T(8,128)S(1)}) custom-call(s32[9]{0:T(128)S(1)} %copy-done.14, bf16[1024,1024]{1,0:T(8,128)(2,1)S(1)} %copy-done, f32[8,128]{1,0:T(8,128)S(1)} %get-tuple-element.171._, bf16[32,32,128]{2,1,0:T(8,128)(2,1)S(1)} %copy-done.3, ...), custom_call_target="tpu_custom_call", output_to_operand_aliasing={{0}: (11, {})} | custom-call | flops 2147483648 | bytes 8388608 | tf_op jit(solution)/shard_map/update/pallas_call | solution.py:351
  439.9 4.1 update.9
  (261 shorter events, 35.4 us)
Async XLA Ops:
  23.8 29.2 %collective-permute-start.2 = (bf16[32,16,128]{2,1,0:T(8,128)(2,1)}, bf16[32,16,128]{2,1,0:T(8,128)(2,1)S(1)}, u32[]{:S(2)}, u32[]{:S(2)}) collective-permute-start(bf16[32,16,128]{2,1,0:T(8,128)(2,1)} %get-tuple-element.100), channel_id=1, source_target_pairs={{0,1},{1,0},{2,3},{3,2},{4,5},{5,4},{6,7},{7,6},{8,9},{9,8},{10,11... | collective-permute-start | bytes 393224 | tf_op jit(solution)/shard_map/ppermute | solution.py:389
  33.4 20.7 %collective-permute-start.3 = (bf16[32,16,128]{2,1,0:T(8,128)(2,1)}, bf16[32,16,128]{2,1,0:T(8,128)(2,1)S(1)}, u32[]{:S(2)}, u32[]{:S(2)}) collective-permute-start(bf16[32,16,128]{2,1,0:T(8,128)(2,1)} %get-tuple-element.101), channel_id=1, source_target_pairs={{0,4},{1,5},{2,6},{3,7},{4,0},{5,1},{6,2},{7,3},{8,12},{9,13},{10,... | collective-permute-start | bytes 393224 | tf_op jit(solution)/shard_map/ppermute | solution.py:389
  36.0 20.1 %collective-permute-start.4 = (bf16[32,16,128]{2,1,0:T(8,128)(2,1)}, bf16[32,16,128]{2,1,0:T(8,128)(2,1)S(1)}, u32[]{:S(2)}, u32[]{:S(2)}) collective-permute-start(bf16[32,16,128]{2,1,0:T(8,128)(2,1)} %get-tuple-element.102), channel_id=1, source_target_pairs={{0,5},{1,4},{2,7},{3,6},{4,1},{5,0},{6,3},{7,2},{8,13},{9,12},{10,... | collective-permute-start | bytes 393224 | tf_op jit(solution)/shard_map/ppermute | solution.py:389
  36.0 20.4 %collective-permute-start.5 = (bf16[32,16,128]{2,1,0:T(8,128)(2,1)}, bf16[32,16,128]{2,1,0:T(8,128)(2,1)S(1)}, u32[]{:S(2)}, u32[]{:S(2)}) collective-permute-start(bf16[32,16,128]{2,1,0:T(8,128)(2,1)} %get-tuple-element.103), channel_id=1, source_target_pairs={{0,6},{1,7},{2,4},{3,5},{4,2},{5,3},{6,0},{7,1},{8,14},{9,15},{10,... | collective-permute-start | bytes 393224 | tf_op jit(solution)/shard_map/ppermute | solution.py:389
  52.9 25.1 %collective-permute-start.9 = (bf16[32,32,128]{2,1,0:T(8,128)(2,1)}, bf16[32,32,128]{2,1,0:T(8,128)(2,1)S(1)}, u32[]{:S(2)}, u32[]{:S(2)}) collective-permute-start(bf16[32,32,128]{2,1,0:T(8,128)(2,1)} %get-tuple-element.110), channel_id=1, source_target_pairs={{0,1},{1,0},{2,3},{3,2},{4,5},{5,4},{6,7},{7,6},{8,9},{9,8},{10,11... | collective-permute-start | bytes 786440 | tf_op jit(solution)/shard_map/ppermute | solution.py:389
  53.0 25.1 %collective-permute-start.10 = (bf16[32,32,128]{2,1,0:T(8,128)(2,1)}, bf16[32,32,128]{2,1,0:T(8,128)(2,1)S(1)}, u32[]{:S(2)}, u32[]{:S(2)}) collective-permute-start(bf16[32,32,128]{2,1,0:T(8,128)(2,1)} %get-tuple-element.111), channel_id=1, source_target_pairs={{0,4},{1,5},{2,6},{3,7},{4,0},{5,1},{6,2},{7,3},{8,12},{9,13},{10,... | collective-permute-start | bytes 786440 | tf_op jit(solution)/shard_map/ppermute | solution.py:389
  56.0 18.4 %collective-permute-start.7 = (bf16[32,16,128]{2,1,0:T(8,128)(2,1)S(1)}, bf16[32,16,128]{2,1,0:T(8,128)(2,1)S(1)}, u32[]{:S(2)}, u32[]{:S(2)}) collective-permute-start(bf16[32,16,128]{2,1,0:T(8,128)(2,1)S(1)} %copy-done.73), channel_id=1, source_target_pairs={{0,2},{1,3},{2,0},{3,1},{4,6},{5,7},{6,4},{7,5},{8,10},{9,11},{10,... | collective-permute-start | bytes 393224 | tf_op jit(solution)/shard_map/ppermute | solution.py:389
  56.4 20.0 %collective-permute-start.8 = (bf16[32,16,128]{2,1,0:T(8,128)(2,1)S(1)}, bf16[32,16,128]{2,1,0:T(8,128)(2,1)S(1)}, u32[]{:S(2)}, u32[]{:S(2)}) collective-permute-start(bf16[32,16,128]{2,1,0:T(8,128)(2,1)S(1)} %copy-done.71), channel_id=1, source_target_pairs={{0,3},{1,2},{2,1},{3,0},{4,7},{5,6},{6,5},{7,4},{8,11},{9,10},{10,... | collective-permute-start | bytes 393224 | tf_op jit(solution)/shard_map/ppermute | solution.py:389
  65.2 36.6 %collective-permute-start.11 = (bf16[32,32,128]{2,1,0:T(8,128)(2,1)}, bf16[32,32,128]{2,1,0:T(8,128)(2,1)S(1)}, u32[]{:S(2)}, u32[]{:S(2)}) collective-permute-start(bf16[32,32,128]{2,1,0:T(8,128)(2,1)} %get-tuple-element.112), channel_id=1, source_target_pairs={{0,5},{1,4},{2,7},{3,6},{4,1},{5,0},{6,3},{7,2},{8,13},{9,12},{10,... | collective-permute-start | bytes 786440 | tf_op jit(solution)/shard_map/ppermute | solution.py:389
  74.4 27.9 %collective-permute-start.12 = (bf16[32,32,128]{2,1,0:T(8,128)(2,1)}, bf16[32,32,128]{2,1,0:T(8,128)(2,1)S(1)}, u32[]{:S(2)}, u32[]{:S(2)}) collective-permute-start(bf16[32,32,128]{2,1,0:T(8,128)(2,1)} %get-tuple-element.113), channel_id=1, source_target_pairs={{0,6},{1,7},{2,4},{3,5},{4,2},{5,3},{6,0},{7,1},{8,14},{9,15},{10,... | collective-permute-start | bytes 786440 | tf_op jit(solution)/shard_map/ppermute | solution.py:389
  76.4 29.1 %collective-permute-start.13 = (bf16[32,32,128]{2,1,0:T(8,128)(2,1)}, bf16[32,32,128]{2,1,0:T(8,128)(2,1)S(1)}, u32[]{:S(2)}, u32[]{:S(2)}) collective-permute-start(bf16[32,32,128]{2,1,0:T(8,128)(2,1)} %get-tuple-element.114), channel_id=1, source_target_pairs={{0,7},{1,6},{2,5},{3,4},{4,3},{5,2},{6,1},{7,0},{8,15},{9,14},{10,... | collective-permute-start | bytes 786440 | tf_op jit(solution)/shard_map/ppermute | solution.py:389
  78.0 35.4 %collective-permute-start.14 = (bf16[32,32,128]{2,1,0:T(8,128)(2,1)}, bf16[32,32,128]{2,1,0:T(8,128)(2,1)S(1)}, u32[]{:S(2)}, u32[]{:S(2)}) collective-permute-start(bf16[32,32,128]{2,1,0:T(8,128)(2,1)} %get-tuple-element.115), channel_id=1, source_target_pairs={{0,2},{1,3},{2,0},{3,1},{4,6},{5,7},{6,4},{7,5},{8,10},{9,11},{10,... | collective-permute-start | bytes 786440 | tf_op jit(solution)/shard_map/ppermute | solution.py:389
  78.1 37.3 %collective-permute-start.15 = (bf16[32,32,128]{2,1,0:T(8,128)(2,1)}, bf16[32,32,128]{2,1,0:T(8,128)(2,1)S(1)}, u32[]{:S(2)}, u32[]{:S(2)}) collective-permute-start(bf16[32,32,128]{2,1,0:T(8,128)(2,1)} %get-tuple-element.116), channel_id=1, source_target_pairs={{0,3},{1,2},{2,1},{3,0},{4,7},{5,6},{6,5},{7,4},{8,11},{9,10},{10,... | collective-permute-start | bytes 786440 | tf_op jit(solution)/shard_map/ppermute | solution.py:389
  101.8 13.5 %collective-permute-start.23 = (bf16[32,16,128]{2,1,0:T(8,128)(2,1)}, bf16[32,16,128]{2,1,0:T(8,128)(2,1)S(1)}, u32[]{:S(2)}, u32[]{:S(2)}) collective-permute-start(bf16[32,16,128]{2,1,0:T(8,128)(2,1)} %get-tuple-element.128), channel_id=1, source_target_pairs={{0,1},{1,0},{2,3},{3,2},{4,5},{5,4},{6,7},{7,6},{8,9},{9,8},{10,11... | collective-permute-start | bytes 393224 | tf_op jit(solution)/shard_map/ppermute | solution.py:389
  102.3 13.7 %collective-permute-start.24 = (bf16[32,16,128]{2,1,0:T(8,128)(2,1)}, bf16[32,16,128]{2,1,0:T(8,128)(2,1)S(1)}, u32[]{:S(2)}, u32[]{:S(2)}) collective-permute-start(bf16[32,16,128]{2,1,0:T(8,128)(2,1)} %get-tuple-element.129), channel_id=1, source_target_pairs={{0,4},{1,5},{2,6},{3,7},{4,0},{5,1},{6,2},{7,3},{8,12},{9,13},{10,... | collective-permute-start | bytes 393224 | tf_op jit(solution)/shard_map/ppermute | solution.py:389
  105.5 26.2 %collective-permute-start.25 = (bf16[32,16,128]{2,1,0:T(8,128)(2,1)}, bf16[32,16,128]{2,1,0:T(8,128)(2,1)S(1)}, u32[]{:S(2)}, u32[]{:S(2)}) collective-permute-start(bf16[32,16,128]{2,1,0:T(8,128)(2,1)} %get-tuple-element.130), channel_id=1, source_target_pairs={{0,5},{1,4},{2,7},{3,6},{4,1},{5,0},{6,3},{7,2},{8,13},{9,12},{10,... | collective-permute-start | bytes 393224 | tf_op jit(solution)/shard_map/ppermute | solution.py:389
  113.4 19.0 %collective-permute-start.26 = (bf16[32,16,128]{2,1,0:T(8,128)(2,1)}, bf16[32,16,128]{2,1,0:T(8,128)(2,1)S(1)}, u32[]{:S(2)}, u32[]{:S(2)}) collective-permute-start(bf16[32,16,128]{2,1,0:T(8,128)(2,1)} %get-tuple-element.131), channel_id=1, source_target_pairs={{0,6},{1,7},{2,4},{3,5},{4,2},{5,3},{6,0},{7,1},{8,14},{9,15},{10,... | collective-permute-start | bytes 393224 | tf_op jit(solution)/shard_map/ppermute | solution.py:389
  115.3 39.8 %collective-permute-start.16 = (bf16[32,32,128]{2,1,0:T(8,128)(2,1)}, bf16[32,32,128]{2,1,0:T(8,128)(2,1)S(1)}, u32[]{:S(2)}, u32[]{:S(2)}) collective-permute-start(bf16[32,32,128]{2,1,0:T(8,128)(2,1)} %get-tuple-element.120), channel_id=1, source_target_pairs={{0,1},{1,0},{2,3},{3,2},{4,5},{5,4},{6,7},{7,6},{8,9},{9,8},{10,11... | collective-permute-start | bytes 786440 | tf_op jit(solution)/shard_map/ppermute | solution.py:389
  116.0 39.0 %collective-permute-start.17 = (bf16[32,32,128]{2,1,0:T(8,128)(2,1)}, bf16[32,32,128]{2,1,0:T(8,128)(2,1)S(1)}, u32[]{:S(2)}, u32[]{:S(2)}) collective-permute-start(bf16[32,32,128]{2,1,0:T(8,128)(2,1)} %get-tuple-element.121), channel_id=1, source_target_pairs={{0,4},{1,5},{2,6},{3,7},{4,0},{5,1},{6,2},{7,3},{8,12},{9,13},{10,... | collective-permute-start | bytes 786440 | tf_op jit(solution)/shard_map/ppermute | solution.py:389
  116.7 33.5 %collective-permute-start.27 = (bf16[32,16,128]{2,1,0:T(8,128)(2,1)}, bf16[32,16,128]{2,1,0:T(8,128)(2,1)S(1)}, u32[]{:S(2)}, u32[]{:S(2)}) collective-permute-start(bf16[32,16,128]{2,1,0:T(8,128)(2,1)} %get-tuple-element.132), channel_id=1, source_target_pairs={{0,7},{1,6},{2,5},{3,4},{4,3},{5,2},{6,1},{7,0},{8,15},{9,14},{10,... | collective-permute-start | bytes 393224 | tf_op jit(solution)/shard_map/ppermute | solution.py:389
  132.4 18.4 %collective-permute-start.28 = (bf16[32,16,128]{2,1,0:T(8,128)(2,1)}, bf16[32,16,128]{2,1,0:T(8,128)(2,1)S(1)}, u32[]{:S(2)}, u32[]{:S(2)}) collective-permute-start(bf16[32,16,128]{2,1,0:T(8,128)(2,1)} %get-tuple-element.133), channel_id=1, source_target_pairs={{0,2},{1,3},{2,0},{3,1},{4,6},{5,7},{6,4},{7,5},{8,10},{9,11},{10,... | collective-permute-start | bytes 393224 | tf_op jit(solution)/shard_map/ppermute | solution.py:389
  133.1 19.6 %collective-permute-start.29 = (bf16[32,16,128]{2,1,0:T(8,128)(2,1)}, bf16[32,16,128]{2,1,0:T(8,128)(2,1)S(1)}, u32[]{:S(2)}, u32[]{:S(2)}) collective-permute-start(bf16[32,16,128]{2,1,0:T(8,128)(2,1)} %get-tuple-element.134), channel_id=1, source_target_pairs={{0,3},{1,2},{2,1},{3,0},{4,7},{5,6},{6,5},{7,4},{8,11},{9,10},{10,... | collective-permute-start | bytes 393224 | tf_op jit(solution)/shard_map/ppermute | solution.py:389
  150.3 31.1 %collective-permute-start.18 = (bf16[32,32,128]{2,1,0:T(8,128)(2,1)}, bf16[32,32,128]{2,1,0:T(8,128)(2,1)}, u32[]{:S(2)}, u32[]{:S(2)}) collective-permute-start(bf16[32,32,128]{2,1,0:T(8,128)(2,1)} %get-tuple-element.122), channel_id=1, source_target_pairs={{0,5},{1,4},{2,7},{3,6},{4,1},{5,0},{6,3},{7,2},{8,13},{9,12},{10,... | collective-permute-start | bytes 786440 | tf_op jit(solution)/shard_map/ppermute | solution.py:389
  150.8 31.7 %collective-permute-start.19 = (bf16[32,32,128]{2,1,0:T(8,128)(2,1)}, bf16[32,32,128]{2,1,0:T(8,128)(2,1)}, u32[]{:S(2)}, u32[]{:S(2)}) collective-permute-start(bf16[32,32,128]{2,1,0:T(8,128)(2,1)} %get-tuple-element.123), channel_id=1, source_target_pairs={{0,6},{1,7},{2,4},{3,5},{4,2},{5,3},{6,0},{7,1},{8,14},{9,15},{10,... | collective-permute-start | bytes 786440 | tf_op jit(solution)/shard_map/ppermute | solution.py:389
  152.7 31.1 %collective-permute-start.20 = (bf16[32,32,128]{2,1,0:T(8,128)(2,1)}, bf16[32,32,128]{2,1,0:T(8,128)(2,1)}, u32[]{:S(2)}, u32[]{:S(2)}) collective-permute-start(bf16[32,32,128]{2,1,0:T(8,128)(2,1)} %get-tuple-element.124), channel_id=1, source_target_pairs={{0,7},{1,6},{2,5},{3,4},{4,3},{5,2},{6,1},{7,0},{8,15},{9,14},{10,... | collective-permute-start | bytes 786440 | tf_op jit(solution)/shard_map/ppermute | solution.py:389
  155.1 36.6 %collective-permute-start.21 = (bf16[32,32,128]{2,1,0:T(8,128)(2,1)}, bf16[32,32,128]{2,1,0:T(8,128)(2,1)}, u32[]{:S(2)}, u32[]{:S(2)}) collective-permute-start(bf16[32,32,128]{2,1,0:T(8,128)(2,1)} %get-tuple-element.125), channel_id=1, source_target_pairs={{0,2},{1,3},{2,0},{3,1},{4,6},{5,7},{6,4},{7,5},{8,10},{9,11},{10,... | collective-permute-start | bytes 786440 | tf_op jit(solution)/shard_map/ppermute | solution.py:389
  155.1 38.5 %collective-permute-start.22 = (bf16[32,32,128]{2,1,0:T(8,128)(2,1)}, bf16[32,32,128]{2,1,0:T(8,128)(2,1)}, u32[]{:S(2)}, u32[]{:S(2)}) collective-permute-start(bf16[32,32,128]{2,1,0:T(8,128)(2,1)} %get-tuple-element.126), channel_id=1, source_target_pairs={{0,3},{1,2},{2,1},{3,0},{4,7},{5,6},{6,5},{7,4},{8,11},{9,10},{10,... | collective-permute-start | bytes 786440 | tf_op jit(solution)/shard_map/ppermute | solution.py:389
  181.3 14.0 %collective-permute-start.44 = (bf16[32,16,128]{2,1,0:T(8,128)(2,1)}, bf16[32,16,128]{2,1,0:T(8,128)(2,1)S(1)}, u32[]{:S(2)}, u32[]{:S(2)}) collective-permute-start(bf16[32,16,128]{2,1,0:T(8,128)(2,1)} %get-tuple-element.155), channel_id=1, source_target_pairs={{0,1},{1,0},{2,3},{3,2},{4,5},{5,4},{6,7},{7,6},{8,9},{9,8},{10,11... | collective-permute-start | bytes 393224 | tf_op jit(solution)/shard_map/ppermute | solution.py:389
  183.8 26.7 %collective-permute-start.46 = (bf16[32,16,128]{2,1,0:T(8,128)(2,1)}, bf16[32,16,128]{2,1,0:T(8,128)(2,1)S(1)}, u32[]{:S(2)}, u32[]{:S(2)}) collective-permute-start(bf16[32,16,128]{2,1,0:T(8,128)(2,1)} %get-tuple-element.157), channel_id=1, source_target_pairs={{0,5},{1,4},{2,7},{3,6},{4,1},{5,0},{6,3},{7,2},{8,13},{9,12},{10,... | collective-permute-start | bytes 393224 | tf_op jit(solution)/shard_map/ppermute | solution.py:389
  191.7 18.8 %collective-permute-start.47 = (bf16[32,16,128]{2,1,0:T(8,128)(2,1)}, bf16[32,16,128]{2,1,0:T(8,128)(2,1)S(1)}, u32[]{:S(2)}, u32[]{:S(2)}) collective-permute-start(bf16[32,16,128]{2,1,0:T(8,128)(2,1)} %get-tuple-element.158), channel_id=1, source_target_pairs={{0,6},{1,7},{2,4},{3,5},{4,2},{5,3},{6,0},{7,1},{8,14},{9,15},{10,... | collective-permute-start | bytes 393224 | tf_op jit(solution)/shard_map/ppermute | solution.py:389
  193.6 25.7 %collective-permute-start.48 = (bf16[32,16,128]{2,1,0:T(8,128)(2,1)}, bf16[32,16,128]{2,1,0:T(8,128)(2,1)S(1)}, u32[]{:S(2)}, u32[]{:S(2)}) collective-permute-start(bf16[32,16,128]{2,1,0:T(8,128)(2,1)} %get-tuple-element.159), channel_id=1, source_target_pairs={{0,7},{1,6},{2,5},{3,4},{4,3},{5,2},{6,1},{7,0},{8,15},{9,14},{10,... | collective-permute-start | bytes 393224 | tf_op jit(solution)/shard_map/ppermute | solution.py:389
  195.3 45.2 %collective-permute-start.30 = (bf16[32,32,128]{2,1,0:T(8,128)(2,1)}, bf16[32,32,128]{2,1,0:T(8,128)(2,1)}, u32[]{:S(2)}, u32[]{:S(2)}) collective-permute-start(bf16[32,32,128]{2,1,0:T(8,128)(2,1)} %get-tuple-element.137), channel_id=1, source_target_pairs={{0,1},{1,0},{2,3},{3,2},{4,5},{5,4},{6,7},{7,6},{8,9},{9,8},{10,11... | collective-permute-start | bytes 786440 | tf_op jit(solution)/shard_map/ppermute | solution.py:389
  195.7 44.9 %collective-permute-start.31 = (bf16[32,32,128]{2,1,0:T(8,128)(2,1)}, bf16[32,32,128]{2,1,0:T(8,128)(2,1)}, u32[]{:S(2)}, u32[]{:S(2)}) collective-permute-start(bf16[32,32,128]{2,1,0:T(8,128)(2,1)} %get-tuple-element.138), channel_id=1, source_target_pairs={{0,4},{1,5},{2,6},{3,7},{4,0},{5,1},{6,2},{7,3},{8,12},{9,13},{10,... | collective-permute-start | bytes 786440 | tf_op jit(solution)/shard_map/ppermute | solution.py:389
  210.5 31.8 %collective-permute-start.32 = (bf16[32,32,128]{2,1,0:T(8,128)(2,1)S(1)}, bf16[32,32,128]{2,1,0:T(8,128)(2,1)}, u32[]{:S(2)}, u32[]{:S(2)}) collective-permute-start(bf16[32,32,128]{2,1,0:T(8,128)(2,1)S(1)} %copy-done.44), channel_id=1, source_target_pairs={{0,5},{1,4},{2,7},{3,6},{4,1},{5,0},{6,3},{7,2},{8,13},{9,12},{10,... | collective-permute-start | bytes 786440 | tf_op jit(solution)/shard_map/ppermute | solution.py:389
  210.6 26.3 %collective-permute-start.49 = (bf16[32,16,128]{2,1,0:T(8,128)(2,1)}, bf16[32,16,128]{2,1,0:T(8,128)(2,1)S(1)}, u32[]{:S(2)}, u32[]{:S(2)}) collective-permute-start(bf16[32,16,128]{2,1,0:T(8,128)(2,1)} %get-tuple-element.160), channel_id=1, source_target_pairs={{0,2},{1,3},{2,0},{3,1},{4,6},{5,7},{6,4},{7,5},{8,10},{9,11},{10,... | collective-permute-start | bytes 393224 | tf_op jit(solution)/shard_map/ppermute | solution.py:389
  219.3 19.6 %collective-permute-start.50 = (bf16[32,16,128]{2,1,0:T(8,128)(2,1)}, bf16[32,16,128]{2,1,0:T(8,128)(2,1)}, u32[]{:S(2)}, u32[]{:S(2)}) collective-permute-start(bf16[32,16,128]{2,1,0:T(8,128)(2,1)} %get-tuple-element.161), channel_id=1, source_target_pairs={{0,3},{1,2},{2,1},{3,0},{4,7},{5,6},{6,5},{7,4},{8,11},{9,10},{10,... | collective-permute-start | bytes 393224 | tf_op jit(solution)/shard_map/ppermute | solution.py:389
  238.9 19.8 %collective-permute-start.34 = (bf16[32,32,128]{2,1,0:T(8,128)(2,1)S(1)}, bf16[32,32,128]{2,1,0:T(8,128)(2,1)S(1)}, u32[]{:S(2)}, u32[]{:S(2)}) collective-permute-start(bf16[32,32,128]{2,1,0:T(8,128)(2,1)S(1)} %copy-done.42), channel_id=1, source_target_pairs={{0,7},{1,6},{2,5},{3,4},{4,3},{5,2},{6,1},{7,0},{8,15},{9,14},{10,... | collective-permute-start | bytes 786440 | tf_op jit(solution)/shard_map/ppermute | solution.py:389
  240.5 23.5 %collective-permute-start.35 = (bf16[32,32,128]{2,1,0:T(8,128)(2,1)S(1)}, bf16[32,32,128]{2,1,0:T(8,128)(2,1)S(1)}, u32[]{:S(2)}, u32[]{:S(2)}) collective-permute-start(bf16[32,32,128]{2,1,0:T(8,128)(2,1)S(1)} %copy-done.40), channel_id=1, source_target_pairs={{0,2},{1,3},{2,0},{3,1},{4,6},{5,7},{6,4},{7,5},{8,10},{9,11},{10,... | collective-permute-start | bytes 786440 | tf_op jit(solution)/shard_map/ppermute | solution.py:389
  240.6 25.7 %collective-permute-start.36 = (bf16[32,32,128]{2,1,0:T(8,128)(2,1)S(1)}, bf16[32,32,128]{2,1,0:T(8,128)(2,1)S(1)}, u32[]{:S(2)}, u32[]{:S(2)}) collective-permute-start(bf16[32,32,128]{2,1,0:T(8,128)(2,1)S(1)} %copy-done.38), channel_id=1, source_target_pairs={{0,3},{1,2},{2,1},{3,0},{4,7},{5,6},{6,5},{7,4},{8,11},{9,10},{10,... | collective-permute-start | bytes 786440 | tf_op jit(solution)/shard_map/ppermute | solution.py:389
  242.3 24.1 %collective-permute-start.51 = (bf16[32,32,128]{2,1,0:T(8,128)(2,1)}, bf16[32,32,128]{2,1,0:T(8,128)(2,1)S(1)}, u32[]{:S(2)}, u32[]{:S(2)}) collective-permute-start(bf16[32,32,128]{2,1,0:T(8,128)(2,1)} %get-tuple-element.163), channel_id=1, source_target_pairs={{0,1},{1,0},{2,3},{3,2},{4,5},{5,4},{6,7},{7,6},{8,9},{9,8},{10,11... | collective-permute-start | bytes 786440 | tf_op jit(solution)/shard_map/ppermute | solution.py:389
  248.1 43.3 %collective-permute-start.52 = (bf16[32,32,128]{2,1,0:T(8,128)(2,1)}, bf16[32,32,128]{2,1,0:T(8,128)(2,1)S(1)}, u32[]{:S(2)}, u32[]{:S(2)}) collective-permute-start(bf16[32,32,128]{2,1,0:T(8,128)(2,1)} %get-tuple-element.164), channel_id=1, source_target_pairs={{0,4},{1,5},{2,6},{3,7},{4,0},{5,1},{6,2},{7,3},{8,12},{9,13},{10,... | collective-permute-start | bytes 786440 | tf_op jit(solution)/shard_map/ppermute | solution.py:389
  258.7 42.2 %collective-permute-start.53 = (bf16[32,32,128]{2,1,0:T(8,128)(2,1)}, bf16[32,32,128]{2,1,0:T(8,128)(2,1)S(1)}, u32[]{:S(2)}, u32[]{:S(2)}) collective-permute-start(bf16[32,32,128]{2,1,0:T(8,128)(2,1)} %get-tuple-element.165), channel_id=1, source_target_pairs={{0,5},{1,4},{2,7},{3,6},{4,1},{5,0},{6,3},{7,2},{8,13},{9,12},{10,... | collective-permute-start | bytes 786440 | tf_op jit(solution)/shard_map/ppermute | solution.py:389
  264.0 38.8 %collective-permute-start.54 = (bf16[32,32,128]{2,1,0:T(8,128)(2,1)}, bf16[32,32,128]{2,1,0:T(8,128)(2,1)S(1)}, u32[]{:S(2)}, u32[]{:S(2)}) collective-permute-start(bf16[32,32,128]{2,1,0:T(8,128)(2,1)} %get-tuple-element.166), channel_id=1, source_target_pairs={{0,6},{1,7},{2,4},{3,5},{4,2},{5,3},{6,0},{7,1},{8,14},{9,15},{10,... | collective-permute-start | bytes 786440 | tf_op jit(solution)/shard_map/ppermute | solution.py:389
  266.2 39.4 %collective-permute-start.37 = (bf16[32,32,128]{2,1,0:T(8,128)(2,1)}, bf16[32,32,128]{2,1,0:T(8,128)(2,1)S(1)}, u32[]{:S(2)}, u32[]{:S(2)}) collective-permute-start(bf16[32,32,128]{2,1,0:T(8,128)(2,1)} %get-tuple-element.145), channel_id=1, source_target_pairs={{0,1},{1,0},{2,3},{3,2},{4,5},{5,4},{6,7},{7,6},{8,9},{9,8},{10,11... | collective-permute-start | bytes 786440 | tf_op jit(solution)/shard_map/ppermute | solution.py:389
  266.4 58.8 %collective-permute-start.38 = (bf16[32,32,128]{2,1,0:T(8,128)(2,1)}, bf16[32,32,128]{2,1,0:T(8,128)(2,1)S(1)}, u32[]{:S(2)}, u32[]{:S(2)}) collective-permute-start(bf16[32,32,128]{2,1,0:T(8,128)(2,1)} %get-tuple-element.146), channel_id=1, source_target_pairs={{0,4},{1,5},{2,6},{3,7},{4,0},{5,1},{6,2},{7,3},{8,12},{9,13},{10,... | collective-permute-start | bytes 786440 | tf_op jit(solution)/shard_map/ppermute | solution.py:389
  291.4 60.3 %collective-permute-start.39 = (bf16[32,32,128]{2,1,0:T(8,128)(2,1)}, bf16[32,32,128]{2,1,0:T(8,128)(2,1)}, u32[]{:S(2)}, u32[]{:S(2)}) collective-permute-start(bf16[32,32,128]{2,1,0:T(8,128)(2,1)} %get-tuple-element.147), channel_id=1, source_target_pairs={{0,5},{1,4},{2,7},{3,6},{4,1},{5,0},{6,3},{7,2},{8,13},{9,12},{10,... | collective-permute-start | bytes 786440 | tf_op jit(solution)/shard_map/ppermute | solution.py:389
  301.0 51.6 %collective-permute-start.40 = (bf16[32,32,128]{2,1,0:T(8,128)(2,1)}, bf16[32,32,128]{2,1,0:T(8,128)(2,1)}, u32[]{:S(2)}, u32[]{:S(2)}) collective-permute-start(bf16[32,32,128]{2,1,0:T(8,128)(2,1)} %get-tuple-element.148), channel_id=1, source_target_pairs={{0,6},{1,7},{2,4},{3,5},{4,2},{5,3},{6,0},{7,1},{8,14},{9,15},{10,... | collective-permute-start | bytes 786440 | tf_op jit(solution)/shard_map/ppermute | solution.py:389
  302.9 51.7 %collective-permute-start.41 = (bf16[32,32,128]{2,1,0:T(8,128)(2,1)}, bf16[32,32,128]{2,1,0:T(8,128)(2,1)}, u32[]{:S(2)}, u32[]{:S(2)}) collective-permute-start(bf16[32,32,128]{2,1,0:T(8,128)(2,1)} %get-tuple-element.149), channel_id=1, source_target_pairs={{0,7},{1,6},{2,5},{3,4},{4,3},{5,2},{6,1},{7,0},{8,15},{9,14},{10,... | collective-permute-start | bytes 786440 | tf_op jit(solution)/shard_map/ppermute | solution.py:389
  305.6 49.6 %collective-permute-start.42 = (bf16[32,32,128]{2,1,0:T(8,128)(2,1)}, bf16[32,32,128]{2,1,0:T(8,128)(2,1)}, u32[]{:S(2)}, u32[]{:S(2)}) collective-permute-start(bf16[32,32,128]{2,1,0:T(8,128)(2,1)} %get-tuple-element.150), channel_id=1, source_target_pairs={{0,2},{1,3},{2,0},{3,1},{4,6},{5,7},{6,4},{7,5},{8,10},{9,11},{10,... | collective-permute-start | bytes 786440 | tf_op jit(solution)/shard_map/ppermute | solution.py:389
  325.9 29.3 %collective-permute-start.43 = (bf16[32,32,128]{2,1,0:T(8,128)(2,1)}, bf16[32,32,128]{2,1,0:T(8,128)(2,1)}, u32[]{:S(2)}, u32[]{:S(2)}) collective-permute-start(bf16[32,32,128]{2,1,0:T(8,128)(2,1)} %get-tuple-element.151), channel_id=1, source_target_pairs={{0,3},{1,2},{2,1},{3,0},{4,7},{5,6},{6,5},{7,4},{8,11},{9,10},{10,... | collective-permute-start | bytes 786440 | tf_op jit(solution)/shard_map/ppermute | solution.py:389
  351.7 22.6 %collective-permute-start.55 = (bf16[32,32,128]{2,1,0:T(8,128)(2,1)}, bf16[32,32,128]{2,1,0:T(8,128)(2,1)}, u32[]{:S(2)}, u32[]{:S(2)}) collective-permute-start(bf16[32,32,128]{2,1,0:T(8,128)(2,1)} %get-tuple-element.167), channel_id=1, source_target_pairs={{0,7},{1,6},{2,5},{3,4},{4,3},{5,2},{6,1},{7,0},{8,15},{9,14},{10,... | collective-permute-start | bytes 786440 | tf_op jit(solution)/shard_map/ppermute | solution.py:389
  352.6 21.9 %collective-permute-start.56 = (bf16[32,32,128]{2,1,0:T(8,128)(2,1)}, bf16[32,32,128]{2,1,0:T(8,128)(2,1)}, u32[]{:S(2)}, u32[]{:S(2)}) collective-permute-start(bf16[32,32,128]{2,1,0:T(8,128)(2,1)} %get-tuple-element.168), channel_id=1, source_target_pairs={{0,2},{1,3},{2,0},{3,1},{4,6},{5,7},{6,4},{7,5},{8,10},{9,11},{10,... | collective-permute-start | bytes 786440 | tf_op jit(solution)/shard_map/ppermute | solution.py:389
  354.5 31.2 %collective-permute-start.57 = (bf16[32,32,128]{2,1,0:T(8,128)(2,1)}, bf16[32,32,128]{2,1,0:T(8,128)(2,1)}, u32[]{:S(2)}, u32[]{:S(2)}) collective-permute-start(bf16[32,32,128]{2,1,0:T(8,128)(2,1)} %get-tuple-element.169), channel_id=1, source_target_pairs={{0,3},{1,2},{2,1},{3,0},{4,7},{5,6},{6,5},{7,4},{8,11},{9,10},{10,... | collective-permute-start | bytes 786440 | tf_op jit(solution)/shard_map/ppermute | solution.py:389
  355.2 35.7 %collective-permute-start.58 = (bf16[32,32,128]{2,1,0:T(8,128)(2,1)}, bf16[32,32,128]{2,1,0:T(8,128)(2,1)}, u32[]{:S(2)}, u32[]{:S(2)}) collective-permute-start(bf16[32,32,128]{2,1,0:T(8,128)(2,1)} %get-tuple-element.172), channel_id=1, source_target_pairs={{0,1},{1,0},{2,3},{3,2},{4,5},{5,4},{6,7},{7,6},{8,9},{9,8},{10,11... | collective-permute-start | bytes 786440 | tf_op jit(solution)/shard_map/ppermute | solution.py:389
  355.2 35.7 %collective-permute-start.59 = (bf16[32,32,128]{2,1,0:T(8,128)(2,1)}, bf16[32,32,128]{2,1,0:T(8,128)(2,1)}, u32[]{:S(2)}, u32[]{:S(2)}) collective-permute-start(bf16[32,32,128]{2,1,0:T(8,128)(2,1)} %get-tuple-element.173), channel_id=1, source_target_pairs={{0,4},{1,5},{2,6},{3,7},{4,0},{5,1},{6,2},{7,3},{8,12},{9,13},{10,... | collective-permute-start | bytes 786440 | tf_op jit(solution)/shard_map/ppermute | solution.py:389
  385.7 26.3 %collective-permute-start.60 = (bf16[32,32,128]{2,1,0:T(8,128)(2,1)}, bf16[32,32,128]{2,1,0:T(8,128)(2,1)S(1)}, u32[]{:S(2)}, u32[]{:S(2)}) collective-permute-start(bf16[32,32,128]{2,1,0:T(8,128)(2,1)} %get-tuple-element.174), channel_id=1, source_target_pairs={{0,5},{1,4},{2,7},{3,6},{4,1},{5,0},{6,3},{7,2},{8,13},{9,12},{10,... | collective-permute-start | bytes 786440 | tf_op jit(solution)/shard_map/ppermute | solution.py:389
  385.8 26.3 %collective-permute-start.61 = (bf16[32,32,128]{2,1,0:T(8,128)(2,1)}, bf16[32,32,128]{2,1,0:T(8,128)(2,1)S(1)}, u32[]{:S(2)}, u32[]{:S(2)}) collective-permute-start(bf16[32,32,128]{2,1,0:T(8,128)(2,1)} %get-tuple-element.175), channel_id=1, source_target_pairs={{0,6},{1,7},{2,4},{3,5},{4,2},{5,3},{6,0},{7,1},{8,14},{9,15},{10,... | collective-permute-start | bytes 786440 | tf_op jit(solution)/shard_map/ppermute | solution.py:389
  387.8 26.3 %collective-permute-start.62 = (bf16[32,32,128]{2,1,0:T(8,128)(2,1)}, bf16[32,32,128]{2,1,0:T(8,128)(2,1)S(1)}, u32[]{:S(2)}, u32[]{:S(2)}) collective-permute-start(bf16[32,32,128]{2,1,0:T(8,128)(2,1)} %get-tuple-element.176), channel_id=1, source_target_pairs={{0,7},{1,6},{2,5},{3,4},{4,3},{5,2},{6,1},{7,0},{8,15},{9,14},{10,... | collective-permute-start | bytes 786440 | tf_op jit(solution)/shard_map/ppermute | solution.py:389
  390.8 25.8 %collective-permute-start.63 = (bf16[32,32,128]{2,1,0:T(8,128)(2,1)}, bf16[32,32,128]{2,1,0:T(8,128)(2,1)S(1)}, u32[]{:S(2)}, u32[]{:S(2)}) collective-permute-start(bf16[32,32,128]{2,1,0:T(8,128)(2,1)} %get-tuple-element.177), channel_id=1, source_target_pairs={{0,2},{1,3},{2,0},{3,1},{4,6},{5,7},{6,4},{7,5},{8,10},{9,11},{10,... | collective-permute-start | bytes 786440 | tf_op jit(solution)/shard_map/ppermute | solution.py:389
  390.9 41.7 %collective-permute-start.64 = (bf16[32,32,128]{2,1,0:T(8,128)(2,1)}, bf16[32,32,128]{2,1,0:T(8,128)(2,1)S(1)}, u32[]{:S(2)}, u32[]{:S(2)}) collective-permute-start(bf16[32,32,128]{2,1,0:T(8,128)(2,1)} %get-tuple-element.178), channel_id=1, source_target_pairs={{0,3},{1,2},{2,1},{3,0},{4,7},{5,6},{6,5},{7,4},{8,11},{9,10},{10,... | collective-permute-start | bytes 786440 | tf_op jit(solution)/shard_map/ppermute | solution.py:389
  412.0 27.1 %collective-permute-start.67 = (bf16[32,16,128]{2,1,0:T(8,128)(2,1)S(1)}, bf16[32,16,128]{2,1,0:T(8,128)(2,1)S(1)}, u32[]{:S(2)}, u32[]{:S(2)}) collective-permute-start(bf16[32,16,128]{2,1,0:T(8,128)(2,1)S(1)} %copy-done.66), channel_id=1, source_target_pairs={{0,5},{1,4},{2,7},{3,6},{4,1},{5,0},{6,3},{7,2},{8,13},{9,12},{10,... | collective-permute-start | bytes 393224 | tf_op jit(solution)/shard_map/ppermute | solution.py:389
  412.1 27.1 %collective-permute-start.68 = (bf16[32,16,128]{2,1,0:T(8,128)(2,1)S(1)}, bf16[32,16,128]{2,1,0:T(8,128)(2,1)S(1)}, u32[]{:S(2)}, u32[]{:S(2)}) collective-permute-start(bf16[32,16,128]{2,1,0:T(8,128)(2,1)S(1)} %copy-done.65), channel_id=1, source_target_pairs={{0,6},{1,7},{2,4},{3,5},{4,2},{5,3},{6,0},{7,1},{8,14},{9,15},{10,... | collective-permute-start | bytes 393224 | tf_op jit(solution)/shard_map/ppermute | solution.py:389
  414.0 25.1 %collective-permute-start.69 = (bf16[32,16,128]{2,1,0:T(8,128)(2,1)S(1)}, bf16[32,16,128]{2,1,0:T(8,128)(2,1)S(1)}, u32[]{:S(2)}, u32[]{:S(2)}) collective-permute-start(bf16[32,16,128]{2,1,0:T(8,128)(2,1)S(1)} %copy-done.64), channel_id=1, source_target_pairs={{0,7},{1,6},{2,5},{3,4},{4,3},{5,2},{6,1},{7,0},{8,15},{9,14},{10,... | collective-permute-start | bytes 393224 | tf_op jit(solution)/shard_map/ppermute | solution.py:389
  416.6 22.6 %collective-permute-start.70 = (bf16[32,16,128]{2,1,0:T(8,128)(2,1)S(1)}, bf16[32,16,128]{2,1,0:T(8,128)(2,1)S(1)}, u32[]{:S(2)}, u32[]{:S(2)}) collective-permute-start(bf16[32,16,128]{2,1,0:T(8,128)(2,1)S(1)} %copy-done.63), channel_id=1, source_target_pairs={{0,2},{1,3},{2,0},{3,1},{4,6},{5,7},{6,4},{7,5},{8,10},{9,11},{10,... | collective-permute-start | bytes 393224 | tf_op jit(solution)/shard_map/ppermute | solution.py:389
  (85 other events, 2588.1 us)

commit v19 on v16

--- a/solution.py
+++ b/solution.py
@@ -382,7 +382,7 @@
 def slots_of(peers):
     order = [0]
     for slot in range(peers // 2):
-        order += [peers // 2 + slot] + ([slot + 1] if slot + 1 < peers // 2 else [])
+        order += ([slot + 1] if slot + 1 < peers // 2 else []) + [peers // 2 + slot]
     return order
 
 

time: 423 us -> 419 us (level)
  waiting for transfers between devices: 108 us -> 96.5 us
    ppermute x70, waiting for transfers between devices: 105 us -> 93.4 us  [exchanged(): lax.ppermute(arrays[slot], 'shot', [(i, i ^ slot) for i in range(peers)])]
  transfers between devices with their start and end apart: 72 -> 72, of which waited for: 18 -> 14; matrix products, arithmetic and copies ran while one was open for 1% -> 1% of each run, Pallas kernels for 32% -> 33%
where the time goes in v19:
time: 419 us; the launch traced here: 413 us
  Pallas kernels  149 us (36%)
  starting transfers between devices  133 us (32%)
  waiting for transfers between devices  96.5 us (23%)
  local copies, waits for them, and re-layouts  20.4 us (5%)
  blocking collectives  9.91 us (2%)
    ppermute x70, starting transfers between devices, exchanged(): lax.ppermute(arrays[slot], 'shot', [(i, i ^ slot) for i in range(peers)])  130 us
    ppermute x70, waiting for transfers between devices, exchanged(): lax.ppermute(arrays[slot], 'shot', [(i, i ^ slot) for i in range(peers)])  93.4 us
    pallas_call x5, Pallas kernels, spectra_of(): pl.pallas_call(spectra_kernel, grid_spec=pltpu.PrefetchScalarGridSpec(num...  64.6 us
    pallas_call x5, Pallas kernels, shrunk_of(): pl.pallas_call(shots_kernel, grid_spec=pltpu.PrefetchScalarGridSpec(num_s...  58.6 us
    pallas_call x5, Pallas kernels, updated_of(): pl.pallas_call(functools.partial(update_kernel, len(restored)), grid_spec...  26 us
    unnamed x154, local copies, waits for them, and re-layouts  16.6 us
    psum x1, blocking collectives, local(): lax.psum(jnp.sum(energy, axis=1), 'patch')  9.91 us
  transfers between devices with their start and end apart: 72, of which 14 were waited for; matrix products, arithmetic and copies ran while one was open for 1% of the time, Pallas kernels for 33%

profile of v19, /device:TPU:0, one launch (start us, length us, event | category | flops | bytes accessed | tf_op | source)
XLA Modules:
  0.0 413.2 jit_solution(15649626496936269609)
XLA Ops:
  3.1 2.4 collective-permute-start
  6.4 1.3 collective-permute-start.1
  9.8 3.2 collective-permute-done.1.after_ref
  13.8 9.9 %spectra.5 = (bf16[32,16,128]{2,1,0:T(8,128)(2,1)}, bf16[32,16,128]{2,1,0:T(8,128)(2,1)}, bf16[32,16,128]{2,1,0:T(8,128)(2,1)}, bf16[32,16,128]{2,1,0:T(8,128)(2...) custom-call(s32[9]{0:T(128)} %pad_add_fusion.meta_ref, ...), custom_call_target="tpu_custom_call" | custom-call | flops 1073741824 | bytes 5242880 | tf_op jit(solution)/shard_map/spectra/pallas_call | solution.py:270
  23.8 9.6 %collective-permute-start.2 = (bf16[32,16,128]{2,1,0:T(8,128)(2,1)}, bf16[32,16,128]{2,1,0:T(8,128)(2,1)S(1)}, u32[]{:S(2)}, u32[]{:S(2)}) collective-permute-start(bf16[32,16,128]{2,1,0:T(8,128)(2,1)} %get-tuple-element.100), channel_id=1, source_target_pairs={{0,1},{1,0},{2,3},{3,2},{4,5},{5,4},{6,7},{7,6},{8,9},{9,8},{10,11... | collective-permute-start | bytes 393224 | tf_op jit(solution)/shard_map/ppermute | solution.py:392
  33.4 2.6 collective-permute-start.3
  37.0 14.9 %spectra.6 = (bf16[32,32,128]{2,1,0:T(8,128)(2,1)}, bf16[32,32,128]{2,1,0:T(8,128)(2,1)}, bf16[32,32,128]{2,1,0:T(8,128)(2,1)}, bf16[32,32,128]{2,1,0:T(8,128)(2...) custom-call(s32[9]{0:T(128)} %pad_add_fusion.meta_ref, ...), custom_call_target="tpu_custom_call" | custom-call | flops 2147483648 | bytes 8388608 | tf_op jit(solution)/shard_map/spectra/pallas_call | solution.py:270
  53.9 1.5 collective-permute-start.6
  55.4 1.4 collective-permute-start.7
  56.8 2.6 collective-permute-start.8
  59.4 4.2 %collective-permute-done.6.refs_5_ = bf16[32,16,128]{2,1,0:T(8,128)(2,1)S(1)} collective-permute-done((bf16[32,16,128]{2,1,0:T(8,128)(2,1)S(1)}, bf16[32,16,128]{2,1,0:T(8,128)(2,1)S(1)}, u32[]{:S(2)}, u32[]{:S(2)}) %collective-permute-start.6) | collective-permute-done | bytes 131104 | tf_op jit(solution)/shard_map/ppermute | solution.py:392
  64.4 4.5 %collective-permute-done.7.refs_6_ = bf16[32,16,128]{2,1,0:T(8,128)(2,1)S(1)} collective-permute-done((bf16[32,16,128]{2,1,0:T(8,128)(2,1)S(1)}, bf16[32,16,128]{2,1,0:T(8,128)(2,1)S(1)}, u32[]{:S(2)}, u32[]{:S(2)}) %collective-permute-start.7) | collective-permute-done | bytes 131104 | tf_op jit(solution)/shard_map/ppermute | solution.py:392
  68.9 8.1 %collective-permute-start.12 = (bf16[32,32,128]{2,1,0:T(8,128)(2,1)}, bf16[32,32,128]{2,1,0:T(8,128)(2,1)S(1)}, u32[]{:S(2)}, u32[]{:S(2)}) collective-permute-start(bf16[32,32,128]{2,1,0:T(8,128)(2,1)} %get-tuple-element.113), channel_id=1, source_target_pairs={{0,5},{1,4},{2,7},{3,6},{4,1},{5,0},{6,3},{7,2},{8,13},{9,12},{10,... | collective-permute-start | bytes 786440 | tf_op jit(solution)/shard_map/ppermute | solution.py:392
  77.0 2.2 collective-permute-start.13
  79.3 2.0 collective-permute-start.14
  81.3 1.5 collective-permute-start.15
  82.9 14.7 %spectra.7 = (bf16[32,32,128]{2,1,0:T(8,128)(2,1)}, bf16[32,32,128]{2,1,0:T(8,128)(2,1)}, bf16[32,32,128]{2,1,0:T(8,128)(2,1)}, bf16[32,32,128]{2,1,0:T(8,128)(2...) custom-call(s32[9]{0:T(128)} %pad_add_fusion.meta_ref, ...), custom_call_target="tpu_custom_call" | custom-call | flops 2147483648 | bytes 8388608 | tf_op jit(solution)/shard_map/spectra/pallas_call | solution.py:270
  97.7 7.2 %shrink.5 = (bf16[32,16,128]{2,1,0:T(8,128)(2,1)}, bf16[32,16,128]{2,1,0:T(8,128)(2,1)}, bf16[32,16,128]{2,1,0:T(8,128)(2,1)}, bf16[32,16,128]{2,1,0:T(8,128)(2,...) custom-call(s32[9]{0:T(128)} %pad_add_fusion.meta_ref, ...), custom_call_target="tpu_custom_call" | custom-call | flops 1073741824 | bytes 2359296 | tf_op jit(solution)/shard_map/shrink/pallas_call | solution.py:320
  105.4 2.6 collective-permute-start.25
  109.2 11.1 %collective-permute-start.17 = (bf16[32,32,128]{2,1,0:T(8,128)(2,1)}, bf16[32,32,128]{2,1,0:T(8,128)(2,1)S(1)}, u32[]{:S(2)}, u32[]{:S(2)}) collective-permute-start(bf16[32,32,128]{2,1,0:T(8,128)(2,1)} %get-tuple-element.121), channel_id=1, source_target_pairs={{0,4},{1,5},{2,6},{3,7},{4,0},{5,1},{6,2},{7,3},{8,12},{9,13},{10,... | collective-permute-start | bytes 786440 | tf_op jit(solution)/shard_map/ppermute | solution.py:392
  122.8 1.9 collective-permute-start.28
  124.7 4.8 %collective-permute-done.26.refs_4_ = bf16[32,16,128]{2,1,0:T(8,128)(2,1)S(1)} collective-permute-done((bf16[32,16,128]{2,1,0:T(8,128)(2,1)}, bf16[32,16,128]{2,1,0:T(8,128)(2,1)S(1)}, u32[]{:S(2)}, u32[]{:S(2)}) %collective-permute-start.26) | collective-permute-done | bytes 131104 | tf_op jit(solution)/shard_map/ppermute | solution.py:392
  130.1 1.9 collective-permute-start.29
  132.0 14.7 %spectra.8 = (bf16[32,32,128]{2,1,0:T(8,128)(2,1)}, bf16[32,32,128]{2,1,0:T(8,128)(2,1)}, bf16[32,32,128]{2,1,0:T(8,128)(2,1)}, bf16[32,32,128]{2,1,0:T(8,128)(2...) custom-call(s32[9]{0:T(128)} %pad_add_fusion.meta_ref, ...), custom_call_target="tpu_custom_call" | custom-call | flops 2147483648 | bytes 8388608 | tf_op jit(solution)/shard_map/spectra/pallas_call | solution.py:270
  146.8 1.9 collective-permute-start.19
  149.0 2.0 collective-permute-start.21
  151.1 1.5 collective-permute-start.22
  152.6 14.7 %shrink.6 = (bf16[32,32,128]{2,1,0:T(8,128)(2,1)}, bf16[32,32,128]{2,1,0:T(8,128)(2,1)}, bf16[32,32,128]{2,1,0:T(8,128)(2,1)}, bf16[32,32,128]{2,1,0:T(8,128)(2,...) custom-call(s32[9]{0:T(128)} %pad_add_fusion.meta_ref, ...), custom_call_target="tpu_custom_call" | custom-call | flops 2147483648 | bytes 4456448 | tf_op jit(solution)/shard_map/shrink/pallas_call | solution.py:320
  167.4 10.3 %spectra.9 = (bf16[32,16,128]{2,1,0:T(8,128)(2,1)}, bf16[32,16,128]{2,1,0:T(8,128)(2,1)}, bf16[32,16,128]{2,1,0:T(8,128)(2,1)}, bf16[32,16,128]{2,1,0:T(8,128)(2...) custom-call(s32[9]{0:T(128)} %pad_add_fusion.meta_ref, ...), custom_call_target="tpu_custom_call" | custom-call | flops 1073741824 | bytes 5242880 | tf_op jit(solution)/shard_map/spectra/pallas_call | solution.py:270
  178.9 1.9 collective-permute-start.46
  180.9 10.2 %collective-permute-start.48 = (bf16[32,16,128]{2,1,0:T(8,128)(2,1)}, bf16[32,16,128]{2,1,0:T(8,128)(2,1)S(1)}, u32[]{:S(2)}, u32[]{:S(2)}) collective-permute-start(bf16[32,16,128]{2,1,0:T(8,128)(2,1)} %get-tuple-element.159), channel_id=1, source_target_pairs={{0,3},{1,2},{2,1},{3,0},{4,7},{5,6},{6,5},{7,4},{8,11},{9,10},{10,... | collective-permute-start | bytes 393224 | tf_op jit(solution)/shard_map/ppermute | solution.py:392
  191.0 2.8 collective-permute-done.45.refs_2_
  193.9 2.2 collective-permute-start.32
  196.1 2.2 collective-permute-start.49
  198.9 4.5 %collective-permute-start.50 = (bf16[32,16,128]{2,1,0:T(8,128)(2,1)}, bf16[32,16,128]{2,1,0:T(8,128)(2,1)}, u32[]{:S(2)}, u32[]{:S(2)}) collective-permute-start(bf16[32,16,128]{2,1,0:T(8,128)(2,1)} %get-tuple-element.161), channel_id=1, source_target_pairs={{0,7},{1,6},{2,5},{3,4},{4,3},{5,2},{6,1},{7,0},{8,15},{9,14},{10,... | collective-permute-start | bytes 393224 | tf_op jit(solution)/shard_map/ppermute | solution.py:392
  203.5 14.8 %shrink.7 = (bf16[32,32,128]{2,1,0:T(8,128)(2,1)}, bf16[32,32,128]{2,1,0:T(8,128)(2,1)}, bf16[32,32,128]{2,1,0:T(8,128)(2,1)}, bf16[32,32,128]{2,1,0:T(8,128)(2,...) custom-call(s32[9]{0:T(128)} %pad_add_fusion.meta_ref, ...), custom_call_target="tpu_custom_call" | custom-call | flops 2147483648 | bytes 4456448 | tf_op jit(solution)/shard_map/shrink/pallas_call | solution.py:320
  219.0 3.5 collective-permute-start.35
  223.0 25.5 %collective-permute-done.33.refs_4_ = bf16[32,32,128]{2,1,0:T(8,128)(2,1)S(1)} collective-permute-done((bf16[32,32,128]{2,1,0:T(8,128)(2,1)S(1)}, bf16[32,32,128]{2,1,0:T(8,128)(2,1)S(1)}, u32[]{:S(2)}, u32[]{:S(2)}) %collective-permute-start.33) | collective-permute-done | bytes 262176 | tf_op jit(solution)/shard_map/ppermute | solution.py:392
  248.6 4.8 %collective-permute-start.54 = (bf16[32,32,128]{2,1,0:T(8,128)(2,1)}, bf16[32,32,128]{2,1,0:T(8,128)(2,1)S(1)}, u32[]{:S(2)}, u32[]{:S(2)}) collective-permute-start(bf16[32,32,128]{2,1,0:T(8,128)(2,1)} %get-tuple-element.166), channel_id=1, source_target_pairs={{0,5},{1,4},{2,7},{3,6},{4,1},{5,0},{6,3},{7,2},{8,13},{9,12},{10,... | collective-permute-start | bytes 786440 | tf_op jit(solution)/shard_map/ppermute | solution.py:392
  253.4 12.4 %collective-permute-start.38 = (bf16[32,32,128]{2,1,0:T(8,128)(2,1)}, bf16[32,32,128]{2,1,0:T(8,128)(2,1)S(1)}, u32[]{:S(2)}, u32[]{:S(2)}) collective-permute-start(bf16[32,32,128]{2,1,0:T(8,128)(2,1)} %get-tuple-element.146), channel_id=1, source_target_pairs={{0,4},{1,5},{2,6},{3,7},{4,0},{5,1},{6,2},{7,3},{8,12},{9,13},{10,... | collective-permute-start | bytes 786440 | tf_op jit(solution)/shard_map/ppermute | solution.py:392
  265.9 9.8 %collective-permute-done.52.refs_2_ = bf16[32,32,128]{2,1,0:T(8,128)(2,1)S(1)} collective-permute-done((bf16[32,32,128]{2,1,0:T(8,128)(2,1)}, bf16[32,32,128]{2,1,0:T(8,128)(2,1)S(1)}, u32[]{:S(2)}, u32[]{:S(2)}) %collective-permute-start.52) | collective-permute-done | bytes 262176 | tf_op jit(solution)/shard_map/ppermute | solution.py:392
  275.7 2.1 collective-permute-start.40
  277.9 4.5 %collective-permute-done.54.refs_4_ = bf16[32,32,128]{2,1,0:T(8,128)(2,1)S(1)} collective-permute-done((bf16[32,32,128]{2,1,0:T(8,128)(2,1)}, bf16[32,32,128]{2,1,0:T(8,128)(2,1)S(1)}, u32[]{:S(2)}, u32[]{:S(2)}) %collective-permute-start.54) | collective-permute-done | bytes 262176 | tf_op jit(solution)/shard_map/ppermute | solution.py:392
  282.3 1.3 collective-permute-start.42
  283.6 9.1 %collective-permute-done.38.refs_2_ = bf16[32,32,128]{2,1,0:T(8,128)(2,1)S(1)} collective-permute-done((bf16[32,32,128]{2,1,0:T(8,128)(2,1)}, bf16[32,32,128]{2,1,0:T(8,128)(2,1)S(1)}, u32[]{:S(2)}, u32[]{:S(2)}) %collective-permute-start.38) | collective-permute-done | bytes 262176 | tf_op jit(solution)/shard_map/ppermute | solution.py:392
  293.4 1.8 collective-permute-start.43
  302.5 3.2 update.5
  306.4 14.6 %shrink.8 = (bf16[32,32,128]{2,1,0:T(8,128)(2,1)}, bf16[32,32,128]{2,1,0:T(8,128)(2,1)}, bf16[32,32,128]{2,1,0:T(8,128)(2,1)}, bf16[32,32,128]{2,1,0:T(8,128)(2,...) custom-call(s32[9]{0:T(128)} %pad_add_fusion.meta_ref, ...), custom_call_target="tpu_custom_call" | custom-call | flops 2147483648 | bytes 4456448 | tf_op jit(solution)/shard_map/shrink/pallas_call | solution.py:320
  321.1 2.4 collective-permute-start.56
  323.5 1.4 collective-permute-start.57
  328.5 6.4 %update.6 = (f32[32,128,1024]{2,1,0:T(8,128)}, f32[8,128]{1,0:T(8,128)S(1)}) custom-call(s32[9]{0:T(128)S(1)} %copy-done.13, bf16[1024,1024]{1,0:T(8,128)(2,1)S(1)} %copy-done, bf16[32,32,128]{2,1,0:T(8,128)(2,1)S(1)} %copy-done.2, bf16[32,32,128]{2,1,0:T(8,128)(2,1)S(1)} %copy-done.1, ...), custom_call_target="tpu_custom_call", output_to_operand_aliasing={{0}: (11, {})} | custom-call | flops 2147483648 | bytes 8388608 | tf_op jit(solution)/shard_map/update/pallas_call | solution.py:351
  335.5 7.3 %shrink.9 = (bf16[32,16,128]{2,1,0:T(8,128)(2,1)}, bf16[32,16,128]{2,1,0:T(8,128)(2,1)}, bf16[32,16,128]{2,1,0:T(8,128)(2,1)}, bf16[32,16,128]{2,1,0:T(8,128)(2,...) custom-call(s32[9]{0:T(128)} %pad_add_fusion.meta_ref, ...), custom_call_target="tpu_custom_call" | custom-call | flops 1073741824 | bytes 2359296 | tf_op jit(solution)/shard_map/shrink/pallas_call | solution.py:320
  343.0 6.7 %collective-permute-start.66 = (bf16[32,16,128]{2,1,0:T(8,128)(2,1)}, bf16[32,16,128]{2,1,0:T(8,128)(2,1)}, u32[]{:S(2)}, u32[]{:S(2)}) collective-permute-start(bf16[32,16,128]{2,1,0:T(8,128)(2,1)} %get-tuple-element.182), channel_id=1, source_target_pairs={{0,4},{1,5},{2,6},{3,7},{4,0},{5,1},{6,2},{7,3},{8,12},{9,13},{10,... | collective-permute-start | bytes 393224 | tf_op jit(solution)/shard_map/ppermute | solution.py:392
  349.9 9.9 %psum.7 = f32[32]{0:T(128)S(1)} all-reduce(f32[32]{0:T(128)S(1)} %add_reduce_fusion), channel_id=1, replica_groups=mesh['patch'=4,'shot'=8] {'patch'}, use_global_device_ids=true, to_apply=%region_1.0 | all-reduce | flops 32 | bytes 256 | tf_op jit(solution)/shard_map/psum | solution.py:517
  360.0 5.8 %collective-permute-done.66.refs_2_ = bf16[32,16,128]{2,1,0:T(8,128)(2,1)} collective-permute-done((bf16[32,16,128]{2,1,0:T(8,128)(2,1)}, bf16[32,16,128]{2,1,0:T(8,128)(2,1)}, u32[]{:S(2)}, u32[]{:S(2)}) %collective-permute-start.66) | collective-permute-done | bytes 131104 | tf_op jit(solution)/shard_map/ppermute | solution.py:392
  365.7 1.9 collective-permute-start.63
  369.5 6.2 %update.7 = (f32[32,128,1024]{2,1,0:T(8,128)}, f32[8,128]{1,0:T(8,128)S(1)}) custom-call(s32[9]{0:T(128)S(1)} %copy-done.14, bf16[1024,1024]{1,0:T(8,128)(2,1)S(1)} %copy-done, bf16[32,16,128]{2,1,0:T(8,128)(2,1)S(1)} %copy-done.4, bf16[32,32,128]{2,1,0:T(8,128)(2,1)S(1)} %copy-done.6, ...), custom_call_target="tpu_custom_call", output_to_operand_aliasing={{0}: (11, {})} | custom-call | flops 2147483648 | bytes 8388608 | tf_op jit(solution)/shard_map/update/pallas_call | solution.py:351
  375.7 1.3 collective-permute-start.67
  377.0 2.2 collective-permute-start.68
  379.2 13.6 %collective-permute-done.62.refs_5_ = bf16[32,32,128]{2,1,0:T(8,128)(2,1)S(1)} collective-permute-done((bf16[32,32,128]{2,1,0:T(8,128)(2,1)}, bf16[32,32,128]{2,1,0:T(8,128)(2,1)S(1)}, u32[]{:S(2)}, u32[]{:S(2)}) %collective-permute-start.62) | collective-permute-done | bytes 262176 | tf_op jit(solution)/shard_map/ppermute | solution.py:392
  392.8 2.4 collective-permute-start.70
  396.1 6.1 %update.8 = (f32[32,128,1024]{2,1,0:T(8,128)}, f32[8,128]{1,0:T(8,128)S(1)}) custom-call(s32[9]{0:T(128)S(1)} %copy-done.14, bf16[1024,1024]{1,0:T(8,128)(2,1)S(1)} %copy-done, f32[8,128]{1,0:T(8,128)S(1)} %get-tuple-element.171._, bf16[32,32,128]{2,1,0:T(8,128)(2,1)S(1)} %copy-done.3, ...), custom_call_target="tpu_custom_call", output_to_operand_aliasing={{0}: (11, {})} | custom-call | flops 2147483648 | bytes 8388608 | tf_op jit(solution)/shard_map/update/pallas_call | solution.py:351
  402.2 6.9 %collective-permute-done.68.refs_4_ = bf16[32,16,128]{2,1,0:T(8,128)(2,1)S(1)} collective-permute-done((bf16[32,16,128]{2,1,0:T(8,128)(2,1)S(1)}, bf16[32,16,128]{2,1,0:T(8,128)(2,1)S(1)}, u32[]{:S(2)}, u32[]{:S(2)}) %collective-permute-start.68) | collective-permute-done | bytes 131104 | tf_op jit(solution)/shard_map/ppermute | solution.py:392
  409.1 4.1 update.9
  (261 shorter events, 34.5 us)
Async XLA Ops:
  23.8 29.1 %collective-permute-start.2 = (bf16[32,16,128]{2,1,0:T(8,128)(2,1)}, bf16[32,16,128]{2,1,0:T(8,128)(2,1)S(1)}, u32[]{:S(2)}, u32[]{:S(2)}) collective-permute-start(bf16[32,16,128]{2,1,0:T(8,128)(2,1)} %get-tuple-element.100), channel_id=1, source_target_pairs={{0,1},{1,0},{2,3},{3,2},{4,5},{5,4},{6,7},{7,6},{8,9},{9,8},{10,11... | collective-permute-start | bytes 393224 | tf_op jit(solution)/shard_map/ppermute | solution.py:392
  33.4 20.5 %collective-permute-start.3 = (bf16[32,16,128]{2,1,0:T(8,128)(2,1)}, bf16[32,16,128]{2,1,0:T(8,128)(2,1)S(1)}, u32[]{:S(2)}, u32[]{:S(2)}) collective-permute-start(bf16[32,16,128]{2,1,0:T(8,128)(2,1)} %get-tuple-element.101), channel_id=1, source_target_pairs={{0,4},{1,5},{2,6},{3,7},{4,0},{5,1},{6,2},{7,3},{8,12},{9,13},{10,... | collective-permute-start | bytes 393224 | tf_op jit(solution)/shard_map/ppermute | solution.py:392
  36.0 19.4 %collective-permute-start.4 = (bf16[32,16,128]{2,1,0:T(8,128)(2,1)}, bf16[32,16,128]{2,1,0:T(8,128)(2,1)S(1)}, u32[]{:S(2)}, u32[]{:S(2)}) collective-permute-start(bf16[32,16,128]{2,1,0:T(8,128)(2,1)} %get-tuple-element.102), channel_id=1, source_target_pairs={{0,2},{1,3},{2,0},{3,1},{4,6},{5,7},{6,4},{7,5},{8,10},{9,11},{10,... | collective-permute-start | bytes 393224 | tf_op jit(solution)/shard_map/ppermute | solution.py:392
  36.0 20.9 %collective-permute-start.5 = (bf16[32,16,128]{2,1,0:T(8,128)(2,1)}, bf16[32,16,128]{2,1,0:T(8,128)(2,1)S(1)}, u32[]{:S(2)}, u32[]{:S(2)}) collective-permute-start(bf16[32,16,128]{2,1,0:T(8,128)(2,1)} %get-tuple-element.103), channel_id=1, source_target_pairs={{0,5},{1,4},{2,7},{3,6},{4,1},{5,0},{6,3},{7,2},{8,13},{9,12},{10,... | collective-permute-start | bytes 393224 | tf_op jit(solution)/shard_map/ppermute | solution.py:392
  51.9 27.4 %collective-permute-start.9 = (bf16[32,32,128]{2,1,0:T(8,128)(2,1)}, bf16[32,32,128]{2,1,0:T(8,128)(2,1)S(1)}, u32[]{:S(2)}, u32[]{:S(2)}) collective-permute-start(bf16[32,32,128]{2,1,0:T(8,128)(2,1)} %get-tuple-element.110), channel_id=1, source_target_pairs={{0,1},{1,0},{2,3},{3,2},{4,5},{5,4},{6,7},{7,6},{8,9},{9,8},{10,11... | collective-permute-start | bytes 786440 | tf_op jit(solution)/shard_map/ppermute | solution.py:392
  52.9 28.4 %collective-permute-start.10 = (bf16[32,32,128]{2,1,0:T(8,128)(2,1)}, bf16[32,32,128]{2,1,0:T(8,128)(2,1)S(1)}, u32[]{:S(2)}, u32[]{:S(2)}) collective-permute-start(bf16[32,32,128]{2,1,0:T(8,128)(2,1)} %get-tuple-element.111), channel_id=1, source_target_pairs={{0,4},{1,5},{2,6},{3,7},{4,0},{5,1},{6,2},{7,3},{8,12},{9,13},{10,... | collective-permute-start | bytes 786440 | tf_op jit(solution)/shard_map/ppermute | solution.py:392
  56.8 20.2 %collective-permute-start.8 = (bf16[32,16,128]{2,1,0:T(8,128)(2,1)S(1)}, bf16[32,16,128]{2,1,0:T(8,128)(2,1)S(1)}, u32[]{:S(2)}, u32[]{:S(2)}) collective-permute-start(bf16[32,16,128]{2,1,0:T(8,128)(2,1)S(1)} %copy-done.71), channel_id=1, source_target_pairs={{0,7},{1,6},{2,5},{3,4},{4,3},{5,2},{6,1},{7,0},{8,15},{9,14},{10,... | collective-permute-start | bytes 393224 | tf_op jit(solution)/shard_map/ppermute | solution.py:392
  63.7 41.3 %collective-permute-start.11 = (bf16[32,32,128]{2,1,0:T(8,128)(2,1)}, bf16[32,32,128]{2,1,0:T(8,128)(2,1)S(1)}, u32[]{:S(2)}, u32[]{:S(2)}) collective-permute-start(bf16[32,32,128]{2,1,0:T(8,128)(2,1)} %get-tuple-element.112), channel_id=1, source_target_pairs={{0,2},{1,3},{2,0},{3,1},{4,6},{5,7},{6,4},{7,5},{8,10},{9,11},{10,... | collective-permute-start | bytes 786440 | tf_op jit(solution)/shard_map/ppermute | solution.py:392
  68.9 36.5 %collective-permute-start.12 = (bf16[32,32,128]{2,1,0:T(8,128)(2,1)}, bf16[32,32,128]{2,1,0:T(8,128)(2,1)S(1)}, u32[]{:S(2)}, u32[]{:S(2)}) collective-permute-start(bf16[32,32,128]{2,1,0:T(8,128)(2,1)} %get-tuple-element.113), channel_id=1, source_target_pairs={{0,5},{1,4},{2,7},{3,6},{4,1},{5,0},{6,3},{7,2},{8,13},{9,12},{10,... | collective-permute-start | bytes 786440 | tf_op jit(solution)/shard_map/ppermute | solution.py:392
  77.0 28.3 %collective-permute-start.13 = (bf16[32,32,128]{2,1,0:T(8,128)(2,1)}, bf16[32,32,128]{2,1,0:T(8,128)(2,1)S(1)}, u32[]{:S(2)}, u32[]{:S(2)}) collective-permute-start(bf16[32,32,128]{2,1,0:T(8,128)(2,1)} %get-tuple-element.114), channel_id=1, source_target_pairs={{0,3},{1,2},{2,1},{3,0},{4,7},{5,6},{6,5},{7,4},{8,11},{9,10},{10,... | collective-permute-start | bytes 786440 | tf_op jit(solution)/shard_map/ppermute | solution.py:392
  79.3 28.7 %collective-permute-start.14 = (bf16[32,32,128]{2,1,0:T(8,128)(2,1)}, bf16[32,32,128]{2,1,0:T(8,128)(2,1)S(1)}, u32[]{:S(2)}, u32[]{:S(2)}) collective-permute-start(bf16[32,32,128]{2,1,0:T(8,128)(2,1)} %get-tuple-element.115), channel_id=1, source_target_pairs={{0,6},{1,7},{2,4},{3,5},{4,2},{5,3},{6,0},{7,1},{8,14},{9,15},{10,... | collective-permute-start | bytes 786440 | tf_op jit(solution)/shard_map/ppermute | solution.py:392
  81.3 26.7 %collective-permute-start.15 = (bf16[32,32,128]{2,1,0:T(8,128)(2,1)}, bf16[32,32,128]{2,1,0:T(8,128)(2,1)S(1)}, u32[]{:S(2)}, u32[]{:S(2)}) collective-permute-start(bf16[32,32,128]{2,1,0:T(8,128)(2,1)} %get-tuple-element.116), channel_id=1, source_target_pairs={{0,7},{1,6},{2,5},{3,4},{4,3},{5,2},{6,1},{7,0},{8,15},{9,14},{10,... | collective-permute-start | bytes 786440 | tf_op jit(solution)/shard_map/ppermute | solution.py:392
  105.4 16.1 %collective-permute-start.24 = (bf16[32,16,128]{2,1,0:T(8,128)(2,1)}, bf16[32,16,128]{2,1,0:T(8,128)(2,1)S(1)}, u32[]{:S(2)}, u32[]{:S(2)}) collective-permute-start(bf16[32,16,128]{2,1,0:T(8,128)(2,1)} %get-tuple-element.129), channel_id=1, source_target_pairs={{0,4},{1,5},{2,6},{3,7},{4,0},{5,1},{6,2},{7,3},{8,12},{9,13},{10,... | collective-permute-start | bytes 393224 | tf_op jit(solution)/shard_map/ppermute | solution.py:392
  105.4 16.8 %collective-permute-start.25 = (bf16[32,16,128]{2,1,0:T(8,128)(2,1)}, bf16[32,16,128]{2,1,0:T(8,128)(2,1)S(1)}, u32[]{:S(2)}, u32[]{:S(2)}) collective-permute-start(bf16[32,16,128]{2,1,0:T(8,128)(2,1)} %get-tuple-element.130), channel_id=1, source_target_pairs={{0,2},{1,3},{2,0},{3,1},{4,6},{5,7},{6,4},{7,5},{8,10},{9,11},{10,... | collective-permute-start | bytes 393224 | tf_op jit(solution)/shard_map/ppermute | solution.py:392
  108.0 21.5 %collective-permute-start.26 = (bf16[32,16,128]{2,1,0:T(8,128)(2,1)}, bf16[32,16,128]{2,1,0:T(8,128)(2,1)S(1)}, u32[]{:S(2)}, u32[]{:S(2)}) collective-permute-start(bf16[32,16,128]{2,1,0:T(8,128)(2,1)} %get-tuple-element.131), channel_id=1, source_target_pairs={{0,5},{1,4},{2,7},{3,6},{4,1},{5,0},{6,3},{7,2},{8,13},{9,12},{10,... | collective-permute-start | bytes 393224 | tf_op jit(solution)/shard_map/ppermute | solution.py:392
  108.0 41.0 %collective-permute-start.16 = (bf16[32,32,128]{2,1,0:T(8,128)(2,1)}, bf16[32,32,128]{2,1,0:T(8,128)(2,1)S(1)}, u32[]{:S(2)}, u32[]{:S(2)}) collective-permute-start(bf16[32,32,128]{2,1,0:T(8,128)(2,1)} %get-tuple-element.120), channel_id=1, source_target_pairs={{0,1},{1,0},{2,3},{3,2},{4,5},{5,4},{6,7},{7,6},{8,9},{9,8},{10,11... | collective-permute-start | bytes 786440 | tf_op jit(solution)/shard_map/ppermute | solution.py:392
  109.2 41.8 %collective-permute-start.17 = (bf16[32,32,128]{2,1,0:T(8,128)(2,1)}, bf16[32,32,128]{2,1,0:T(8,128)(2,1)S(1)}, u32[]{:S(2)}, u32[]{:S(2)}) collective-permute-start(bf16[32,32,128]{2,1,0:T(8,128)(2,1)} %get-tuple-element.121), channel_id=1, source_target_pairs={{0,4},{1,5},{2,6},{3,7},{4,0},{5,1},{6,2},{7,3},{8,12},{9,13},{10,... | collective-permute-start | bytes 786440 | tf_op jit(solution)/shard_map/ppermute | solution.py:392
  122.1 24.6 %collective-permute-start.27 = (bf16[32,16,128]{2,1,0:T(8,128)(2,1)}, bf16[32,16,128]{2,1,0:T(8,128)(2,1)S(1)}, u32[]{:S(2)}, u32[]{:S(2)}) collective-permute-start(bf16[32,16,128]{2,1,0:T(8,128)(2,1)} %get-tuple-element.132), channel_id=1, source_target_pairs={{0,3},{1,2},{2,1},{3,0},{4,7},{5,6},{6,5},{7,4},{8,11},{9,10},{10,... | collective-permute-start | bytes 393224 | tf_op jit(solution)/shard_map/ppermute | solution.py:392
  122.8 24.0 %collective-permute-start.28 = (bf16[32,16,128]{2,1,0:T(8,128)(2,1)}, bf16[32,16,128]{2,1,0:T(8,128)(2,1)S(1)}, u32[]{:S(2)}, u32[]{:S(2)}) collective-permute-start(bf16[32,16,128]{2,1,0:T(8,128)(2,1)} %get-tuple-element.133), channel_id=1, source_target_pairs={{0,6},{1,7},{2,4},{3,5},{4,2},{5,3},{6,0},{7,1},{8,14},{9,15},{10,... | collective-permute-start | bytes 393224 | tf_op jit(solution)/shard_map/ppermute | solution.py:392
  130.1 18.6 %collective-permute-start.29 = (bf16[32,16,128]{2,1,0:T(8,128)(2,1)}, bf16[32,16,128]{2,1,0:T(8,128)(2,1)S(1)}, u32[]{:S(2)}, u32[]{:S(2)}) collective-permute-start(bf16[32,16,128]{2,1,0:T(8,128)(2,1)} %get-tuple-element.134), channel_id=1, source_target_pairs={{0,7},{1,6},{2,5},{3,4},{4,3},{5,2},{6,1},{7,0},{8,15},{9,14},{10,... | collective-permute-start | bytes 393224 | tf_op jit(solution)/shard_map/ppermute | solution.py:392
  146.7 31.0 %collective-permute-start.18 = (bf16[32,32,128]{2,1,0:T(8,128)(2,1)}, bf16[32,32,128]{2,1,0:T(8,128)(2,1)}, u32[]{:S(2)}, u32[]{:S(2)}) collective-permute-start(bf16[32,32,128]{2,1,0:T(8,128)(2,1)} %get-tuple-element.122), channel_id=1, source_target_pairs={{0,2},{1,3},{2,0},{3,1},{4,6},{5,7},{6,4},{7,5},{8,10},{9,11},{10,... | collective-permute-start | bytes 786440 | tf_op jit(solution)/shard_map/ppermute | solution.py:392
  146.8 31.4 %collective-permute-start.19 = (bf16[32,32,128]{2,1,0:T(8,128)(2,1)}, bf16[32,32,128]{2,1,0:T(8,128)(2,1)}, u32[]{:S(2)}, u32[]{:S(2)}) collective-permute-start(bf16[32,32,128]{2,1,0:T(8,128)(2,1)} %get-tuple-element.123), channel_id=1, source_target_pairs={{0,5},{1,4},{2,7},{3,6},{4,1},{5,0},{6,3},{7,2},{8,13},{9,12},{10,... | collective-permute-start | bytes 786440 | tf_op jit(solution)/shard_map/ppermute | solution.py:392
  148.8 30.2 %collective-permute-start.20 = (bf16[32,32,128]{2,1,0:T(8,128)(2,1)}, bf16[32,32,128]{2,1,0:T(8,128)(2,1)}, u32[]{:S(2)}, u32[]{:S(2)}) collective-permute-start(bf16[32,32,128]{2,1,0:T(8,128)(2,1)} %get-tuple-element.124), channel_id=1, source_target_pairs={{0,3},{1,2},{2,1},{3,0},{4,7},{5,6},{6,5},{7,4},{8,11},{9,10},{10,... | collective-permute-start | bytes 786440 | tf_op jit(solution)/shard_map/ppermute | solution.py:392
  149.0 31.8 %collective-permute-start.21 = (bf16[32,32,128]{2,1,0:T(8,128)(2,1)}, bf16[32,32,128]{2,1,0:T(8,128)(2,1)}, u32[]{:S(2)}, u32[]{:S(2)}) collective-permute-start(bf16[32,32,128]{2,1,0:T(8,128)(2,1)} %get-tuple-element.125), channel_id=1, source_target_pairs={{0,6},{1,7},{2,4},{3,5},{4,2},{5,3},{6,0},{7,1},{8,14},{9,15},{10,... | collective-permute-start | bytes 786440 | tf_op jit(solution)/shard_map/ppermute | solution.py:392
  151.1 29.8 %collective-permute-start.22 = (bf16[32,32,128]{2,1,0:T(8,128)(2,1)}, bf16[32,32,128]{2,1,0:T(8,128)(2,1)}, u32[]{:S(2)}, u32[]{:S(2)}) collective-permute-start(bf16[32,32,128]{2,1,0:T(8,128)(2,1)} %get-tuple-element.126), channel_id=1, source_target_pairs={{0,7},{1,6},{2,5},{3,4},{4,3},{5,2},{6,1},{7,0},{8,15},{9,14},{10,... | collective-permute-start | bytes 786440 | tf_op jit(solution)/shard_map/ppermute | solution.py:392
  178.3 15.6 %collective-permute-start.45 = (bf16[32,16,128]{2,1,0:T(8,128)(2,1)}, bf16[32,16,128]{2,1,0:T(8,128)(2,1)S(1)}, u32[]{:S(2)}, u32[]{:S(2)}) collective-permute-start(bf16[32,16,128]{2,1,0:T(8,128)(2,1)} %get-tuple-element.156), channel_id=1, source_target_pairs={{0,4},{1,5},{2,6},{3,7},{4,0},{5,1},{6,2},{7,3},{8,12},{9,13},{10,... | collective-permute-start | bytes 393224 | tf_op jit(solution)/shard_map/ppermute | solution.py:392
  180.8 15.2 %collective-permute-start.47 = (bf16[32,16,128]{2,1,0:T(8,128)(2,1)}, bf16[32,16,128]{2,1,0:T(8,128)(2,1)S(1)}, u32[]{:S(2)}, u32[]{:S(2)}) collective-permute-start(bf16[32,16,128]{2,1,0:T(8,128)(2,1)} %get-tuple-element.158), channel_id=1, source_target_pairs={{0,5},{1,4},{2,7},{3,6},{4,1},{5,0},{6,3},{7,2},{8,13},{9,12},{10,... | collective-permute-start | bytes 393224 | tf_op jit(solution)/shard_map/ppermute | solution.py:392
  180.9 18.1 %collective-permute-start.48 = (bf16[32,16,128]{2,1,0:T(8,128)(2,1)}, bf16[32,16,128]{2,1,0:T(8,128)(2,1)S(1)}, u32[]{:S(2)}, u32[]{:S(2)}) collective-permute-start(bf16[32,16,128]{2,1,0:T(8,128)(2,1)} %get-tuple-element.159), channel_id=1, source_target_pairs={{0,3},{1,2},{2,1},{3,0},{4,7},{5,6},{6,5},{7,4},{8,11},{9,10},{10,... | collective-permute-start | bytes 393224 | tf_op jit(solution)/shard_map/ppermute | solution.py:392
  191.0 28.0 %collective-permute-start.30 = (bf16[32,32,128]{2,1,0:T(8,128)(2,1)}, bf16[32,32,128]{2,1,0:T(8,128)(2,1)}, u32[]{:S(2)}, u32[]{:S(2)}) collective-permute-start(bf16[32,32,128]{2,1,0:T(8,128)(2,1)} %get-tuple-element.137), channel_id=1, source_target_pairs={{0,1},{1,0},{2,3},{3,2},{4,5},{5,4},{6,7},{7,6},{8,9},{9,8},{10,11... | collective-permute-start | bytes 786440 | tf_op jit(solution)/shard_map/ppermute | solution.py:392
  193.8 28.6 %collective-permute-start.31 = (bf16[32,32,128]{2,1,0:T(8,128)(2,1)}, bf16[32,32,128]{2,1,0:T(8,128)(2,1)}, u32[]{:S(2)}, u32[]{:S(2)}) collective-permute-start(bf16[32,32,128]{2,1,0:T(8,128)(2,1)} %get-tuple-element.138), channel_id=1, source_target_pairs={{0,4},{1,5},{2,6},{3,7},{4,0},{5,1},{6,2},{7,3},{8,12},{9,13},{10,... | collective-permute-start | bytes 786440 | tf_op jit(solution)/shard_map/ppermute | solution.py:392
  193.9 29.0 %collective-permute-start.32 = (bf16[32,32,128]{2,1,0:T(8,128)(2,1)S(1)}, bf16[32,32,128]{2,1,0:T(8,128)(2,1)}, u32[]{:S(2)}, u32[]{:S(2)}) collective-permute-start(bf16[32,32,128]{2,1,0:T(8,128)(2,1)S(1)} %copy-done.44), channel_id=1, source_target_pairs={{0,2},{1,3},{2,0},{3,1},{4,6},{5,7},{6,4},{7,5},{8,10},{9,11},{10,... | collective-permute-start | bytes 786440 | tf_op jit(solution)/shard_map/ppermute | solution.py:392
  196.1 22.2 %collective-permute-start.49 = (bf16[32,16,128]{2,1,0:T(8,128)(2,1)}, bf16[32,16,128]{2,1,0:T(8,128)(2,1)S(1)}, u32[]{:S(2)}, u32[]{:S(2)}) collective-permute-start(bf16[32,16,128]{2,1,0:T(8,128)(2,1)} %get-tuple-element.160), channel_id=1, source_target_pairs={{0,6},{1,7},{2,4},{3,5},{4,2},{5,3},{6,0},{7,1},{8,14},{9,15},{10,... | collective-permute-start | bytes 393224 | tf_op jit(solution)/shard_map/ppermute | solution.py:392
  198.9 19.5 %collective-permute-start.50 = (bf16[32,16,128]{2,1,0:T(8,128)(2,1)}, bf16[32,16,128]{2,1,0:T(8,128)(2,1)}, u32[]{:S(2)}, u32[]{:S(2)}) collective-permute-start(bf16[32,16,128]{2,1,0:T(8,128)(2,1)} %get-tuple-element.161), channel_id=1, source_target_pairs={{0,7},{1,6},{2,5},{3,4},{4,3},{5,2},{6,1},{7,0},{8,15},{9,14},{10,... | collective-permute-start | bytes 393224 | tf_op jit(solution)/shard_map/ppermute | solution.py:392
  218.3 30.2 %collective-permute-start.33 = (bf16[32,32,128]{2,1,0:T(8,128)(2,1)S(1)}, bf16[32,32,128]{2,1,0:T(8,128)(2,1)S(1)}, u32[]{:S(2)}, u32[]{:S(2)}) collective-permute-start(bf16[32,32,128]{2,1,0:T(8,128)(2,1)S(1)} %copy-done.43), channel_id=1, source_target_pairs={{0,5},{1,4},{2,7},{3,6},{4,1},{5,0},{6,3},{7,2},{8,13},{9,12},{10,... | collective-permute-start | bytes 786440 | tf_op jit(solution)/shard_map/ppermute | solution.py:392
  218.4 30.1 %collective-permute-start.34 = (bf16[32,32,128]{2,1,0:T(8,128)(2,1)S(1)}, bf16[32,32,128]{2,1,0:T(8,128)(2,1)S(1)}, u32[]{:S(2)}, u32[]{:S(2)}) collective-permute-start(bf16[32,32,128]{2,1,0:T(8,128)(2,1)S(1)} %copy-done.42), channel_id=1, source_target_pairs={{0,3},{1,2},{2,1},{3,0},{4,7},{5,6},{6,5},{7,4},{8,11},{9,10},{10,... | collective-permute-start | bytes 786440 | tf_op jit(solution)/shard_map/ppermute | solution.py:392
  219.0 29.6 %collective-permute-start.35 = (bf16[32,32,128]{2,1,0:T(8,128)(2,1)S(1)}, bf16[32,32,128]{2,1,0:T(8,128)(2,1)S(1)}, u32[]{:S(2)}, u32[]{:S(2)}) collective-permute-start(bf16[32,32,128]{2,1,0:T(8,128)(2,1)S(1)} %copy-done.40), channel_id=1, source_target_pairs={{0,6},{1,7},{2,4},{3,5},{4,2},{5,3},{6,0},{7,1},{8,14},{9,15},{10,... | collective-permute-start | bytes 786440 | tf_op jit(solution)/shard_map/ppermute | solution.py:392
  222.5 30.9 %collective-permute-start.36 = (bf16[32,32,128]{2,1,0:T(8,128)(2,1)S(1)}, bf16[32,32,128]{2,1,0:T(8,128)(2,1)S(1)}, u32[]{:S(2)}, u32[]{:S(2)}) collective-permute-start(bf16[32,32,128]{2,1,0:T(8,128)(2,1)S(1)} %copy-done.38), channel_id=1, source_target_pairs={{0,7},{1,6},{2,5},{3,4},{4,3},{5,2},{6,1},{7,0},{8,15},{9,14},{10,... | collective-permute-start | bytes 786440 | tf_op jit(solution)/shard_map/ppermute | solution.py:392
  222.8 30.6 %collective-permute-start.51 = (bf16[32,32,128]{2,1,0:T(8,128)(2,1)}, bf16[32,32,128]{2,1,0:T(8,128)(2,1)S(1)}, u32[]{:S(2)}, u32[]{:S(2)}) collective-permute-start(bf16[32,32,128]{2,1,0:T(8,128)(2,1)} %get-tuple-element.163), channel_id=1, source_target_pairs={{0,1},{1,0},{2,3},{3,2},{4,5},{5,4},{6,7},{7,6},{8,9},{9,8},{10,11... | collective-permute-start | bytes 786440 | tf_op jit(solution)/shard_map/ppermute | solution.py:392
  248.5 27.2 %collective-permute-start.52 = (bf16[32,32,128]{2,1,0:T(8,128)(2,1)}, bf16[32,32,128]{2,1,0:T(8,128)(2,1)S(1)}, u32[]{:S(2)}, u32[]{:S(2)}) collective-permute-start(bf16[32,32,128]{2,1,0:T(8,128)(2,1)} %get-tuple-element.164), channel_id=1, source_target_pairs={{0,4},{1,5},{2,6},{3,7},{4,0},{5,1},{6,2},{7,3},{8,12},{9,13},{10,... | collective-permute-start | bytes 786440 | tf_op jit(solution)/shard_map/ppermute | solution.py:392
  248.5 27.2 %collective-permute-start.53 = (bf16[32,32,128]{2,1,0:T(8,128)(2,1)}, bf16[32,32,128]{2,1,0:T(8,128)(2,1)S(1)}, u32[]{:S(2)}, u32[]{:S(2)}) collective-permute-start(bf16[32,32,128]{2,1,0:T(8,128)(2,1)} %get-tuple-element.165), channel_id=1, source_target_pairs={{0,2},{1,3},{2,0},{3,1},{4,6},{5,7},{6,4},{7,5},{8,10},{9,11},{10,... | collective-permute-start | bytes 786440 | tf_op jit(solution)/shard_map/ppermute | solution.py:392
  248.6 33.7 %collective-permute-start.54 = (bf16[32,32,128]{2,1,0:T(8,128)(2,1)}, bf16[32,32,128]{2,1,0:T(8,128)(2,1)S(1)}, u32[]{:S(2)}, u32[]{:S(2)}) collective-permute-start(bf16[32,32,128]{2,1,0:T(8,128)(2,1)} %get-tuple-element.166), channel_id=1, source_target_pairs={{0,5},{1,4},{2,7},{3,6},{4,1},{5,0},{6,3},{7,2},{8,13},{9,12},{10,... | collective-permute-start | bytes 786440 | tf_op jit(solution)/shard_map/ppermute | solution.py:392
  253.4 28.9 %collective-permute-start.37 = (bf16[32,32,128]{2,1,0:T(8,128)(2,1)}, bf16[32,32,128]{2,1,0:T(8,128)(2,1)S(1)}, u32[]{:S(2)}, u32[]{:S(2)}) collective-permute-start(bf16[32,32,128]{2,1,0:T(8,128)(2,1)} %get-tuple-element.145), channel_id=1, source_target_pairs={{0,1},{1,0},{2,3},{3,2},{4,5},{5,4},{6,7},{7,6},{8,9},{9,8},{10,11... | collective-permute-start | bytes 786440 | tf_op jit(solution)/shard_map/ppermute | solution.py:392
  253.4 39.3 %collective-permute-start.38 = (bf16[32,32,128]{2,1,0:T(8,128)(2,1)}, bf16[32,32,128]{2,1,0:T(8,128)(2,1)S(1)}, u32[]{:S(2)}, u32[]{:S(2)}) collective-permute-start(bf16[32,32,128]{2,1,0:T(8,128)(2,1)} %get-tuple-element.146), channel_id=1, source_target_pairs={{0,4},{1,5},{2,6},{3,7},{4,0},{5,1},{6,2},{7,3},{8,12},{9,13},{10,... | collective-permute-start | bytes 786440 | tf_op jit(solution)/shard_map/ppermute | solution.py:392
  275.7 45.3 %collective-permute-start.39 = (bf16[32,32,128]{2,1,0:T(8,128)(2,1)}, bf16[32,32,128]{2,1,0:T(8,128)(2,1)}, u32[]{:S(2)}, u32[]{:S(2)}) collective-permute-start(bf16[32,32,128]{2,1,0:T(8,128)(2,1)} %get-tuple-element.147), channel_id=1, source_target_pairs={{0,2},{1,3},{2,0},{3,1},{4,6},{5,7},{6,4},{7,5},{8,10},{9,11},{10,... | collective-permute-start | bytes 786440 | tf_op jit(solution)/shard_map/ppermute | solution.py:392
  275.7 45.4 %collective-permute-start.40 = (bf16[32,32,128]{2,1,0:T(8,128)(2,1)}, bf16[32,32,128]{2,1,0:T(8,128)(2,1)}, u32[]{:S(2)}, u32[]{:S(2)}) collective-permute-start(bf16[32,32,128]{2,1,0:T(8,128)(2,1)} %get-tuple-element.148), channel_id=1, source_target_pairs={{0,5},{1,4},{2,7},{3,6},{4,1},{5,0},{6,3},{7,2},{8,13},{9,12},{10,... | collective-permute-start | bytes 786440 | tf_op jit(solution)/shard_map/ppermute | solution.py:392
  282.3 41.2 %collective-permute-start.41 = (bf16[32,32,128]{2,1,0:T(8,128)(2,1)}, bf16[32,32,128]{2,1,0:T(8,128)(2,1)}, u32[]{:S(2)}, u32[]{:S(2)}) collective-permute-start(bf16[32,32,128]{2,1,0:T(8,128)(2,1)} %get-tuple-element.149), channel_id=1, source_target_pairs={{0,3},{1,2},{2,1},{3,0},{4,7},{5,6},{6,5},{7,4},{8,11},{9,10},{10,... | collective-permute-start | bytes 786440 | tf_op jit(solution)/shard_map/ppermute | solution.py:392
  282.3 42.6 %collective-permute-start.42 = (bf16[32,32,128]{2,1,0:T(8,128)(2,1)}, bf16[32,32,128]{2,1,0:T(8,128)(2,1)}, u32[]{:S(2)}, u32[]{:S(2)}) collective-permute-start(bf16[32,32,128]{2,1,0:T(8,128)(2,1)} %get-tuple-element.150), channel_id=1, source_target_pairs={{0,6},{1,7},{2,4},{3,5},{4,2},{5,3},{6,0},{7,1},{8,14},{9,15},{10,... | collective-permute-start | bytes 786440 | tf_op jit(solution)/shard_map/ppermute | solution.py:392
  293.4 31.7 %collective-permute-start.43 = (bf16[32,32,128]{2,1,0:T(8,128)(2,1)}, bf16[32,32,128]{2,1,0:T(8,128)(2,1)}, u32[]{:S(2)}, u32[]{:S(2)}) collective-permute-start(bf16[32,32,128]{2,1,0:T(8,128)(2,1)} %get-tuple-element.151), channel_id=1, source_target_pairs={{0,7},{1,6},{2,5},{3,4},{4,3},{5,2},{6,1},{7,0},{8,15},{9,14},{10,... | collective-permute-start | bytes 786440 | tf_op jit(solution)/shard_map/ppermute | solution.py:392
  321.0 21.8 %collective-permute-start.55 = (bf16[32,32,128]{2,1,0:T(8,128)(2,1)}, bf16[32,32,128]{2,1,0:T(8,128)(2,1)}, u32[]{:S(2)}, u32[]{:S(2)}) collective-permute-start(bf16[32,32,128]{2,1,0:T(8,128)(2,1)} %get-tuple-element.167), channel_id=1, source_target_pairs={{0,3},{1,2},{2,1},{3,0},{4,7},{5,6},{6,5},{7,4},{8,11},{9,10},{10,... | collective-permute-start | bytes 786440 | tf_op jit(solution)/shard_map/ppermute | solution.py:392
  321.1 21.9 %collective-permute-start.56 = (bf16[32,32,128]{2,1,0:T(8,128)(2,1)}, bf16[32,32,128]{2,1,0:T(8,128)(2,1)}, u32[]{:S(2)}, u32[]{:S(2)}) collective-permute-start(bf16[32,32,128]{2,1,0:T(8,128)(2,1)} %get-tuple-element.168), channel_id=1, source_target_pairs={{0,6},{1,7},{2,4},{3,5},{4,2},{5,3},{6,0},{7,1},{8,14},{9,15},{10,... | collective-permute-start | bytes 786440 | tf_op jit(solution)/shard_map/ppermute | solution.py:392
  323.5 36.3 %collective-permute-start.57 = (bf16[32,32,128]{2,1,0:T(8,128)(2,1)}, bf16[32,32,128]{2,1,0:T(8,128)(2,1)}, u32[]{:S(2)}, u32[]{:S(2)}) collective-permute-start(bf16[32,32,128]{2,1,0:T(8,128)(2,1)} %get-tuple-element.169), channel_id=1, source_target_pairs={{0,7},{1,6},{2,5},{3,4},{4,3},{5,2},{6,1},{7,0},{8,15},{9,14},{10,... | collective-permute-start | bytes 786440 | tf_op jit(solution)/shard_map/ppermute | solution.py:392
  324.9 40.8 %collective-permute-start.58 = (bf16[32,32,128]{2,1,0:T(8,128)(2,1)}, bf16[32,32,128]{2,1,0:T(8,128)(2,1)}, u32[]{:S(2)}, u32[]{:S(2)}) collective-permute-start(bf16[32,32,128]{2,1,0:T(8,128)(2,1)} %get-tuple-element.172), channel_id=1, source_target_pairs={{0,1},{1,0},{2,3},{3,2},{4,5},{5,4},{6,7},{7,6},{8,9},{9,8},{10,11... | collective-permute-start | bytes 786440 | tf_op jit(solution)/shard_map/ppermute | solution.py:392
  325.1 42.5 %collective-permute-start.59 = (bf16[32,32,128]{2,1,0:T(8,128)(2,1)}, bf16[32,32,128]{2,1,0:T(8,128)(2,1)}, u32[]{:S(2)}, u32[]{:S(2)}) collective-permute-start(bf16[32,32,128]{2,1,0:T(8,128)(2,1)} %get-tuple-element.173), channel_id=1, source_target_pairs={{0,4},{1,5},{2,6},{3,7},{4,0},{5,1},{6,2},{7,3},{8,12},{9,13},{10,... | collective-permute-start | bytes 786440 | tf_op jit(solution)/shard_map/ppermute | solution.py:392
  342.8 17.1 %collective-permute-start.65 = (bf16[32,16,128]{2,1,0:T(8,128)(2,1)}, bf16[32,16,128]{2,1,0:T(8,128)(2,1)S(1)}, u32[]{:S(2)}, u32[]{:S(2)}) collective-permute-start(bf16[32,16,128]{2,1,0:T(8,128)(2,1)} %get-tuple-element.181), channel_id=1, source_target_pairs={{0,1},{1,0},{2,3},{3,2},{4,5},{5,4},{6,7},{7,6},{8,9},{9,8},{10,11... | collective-permute-start | bytes 393224 | tf_op jit(solution)/shard_map/ppermute | solution.py:392
  343.0 22.7 %collective-permute-start.66 = (bf16[32,16,128]{2,1,0:T(8,128)(2,1)}, bf16[32,16,128]{2,1,0:T(8,128)(2,1)}, u32[]{:S(2)}, u32[]{:S(2)}) collective-permute-start(bf16[32,16,128]{2,1,0:T(8,128)(2,1)} %get-tuple-element.182), channel_id=1, source_target_pairs={{0,4},{1,5},{2,6},{3,7},{4,0},{5,1},{6,2},{7,3},{8,12},{9,13},{10,... | collective-permute-start | bytes 393224 | tf_op jit(solution)/shard_map/ppermute | solution.py:392
  359.8 15.9 %collective-permute-start.60 = (bf16[32,32,128]{2,1,0:T(8,128)(2,1)}, bf16[32,32,128]{2,1,0:T(8,128)(2,1)S(1)}, u32[]{:S(2)}, u32[]{:S(2)}) collective-permute-start(bf16[32,32,128]{2,1,0:T(8,128)(2,1)} %get-tuple-element.174), channel_id=1, source_target_pairs={{0,2},{1,3},{2,0},{3,1},{4,6},{5,7},{6,4},{7,5},{8,10},{9,11},{10,... | collective-permute-start | bytes 786440 | tf_op jit(solution)/shard_map/ppermute | solution.py:392
  359.9 17.1 %collective-permute-start.61 = (bf16[32,32,128]{2,1,0:T(8,128)(2,1)}, bf16[32,32,128]{2,1,0:T(8,128)(2,1)S(1)}, u32[]{:S(2)}, u32[]{:S(2)}) collective-permute-start(bf16[32,32,128]{2,1,0:T(8,128)(2,1)} %get-tuple-element.175), channel_id=1, source_target_pairs={{0,5},{1,4},{2,7},{3,6},{4,1},{5,0},{6,3},{7,2},{8,13},{9,12},{10,... | collective-permute-start | bytes 786440 | tf_op jit(solution)/shard_map/ppermute | solution.py:392
  365.7 27.1 %collective-permute-start.62 = (bf16[32,32,128]{2,1,0:T(8,128)(2,1)}, bf16[32,32,128]{2,1,0:T(8,128)(2,1)S(1)}, u32[]{:S(2)}, u32[]{:S(2)}) collective-permute-start(bf16[32,32,128]{2,1,0:T(8,128)(2,1)} %get-tuple-element.176), channel_id=1, source_target_pairs={{0,3},{1,2},{2,1},{3,0},{4,7},{5,6},{6,5},{7,4},{8,11},{9,10},{10,... | collective-permute-start | bytes 786440 | tf_op jit(solution)/shard_map/ppermute | solution.py:392
  365.7 27.1 %collective-permute-start.63 = (bf16[32,32,128]{2,1,0:T(8,128)(2,1)}, bf16[32,32,128]{2,1,0:T(8,128)(2,1)S(1)}, u32[]{:S(2)}, u32[]{:S(2)}) collective-permute-start(bf16[32,32,128]{2,1,0:T(8,128)(2,1)} %get-tuple-element.177), channel_id=1, source_target_pairs={{0,6},{1,7},{2,4},{3,5},{4,2},{5,3},{6,0},{7,1},{8,14},{9,15},{10,... | collective-permute-start | bytes 786440 | tf_op jit(solution)/shard_map/ppermute | solution.py:392
  367.6 27.6 %collective-permute-start.64 = (bf16[32,32,128]{2,1,0:T(8,128)(2,1)}, bf16[32,32,128]{2,1,0:T(8,128)(2,1)S(1)}, u32[]{:S(2)}, u32[]{:S(2)}) collective-permute-start(bf16[32,32,128]{2,1,0:T(8,128)(2,1)} %get-tuple-element.178), channel_id=1, source_target_pairs={{0,7},{1,6},{2,5},{3,4},{4,3},{5,2},{6,1},{7,0},{8,15},{9,14},{10,... | collective-permute-start | bytes 786440 | tf_op jit(solution)/shard_map/ppermute | solution.py:392
  375.7 26.5 %collective-permute-start.67 = (bf16[32,16,128]{2,1,0:T(8,128)(2,1)S(1)}, bf16[32,16,128]{2,1,0:T(8,128)(2,1)S(1)}, u32[]{:S(2)}, u32[]{:S(2)}) collective-permute-start(bf16[32,16,128]{2,1,0:T(8,128)(2,1)S(1)} %copy-done.66), channel_id=1, source_target_pairs={{0,2},{1,3},{2,0},{3,1},{4,6},{5,7},{6,4},{7,5},{8,10},{9,11},{10,... | collective-permute-start | bytes 393224 | tf_op jit(solution)/shard_map/ppermute | solution.py:392
  377.0 32.1 %collective-permute-start.68 = (bf16[32,16,128]{2,1,0:T(8,128)(2,1)S(1)}, bf16[32,16,128]{2,1,0:T(8,128)(2,1)S(1)}, u32[]{:S(2)}, u32[]{:S(2)}) collective-permute-start(bf16[32,16,128]{2,1,0:T(8,128)(2,1)S(1)} %copy-done.65), channel_id=1, source_target_pairs={{0,5},{1,4},{2,7},{3,6},{4,1},{5,0},{6,3},{7,2},{8,13},{9,12},{10,... | collective-permute-start | bytes 393224 | tf_op jit(solution)/shard_map/ppermute | solution.py:392
  392.8 16.3 %collective-permute-start.69 = (bf16[32,16,128]{2,1,0:T(8,128)(2,1)S(1)}, bf16[32,16,128]{2,1,0:T(8,128)(2,1)S(1)}, u32[]{:S(2)}, u32[]{:S(2)}) collective-permute-start(bf16[32,16,128]{2,1,0:T(8,128)(2,1)S(1)} %copy-done.64), channel_id=1, source_target_pairs={{0,3},{1,2},{2,1},{3,0},{4,7},{5,6},{6,5},{7,4},{8,11},{9,10},{10,... | collective-permute-start | bytes 393224 | tf_op jit(solution)/shard_map/ppermute | solution.py:392
  392.8 16.3 %collective-permute-start.70 = (bf16[32,16,128]{2,1,0:T(8,128)(2,1)S(1)}, bf16[32,16,128]{2,1,0:T(8,128)(2,1)S(1)}, u32[]{:S(2)}, u32[]{:S(2)}) collective-permute-start(bf16[32,16,128]{2,1,0:T(8,128)(2,1)S(1)} %copy-done.63), channel_id=1, source_target_pairs={{0,6},{1,7},{2,4},{3,5},{4,2},{5,3},{6,0},{7,1},{8,14},{9,15},{10,... | collective-permute-start | bytes 393224 | tf_op jit(solution)/shard_map/ppermute | solution.py:392
  (85 other events, 2300.0 us)
